TPU v7x, 32 devices: a whole 2x2x4 slice. The times are simulated.
32 devices in a mesh: section: 4 (over x, core), expert: 8 (over z, y).
Axes of the slice: x: 2, y: 2, z: 4, core: 2. Of those that a mesh axis runs over, the one named last changes fastest.
Arguments:
- ahead_rows: bfloat16 [4, 384, 7168], P('section', None, 'expert'), may hold values from -6 to 6
- behind_rows: bfloat16 [4, 384, 7168], P('section', None, 'expert'), may hold values from -6 to 6
- behind_grad: bfloat16 [4, 384, 7168], P('section', None, 'expert'), may hold values from -6 to 6
- route_scores: float32 [4, 2, 384], P('section'), may hold values from 0.1 to 1
- route_counts: int32 [4, 2], P('section'), may hold values from 96 to 384, as said below
- gate_up: bfloat16 [4, 8, 2, 1024, 1792], P('section', 'expert'), may hold values from -0.0625 to 0.0625
- down_proj: bfloat16 [4, 8, 1024, 1792], P('section', 'expert'), may hold values from -0.125 to 0.125
Outputs:
- ahead_sent: bfloat16 [4, 384, 7168], P('section', None, 'expert')
- behind_sent: bfloat16 [4, 384, 7168], P('section', None, 'expert')
Inputs may be any that keep to these rules, and one draw needn't show every extreme that they name: `route_counts`: live slots of each section's expert per micro-batch; in each micro-batch some section has all 384 slots live.
All inputs are finite; a program needn't handle non-finite values.
Results may differ from a plain program's by a relative error of at most 0.02.
Values may be sent and summed in bfloat16 or wider, within the bound.
No kernel may reach another device: no remote copies, remote signals or barrier semaphores. Data moves between devices by JAX's collectives and lax.ppermute only.
A program may use at most 64 MiB of HBM per device.

v0:
```python
import jax
import jax.numpy as jnp
from jax import lax
from jax.sharding import PartitionSpec as P

DBLOCKS = 4


def partner_2(value, axis, stride):
    mask = 2**stride
    pairs = [(source, source ^ mask) for source in range(lax.axis_size(axis))]
    return lax.ppermute(value, axis, pairs)


def from_behind(shard, axis, by):
    devices = lax.axis_size(axis)
    pairs = [(i, i + by) for i in range(devices) if 0 <= i + by < devices]
    return lax.ppermute(shard, axis, pairs)


def silu_float(value):
    return value * jax.nn.sigmoid(value)


def upper_side(own_index, bit_level):
    return own_index >> bit_level & 1 == 1


def activate(partials, units):
    pre_ahead = partials[:, : 2 * units]
    gate_val = partials[:, 2 * units : 3 * units]
    up_val = partials[:, 3 * units : 4 * units]
    expanded = partials[:, 4 * units :]
    hidden = (silu_float(pre_ahead[:, :units]) * pre_ahead[:, units:]).astype(jnp.bfloat16)
    sigmoid_gate = jax.nn.sigmoid(gate_val)
    grad_gate = (expanded * up_val * sigmoid_gate * (1.0 + gate_val * (1.0 - sigmoid_gate))).astype(
        jnp.bfloat16
    )
    grad_up = (expanded * gate_val * sigmoid_gate).astype(jnp.bfloat16)
    return (hidden, grad_gate, grad_up)


def body(ahead_rows, behind_rows, behind_grad, route_scores, route_counts, gate_up, down_proj):
    groups = lax.axis_size("expert")
    fgroups = groups // DBLOCKS
    low_bits = fgroups.bit_length() - 1
    height = ahead_rows.shape[1]
    own_index = lax.axis_index("expert")
    weights_in = gate_up[0, 0]
    weights_out = down_proj[0, 0]
    units = weights_in.shape[1]
    slot_ids = jnp.arange(height, dtype=jnp.int32)
    scale_ahead = route_scores[0, 0] * (slot_ids < route_counts[0, 0]).astype(jnp.float32)
    scale_behind = route_scores[0, 1] * (slot_ids < route_counts[0, 1]).astype(jnp.float32)
    scaled_grad = (behind_grad[0].astype(jnp.float32) * scale_behind[:, None]).astype(jnp.bfloat16)
    block_rows = jnp.stack([ahead_rows[0], behind_rows[0], scaled_grad])
    for bit_level in range(low_bits):
        partner = partner_2(block_rows, "expert", bit_level)
        block_rows = jnp.where(
            upper_side(own_index, bit_level),
            jnp.concatenate([partner, block_rows], axis=2),
            jnp.concatenate([block_rows, partner], axis=2),
        )
    pre_both = jnp.einsum(
        "mcd,kfd->mckf", block_rows[:2], weights_in, preferred_element_type=jnp.float32
    )
    expanded = lax.dot_general(
        block_rows[2], weights_out, (((1,), (1,)), ((), ())), preferred_element_type=jnp.float32
    )
    partials = jnp.concatenate(
        [pre_both[0].reshape(height, 2 * units), pre_both[1].reshape(height, 2 * units), expanded],
        axis=1,
    )
    for bit_level in (low_bits, low_bits + 1):
        partials = partials + partner_2(partials.astype(jnp.bfloat16), "expert", bit_level).astype(
            partials.dtype
        )
    hidden, grad_gate, grad_up = activate(partials, units)
    part_ahead = jnp.dot(hidden, weights_out, preferred_element_type=jnp.float32)
    grads_stacked = jnp.stack([grad_gate, grad_up], axis=1)
    part_behind = jnp.einsum(
        "ckf,kfd->cd", grads_stacked, weights_in, preferred_element_type=jnp.float32
    )
    outputs = jnp.stack([part_ahead, part_behind])
    for bit_level in reversed(range(low_bits)):
        half = outputs.shape[2] // 2
        upper_half = upper_side(own_index, bit_level)
        keep_part = jnp.where(upper_half, outputs[:, :, half:], outputs[:, :, :half])
        send_part = jnp.where(upper_half, outputs[:, :, :half], outputs[:, :, half:])
        outputs = keep_part + partner_2(send_part.astype(jnp.bfloat16), "expert", bit_level).astype(
            send_part.dtype
        )
    ahead_out = (outputs[0] * scale_ahead[:, None]).astype(jnp.bfloat16)
    behind_out = outputs[1].astype(jnp.bfloat16)
    moved_ahead = from_behind(ahead_out, "section", 1)
    moved_behind = from_behind(behind_out, "section", -1)
    return (moved_ahead[None], moved_behind[None])


def solution(mesh):
    in_specs = (
        P("section", None, "expert"),
        P("section", None, "expert"),
        P("section", None, "expert"),
        P("section", None, None),
        P("section", None),
        P("section", "expert", None, None, None),
        P("section", "expert", None, None),
    )
    out_specs = (P("section", None, "expert"), P("section", None, "expert"))
    return jax.shard_map(body, mesh=mesh, in_specs=in_specs, out_specs=out_specs, check_vma=False)
```

profile of v0, /device:TPU:1, one launch (start us, length us, event | category | flops | bytes accessed | tf_op | source)
XLA Modules:
  0.0 399.0 jit_solution(2447449330654431172)
XLA Ops:
  0.7 1.4 fusion.36
  4.7 2.9 pad_maximum_fusion.2
  7.6 2.1 collective-permute-start
  9.7 45.0 %collective-permute-done = bf16[3,384,896]{2,1,0:T(8,128)(2,1)} collective-permute-done((bf16[3,384,896]{2,1,0:T(8,128)(2,1)}, bf16[3,384,896]{2,1,0:T(8,128)(2,1)}, u32[]{:S(2)}, u32[]{:S(2)}) %collective-permute-start) | collective-permute-done | bytes 2064416 | tf_op jit(solution)/shard_map/ppermute | solution.py:12
  54.7 3.7 maximum_select_fusion
  58.4 2.8 fusion.7
  61.2 5.9 %fusion = f32[2,384,2,1024]{3,1,2,0:T(8,128)S(1)} fusion(bf16[1,1,2,1024,1792]{4,3,2,1,0:T(8,128)(2,1)S(1)} %bitcast.52, bf16[3,384,1792]{2,1,0:T(8,128)(2,1)S(1)} %maximum_select_fusion), kind=kOutput, calls=%fused_computation.3 | convolution fusion | flops 5637144576 | bytes 16384000 | tf_op jit(solution)/shard_map/mcd,kfd->mckf/dot_general | solution.py:64
  67.1 2.3 fusion.35
  69.4 2.4 copy.9
  71.8 2.4 copy.11
  74.1 3.6 copy.10
  77.7 3.5 copy.12
  81.3 2.8 fusion.4
  85.4 84.0 %collective-permute-done.1 = bf16[384,5120]{1,0:T(8,128)(2,1)S(1)} collective-permute-done((bf16[384,5120]{1,0:T(8,128)(2,1)S(1)}, bf16[384,5120]{1,0:T(8,128)(2,1)S(1)}, u32[]{:S(2)}, u32[]{:S(2)}) %collective-permute-start.1) | collective-permute-done | bytes 3932192 | tf_op jit(solution)/shard_map/ppermute | solution.py:12
  170.4 1.9 collective-permute-start.2
  172.3 169.5 %collective-permute-done.2 = bf16[384,5120]{1,0:T(8,128)(2,1)S(1)} collective-permute-done((bf16[384,5120]{1,0:T(8,128)(2,1)S(1)}, bf16[384,5120]{1,0:T(8,128)(2,1)S(1)}, u32[]{:S(2)}, u32[]{:S(2)}) %collective-permute-start.2) | collective-permute-done | bytes 3932192 | tf_op jit(solution)/shard_map/ppermute | solution.py:12
  341.9 1.8 convert_add_fusion
  344.6 4.1 %fusion.10 = f32[1,384,1792]{2,1,0:T(8,128)S(1)} fusion(bf16[1,1,1024,1792]{3,2,1,0:T(8,128)(2,1)} %param.13, f32[384,5120]{1,0:T(8,128)S(1)} %convert_add_fusion), kind=kOutput, calls=%fused_computation.16 | convolution fusion | flops 1411645440 | bytes 9568256 | tf_op jit(solution)/shard_map/dot_general | solution.py:79
  348.8 3.1 fusion.13
  353.2 29.5 %collective-permute-done.3 = bf16[2,384,896]{2,1,0:T(8,128)(2,1)S(1)} collective-permute-done((bf16[2,384,896]{2,1,0:T(8,128)(2,1)S(1)}, bf16[2,384,896]{2,1,0:T(8,128)(2,1)S(1)}, u32[]{:S(2)}, u32[]{:S(2)}) %collective-permute-start.3) | collective-permute-done | bytes 1376288 | tf_op jit(solution)/shard_map/ppermute | solution.py:12
  383.2 4.0 collective-permute-start.5
  387.3 2.2 collective-permute-start.4
  389.5 6.5 %collective-permute-done.5 = bf16[384,896]{1,0:T(8,128)(2,1)S(1)} collective-permute-done((bf16[384,896]{1,0:T(8,128)(2,1)S(1)}, bf16[384,896]{1,0:T(8,128)(2,1)S(1)}, u32[]{:S(2)}, u32[]{:S(2)}) %collective-permute-start.5) | collective-permute-done | bytes 688160 | tf_op jit(solution)/shard_map/ppermute | solution.py:18
  396.0 1.3 collective-permute-done.4
  (34 shorter events, 9.6 us)
Async XLA Ops:
  0.6 54.0 %copy-start.2 = (bf16[1,384,896]{2,1,0:T(8,128)(2,1)S(1)}, bf16[1,384,896]{2,1,0:T(8,128)(2,1)}, u32[]{:S(2)}) copy-start(bf16[1,384,896]{2,1,0:T(8,128)(2,1)} %param.8) | copy-start | bytes 2064388
  0.6 54.0 %copy-start.3 = (bf16[1,384,896]{2,1,0:T(8,128)(2,1)S(1)}, bf16[1,384,896]{2,1,0:T(8,128)(2,1)}, u32[]{:S(2)}) copy-start(bf16[1,384,896]{2,1,0:T(8,128)(2,1)} %param.7) | copy-start | bytes 2064388
  7.6 47.0 %collective-permute-start = (bf16[3,384,896]{2,1,0:T(8,128)(2,1)}, bf16[3,384,896]{2,1,0:T(8,128)(2,1)}, u32[]{:S(2)}, u32[]{:S(2)}) collective-permute-start(bf16[3,384,896]{2,1,0:T(8,128)(2,1)} %pad_maximum_fusion.2), channel_id=1, source_target_pairs={{0,1},{1,0},{2,3},{3,2},{4,5},{5,4},{6,7},{7,6},{8,9},{9,8},{10,11... | collective-permute-start | bytes 6193160 | tf_op jit(solution)/shard_map/ppermute | solution.py:12
  9.7 48.7 %copy-start.4 = (bf16[1,1,1024,1792]{3,2,1,0:T(8,128)(2,1)S(1)}, bf16[1,1,1024,1792]{3,2,1,0:T(8,128)(2,1)}, u32[]{:S(2)}) copy-start(bf16[1,1,1024,1792]{3,2,1,0:T(8,128)(2,1)} %param.13) | copy-start | bytes 11010052
  54.7 6.5 %slice-start = ((s8[7340032]{0:T(1024)(128)(4,1)}), s8[4194304]{0:T(1024)(128)(4,1)S(1)}, s32[]{:S(2)}) async-start(s8[7340032]{0:T(1024)(128)(4,1)} %bitcast.51), calls=%async_computation | async-start | bytes 8388608
  58.4 2.8 slice-start.1
  81.3 88.1 %copy-start = (f32[384,2048]{1,0:T(8,128)S(1)}, f32[384,2048]{1,0:T(8,128)}, u32[]{:S(2)}) copy-start(f32[384,2048]{1,0:T(8,128)} %copy.12) | copy-start | bytes 9437188
  81.3 88.1 %copy-start.1 = (f32[384,1024]{1,0:T(8,128)S(1)}, f32[384,1024]{1,0:T(8,128)}, u32[]{:S(2)}) copy-start(f32[384,1024]{1,0:T(8,128)} %fusion.7) | copy-start | bytes 4718596
  84.1 85.3 %collective-permute-start.1 = (bf16[384,5120]{1,0:T(8,128)(2,1)S(1)}, bf16[384,5120]{1,0:T(8,128)(2,1)S(1)}, u32[]{:S(2)}, u32[]{:S(2)}) collective-permute-start(bf16[384,5120]{1,0:T(8,128)(2,1)S(1)} %fusion.4), channel_id=1, source_target_pairs={{0,2},{1,3},{2,0},{3,1},{4,6},{5,7},{6,4},{7,5},{8,10},{9,11},{10,... | collective-permute-start | bytes 11796488 | tf_op jit(solution)/shard_map/ppermute | solution.py:12
  170.4 171.5 %collective-permute-start.2 = (bf16[384,5120]{1,0:T(8,128)(2,1)S(1)}, bf16[384,5120]{1,0:T(8,128)(2,1)S(1)}, u32[]{:S(2)}, u32[]{:S(2)}) collective-permute-start(bf16[384,5120]{1,0:T(8,128)(2,1)S(1)} %fusion.9), channel_id=1, source_target_pairs={{0,4},{1,5},{2,6},{3,7},{4,0},{5,1},{6,2},{7,3},{8,12},{9,13},{10,... | collective-permute-start | bytes 11796488 | tf_op jit(solution)/shard_map/ppermute | solution.py:12
  343.6 5.1 %slice-start.2 = ((s8[7340032]{0:T(1024)(128)(4,1)}), s8[4194304]{0:T(1024)(128)(4,1)S(1)}, s32[]{:S(2)}) async-start(s8[7340032]{0:T(1024)(128)(4,1)} %bitcast.53), calls=%async_computation.2 | async-start | bytes 8388608
  344.6 4.2 %slice-start.3 = ((s8[7340032]{0:T(1024)(128)(4,1)}), s8[3145728]{0:T(1024)(128)(4,1)S(1)}, s32[]{:S(2)}) async-start(s8[7340032]{0:T(1024)(128)(4,1)} %bitcast.53), calls=%async_computation.3 | async-start | bytes 6291456
  352.1 30.6 %collective-permute-start.3 = (bf16[2,384,896]{2,1,0:T(8,128)(2,1)S(1)}, bf16[2,384,896]{2,1,0:T(8,128)(2,1)S(1)}, u32[]{:S(2)}, u32[]{:S(2)}) collective-permute-start(bf16[2,384,896]{2,1,0:T(8,128)(2,1)S(1)} %select_convert_fusion), channel_id=1, source_target_pairs={{0,1},{1,0},{2,3},{3,2},{4,5},{5,4},{6,7},{7,6},{8,9},{9,8},{10,11... | collective-permute-start | bytes 4128776 | tf_op jit(solution)/shard_map/ppermute | solution.py:12
  383.2 12.9 %collective-permute-start.5 = (bf16[384,896]{1,0:T(8,128)(2,1)S(1)}, bf16[384,896]{1,0:T(8,128)(2,1)S(1)}, u32[]{:S(2)}, u32[]{:S(2)}) collective-permute-start(bf16[384,896]{1,0:T(8,128)(2,1)S(1)} %fusion.30), channel_id=1, source_target_pairs={{8,0},{16,8},{24,16},{9,1},{17,9},{25,17},{10,2},{18,10},{26,18},{... | collective-permute-start | bytes 2064392 | tf_op jit(solution)/shard_map/ppermute | solution.py:18
  387.3 10.1 %collective-permute-start.4 = (bf16[384,896]{1,0:T(8,128)(2,1)S(1)}, bf16[384,896]{1,0:T(8,128)(2,1)S(1)}, u32[]{:S(2)}, u32[]{:S(2)}) collective-permute-start(bf16[384,896]{1,0:T(8,128)(2,1)S(1)} %fusion.25), channel_id=1, source_target_pairs={{0,8},{8,16},{16,24},{1,9},{9,17},{17,25},{2,10},{10,18},{18,26},{... | collective-permute-start | bytes 2064392 | tf_op jit(solution)/shard_map/ppermute | solution.py:18
where the time goes:
time: 400 us; the launch traced here: 399 us
  waiting for transfers between devices  336 us (84%)
  local copies, waits for them, and re-layouts  18.1 us (5%)
  other arithmetic  16.5 us (4%)
  matrix products  15.8 us (4%)
  starting transfers between devices  11.9 us (3%)
    ppermute x4, waiting for transfers between devices, partner_2(): return lax.ppermute(value, axis, pairs)  328 us
  transfers between devices with their start and end apart: 6, of which 6 were waited for; matrix products, arithmetic and copies ran while one was open for 0% of the time, Pallas kernels for 0%

commit v1 on v0

v1 whole, which is shorter than its diff:
```python
import jax
import jax.numpy as jnp
from jax import lax
from jax.sharding import PartitionSpec as P

DBLOCKS = 4
BF16 = jnp.bfloat16
F32 = jnp.float32


def shift(shard, axis, by):
    devices = lax.axis_size(axis)
    pairs = [(i, i + by) for i in range(devices) if 0 <= i + by < devices]
    return lax.ppermute(shard, axis, pairs)


def body(ahead_rows, behind_rows, behind_grad, route_scores, route_counts, gate_up, down_proj):
    groups = lax.axis_size("expert")
    fgroups = groups // DBLOCKS
    low = [[q * fgroups + f for f in range(fgroups)] for q in range(DBLOCKS)]
    high = [[q * fgroups + f for q in range(DBLOCKS)] for f in range(fgroups)]
    height = ahead_rows.shape[1]
    weights_in = gate_up[0, 0]
    weights_out = down_proj[0, 0]
    units = weights_in.shape[1]
    part = units // DBLOCKS
    own = lax.axis_index("expert")
    block = own // fgroups

    def wide(rows):
        return lax.all_gather(rows, "expert", axis_index_groups=low, axis=1, tiled=True)

    def reduced(partials):
        flat = partials.reshape(-1, partials.shape[-1])
        total = lax.psum_scatter(
            flat, "expert", axis_index_groups=high, scatter_dimension=0, tiled=True
        )
        return total.astype(F32).reshape(partials.shape[1:])

    def spread(values):
        return lax.all_gather(values, "expert", axis_index_groups=high, axis=0, tiled=False)

    def narrowed(values):
        return lax.psum_scatter(
            values.astype(BF16), "expert", axis_index_groups=low, scatter_dimension=1, tiled=True
        )

    slot_ids = jnp.arange(height, dtype=jnp.int32)
    scale_ahead = route_scores[0, 0] * (slot_ids < route_counts[0, 0]).astype(F32)
    scale_behind = route_scores[0, 1] * (slot_ids < route_counts[0, 1]).astype(F32)
    gates = weights_in.reshape(2, DBLOCKS, part, -1)
    downs = weights_out.reshape(DBLOCKS, part, -1)

    ahead_wide = wide(ahead_rows[0])
    pre_a = jnp.einsum("cd,kqfd->qkcf", ahead_wide, gates, preferred_element_type=F32).astype(BF16)
    sum_a = reduced(pre_a)
    hidden = (sum_a[0] * jax.nn.sigmoid(sum_a[0]) * sum_a[1]).astype(BF16)
    hidden_all = spread(hidden)

    behind_wide = wide(behind_rows[0])
    grad_wide = wide(behind_grad[0])
    pre_b = jnp.einsum("cd,kqfd->qkcf", behind_wide, gates, preferred_element_type=F32).astype(BF16)
    exp_b = jnp.einsum("cd,qfd->qcf", grad_wide, downs, preferred_element_type=F32).astype(BF16)
    sum_b = reduced(jnp.concatenate([pre_b, exp_b[:, None]], axis=1))
    gate, up, expanded = sum_b[0], sum_b[1], sum_b[2] * scale_behind[:, None]
    sig = jax.nn.sigmoid(gate)
    grad_gate = (expanded * up * sig * (1.0 + gate * (1.0 - sig))).astype(BF16)
    grad_up = (expanded * gate * sig).astype(BF16)
    grads_all = spread(jnp.stack([grad_gate, grad_up]))

    out_a = jnp.einsum("qcf,qfd->cd", hidden_all, downs, preferred_element_type=F32)
    ahead_out = (narrowed(out_a).astype(F32) * scale_ahead[:, None]).astype(BF16)
    moved_ahead = shift(ahead_out, "section", 1)
    out_b = jnp.einsum("qkcf,kqfd->cd", grads_all, gates, preferred_element_type=F32)
    behind_out = narrowed(out_b)
    moved_behind = shift(behind_out, "section", -1)
    return (moved_ahead[None], moved_behind[None])


def solution(mesh):
    in_specs = (
        P("section", None, "expert"),
        P("section", None, "expert"),
        P("section", None, "expert"),
        P("section", None, None),
        P("section", None),
        P("section", "expert", None, None, None),
        P("section", "expert", None, None),
    )
    out_specs = (P("section", None, "expert"), P("section", None, "expert"))
    return jax.shard_map(body, mesh=mesh, in_specs=in_specs, out_specs=out_specs, check_vma=False)
```

time: 400 us -> 295 us (0.74)
  waiting for transfers between devices: 336 us -> 207 us
  blocking collectives: 0 us -> 19 us
  matrix products: 15.8 us -> 29.6 us
  between operations: 0.85 us -> 14.2 us
  other arithmetic: 16.5 us -> 5.06 us
  starting transfers between devices: 11.9 us -> 6.73 us
  local copies, waits for them, and re-layouts: 18.1 us -> 13 us
    ppermute x6 -> x2, waiting for transfers between devices: 336 us -> 9.68 us  [shift(): return lax.ppermute(shard, axis, pairs)]
    all_gather x0 -> x4, waiting for transfers between devices: none -> 83.9 us  [the longest x3 65.6 us: wide(): lax.all_gather(rows, 'expert', axis_index_groups=low, axis=1, tiled=True)]
    reduce_scatter x0 -> x2, waiting for transfers between devices: none -> 73.8 us  [reduced(): lax.psum_scatter(flat, 'expert', axis_index_groups=high, scatter_dimensio...]
    unnamed x0 -> x10, waiting for transfers between devices: none -> 39.5 us
    all_gather x0 -> x1, blocking collectives: none -> 19 us  [spread(): lax.all_gather(values, 'expert', axis_index_groups=high, axis=0, tiled=Fa...]
    dot_general x4 -> x5, matrix products: 15.8 us -> 29.6 us  [the longest x1 7.43 us: body(): jnp.einsum('cd,kqfd->qkcf', behind_wide, gates, preferred_element_type=F32)]
    slice x5 -> x2, local copies, waits for them, and re-layouts: 10.4 us -> 0.6 us  [the longest x1 0.58 us: body(): route_counts[0, 1]]
    unnamed x20 -> x10, local copies, waits for them, and re-layouts: 1.74 us -> 8.25 us
  transfers between devices with their start and end apart: 6 -> 10, of which waited for: 6 -> 9; matrix products, arithmetic and copies ran while one was open for 0% -> 15% of each run, Pallas kernels for 0% -> 0%
where the time goes in v1:
time: 295 us
  waiting for transfers between devices  207 us (70%)
  matrix products  29.6 us (10%)
  blocking collectives  19 us (6%)
  between operations  14.2 us (5%)
  local copies, waits for them, and re-layouts  13 us (4%)
  starting transfers between devices  6.73 us (2%)
  other arithmetic  5.06 us (2%)
    reduce_scatter x2, waiting for transfers between devices, reduced(): lax.psum_scatter(flat, 'expert', axis_index_groups=high, scatter_dimensio...  73.8 us
    all_gather x3, waiting for transfers between devices, wide(): lax.all_gather(rows, 'expert', axis_index_groups=low, axis=1, tiled=True)  65.6 us
    unnamed x10, waiting for transfers between devices  39.5 us
    all_gather x1, blocking collectives, spread(): lax.all_gather(values, 'expert', axis_index_groups=high, axis=0, tiled=Fa...  19 us
    all_gather x1, waiting for transfers between devices, spread(): lax.all_gather(values, 'expert', axis_index_groups=high, axis=0, tiled=Fa...  18.3 us
    ppermute x2, waiting for transfers between devices, shift(): return lax.ppermute(shard, axis, pairs)  9.68 us
    unnamed x10, local copies, waits for them, and re-layouts  8.25 us
    dot_general x1, matrix products, body(): jnp.einsum('cd,kqfd->qkcf', behind_wide, gates, preferred_element_type=F32)  7.43 us
  transfers between devices with their start and end apart: 10, of which 9 were waited for; matrix products, arithmetic and copies ran while one was open for 15% of the time, Pallas kernels for 0%

profile of v1, /device:TPU:1, one launch (start us, length us, event | category | flops | bytes accessed | tf_op | source)
XLA Modules:
  0.0 294.5 jit_solution(7025315402517271172)
XLA Ops:
  9.4 27.2 %all-gather.14.cloned.1.call-done = bf16[1,384,1792]{2,1,0:T(8,128)(2,1)} async-done(((bf16[1,384,896]{2,1,0:T(8,128)(2,1)}), bf16[1,384,1792]{2,1,0:T(8,128)(2,1)}) %all-gather.14.cloned.1.call-update) | async-done | bytes 1376272 | tf_op jit(solution)/shard_map/all_gather | solution.py:31
  36.7 4.5 %fusion.8 = bf16[4,1,384,256]{2,3,0,1:T(8,128)(2,1)S(1)} fusion(bf16[4,256,1792]{2,1,0:T(8,128)(2,1)} %bitcast.74, bf16[1,384,1792]{2,1,0:T(8,128)(2,1)} %all-gather.14.cloned.1.call-done), kind=kOutput, calls=%fused_computation.15 | convolution fusion | flops 1409679360 | bytes 5832704 | tf_op jit(solution)/shard_map/cd,qfd->qcf/dot_general | solution.py:63
  41.2 22.1 %all-gather.12.cloned.1.call-done = bf16[1,384,1792]{2,1,0:T(8,128)(2,1)} async-done(((bf16[1,384,896]{2,1,0:T(8,128)(2,1)}), bf16[1,384,1792]{2,1,0:T(8,128)(2,1)}) %all-gather.12.cloned.1.call-update) | async-done | bytes 1376272 | tf_op jit(solution)/shard_map/all_gather | solution.py:31
  63.2 7.4 %fusion.4 = bf16[4,2,384,256]{2,3,0,1:T(8,128)(2,1)S(1)} fusion(bf16[2,4,256,1792]{3,2,1,0:T(8,128)(2,1)} %bitcast.71, bf16[1,384,1792]{2,1,0:T(8,128)(2,1)} %all-gather.12.cloned.1.call-done), kind=kOutput, calls=%fused_computation.9 | convolution fusion | flops 2819358720 | bytes 10289152 | tf_op jit(solution)/shard_map/cd,kqfd->qkcf/dot_general | solution.py:62
  70.9 2.5 copy.13
  73.5 16.3 %all-gather.10.cloned.1.call-done = bf16[1,384,1792]{2,1,0:T(8,128)(2,1)} async-done(((bf16[1,384,896]{2,1,0:T(8,128)(2,1)}), bf16[1,384,1792]{2,1,0:T(8,128)(2,1)}) %all-gather.10.cloned.1.call-update) | async-done | bytes 1376272 | tf_op jit(solution)/shard_map/all_gather | solution.py:31
  89.8 7.4 %fusion.3 = bf16[4,2,384,256]{2,3,0,1:T(8,128)(2,1)S(1)} fusion(bf16[2,4,256,1792]{3,2,1,0:T(8,128)(2,1)} %bitcast.72, bf16[1,384,1792]{2,1,0:T(8,128)(2,1)} %all-gather.10.cloned.1.call-done), kind=kOutput, calls=%fused_computation.8 | convolution fusion | flops 2819358720 | bytes 10289152 | tf_op jit(solution)/shard_map/cd,kqfd->qkcf/dot_general | solution.py:55
  97.2 1.6 copy.12
  100.8 39.1 %reduce-scatter.11.cloned.1.call-done = bf16[1152,256]{1,0:T(8,128)(2,1)} async-done(((bf16[4608,256]{1,0:T(8,128)(2,1)}), bf16[1152,256]{1,0:T(8,128)(2,1)}) %reduce-scatter.11.cloned.1.call-update) | async-done | bytes 589840 | tf_op jit(solution)/shard_map/reduce_scatter | solution.py:35
  139.9 1.1 convert_element_type.58
  142.1 34.8 %reduce-scatter.9.cloned.1.call-done = bf16[768,256]{1,0:T(8,128)(2,1)} async-done(((bf16[3072,256]{1,0:T(8,128)(2,1)}), bf16[768,256]{1,0:T(8,128)(2,1)}) %reduce-scatter.9.cloned.1.call-update) | async-done | bytes 393232 | tf_op jit(solution)/shard_map/reduce_scatter | solution.py:35
  178.0 19.0 %all-gather.1 = bf16[1536,256]{1,0:T(8,128)(2,1)S(1)} all-gather(bf16[384,256]{1,0:T(8,128)(2,1)S(1)} %fusion.14), channel_id=3, replica_groups={{0,2,4,6},{1,3,5,7},{8,10,12,14},{9,11,13,15},{16,18,20,22},{17,19,21,2..., dimensions={0}, use_global_device_ids=true | all-gather | bytes 983040 | tf_op jit(solution)/shard_map/all_gather | solution.py:41
  197.1 3.6 %fusion = bf16[384,1792]{1,0:T(8,128)(2,1)S(1)} fusion(bf16[4,384,256]{2,1,0:T(8,128)(2,1)S(1)} %bitcast.66, bf16[4,256,1792]{2,1,0:T(8,128)(2,1)} %bitcast.75), kind=kOutput, calls=%fused_computation.2 | convolution fusion | flops 1409974272 | bytes 5832704 | tf_op jit(solution)/shard_map/qcf,qfd->cd/dot_general | solution.py:71
  200.7 1.6 copy.18
  202.5 18.3 %all-gather.16.cloned.1.call-done = bf16[8,384,256]{2,1,0:T(8,128)(2,1)} async-done(((bf16[2,384,256]{2,1,0:T(8,128)(2,1)}), bf16[8,384,256]{2,1,0:T(8,128)(2,1)}) %all-gather.16.cloned.1.call-update) | async-done | bytes 1572880 | tf_op jit(solution)/shard_map/all_gather | solution.py:41
  220.9 6.6 %fusion.1 = bf16[384,1792]{1,0:T(8,128)(2,1)S(1)} fusion(bf16[2,4,256,1792]{3,2,1,0:T(8,128)(2,1)} %bitcast.73, bf16[4,2,384,256]{3,2,1,0:T(8,128)(2,1)} %bitcast.76), kind=kOutput, calls=%fused_computation.3 | convolution fusion | flops 2819260416 | bytes 10289152 | tf_op jit(solution)/shard_map/qkcf,kqfd->cd/dot_general | solution.py:74
  227.4 1.6 copy.20
  229.7 16.3 %reduce-scatter.13.cloned.1.call-done = bf16[896,384]{1,0:T(8,128)(2,1)} async-done(((bf16[1792,384]{1,0:T(8,128)(2,1)}), bf16[896,384]{1,0:T(8,128)(2,1)}) %reduce-scatter.13.cloned.1.call-update) | async-done | bytes 688144
  246.0 1.4 copy.19
  247.6 3.6 %collective-permute-start = (bf16[384,896]{1,0:T(8,128)(2,1)S(1)}, bf16[384,896]{1,0:T(8,128)(2,1)S(1)}, u32[]{:S(2)}, u32[]{:S(2)}) collective-permute-start(bf16[384,896]{1,0:T(8,128)(2,1)S(1)} %multiply_convert_fusion), channel_id=1, source_target_pairs={{0,8},{8,16},{16,24},{1,9},{9,17},{17,25},{2,10},{10,18},{18,26},{... | collective-permute-start | bytes 2064392 | tf_op jit(solution)/shard_map/ppermute | solution.py:14
  251.2 21.0 %reduce-scatter.15.cloned.1.call-done = bf16[896,384]{1,0:T(8,128)(2,1)} async-done(((bf16[1792,384]{1,0:T(8,128)(2,1)}), bf16[896,384]{1,0:T(8,128)(2,1)}) %reduce-scatter.15.cloned.1.call-update) | async-done | bytes 688144
  272.3 1.4 copy.21
  273.7 2.6 collective-permute-start.1
  276.3 9.7 %collective-permute-done.1 = bf16[384,896]{1,0:T(8,128)(2,1)S(1)} collective-permute-done((bf16[384,896]{1,0:T(8,128)(2,1)S(1)}, bf16[384,896]{1,0:T(8,128)(2,1)S(1)}, u32[]{:S(2)}, u32[]{:S(2)}) %collective-permute-start.1) | collective-permute-done | bytes 688160 | tf_op jit(solution)/shard_map/ppermute | solution.py:14
  (33 shorter events, 9.4 us)
Async XLA Ops:
  7.2 29.5 %all-gather.14.cloned.1.call-start = ((), (), s32[]{:S(2)}) async-start(), calls=%async_computation.8 | async-start | bytes 2064384 | tf_op jit(solution)/shard_map/all_gather | solution.py:31
  7.9 55.3 %all-gather.12.cloned.1.call-start = ((), (), s32[]{:S(2)}) async-start(), calls=%async_computation.7 | async-start | bytes 2064384 | tf_op jit(solution)/shard_map/all_gather | solution.py:31
  8.6 81.2 %all-gather.10.cloned.1.call-start = ((), (), s32[]{:S(2)}) async-start(), calls=%async_computation.6 | async-start | bytes 2064384 | tf_op jit(solution)/shard_map/all_gather | solution.py:31
  9.4 130.5 %reduce-scatter.11.cloned.1.call-start = ((), (), s32[]{:S(2)}) async-start(), calls=%async_computation.5 | async-start | bytes 2949120 | tf_op jit(solution)/shard_map/reduce_scatter | solution.py:35
  73.5 103.4 %reduce-scatter.9.cloned.1.call-start = ((), (), s32[]{:S(2)}) async-start(), calls=%async_computation.4 | async-start | bytes 1966080 | tf_op jit(solution)/shard_map/reduce_scatter | solution.py:35
  98.9 0.7 copy-start.1
  98.9 1.2 copy-start
  98.9 121.9 %all-gather.16.cloned.1.call-start = ((), (), s32[]{:S(2)}) async-start(), calls=%async_computation.9 | async-start | bytes 1966080 | tf_op jit(solution)/shard_map/all_gather | solution.py:41
  142.1 103.9 %reduce-scatter.13.cloned.1.call-start = ((), (), s32[]{:S(2)}) async-start(), calls=%async_computation.10 | async-start | bytes 2064384
  202.3 69.9 %reduce-scatter.15.cloned.1.call-start = ((), (), s32[]{:S(2)}) async-start(), calls=%async_computation.11 | async-start | bytes 2064384
  247.6 28.7 %collective-permute-start = (bf16[384,896]{1,0:T(8,128)(2,1)S(1)}, bf16[384,896]{1,0:T(8,128)(2,1)S(1)}, u32[]{:S(2)}, u32[]{:S(2)}) collective-permute-start(bf16[384,896]{1,0:T(8,128)(2,1)S(1)} %multiply_convert_fusion), channel_id=1, source_target_pairs={{0,8},{8,16},{16,24},{1,9},{9,17},{17,25},{2,10},{10,18},{18,26},{... | collective-permute-start | bytes 2064392 | tf_op jit(solution)/shard_map/ppermute | solution.py:14
  273.7 12.3 %collective-permute-start.1 = (bf16[384,896]{1,0:T(8,128)(2,1)S(1)}, bf16[384,896]{1,0:T(8,128)(2,1)S(1)}, u32[]{:S(2)}, u32[]{:S(2)}) collective-permute-start(bf16[384,896]{1,0:T(8,128)(2,1)S(1)} %copy.21), channel_id=1, source_target_pairs={{8,0},{16,8},{24,16},{9,1},{17,9},{25,17},{10,2},{18,10},{26,18},{... | collective-permute-start | bytes 2064392 | tf_op jit(solution)/shard_map/ppermute | solution.py:14
Sparse Core Ops, SparseCore 0:
  9.5 27.0 all-gather.13
  38.2 24.9 all-gather.11
  64.8 24.9 all-gather.9
  92.0 47.8 reduce-scatter.10
  142.0 34.8 reduce-scatter.8
  178.9 41.9 all-gather.15
  223.1 22.8 reduce-scatter.12
  248.3 23.8 reduce-scatter.14

commit v2 on v1

--- a/solution.py
+++ b/solution.py
@@ -1,17 +1,254 @@
+import functools
+
 import jax
 import jax.numpy as jnp
 from jax import lax
+from jax.experimental import pallas as pl
+from jax.experimental.pallas import tpu as pltpu
 from jax.sharding import PartitionSpec as P
 
 DBLOCKS = 4
 BF16 = jnp.bfloat16
 F32 = jnp.float32
+VMEM_LIMIT = 40 * 1024 * 1024
 
 
 def shift(shard, axis, by):
     devices = lax.axis_size(axis)
     pairs = [(i, i + by) for i in range(devices) if 0 <= i + by < devices]
     return lax.ppermute(shard, axis, pairs)
+
+
+def call(kernel, flops, size, **kwargs):
+    return pl.pallas_call(
+        kernel,
+        compiler_params=pltpu.CompilerParams(vmem_limit_bytes=VMEM_LIMIT),
+        cost_estimate=pl.CostEstimate(flops=flops, bytes_accessed=size, transcendentals=0),
+        **kwargs,
+    )
+
+
+def join_rows(own_col, width, own, partner, joined):
+    at = pl.multiple_of(own_col * width, 128)
+    other = pl.multiple_of((1 - own_col) * width, 128)
+    joined[:, pl.ds(at, width)] = own[...]
+    joined[:, pl.ds(other, width)] = partner[...]
+
+
+def times_transposed(rows, tile):
+    return lax.dot_general(
+        rows, tile, (((1,), (1,)), ((), ())), preferred_element_type=F32
+    ).astype(BF16)
+
+
+def ahead_first_kernel(width, which, own, partner, gates, out, joined):
+    @pl.when((pl.program_id(0) == 0) & (pl.program_id(1) == 0))
+    def _():
+        join_rows(which[1], width, own, partner, joined)
+
+    out[0] = times_transposed(joined[...], gates[0])
+
+
+def behind_first_kernel(
+    width, which, own, partner, grad_own, grad_partner, gates, downs, out, joined, grad_joined
+):
+    @pl.when((pl.program_id(0) == 0) & (pl.program_id(1) == 0))
+    def _():
+        join_rows(which[1], width, own, partner, joined)
+        join_rows(which[1], width, grad_own, grad_partner, grad_joined)
+
+    @pl.when(pl.program_id(0) < 2)
+    def _():
+        out[0] = times_transposed(joined[...], gates[0])
+
+    @pl.when(pl.program_id(0) == 2)
+    def _():
+        out[0] = times_transposed(grad_joined[...], downs[...])
+
+
+def first_product(which, rows, grads, gate_up, down):
+    slots, width = rows[0].shape
+    units, features = gate_up.shape[1:]
+    half = units // 2
+    tile = min(256, half)
+    steps = half // tile
+    parts = 3 if grads else 2
+    row_spec = pl.BlockSpec((slots, width), lambda k, j, w: (0, 0))
+
+    def gate_at(k, j, w):
+        return (jnp.minimum(k, 1), w[0] * steps + jnp.where(k < 2, j, steps - 1), 0)
+
+    def down_at(k, j, w):
+        return (w[0] * steps + jnp.where(k < 2, 0, j), 0)
+
+    in_specs = [row_spec] * (2 * (parts - 1)) + [pl.BlockSpec((1, tile, features), gate_at)]
+    operands = [*rows, *(grads or ()), gate_up]
+    if grads:
+        in_specs.append(pl.BlockSpec((tile, features), down_at))
+        operands.append(down)
+    kernel = behind_first_kernel if grads else ahead_first_kernel
+    return call(
+        functools.partial(kernel, width),
+        2 * slots * features * half * parts,
+        2 * (features * half * parts + slots * half * parts + slots * features * (parts - 1)),
+        out_shape=jax.ShapeDtypeStruct((parts, slots, half), BF16),
+        grid_spec=pltpu.PrefetchScalarGridSpec(
+            num_scalar_prefetch=1,
+            grid=(parts, steps),
+            in_specs=in_specs,
+            out_specs=pl.BlockSpec((1, slots, tile), lambda k, j, w: (k, 0, j)),
+            scratch_shapes=[pltpu.VMEM((slots, features), BF16)] * (parts - 1),
+        ),
+    )(which, *operands)
+
+
+def ahead_act_kernel(near, arrived, out):
+    gate = near[0].astype(F32) + arrived[0].astype(F32)
+    up = near[1].astype(F32) + arrived[1].astype(F32)
+    out[0] = (gate * jax.nn.sigmoid(gate) * up).astype(BF16)
+
+
+def behind_act_kernel(near, arrived, scale, out):
+    gate = near[0].astype(F32) + arrived[0].astype(F32)
+    up = near[1].astype(F32) + arrived[1].astype(F32)
+    expanded = (near[2].astype(F32) + arrived[2].astype(F32)) * scale[...]
+    sig = jax.nn.sigmoid(gate)
+    out[0] = (expanded * up * sig * (1.0 + gate * (1.0 - sig))).astype(BF16)
+    out[1] = (expanded * gate * sig).astype(BF16)
+
+
+def activation(near, arrived, scale):
+    parts, slots, half = near.shape
+    kernel = ahead_act_kernel if scale is None else behind_act_kernel
+    operands = (near, arrived) if scale is None else (near, arrived, scale)
+    return call(
+        kernel,
+        10 * slots * half,
+        2 * (3 * parts - 1) * slots * half,
+        out_shape=jax.ShapeDtypeStruct((parts - 1, slots, half), BF16),
+    )(*operands)
+
+
+def second_kernel(kinds, which, own, one, two, three, tile, out, total):
+    far = pl.program_id(0)
+    kind = pl.program_id(1)
+    last = (far == 1) & (kind == kinds - 1)
+    at_end = which[2] == 1
+
+    def add(values):
+        product = jnp.dot(
+            values[0], tile[0], preferred_element_type=F32
+        )
+
+        @pl.when((far == 0) & (kind == 0))
+        def _():
+            total[...] = product
+
+        @pl.when((far == 1) | (kind > 0))
+        def _():
+            total[...] += product
+
+    near_value = jnp.where(at_end, own[...], one[...])
+    far_value = jnp.where(at_end, three[...], two[...])
+    add(jnp.where(far == 0, near_value, far_value))
+
+    @pl.when(last)
+    def _():
+        out[...] = total[...].astype(out.dtype)
+
+
+def second_product(which, column, values, weights, dtype):
+    kinds, slots, half = values[0].shape
+    width = weights.shape[2] // 2
+
+    def tile_at(far, kind, w):
+        return (kind, jnp.where(far == 0, w[0], 1 - w[0]), jnp.where(column, w[1], 1 - w[1]))
+
+    value_spec = pl.BlockSpec((1, slots, half), lambda far, kind, w: (kind, 0, 0))
+    return call(
+        functools.partial(second_kernel, kinds),
+        4 * slots * half * width * kinds,
+        2 * (2 * half * width * kinds + slots * width * 2 + 4 * slots * half * kinds),
+        out_shape=jax.ShapeDtypeStruct((slots, width), dtype),
+        grid_spec=pltpu.PrefetchScalarGridSpec(
+            num_scalar_prefetch=1,
+            grid=(2, kinds),
+            in_specs=[value_spec] * 4 + [pl.BlockSpec((1, half, width), tile_at)],
+            out_specs=pl.BlockSpec((slots, width), lambda far, kind, w: (0, 0)),
+            scratch_shapes=[pltpu.VMEM((slots, width), F32)],
+        ),
+    )(which, *values, weights)
+
+
+def added(mine, arrived):
+    return (mine.astype(F32) + arrived.astype(F32)).astype(BF16)
+
+
+def piece_body(ahead_rows, behind_rows, behind_grad, route_scores, route_counts, gate_up, down_proj):
+    height = ahead_rows.shape[1]
+    gates = gate_up[0, 0]
+    downs = down_proj[0, 0]
+    own = lax.axis_index("expert")
+    block, group = own // 2, own % 2
+    near = (block >= DBLOCKS // 2).astype(jnp.int32)
+    at_end = ((block == 0) | (block == DBLOCKS - 1)).astype(jnp.int32)
+    near_which = jnp.stack([near, group, at_end])
+    far_which = jnp.stack([1 - near, group, at_end])
+
+    def over_blocks(value, pairs):
+        full = [(a * 2 + f, b * 2 + f) for a, b in pairs for f in range(2)]
+        return lax.ppermute(value, "expert", full)
+
+    def inward(value):
+        return over_blocks(value, [(0, 1), (3, 2)])
+
+    def across(value):
+        return over_blocks(value, [(1, 2), (2, 1)])
+
+    def outward(value):
+        return over_blocks(value, [(1, 0), (2, 3)])
+
+    def partner(value):
+        return lax.ppermute(value, "expert", [(i, i ^ 1) for i in range(2 * DBLOCKS)])
+
+    slot_ids = jnp.arange(height, dtype=jnp.int32)[None]
+    live = slot_ids < route_counts[0][:, None]
+    scales = jnp.where(live, route_scores[0], 0.0)[:, :, None]
+
+    def piece(kind, start, size):
+        def cut(array):
+            return array[0, start : start + size]
+
+        scale = scales[kind, start : start + size]
+        if kind == 0:
+            rows = cut(ahead_rows)
+            rows, grads = (rows, partner(rows)), None
+        else:
+            rows, grads = cut(behind_rows), cut(behind_grad)
+            rows, grads = (rows, partner(rows)), (grads, partner(grads))
+        far = first_product(far_which, rows, grads, gates, downs)
+        arrived = inward(far)
+        near = first_product(near_which, rows, grads, gates, downs)
+        arrived = across(added(far, arrived))
+        arrived = outward(added(near, arrived))
+        act = activation(near, arrived, None if kind == 0 else scale)
+        one = inward(act)
+        two = across(one)
+        three = outward(two)
+        weights = downs[None] if kind == 0 else gates
+        values = (act, one, two, three)
+        give = second_product(near_which, 0, values, weights, BF16)
+        given = partner(give)
+        keep = second_product(near_which, 1, values, weights, F32)
+        total = keep + given.astype(F32)
+        if kind == 0:
+            total = total * scale
+        return shift(total.astype(BF16), "section", 1 if kind == 0 else -1)
+
+    size = height // 2
+    order = [(0, 0), (1, 0), (1, 1), (0, 1)]
+    done = {(kind, i): piece(kind, i * size, size) for kind, i in order}
+    return tuple(jnp.concatenate([done[kind, 0], done[kind, 1]])[None] for kind in (0, 1))
 
 
 def body(ahead_rows, behind_rows, behind_grad, route_scores, route_counts, gate_up, down_proj):
@@ -24,8 +261,6 @@
     weights_out = down_proj[0, 0]
     units = weights_in.shape[1]
     part = units // DBLOCKS
-    own = lax.axis_index("expert")
-    block = own // fgroups
 
     def wide(rows):
         return lax.all_gather(rows, "expert", axis_index_groups=low, axis=1, tiled=True)
@@ -88,4 +323,5 @@
         P("section", "expert", None, None),
     )
     out_specs = (P("section", None, "expert"), P("section", None, "expert"))
-    return jax.shard_map(body, mesh=mesh, in_specs=in_specs, out_specs=out_specs, check_vma=False)
+    chosen = piece_body if mesh.shape["expert"] == 2 * DBLOCKS else body
+    return jax.shard_map(chosen, mesh=mesh, in_specs=in_specs, out_specs=out_specs, check_vma=False)

time: 295 us -> 206 us (0.70)
  waiting for transfers between devices: 207 us -> 45.9 us
  starting transfers between devices: 6.73 us -> 92.3 us
  Pallas kernels: 0 us -> 50.2 us
  matrix products: 29.6 us -> 0 us
  blocking collectives: 19 us -> 0 us
  between operations: 14.2 us -> 1.42 us
  local copies, waits for them, and re-layouts: 13 us -> 9.02 us
    all_gather x4 -> x0, waiting for transfers between devices: 83.9 us -> none  [the longest x3 65.6 us: wide(): lax.all_gather(rows, 'expert', axis_index_groups=low, axis=1, tiled=True)]
    ppermute x0 -> x34, starting transfers between devices: none -> 74.6 us  [the longest x24 65 us: over_blocks(): return lax.ppermute(value, 'expert', full)]
    reduce_scatter x2 -> x0, waiting for transfers between devices: 73.8 us -> none  [reduced(): lax.psum_scatter(flat, 'expert', axis_index_groups=high, scatter_dimensio...]
    pallas_call x0 -> x20, Pallas kernels: none -> 50.2 us  [the longest x8 29.2 us: first_product(): call(functools.partial(kernel, width), 2 * slots * features * half * part...]
    ppermute x0 -> x34, waiting for transfers between devices: none -> 41 us  [the longest x24 26.6 us: over_blocks(): return lax.ppermute(value, 'expert', full)]
    unnamed x10 -> x0, waiting for transfers between devices: 39.5 us -> none
    dot_general x5 -> x0, matrix products: 29.6 us -> none  [the longest x1 7.43 us: body(): jnp.einsum('cd,kqfd->qkcf', behind_wide, gates, preferred_element_type=F32)]
    all_gather x1 -> x0, blocking collectives: 19 us -> none  [spread(): lax.all_gather(values, 'expert', axis_index_groups=high, axis=0, tiled=Fa...]
  transfers between devices with their start and end apart: 10 -> 38, of which waited for: 9 -> 12; matrix products, arithmetic and copies ran while one was open for 15% -> 3% of each run, Pallas kernels for 0% -> 25%
where the time goes in v2:
time: 206 us; the launch traced here: 205 us
  starting transfers between devices  92.3 us (45%)
  Pallas kernels  50.2 us (24%)
  waiting for transfers between devices  45.9 us (22%)
  local copies, waits for them, and re-layouts  9.02 us (4%)
  other arithmetic  5.8 us (3%)
    ppermute x24, starting transfers between devices, over_blocks(): return lax.ppermute(value, 'expert', full)  65 us
    pallas_call x8, Pallas kernels, first_product(): call(functools.partial(kernel, width), 2 * slots * features * half * part...  29.2 us
    ppermute x24, waiting for transfers between devices, over_blocks(): return lax.ppermute(value, 'expert', full)  26.6 us
    pallas_call x8, Pallas kernels, second_product(): call(functools.partial(second_kernel, kinds), 4 * slots * half * width *...  18.1 us
    ppermute x4, starting transfers between devices, shift(): return lax.ppermute(shard, axis, pairs)  17.8 us
    ppermute x10, waiting for transfers between devices, partner(): lax.ppermute(value, 'expert', [(i, i ^ 1) for i in range(2 * DBLOCKS)])  14.5 us
    ppermute x10, starting transfers between devices, partner(): lax.ppermute(value, 'expert', [(i, i ^ 1) for i in range(2 * DBLOCKS)])  9.54 us
    unnamed x34, local copies, waits for them, and re-layouts  7.35 us
  transfers between devices with their start and end apart: 38, of which 12 were waited for; matrix products, arithmetic and copies ran while one was open for 3% of the time, Pallas kernels for 25%

profile of v2, /device:TPU:1, one launch (start us, length us, event | category | flops | bytes accessed | tf_op | source)
XLA Modules:
  0.0 204.7 jit_solution(14174518296057410882)
XLA Ops:
  7.4 4.4 %collective-permute-done.18.partner = bf16[192,896]{1,0:T(8,128)(2,1)S(1)} collective-permute-done((bf16[192,896]{1,0:T(8,128)(2,1)S(1)}, bf16[192,896]{1,0:T(8,128)(2,1)S(1)}, u32[]{:S(2)}, u32[]{:S(2)}) %collective-permute-start.18) | collective-permute-done | bytes 344096 | tf_op jit(solution)/shard_map/ppermute | solution.py:212
  13.1 6.2 %collective-permute-done.19.grad_partner = bf16[192,896]{1,0:T(8,128)(2,1)S(1)} collective-permute-done((bf16[192,896]{1,0:T(8,128)(2,1)S(1)}, bf16[192,896]{1,0:T(8,128)(2,1)S(1)}, u32[]{:S(2)}, u32[]{:S(2)}) %collective-permute-start.19) | collective-permute-done | bytes 344096 | tf_op jit(solution)/shard_map/ppermute | solution.py:212
  19.2 3.2 %copy-done = bf16[1,1,2,1024,1792]{4,3,2,1,0:T(8,128)(2,1)S(1)} copy-done((bf16[1,1,2,1024,1792]{4,3,2,1,0:T(8,128)(2,1)S(1)}, bf16[1,1,2,1024,1792]{4,3,2,1,0:T(8,128)(2,1)}, u32[]{:S(2)}) %copy-start) | copy-done | bytes 7340056
  24.5 3.7 %shard_map.97 = bf16[3,192,512]{2,1,0:T(8,128)(2,1)S(1)} custom-call(s32[3]{0:T(128)S(1)} %add_add_fusion.1.which, bf16[192,896]{1,0:T(8,128)(2,1)S(1)} %get-tuple-element.4.own, bf16[192,896]{1,0:T(8,128)(2,1)S(1)} %collective-permute-done.18.partner, bf16[192,896]{1,0:T(8,128)(2,1)S(1)} %get-tuple-element.2.grad_own, ...), custom_call_target="tpu_custom_call" | custom-call | flops 1056964608 | bytes 7471104 | tf_op jit(solution)/shard_map/pallas_call | solution.py:90
  28.2 3.4 %collective-permute-start.20 = (bf16[3,192,512]{2,1,0:T(8,128)(2,1)S(1)}, bf16[3,192,512]{2,1,0:T(8,128)(2,1)S(1)}, u32[]{:S(2)}, u32[]{:S(2)}) collective-permute-start(bf16[3,192,512]{2,1,0:T(8,128)(2,1)S(1)} %shard_map.97), channel_id=1, source_target_pairs={{0,2},{1,3},{6,4},{7,5},{8,10},{9,11},{14,12},{15,13},{16,18},{17,... | collective-permute-start | bytes 1769480 | tf_op jit(solution)/shard_map/ppermute | solution.py:200
  34.1 4.7 %shard_map.102 = bf16[3,192,512]{2,1,0:T(8,128)(2,1)S(1)} custom-call(s32[3]{0:T(128)S(1)} %add_add_fusion.1.which, bf16[192,896]{1,0:T(8,128)(2,1)S(1)} %get-tuple-element.5.own, bf16[192,896]{1,0:T(8,128)(2,1)S(1)} %collective-permute-done.28.partner, bf16[192,896]{1,0:T(8,128)(2,1)S(1)} %get-tuple-element.3.grad_own, ...), custom_call_target="tpu_custom_call" | custom-call | flops 1056964608 | bytes 7471104 | tf_op jit(solution)/shard_map/pallas_call | solution.py:90
  38.8 3.1 %collective-permute-start.30 = (bf16[3,192,512]{2,1,0:T(8,128)(2,1)S(1)}, bf16[3,192,512]{2,1,0:T(8,128)(2,1)S(1)}, u32[]{:S(2)}, u32[]{:S(2)}) collective-permute-start(bf16[3,192,512]{2,1,0:T(8,128)(2,1)S(1)} %shard_map.102), channel_id=1, source_target_pairs={{0,2},{1,3},{6,4},{7,5},{8,10},{9,11},{14,12},{15,13},{16,18},{17,... | collective-permute-start | bytes 1769480 | tf_op jit(solution)/shard_map/ppermute | solution.py:200
  41.9 3.6 %shard_map.87 = bf16[2,192,512]{2,1,0:T(8,128)(2,1)S(1)} custom-call(s32[3]{0:T(128)S(1)} %add_add_fusion.1.which, bf16[192,896]{1,0:T(8,128)(2,1)S(1)} %get-tuple-element.6.own, bf16[192,896]{1,0:T(8,128)(2,1)} %collective-permute-done.partner, bf16[2,1024,1792]{2,1,0:T(8,128)(2,1)S(1)} %bitcast.34), custom_call_target="tpu_custom_call" | custom-call | flops 704643072 | bytes 4751360 | tf_op jit(solution)/shard_map/pallas_call | solution.py:90
  45.5 2.8 %collective-permute-start.1 = (bf16[2,192,512]{2,1,0:T(8,128)(2,1)S(1)}, bf16[2,192,512]{2,1,0:T(8,128)(2,1)S(1)}, u32[]{:S(2)}, u32[]{:S(2)}) collective-permute-start(bf16[2,192,512]{2,1,0:T(8,128)(2,1)S(1)} %shard_map.87), channel_id=1, source_target_pairs={{0,2},{1,3},{6,4},{7,5},{8,10},{9,11},{14,12},{15,13},{16,18},{17,... | collective-permute-start | bytes 1179656 | tf_op jit(solution)/shard_map/ppermute | solution.py:200
  51.4 3.3 %collective-permute-start.10 = (bf16[2,192,512]{2,1,0:T(8,128)(2,1)S(1)}, bf16[2,192,512]{2,1,0:T(8,128)(2,1)S(1)}, u32[]{:S(2)}, u32[]{:S(2)}) collective-permute-start(bf16[2,192,512]{2,1,0:T(8,128)(2,1)S(1)} %shard_map.92), channel_id=1, source_target_pairs={{0,2},{1,3},{6,4},{7,5},{8,10},{9,11},{14,12},{15,13},{16,18},{17,... | collective-permute-start | bytes 1179656 | tf_op jit(solution)/shard_map/ppermute | solution.py:200
  54.6 3.7 %shard_map.96.near = bf16[3,192,512]{2,1,0:T(8,128)(2,1)S(1)} custom-call(s32[3]{0:T(128)S(1)} %add_add_fusion.which, bf16[192,896]{1,0:T(8,128)(2,1)S(1)} %get-tuple-element.4.own, bf16[192,896]{1,0:T(8,128)(2,1)S(1)} %collective-permute-done.18.partner, bf16[192,896]{1,0:T(8,128)(2,1)S(1)} %get-tuple-element.2.grad_own, bf16[192,896]{1,0:T(8,128)(2,1)S(1)} %copy-done.6, ...), custom_call_target="tpu_custom_call" | custom-call | flops 1056964608 | bytes 7471104 | tf_op jit(solution)/shard_map/pallas_call | solution.py:90
  58.4 4.7 %shard_map.101.near = bf16[3,192,512]{2,1,0:T(8,128)(2,1)S(1)} custom-call(s32[3]{0:T(128)S(1)} %add_add_fusion.which, bf16[192,896]{1,0:T(8,128)(2,1)S(1)} %get-tuple-element.5.own, bf16[192,896]{1,0:T(8,128)(2,1)S(1)} %copy-done.8, bf16[192,896]{1,0:T(8,128)(2,1)S(1)} %get-tuple-element.3.grad_own, bf16[192,896]{1,0:T(8,128)(2,1)} %collective-permute-done.29.grad_partner, ...), custom_call_target="tpu_custom_call" | custom-call | flops 1056964608 | bytes 7471104 | tf_op jit(solution)/shard_map/pallas_call | solution.py:90
  63.1 3.6 %shard_map.86.near = bf16[2,192,512]{2,1,0:T(8,128)(2,1)S(1)} custom-call(s32[3]{0:T(128)S(1)} %add_add_fusion.which, bf16[192,896]{1,0:T(8,128)(2,1)S(1)} %get-tuple-element.6.own, bf16[192,896]{1,0:T(8,128)(2,1)} %collective-permute-done.partner, bf16[2,1024,1792]{2,1,0:T(8,128)(2,1)S(1)} %bitcast.40), custom_call_target="tpu_custom_call" | custom-call | flops 704643072 | bytes 4751360 | tf_op jit(solution)/shard_map/pallas_call | solution.py:90
  80.9 5.6 %collective-permute-done.3.arrived = bf16[2,192,512]{2,1,0:T(8,128)(2,1)S(1)} collective-permute-done((bf16[2,192,512]{2,1,0:T(8,128)(2,1)S(1)}, bf16[2,192,512]{2,1,0:T(8,128)(2,1)S(1)}, u32[]{:S(2)}, u32[]{:S(2)}) %collective-permute-start.3) | collective-permute-done | bytes 393248 | tf_op jit(solution)/shard_map/ppermute | solution.py:200
  86.6 31.5 %collective-permute-start.4 = (bf16[1,192,512]{2,1,0:T(8,128)(2,1)S(1)}, bf16[1,192,512]{2,1,0:T(8,128)(2,1)S(1)}, u32[]{:S(2)}, u32[]{:S(2)}) collective-permute-start(bf16[1,192,512]{2,1,0:T(8,128)(2,1)S(1)} %shard_map.88.own), channel_id=1, source_target_pairs={{0,2},{1,3},{6,4},{7,5},{8,10},{9,11},{14,12},{15,13},{16,18},{17,... | collective-permute-start | bytes 589832 | tf_op jit(solution)/shard_map/ppermute | solution.py:200
  130.9 11.3 %collective-permute-done.13.one = bf16[1,192,512]{2,1,0:T(8,128)(2,1)S(1)} collective-permute-done((bf16[1,192,512]{2,1,0:T(8,128)(2,1)S(1)}, bf16[1,192,512]{2,1,0:T(8,128)(2,1)S(1)}, u32[]{:S(2)}, u32[]{:S(2)}) %collective-permute-start.13) | collective-permute-done | bytes 196640 | tf_op jit(solution)/shard_map/ppermute | solution.py:200
  151.2 7.8 %collective-permute-done.15.three = bf16[1,192,512]{2,1,0:T(8,128)(2,1)S(1)} collective-permute-done((bf16[1,192,512]{2,1,0:T(8,128)(2,1)S(1)}, bf16[1,192,512]{2,1,0:T(8,128)(2,1)S(1)}, u32[]{:S(2)}, u32[]{:S(2)}) %collective-permute-start.15) | collective-permute-done | bytes 196640 | tf_op jit(solution)/shard_map/ppermute | solution.py:200
  165.9 10.2 %collective-permute-start.8 = (bf16[192,896]{1,0:T(8,128)(2,1)S(1)}, bf16[192,896]{1,0:T(8,128)(2,1)S(1)}, u32[]{:S(2)}, u32[]{:S(2)}) collective-permute-start(bf16[192,896]{1,0:T(8,128)(2,1)S(1)} %multiply_convert_fusion.1), channel_id=1, source_target_pairs={{0,8},{8,16},{16,24},{1,9},{9,17},{17,25},{2,10},{10,18},{18,26},{... | collective-permute-start | bytes 1032200 | tf_op jit(solution)/shard_map/ppermute | solution.py:19
  176.1 2.8 %shard_map.100 = bf16[192,896]{1,0:T(8,128)(2,1)S(1)} custom-call(s32[3]{0:T(128)S(1)} %add_add_fusion.which, bf16[2,192,512]{2,1,0:T(8,128)(2,1)S(1)} %shard_map.98.own, bf16[2,192,512]{2,1,0:T(8,128)(2,1)S(1)} %collective-permute-done.23.one, bf16[2,192,512]{2,1,0:T(8,128)(2,1)S(1)} %collective-permute-done.24.two, ...), custom_call_target="tpu_custom_call" | custom-call | flops 704643072 | bytes 5931008 | tf_op jit(solution)/shard_map/pallas_call | solution.py:168
  182.6 2.8 %shard_map.105 = bf16[192,896]{1,0:T(8,128)(2,1)S(1)} custom-call(s32[3]{0:T(128)S(1)} %add_add_fusion.which, bf16[2,192,512]{2,1,0:T(8,128)(2,1)S(1)} %shard_map.103.own, bf16[2,192,512]{2,1,0:T(8,128)(2,1)S(1)} %collective-permute-done.33.one, bf16[2,192,512]{2,1,0:T(8,128)(2,1)S(1)} %collective-permute-done.34.two, ...), custom_call_target="tpu_custom_call" | custom-call | flops 704643072 | bytes 5931008 | tf_op jit(solution)/shard_map/pallas_call | solution.py:168
  185.7 2.8 %shard_map.99 = f32[192,896]{1,0:T(8,128)S(1)} custom-call(s32[3]{0:T(128)S(1)} %add_add_fusion.which, bf16[2,192,512]{2,1,0:T(8,128)(2,1)S(1)} %shard_map.98.own, bf16[2,192,512]{2,1,0:T(8,128)(2,1)S(1)} %collective-permute-done.23.one, bf16[2,192,512]{2,1,0:T(8,128)(2,1)S(1)} %collective-permute-done.24.two, ...), custom_call_target="tpu_custom_call" | custom-call | flops 704643072 | bytes 5931008 | tf_op jit(solution)/shard_map/pallas_call | solution.py:168
  188.6 2.9 %shard_map.104 = f32[192,896]{1,0:T(8,128)S(1)} custom-call(s32[3]{0:T(128)S(1)} %add_add_fusion.which, bf16[2,192,512]{2,1,0:T(8,128)(2,1)S(1)} %shard_map.103.own, bf16[2,192,512]{2,1,0:T(8,128)(2,1)S(1)} %collective-permute-done.33.one, bf16[2,192,512]{2,1,0:T(8,128)(2,1)S(1)} %collective-permute-done.34.two, ...), custom_call_target="tpu_custom_call" | custom-call | flops 704643072 | bytes 5931008 | tf_op jit(solution)/shard_map/pallas_call | solution.py:168
  195.0 3.0 %collective-permute-start.37 = (bf16[192,896]{1,0:T(8,128)(2,1)S(1)}, bf16[192,896]{1,0:T(8,128)(2,1)S(1)}, u32[]{:S(2)}, u32[]{:S(2)}) collective-permute-start(bf16[192,896]{1,0:T(8,128)(2,1)S(1)} %add_convert_fusion.8), channel_id=1, source_target_pairs={{8,0},{16,8},{24,16},{9,1},{17,9},{25,17},{10,2},{18,10},{26,18},{... | collective-permute-start | bytes 1032200 | tf_op jit(solution)/shard_map/ppermute | solution.py:19
  200.1 3.7 %collective-permute-done.37 = bf16[192,896]{1,0:T(8,128)(2,1)S(1)} collective-permute-done((bf16[192,896]{1,0:T(8,128)(2,1)S(1)}, bf16[192,896]{1,0:T(8,128)(2,1)S(1)}, u32[]{:S(2)}, u32[]{:S(2)}) %collective-permute-start.37) | collective-permute-done | bytes 344096 | tf_op jit(solution)/shard_map/ppermute | solution.py:19
  (131 shorter events, 68.5 us)
Async XLA Ops:
  4.1 15.1 %collective-permute-start.19 = (bf16[192,896]{1,0:T(8,128)(2,1)S(1)}, bf16[192,896]{1,0:T(8,128)(2,1)S(1)}, u32[]{:S(2)}, u32[]{:S(2)}) collective-permute-start(bf16[192,896]{1,0:T(8,128)(2,1)S(1)} %get-tuple-element.2.grad_own), channel_id=1, source_target_pairs={{0,1},{1,0},{2,3},{3,2},{4,5},{5,4},{6,7},{7,6},{8,9},{9,8},{10,11... | collective-permute-start | bytes 1032200 | tf_op jit(solution)/shard_map/ppermute | solution.py:212
  4.2 27.4 %collective-permute-start.28 = (bf16[192,896]{1,0:T(8,128)(2,1)S(1)}, bf16[192,896]{1,0:T(8,128)(2,1)S(1)}, u32[]{:S(2)}, u32[]{:S(2)}) collective-permute-start(bf16[192,896]{1,0:T(8,128)(2,1)S(1)} %get-tuple-element.5.own), channel_id=1, source_target_pairs={{0,1},{1,0},{2,3},{3,2},{4,5},{5,4},{6,7},{7,6},{8,9},{9,8},{10,11... | collective-permute-start | bytes 1032200 | tf_op jit(solution)/shard_map/ppermute | solution.py:212
  5.7 28.4 %collective-permute-start.29 = (bf16[192,896]{1,0:T(8,128)(2,1)S(1)}, bf16[192,896]{1,0:T(8,128)(2,1)}, u32[]{:S(2)}, u32[]{:S(2)}) collective-permute-start(bf16[192,896]{1,0:T(8,128)(2,1)S(1)} %get-tuple-element.3.grad_own), channel_id=1, source_target_pairs={{0,1},{1,0},{2,3},{3,2},{4,5},{5,4},{6,7},{7,6},{8,9},{9,8},{10,11... | collective-permute-start | bytes 1032200 | tf_op jit(solution)/shard_map/ppermute | solution.py:212
  5.8 36.1 %collective-permute-start = (bf16[192,896]{1,0:T(8,128)(2,1)S(1)}, bf16[192,896]{1,0:T(8,128)(2,1)}, u32[]{:S(2)}, u32[]{:S(2)}) collective-permute-start(bf16[192,896]{1,0:T(8,128)(2,1)S(1)} %get-tuple-element.6.own), channel_id=1, source_target_pairs={{0,1},{1,0},{2,3},{3,2},{4,5},{5,4},{6,7},{7,6},{8,9},{9,8},{10,11... | collective-permute-start | bytes 1032200 | tf_op jit(solution)/shard_map/ppermute | solution.py:212
  11.8 36.9 %collective-permute-start.9 = (bf16[192,896]{1,0:T(8,128)(2,1)S(1)}, bf16[192,896]{1,0:T(8,128)(2,1)S(1)}, u32[]{:S(2)}, u32[]{:S(2)}) collective-permute-start(bf16[192,896]{1,0:T(8,128)(2,1)S(1)} %get-tuple-element.7.own), channel_id=1, source_target_pairs={{0,1},{1,0},{2,3},{3,2},{4,5},{5,4},{6,7},{7,6},{8,9},{9,8},{10,11... | collective-permute-start | bytes 1032200 | tf_op jit(solution)/shard_map/ppermute | solution.py:212
  28.2 41.9 %collective-permute-start.20 = (bf16[3,192,512]{2,1,0:T(8,128)(2,1)S(1)}, bf16[3,192,512]{2,1,0:T(8,128)(2,1)S(1)}, u32[]{:S(2)}, u32[]{:S(2)}) collective-permute-start(bf16[3,192,512]{2,1,0:T(8,128)(2,1)S(1)} %shard_map.97), channel_id=1, source_target_pairs={{0,2},{1,3},{6,4},{7,5},{8,10},{9,11},{14,12},{15,13},{16,18},{17,... | collective-permute-start | bytes 1769480 | tf_op jit(solution)/shard_map/ppermute | solution.py:200
  38.8 32.2 %collective-permute-start.30 = (bf16[3,192,512]{2,1,0:T(8,128)(2,1)S(1)}, bf16[3,192,512]{2,1,0:T(8,128)(2,1)S(1)}, u32[]{:S(2)}, u32[]{:S(2)}) collective-permute-start(bf16[3,192,512]{2,1,0:T(8,128)(2,1)S(1)} %shard_map.102), channel_id=1, source_target_pairs={{0,2},{1,3},{6,4},{7,5},{8,10},{9,11},{14,12},{15,13},{16,18},{17,... | collective-permute-start | bytes 1769480 | tf_op jit(solution)/shard_map/ppermute | solution.py:200
  45.5 23.8 %collective-permute-start.1 = (bf16[2,192,512]{2,1,0:T(8,128)(2,1)S(1)}, bf16[2,192,512]{2,1,0:T(8,128)(2,1)S(1)}, u32[]{:S(2)}, u32[]{:S(2)}) collective-permute-start(bf16[2,192,512]{2,1,0:T(8,128)(2,1)S(1)} %shard_map.87), channel_id=1, source_target_pairs={{0,2},{1,3},{6,4},{7,5},{8,10},{9,11},{14,12},{15,13},{16,18},{17,... | collective-permute-start | bytes 1179656 | tf_op jit(solution)/shard_map/ppermute | solution.py:200
  51.4 20.6 %collective-permute-start.10 = (bf16[2,192,512]{2,1,0:T(8,128)(2,1)S(1)}, bf16[2,192,512]{2,1,0:T(8,128)(2,1)S(1)}, u32[]{:S(2)}, u32[]{:S(2)}) collective-permute-start(bf16[2,192,512]{2,1,0:T(8,128)(2,1)S(1)} %shard_map.92), channel_id=1, source_target_pairs={{0,2},{1,3},{6,4},{7,5},{8,10},{9,11},{14,12},{15,13},{16,18},{17,... | collective-permute-start | bytes 1179656 | tf_op jit(solution)/shard_map/ppermute | solution.py:200
  75.1 43.1 %collective-permute-start.22 = (bf16[3,192,512]{2,1,0:T(8,128)(2,1)}, bf16[3,192,512]{2,1,0:T(8,128)(2,1)}, u32[]{:S(2)}, u32[]{:S(2)}) collective-permute-start(bf16[3,192,512]{2,1,0:T(8,128)(2,1)} %add_convert_fusion.2), channel_id=1, source_target_pairs={{2,0},{3,1},{4,6},{5,7},{10,8},{11,9},{12,14},{13,15},{18,16},{19,... | collective-permute-start | bytes 1769480 | tf_op jit(solution)/shard_map/ppermute | solution.py:200
  77.4 43.7 %collective-permute-start.32 = (bf16[3,192,512]{2,1,0:T(8,128)(2,1)}, bf16[3,192,512]{2,1,0:T(8,128)(2,1)S(1)}, u32[]{:S(2)}, u32[]{:S(2)}) collective-permute-start(bf16[3,192,512]{2,1,0:T(8,128)(2,1)} %add_convert_fusion), channel_id=1, source_target_pairs={{2,0},{3,1},{4,6},{5,7},{10,8},{11,9},{12,14},{13,15},{18,16},{19,... | collective-permute-start | bytes 1769480 | tf_op jit(solution)/shard_map/ppermute | solution.py:200
  79.6 45.6 %collective-permute-start.12 = (bf16[2,192,512]{2,1,0:T(8,128)(2,1)}, bf16[2,192,512]{2,1,0:T(8,128)(2,1)}, u32[]{:S(2)}, u32[]{:S(2)}) collective-permute-start(bf16[2,192,512]{2,1,0:T(8,128)(2,1)} %add_convert_fusion.4), channel_id=1, source_target_pairs={{2,0},{3,1},{4,6},{5,7},{10,8},{11,9},{12,14},{13,15},{18,16},{19,... | collective-permute-start | bytes 1179656 | tf_op jit(solution)/shard_map/ppermute | solution.py:200
  86.6 36.2 %collective-permute-start.4 = (bf16[1,192,512]{2,1,0:T(8,128)(2,1)S(1)}, bf16[1,192,512]{2,1,0:T(8,128)(2,1)S(1)}, u32[]{:S(2)}, u32[]{:S(2)}) collective-permute-start(bf16[1,192,512]{2,1,0:T(8,128)(2,1)S(1)} %shard_map.88.own), channel_id=1, source_target_pairs={{0,2},{1,3},{6,4},{7,5},{8,10},{9,11},{14,12},{15,13},{16,18},{17,... | collective-permute-start | bytes 589832 | tf_op jit(solution)/shard_map/ppermute | solution.py:200
  121.4 21.4 %collective-permute-start.33 = (bf16[2,192,512]{2,1,0:T(8,128)(2,1)S(1)}, bf16[2,192,512]{2,1,0:T(8,128)(2,1)S(1)}, u32[]{:S(2)}, u32[]{:S(2)}) collective-permute-start(bf16[2,192,512]{2,1,0:T(8,128)(2,1)S(1)} %shard_map.103.own), channel_id=1, source_target_pairs={{0,2},{1,3},{6,4},{7,5},{8,10},{9,11},{14,12},{15,13},{16,18},{17,... | collective-permute-start | bytes 1179656 | tf_op jit(solution)/shard_map/ppermute | solution.py:200
  126.3 15.9 %collective-permute-start.13 = (bf16[1,192,512]{2,1,0:T(8,128)(2,1)S(1)}, bf16[1,192,512]{2,1,0:T(8,128)(2,1)S(1)}, u32[]{:S(2)}, u32[]{:S(2)}) collective-permute-start(bf16[1,192,512]{2,1,0:T(8,128)(2,1)S(1)} %shard_map.93.own), channel_id=1, source_target_pairs={{0,2},{1,3},{6,4},{7,5},{8,10},{9,11},{14,12},{15,13},{16,18},{17,... | collective-permute-start | bytes 589832 | tf_op jit(solution)/shard_map/ppermute | solution.py:200
  128.9 14.7 %collective-permute-start.6 = (bf16[1,192,512]{2,1,0:T(8,128)(2,1)S(1)}, bf16[1,192,512]{2,1,0:T(8,128)(2,1)S(1)}, u32[]{:S(2)}, u32[]{:S(2)}) collective-permute-start(bf16[1,192,512]{2,1,0:T(8,128)(2,1)S(1)} %collective-permute-done.5.two), channel_id=1, source_target_pairs={{2,0},{3,1},{4,6},{5,7},{10,8},{11,9},{12,14},{13,15},{18,16},{19,... | collective-permute-start | bytes 589832 | tf_op jit(solution)/shard_map/ppermute | solution.py:200
  130.2 19.7 %collective-permute-start.24 = (bf16[2,192,512]{2,1,0:T(8,128)(2,1)S(1)}, bf16[2,192,512]{2,1,0:T(8,128)(2,1)S(1)}, u32[]{:S(2)}, u32[]{:S(2)}) collective-permute-start(bf16[2,192,512]{2,1,0:T(8,128)(2,1)S(1)} %collective-permute-done.23.one), channel_id=1, source_target_pairs={{2,4},{3,5},{4,2},{5,3},{10,12},{11,13},{12,10},{13,11},{18,20},{1... | collective-permute-start | bytes 1179656 | tf_op jit(solution)/shard_map/ppermute | solution.py:200
  142.8 21.6 %collective-permute-start.34 = (bf16[2,192,512]{2,1,0:T(8,128)(2,1)S(1)}, bf16[2,192,512]{2,1,0:T(8,128)(2,1)S(1)}, u32[]{:S(2)}, u32[]{:S(2)}) collective-permute-start(bf16[2,192,512]{2,1,0:T(8,128)(2,1)S(1)} %collective-permute-done.33.one), channel_id=1, source_target_pairs={{2,4},{3,5},{4,2},{5,3},{10,12},{11,13},{12,10},{13,11},{18,20},{1... | collective-permute-start | bytes 1179656 | tf_op jit(solution)/shard_map/ppermute | solution.py:200
  147.3 18.5 %collective-permute-start.7 = (bf16[192,896]{1,0:T(8,128)(2,1)S(1)}, bf16[192,896]{1,0:T(8,128)(2,1)S(1)}, u32[]{:S(2)}, u32[]{:S(2)}) collective-permute-start(bf16[192,896]{1,0:T(8,128)(2,1)S(1)} %shard_map.90), channel_id=1, source_target_pairs={{0,1},{1,0},{2,3},{3,2},{4,5},{5,4},{6,7},{7,6},{8,9},{9,8},{10,11... | collective-permute-start | bytes 1032200 | tf_op jit(solution)/shard_map/ppermute | solution.py:212
  149.9 26.2 %collective-permute-start.25 = (bf16[2,192,512]{2,1,0:T(8,128)(2,1)S(1)}, bf16[2,192,512]{2,1,0:T(8,128)(2,1)S(1)}, u32[]{:S(2)}, u32[]{:S(2)}) collective-permute-start(bf16[2,192,512]{2,1,0:T(8,128)(2,1)S(1)} %collective-permute-done.24.two), channel_id=1, source_target_pairs={{2,0},{3,1},{4,6},{5,7},{10,8},{11,9},{12,14},{13,15},{18,16},{19,... | collective-permute-start | bytes 1179656 | tf_op jit(solution)/shard_map/ppermute | solution.py:200
  160.8 19.4 %collective-permute-start.16 = (bf16[192,896]{1,0:T(8,128)(2,1)S(1)}, bf16[192,896]{1,0:T(8,128)(2,1)S(1)}, u32[]{:S(2)}, u32[]{:S(2)}) collective-permute-start(bf16[192,896]{1,0:T(8,128)(2,1)S(1)} %shard_map.95), channel_id=1, source_target_pairs={{0,1},{1,0},{2,3},{3,2},{4,5},{5,4},{6,7},{7,6},{8,9},{9,8},{10,11... | collective-permute-start | bytes 1032200 | tf_op jit(solution)/shard_map/ppermute | solution.py:212
  164.5 18.1 %collective-permute-start.35 = (bf16[2,192,512]{2,1,0:T(8,128)(2,1)S(1)}, bf16[2,192,512]{2,1,0:T(8,128)(2,1)S(1)}, u32[]{:S(2)}, u32[]{:S(2)}) collective-permute-start(bf16[2,192,512]{2,1,0:T(8,128)(2,1)S(1)} %collective-permute-done.34.two), channel_id=1, source_target_pairs={{2,0},{3,1},{4,6},{5,7},{10,8},{11,9},{12,14},{13,15},{18,16},{19,... | collective-permute-start | bytes 1179656 | tf_op jit(solution)/shard_map/ppermute | solution.py:200
  165.9 32.1 %collective-permute-start.8 = (bf16[192,896]{1,0:T(8,128)(2,1)S(1)}, bf16[192,896]{1,0:T(8,128)(2,1)S(1)}, u32[]{:S(2)}, u32[]{:S(2)}) collective-permute-start(bf16[192,896]{1,0:T(8,128)(2,1)S(1)} %multiply_convert_fusion.1), channel_id=1, source_target_pairs={{0,8},{8,16},{16,24},{1,9},{9,17},{17,25},{2,10},{10,18},{18,26},{... | collective-permute-start | bytes 1032200 | tf_op jit(solution)/shard_map/ppermute | solution.py:19
  180.4 17.6 %collective-permute-start.17 = (bf16[192,896]{1,0:T(8,128)(2,1)S(1)}, bf16[192,896]{1,0:T(8,128)(2,1)S(1)}, u32[]{:S(2)}, u32[]{:S(2)}) collective-permute-start(bf16[192,896]{1,0:T(8,128)(2,1)S(1)} %multiply_convert_fusion), channel_id=1, source_target_pairs={{0,8},{8,16},{16,24},{1,9},{9,17},{17,25},{2,10},{10,18},{18,26},{... | collective-permute-start | bytes 1032200 | tf_op jit(solution)/shard_map/ppermute | solution.py:19
  (31 other events, 270.7 us)

commit v3 on v1

--- a/solution.py
+++ b/solution.py
@@ -1,17 +1,296 @@
+import functools
+
 import jax
 import jax.numpy as jnp
 from jax import lax
+from jax.experimental import pallas as pl
+from jax.experimental.pallas import tpu as pltpu
 from jax.sharding import PartitionSpec as P
 
 DBLOCKS = 4
 BF16 = jnp.bfloat16
 F32 = jnp.float32
+VMEM_LIMIT = 40 * 1024 * 1024
+
+ROW_PIECES = {"F": 1, "B": 1}
+UNIT_PIECES = {"F": 2, "B": 2}
+ORDER = (
+    "YX0", "YG0", "YF0", "B00g.mf", "B01g.mf", "B01g.P1", "B00g.P1", "B00g.mn", "B01g.mn",
+    "B01g.a1", "B01g.P2", "B01e.mf", "B00e.mn", "B01e.mn", "B01e.P1", "B00e.mf", "B00e.P1",
+    "B00g.a1", "B00g.P2", "B01g.a2", "B01g.P3", "B01e.a1", "B01e.P2", "F00.mf", "F00.P1", "F00.mn",
+    "B00g.a2", "B00g.P3", "B00e.a1", "B00e.P2", "B01e.a2", "F01.mf", "F01.P1", "B01e.P3", "F00.a1",
+    "F00.P2", "B00e.a2", "B00e.P3", "F01.mn", "B01.act", "B01.Q1", "F01.a1", "F01.P2", "F00.a2",
+    "F00.P3", "B00.act", "B00.Q1", "B01.Q2", "F01.a2", "F01.P3", "F00.act", "F00.Q1", "B00.Q2",
+    "B01.Q3", "F00.Q2", "F01.act", "F01.Q1", "B00.Q3", "F01.Q2", "F00.Q3", "F01.Q3", "OB00.ms",
+    "OB00.Y", "OB00.mk", "OB00.X", "OF00.mk", "OF00.X", "OF00.ms", "OF00.Y", "OB00.add",
+    "OF00.add",
+)
 
 
 def shift(shard, axis, by):
     devices = lax.axis_size(axis)
     pairs = [(i, i + by) for i in range(devices) if 0 <= i + by < devices]
     return lax.ppermute(shard, axis, pairs)
+
+
+ANY = pl.BlockSpec(memory_space=pl.ANY)
+
+
+def call(kernel, micros, operands, after, out_shape, scalars=(), grid=(), in_specs=None, out_specs=None, scratch=()):
+    count, unread = len(scalars) + len(operands), len(after)
+
+    def run(*refs):
+        kernel(*refs[:count], *refs[count + unread :])
+
+    if in_specs is None:
+        in_specs = [pl.BlockSpec(o.shape, functools.partial(lambda n, *_: (0,) * n, o.ndim)) for o in operands]
+    if out_specs is None:
+        out_specs = pl.BlockSpec(out_shape.shape, functools.partial(lambda n, *_: (0,) * n, len(out_shape.shape)))
+    return pl.pallas_call(
+        run,
+        compiler_params=pltpu.CompilerParams(vmem_limit_bytes=VMEM_LIMIT),
+        cost_estimate=pl.CostEstimate(flops=int(micros * 1.1e9), bytes_accessed=1024, transcendentals=0),
+        out_shape=out_shape,
+        grid_spec=pltpu.PrefetchScalarGridSpec(
+            num_scalar_prefetch=len(scalars),
+            grid=grid or (1,),
+            in_specs=[*in_specs, *[ANY] * unread],
+            out_specs=out_specs,
+            scratch_shapes=list(scratch),
+        ),
+    )(*scalars, *operands, *after)
+
+
+def first_kernel(width, which, own, partner, tile, out, joined):
+    @pl.when((pl.program_id(0) == 0) & (pl.program_id(1) == 0))
+    def _():
+        at = pl.multiple_of(which[1] * width, 128)
+        other = pl.multiple_of((1 - which[1]) * width, 128)
+        joined[:, pl.ds(at, width)] = own[...]
+        joined[:, pl.ds(other, width)] = partner[...]
+
+    out[0] = lax.dot_general(
+        joined[...], tile[0], (((1,), (1,)), ((), ())), preferred_element_type=F32
+    ).astype(BF16)
+
+
+def first_product(which, rows, weights, piece, pieces, after):
+    slots, width = rows[0].shape
+    kinds, units, features = weights.shape
+    half = units // 2
+    size = half // pieces
+    tile = min(256, size)
+    steps = size // tile
+
+    def tile_at(k, j, w):
+        return (k, (w[0] * pieces + piece) * steps + j, 0)
+
+    return call(
+        functools.partial(first_kernel, width),
+        0.5 + 2.1 * kinds / 2 / pieces,
+        (*rows, weights),
+        after,
+        jax.ShapeDtypeStruct((kinds, slots, size), BF16),
+        scalars=(which,),
+        grid=(kinds, steps),
+        in_specs=[pl.BlockSpec((slots, width), lambda k, j, w: (0, 0))] * 2
+        + [pl.BlockSpec((1, tile, features), tile_at)],
+        out_specs=pl.BlockSpec((1, slots, tile), lambda k, j, w: (k, 0, j)),
+        scratch=[pltpu.VMEM((slots, features), BF16)],
+    )
+
+
+def add_kernel(mine, arrived, out):
+    out[...] = (mine[...].astype(F32) + arrived[...].astype(F32)).astype(BF16)
+
+
+def added(mine, arrived, after):
+    return call(add_kernel, 0.4, (mine, arrived), after, jax.ShapeDtypeStruct(mine.shape, BF16))
+
+
+def ahead_act_kernel(near, arrived, out):
+    gate = near[0].astype(F32) + arrived[0].astype(F32)
+    up = near[1].astype(F32) + arrived[1].astype(F32)
+    out[0] = (gate * jax.nn.sigmoid(gate) * up).astype(BF16)
+
+
+def behind_act_kernel(near, arrived, near_e, arrived_e, scale, out):
+    gate = near[0].astype(F32) + arrived[0].astype(F32)
+    up = near[1].astype(F32) + arrived[1].astype(F32)
+    expanded = (near_e[0].astype(F32) + arrived_e[0].astype(F32)) * scale[...]
+    sig = jax.nn.sigmoid(gate)
+    out[0] = (expanded * up * sig * (1.0 + gate * (1.0 - sig))).astype(BF16)
+    out[1] = (expanded * gate * sig).astype(BF16)
+
+
+def second_kernel(kinds, pieces, scaled, which, *refs):
+    values, refs = refs[: 4 * pieces], refs[4 * pieces :]
+    scale, refs = (refs[0], refs[1:]) if scaled else (None, refs)
+    tile, out, total = refs
+    far, kind = pl.program_id(0), pl.program_id(1)
+    at_end = which[2] == 1
+    product = None
+    for piece in range(pieces):
+        own, one, two, three = values[4 * piece : 4 * piece + 4]
+        size = own.shape[2]
+        near_value = jnp.where(at_end, own[0], one[0])
+        far_value = jnp.where(at_end, three[0], two[0])
+        value = jnp.where(far == 0, near_value, far_value)
+        part = jnp.dot(value, tile[0, piece * size : (piece + 1) * size], preferred_element_type=F32)
+        product = part if product is None else product + part
+    first = (far == 0) & (kind == 0)
+    last = (far == 1) & (kind == kinds - 1)
+
+    @pl.when(first)
+    def _():
+        total[...] = product
+
+    @pl.when(jnp.logical_not(first) & jnp.logical_not(last))
+    def _():
+        total[...] += product
+
+    @pl.when(last)
+    def _():
+        result = total[...] + product
+        if scaled:
+            result = result * scale[...]
+        out[...] = result.astype(BF16)
+
+
+def second_product(which, partner, values, scale, weights, after):
+    kinds, slots = values[0][0].shape[:2]
+    half = weights.shape[1] // 2
+    width = weights.shape[2] // 2
+
+    def tile_at(far, kind, w):
+        return (kind, jnp.where(far == 0, w[0], 1 - w[0]), (1 - w[1]) if partner else w[1])
+
+    flat = [v for four in values for v in four]
+    specs = [pl.BlockSpec((1, slots, v.shape[2]), lambda far, kind, w: (kind, 0, 0)) for v in flat]
+    if scale is not None:
+        flat.append(scale)
+        specs.append(pl.BlockSpec((slots, 1), lambda far, kind, w: (0, 0)))
+    return call(
+        functools.partial(second_kernel, kinds, len(values), scale is not None),
+        0.5 + 1.2 * kinds,
+        (*flat, weights),
+        after,
+        jax.ShapeDtypeStruct((slots, width), BF16),
+        scalars=(which,),
+        grid=(2, kinds),
+        in_specs=[*specs, pl.BlockSpec((1, half, width), tile_at)],
+        out_specs=pl.BlockSpec((slots, width), lambda far, kind, w: (0, 0)),
+        scratch=[pltpu.VMEM((slots, width), F32)],
+    )
+
+
+def piece_body(ahead_rows, behind_rows, behind_grad, route_scores, route_counts, gate_up, down_proj):
+    height = ahead_rows.shape[1]
+    gates = gate_up[0, 0]
+    downs = down_proj[0]
+    own = lax.axis_index("expert")
+    sections = lax.axis_size("section")
+    block, group = own // 2, own % 2
+    near = (block >= DBLOCKS // 2).astype(jnp.int32)
+    at_end = ((block == 0) | (block == DBLOCKS - 1)).astype(jnp.int32)
+    near_which = jnp.stack([near, group, at_end])
+    far_which = jnp.stack([1 - near, group, at_end])
+    slot_ids = jnp.arange(height, dtype=jnp.int32)[None]
+    live = slot_ids < route_counts[0][:, None]
+    scales = jnp.where(live, route_scores[0], 0.0)[:, :, None]
+
+    def over_blocks(value, pairs):
+        full = [(a * 2 + f, b * 2 + f) for a, b in pairs for f in range(2)]
+        return lax.ppermute(value, "expert", full)
+
+    def to_section(value, by, flip):
+        devices = 2 * DBLOCKS
+        pairs = [
+            (s * devices + e, (s + by) * devices + (e ^ flip))
+            for s in range(sections)
+            if 0 <= s + by < sections
+            for e in range(devices)
+        ]
+        return lax.ppermute(value, ("section", "expert"), pairs)
+
+    hops = {
+        "1": [(0, 1), (3, 2)],
+        "2": [(1, 2), (2, 1)],
+        "3": [(1, 0), (2, 3)],
+    }
+    inputs = {"F": ahead_rows[0], "g": behind_rows[0], "e": behind_grad[0]}
+    got = {}
+    recent = []
+
+    def rows_of(kind, i):
+        pieces = ROW_PIECES["F" if kind == "F" else "B"]
+        size = height // pieces
+        return inputs[kind][i * size : (i + 1) * size]
+
+    def scale_of(kind, i):
+        size = height // ROW_PIECES[kind]
+        return scales["FB".index(kind), i * size : (i + 1) * size]
+
+    def exchanged(name):
+        kind = {"YF": "F", "YX": "g", "YG": "e"}[name[:2]]
+        rows = rows_of(kind, int(name[2]))
+        pairs = [(i, i ^ 1) for i in range(2 * DBLOCKS)]
+        got[kind, int(name[2])] = (rows, lax.ppermute(rows, "expert", pairs))
+
+    def step(name):
+        if name[0] == "Y":
+            return exchanged(name)
+        piece, op = name.split(".")
+        if op in ("Y", "X"):
+            source = got[piece + (".ms" if op == "Y" else ".mk")]
+            got[name] = to_section(source, 1 if piece[1] == "F" else -1, op == "Y")
+            return
+        if op[0] in "PQ":
+            before = {"P1": "mf", "P2": "a1", "P3": "a2", "Q1": "act", "Q2": "Q1", "Q3": "Q2"}[op]
+            got[name] = over_blocks(got[piece + "." + before], hops[op[1]])
+            return
+        kind = piece[0]
+        if op in ("mf", "mn"):
+            rows = got[piece[3] if kind == "B" else "F", int(piece[1])]
+            weights = downs if piece[3:] == "e" else gates
+            which = far_which if op == "mf" else near_which
+            made = first_product(which, rows, weights, int(piece[2]), UNIT_PIECES[kind], recent)
+        elif op == "a1":
+            made = added(got[piece + ".mf"], got[piece + ".P1"], recent)
+        elif op == "a2":
+            made = added(got[piece + ".mn"], got[piece + ".P2"], recent)
+        elif op == "act":
+            parts = [piece] if kind == "F" else [piece + "g", piece + "e"]
+            operands = [got[p + s] for p in parts for s in (".mn", ".P3")]
+            if kind == "B":
+                operands.append(scale_of(kind, int(piece[1])))
+            shape = (1 if kind == "F" else 2, *operands[0].shape[1:])
+            kernel = ahead_act_kernel if kind == "F" else behind_act_kernel
+            made = call(kernel, 0.6, operands, recent, jax.ShapeDtypeStruct(shape, BF16))
+        elif op in ("ms", "mk"):
+            kind, i = piece[1], piece[2]
+            values = [
+                [got[f"{kind}{i}{u}.{s}"] for s in ("act", "Q1", "Q2", "Q3")]
+                for u in range(UNIT_PIECES[kind])
+            ]
+            scale = scale_of(kind, int(i)) if kind == "F" else None
+            weights = downs if kind == "F" else gates
+            made = second_product(near_which, op == "ms", values, scale, weights, recent)
+        got[name] = made
+        recent[:] = [made]
+
+    for name in ORDER:
+        if not name.endswith(".add"):
+            step(name)
+
+    def result(kind):
+        shares = [
+            (got[f"O{kind}{i}0.Y"].astype(F32) + got[f"O{kind}{i}0.X"].astype(F32)).astype(BF16)
+            for i in range(ROW_PIECES[kind])
+        ]
+        return (shares[0] if len(shares) == 1 else jnp.concatenate(shares))[None]
+
+    return result("F"), result("B")
 
 
 def body(ahead_rows, behind_rows, behind_grad, route_scores, route_counts, gate_up, down_proj):
@@ -24,8 +303,6 @@
     weights_out = down_proj[0, 0]
     units = weights_in.shape[1]
     part = units // DBLOCKS
-    own = lax.axis_index("expert")
-    block = own // fgroups
 
     def wide(rows):
         return lax.all_gather(rows, "expert", axis_index_groups=low, axis=1, tiled=True)
@@ -88,4 +365,5 @@
         P("section", "expert", None, None),
     )
     out_specs = (P("section", None, "expert"), P("section", None, "expert"))
-    return jax.shard_map(body, mesh=mesh, in_specs=in_specs, out_specs=out_specs, check_vma=False)
+    chosen = piece_body if mesh.shape["expert"] == 2 * DBLOCKS else body
+    return jax.shard_map(chosen, mesh=mesh, in_specs=in_specs, out_specs=out_specs, check_vma=False)

time: 295 us -> 193 us (0.65)
  waiting for transfers between devices: 207 us -> 37.6 us
  starting transfers between devices: 6.73 us -> 90.6 us
  Pallas kernels: 0 us -> 42 us
  matrix products: 29.6 us -> 0 us
  blocking collectives: 19 us -> 0 us
  between operations: 14.2 us -> 1.44 us
    ppermute x2 -> x37, starting transfers between devices: 6.23 us -> 90.6 us  [the longest x30 62.1 us: over_blocks(): return lax.ppermute(value, 'expert', full)]
    all_gather x4 -> x0, waiting for transfers between devices: 83.9 us -> none  [the longest x3 65.6 us: wide(): lax.all_gather(rows, 'expert', axis_index_groups=low, axis=1, tiled=True)]
    reduce_scatter x2 -> x0, waiting for transfers between devices: 73.8 us -> none  [reduced(): lax.psum_scatter(flat, 'expert', axis_index_groups=high, scatter_dimensio...]
    pallas_call x0 -> x32, Pallas kernels: none -> 42 us  [call(): pl.pallas_call(run, compiler_params=pltpu.CompilerParams(vmem_limit_bytes...]
    unnamed x10 -> x0, waiting for transfers between devices: 39.5 us -> none
    dot_general x5 -> x0, matrix products: 29.6 us -> none  [the longest x1 7.43 us: body(): jnp.einsum('cd,kqfd->qkcf', behind_wide, gates, preferred_element_type=F32)]
    ppermute x2 -> x37, waiting for transfers between devices: 9.68 us -> 37.6 us  [the longest x3 13.1 us: exchanged(): got[kind, int(name[2])] = (rows, lax.ppermute(rows, 'expert', pairs))]
    all_gather x1 -> x0, blocking collectives: 19 us -> none  [spread(): lax.all_gather(values, 'expert', axis_index_groups=high, axis=0, tiled=Fa...]
  transfers between devices with their start and end apart: 10 -> 37, of which waited for: 9 -> 8; matrix products, arithmetic and copies ran while one was open for 15% -> 2% of each run, Pallas kernels for 0% -> 22%
where the time goes in v3:
time: 193 us; the launch traced here: 190 us
  starting transfers between devices  90.6 us (47%)
  Pallas kernels  42 us (22%)
  waiting for transfers between devices  37.6 us (19%)
  local copies, waits for them, and re-layouts  15.5 us (8%)
  other arithmetic  2.94 us (2%)
    ppermute x30, starting transfers between devices, over_blocks(): return lax.ppermute(value, 'expert', full)  62.1 us
    pallas_call x32, Pallas kernels, call(): pl.pallas_call(run, compiler_params=pltpu.CompilerParams(vmem_limit_bytes...  42 us
    ppermute x4, starting transfers between devices, to_section(): return lax.ppermute(value, ('section', 'expert'), pairs)  24.9 us
    unnamed x44, local copies, waits for them, and re-layouts  14.5 us
    ppermute x3, waiting for transfers between devices, exchanged(): got[kind, int(name[2])] = (rows, lax.ppermute(rows, 'expert', pairs))  13.1 us
    ppermute x30, waiting for transfers between devices, over_blocks(): return lax.ppermute(value, 'expert', full)  12.3 us
    ppermute x4, waiting for transfers between devices, to_section(): return lax.ppermute(value, ('section', 'expert'), pairs)  12.2 us
  transfers between devices with their start and end apart: 37, of which 8 were waited for; matrix products, arithmetic and copies ran while one was open for 2% of the time, Pallas kernels for 22%

profile of v3, /device:TPU:1, one launch (start us, length us, event | category | flops | bytes accessed | tf_op | source)
XLA Modules:
  0.0 190.1 jit_solution(3856014279778639246)
XLA Ops:
  0.6 2.1 %collective-permute-start.2 = (bf16[384,896]{1,0:T(8,128)(2,1)}, bf16[384,896]{1,0:T(8,128)(2,1)S(1)}, u32[]{:S(2)}, u32[]{:S(2)}) collective-permute-start(bf16[384,896]{1,0:T(8,128)(2,1)} %bitcast.38), channel_id=1, source_target_pairs={{0,1},{1,0},{2,3},{3,2},{4,5},{5,4},{6,7},{7,6},{8,9},{9,8},{10,11... | collective-permute-start | bytes 2064392 | tf_op jit(solution)/shard_map/ppermute | solution.py:238
  5.1 13.1 %collective-permute-done.2.refs_2_ = bf16[384,896]{1,0:T(8,128)(2,1)S(1)} collective-permute-done((bf16[384,896]{1,0:T(8,128)(2,1)}, bf16[384,896]{1,0:T(8,128)(2,1)S(1)}, u32[]{:S(2)}, u32[]{:S(2)}) %collective-permute-start.2) | collective-permute-done | bytes 688160 | tf_op jit(solution)/shard_map/ppermute | solution.py:238
  18.1 3.1 %copy-done = bf16[1,1,2,1024,1792]{4,3,2,1,0:T(8,128)(2,1)S(1)} copy-done((bf16[1,1,2,1024,1792]{4,3,2,1,0:T(8,128)(2,1)S(1)}, bf16[1,1,2,1024,1792]{4,3,2,1,0:T(8,128)(2,1)}, u32[]{:S(2)}) %copy-start) | copy-done | bytes 7340056
  26.0 3.1 %collective-permute-start.3 = (bf16[2,384,256]{2,1,0:T(8,128)(2,1)S(1)}, bf16[2,384,256]{2,1,0:T(8,128)(2,1)S(1)}, u32[]{:S(2)}, u32[]{:S(2)}) collective-permute-start(bf16[2,384,256]{2,1,0:T(8,128)(2,1)S(1)} %shard_map.87.refs_4_.refs_0_), channel_id=1, source_target_pairs={{0,2},{1,3},{6,4},{7,5},{8,10},{9,11},{14,12},{15,13},{16,18},{17,... | collective-permute-start | bytes 1179656 | tf_op jit(solution)/shard_map/ppermute | solution.py:204
  36.8 6.6 %collective-permute-start.4 = (bf16[1,384,256]{2,1,0:T(8,128)(2,1)S(1)}, bf16[1,384,256]{2,1,0:T(8,128)(2,1)S(1)}, u32[]{:S(2)}, u32[]{:S(2)}) collective-permute-start(bf16[1,384,256]{2,1,0:T(8,128)(2,1)S(1)} %shard_map.91.refs_4_.refs_0_), channel_id=1, source_target_pairs={{0,2},{1,3},{6,4},{7,5},{8,10},{9,11},{14,12},{15,13},{16,18},{17,... | collective-permute-start | bytes 589832 | tf_op jit(solution)/shard_map/ppermute | solution.py:204
  53.9 6.2 %collective-permute-start.7 = (bf16[2,384,256]{2,1,0:T(8,128)(2,1)S(1)}, bf16[2,384,256]{2,1,0:T(8,128)(2,1)S(1)}, u32[]{:S(2)}, u32[]{:S(2)}) collective-permute-start(bf16[2,384,256]{2,1,0:T(8,128)(2,1)S(1)} %shard_map.98.refs_4_.refs_0_), channel_id=1, source_target_pairs={{0,2},{1,3},{6,4},{7,5},{8,10},{9,11},{14,12},{15,13},{16,18},{17,... | collective-permute-start | bytes 1179656 | tf_op jit(solution)/shard_map/ppermute | solution.py:204
  66.1 2.5 %shard_map.103.refs_2_.refs_0_ = bf16[2,384,256]{2,1,0:T(8,128)(2,1)} custom-call(s32[3]{0:T(128)S(1)} %add_add_fusion.1.refs_0_, bf16[384,896]{1,0:T(8,128)(2,1)S(1)} %bitcast.51, bf16[384,896]{1,0:T(8,128)(2,1)S(1)} %collective-permute-done.refs_2_, bf16[2,1024,1792]{2,1,0:T(8,128)(2,1)S(1)} %bitcast.28, bf16[1,384,256]{2,1,0:T(8,128)(2,1)S(1)} %shard_map.102.refs_4_), custom_call_target="tpu_custom_call" | custom-call | flops 1704999936 | bytes 1024 | tf_op jit(solution)/shard_map/pallas_call | solution.py:49
  68.6 8.0 %collective-permute-start.12 = (bf16[2,384,256]{2,1,0:T(8,128)(2,1)}, bf16[2,384,256]{2,1,0:T(8,128)(2,1)}, u32[]{:S(2)}, u32[]{:S(2)}) collective-permute-start(bf16[2,384,256]{2,1,0:T(8,128)(2,1)} %shard_map.103.refs_2_.refs_0_), channel_id=1, source_target_pairs={{0,2},{1,3},{6,4},{7,5},{8,10},{9,11},{14,12},{15,13},{16,18},{17,... | collective-permute-start | bytes 1179656 | tf_op jit(solution)/shard_map/ppermute | solution.py:204
  82.8 3.1 %copy-done.1 = bf16[1,1,2,1024,1792]{4,3,2,1,0:T(8,128)(2,1)S(1)} copy-done((bf16[1,1,2,1024,1792]{4,3,2,1,0:T(8,128)(2,1)S(1)}, bf16[1,1,2,1024,1792]{4,3,2,1,0:T(8,128)(2,1)}, u32[]{:S(2)}) %copy-start.1) | copy-done | bytes 7340056
  91.9 5.4 %collective-permute-start.30 = (bf16[2,384,256]{2,1,0:T(8,128)(2,1)S(1)}, bf16[2,384,256]{2,1,0:T(8,128)(2,1)S(1)}, u32[]{:S(2)}, u32[]{:S(2)}) collective-permute-start(bf16[2,384,256]{2,1,0:T(8,128)(2,1)S(1)} %shard_map.107.refs_2_.refs_5_), channel_id=1, source_target_pairs={{0,2},{1,3},{6,4},{7,5},{8,10},{9,11},{14,12},{15,13},{16,18},{17,... | collective-permute-start | bytes 1179656 | tf_op jit(solution)/shard_map/ppermute | solution.py:204
  106.9 2.7 %collective-permute-done.16.refs_1_ = bf16[2,384,256]{2,1,0:T(8,128)(2,1)S(1)} collective-permute-done((bf16[2,384,256]{2,1,0:T(8,128)(2,1)S(1)}, bf16[2,384,256]{2,1,0:T(8,128)(2,1)S(1)}, u32[]{:S(2)}, u32[]{:S(2)}) %collective-permute-start.16) | collective-permute-done | bytes 393248 | tf_op jit(solution)/shard_map/ppermute | solution.py:204
  109.7 4.6 %collective-permute-start.20 = (bf16[1,384,256]{2,1,0:T(8,128)(2,1)S(1)}, bf16[1,384,256]{2,1,0:T(8,128)(2,1)}, u32[]{:S(2)}, u32[]{:S(2)}) collective-permute-start(bf16[1,384,256]{2,1,0:T(8,128)(2,1)S(1)} %shard_map.112.refs_2_.refs_1_), channel_id=1, source_target_pairs={{0,2},{1,3},{6,4},{7,5},{8,10},{9,11},{14,12},{15,13},{16,18},{17,... | collective-permute-start | bytes 589832 | tf_op jit(solution)/shard_map/ppermute | solution.py:204
  125.4 3.0 %collective-permute-done.32.refs_8_ = bf16[2,384,256]{2,1,0:T(8,128)(2,1)S(1)} collective-permute-done((bf16[2,384,256]{2,1,0:T(8,128)(2,1)S(1)}, bf16[2,384,256]{2,1,0:T(8,128)(2,1)S(1)}, u32[]{:S(2)}, u32[]{:S(2)}) %collective-permute-start.32) | collective-permute-done | bytes 393248 | tf_op jit(solution)/shard_map/ppermute | solution.py:204
  128.4 4.2 %collective-permute-done.29.refs_4_ = bf16[2,384,256]{2,1,0:T(8,128)(2,1)S(1)} collective-permute-done((bf16[2,384,256]{2,1,0:T(8,128)(2,1)S(1)}, bf16[2,384,256]{2,1,0:T(8,128)(2,1)S(1)}, u32[]{:S(2)}, u32[]{:S(2)}) %collective-permute-start.29) | collective-permute-done | bytes 393248 | tf_op jit(solution)/shard_map/ppermute | solution.py:204
  132.6 3.1 %copy-done.2 = bf16[1,1,2,1024,1792]{4,3,2,1,0:T(8,128)(2,1)S(1)} copy-done((bf16[1,1,2,1024,1792]{4,3,2,1,0:T(8,128)(2,1)S(1)}, bf16[1,1,2,1024,1792]{4,3,2,1,0:T(8,128)(2,1)}, u32[]{:S(2)}) %copy-start.2) | copy-done | bytes 7340056
  136.6 3.7 %shard_map.114.refs_10_ = bf16[384,896]{1,0:T(8,128)(2,1)S(1)} custom-call(s32[3]{0:T(128)S(1)} %add_add_fusion.refs_0_, bf16[2,384,256]{2,1,0:T(8,128)(2,1)S(1)} %shard_map.110.refs_2_.refs_1_, bf16[2,384,256]{2,1,0:T(8,128)(2,1)S(1)} %collective-permute-done.27.refs_2_, bf16[2,384,256]{2,1,0:T(8,128)(2,1)S(1)} %collective-permute-done.28.refs_3_, ...), custom_call_target="tpu_custom_call" | custom-call | flops 3190000128 | bytes 1024 | tf_op jit(solution)/shard_map/pallas_call | solution.py:49
  140.4 17.5 %collective-permute-start.35 = (bf16[384,896]{1,0:T(8,128)(2,1)S(1)}, bf16[384,896]{1,0:T(8,128)(2,1)S(1)}, u32[]{:S(2)}, u32[]{:S(2)}) collective-permute-start(bf16[384,896]{1,0:T(8,128)(2,1)S(1)} %shard_map.114.refs_10_), channel_id=1, source_target_pairs={{8,1},{9,0},{10,3},{11,2},{12,5},{13,4},{14,7},{15,6},{16,9},{17,8... | collective-permute-start | bytes 2064392 | tf_op jit(solution)/shard_map/ppermute | solution.py:214
  157.8 3.7 %shard_map.115.refs_11_ = bf16[384,896]{1,0:T(8,128)(2,1)S(1)} custom-call(s32[3]{0:T(128)S(1)} %add_add_fusion.refs_0_, bf16[2,384,256]{2,1,0:T(8,128)(2,1)S(1)} %shard_map.110.refs_2_.refs_1_, bf16[2,384,256]{2,1,0:T(8,128)(2,1)S(1)} %collective-permute-done.27.refs_2_, bf16[2,384,256]{2,1,0:T(8,128)(2,1)S(1)} %collective-permute-done.28.refs_3_, ...), custom_call_target="tpu_custom_call" | custom-call | flops 3190000128 | bytes 1024 | tf_op jit(solution)/shard_map/pallas_call | solution.py:49
  163.5 3.4 %shard_map.116.refs_11_ = bf16[384,896]{1,0:T(8,128)(2,1)S(1)} custom-call(s32[3]{0:T(128)S(1)} %add_add_fusion.refs_0_, bf16[1,384,256]{2,1,0:T(8,128)(2,1)S(1)} %copy-done.13, bf16[1,384,256]{2,1,0:T(8,128)(2,1)} %collective-permute-done.20.refs_2_, bf16[1,384,256]{2,1,0:T(8,128)(2,1)} %collective-permute-done.21.refs_3_, ...), custom_call_target="tpu_custom_call" | custom-call | flops 1870000000 | bytes 1024 | tf_op jit(solution)/shard_map/pallas_call | solution.py:49
  166.9 3.4 %shard_map.117 = bf16[384,896]{1,0:T(8,128)(2,1)S(1)} custom-call(s32[3]{0:T(128)S(1)} %add_add_fusion.refs_0_, bf16[1,384,256]{2,1,0:T(8,128)(2,1)S(1)} %copy-done.13, bf16[1,384,256]{2,1,0:T(8,128)(2,1)} %collective-permute-done.20.refs_2_, bf16[1,384,256]{2,1,0:T(8,128)(2,1)} %collective-permute-done.21.refs_3_, ...), custom_call_target="tpu_custom_call" | custom-call | flops 1870000000 | bytes 1024 | tf_op jit(solution)/shard_map/pallas_call | solution.py:49
  170.3 3.6 %collective-permute-start.33 = (bf16[384,896]{1,0:T(8,128)(2,1)S(1)}, bf16[384,896]{1,0:T(8,128)(2,1)S(1)}, u32[]{:S(2)}, u32[]{:S(2)}) collective-permute-start(bf16[384,896]{1,0:T(8,128)(2,1)S(1)} %shard_map.117), channel_id=1, source_target_pairs={{0,9},{1,8},{2,11},{3,10},{4,13},{5,12},{6,15},{7,14},{8,17},{9,16... | collective-permute-start | bytes 2064392 | tf_op jit(solution)/shard_map/ppermute | solution.py:214
  173.8 2.0 %collective-permute-start.34 = (bf16[384,896]{1,0:T(8,128)(2,1)S(1)}, bf16[384,896]{1,0:T(8,128)(2,1)S(1)}, u32[]{:S(2)}, u32[]{:S(2)}) collective-permute-start(bf16[384,896]{1,0:T(8,128)(2,1)S(1)} %shard_map.116.refs_11_), channel_id=1, source_target_pairs={{0,8},{1,9},{2,10},{3,11},{4,12},{5,13},{6,14},{7,15},{8,16},{9,17... | collective-permute-start | bytes 2064392 | tf_op jit(solution)/shard_map/ppermute | solution.py:214
  176.9 5.6 %collective-permute-done.33 = bf16[384,896]{1,0:T(8,128)(2,1)S(1)} collective-permute-done((bf16[384,896]{1,0:T(8,128)(2,1)S(1)}, bf16[384,896]{1,0:T(8,128)(2,1)S(1)}, u32[]{:S(2)}, u32[]{:S(2)}) %collective-permute-start.33) | collective-permute-done | bytes 688160 | tf_op jit(solution)/shard_map/ppermute | solution.py:214
  182.5 6.6 %collective-permute-done.34 = bf16[384,896]{1,0:T(8,128)(2,1)S(1)} collective-permute-done((bf16[384,896]{1,0:T(8,128)(2,1)S(1)}, bf16[384,896]{1,0:T(8,128)(2,1)S(1)}, u32[]{:S(2)}, u32[]{:S(2)}) %collective-permute-start.34) | collective-permute-done | bytes 688160 | tf_op jit(solution)/shard_map/ppermute | solution.py:214
  (135 shorter events, 68.5 us)
Async XLA Ops:
  0.6 17.5 %collective-permute-start.2 = (bf16[384,896]{1,0:T(8,128)(2,1)}, bf16[384,896]{1,0:T(8,128)(2,1)S(1)}, u32[]{:S(2)}, u32[]{:S(2)}) collective-permute-start(bf16[384,896]{1,0:T(8,128)(2,1)} %bitcast.38), channel_id=1, source_target_pairs={{0,1},{1,0},{2,3},{3,2},{4,5},{5,4},{6,7},{7,6},{8,9},{9,8},{10,11... | collective-permute-start | bytes 2064392 | tf_op jit(solution)/shard_map/ppermute | solution.py:238
  2.8 32.8 %collective-permute-start.1 = (bf16[384,896]{1,0:T(8,128)(2,1)}, bf16[384,896]{1,0:T(8,128)(2,1)S(1)}, u32[]{:S(2)}, u32[]{:S(2)}) collective-permute-start(bf16[384,896]{1,0:T(8,128)(2,1)} %bitcast.43), channel_id=1, source_target_pairs={{0,1},{1,0},{2,3},{3,2},{4,5},{5,4},{6,7},{7,6},{8,9},{9,8},{10,11... | collective-permute-start | bytes 2064392 | tf_op jit(solution)/shard_map/ppermute | solution.py:238
  2.8 49.2 %collective-permute-start = (bf16[384,896]{1,0:T(8,128)(2,1)}, bf16[384,896]{1,0:T(8,128)(2,1)S(1)}, u32[]{:S(2)}, u32[]{:S(2)}) collective-permute-start(bf16[384,896]{1,0:T(8,128)(2,1)} %bitcast.48), channel_id=1, source_target_pairs={{0,1},{1,0},{2,3},{3,2},{4,5},{5,4},{6,7},{7,6},{8,9},{9,8},{10,11... | collective-permute-start | bytes 2064392 | tf_op jit(solution)/shard_map/ppermute | solution.py:238
  29.2 19.0 %collective-permute-start.6 = (bf16[2,384,256]{2,1,0:T(8,128)(2,1)S(1)}, bf16[2,384,256]{2,1,0:T(8,128)(2,1)S(1)}, u32[]{:S(2)}, u32[]{:S(2)}) collective-permute-start(bf16[2,384,256]{2,1,0:T(8,128)(2,1)S(1)} %shard_map.86.refs_4_.refs_0_), channel_id=1, source_target_pairs={{0,2},{1,3},{6,4},{7,5},{8,10},{9,11},{14,12},{15,13},{16,18},{17,... | collective-permute-start | bytes 1179656 | tf_op jit(solution)/shard_map/ppermute | solution.py:204
  34.9 14.3 %collective-permute-start.5 = (bf16[2,384,256]{2,1,0:T(8,128)(2,1)S(1)}, bf16[2,384,256]{2,1,0:T(8,128)(2,1)S(1)}, u32[]{:S(2)}, u32[]{:S(2)}) collective-permute-start(bf16[2,384,256]{2,1,0:T(8,128)(2,1)S(1)} %shard_map.90.refs_4_), channel_id=1, source_target_pairs={{2,4},{3,5},{4,2},{5,3},{10,12},{11,13},{12,10},{13,11},{18,20},{1... | collective-permute-start | bytes 1179656 | tf_op jit(solution)/shard_map/ppermute | solution.py:204
  36.8 14.5 %collective-permute-start.4 = (bf16[1,384,256]{2,1,0:T(8,128)(2,1)S(1)}, bf16[1,384,256]{2,1,0:T(8,128)(2,1)S(1)}, u32[]{:S(2)}, u32[]{:S(2)}) collective-permute-start(bf16[1,384,256]{2,1,0:T(8,128)(2,1)S(1)} %shard_map.91.refs_4_.refs_0_), channel_id=1, source_target_pairs={{0,2},{1,3},{6,4},{7,5},{8,10},{9,11},{14,12},{15,13},{16,18},{17,... | collective-permute-start | bytes 589832 | tf_op jit(solution)/shard_map/ppermute | solution.py:204
  46.9 17.1 %collective-permute-start.9 = (bf16[1,384,256]{2,1,0:T(8,128)(2,1)S(1)}, bf16[1,384,256]{2,1,0:T(8,128)(2,1)S(1)}, u32[]{:S(2)}, u32[]{:S(2)}) collective-permute-start(bf16[1,384,256]{2,1,0:T(8,128)(2,1)S(1)} %shard_map.94.refs_2_.refs_0_), channel_id=1, source_target_pairs={{0,2},{1,3},{6,4},{7,5},{8,10},{9,11},{14,12},{15,13},{16,18},{17,... | collective-permute-start | bytes 589832 | tf_op jit(solution)/shard_map/ppermute | solution.py:204
  48.3 13.5 %collective-permute-start.10 = (bf16[2,384,256]{2,1,0:T(8,128)(2,1)S(1)}, bf16[2,384,256]{2,1,0:T(8,128)(2,1)S(1)}, u32[]{:S(2)}, u32[]{:S(2)}) collective-permute-start(bf16[2,384,256]{2,1,0:T(8,128)(2,1)S(1)} %shard_map.95.refs_2_), channel_id=1, source_target_pairs={{2,4},{3,5},{4,2},{5,3},{10,12},{11,13},{12,10},{13,11},{18,20},{1... | collective-permute-start | bytes 1179656 | tf_op jit(solution)/shard_map/ppermute | solution.py:204
  50.0 37.7 %collective-permute-start.13 = (bf16[2,384,256]{2,1,0:T(8,128)(2,1)}, bf16[2,384,256]{2,1,0:T(8,128)(2,1)}, u32[]{:S(2)}, u32[]{:S(2)}) collective-permute-start(bf16[2,384,256]{2,1,0:T(8,128)(2,1)} %shard_map.96.refs_2_), channel_id=1, source_target_pairs={{2,0},{3,1},{4,6},{5,7},{10,8},{11,9},{12,14},{13,15},{18,16},{19,... | collective-permute-start | bytes 1179656 | tf_op jit(solution)/shard_map/ppermute | solution.py:204
  51.3 13.4 %collective-permute-start.8 = (bf16[1,384,256]{2,1,0:T(8,128)(2,1)S(1)}, bf16[1,384,256]{2,1,0:T(8,128)(2,1)S(1)}, u32[]{:S(2)}, u32[]{:S(2)}) collective-permute-start(bf16[1,384,256]{2,1,0:T(8,128)(2,1)S(1)} %shard_map.97.refs_4_), channel_id=1, source_target_pairs={{2,4},{3,5},{4,2},{5,3},{10,12},{11,13},{12,10},{13,11},{18,20},{1... | collective-permute-start | bytes 589832 | tf_op jit(solution)/shard_map/ppermute | solution.py:204
  53.9 14.7 %collective-permute-start.7 = (bf16[2,384,256]{2,1,0:T(8,128)(2,1)S(1)}, bf16[2,384,256]{2,1,0:T(8,128)(2,1)S(1)}, u32[]{:S(2)}, u32[]{:S(2)}) collective-permute-start(bf16[2,384,256]{2,1,0:T(8,128)(2,1)S(1)} %shard_map.98.refs_4_.refs_0_), channel_id=1, source_target_pairs={{0,2},{1,3},{6,4},{7,5},{8,10},{9,11},{14,12},{15,13},{16,18},{17,... | collective-permute-start | bytes 1179656 | tf_op jit(solution)/shard_map/ppermute | solution.py:204
  62.7 35.7 %collective-permute-start.18 = (bf16[2,384,256]{2,1,0:T(8,128)(2,1)}, bf16[2,384,256]{2,1,0:T(8,128)(2,1)}, u32[]{:S(2)}, u32[]{:S(2)}) collective-permute-start(bf16[2,384,256]{2,1,0:T(8,128)(2,1)} %shard_map.100.refs_2_), channel_id=1, source_target_pairs={{2,0},{3,1},{4,6},{5,7},{10,8},{11,9},{12,14},{13,15},{18,16},{19,... | collective-permute-start | bytes 1179656 | tf_op jit(solution)/shard_map/ppermute | solution.py:204
  64.1 13.4 %collective-permute-start.15 = (bf16[1,384,256]{2,1,0:T(8,128)(2,1)S(1)}, bf16[1,384,256]{2,1,0:T(8,128)(2,1)S(1)}, u32[]{:S(2)}, u32[]{:S(2)}) collective-permute-start(bf16[1,384,256]{2,1,0:T(8,128)(2,1)S(1)} %shard_map.101.refs_2_), channel_id=1, source_target_pairs={{2,4},{3,5},{4,2},{5,3},{10,12},{11,13},{12,10},{13,11},{18,20},{1... | collective-permute-start | bytes 589832 | tf_op jit(solution)/shard_map/ppermute | solution.py:204
  64.8 16.6 %collective-permute-start.14 = (bf16[1,384,256]{2,1,0:T(8,128)(2,1)S(1)}, bf16[1,384,256]{2,1,0:T(8,128)(2,1)S(1)}, u32[]{:S(2)}, u32[]{:S(2)}) collective-permute-start(bf16[1,384,256]{2,1,0:T(8,128)(2,1)S(1)} %shard_map.102.refs_4_), channel_id=1, source_target_pairs={{2,0},{3,1},{4,6},{5,7},{10,8},{11,9},{12,14},{13,15},{18,16},{19,... | collective-permute-start | bytes 589832 | tf_op jit(solution)/shard_map/ppermute | solution.py:204
  68.6 21.4 %collective-permute-start.12 = (bf16[2,384,256]{2,1,0:T(8,128)(2,1)}, bf16[2,384,256]{2,1,0:T(8,128)(2,1)}, u32[]{:S(2)}, u32[]{:S(2)}) collective-permute-start(bf16[2,384,256]{2,1,0:T(8,128)(2,1)} %shard_map.103.refs_2_.refs_0_), channel_id=1, source_target_pairs={{0,2},{1,3},{6,4},{7,5},{8,10},{9,11},{14,12},{15,13},{16,18},{17,... | collective-permute-start | bytes 1179656 | tf_op jit(solution)/shard_map/ppermute | solution.py:204
  78.1 19.2 %collective-permute-start.11 = (bf16[2,384,256]{2,1,0:T(8,128)(2,1)}, bf16[2,384,256]{2,1,0:T(8,128)(2,1)}, u32[]{:S(2)}, u32[]{:S(2)}) collective-permute-start(bf16[2,384,256]{2,1,0:T(8,128)(2,1)} %shard_map.104.refs_2_), channel_id=1, source_target_pairs={{2,4},{3,5},{4,2},{5,3},{10,12},{11,13},{12,10},{13,11},{18,20},{1... | collective-permute-start | bytes 1179656 | tf_op jit(solution)/shard_map/ppermute | solution.py:204
  81.4 17.0 %collective-permute-start.19 = (bf16[1,384,256]{2,1,0:T(8,128)(2,1)S(1)}, bf16[1,384,256]{2,1,0:T(8,128)(2,1)S(1)}, u32[]{:S(2)}, u32[]{:S(2)}) collective-permute-start(bf16[1,384,256]{2,1,0:T(8,128)(2,1)S(1)} %shard_map.105.refs_4_), channel_id=1, source_target_pairs={{2,0},{3,1},{4,6},{5,7},{10,8},{11,9},{12,14},{13,15},{18,16},{19,... | collective-permute-start | bytes 589832 | tf_op jit(solution)/shard_map/ppermute | solution.py:204
  103.8 13.4 %collective-permute-start.31 = (bf16[2,384,256]{2,1,0:T(8,128)(2,1)S(1)}, bf16[2,384,256]{2,1,0:T(8,128)(2,1)S(1)}, u32[]{:S(2)}, u32[]{:S(2)}) collective-permute-start(bf16[2,384,256]{2,1,0:T(8,128)(2,1)S(1)} %collective-permute-done.30.refs_6_), channel_id=1, source_target_pairs={{2,4},{3,5},{4,2},{5,3},{10,12},{11,13},{12,10},{13,11},{18,20},{1... | collective-permute-start | bytes 1179656 | tf_op jit(solution)/shard_map/ppermute | solution.py:204
  118.5 14.1 %collective-permute-start.29 = (bf16[2,384,256]{2,1,0:T(8,128)(2,1)S(1)}, bf16[2,384,256]{2,1,0:T(8,128)(2,1)S(1)}, u32[]{:S(2)}, u32[]{:S(2)}) collective-permute-start(bf16[2,384,256]{2,1,0:T(8,128)(2,1)S(1)} %collective-permute-done.28.refs_3_), channel_id=1, source_target_pairs={{2,0},{3,1},{4,6},{5,7},{10,8},{11,9},{12,14},{13,15},{18,16},{19,... | collective-permute-start | bytes 1179656 | tf_op jit(solution)/shard_map/ppermute | solution.py:204
  122.6 40.8 %collective-permute-start.22 = (bf16[1,384,256]{2,1,0:T(8,128)(2,1)}, bf16[1,384,256]{2,1,0:T(8,128)(2,1)S(1)}, u32[]{:S(2)}, u32[]{:S(2)}) collective-permute-start(bf16[1,384,256]{2,1,0:T(8,128)(2,1)} %collective-permute-done.21.refs_3_), channel_id=1, source_target_pairs={{2,0},{3,1},{4,6},{5,7},{10,8},{11,9},{12,14},{13,15},{18,16},{19,... | collective-permute-start | bytes 589832 | tf_op jit(solution)/shard_map/ppermute | solution.py:204
  123.9 39.5 %collective-permute-start.26 = (bf16[1,384,256]{2,1,0:T(8,128)(2,1)}, bf16[1,384,256]{2,1,0:T(8,128)(2,1)S(1)}, u32[]{:S(2)}, u32[]{:S(2)}) collective-permute-start(bf16[1,384,256]{2,1,0:T(8,128)(2,1)} %collective-permute-done.25.refs_7_), channel_id=1, source_target_pairs={{2,0},{3,1},{4,6},{5,7},{10,8},{11,9},{12,14},{13,15},{18,16},{19,... | collective-permute-start | bytes 589832 | tf_op jit(solution)/shard_map/ppermute | solution.py:204
  140.4 35.5 %collective-permute-start.35 = (bf16[384,896]{1,0:T(8,128)(2,1)S(1)}, bf16[384,896]{1,0:T(8,128)(2,1)S(1)}, u32[]{:S(2)}, u32[]{:S(2)}) collective-permute-start(bf16[384,896]{1,0:T(8,128)(2,1)S(1)} %shard_map.114.refs_10_), channel_id=1, source_target_pairs={{8,1},{9,0},{10,3},{11,2},{12,5},{13,4},{14,7},{15,6},{16,9},{17,8... | collective-permute-start | bytes 2064392 | tf_op jit(solution)/shard_map/ppermute | solution.py:214
  161.5 14.3 %collective-permute-start.36 = (bf16[384,896]{1,0:T(8,128)(2,1)S(1)}, bf16[384,896]{1,0:T(8,128)(2,1)S(1)}, u32[]{:S(2)}, u32[]{:S(2)}) collective-permute-start(bf16[384,896]{1,0:T(8,128)(2,1)S(1)} %shard_map.115.refs_11_), channel_id=1, source_target_pairs={{8,0},{9,1},{10,2},{11,3},{12,4},{13,5},{14,6},{15,7},{16,8},{17,9... | collective-permute-start | bytes 2064392 | tf_op jit(solution)/shard_map/ppermute | solution.py:214
  173.8 15.3 %collective-permute-start.34 = (bf16[384,896]{1,0:T(8,128)(2,1)S(1)}, bf16[384,896]{1,0:T(8,128)(2,1)S(1)}, u32[]{:S(2)}, u32[]{:S(2)}) collective-permute-start(bf16[384,896]{1,0:T(8,128)(2,1)S(1)} %shard_map.116.refs_11_), channel_id=1, source_target_pairs={{0,8},{1,9},{2,10},{3,11},{4,12},{5,13},{6,14},{7,15},{8,16},{9,17... | collective-permute-start | bytes 2064392 | tf_op jit(solution)/shard_map/ppermute | solution.py:214
  (35 other events, 253.8 us)

commit v4 on v1

--- a/solution.py
+++ b/solution.py
@@ -1,17 +1,248 @@
+import functools
+
 import jax
 import jax.numpy as jnp
 from jax import lax
+from jax.experimental import pallas as pl
+from jax.experimental.pallas import tpu as pltpu
 from jax.sharding import PartitionSpec as P
 
 DBLOCKS = 4
 BF16 = jnp.bfloat16
 F32 = jnp.float32
+MIB = 1024 * 1024
 
 
 def shift(shard, axis, by):
     devices = lax.axis_size(axis)
     pairs = [(i, i + by) for i in range(devices) if 0 <= i + by < devices]
     return lax.ppermute(shard, axis, pairs)
+
+
+def whole(array):
+    return pl.BlockSpec(array.shape, functools.partial(lambda n, *_: (0,) * n, array.ndim))
+
+
+def call(kernel, micros, operands, after, out_shape, scalars=(), grid=(1,), in_specs=None, out_specs=None, scratch=(), limit=16):
+    count, unread = len(scalars) + len(operands), len(after)
+
+    def run(*refs):
+        kernel(*refs[:count], *refs[count + unread :])
+
+    if in_specs is None:
+        in_specs = [whole(o) for o in operands]
+    if out_specs is None:
+        out_specs = jax.tree.map(whole, out_shape)
+    return pl.pallas_call(
+        run,
+        compiler_params=pltpu.CompilerParams(vmem_limit_bytes=limit * MIB),
+        cost_estimate=pl.CostEstimate(flops=int(micros * 4e9), bytes_accessed=1024, transcendentals=0),
+        out_shape=out_shape,
+        grid_spec=pltpu.PrefetchScalarGridSpec(
+            num_scalar_prefetch=len(scalars),
+            grid=grid,
+            in_specs=[*in_specs, *[pl.BlockSpec(memory_space=pl.ANY)] * unread],
+            out_specs=out_specs,
+            scratch_shapes=list(scratch),
+        ),
+    )(*scalars, *operands, *after)
+
+
+def first_kernel(width, where, own, partner, tile, out, joined):
+    @pl.when((pl.program_id(0) == 0) & (pl.program_id(1) == 0))
+    def _():
+        at = pl.multiple_of(where[1] * width, 128)
+        other = pl.multiple_of((1 - where[1]) * width, 128)
+        joined[:, pl.ds(at, width)] = own[...]
+        joined[:, pl.ds(other, width)] = partner[...]
+
+    out[0, 0] = lax.dot_general(
+        joined[...], tile[0], (((1,), (1,)), ((), ())), preferred_element_type=F32
+    ).astype(BF16)
+
+
+def first_product(where, rows, weights, quarters, after):
+    slots, width = rows[0].shape
+    kinds, units, features = weights.shape
+    size = units // DBLOCKS
+
+    def tile_at(q, k, w):
+        return (k, quarters(q, w), 0)
+
+    count = DBLOCKS if quarters is natural else 1
+    return call(
+        functools.partial(first_kernel, width),
+        0.5 + 0.65 * kinds * count,
+        (*rows, weights),
+        after,
+        jax.ShapeDtypeStruct((count, kinds, slots, size), BF16),
+        scalars=(where,),
+        grid=(count, kinds),
+        in_specs=[pl.BlockSpec((slots, width), lambda q, k, w: (0, 0))] * 2
+        + [pl.BlockSpec((1, size, features), tile_at)],
+        out_specs=pl.BlockSpec((1, 1, slots, size), lambda q, k, w: (q, k, 0, 0)),
+        scratch=[pltpu.VMEM((slots, features), BF16)],
+    )
+
+
+def natural(q, w):
+    return q
+
+
+def other_block(mask):
+    return lambda q, w: w[0] ^ mask
+
+
+def total_of(refs, kind):
+    total = refs[0][0, kind].astype(F32)
+    for ref in refs[1:]:
+        total += ref[0, kind].astype(F32)
+    return total
+
+
+def ahead_act_kernel(*refs):
+    terms, out = refs[:-1], refs[-1]
+    gate, up = total_of(terms, 0), total_of(terms, 1)
+    out[...] = (gate * jax.nn.sigmoid(gate) * up).astype(BF16)
+
+
+def behind_act_kernel(sums, scale, *refs):
+    terms, out = refs[:-1], refs[-1]
+    gate, up = sums[0].astype(F32), sums[1].astype(F32)
+    expanded = total_of(terms, 0) * scale[...]
+    sig = jax.nn.sigmoid(gate)
+    out[0] = (expanded * up * sig * (1.0 + gate * (1.0 - sig))).astype(BF16)
+    out[1] = (expanded * gate * sig).astype(BF16)
+
+
+def second_dot(joined, tile):
+    kinds, units, width = tile.shape
+    return jnp.dot(joined[...], tile[...].reshape(kinds * units, width), preferred_element_type=F32)
+
+
+def store_share(share, give, keep):
+    @pl.when(pl.program_id(0) == 0)
+    def _():
+        give[...] = share.astype(BF16)
+
+    @pl.when(pl.program_id(0) == 1)
+    def _():
+        keep[...] = share.astype(BF16)
+
+
+def ahead_second_kernel(where, *refs):
+    values, (scale, tile, give, keep, joined) = refs[:DBLOCKS], refs[DBLOCKS:]
+
+    @pl.when(pl.program_id(0) == 0)
+    def _():
+        for mask, value in enumerate(values):
+            size = value.shape[1]
+            at = pl.multiple_of((where[0] ^ mask) * size, 128)
+            joined[:, pl.ds(at, size)] = value[...]
+
+    store_share(second_dot(joined, tile) * scale[...], give, keep)
+
+
+def behind_second_kernel(where, values, tile, give, keep, joined):
+    @pl.when(pl.program_id(0) == 0)
+    def _():
+        quarters, kinds, _, size = values.shape
+        for kind in range(kinds):
+            for q in range(quarters):
+                at = (kind * quarters + q) * size
+                joined[:, at : at + size] = values[q, kind]
+
+    store_share(second_dot(joined, tile), give, keep)
+
+
+def second_product(kernel, where, values, weights, after):
+    kinds, units, features = weights.shape
+    slots = values[0].shape[-2]
+    width = features // 2
+
+    def tile_at(own, w):
+        return (0, 0, jnp.where(own == 0, 1 - w[1], w[1]))
+
+    share = jax.ShapeDtypeStruct((slots, width), BF16)
+    return call(
+        kernel,
+        1 + 3 * kinds,
+        (*values, weights),
+        after,
+        (share, share),
+        scalars=(where,),
+        grid=(2,),
+        in_specs=[*[whole(v) for v in values], pl.BlockSpec((kinds, units, width), tile_at)],
+        scratch=[pltpu.VMEM((slots, kinds * units), BF16)],
+        limit=28,
+    )
+
+
+def direct_body(ahead_rows, behind_rows, behind_grad, route_scores, route_counts, gate_up, down_proj):
+    height = ahead_rows.shape[1]
+    gates = gate_up[0, 0]
+    downs = down_proj[0]
+    units = gates.shape[1]
+    size = units // DBLOCKS
+    own = lax.axis_index("expert")
+    sections = lax.axis_size("section")
+    devices = 2 * DBLOCKS
+    where = jnp.stack([own // 2, own % 2])
+    high = [[q * 2 + f for q in range(DBLOCKS)] for f in range(2)]
+    slot_ids = jnp.arange(height, dtype=jnp.int32)[None]
+    live = slot_ids < route_counts[0][:, None]
+    scales = jnp.where(live, route_scores[0], 0.0)[:, :, None]
+
+    def swapped(value, mask):
+        return lax.ppermute(value, "expert", [(i, i ^ mask) for i in range(devices)])
+
+    def to_section(value, by, flip):
+        pairs = [
+            (s * devices + e, (s + by) * devices + (e ^ flip))
+            for s in range(sections)
+            if 0 <= s + by < sections
+            for e in range(devices)
+        ]
+        return lax.ppermute(value, ("section", "expert"), pairs)
+
+    def joined(shares, by):
+        give, keep = shares
+        arrived = to_section(give, by, 1).astype(F32) + to_section(keep, by, 0).astype(F32)
+        return arrived.astype(BF16)[None]
+
+    rows = {"b": behind_rows[0], "a": ahead_rows[0], "g": behind_grad[0]}
+    rows = {name: (value, swapped(value, 1)) for name, value in rows.items()}
+
+    pre_b = first_product(where, rows["b"], gates, natural, [])
+    sum_b = lax.psum_scatter(
+        pre_b.reshape(-1, size), "expert", axis_index_groups=high, scatter_dimension=0, tiled=True
+    ).reshape(2, height, size)
+
+    def direct(rows, weights, after):
+        terms = []
+        for mask in (2, 3, 1, 0):
+            term = first_product(where, rows, weights, other_block(mask), after)
+            after = [term]
+            terms.append(swapped(term, 2 * mask) if mask else term)
+        return terms, after
+
+    pre_a, after = direct(rows["a"], gates, [pre_b])
+    exp_b, after = direct(rows["g"], downs, after)
+    grads = call(
+        behind_act_kernel,
+        2,
+        (sum_b, scales[1], *exp_b),
+        after,
+        jax.ShapeDtypeStruct((2, height, size), BF16),
+    )
+    grads_all = lax.all_gather(grads, "expert", axis_index_groups=high, axis=0, tiled=False)
+    hidden = call(
+        ahead_act_kernel, 2, pre_a, [grads], jax.ShapeDtypeStruct((height, size), BF16)
+    )
+    hidden_all = [hidden, *[swapped(hidden, 2 * mask) for mask in (1, 2, 3)]]
+    shares_a = second_product(ahead_second_kernel, where, [*hidden_all, scales[0]], downs, [])
+    shares_b = second_product(behind_second_kernel, where, [grads_all], gates, [shares_a[0]])
+    return joined(shares_a, 1), joined(shares_b, -1)
 
 
 def body(ahead_rows, behind_rows, behind_grad, route_scores, route_counts, gate_up, down_proj):
@@ -24,8 +255,6 @@
     weights_out = down_proj[0, 0]
     units = weights_in.shape[1]
     part = units // DBLOCKS
-    own = lax.axis_index("expert")
-    block = own // fgroups
 
     def wide(rows):
         return lax.all_gather(rows, "expert", axis_index_groups=low, axis=1, tiled=True)
@@ -88,4 +317,5 @@
         P("section", "expert", None, None),
     )
     out_specs = (P("section", None, "expert"), P("section", None, "expert"))
-    return jax.shard_map(body, mesh=mesh, in_specs=in_specs, out_specs=out_specs, check_vma=False)
+    chosen = direct_body if mesh.shape["expert"] == 2 * DBLOCKS else body
+    return jax.shard_map(chosen, mesh=mesh, in_specs=in_specs, out_specs=out_specs, check_vma=False)

time: 295 us -> 216 us (0.73); the launches traced: 295 us -> 212 us
  waiting for transfers between devices: 207 us -> 116 us
  matrix products: 29.6 us -> 0 us
  Pallas kernels: 0 us -> 28.8 us
  starting transfers between devices: 6.73 us -> 33.6 us
  blocking collectives: 19 us -> 0 us
  local copies, waits for them, and re-layouts: 13 us -> 17.1 us
    ppermute x2 -> x16, waiting for transfers between devices: 9.68 us -> 107 us  [the longest x12 92.5 us: swapped(): lax.ppermute(value, 'expert', [(i, i ^ mask) for i in range(devices)])]
    all_gather x4 -> x1, waiting for transfers between devices: 83.9 us -> 8.27 us  [direct_body(): lax.all_gather(grads, 'expert', axis_index_groups=high, axis=0, tiled=False)]
    reduce_scatter x2 -> x1, waiting for transfers between devices: 73.8 us -> 0.01 us  [direct_body(): lax.psum_scatter(pre_b.reshape(-1, size), 'expert', axis_index_groups=hig...]
    unnamed x10 -> x2, waiting for transfers between devices: 39.5 us -> 0.03 us
    dot_general x5 -> x0, matrix products: 29.6 us -> none  [the longest x1 7.43 us: body(): jnp.einsum('cd,kqfd->qkcf', behind_wide, gates, preferred_element_type=F32)]
    pallas_call x0 -> x13, Pallas kernels: none -> 28.8 us  [call(): pl.pallas_call(run, compiler_params=pltpu.CompilerParams(vmem_limit_bytes...]
    ppermute x2 -> x16, starting transfers between devices: 6.23 us -> 33.5 us  [the longest x12 17.1 us: swapped(): lax.ppermute(value, 'expert', [(i, i ^ mask) for i in range(devices)])]
    all_gather x1 -> x0, blocking collectives: 19 us -> none  [spread(): lax.all_gather(values, 'expert', axis_index_groups=high, axis=0, tiled=Fa...]
  transfers between devices with their start and end apart: 10 -> 18, of which waited for: 9 -> 9; matrix products, arithmetic and copies ran while one was open for 15% -> 1% of each run, Pallas kernels for 0% -> 14%
where the time goes in v4:
time: 216 us; the launch traced here: 212 us
  waiting for transfers between devices  116 us (54%)
  starting transfers between devices  33.6 us (16%)
  Pallas kernels  28.8 us (13%)
  local copies, waits for them, and re-layouts  17.1 us (8%)
  between operations  14.3 us (7%)
  other arithmetic  2.86 us (1%)
    ppermute x12, waiting for transfers between devices, swapped(): lax.ppermute(value, 'expert', [(i, i ^ mask) for i in range(devices)])  92.5 us
    pallas_call x13, Pallas kernels, call(): pl.pallas_call(run, compiler_params=pltpu.CompilerParams(vmem_limit_bytes...  28.8 us
    ppermute x12, starting transfers between devices, swapped(): lax.ppermute(value, 'expert', [(i, i ^ mask) for i in range(devices)])  17.1 us
    unnamed x30, local copies, waits for them, and re-layouts  16.8 us
    ppermute x4, starting transfers between devices, to_section(): return lax.ppermute(value, ('section', 'expert'), pairs)  16.5 us
    ppermute x4, waiting for transfers between devices, to_section(): return lax.ppermute(value, ('section', 'expert'), pairs)  14.9 us
    all_gather x1, waiting for transfers between devices, direct_body(): lax.all_gather(grads, 'expert', axis_index_groups=high, axis=0, tiled=False)  8.27 us
  transfers between devices with their start and end apart: 18, of which 9 were waited for; matrix products, arithmetic and copies ran while one was open for 1% of the time, Pallas kernels for 14%

profile of v4, /device:TPU:1, one launch (start us, length us, event | category | flops | bytes accessed | tf_op | source)
XLA Modules:
  0.0 212.4 jit_solution(4719343578750591088)
XLA Ops:
  11.8 12.9 %collective-permute-done.1.refs_2_ = bf16[384,896]{1,0:T(8,128)(2,1)S(1)} collective-permute-done((bf16[384,896]{1,0:T(8,128)(2,1)}, bf16[384,896]{1,0:T(8,128)(2,1)S(1)}, u32[]{:S(2)}, u32[]{:S(2)}) %collective-permute-start.1) | collective-permute-done | bytes 688160 | tf_op jit(solution)/shard_map/ppermute | solution.py:197
  24.7 3.1 %copy-done = bf16[1,1,2,1024,1792]{4,3,2,1,0:T(8,128)(2,1)S(1)} copy-done((bf16[1,1,2,1024,1792]{4,3,2,1,0:T(8,128)(2,1)S(1)}, bf16[1,1,2,1024,1792]{4,3,2,1,0:T(8,128)(2,1)}, u32[]{:S(2)}) %copy-start) | copy-done | bytes 7340056
  28.9 6.2 %shard_map.86.refs_4_ = bf16[4,2,384,256]{3,2,1,0:T(8,128)(2,1)} custom-call(s32[2]{0:T(128)S(1)} %pad_add_fusion.refs_0_, bf16[384,896]{1,0:T(8,128)(2,1)S(1)} %bitcast.34, bf16[384,896]{1,0:T(8,128)(2,1)S(1)} %collective-permute-done.1.refs_2_, bf16[2,1024,1792]{2,1,0:T(8,128)(2,1)S(1)} %bitcast.21), custom_call_target="tpu_custom_call" | custom-call | flops 22799998976 | bytes 1024 | tf_op jit(solution)/shard_map/pallas_call | solution.py:36
  35.1 4.4 %collective-permute-done.refs_2_ = bf16[384,896]{1,0:T(8,128)(2,1)S(1)} collective-permute-done((bf16[384,896]{1,0:T(8,128)(2,1)}, bf16[384,896]{1,0:T(8,128)(2,1)S(1)}, u32[]{:S(2)}, u32[]{:S(2)}) %collective-permute-start) | collective-permute-done | bytes 688160 | tf_op jit(solution)/shard_map/ppermute | solution.py:197
  41.3 2.3 %collective-permute-start.2 = (bf16[1,2,384,256]{3,2,1,0:T(8,128)(2,1)S(1)}, bf16[1,2,384,256]{3,2,1,0:T(8,128)(2,1)S(1)}, u32[]{:S(2)}, u32[]{:S(2)}) collective-permute-start(bf16[1,2,384,256]{3,2,1,0:T(8,128)(2,1)S(1)} %shard_map.87.refs_4_), channel_id=1, source_target_pairs={{0,4},{1,5},{2,6},{3,7},{4,0},{5,1},{6,2},{7,3},{8,12},{9,13},{10,... | collective-permute-start | bytes 1179656 | tf_op jit(solution)/shard_map/ppermute | solution.py:197
  43.6 3.1 %copy-done.2 = bf16[1,1,2,1024,1792]{4,3,2,1,0:T(8,128)(2,1)S(1)} copy-done((bf16[1,1,2,1024,1792]{4,3,2,1,0:T(8,128)(2,1)S(1)}, bf16[1,1,2,1024,1792]{4,3,2,1,0:T(8,128)(2,1)}, u32[]{:S(2)}) %copy-start.2) | copy-done | bytes 7340056
  46.7 2.5 %shard_map.88.refs_4_ = bf16[1,2,384,256]{3,2,1,0:T(8,128)(2,1)} custom-call(s32[2]{0:T(128)S(1)} %pad_add_fusion.refs_0_, bf16[384,896]{1,0:T(8,128)(2,1)S(1)} %bitcast.37, bf16[384,896]{1,0:T(8,128)(2,1)S(1)} %collective-permute-done.refs_2_, bf16[2,1024,1792]{2,1,0:T(8,128)(2,1)S(1)} %bitcast.23, bf16[1,2,384,256]{3,2,1,0:T(8,128)(2,1)S(1)} %shard_map.87.refs_4_), custom_call_target="tpu_custom_call" | custom-call | flops 7200000000 | bytes 1024 | tf_op jit(solution)/shard_map/pallas_call | solution.py:36
  50.3 2.5 %shard_map.89.refs_4_ = bf16[1,2,384,256]{3,2,1,0:T(8,128)(2,1)} custom-call(s32[2]{0:T(128)S(1)} %pad_add_fusion.refs_0_, bf16[384,896]{1,0:T(8,128)(2,1)S(1)} %bitcast.38, bf16[384,896]{1,0:T(8,128)(2,1)S(1)} %collective-permute-done.refs_2_, bf16[2,1024,1792]{2,1,0:T(8,128)(2,1)S(1)} %bitcast.24, bf16[1,2,384,256]{3,2,1,0:T(8,128)(2,1)} %shard_map.88.refs_4_), custom_call_target="tpu_custom_call" | custom-call | flops 7200000000 | bytes 1024 | tf_op jit(solution)/shard_map/pallas_call | solution.py:36
  63.4 52.2 %collective-permute-done.6.refs_2_ = bf16[1,1,384,256]{3,2,1,0:T(8,128)(2,1)S(1)} collective-permute-done((bf16[1,1,384,256]{3,2,1,0:T(8,128)(2,1)S(1)}, bf16[1,1,384,256]{3,2,1,0:T(8,128)(2,1)S(1)}, u32[]{:S(2)}, u32[]{:S(2)}) %collective-permute-start.6) | collective-permute-done | bytes 196640 | tf_op jit(solution)/shard_map/ppermute | solution.py:197
  119.8 4.6 %collective-permute-done.4.refs_2_ = bf16[1,2,384,256]{3,2,1,0:T(8,128)(2,1)S(1)} collective-permute-done((bf16[1,2,384,256]{3,2,1,0:T(8,128)(2,1)}, bf16[1,2,384,256]{3,2,1,0:T(8,128)(2,1)S(1)}, u32[]{:S(2)}, u32[]{:S(2)}) %collective-permute-start.4) | collective-permute-done | bytes 393248 | tf_op jit(solution)/shard_map/ppermute | solution.py:197
  124.7 2.2 %collective-permute-start.9 = (bf16[384,256]{1,0:T(8,128)(2,1)S(1)}, bf16[384,256]{1,0:T(8,128)(2,1)S(1)}, u32[]{:S(2)}, u32[]{:S(2)}) collective-permute-start(bf16[384,256]{1,0:T(8,128)(2,1)S(1)} %shard_map.96.refs_1_), channel_id=1, source_target_pairs={{0,2},{1,3},{2,0},{3,1},{4,6},{5,7},{6,4},{7,5},{8,10},{9,11},{10,... | collective-permute-start | bytes 589832 | tf_op jit(solution)/shard_map/ppermute | solution.py:197
  126.9 3.6 %collective-permute-start.10 = (bf16[384,256]{1,0:T(8,128)(2,1)S(1)}, bf16[384,256]{1,0:T(8,128)(2,1)S(1)}, u32[]{:S(2)}, u32[]{:S(2)}) collective-permute-start(bf16[384,256]{1,0:T(8,128)(2,1)S(1)} %shard_map.96.refs_1_), channel_id=1, source_target_pairs={{0,4},{1,5},{2,6},{3,7},{4,0},{5,1},{6,2},{7,3},{8,12},{9,13},{10,... | collective-permute-start | bytes 589832 | tf_op jit(solution)/shard_map/ppermute | solution.py:197
  130.7 7.5 %collective-permute-done.10.refs_3_ = bf16[384,256]{1,0:T(8,128)(2,1)S(1)} collective-permute-done((bf16[384,256]{1,0:T(8,128)(2,1)S(1)}, bf16[384,256]{1,0:T(8,128)(2,1)S(1)}, u32[]{:S(2)}, u32[]{:S(2)}) %collective-permute-start.10) | collective-permute-done | bytes 196640 | tf_op jit(solution)/shard_map/ppermute | solution.py:197
  138.2 11.0 %collective-permute-done.11.refs_4_ = bf16[384,256]{1,0:T(8,128)(2,1)S(1)} collective-permute-done((bf16[384,256]{1,0:T(8,128)(2,1)S(1)}, bf16[384,256]{1,0:T(8,128)(2,1)S(1)}, u32[]{:S(2)}, u32[]{:S(2)}) %collective-permute-start.11) | collective-permute-done | bytes 196640 | tf_op jit(solution)/shard_map/ppermute | solution.py:197
  151.1 3.1 %shard_map.97 = (bf16[384,896]{1,0:T(8,128)(2,1)S(1)}, bf16[384,896]{1,0:T(8,128)(2,1)S(1)}) custom-call(s32[2]{0:T(128)S(1)} %pad_add_fusion.refs_0_, bf16[384,256]{1,0:T(8,128)(2,1)S(1)} %shard_map.96.refs_1_, bf16[384,256]{1,0:T(8,128)(2,1)S(1)} %collective-permute-done.9.refs_2_, bf16[384,256]{1,0:T(8,128)(2,1)S(1)} %collective-permute-done.10.refs_3_, ...), custom_call_target="tpu_custom_call" | custom-call | flops 16000000000 | bytes 1024 | tf_op jit(solution)/shard_map/pallas_call | solution.py:36
  154.3 8.8 %collective-permute-start.13 = (bf16[384,896]{1,0:T(8,128)(2,1)S(1)}, bf16[384,896]{1,0:T(8,128)(2,1)S(1)}, u32[]{:S(2)}, u32[]{:S(2)}) collective-permute-start(bf16[384,896]{1,0:T(8,128)(2,1)S(1)} %get-tuple-element.7), channel_id=1, source_target_pairs={{0,8},{1,9},{2,10},{3,11},{4,12},{5,13},{6,14},{7,15},{8,16},{9,17... | collective-permute-start | bytes 2064392 | tf_op jit(solution)/shard_map/ppermute | solution.py:206
  163.0 2.9 %collective-permute-start.12 = (bf16[384,896]{1,0:T(8,128)(2,1)S(1)}, bf16[384,896]{1,0:T(8,128)(2,1)S(1)}, u32[]{:S(2)}, u32[]{:S(2)}) collective-permute-start(bf16[384,896]{1,0:T(8,128)(2,1)S(1)} %get-tuple-element.6.refs_3_), channel_id=1, source_target_pairs={{0,9},{1,8},{2,11},{3,10},{4,13},{5,12},{6,15},{7,14},{8,17},{9,16... | collective-permute-start | bytes 2064392 | tf_op jit(solution)/shard_map/ppermute | solution.py:206
  166.0 8.3 %all-gather.3.cloned.1.call-done = bf16[8,384,256]{2,1,0:T(8,128)(2,1)} async-done(((bf16[2,384,256]{2,1,0:T(8,128)(2,1)}), bf16[8,384,256]{2,1,0:T(8,128)(2,1)}) %all-gather.3.cloned.1.call-update) | async-done | bytes 1572880 | tf_op jit(solution)/shard_map/all_gather | solution.py:238
  174.2 3.1 %copy-done.3 = bf16[1,1,2,1024,1792]{4,3,2,1,0:T(8,128)(2,1)S(1)} copy-done((bf16[1,1,2,1024,1792]{4,3,2,1,0:T(8,128)(2,1)S(1)}, bf16[1,1,2,1024,1792]{4,3,2,1,0:T(8,128)(2,1)}, u32[]{:S(2)}) %copy-start.3) | copy-done | bytes 7340056
  178.7 5.1 %shard_map.98 = (bf16[384,896]{1,0:T(8,128)(2,1)S(1)}, bf16[384,896]{1,0:T(8,128)(2,1)S(1)}) custom-call(s32[2]{0:T(128)S(1)} %pad_add_fusion.refs_0_, bf16[4,2,384,256]{3,2,1,0:T(8,128)(2,1)S(1)} %bitcast.32, bf16[2,1024,1792]{2,1,0:T(8,128)(2,1)S(1)} %bitcast.26, bf16[384,896]{1,0:T(8,128)(2,1)S(1)} %get-tuple-element.6.refs_3_), custom_call_target="tpu_custom_call" | custom-call | flops 28000000000 | bytes 1024 | tf_op jit(solution)/shard_map/pallas_call | solution.py:36
  183.8 2.4 %collective-permute-start.15 = (bf16[384,896]{1,0:T(8,128)(2,1)S(1)}, bf16[384,896]{1,0:T(8,128)(2,1)S(1)}, u32[]{:S(2)}, u32[]{:S(2)}) collective-permute-start(bf16[384,896]{1,0:T(8,128)(2,1)S(1)} %get-tuple-element.9), channel_id=1, source_target_pairs={{8,0},{9,1},{10,2},{11,3},{12,4},{13,5},{14,6},{15,7},{16,8},{17,9... | collective-permute-start | bytes 2064392 | tf_op jit(solution)/shard_map/ppermute | solution.py:206
  186.2 2.4 %collective-permute-start.14 = (bf16[384,896]{1,0:T(8,128)(2,1)S(1)}, bf16[384,896]{1,0:T(8,128)(2,1)S(1)}, u32[]{:S(2)}, u32[]{:S(2)}) collective-permute-start(bf16[384,896]{1,0:T(8,128)(2,1)S(1)} %get-tuple-element.8), channel_id=1, source_target_pairs={{8,1},{9,0},{10,3},{11,2},{12,5},{13,4},{14,7},{15,6},{16,9},{17,8... | collective-permute-start | bytes 2064392 | tf_op jit(solution)/shard_map/ppermute | solution.py:206
  189.7 6.7 %collective-permute-done.15 = bf16[384,896]{1,0:T(8,128)(2,1)S(1)} collective-permute-done((bf16[384,896]{1,0:T(8,128)(2,1)S(1)}, bf16[384,896]{1,0:T(8,128)(2,1)S(1)}, u32[]{:S(2)}, u32[]{:S(2)}) %collective-permute-start.15) | collective-permute-done | bytes 688160 | tf_op jit(solution)/shard_map/ppermute | solution.py:206
  196.4 8.1 %collective-permute-done.14 = bf16[384,896]{1,0:T(8,128)(2,1)S(1)} collective-permute-done((bf16[384,896]{1,0:T(8,128)(2,1)S(1)}, bf16[384,896]{1,0:T(8,128)(2,1)S(1)}, u32[]{:S(2)}, u32[]{:S(2)}) %collective-permute-start.14) | collective-permute-done | bytes 688160 | tf_op jit(solution)/shard_map/ppermute | solution.py:206
  (64 shorter events, 29.3 us)
Async XLA Ops:
  7.2 109.6 %reduce-scatter.2.cloned.1.call-start = ((), (), s32[]{:S(2)}) async-start(), calls=%async_computation.1 | async-start | bytes 1966080 | tf_op jit(solution)/shard_map/reduce_scatter | solution.py:217
  7.2 17.5 %collective-permute-start.1 = (bf16[384,896]{1,0:T(8,128)(2,1)}, bf16[384,896]{1,0:T(8,128)(2,1)S(1)}, u32[]{:S(2)}, u32[]{:S(2)}) collective-permute-start(bf16[384,896]{1,0:T(8,128)(2,1)} %bitcast.33), channel_id=1, source_target_pairs={{0,1},{1,0},{2,3},{3,2},{4,5},{5,4},{6,7},{7,6},{8,9},{9,8},{10,11... | collective-permute-start | bytes 2064392 | tf_op jit(solution)/shard_map/ppermute | solution.py:197
  9.3 30.1 %collective-permute-start = (bf16[384,896]{1,0:T(8,128)(2,1)}, bf16[384,896]{1,0:T(8,128)(2,1)S(1)}, u32[]{:S(2)}, u32[]{:S(2)}) collective-permute-start(bf16[384,896]{1,0:T(8,128)(2,1)} %bitcast.35), channel_id=1, source_target_pairs={{0,1},{1,0},{2,3},{3,2},{4,5},{5,4},{6,7},{7,6},{8,9},{9,8},{10,11... | collective-permute-start | bytes 2064392 | tf_op jit(solution)/shard_map/ppermute | solution.py:197
  9.4 45.2 %collective-permute-start.5 = (bf16[384,896]{1,0:T(8,128)(2,1)}, bf16[384,896]{1,0:T(8,128)(2,1)S(1)}, u32[]{:S(2)}, u32[]{:S(2)}) collective-permute-start(bf16[384,896]{1,0:T(8,128)(2,1)} %bitcast.40), channel_id=1, source_target_pairs={{0,1},{1,0},{2,3},{3,2},{4,5},{5,4},{6,7},{7,6},{8,9},{9,8},{10,11... | collective-permute-start | bytes 2064392 | tf_op jit(solution)/shard_map/ppermute | solution.py:197
  24.7 3.1 %copy-start = (bf16[1,1,2,1024,1792]{4,3,2,1,0:T(8,128)(2,1)S(1)}, bf16[1,1,2,1024,1792]{4,3,2,1,0:T(8,128)(2,1)}, u32[]{:S(2)}) copy-start(bf16[1,1,2,1024,1792]{4,3,2,1,0:T(8,128)(2,1)} %param.12) | copy-start | bytes 22020100
  28.9 10.6 %copy-start.1 = (bf16[1,1,2,1024,1792]{4,3,2,1,0:T(8,128)(2,1)S(1)}, bf16[1,1,2,1024,1792]{4,3,2,1,0:T(8,128)(2,1)}, u32[]{:S(2)}) copy-start(bf16[1,1,2,1024,1792]{4,3,2,1,0:T(8,128)(2,1)} %param.12) | copy-start | bytes 22020100
  28.9 10.6 %copy-start.8 = (bf16[1,384,896]{2,1,0:T(8,128)(2,1)S(1)}, bf16[1,384,896]{2,1,0:T(8,128)(2,1)}, u32[]{:S(2)}) copy-start(bf16[1,384,896]{2,1,0:T(8,128)(2,1)} %param.7) | copy-start | bytes 2064388
  41.3 78.5 %collective-permute-start.2 = (bf16[1,2,384,256]{3,2,1,0:T(8,128)(2,1)S(1)}, bf16[1,2,384,256]{3,2,1,0:T(8,128)(2,1)S(1)}, u32[]{:S(2)}, u32[]{:S(2)}) collective-permute-start(bf16[1,2,384,256]{3,2,1,0:T(8,128)(2,1)S(1)} %shard_map.87.refs_4_), channel_id=1, source_target_pairs={{0,4},{1,5},{2,6},{3,7},{4,0},{5,1},{6,2},{7,3},{8,12},{9,13},{10,... | collective-permute-start | bytes 1179656 | tf_op jit(solution)/shard_map/ppermute | solution.py:197
  43.6 130.6 %all-gather.3.cloned.1.call-start = ((), (), s32[]{:S(2)}) async-start(), calls=%async_computation.2 | async-start | bytes 1966080 | tf_op jit(solution)/shard_map/all_gather | solution.py:238
  43.6 3.1 %copy-start.2 = (bf16[1,1,2,1024,1792]{4,3,2,1,0:T(8,128)(2,1)S(1)}, bf16[1,1,2,1024,1792]{4,3,2,1,0:T(8,128)(2,1)}, u32[]{:S(2)}) copy-start(bf16[1,1,2,1024,1792]{4,3,2,1,0:T(8,128)(2,1)} %param.12) | copy-start | bytes 22020100
  49.2 70.6 %collective-permute-start.3 = (bf16[1,2,384,256]{3,2,1,0:T(8,128)(2,1)}, bf16[1,2,384,256]{3,2,1,0:T(8,128)(2,1)S(1)}, u32[]{:S(2)}, u32[]{:S(2)}) collective-permute-start(bf16[1,2,384,256]{3,2,1,0:T(8,128)(2,1)} %shard_map.88.refs_4_), channel_id=1, source_target_pairs={{0,6},{1,7},{2,4},{3,5},{4,2},{5,3},{6,0},{7,1},{8,14},{9,15},{10,... | collective-permute-start | bytes 1179656 | tf_op jit(solution)/shard_map/ppermute | solution.py:197
  56.1 59.4 %collective-permute-start.6 = (bf16[1,1,384,256]{3,2,1,0:T(8,128)(2,1)S(1)}, bf16[1,1,384,256]{3,2,1,0:T(8,128)(2,1)S(1)}, u32[]{:S(2)}, u32[]{:S(2)}) collective-permute-start(bf16[1,1,384,256]{3,2,1,0:T(8,128)(2,1)S(1)} %shard_map.91.refs_4_), channel_id=1, source_target_pairs={{0,4},{1,5},{2,6},{3,7},{4,0},{5,1},{6,2},{7,3},{8,12},{9,13},{10,... | collective-permute-start | bytes 589832 | tf_op jit(solution)/shard_map/ppermute | solution.py:197
  58.9 57.9 %collective-permute-start.7 = (bf16[1,1,384,256]{3,2,1,0:T(8,128)(2,1)S(1)}, bf16[1,1,384,256]{3,2,1,0:T(8,128)(2,1)S(1)}, u32[]{:S(2)}, u32[]{:S(2)}) collective-permute-start(bf16[1,1,384,256]{3,2,1,0:T(8,128)(2,1)S(1)} %shard_map.92.refs_4_), channel_id=1, source_target_pairs={{0,6},{1,7},{2,4},{3,5},{4,2},{5,3},{6,0},{7,1},{8,14},{9,15},{10,... | collective-permute-start | bytes 589832 | tf_op jit(solution)/shard_map/ppermute | solution.py:197
  61.2 55.6 %collective-permute-start.8 = (bf16[1,1,384,256]{3,2,1,0:T(8,128)(2,1)S(1)}, bf16[1,1,384,256]{3,2,1,0:T(8,128)(2,1)S(1)}, u32[]{:S(2)}, u32[]{:S(2)}) collective-permute-start(bf16[1,1,384,256]{3,2,1,0:T(8,128)(2,1)S(1)} %shard_map.93.refs_4_), channel_id=1, source_target_pairs={{0,2},{1,3},{2,0},{3,1},{4,6},{5,7},{6,4},{7,5},{8,10},{9,11},{10,... | collective-permute-start | bytes 589832 | tf_op jit(solution)/shard_map/ppermute | solution.py:197
  115.6 8.9 %collective-permute-start.4 = (bf16[1,2,384,256]{3,2,1,0:T(8,128)(2,1)}, bf16[1,2,384,256]{3,2,1,0:T(8,128)(2,1)S(1)}, u32[]{:S(2)}, u32[]{:S(2)}) collective-permute-start(bf16[1,2,384,256]{3,2,1,0:T(8,128)(2,1)} %shard_map.89.refs_4_), channel_id=1, source_target_pairs={{0,2},{1,3},{2,0},{3,1},{4,6},{5,7},{6,4},{7,5},{8,10},{9,11},{10,... | collective-permute-start | bytes 1179656 | tf_op jit(solution)/shard_map/ppermute | solution.py:197
  118.7 5.7 %copy-start.12 = (bf16[1,2,384,256]{3,2,1,0:T(8,128)(2,1)S(1)}, bf16[1,2,384,256]{3,2,1,0:T(8,128)(2,1)}, u32[]{:S(2)}) copy-start(bf16[1,2,384,256]{3,2,1,0:T(8,128)(2,1)} %copy-done.11) | copy-start | bytes 1179652
  124.7 6.0 %collective-permute-start.9 = (bf16[384,256]{1,0:T(8,128)(2,1)S(1)}, bf16[384,256]{1,0:T(8,128)(2,1)S(1)}, u32[]{:S(2)}, u32[]{:S(2)}) collective-permute-start(bf16[384,256]{1,0:T(8,128)(2,1)S(1)} %shard_map.96.refs_1_), channel_id=1, source_target_pairs={{0,2},{1,3},{2,0},{3,1},{4,6},{5,7},{6,4},{7,5},{8,10},{9,11},{10,... | collective-permute-start | bytes 589832 | tf_op jit(solution)/shard_map/ppermute | solution.py:197
  126.9 11.3 %collective-permute-start.10 = (bf16[384,256]{1,0:T(8,128)(2,1)S(1)}, bf16[384,256]{1,0:T(8,128)(2,1)S(1)}, u32[]{:S(2)}, u32[]{:S(2)}) collective-permute-start(bf16[384,256]{1,0:T(8,128)(2,1)S(1)} %shard_map.96.refs_1_), channel_id=1, source_target_pairs={{0,4},{1,5},{2,6},{3,7},{4,0},{5,1},{6,2},{7,3},{8,12},{9,13},{10,... | collective-permute-start | bytes 589832 | tf_op jit(solution)/shard_map/ppermute | solution.py:197
  130.5 18.6 %collective-permute-start.11 = (bf16[384,256]{1,0:T(8,128)(2,1)S(1)}, bf16[384,256]{1,0:T(8,128)(2,1)S(1)}, u32[]{:S(2)}, u32[]{:S(2)}) collective-permute-start(bf16[384,256]{1,0:T(8,128)(2,1)S(1)} %shard_map.96.refs_1_), channel_id=1, source_target_pairs={{0,6},{1,7},{2,4},{3,5},{4,2},{5,3},{6,0},{7,1},{8,14},{9,15},{10,... | collective-permute-start | bytes 589832 | tf_op jit(solution)/shard_map/ppermute | solution.py:197
  154.3 34.4 %collective-permute-start.13 = (bf16[384,896]{1,0:T(8,128)(2,1)S(1)}, bf16[384,896]{1,0:T(8,128)(2,1)S(1)}, u32[]{:S(2)}, u32[]{:S(2)}) collective-permute-start(bf16[384,896]{1,0:T(8,128)(2,1)S(1)} %get-tuple-element.7), channel_id=1, source_target_pairs={{0,8},{1,9},{2,10},{3,11},{4,12},{5,13},{6,14},{7,15},{8,16},{9,17... | collective-permute-start | bytes 2064392 | tf_op jit(solution)/shard_map/ppermute | solution.py:206
  163.0 25.6 %collective-permute-start.12 = (bf16[384,896]{1,0:T(8,128)(2,1)S(1)}, bf16[384,896]{1,0:T(8,128)(2,1)S(1)}, u32[]{:S(2)}, u32[]{:S(2)}) collective-permute-start(bf16[384,896]{1,0:T(8,128)(2,1)S(1)} %get-tuple-element.6.refs_3_), channel_id=1, source_target_pairs={{0,9},{1,8},{2,11},{3,10},{4,13},{5,12},{6,15},{7,14},{8,17},{9,16... | collective-permute-start | bytes 2064392 | tf_op jit(solution)/shard_map/ppermute | solution.py:206
  174.2 3.1 %copy-start.3 = (bf16[1,1,2,1024,1792]{4,3,2,1,0:T(8,128)(2,1)S(1)}, bf16[1,1,2,1024,1792]{4,3,2,1,0:T(8,128)(2,1)}, u32[]{:S(2)}) copy-start(bf16[1,1,2,1024,1792]{4,3,2,1,0:T(8,128)(2,1)} %param.12) | copy-start | bytes 22020100
  183.8 12.6 %collective-permute-start.15 = (bf16[384,896]{1,0:T(8,128)(2,1)S(1)}, bf16[384,896]{1,0:T(8,128)(2,1)S(1)}, u32[]{:S(2)}, u32[]{:S(2)}) collective-permute-start(bf16[384,896]{1,0:T(8,128)(2,1)S(1)} %get-tuple-element.9), channel_id=1, source_target_pairs={{8,0},{9,1},{10,2},{11,3},{12,4},{13,5},{14,6},{15,7},{16,8},{17,9... | collective-permute-start | bytes 2064392 | tf_op jit(solution)/shard_map/ppermute | solution.py:206
  186.2 18.3 %collective-permute-start.14 = (bf16[384,896]{1,0:T(8,128)(2,1)S(1)}, bf16[384,896]{1,0:T(8,128)(2,1)S(1)}, u32[]{:S(2)}, u32[]{:S(2)}) collective-permute-start(bf16[384,896]{1,0:T(8,128)(2,1)S(1)} %get-tuple-element.8), channel_id=1, source_target_pairs={{8,1},{9,0},{10,3},{11,2},{12,5},{13,4},{14,7},{15,6},{16,9},{17,8... | collective-permute-start | bytes 2064392 | tf_op jit(solution)/shard_map/ppermute | solution.py:206
  (9 other events, 12.9 us)
Sparse Core Ops, SparseCore 0:
  43.7 60.0 reduce-scatter.1
  119.9 54.2 all-gather.2

commit v5 on v1

--- a/solution.py
+++ b/solution.py
@@ -1,17 +1,389 @@
+import functools
+
 import jax
 import jax.numpy as jnp
 from jax import lax
+from jax.experimental import pallas as pl
+from jax.experimental.pallas import tpu as pltpu
 from jax.sharding import PartitionSpec as P
 
 DBLOCKS = 4
 BF16 = jnp.bfloat16
 F32 = jnp.float32
+MIB = 1024 * 1024
+PIECES = 2
 
 
 def shift(shard, axis, by):
     devices = lax.axis_size(axis)
     pairs = [(i, i + by) for i in range(devices) if 0 <= i + by < devices]
     return lax.ppermute(shard, axis, pairs)
+
+
+def whole(array):
+    return pl.BlockSpec(array.shape, functools.partial(lambda n, *_: (0,) * n, array.ndim))
+
+
+def call(kernel, micros, operands, after, out_shape, scalars=(), grid=(1,), in_specs=None, out_specs=None, scratch=(), limit=24):
+    count, unread = len(scalars) + len(operands), len(after)
+
+    def run(*refs):
+        kernel(*refs[:count], *refs[count + unread :])
+
+    if in_specs is None:
+        in_specs = [whole(o) for o in operands]
+    if out_specs is None:
+        out_specs = jax.tree.map(whole, out_shape)
+    return pl.pallas_call(
+        run,
+        compiler_params=pltpu.CompilerParams(vmem_limit_bytes=limit * MIB),
+        cost_estimate=pl.CostEstimate(flops=int(micros * 4e9), bytes_accessed=1024, transcendentals=0),
+        out_shape=out_shape,
+        grid_spec=pltpu.PrefetchScalarGridSpec(
+            num_scalar_prefetch=len(scalars),
+            grid=grid,
+            in_specs=[*in_specs, *[pl.BlockSpec(memory_space=pl.ANY)] * unread],
+            out_specs=out_specs,
+            scratch_shapes=list(scratch),
+        ),
+    )(*scalars, *operands, *after)
+
+
+def first_kernel(width, where, own, partner, tile, out, joined):
+    @pl.when((pl.program_id(0) == 0) & (pl.program_id(1) == 0))
+    def _():
+        at = pl.multiple_of(where[1] * width, 128)
+        other = pl.multiple_of((1 - where[1]) * width, 128)
+        joined[:, pl.ds(at, width)] = own[...]
+        joined[:, pl.ds(other, width)] = partner[...]
+
+    out[0] = lax.dot_general(
+        joined[...], tile[0], (((1,), (1,)), ((), ())), preferred_element_type=F32
+    ).astype(BF16)
+
+
+def behind_first_kernel(width, where, own, partner, grad, grad_partner, tile, down, out, joined, joined_grad):
+    at = pl.multiple_of(where[1] * width, 128)
+    other = pl.multiple_of((1 - where[1]) * width, 128)
+
+    @pl.when((pl.program_id(0) == 0) & (pl.program_id(1) == 0))
+    def _():
+        joined[:, pl.ds(at, width)] = own[...]
+        joined[:, pl.ds(other, width)] = partner[...]
+        joined_grad[:, pl.ds(at, width)] = grad[...]
+        joined_grad[:, pl.ds(other, width)] = grad_partner[...]
+
+    @pl.when(pl.program_id(0) < 2)
+    def _():
+        out[0] = lax.dot_general(
+            joined[...], tile[0], (((1,), (1,)), ((), ())), preferred_element_type=F32
+        ).astype(BF16)
+
+    @pl.when(pl.program_id(0) == 2)
+    def _():
+        out[0] = lax.dot_general(
+            joined_grad[...], down[...], (((1,), (1,)), ((), ())), preferred_element_type=F32
+        ).astype(BF16)
+
+
+def first_product(where, far, rows, gates, downs, after):
+    slots, width = rows[0].shape
+    units, features = gates.shape[1:]
+    half = units // 2
+    tile = min(256, half)
+    steps = half // tile
+    parts = 1 + len(rows) // 2
+
+    def side(w):
+        return (1 - w[0]) * steps if far else w[0] * steps
+
+    def gate_at(k, j, w):
+        return (jnp.minimum(k, 1), side(w) + jnp.where(k < 2, j, steps - 1), 0)
+
+    def down_at(k, j, w):
+        return (side(w) + jnp.where(k < 2, 0, j), 0)
+
+    in_specs = [whole(r) for r in rows] + [pl.BlockSpec((1, tile, features), gate_at)]
+    operands = [*rows, gates]
+    if parts == 3:
+        in_specs.append(pl.BlockSpec((tile, features), down_at))
+        operands.append(downs)
+    return call(
+        functools.partial(behind_first_kernel if parts == 3 else first_kernel, width),
+        1.3 * parts,
+        operands,
+        after,
+        jax.ShapeDtypeStruct((parts, slots, half), BF16),
+        scalars=(where,),
+        grid=(parts, steps),
+        in_specs=in_specs,
+        out_specs=pl.BlockSpec((1, slots, tile), lambda k, j, w: (k, 0, j)),
+        scratch=[pltpu.VMEM((slots, features), BF16)] * (parts - 1),
+    )
+
+
+def sum_kernel(mine, arrived, out):
+    out[...] = (mine[...].astype(F32) + arrived[...].astype(F32)).astype(BF16)
+
+
+def end_or_sum_kernel(where, at_end, mine, arrived, out):
+    @pl.when(where[2] == 1)
+    def _():
+        parts = at_end.shape[0]
+        out[:parts] = at_end[...]
+        if parts < out.shape[0]:
+            out[parts:] = jnp.zeros_like(out[parts:])
+
+    @pl.when(where[2] == 0)
+    def _():
+        out[...] = (mine[...].astype(F32) + arrived[...].astype(F32)).astype(BF16)
+
+
+def end_or_pass_kernel(where, at_end, passed, out):
+    @pl.when(where[2] == 1)
+    def _():
+        out[...] = at_end[...]
+
+    @pl.when(where[2] == 0)
+    def _():
+        out[...] = passed[...]
+
+
+def ahead_act_kernel(near, arrived, out):
+    gate = near[0].astype(F32) + arrived[0].astype(F32)
+    up = near[1].astype(F32) + arrived[1].astype(F32)
+    out[0] = (gate * jax.nn.sigmoid(gate) * up).astype(BF16)
+
+
+def behind_act_kernel(near, arrived, scale, out):
+    gate = near[0].astype(F32) + arrived[0].astype(F32)
+    up = near[1].astype(F32) + arrived[1].astype(F32)
+    expanded = (near[2].astype(F32) + arrived[2].astype(F32)) * scale[...]
+    sig = jax.nn.sigmoid(gate)
+    out[0] = (expanded * up * sig * (1.0 + gate * (1.0 - sig))).astype(BF16)
+    out[1] = (expanded * gate * sig).astype(BF16)
+
+
+def second_kernel(scaled, where, act, one, two, three, *refs):
+    scale, refs = (refs[0], refs[1:]) if scaled else (None, refs)
+    tile, give, keep, joined = refs
+    kinds, _, half = act.shape
+
+    def place(near, far):
+        for kind in range(kinds):
+            at = pl.multiple_of((2 * kind + where[0]) * half, 128)
+            other = pl.multiple_of((2 * kind + 1 - where[0]) * half, 128)
+            joined[:, pl.ds(at, half)] = near[kind]
+            joined[:, pl.ds(other, half)] = far[kind]
+
+    first = pl.program_id(0) == 0
+
+    @pl.when(first & (where[2] == 1))
+    def _():
+        place(act, three)
+
+    @pl.when(first & (where[2] == 0))
+    def _():
+        place(one, two)
+
+    kinds, units, width = tile.shape
+    share = jnp.dot(
+        joined[...], tile[...].reshape(kinds * units, width), preferred_element_type=F32
+    )
+    if scaled:
+        share = share * scale[...]
+
+    @pl.when(first)
+    def _():
+        give[...] = share.astype(BF16)
+
+    @pl.when(pl.program_id(0) == 1)
+    def _():
+        keep[...] = share.astype(BF16)
+
+
+def second_product(where, values, scale, weights, after):
+    kinds, units, features = weights.shape
+    slots = values[0].shape[1]
+    width = features // 2
+
+    def tile_at(own, w):
+        return (0, 0, jnp.where(own == 0, 1 - w[1], w[1]))
+
+    operands = [*values] + ([] if scale is None else [scale])
+    share = jax.ShapeDtypeStruct((slots, width), BF16)
+    return call(
+        functools.partial(second_kernel, scale is not None),
+        1 + 2 * kinds,
+        (*operands, weights),
+        after,
+        (share, share),
+        scalars=(where,),
+        grid=(2,),
+        in_specs=[*[whole(v) for v in operands], pl.BlockSpec((kinds, units, width), tile_at)],
+        scratch=[pltpu.VMEM((slots, kinds * units), BF16)],
+    )
+
+
+def chain_body(ahead_rows, behind_rows, behind_grad, route_scores, route_counts, gate_up, down_proj):
+    height = ahead_rows.shape[1]
+    gates = gate_up[0, 0]
+    downs = down_proj[0]
+    own = lax.axis_index("expert")
+    sections = lax.axis_size("section")
+    devices = 2 * DBLOCKS
+    block, group = own // 2, own % 2
+    near_half = (block >= DBLOCKS // 2).astype(jnp.int32)
+    at_end = ((block == 0) | (block == DBLOCKS - 1)).astype(jnp.int32)
+    where = jnp.stack([near_half, group, at_end])
+    slot_ids = jnp.arange(height, dtype=jnp.int32)[None]
+    live = slot_ids < route_counts[0][:, None]
+    scales = jnp.where(live, route_scores[0], 0.0)[:, :, None]
+
+    def between(value, to):
+        pairs = [(q * 2 + f, to[q] * 2 + f) for q in range(DBLOCKS) for f in range(2)]
+        return lax.ppermute(value, "expert", pairs)
+
+    def outer(value):
+        return between(value, (1, 0, 3, 2))
+
+    def middle(value):
+        return between(value, (0, 2, 1, 3))
+
+    def swapped(value):
+        return lax.ppermute(value, "expert", [(i, i ^ 1) for i in range(devices)])
+
+    def to_section(value, by, flip):
+        pairs = [
+            (s * devices + e, (s + by) * devices + (e ^ flip))
+            for s in range(sections)
+            if 0 <= s + by < sections
+            for e in range(devices)
+        ]
+        return lax.ppermute(value, ("section", "expert"), pairs)
+
+    recent = []
+
+    def kernel_call(kernel, micros, operands, shape, scalars=()):
+        made = call(kernel, micros, operands, list(recent), jax.ShapeDtypeStruct(shape, BF16), scalars)
+        recent[:] = [made]
+        return made
+
+    class Chain:
+        def __init__(self, inputs, scale, by):
+            self.inputs, self.scale, self.by = inputs, scale, by
+            self.parts = 1 + len(inputs)
+            self.rows, self.far, self.near, self.act = {}, {}, {}, {}
+            self.out, self.mid, self.one, self.shares = {}, {}, {}, {}
+
+        def cut(self, array, c):
+            size = height // PIECES
+            return array[c * size : (c + 1) * size]
+
+        def fetch(self, c):
+            rows = [self.cut(array, c) for array in self.inputs]
+            self.rows[c] = [r for row in rows for r in (row, swapped(row))]
+
+        def product(self, c, far):
+            made = first_product(where, far, self.rows[c], gates, downs[0], list(recent))
+            recent[:] = [made]
+            (self.far if far else self.near)[c] = made
+
+        def outer_sum(self, c):
+            if c == 0:
+                value = self.far[0]
+            else:
+                first = self.far[c] if c < PIECES else self.act[0]
+                mine = self.near[c - 1]
+                value = kernel_call(
+                    end_or_sum_kernel, 0.4, (first, mine, self.mid[c - 1]), mine.shape, (where,)
+                )
+            self.out[c] = outer(value)
+
+        def middle_sum(self, c):
+            mine = self.far[c]
+            self.mid[c] = middle(kernel_call(sum_kernel, 0.4, (mine, self.out[c]), mine.shape))
+
+        def activate(self, c):
+            near = self.near[c]
+            operands = [near, self.out[c + 1]]
+            kernel = ahead_act_kernel
+            if self.parts == 3:
+                operands.append(self.cut(self.scale, c))
+                kernel = behind_act_kernel
+            shape = (self.parts - 1, *near.shape[1:])
+            self.act[c] = kernel_call(kernel, 0.8, operands, shape)
+
+        def outer_pass(self, c):
+            value = self.mid[PIECES + c - 1]
+            if c < PIECES:
+                value = kernel_call(
+                    end_or_pass_kernel, 0.3, (self.act[c], value), value.shape, (where,)
+                )
+            self.out[PIECES + c] = outer(value)
+
+        def middle_pass(self, c):
+            value = self.out[PIECES + c]
+            if c == 0:
+                value = value[: self.parts - 1]
+            self.one[c] = value
+            self.mid[PIECES + c] = middle(value)
+
+        def finish(self, c):
+            values = [
+                self.act[c],
+                self.one[c],
+                self.mid[PIECES + c],
+                self.out[PIECES + c + 1],
+            ]
+            scaled = self.parts == 2
+            scale = self.cut(self.scale, c) if scaled else None
+            weights = downs if scaled else gates
+            give, keep = second_product(where, values, scale, weights, list(recent))
+            recent[:] = [give]
+            arrived = to_section(give, self.by, 1), to_section(keep, self.by, 0)
+            self.shares[c] = arrived
+
+        def result(self):
+            sums = [
+                (a.astype(F32) + b.astype(F32)).astype(BF16)
+                for a, b in (self.shares[c] for c in range(PIECES))
+            ]
+            return jnp.concatenate(sums)[None]
+
+    ahead = Chain([ahead_rows[0]], scales[0], 1)
+    behind = Chain([behind_rows[0], behind_grad[0]], scales[1], -1)
+    both = (ahead, behind)
+    for c in range(PIECES):
+        for chain in both:
+            chain.fetch(c)
+    for chain in both:
+        chain.product(0, True)
+        chain.outer_sum(0)
+        chain.product(0, False)
+    for c in range(PIECES):
+        for chain in both:
+            chain.middle_sum(c)
+            if c > 0:
+                chain.activate(c - 1)
+            if c + 1 < PIECES:
+                chain.product(c + 1, True)
+        for chain in both:
+            chain.outer_sum(c + 1)
+            if c + 1 < PIECES:
+                chain.product(c + 1, False)
+    for c in range(PIECES):
+        for chain in both:
+            chain.middle_pass(c)
+            if c == 0:
+                chain.activate(PIECES - 1)
+            else:
+                chain.finish(c - 1)
+        for chain in both:
+            chain.outer_pass(c + 1)
+    for chain in both:
+        chain.finish(PIECES - 1)
+    return ahead.result(), behind.result()
 
 
 def body(ahead_rows, behind_rows, behind_grad, route_scores, route_counts, gate_up, down_proj):
@@ -24,8 +396,6 @@
     weights_out = down_proj[0, 0]
     units = weights_in.shape[1]
     part = units // DBLOCKS
-    own = lax.axis_index("expert")
-    block = own // fgroups
 
     def wide(rows):
         return lax.all_gather(rows, "expert", axis_index_groups=low, axis=1, tiled=True)
@@ -88,4 +458,5 @@
         P("section", "expert", None, None),
     )
     out_specs = (P("section", None, "expert"), P("section", None, "expert"))
-    return jax.shard_map(body, mesh=mesh, in_specs=in_specs, out_specs=out_specs, check_vma=False)
+    chosen = chain_body if mesh.shape["expert"] == 2 * DBLOCKS else body
+    return jax.shard_map(chosen, mesh=mesh, in_specs=in_specs, out_specs=out_specs, check_vma=False)

time: 295 us -> 175 us (0.59)
  waiting for transfers between devices: 207 us -> 40.4 us
  starting transfers between devices: 6.73 us -> 75.2 us
  Pallas kernels: 0 us -> 43.9 us
  matrix products: 29.6 us -> 0 us
  blocking collectives: 19 us -> 0 us
  between operations: 14.2 us -> 1.39 us
    all_gather x4 -> x0, waiting for transfers between devices: 83.9 us -> none  [the longest x3 65.6 us: wide(): lax.all_gather(rows, 'expert', axis_index_groups=low, axis=1, tiled=True)]
    reduce_scatter x2 -> x0, waiting for transfers between devices: 73.8 us -> none  [reduced(): lax.psum_scatter(flat, 'expert', axis_index_groups=high, scatter_dimensio...]
    ppermute x2 -> x32, starting transfers between devices: 6.23 us -> 75.2 us  [the longest x18 36.8 us: between(): return lax.ppermute(value, 'expert', pairs)]
    pallas_call x0 -> x26, Pallas kernels: none -> 43.9 us  [call(): pl.pallas_call(run, compiler_params=pltpu.CompilerParams(vmem_limit_bytes...]
    unnamed x10 -> x0, waiting for transfers between devices: 39.5 us -> none
    ppermute x2 -> x32, waiting for transfers between devices: 9.68 us -> 40.4 us  [the longest x18 26.8 us: between(): return lax.ppermute(value, 'expert', pairs)]
    dot_general x5 -> x0, matrix products: 29.6 us -> none  [the longest x1 7.43 us: body(): jnp.einsum('cd,kqfd->qkcf', behind_wide, gates, preferred_element_type=F32)]
    all_gather x1 -> x0, blocking collectives: 19 us -> none  [spread(): lax.all_gather(values, 'expert', axis_index_groups=high, axis=0, tiled=Fa...]
  transfers between devices with their start and end apart: 10 -> 32, of which waited for: 9 -> 10; matrix products, arithmetic and copies ran while one was open for 15% -> 1% of each run, Pallas kernels for 0% -> 25%
where the time goes in v5:
time: 175 us; the launch traced here: 174 us
  starting transfers between devices  75.2 us (43%)
  Pallas kernels  43.9 us (25%)
  waiting for transfers between devices  40.4 us (23%)
  local copies, waits for them, and re-layouts  10.7 us (6%)
  other arithmetic  2.31 us (1%)
    pallas_call x26, Pallas kernels, call(): pl.pallas_call(run, compiler_params=pltpu.CompilerParams(vmem_limit_bytes...  43.9 us
    ppermute x18, starting transfers between devices, between(): return lax.ppermute(value, 'expert', pairs)  36.8 us
    ppermute x8, starting transfers between devices, to_section(): return lax.ppermute(value, ('section', 'expert'), pairs)  32.1 us
    ppermute x18, waiting for transfers between devices, between(): return lax.ppermute(value, 'expert', pairs)  26.8 us
    unnamed x48, local copies, waits for them, and re-layouts  8.81 us
    ppermute x6, waiting for transfers between devices, swapped(): return lax.ppermute(value, 'expert', [(i, i ^ 1) for i in range(devices)])  7.82 us
    ppermute x6, starting transfers between devices, swapped(): return lax.ppermute(value, 'expert', [(i, i ^ 1) for i in range(devices)])  6.34 us
    ppermute x8, waiting for transfers between devices, to_section(): return lax.ppermute(value, ('section', 'expert'), pairs)  5.76 us
  transfers between devices with their start and end apart: 32, of which 10 were waited for; matrix products, arithmetic and copies ran while one was open for 1% of the time, Pallas kernels for 25%

profile of v5, /device:TPU:1, one launch (start us, length us, event | category | flops | bytes accessed | tf_op | source)
XLA Modules:
  0.0 173.9 jit_solution(10849449873993659453)
XLA Ops:
  7.4 4.6 %collective-permute-done.refs_2_ = bf16[192,896]{1,0:T(8,128)(2,1)} collective-permute-done((bf16[192,896]{1,0:T(8,128)(2,1)S(1)}, bf16[192,896]{1,0:T(8,128)(2,1)}, u32[]{:S(2)}, u32[]{:S(2)}) %collective-permute-start) | collective-permute-done | bytes 344096 | tf_op jit(solution)/shard_map/ppermute | solution.py:254
  13.1 3.1 %copy-done = bf16[1,1,2,1024,1792]{4,3,2,1,0:T(8,128)(2,1)S(1)} copy-done((bf16[1,1,2,1024,1792]{4,3,2,1,0:T(8,128)(2,1)S(1)}, bf16[1,1,2,1024,1792]{4,3,2,1,0:T(8,128)(2,1)}, u32[]{:S(2)}) %copy-start) | copy-done | bytes 7340056
  16.2 3.9 %shard_map.86.refs_4_.refs_0_ = bf16[2,192,512]{2,1,0:T(8,128)(2,1)S(1)} custom-call(s32[3]{0:T(128)S(1)} %pad_add_fusion.refs_0_, bf16[192,896]{1,0:T(8,128)(2,1)S(1)} %get-tuple-element.22.refs_1_, bf16[192,896]{1,0:T(8,128)(2,1)} %collective-permute-done.refs_2_, bf16[2,1024,1792]{2,1,0:T(8,128)(2,1)S(1)} %bitcast.33), custom_call_target="tpu_custom_call" | custom-call | flops 10400000000 | bytes 1024 | tf_op jit(solution)/shard_map/pallas_call | solution.py:37
  20.1 3.9 %shard_map.87.refs_7_.refs_2_.refs_0_ = bf16[2,192,512]{2,1,0:T(8,128)(2,1)S(1)} custom-call(s32[3]{0:T(128)S(1)} %pad_add_fusion.refs_0_, bf16[192,896]{1,0:T(8,128)(2,1)S(1)} %get-tuple-element.22.refs_1_, bf16[192,896]{1,0:T(8,128)(2,1)} %collective-permute-done.refs_2_, bf16[2,1024,1792]{2,1,0:T(8,128)(2,1)S(1)} %bitcast.34, ...), custom_call_target="tpu_custom_call" | custom-call | flops 10400000000 | bytes 1024 | tf_op jit(solution)/shard_map/pallas_call | solution.py:37
  26.6 3.8 %shard_map.88.refs_7_.refs_0_ = bf16[3,192,512]{2,1,0:T(8,128)(2,1)S(1)} custom-call(s32[3]{0:T(128)S(1)} %pad_add_fusion.refs_0_, bf16[192,896]{1,0:T(8,128)(2,1)S(1)} %get-tuple-element.21.refs_1_, bf16[192,896]{1,0:T(8,128)(2,1)S(1)} %collective-permute-done.3.refs_2_, bf16[192,896]{1,0:T(8,128)(2,1)S(1)} %get-tuple-element.19.refs_3_, ...), custom_call_target="tpu_custom_call" | custom-call | flops 15600000000 | bytes 1024 | tf_op jit(solution)/shard_map/pallas_call | solution.py:37
  31.6 3.8 %shard_map.89.refs_2_.refs_0_ = bf16[3,192,512]{2,1,0:T(8,128)(2,1)S(1)} custom-call(s32[3]{0:T(128)S(1)} %pad_add_fusion.refs_0_, bf16[192,896]{1,0:T(8,128)(2,1)S(1)} %get-tuple-element.21.refs_1_, bf16[192,896]{1,0:T(8,128)(2,1)S(1)} %collective-permute-done.3.refs_2_, bf16[192,896]{1,0:T(8,128)(2,1)S(1)} %get-tuple-element.19.refs_3_, ...), custom_call_target="tpu_custom_call" | custom-call | flops 15600000000 | bytes 1024 | tf_op jit(solution)/shard_map/pallas_call | solution.py:37
  38.9 7.0 %collective-permute-done.8.refs_1_ = bf16[3,192,512]{2,1,0:T(8,128)(2,1)S(1)} collective-permute-done((bf16[3,192,512]{2,1,0:T(8,128)(2,1)S(1)}, bf16[3,192,512]{2,1,0:T(8,128)(2,1)S(1)}, u32[]{:S(2)}, u32[]{:S(2)}) %collective-permute-start.8) | collective-permute-done | bytes 589856 | tf_op jit(solution)/shard_map/ppermute | solution.py:245
  48.7 3.8 %shard_map.93.refs_4_.refs_1_.refs_0_ = bf16[3,192,512]{2,1,0:T(8,128)(2,1)S(1)} custom-call(s32[3]{0:T(128)S(1)} %pad_add_fusion.refs_0_, bf16[192,896]{1,0:T(8,128)(2,1)S(1)} %get-tuple-element.20.refs_1_, bf16[192,896]{1,0:T(8,128)(2,1)S(1)} %collective-permute-done.6.refs_2_, bf16[192,896]{1,0:T(8,128)(2,1)S(1)} %get-tuple-element.18.refs_3_, ...), custom_call_target="tpu_custom_call" | custom-call | flops 15600000000 | bytes 1024 | tf_op jit(solution)/shard_map/pallas_call | solution.py:37
  58.3 4.0 %collective-permute-start.12 = (bf16[3,192,512]{2,1,0:T(8,128)(2,1)S(1)}, bf16[3,192,512]{2,1,0:T(8,128)(2,1)S(1)}, u32[]{:S(2)}, u32[]{:S(2)}) collective-permute-start(bf16[3,192,512]{2,1,0:T(8,128)(2,1)S(1)} %shard_map.96.refs_7_), channel_id=1, source_target_pairs={{0,2},{1,3},{2,0},{3,1},{4,6},{5,7},{6,4},{7,5},{8,10},{9,11},{10,... | collective-permute-start | bytes 1769480 | tf_op jit(solution)/shard_map/ppermute | solution.py:245
  62.2 3.8 %shard_map.97.refs_2_.refs_0_ = bf16[3,192,512]{2,1,0:T(8,128)(2,1)S(1)} custom-call(s32[3]{0:T(128)S(1)} %pad_add_fusion.refs_0_, bf16[192,896]{1,0:T(8,128)(2,1)S(1)} %get-tuple-element.20.refs_1_, bf16[192,896]{1,0:T(8,128)(2,1)S(1)} %collective-permute-done.6.refs_2_, bf16[192,896]{1,0:T(8,128)(2,1)S(1)} %get-tuple-element.18.refs_3_, ...), custom_call_target="tpu_custom_call" | custom-call | flops 15600000000 | bytes 1024 | tf_op jit(solution)/shard_map/pallas_call | solution.py:37
  67.7 7.0 %collective-permute-done.12.refs_1_ = bf16[3,192,512]{2,1,0:T(8,128)(2,1)S(1)} collective-permute-done((bf16[3,192,512]{2,1,0:T(8,128)(2,1)S(1)}, bf16[3,192,512]{2,1,0:T(8,128)(2,1)S(1)}, u32[]{:S(2)}, u32[]{:S(2)}) %collective-permute-start.12) | collective-permute-done | bytes 589856 | tf_op jit(solution)/shard_map/ppermute | solution.py:245
  78.4 3.4 %collective-permute-start.13 = (bf16[2,192,512]{2,1,0:T(8,128)(2,1)S(1)}, bf16[2,192,512]{2,1,0:T(8,128)(2,1)S(1)}, u32[]{:S(2)}, u32[]{:S(2)}) collective-permute-start(bf16[2,192,512]{2,1,0:T(8,128)(2,1)S(1)} %shard_map.102.refs_4_), channel_id=1, source_target_pairs={{0,2},{1,3},{2,0},{3,1},{4,6},{5,7},{6,4},{7,5},{8,10},{9,11},{10,... | collective-permute-start | bytes 1179656 | tf_op jit(solution)/shard_map/ppermute | solution.py:245
  82.4 7.9 %collective-permute-start.16 = (bf16[3,192,512]{2,1,0:T(8,128)(2,1)S(1)}, bf16[3,192,512]{2,1,0:T(8,128)(2,1)S(1)}, u32[]{:S(2)}, u32[]{:S(2)}) collective-permute-start(bf16[3,192,512]{2,1,0:T(8,128)(2,1)S(1)} %shard_map.103.refs_2_), channel_id=1, source_target_pairs={{0,2},{1,3},{2,0},{3,1},{4,6},{5,7},{6,4},{7,5},{8,10},{9,11},{10,... | collective-permute-start | bytes 1769480 | tf_op jit(solution)/shard_map/ppermute | solution.py:245
  91.5 8.4 %collective-permute-done.16.refs_1_ = bf16[3,192,512]{2,1,0:T(8,128)(2,1)S(1)} collective-permute-done((bf16[3,192,512]{2,1,0:T(8,128)(2,1)S(1)}, bf16[3,192,512]{2,1,0:T(8,128)(2,1)S(1)}, u32[]{:S(2)}, u32[]{:S(2)}) %collective-permute-start.16) | collective-permute-done | bytes 589856 | tf_op jit(solution)/shard_map/ppermute | solution.py:245
  101.5 3.4 %collective-permute-start.17 = (bf16[1,192,512]{2,1,0:T(8,128)(2,1)S(1)}, bf16[1,192,512]{2,1,0:T(8,128)(2,1)S(1)}, u32[]{:S(2)}, u32[]{:S(2)}) collective-permute-start(bf16[1,192,512]{2,1,0:T(8,128)(2,1)S(1)} %shard_map.106.refs_3_), channel_id=1, source_target_pairs={{0,2},{1,3},{2,0},{3,1},{4,6},{5,7},{6,4},{7,5},{8,10},{9,11},{10,... | collective-permute-start | bytes 589832 | tf_op jit(solution)/shard_map/ppermute | solution.py:245
  109.2 3.3 %collective-permute-start.23 = (bf16[2,192,512]{2,1,0:T(8,128)(2,1)S(1)}, bf16[2,192,512]{2,1,0:T(8,128)(2,1)S(1)}, u32[]{:S(2)}, u32[]{:S(2)}) collective-permute-start(bf16[2,192,512]{2,1,0:T(8,128)(2,1)S(1)} %shard_map.107.refs_7_), channel_id=1, source_target_pairs={{0,2},{1,3},{2,0},{3,1},{4,6},{5,7},{6,4},{7,5},{8,10},{9,11},{10,... | collective-permute-start | bytes 1179656 | tf_op jit(solution)/shard_map/ppermute | solution.py:245
  114.7 11.6 %collective-permute-start.19 = (bf16[192,896]{1,0:T(8,128)(2,1)S(1)}, bf16[192,896]{1,0:T(8,128)(2,1)S(1)}, u32[]{:S(2)}, u32[]{:S(2)}) collective-permute-start(bf16[192,896]{1,0:T(8,128)(2,1)S(1)} %get-tuple-element.10.refs_6_), channel_id=1, source_target_pairs={{0,9},{1,8},{2,11},{3,10},{4,13},{5,12},{6,15},{7,14},{8,17},{9,16... | collective-permute-start | bytes 1032200 | tf_op jit(solution)/shard_map/ppermute | solution.py:263
  131.5 3.3 %shard_map.109 = (bf16[192,896]{1,0:T(8,128)(2,1)S(1)}, bf16[192,896]{1,0:T(8,128)(2,1)S(1)}) custom-call(s32[3]{0:T(128)S(1)} %pad_add_fusion.refs_0_, bf16[2,192,512]{2,1,0:T(8,128)(2,1)S(1)} %copy-done.13, bf16[2,192,512]{2,1,0:T(8,128)(2,1)S(1)} %slice.100.refs_2_, bf16[2,192,512]{2,1,0:T(8,128)(2,1)S(1)} %collective-permute-done.18.refs_2_.refs_3_, ...), custom_call_target="tpu_custom_call" | custom-call | flops 20000000000 | bytes 1024 | tf_op jit(solution)/shard_map/pallas_call | solution.py:37
  137.9 3.6 %collective-permute-start.24 = (bf16[192,896]{1,0:T(8,128)(2,1)S(1)}, bf16[192,896]{1,0:T(8,128)(2,1)S(1)}, u32[]{:S(2)}, u32[]{:S(2)}) collective-permute-start(bf16[192,896]{1,0:T(8,128)(2,1)S(1)} %get-tuple-element.13.refs_6_), channel_id=1, source_target_pairs={{0,9},{1,8},{2,11},{3,10},{4,13},{5,12},{6,15},{7,14},{8,17},{9,16... | collective-permute-start | bytes 1032200 | tf_op jit(solution)/shard_map/ppermute | solution.py:263
  143.5 4.5 %collective-permute-start.29 = (bf16[2,192,512]{2,1,0:T(8,128)(2,1)S(1)}, bf16[2,192,512]{2,1,0:T(8,128)(2,1)S(1)}, u32[]{:S(2)}, u32[]{:S(2)}) collective-permute-start(bf16[2,192,512]{2,1,0:T(8,128)(2,1)S(1)} %collective-permute-done.28.refs_3_), channel_id=1, source_target_pairs={{0,2},{1,3},{2,0},{3,1},{4,6},{5,7},{6,4},{7,5},{8,10},{9,11},{10,... | collective-permute-start | bytes 1179656 | tf_op jit(solution)/shard_map/ppermute | solution.py:245
  148.1 4.0 %collective-permute-start.26 = (bf16[192,896]{1,0:T(8,128)(2,1)S(1)}, bf16[192,896]{1,0:T(8,128)(2,1)S(1)}, u32[]{:S(2)}, u32[]{:S(2)}) collective-permute-start(bf16[192,896]{1,0:T(8,128)(2,1)S(1)} %get-tuple-element.12.refs_7_), channel_id=1, source_target_pairs={{8,1},{9,0},{10,3},{11,2},{12,5},{13,4},{14,7},{15,6},{16,9},{17,8... | collective-permute-start | bytes 1032200 | tf_op jit(solution)/shard_map/ppermute | solution.py:263
  155.7 3.3 %shard_map.111 = (bf16[192,896]{1,0:T(8,128)(2,1)S(1)}, bf16[192,896]{1,0:T(8,128)(2,1)S(1)}) custom-call(s32[3]{0:T(128)S(1)} %pad_add_fusion.refs_0_, bf16[2,192,512]{2,1,0:T(8,128)(2,1)S(1)} %shard_map.105.refs_3_.refs_1_, bf16[2,192,512]{2,1,0:T(8,128)(2,1)S(1)} %collective-permute-done.23.refs_4_.refs_2_, ...), custom_call_target="tpu_custom_call" | custom-call | flops 20000000000 | bytes 1024 | tf_op jit(solution)/shard_map/pallas_call | solution.py:37
  159.1 5.1 %collective-permute-start.30 = (bf16[192,896]{1,0:T(8,128)(2,1)S(1)}, bf16[192,896]{1,0:T(8,128)(2,1)S(1)}, u32[]{:S(2)}, u32[]{:S(2)}) collective-permute-start(bf16[192,896]{1,0:T(8,128)(2,1)S(1)} %get-tuple-element.16), channel_id=1, source_target_pairs={{8,1},{9,0},{10,3},{11,2},{12,5},{13,4},{14,7},{15,6},{16,9},{17,8... | collective-permute-start | bytes 1032200 | tf_op jit(solution)/shard_map/ppermute | solution.py:263
  167.1 4.9 %collective-permute-done.30 = bf16[192,896]{1,0:T(8,128)(2,1)S(1)} collective-permute-done((bf16[192,896]{1,0:T(8,128)(2,1)S(1)}, bf16[192,896]{1,0:T(8,128)(2,1)S(1)}, u32[]{:S(2)}, u32[]{:S(2)}) %collective-permute-start.30) | collective-permute-done | bytes 344096 | tf_op jit(solution)/shard_map/ppermute | solution.py:263
  (134 shorter events, 57.2 us)
Async XLA Ops:
  4.1 19.8 %collective-permute-start.3 = (bf16[192,896]{1,0:T(8,128)(2,1)S(1)}, bf16[192,896]{1,0:T(8,128)(2,1)S(1)}, u32[]{:S(2)}, u32[]{:S(2)}) collective-permute-start(bf16[192,896]{1,0:T(8,128)(2,1)S(1)} %get-tuple-element.21.refs_1_), channel_id=1, source_target_pairs={{0,1},{1,0},{2,3},{3,2},{4,5},{5,4},{6,7},{7,6},{8,9},{9,8},{10,11... | collective-permute-start | bytes 1032200 | tf_op jit(solution)/shard_map/ppermute | solution.py:254
  4.3 22.3 %collective-permute-start.4 = (bf16[192,896]{1,0:T(8,128)(2,1)S(1)}, bf16[192,896]{1,0:T(8,128)(2,1)S(1)}, u32[]{:S(2)}, u32[]{:S(2)}) collective-permute-start(bf16[192,896]{1,0:T(8,128)(2,1)S(1)} %get-tuple-element.19.refs_3_), channel_id=1, source_target_pairs={{0,1},{1,0},{2,3},{3,2},{4,5},{5,4},{6,7},{7,6},{8,9},{9,8},{10,11... | collective-permute-start | bytes 1032200 | tf_op jit(solution)/shard_map/ppermute | solution.py:254
  5.8 30.5 %collective-permute-start.1 = (bf16[192,896]{1,0:T(8,128)(2,1)S(1)}, bf16[192,896]{1,0:T(8,128)(2,1)S(1)}, u32[]{:S(2)}, u32[]{:S(2)}) collective-permute-start(bf16[192,896]{1,0:T(8,128)(2,1)S(1)} %get-tuple-element.23.refs_1_), channel_id=1, source_target_pairs={{0,1},{1,0},{2,3},{3,2},{4,5},{5,4},{6,7},{7,6},{8,9},{9,8},{10,11... | collective-permute-start | bytes 1032200 | tf_op jit(solution)/shard_map/ppermute | solution.py:254
  5.9 40.8 %collective-permute-start.6 = (bf16[192,896]{1,0:T(8,128)(2,1)S(1)}, bf16[192,896]{1,0:T(8,128)(2,1)S(1)}, u32[]{:S(2)}, u32[]{:S(2)}) collective-permute-start(bf16[192,896]{1,0:T(8,128)(2,1)S(1)} %get-tuple-element.20.refs_1_), channel_id=1, source_target_pairs={{0,1},{1,0},{2,3},{3,2},{4,5},{5,4},{6,7},{7,6},{8,9},{9,8},{10,11... | collective-permute-start | bytes 1032200 | tf_op jit(solution)/shard_map/ppermute | solution.py:254
  11.9 36.8 %collective-permute-start.7 = (bf16[192,896]{1,0:T(8,128)(2,1)S(1)}, bf16[192,896]{1,0:T(8,128)(2,1)S(1)}, u32[]{:S(2)}, u32[]{:S(2)}) collective-permute-start(bf16[192,896]{1,0:T(8,128)(2,1)S(1)} %get-tuple-element.18.refs_3_), channel_id=1, source_target_pairs={{0,1},{1,0},{2,3},{3,2},{4,5},{5,4},{6,7},{7,6},{8,9},{9,8},{10,11... | collective-permute-start | bytes 1032200 | tf_op jit(solution)/shard_map/ppermute | solution.py:254
  24.0 11.5 %collective-permute-start.2 = (bf16[2,192,512]{2,1,0:T(8,128)(2,1)S(1)}, bf16[2,192,512]{2,1,0:T(8,128)(2,1)S(1)}, u32[]{:S(2)}, u32[]{:S(2)}) collective-permute-start(bf16[2,192,512]{2,1,0:T(8,128)(2,1)S(1)} %shard_map.86.refs_4_.refs_0_), channel_id=1, source_target_pairs={{0,2},{1,3},{2,0},{3,1},{4,6},{5,7},{6,4},{7,5},{8,10},{9,11},{10,... | collective-permute-start | bytes 1179656 | tf_op jit(solution)/shard_map/ppermute | solution.py:245
  30.4 15.5 %collective-permute-start.8 = (bf16[3,192,512]{2,1,0:T(8,128)(2,1)S(1)}, bf16[3,192,512]{2,1,0:T(8,128)(2,1)S(1)}, u32[]{:S(2)}, u32[]{:S(2)}) collective-permute-start(bf16[3,192,512]{2,1,0:T(8,128)(2,1)S(1)} %shard_map.88.refs_7_.refs_0_), channel_id=1, source_target_pairs={{0,2},{1,3},{2,0},{3,1},{4,6},{5,7},{6,4},{7,5},{8,10},{9,11},{10,... | collective-permute-start | bytes 1769480 | tf_op jit(solution)/shard_map/ppermute | solution.py:245
  35.5 16.9 %collective-permute-start.5 = (bf16[2,192,512]{2,1,0:T(8,128)(2,1)S(1)}, bf16[2,192,512]{2,1,0:T(8,128)(2,1)S(1)}, u32[]{:S(2)}, u32[]{:S(2)}) collective-permute-start(bf16[2,192,512]{2,1,0:T(8,128)(2,1)S(1)} %shard_map.90.refs_4_), channel_id=1, source_target_pairs={{0,0},{1,1},{2,4},{3,5},{4,2},{5,3},{6,6},{7,7},{8,8},{9,9},{10,12... | collective-permute-start | bytes 1179656 | tf_op jit(solution)/shard_map/ppermute | solution.py:245
  46.0 11.6 %collective-permute-start.10 = (bf16[3,192,512]{2,1,0:T(8,128)(2,1)S(1)}, bf16[3,192,512]{2,1,0:T(8,128)(2,1)S(1)}, u32[]{:S(2)}, u32[]{:S(2)}) collective-permute-start(bf16[3,192,512]{2,1,0:T(8,128)(2,1)S(1)} %shard_map.92.refs_7_), channel_id=1, source_target_pairs={{0,0},{1,1},{2,4},{3,5},{4,2},{5,3},{6,6},{7,7},{8,8},{9,9},{10,12... | collective-permute-start | bytes 1769480 | tf_op jit(solution)/shard_map/ppermute | solution.py:245
  53.1 13.0 %collective-permute-start.9 = (bf16[2,192,512]{2,1,0:T(8,128)(2,1)S(1)}, bf16[2,192,512]{2,1,0:T(8,128)(2,1)S(1)}, u32[]{:S(2)}, u32[]{:S(2)}) collective-permute-start(bf16[2,192,512]{2,1,0:T(8,128)(2,1)S(1)} %shard_map.94.refs_4_), channel_id=1, source_target_pairs={{0,2},{1,3},{2,0},{3,1},{4,6},{5,7},{6,4},{7,5},{8,10},{9,11},{10,... | collective-permute-start | bytes 1179656 | tf_op jit(solution)/shard_map/ppermute | solution.py:245
  58.3 16.4 %collective-permute-start.12 = (bf16[3,192,512]{2,1,0:T(8,128)(2,1)S(1)}, bf16[3,192,512]{2,1,0:T(8,128)(2,1)S(1)}, u32[]{:S(2)}, u32[]{:S(2)}) collective-permute-start(bf16[3,192,512]{2,1,0:T(8,128)(2,1)S(1)} %shard_map.96.refs_7_), channel_id=1, source_target_pairs={{0,2},{1,3},{2,0},{3,1},{4,6},{5,7},{6,4},{7,5},{8,10},{9,11},{10,... | collective-permute-start | bytes 1769480 | tf_op jit(solution)/shard_map/ppermute | solution.py:245
  78.4 12.0 %collective-permute-start.13 = (bf16[2,192,512]{2,1,0:T(8,128)(2,1)S(1)}, bf16[2,192,512]{2,1,0:T(8,128)(2,1)S(1)}, u32[]{:S(2)}, u32[]{:S(2)}) collective-permute-start(bf16[2,192,512]{2,1,0:T(8,128)(2,1)S(1)} %shard_map.102.refs_4_), channel_id=1, source_target_pairs={{0,2},{1,3},{2,0},{3,1},{4,6},{5,7},{6,4},{7,5},{8,10},{9,11},{10,... | collective-permute-start | bytes 1179656 | tf_op jit(solution)/shard_map/ppermute | solution.py:245
  82.4 17.5 %collective-permute-start.16 = (bf16[3,192,512]{2,1,0:T(8,128)(2,1)S(1)}, bf16[3,192,512]{2,1,0:T(8,128)(2,1)S(1)}, u32[]{:S(2)}, u32[]{:S(2)}) collective-permute-start(bf16[3,192,512]{2,1,0:T(8,128)(2,1)S(1)} %shard_map.103.refs_2_), channel_id=1, source_target_pairs={{0,2},{1,3},{2,0},{3,1},{4,6},{5,7},{6,4},{7,5},{8,10},{9,11},{10,... | collective-permute-start | bytes 1769480 | tf_op jit(solution)/shard_map/ppermute | solution.py:245
  90.5 10.4 %collective-permute-start.14 = (bf16[1,192,512]{2,1,0:T(8,128)(2,1)S(1)}, bf16[1,192,512]{2,1,0:T(8,128)(2,1)S(1)}, u32[]{:S(2)}, u32[]{:S(2)}) collective-permute-start(bf16[1,192,512]{2,1,0:T(8,128)(2,1)S(1)} %slice.97.refs_2_), channel_id=1, source_target_pairs={{0,0},{1,1},{2,4},{3,5},{4,2},{5,3},{6,6},{7,7},{8,8},{9,9},{10,12... | collective-permute-start | bytes 589832 | tf_op jit(solution)/shard_map/ppermute | solution.py:245
  108.0 20.3 %collective-permute-start.21 = (bf16[1,192,512]{2,1,0:T(8,128)(2,1)S(1)}, bf16[1,192,512]{2,1,0:T(8,128)(2,1)S(1)}, u32[]{:S(2)}, u32[]{:S(2)}) collective-permute-start(bf16[1,192,512]{2,1,0:T(8,128)(2,1)S(1)} %collective-permute-done.17.refs_4_.refs_2_), channel_id=1, source_target_pairs={{0,0},{1,1},{2,4},{3,5},{4,2},{5,3},{6,6},{7,7},{8,8},{9,9},{10,12... | collective-permute-start | bytes 589832 | tf_op jit(solution)/shard_map/ppermute | solution.py:245
  109.2 19.1 %collective-permute-start.23 = (bf16[2,192,512]{2,1,0:T(8,128)(2,1)S(1)}, bf16[2,192,512]{2,1,0:T(8,128)(2,1)S(1)}, u32[]{:S(2)}, u32[]{:S(2)}) collective-permute-start(bf16[2,192,512]{2,1,0:T(8,128)(2,1)S(1)} %shard_map.107.refs_7_), channel_id=1, source_target_pairs={{0,2},{1,3},{2,0},{3,1},{4,6},{5,7},{6,4},{7,5},{8,10},{9,11},{10,... | collective-permute-start | bytes 1179656 | tf_op jit(solution)/shard_map/ppermute | solution.py:245
  114.7 33.3 %collective-permute-start.19 = (bf16[192,896]{1,0:T(8,128)(2,1)S(1)}, bf16[192,896]{1,0:T(8,128)(2,1)S(1)}, u32[]{:S(2)}, u32[]{:S(2)}) collective-permute-start(bf16[192,896]{1,0:T(8,128)(2,1)S(1)} %get-tuple-element.10.refs_6_), channel_id=1, source_target_pairs={{0,9},{1,8},{2,11},{3,10},{4,13},{5,12},{6,15},{7,14},{8,17},{9,16... | collective-permute-start | bytes 1032200 | tf_op jit(solution)/shard_map/ppermute | solution.py:263
  126.3 21.6 %collective-permute-start.20 = (bf16[192,896]{1,0:T(8,128)(2,1)S(1)}, bf16[192,896]{1,0:T(8,128)(2,1)S(1)}, u32[]{:S(2)}, u32[]{:S(2)}) collective-permute-start(bf16[192,896]{1,0:T(8,128)(2,1)S(1)} %get-tuple-element.11), channel_id=1, source_target_pairs={{0,8},{1,9},{2,10},{3,11},{4,12},{5,13},{6,14},{7,15},{8,16},{9,17... | collective-permute-start | bytes 1032200 | tf_op jit(solution)/shard_map/ppermute | solution.py:263
  137.9 16.1 %collective-permute-start.24 = (bf16[192,896]{1,0:T(8,128)(2,1)S(1)}, bf16[192,896]{1,0:T(8,128)(2,1)S(1)}, u32[]{:S(2)}, u32[]{:S(2)}) collective-permute-start(bf16[192,896]{1,0:T(8,128)(2,1)S(1)} %get-tuple-element.13.refs_6_), channel_id=1, source_target_pairs={{0,9},{1,8},{2,11},{3,10},{4,13},{5,12},{6,15},{7,14},{8,17},{9,16... | collective-permute-start | bytes 1032200 | tf_op jit(solution)/shard_map/ppermute | solution.py:263
  141.5 12.5 %collective-permute-start.25 = (bf16[192,896]{1,0:T(8,128)(2,1)S(1)}, bf16[192,896]{1,0:T(8,128)(2,1)S(1)}, u32[]{:S(2)}, u32[]{:S(2)}) collective-permute-start(bf16[192,896]{1,0:T(8,128)(2,1)S(1)} %get-tuple-element.14), channel_id=1, source_target_pairs={{0,8},{1,9},{2,10},{3,11},{4,12},{5,13},{6,14},{7,15},{8,16},{9,17... | collective-permute-start | bytes 1032200 | tf_op jit(solution)/shard_map/ppermute | solution.py:263
  143.5 12.2 %collective-permute-start.29 = (bf16[2,192,512]{2,1,0:T(8,128)(2,1)S(1)}, bf16[2,192,512]{2,1,0:T(8,128)(2,1)S(1)}, u32[]{:S(2)}, u32[]{:S(2)}) collective-permute-start(bf16[2,192,512]{2,1,0:T(8,128)(2,1)S(1)} %collective-permute-done.28.refs_3_), channel_id=1, source_target_pairs={{0,2},{1,3},{2,0},{3,1},{4,6},{5,7},{6,4},{7,5},{8,10},{9,11},{10,... | collective-permute-start | bytes 1179656 | tf_op jit(solution)/shard_map/ppermute | solution.py:245
  148.1 19.0 %collective-permute-start.26 = (bf16[192,896]{1,0:T(8,128)(2,1)S(1)}, bf16[192,896]{1,0:T(8,128)(2,1)S(1)}, u32[]{:S(2)}, u32[]{:S(2)}) collective-permute-start(bf16[192,896]{1,0:T(8,128)(2,1)S(1)} %get-tuple-element.12.refs_7_), channel_id=1, source_target_pairs={{8,1},{9,0},{10,3},{11,2},{12,5},{13,4},{14,7},{15,6},{16,9},{17,8... | collective-permute-start | bytes 1032200 | tf_op jit(solution)/shard_map/ppermute | solution.py:263
  152.1 14.9 %collective-permute-start.27 = (bf16[192,896]{1,0:T(8,128)(2,1)S(1)}, bf16[192,896]{1,0:T(8,128)(2,1)S(1)}, u32[]{:S(2)}, u32[]{:S(2)}) collective-permute-start(bf16[192,896]{1,0:T(8,128)(2,1)S(1)} %get-tuple-element.15), channel_id=1, source_target_pairs={{8,0},{9,1},{10,2},{11,3},{12,4},{13,5},{14,6},{15,7},{16,8},{17,9... | collective-permute-start | bytes 1032200 | tf_op jit(solution)/shard_map/ppermute | solution.py:263
  159.1 13.0 %collective-permute-start.30 = (bf16[192,896]{1,0:T(8,128)(2,1)S(1)}, bf16[192,896]{1,0:T(8,128)(2,1)S(1)}, u32[]{:S(2)}, u32[]{:S(2)}) collective-permute-start(bf16[192,896]{1,0:T(8,128)(2,1)S(1)} %get-tuple-element.16), channel_id=1, source_target_pairs={{8,1},{9,0},{10,3},{11,2},{12,5},{13,4},{14,7},{15,6},{16,9},{17,8... | collective-permute-start | bytes 1032200 | tf_op jit(solution)/shard_map/ppermute | solution.py:263
  (32 other events, 253.0 us)

commit v6 on v5

--- a/solution.py
+++ b/solution.py
@@ -12,6 +12,7 @@
 F32 = jnp.float32
 MIB = 1024 * 1024
 PIECES = 2
+ROWS, SMALL, ACT, FIRST, AHEAD_OUT, BEHIND_OUT = 20, 1.6, 10, 5.2, 12, 20
 
 
 def shift(shard, axis, by):
@@ -24,7 +25,7 @@
     return pl.BlockSpec(array.shape, functools.partial(lambda n, *_: (0,) * n, array.ndim))
 
 
-def call(kernel, micros, operands, after, out_shape, scalars=(), grid=(1,), in_specs=None, out_specs=None, scratch=(), limit=24):
+def call(kernel, micros, operands, after, out_shape, scalars=(), grid=(1,), in_specs=None, out_specs=None, scratch=(), limit=24, name=None):
     count, unread = len(scalars) + len(operands), len(after)
 
     def run(*refs):
@@ -37,8 +38,9 @@
     return pl.pallas_call(
         run,
         compiler_params=pltpu.CompilerParams(vmem_limit_bytes=limit * MIB),
-        cost_estimate=pl.CostEstimate(flops=int(micros * 4e9), bytes_accessed=1024, transcendentals=0),
+        cost_estimate=pl.CostEstimate(flops=int(micros * 1e9), bytes_accessed=1024, transcendentals=0),
         out_shape=out_shape,
+        name=name,
         grid_spec=pltpu.PrefetchScalarGridSpec(
             num_scalar_prefetch=len(scalars),
             grid=grid,
@@ -49,6 +51,14 @@
     )(*scalars, *operands, *after)
 
 
+def cut_kernel(rows, out):
+    out[...] = rows[...]
+
+
+def cut_first_kernel(value, out):
+    out[...] = value[: out.shape[0]]
+
+
 def first_kernel(width, where, own, partner, tile, out, joined):
     @pl.when((pl.program_id(0) == 0) & (pl.program_id(1) == 0))
     def _():
@@ -62,63 +72,28 @@
     ).astype(BF16)
 
 
-def behind_first_kernel(width, where, own, partner, grad, grad_partner, tile, down, out, joined, joined_grad):
-    at = pl.multiple_of(where[1] * width, 128)
-    other = pl.multiple_of((1 - where[1]) * width, 128)
-
-    @pl.when((pl.program_id(0) == 0) & (pl.program_id(1) == 0))
-    def _():
-        joined[:, pl.ds(at, width)] = own[...]
-        joined[:, pl.ds(other, width)] = partner[...]
-        joined_grad[:, pl.ds(at, width)] = grad[...]
-        joined_grad[:, pl.ds(other, width)] = grad_partner[...]
-
-    @pl.when(pl.program_id(0) < 2)
-    def _():
-        out[0] = lax.dot_general(
-            joined[...], tile[0], (((1,), (1,)), ((), ())), preferred_element_type=F32
-        ).astype(BF16)
-
-    @pl.when(pl.program_id(0) == 2)
-    def _():
-        out[0] = lax.dot_general(
-            joined_grad[...], down[...], (((1,), (1,)), ((), ())), preferred_element_type=F32
-        ).astype(BF16)
-
-
-def first_product(where, far, rows, gates, downs, after):
+def first_product(name, where, far, rows, weights, after):
     slots, width = rows[0].shape
-    units, features = gates.shape[1:]
+    parts, units, features = weights.shape
     half = units // 2
     tile = min(256, half)
     steps = half // tile
-    parts = 1 + len(rows) // 2
-
-    def side(w):
-        return (1 - w[0]) * steps if far else w[0] * steps
-
-    def gate_at(k, j, w):
-        return (jnp.minimum(k, 1), side(w) + jnp.where(k < 2, j, steps - 1), 0)
-
-    def down_at(k, j, w):
-        return (side(w) + jnp.where(k < 2, 0, j), 0)
-
-    in_specs = [whole(r) for r in rows] + [pl.BlockSpec((1, tile, features), gate_at)]
-    operands = [*rows, gates]
-    if parts == 3:
-        in_specs.append(pl.BlockSpec((tile, features), down_at))
-        operands.append(downs)
+
+    def tile_at(k, j, w):
+        return (k, ((1 - w[0]) if far else w[0]) * steps + j, 0)
+
     return call(
-        functools.partial(behind_first_kernel if parts == 3 else first_kernel, width),
-        1.3 * parts,
-        operands,
+        functools.partial(first_kernel, width),
+        FIRST * parts,
+        (*rows, weights),
         after,
         jax.ShapeDtypeStruct((parts, slots, half), BF16),
         scalars=(where,),
         grid=(parts, steps),
-        in_specs=in_specs,
+        in_specs=[*[whole(r) for r in rows], pl.BlockSpec((1, tile, features), tile_at)],
         out_specs=pl.BlockSpec((1, slots, tile), lambda k, j, w: (k, 0, j)),
-        scratch=[pltpu.VMEM((slots, features), BF16)] * (parts - 1),
+        scratch=[pltpu.VMEM((slots, features), BF16)],
+        name=name,
     )
 
 
@@ -155,10 +130,10 @@
     out[0] = (gate * jax.nn.sigmoid(gate) * up).astype(BF16)
 
 
-def behind_act_kernel(near, arrived, scale, out):
+def behind_act_kernel(near, arrived, near_e, arrived_e, scale, out):
     gate = near[0].astype(F32) + arrived[0].astype(F32)
     up = near[1].astype(F32) + arrived[1].astype(F32)
-    expanded = (near[2].astype(F32) + arrived[2].astype(F32)) * scale[...]
+    expanded = (near_e[0].astype(F32) + arrived_e[0].astype(F32)) * scale[...]
     sig = jax.nn.sigmoid(gate)
     out[0] = (expanded * up * sig * (1.0 + gate * (1.0 - sig))).astype(BF16)
     out[1] = (expanded * gate * sig).astype(BF16)
@@ -202,7 +177,7 @@
         keep[...] = share.astype(BF16)
 
 
-def second_product(where, values, scale, weights, after):
+def second_product(name, where, values, scale, weights, after):
     kinds, units, features = weights.shape
     slots = values[0].shape[1]
     width = features // 2
@@ -214,7 +189,7 @@
     share = jax.ShapeDtypeStruct((slots, width), BF16)
     return call(
         functools.partial(second_kernel, scale is not None),
-        1 + 2 * kinds,
+        AHEAD_OUT if kinds == 1 else BEHIND_OUT,
         (*operands, weights),
         after,
         (share, share),
@@ -222,6 +197,7 @@
         grid=(2,),
         in_specs=[*[whole(v) for v in operands], pl.BlockSpec((kinds, units, width), tile_at)],
         scratch=[pltpu.VMEM((slots, kinds * units), BF16)],
+        name=name,
     )
 
 
@@ -264,126 +240,177 @@
 
     recent = []
 
-    def kernel_call(kernel, micros, operands, shape, scalars=()):
-        made = call(kernel, micros, operands, list(recent), jax.ShapeDtypeStruct(shape, BF16), scalars)
+    def kernel_call(name, kernel, micros, operands, shape, scalars=()):
+        made = call(
+            kernel, micros, operands, list(recent), jax.ShapeDtypeStruct(shape, BF16), scalars, name=name
+        )
         recent[:] = [made]
         return made
 
     class Chain:
-        def __init__(self, inputs, scale, by):
-            self.inputs, self.scale, self.by = inputs, scale, by
-            self.parts = 1 + len(inputs)
-            self.rows, self.far, self.near, self.act = {}, {}, {}, {}
-            self.out, self.mid, self.one, self.shares = {}, {}, {}, {}
-
-        def cut(self, array, c):
-            size = height // PIECES
-            return array[c * size : (c + 1) * size]
+        def __init__(self, name, rows, weights, spreads):
+            self.name = name
+            self.rows, self.weights = rows, weights
+            self.spreads = spreads
+            self.pairs, self.far, self.near, self.act = {}, {}, {}, {}
+            self.out, self.mid, self.one, self.back = {}, {}, {}, {}
 
         def fetch(self, c):
-            rows = [self.cut(array, c) for array in self.inputs]
-            self.rows[c] = [r for row in rows for r in (row, swapped(row))]
+            size, width = height // PIECES, self.rows.shape[1]
+            rows = call(
+                cut_kernel,
+                SMALL if c else ROWS,
+                (self.rows,),
+                list(recent),
+                jax.ShapeDtypeStruct((size, width), BF16),
+                in_specs=[pl.BlockSpec((size, width), lambda i: (c, 0))],
+                name=f"{self.name}_rows_{c}",
+            )
+            recent[:] = [rows]
+            self.pairs[c] = rows, swapped(rows)
 
         def product(self, c, far):
-            made = first_product(where, far, self.rows[c], gates, downs[0], list(recent))
+            made = first_product(f"{self.name}_{'far' if far else 'near'}_{c}", where, far, self.pairs[c], self.weights, list(recent))
             recent[:] = [made]
             (self.far if far else self.near)[c] = made
+
+        def products(self, c):
+            self.product(c, True)
+            self.product(c, False)
 
         def outer_sum(self, c):
             if c == 0:
                 value = self.far[0]
             else:
-                first = self.far[c] if c < PIECES else self.act[0]
                 mine = self.near[c - 1]
-                value = kernel_call(
-                    end_or_sum_kernel, 0.4, (first, mine, self.mid[c - 1]), mine.shape, (where,)
-                )
+                first = self.far[c] if c < PIECES else self.act.get(0)
+                if first is None:
+                    value = kernel_call(
+                        f"{self.name}_outer_{c}", sum_kernel, SMALL, (mine, self.mid[c - 1]), mine.shape
+                    )
+                else:
+                    value = kernel_call(
+                        f"{self.name}_outer_{c}",
+                        end_or_sum_kernel,
+                        SMALL,
+                        (first, mine, self.mid[c - 1]),
+                        mine.shape,
+                        (where,),
+                    )
             self.out[c] = outer(value)
 
         def middle_sum(self, c):
             mine = self.far[c]
-            self.mid[c] = middle(kernel_call(sum_kernel, 0.4, (mine, self.out[c]), mine.shape))
-
-        def activate(self, c):
-            near = self.near[c]
-            operands = [near, self.out[c + 1]]
-            kernel = ahead_act_kernel
-            if self.parts == 3:
-                operands.append(self.cut(self.scale, c))
-                kernel = behind_act_kernel
-            shape = (self.parts - 1, *near.shape[1:])
-            self.act[c] = kernel_call(kernel, 0.8, operands, shape)
+            self.mid[c] = middle(
+                kernel_call(
+                    f"{self.name}_middle_{c}", sum_kernel, SMALL, (mine, self.out[c]), mine.shape
+                )
+            )
+
+        def middle_pass(self, c):
+            value = self.out[PIECES] if c == 0 else self.back[c]
+            if value.shape[0] > self.spreads or c > 0:
+                shape = (self.spreads, *value.shape[1:])
+                value = kernel_call(f"{self.name}_first_{c}", cut_first_kernel, SMALL, (value,), shape)
+            self.one[c] = value
+            self.mid[PIECES + c] = middle(value)
 
         def outer_pass(self, c):
             value = self.mid[PIECES + c - 1]
-            if c < PIECES:
+            if c == PIECES:
                 value = kernel_call(
-                    end_or_pass_kernel, 0.3, (self.act[c], value), value.shape, (where,)
+                    f"{self.name}_back_{c}", cut_first_kernel, SMALL, (value,), value.shape
                 )
-            self.out[PIECES + c] = outer(value)
-
-        def middle_pass(self, c):
-            value = self.out[PIECES + c]
-            if c == 0:
-                value = value[: self.parts - 1]
-            self.one[c] = value
-            self.mid[PIECES + c] = middle(value)
-
-        def finish(self, c):
-            values = [
-                self.act[c],
-                self.one[c],
-                self.mid[PIECES + c],
-                self.out[PIECES + c + 1],
-            ]
-            scaled = self.parts == 2
-            scale = self.cut(self.scale, c) if scaled else None
-            weights = downs if scaled else gates
-            give, keep = second_product(where, values, scale, weights, list(recent))
-            recent[:] = [give]
-            arrived = to_section(give, self.by, 1), to_section(keep, self.by, 0)
-            self.shares[c] = arrived
-
-        def result(self):
-            sums = [
-                (a.astype(F32) + b.astype(F32)).astype(BF16)
-                for a, b in (self.shares[c] for c in range(PIECES))
-            ]
-            return jnp.concatenate(sums)[None]
-
-    ahead = Chain([ahead_rows[0]], scales[0], 1)
-    behind = Chain([behind_rows[0], behind_grad[0]], scales[1], -1)
-    both = (ahead, behind)
-    for c in range(PIECES):
-        for chain in both:
-            chain.fetch(c)
-    for chain in both:
+            else:
+                value = kernel_call(
+                    f"{self.name}_back_{c}",
+                    end_or_pass_kernel,
+                    SMALL,
+                    (self.act[c], value),
+                    value.shape,
+                    (where,),
+                )
+            self.back[c] = outer(value)
+
+        def activated(self, c):
+            return self.act[c], self.one[c], self.mid[PIECES + c], self.back[c + 1]
+
+    ahead = Chain("ahead", ahead_rows[0], gates, 1)
+    behind = Chain("behind", behind_rows[0], gates, 2)
+    grad = Chain("grad", behind_grad[0], downs, 0)
+    sent = {}
+
+    def cut(array, c):
+        size = height // PIECES
+        return array[c * size : (c + 1) * size]
+
+    def activate_ahead(c):
+        near = ahead.near[c]
+        operands = (near, ahead.out[c + 1])
+        ahead.act[c] = kernel_call(f"ahead_act_{c}", ahead_act_kernel, ACT, operands, (1, *near.shape[1:]))
+
+    def activate_behind(c):
+        near = behind.near[c]
+        operands = (near, behind.out[c + 1], grad.near[c], grad.out[c + 1], cut(scales[1], c))
+        behind.act[c] = kernel_call(f"behind_act_{c}", behind_act_kernel, ACT, operands, near.shape)
+
+    def finish(chain, c):
+        forward = chain is ahead
+        scale = cut(scales[0], c) if forward else None
+        weights = downs if forward else gates
+        give, keep = second_product(f"{chain.name}_out_{c}", where, chain.activated(c), scale, weights, list(recent))
+        recent[:] = [give]
+        by = 1 if forward else -1
+        sent[forward, c] = to_section(give, by, 1), to_section(keep, by, 0)
+
+    def result(forward):
+        sums = [
+            (a.astype(F32) + b.astype(F32)).astype(BF16)
+            for a, b in (sent[forward, c] for c in range(PIECES))
+        ]
+        return jnp.concatenate(sums)[None]
+
+    chains = (behind, grad, ahead)
+    last = PIECES - 1
+    for chain in chains:
+        chain.fetch(0)
+    for chain in chains:
         chain.product(0, True)
         chain.outer_sum(0)
         chain.product(0, False)
+        if chain is not ahead:
+            chain.fetch(1)
     for c in range(PIECES):
-        for chain in both:
+        for chain in chains:
             chain.middle_sum(c)
-            if c > 0:
-                chain.activate(c - 1)
-            if c + 1 < PIECES:
+            if chain is grad and c > 0:
+                activate_behind(c - 1)
+            if chain is ahead and c > 0:
+                activate_ahead(c - 1)
+            if c == 0 and chain is behind:
+                ahead.fetch(1)
+            if c < last:
                 chain.product(c + 1, True)
-        for chain in both:
+        for chain in chains:
             chain.outer_sum(c + 1)
-            if c + 1 < PIECES:
+            if c < last:
                 chain.product(c + 1, False)
     for c in range(PIECES):
-        for chain in both:
-            chain.middle_pass(c)
-            if c == 0:
-                chain.activate(PIECES - 1)
-            else:
-                chain.finish(c - 1)
-        for chain in both:
-            chain.outer_pass(c + 1)
-    for chain in both:
-        chain.finish(PIECES - 1)
-    return ahead.result(), behind.result()
+        behind.middle_pass(c)
+        if c == 0:
+            activate_behind(last)
+        else:
+            finish(behind, c - 1)
+        ahead.middle_pass(c)
+        if c == 0:
+            activate_ahead(last)
+        else:
+            finish(ahead, c - 1)
+        behind.outer_pass(c + 1)
+        ahead.outer_pass(c + 1)
+    finish(behind, last)
+    finish(ahead, last)
+    return result(True), result(False)
 
 
 def body(ahead_rows, behind_rows, behind_grad, route_scores, route_counts, gate_up, down_proj):

time: 175 us -> 184 us (1.051)
  starting transfers between devices: 75.2 us -> 90.1 us
  waiting for transfers between devices: 40.4 us -> 30.4 us
  Pallas kernels: 43.9 us -> 46 us
    ppermute x18 -> x23, starting transfers between devices: 36.8 us -> 48.7 us  [between(): return lax.ppermute(value, 'expert', pairs)]
    ppermute x18 -> x23, waiting for transfers between devices: 26.8 us -> 18.9 us  [between(): return lax.ppermute(value, 'expert', pairs)]
    ppermute x6, waiting for transfers between devices: 7.82 us -> 5.48 us  [swapped(): return lax.ppermute(value, 'expert', [(i, i ^ 1) for i in range(devices)])]
    unnamed x48 -> x44, local copies, waits for them, and re-layouts: 8.81 us -> 11.1 us
    ppermute x8, starting transfers between devices: 32.1 us -> 34.4 us  [to_section(): return lax.ppermute(value, ('section', 'expert'), pairs)]
    pallas_call x26 -> x45, Pallas kernels: 43.9 us -> 46 us  [call(): pl.pallas_call(run, compiler_params=pltpu.CompilerParams(vmem_limit_bytes...]
  transfers between devices with their start and end apart: 32 -> 37, of which waited for: 10 -> 8; matrix products, arithmetic and copies ran while one was open for 1% -> 1% of each run, Pallas kernels for 25% -> 25%
where the time goes in v6:
time: 184 us; the launch traced here: 183 us
  starting transfers between devices  90.1 us (49%)
  Pallas kernels  46 us (25%)
  waiting for transfers between devices  30.4 us (17%)
  local copies, waits for them, and re-layouts  12.2 us (7%)
  other arithmetic  2.3 us (1%)
    ppermute x23, starting transfers between devices, between(): return lax.ppermute(value, 'expert', pairs)  48.7 us
    pallas_call x45, Pallas kernels, call(): pl.pallas_call(run, compiler_params=pltpu.CompilerParams(vmem_limit_bytes...  46 us
    ppermute x8, starting transfers between devices, to_section(): return lax.ppermute(value, ('section', 'expert'), pairs)  34.4 us
    ppermute x23, waiting for transfers between devices, between(): return lax.ppermute(value, 'expert', pairs)  18.9 us
    unnamed x44, local copies, waits for them, and re-layouts  11.1 us
    ppermute x6, starting transfers between devices, swapped(): return lax.ppermute(value, 'expert', [(i, i ^ 1) for i in range(devices)])  7.06 us
    ppermute x8, waiting for transfers between devices, to_section(): return lax.ppermute(value, ('section', 'expert'), pairs)  6.03 us
    ppermute x6, waiting for transfers between devices, swapped(): return lax.ppermute(value, 'expert', [(i, i ^ 1) for i in range(devices)])  5.48 us
  transfers between devices with their start and end apart: 37, of which 8 were waited for; matrix products, arithmetic and copies ran while one was open for 1% of the time, Pallas kernels for 25%

profile of v6, /device:TPU:1, one launch (start us, length us, event | category | flops | bytes accessed | tf_op | source)
XLA Modules:
  0.0 182.6 jit_solution(5943868268088925801)
XLA Ops:
  7.0 4.8 %collective-permute-done.2.refs_2_ = bf16[192,896]{1,0:T(8,128)(2,1)} collective-permute-done((bf16[192,896]{1,0:T(8,128)(2,1)S(1)}, bf16[192,896]{1,0:T(8,128)(2,1)}, u32[]{:S(2)}, u32[]{:S(2)}) %collective-permute-start.2) | collective-permute-done | bytes 344096 | tf_op jit(solution)/shard_map/ppermute | solution.py:230
  11.8 3.1 %copy-done = bf16[1,1,2,1024,1792]{4,3,2,1,0:T(8,128)(2,1)S(1)} copy-done((bf16[1,1,2,1024,1792]{4,3,2,1,0:T(8,128)(2,1)S(1)}, bf16[1,1,2,1024,1792]{4,3,2,1,0:T(8,128)(2,1)}, u32[]{:S(2)}) %copy-start) | copy-done | bytes 7340056
  14.9 3.6 %behind_far_0.1.refs_4_.refs_0_ = bf16[2,192,512]{2,1,0:T(8,128)(2,1)S(1)} custom-call(s32[3]{0:T(128)S(1)} %pad_add_fusion.refs_0_, bf16[192,896]{1,0:T(8,128)(2,1)S(1)} %behind_rows_0.1.refs_1_, bf16[192,896]{1,0:T(8,128)(2,1)} %collective-permute-done.2.refs_2_, bf16[2,1024,1792]{2,1,0:T(8,128)(2,1)S(1)} %bitcast.23, ...), custom_call_target="tpu_custom_call" | custom-call | flops 10400000000 | bytes 1024 | tf_op jit(solution)/shard_map/behind_far_0/pallas_call | solution.py:38
  19.7 3.1 %copy-done.1 = bf16[1,1,2,1024,1792]{4,3,2,1,0:T(8,128)(2,1)S(1)} copy-done((bf16[1,1,2,1024,1792]{4,3,2,1,0:T(8,128)(2,1)S(1)}, bf16[1,1,2,1024,1792]{4,3,2,1,0:T(8,128)(2,1)}, u32[]{:S(2)}) %copy-start.1) | copy-done | bytes 7340056
  22.8 3.6 %behind_near_0.1.refs_1_.refs_2_.refs_0_ = bf16[2,192,512]{2,1,0:T(8,128)(2,1)S(1)} custom-call(s32[3]{0:T(128)S(1)} %pad_add_fusion.refs_0_, bf16[192,896]{1,0:T(8,128)(2,1)S(1)} %behind_rows_0.1.refs_1_, bf16[192,896]{1,0:T(8,128)(2,1)} %collective-permute-done.2.refs_2_, bf16[2,1024,1792]{2,1,0:T(8,128)(2,1)S(1)} %bitcast.24, ...), custom_call_target="tpu_custom_call" | custom-call | flops 10400000000 | bytes 1024 | tf_op jit(solution)/shard_map/behind_near_0/pallas_call | solution.py:38
  33.3 2.6 %ahead_far_0.1.refs_4_.refs_0_ = bf16[2,192,512]{2,1,0:T(8,128)(2,1)S(1)} custom-call(s32[3]{0:T(128)S(1)} %pad_add_fusion.refs_0_, bf16[192,896]{1,0:T(8,128)(2,1)S(1)} %ahead_rows_0.1.refs_4_.refs_1_, bf16[192,896]{1,0:T(8,128)(2,1)S(1)} %collective-permute-done.refs_2_, bf16[2,1024,1792]{2,1,0:T(8,128)(2,1)S(1)} %bitcast.27, ...), custom_call_target="tpu_custom_call" | custom-call | flops 10400000000 | bytes 1024 | tf_op jit(solution)/shard_map/ahead_far_0/pallas_call | solution.py:38
  41.0 2.6 %behind_far_1.1.refs_2_.refs_1_.refs_0_ = bf16[2,192,512]{2,1,0:T(8,128)(2,1)S(1)} custom-call(s32[3]{0:T(128)S(1)} %pad_add_fusion.refs_0_, bf16[192,896]{1,0:T(8,128)(2,1)S(1)} %behind_rows_1.1.refs_4_.refs_1_, bf16[192,896]{1,0:T(8,128)(2,1)S(1)} %collective-permute-done.8.refs_2_, bf16[2,1024,1792]{2,1,0:T(8,128)(2,1)S(1)} %bitcast.29, ...), custom_call_target="tpu_custom_call" | custom-call | flops 10400000000 | bytes 1024 | tf_op jit(solution)/shard_map/behind_far_1/pallas_call | solution.py:38
  50.8 7.2 %collective-permute-start.13 = (bf16[2,192,512]{2,1,0:T(8,128)(2,1)S(1)}, bf16[2,192,512]{2,1,0:T(8,128)(2,1)S(1)}, u32[]{:S(2)}, u32[]{:S(2)}) collective-permute-start(bf16[2,192,512]{2,1,0:T(8,128)(2,1)S(1)} %behind_outer_1.1.refs_4_), channel_id=1, source_target_pairs={{0,2},{1,3},{2,0},{3,1},{4,6},{5,7},{6,4},{7,5},{8,10},{9,11},{10,... | collective-permute-start | bytes 1179656 | tf_op jit(solution)/shard_map/ppermute | solution.py:221
  69.5 6.8 %collective-permute-done.12.refs_1_ = bf16[2,192,512]{2,1,0:T(8,128)(2,1)S(1)} collective-permute-done((bf16[2,192,512]{2,1,0:T(8,128)(2,1)S(1)}, bf16[2,192,512]{2,1,0:T(8,128)(2,1)S(1)}, u32[]{:S(2)}, u32[]{:S(2)}) %collective-permute-start.12) | collective-permute-done | bytes 393248 | tf_op jit(solution)/shard_map/ppermute | solution.py:221
  77.8 2.8 %collective-permute-start.19 = (bf16[2,192,512]{2,1,0:T(8,128)(2,1)S(1)}, bf16[2,192,512]{2,1,0:T(8,128)(2,1)S(1)}, u32[]{:S(2)}, u32[]{:S(2)}) collective-permute-start(bf16[2,192,512]{2,1,0:T(8,128)(2,1)S(1)} %behind_outer_2.1.refs_2_), channel_id=1, source_target_pairs={{0,2},{1,3},{2,0},{3,1},{4,6},{5,7},{6,4},{7,5},{8,10},{9,11},{10,... | collective-permute-start | bytes 1179656 | tf_op jit(solution)/shard_map/ppermute | solution.py:221
  81.4 8.6 %collective-permute-start.18 = (bf16[2,192,512]{2,1,0:T(8,128)(2,1)S(1)}, bf16[2,192,512]{2,1,0:T(8,128)(2,1)S(1)}, u32[]{:S(2)}, u32[]{:S(2)}) collective-permute-start(bf16[2,192,512]{2,1,0:T(8,128)(2,1)S(1)} %ahead_outer_2.1.refs_5_), channel_id=1, source_target_pairs={{0,2},{1,3},{2,0},{3,1},{4,6},{5,7},{6,4},{7,5},{8,10},{9,11},{10,... | collective-permute-start | bytes 1179656 | tf_op jit(solution)/shard_map/ppermute | solution.py:221
  91.1 8.7 %collective-permute-done.18.refs_0_.refs_1_ = bf16[2,192,512]{2,1,0:T(8,128)(2,1)S(1)} collective-permute-done((bf16[2,192,512]{2,1,0:T(8,128)(2,1)S(1)}, bf16[2,192,512]{2,1,0:T(8,128)(2,1)S(1)}, u32[]{:S(2)}, u32[]{:S(2)}) %collective-permute-start.18) | collective-permute-done | bytes 393248 | tf_op jit(solution)/shard_map/ppermute | solution.py:221
  103.5 8.1 %collective-permute-start.23 = (bf16[1,192,512]{2,1,0:T(8,128)(2,1)S(1)}, bf16[1,192,512]{2,1,0:T(8,128)(2,1)S(1)}, u32[]{:S(2)}, u32[]{:S(2)}) collective-permute-start(bf16[1,192,512]{2,1,0:T(8,128)(2,1)S(1)} %ahead_back_1.1.refs_1_), channel_id=1, source_target_pairs={{0,2},{1,3},{2,0},{3,1},{4,6},{5,7},{6,4},{7,5},{8,10},{9,11},{10,... | collective-permute-start | bytes 589832 | tf_op jit(solution)/shard_map/ppermute | solution.py:221
  112.4 3.1 %copy-done.2 = bf16[1,1,2,1024,1792]{4,3,2,1,0:T(8,128)(2,1)S(1)} copy-done((bf16[1,1,2,1024,1792]{4,3,2,1,0:T(8,128)(2,1)S(1)}, bf16[1,1,2,1024,1792]{4,3,2,1,0:T(8,128)(2,1)}, u32[]{:S(2)}) %copy-start.2) | copy-done | bytes 7340056
  115.5 3.3 %behind_out_0.1 = (bf16[192,896]{1,0:T(8,128)(2,1)S(1)}, bf16[192,896]{1,0:T(8,128)(2,1)S(1)}) custom-call(s32[3]{0:T(128)S(1)} %pad_add_fusion.refs_0_, bf16[2,192,512]{2,1,0:T(8,128)(2,1)S(1)} %behind_act_0.1.refs_2_.refs_1_, bf16[2,192,512]{2,1,0:T(8,128)(2,1)S(1)} %collective-permute-done.19.refs_1_.refs_2_, ...), custom_call_target="tpu_custom_call" | custom-call | flops 20000000000 | bytes 1024 | tf_op jit(solution)/shard_map/behind_out_0/pallas_call | solution.py:38
  118.8 14.4 %collective-permute-start.33 = (bf16[192,896]{1,0:T(8,128)(2,1)S(1)}, bf16[192,896]{1,0:T(8,128)(2,1)S(1)}, u32[]{:S(2)}, u32[]{:S(2)}) collective-permute-start(bf16[192,896]{1,0:T(8,128)(2,1)S(1)} %get-tuple-element.10.refs_1_), channel_id=1, source_target_pairs={{8,1},{9,0},{10,3},{11,2},{12,5},{13,4},{14,7},{15,6},{16,9},{17,8... | collective-permute-start | bytes 1032200 | tf_op jit(solution)/shard_map/ppermute | solution.py:239
  138.5 3.6 %collective-permute-start.25 = (bf16[192,896]{1,0:T(8,128)(2,1)S(1)}, bf16[192,896]{1,0:T(8,128)(2,1)S(1)}, u32[]{:S(2)}, u32[]{:S(2)}) collective-permute-start(bf16[192,896]{1,0:T(8,128)(2,1)S(1)} %get-tuple-element.11.refs_1_), channel_id=1, source_target_pairs={{0,9},{1,8},{2,11},{3,10},{4,13},{5,12},{6,15},{7,14},{8,17},{9,16... | collective-permute-start | bytes 1032200 | tf_op jit(solution)/shard_map/ppermute | solution.py:239
  144.4 4.4 %collective-permute-start.30 = (bf16[2,192,512]{2,1,0:T(8,128)(2,1)S(1)}, bf16[2,192,512]{2,1,0:T(8,128)(2,1)S(1)}, u32[]{:S(2)}, u32[]{:S(2)}) collective-permute-start(bf16[2,192,512]{2,1,0:T(8,128)(2,1)S(1)} %behind_back_2.1.refs_1_), channel_id=1, source_target_pairs={{0,2},{1,3},{2,0},{3,1},{4,6},{5,7},{6,4},{7,5},{8,10},{9,11},{10,... | collective-permute-start | bytes 1179656 | tf_op jit(solution)/shard_map/ppermute | solution.py:221
  150.1 4.4 %collective-permute-start.29 = (bf16[1,192,512]{2,1,0:T(8,128)(2,1)S(1)}, bf16[1,192,512]{2,1,0:T(8,128)(2,1)S(1)}, u32[]{:S(2)}, u32[]{:S(2)}) collective-permute-start(bf16[1,192,512]{2,1,0:T(8,128)(2,1)S(1)} %ahead_back_2.1.refs_6_), channel_id=1, source_target_pairs={{0,2},{1,3},{2,0},{3,1},{4,6},{5,7},{6,4},{7,5},{8,10},{9,11},{10,... | collective-permute-start | bytes 589832 | tf_op jit(solution)/shard_map/ppermute | solution.py:221
  154.6 3.4 %collective-permute-done.30.refs_4_ = bf16[2,192,512]{2,1,0:T(8,128)(2,1)S(1)} collective-permute-done((bf16[2,192,512]{2,1,0:T(8,128)(2,1)S(1)}, bf16[2,192,512]{2,1,0:T(8,128)(2,1)S(1)}, u32[]{:S(2)}, u32[]{:S(2)}) %collective-permute-start.30) | collective-permute-done | bytes 393248 | tf_op jit(solution)/shard_map/ppermute | solution.py:221
  158.0 3.3 %behind_out_1.1 = (bf16[192,896]{1,0:T(8,128)(2,1)S(1)}, bf16[192,896]{1,0:T(8,128)(2,1)S(1)}) custom-call(s32[3]{0:T(128)S(1)} %pad_add_fusion.refs_0_, bf16[2,192,512]{2,1,0:T(8,128)(2,1)S(1)} %copy-done.10, bf16[2,192,512]{2,1,0:T(8,128)(2,1)S(1)} %behind_first_1.1.refs_6_.refs_2_, bf16[2,192,512]{2,1,0:T(8,128)(2,1)S(1)} %collective-permute-done.28.refs_0_.refs_3_, ...), custom_call_target="tpu_custom_call" | custom-call | flops 20000000000 | bytes 1024 | tf_op jit(solution)/shard_map/behind_out_1/pallas_call | solution.py:38
  161.3 4.6 %collective-permute-start.35 = (bf16[192,896]{1,0:T(8,128)(2,1)S(1)}, bf16[192,896]{1,0:T(8,128)(2,1)S(1)}, u32[]{:S(2)}, u32[]{:S(2)}) collective-permute-start(bf16[192,896]{1,0:T(8,128)(2,1)S(1)} %get-tuple-element.13.refs_7_), channel_id=1, source_target_pairs={{8,1},{9,0},{10,3},{11,2},{12,5},{13,4},{14,7},{15,6},{16,9},{17,8... | collective-permute-start | bytes 1032200 | tf_op jit(solution)/shard_map/ppermute | solution.py:239
  170.1 3.6 %collective-permute-start.31 = (bf16[192,896]{1,0:T(8,128)(2,1)S(1)}, bf16[192,896]{1,0:T(8,128)(2,1)S(1)}, u32[]{:S(2)}, u32[]{:S(2)}) collective-permute-start(bf16[192,896]{1,0:T(8,128)(2,1)S(1)} %get-tuple-element.14), channel_id=1, source_target_pairs={{0,9},{1,8},{2,11},{3,10},{4,13},{5,12},{6,15},{7,14},{8,17},{9,16... | collective-permute-start | bytes 1032200 | tf_op jit(solution)/shard_map/ppermute | solution.py:239
  178.6 2.9 %collective-permute-done.32 = bf16[192,896]{1,0:T(8,128)(2,1)S(1)} collective-permute-done((bf16[192,896]{1,0:T(8,128)(2,1)S(1)}, bf16[192,896]{1,0:T(8,128)(2,1)S(1)}, u32[]{:S(2)}, u32[]{:S(2)}) %collective-permute-start.32) | collective-permute-done | bytes 344096 | tf_op jit(solution)/shard_map/ppermute | solution.py:239
  (154 shorter events, 64.6 us)
Async XLA Ops:
  3.9 23.8 %collective-permute-start.1 = (bf16[192,896]{1,0:T(8,128)(2,1)S(1)}, bf16[192,896]{1,0:T(8,128)(2,1)S(1)}, u32[]{:S(2)}, u32[]{:S(2)}) collective-permute-start(bf16[192,896]{1,0:T(8,128)(2,1)S(1)} %grad_rows_0.1.refs_1_), channel_id=1, source_target_pairs={{0,1},{1,0},{2,3},{3,2},{4,5},{5,4},{6,7},{7,6},{8,9},{9,8},{10,11... | collective-permute-start | bytes 1032200 | tf_op jit(solution)/shard_map/ppermute | solution.py:230
  5.0 28.2 %collective-permute-start = (bf16[192,896]{1,0:T(8,128)(2,1)S(1)}, bf16[192,896]{1,0:T(8,128)(2,1)S(1)}, u32[]{:S(2)}, u32[]{:S(2)}) collective-permute-start(bf16[192,896]{1,0:T(8,128)(2,1)S(1)} %ahead_rows_0.1.refs_4_.refs_1_), channel_id=1, source_target_pairs={{0,1},{1,0},{2,3},{3,2},{4,5},{5,4},{6,7},{7,6},{8,9},{9,8},{10,11... | collective-permute-start | bytes 1032200 | tf_op jit(solution)/shard_map/ppermute | solution.py:230
  18.5 21.4 %collective-permute-start.3 = (bf16[2,192,512]{2,1,0:T(8,128)(2,1)S(1)}, bf16[2,192,512]{2,1,0:T(8,128)(2,1)S(1)}, u32[]{:S(2)}, u32[]{:S(2)}) collective-permute-start(bf16[2,192,512]{2,1,0:T(8,128)(2,1)S(1)} %behind_far_0.1.refs_4_.refs_0_), channel_id=1, source_target_pairs={{0,2},{1,3},{2,0},{3,1},{4,6},{5,7},{6,4},{7,5},{8,10},{9,11},{10,... | collective-permute-start | bytes 1179656 | tf_op jit(solution)/shard_map/ppermute | solution.py:221
  26.5 14.3 %collective-permute-start.8 = (bf16[192,896]{1,0:T(8,128)(2,1)S(1)}, bf16[192,896]{1,0:T(8,128)(2,1)S(1)}, u32[]{:S(2)}, u32[]{:S(2)}) collective-permute-start(bf16[192,896]{1,0:T(8,128)(2,1)S(1)} %behind_rows_1.1.refs_4_.refs_1_), channel_id=1, source_target_pairs={{0,1},{1,0},{2,3},{3,2},{4,5},{5,4},{6,7},{7,6},{8,9},{9,8},{10,11... | collective-permute-start | bytes 1032200 | tf_op jit(solution)/shard_map/ppermute | solution.py:230
  30.1 13.6 %collective-permute-start.7 = (bf16[1,192,512]{2,1,0:T(8,128)(2,1)S(1)}, bf16[1,192,512]{2,1,0:T(8,128)(2,1)S(1)}, u32[]{:S(2)}, u32[]{:S(2)}) collective-permute-start(bf16[1,192,512]{2,1,0:T(8,128)(2,1)S(1)} %grad_far_0.1.refs_4_.refs_0_), channel_id=1, source_target_pairs={{0,2},{1,3},{2,0},{3,1},{4,6},{5,7},{6,4},{7,5},{8,10},{9,11},{10,... | collective-permute-start | bytes 589832 | tf_op jit(solution)/shard_map/ppermute | solution.py:221
  32.1 12.3 %collective-permute-start.6 = (bf16[192,896]{1,0:T(8,128)(2,1)S(1)}, bf16[192,896]{1,0:T(8,128)(2,1)S(1)}, u32[]{:S(2)}, u32[]{:S(2)}) collective-permute-start(bf16[192,896]{1,0:T(8,128)(2,1)S(1)} %grad_rows_1.1.refs_4_.refs_1_), channel_id=1, source_target_pairs={{0,1},{1,0},{2,3},{3,2},{4,5},{5,4},{6,7},{7,6},{8,9},{9,8},{10,11... | collective-permute-start | bytes 1032200 | tf_op jit(solution)/shard_map/ppermute | solution.py:230
  40.0 10.2 %collective-permute-start.11 = (bf16[2,192,512]{2,1,0:T(8,128)(2,1)S(1)}, bf16[2,192,512]{2,1,0:T(8,128)(2,1)S(1)}, u32[]{:S(2)}, u32[]{:S(2)}) collective-permute-start(bf16[2,192,512]{2,1,0:T(8,128)(2,1)S(1)} %behind_middle_0.1.refs_1_), channel_id=1, source_target_pairs={{0,0},{1,1},{2,4},{3,5},{4,2},{5,3},{6,6},{7,7},{8,8},{9,9},{10,12... | collective-permute-start | bytes 1179656 | tf_op jit(solution)/shard_map/ppermute | solution.py:221
  43.7 16.8 %collective-permute-start.10 = (bf16[1,192,512]{2,1,0:T(8,128)(2,1)S(1)}, bf16[1,192,512]{2,1,0:T(8,128)(2,1)S(1)}, u32[]{:S(2)}, u32[]{:S(2)}) collective-permute-start(bf16[1,192,512]{2,1,0:T(8,128)(2,1)S(1)} %grad_middle_0.1.refs_4_), channel_id=1, source_target_pairs={{0,0},{1,1},{2,4},{3,5},{4,2},{5,3},{6,6},{7,7},{8,8},{9,9},{10,12... | collective-permute-start | bytes 589832 | tf_op jit(solution)/shard_map/ppermute | solution.py:221
  46.1 16.7 %collective-permute-start.9 = (bf16[2,192,512]{2,1,0:T(8,128)(2,1)S(1)}, bf16[2,192,512]{2,1,0:T(8,128)(2,1)S(1)}, u32[]{:S(2)}, u32[]{:S(2)}) collective-permute-start(bf16[2,192,512]{2,1,0:T(8,128)(2,1)S(1)} %ahead_middle_0.1.refs_4_), channel_id=1, source_target_pairs={{0,0},{1,1},{2,4},{3,5},{4,2},{5,3},{6,6},{7,7},{8,8},{9,9},{10,12... | collective-permute-start | bytes 1179656 | tf_op jit(solution)/shard_map/ppermute | solution.py:221
  50.8 16.9 %collective-permute-start.13 = (bf16[2,192,512]{2,1,0:T(8,128)(2,1)S(1)}, bf16[2,192,512]{2,1,0:T(8,128)(2,1)S(1)}, u32[]{:S(2)}, u32[]{:S(2)}) collective-permute-start(bf16[2,192,512]{2,1,0:T(8,128)(2,1)S(1)} %behind_outer_1.1.refs_4_), channel_id=1, source_target_pairs={{0,2},{1,3},{2,0},{3,1},{4,6},{5,7},{6,4},{7,5},{8,10},{9,11},{10,... | collective-permute-start | bytes 1179656 | tf_op jit(solution)/shard_map/ppermute | solution.py:221
  63.5 12.8 %collective-permute-start.12 = (bf16[2,192,512]{2,1,0:T(8,128)(2,1)S(1)}, bf16[2,192,512]{2,1,0:T(8,128)(2,1)S(1)}, u32[]{:S(2)}, u32[]{:S(2)}) collective-permute-start(bf16[2,192,512]{2,1,0:T(8,128)(2,1)S(1)} %ahead_outer_1.1.refs_4_), channel_id=1, source_target_pairs={{0,2},{1,3},{2,0},{3,1},{4,6},{5,7},{6,4},{7,5},{8,10},{9,11},{10,... | collective-permute-start | bytes 1179656 | tf_op jit(solution)/shard_map/ppermute | solution.py:221
  68.5 12.1 %collective-permute-start.16 = (bf16[1,192,512]{2,1,0:T(8,128)(2,1)S(1)}, bf16[1,192,512]{2,1,0:T(8,128)(2,1)S(1)}, u32[]{:S(2)}, u32[]{:S(2)}) collective-permute-start(bf16[1,192,512]{2,1,0:T(8,128)(2,1)S(1)} %grad_middle_1.1.refs_5_), channel_id=1, source_target_pairs={{0,0},{1,1},{2,4},{3,5},{4,2},{5,3},{6,6},{7,7},{8,8},{9,9},{10,12... | collective-permute-start | bytes 589832 | tf_op jit(solution)/shard_map/ppermute | solution.py:221
  77.8 12.3 %collective-permute-start.19 = (bf16[2,192,512]{2,1,0:T(8,128)(2,1)S(1)}, bf16[2,192,512]{2,1,0:T(8,128)(2,1)S(1)}, u32[]{:S(2)}, u32[]{:S(2)}) collective-permute-start(bf16[2,192,512]{2,1,0:T(8,128)(2,1)S(1)} %behind_outer_2.1.refs_2_), channel_id=1, source_target_pairs={{0,2},{1,3},{2,0},{3,1},{4,6},{5,7},{6,4},{7,5},{8,10},{9,11},{10,... | collective-permute-start | bytes 1179656 | tf_op jit(solution)/shard_map/ppermute | solution.py:221
  81.4 18.3 %collective-permute-start.18 = (bf16[2,192,512]{2,1,0:T(8,128)(2,1)S(1)}, bf16[2,192,512]{2,1,0:T(8,128)(2,1)S(1)}, u32[]{:S(2)}, u32[]{:S(2)}) collective-permute-start(bf16[2,192,512]{2,1,0:T(8,128)(2,1)S(1)} %ahead_outer_2.1.refs_5_), channel_id=1, source_target_pairs={{0,2},{1,3},{2,0},{3,1},{4,6},{5,7},{6,4},{7,5},{8,10},{9,11},{10,... | collective-permute-start | bytes 1179656 | tf_op jit(solution)/shard_map/ppermute | solution.py:221
  100.5 11.2 %collective-permute-start.24 = (bf16[2,192,512]{2,1,0:T(8,128)(2,1)S(1)}, bf16[2,192,512]{2,1,0:T(8,128)(2,1)S(1)}, u32[]{:S(2)}, u32[]{:S(2)}) collective-permute-start(bf16[2,192,512]{2,1,0:T(8,128)(2,1)S(1)} %behind_back_1.1.refs_3_), channel_id=1, source_target_pairs={{0,2},{1,3},{2,0},{3,1},{4,6},{5,7},{6,4},{7,5},{8,10},{9,11},{10,... | collective-permute-start | bytes 1179656 | tf_op jit(solution)/shard_map/ppermute | solution.py:221
  103.5 31.9 %collective-permute-start.23 = (bf16[1,192,512]{2,1,0:T(8,128)(2,1)S(1)}, bf16[1,192,512]{2,1,0:T(8,128)(2,1)S(1)}, u32[]{:S(2)}, u32[]{:S(2)}) collective-permute-start(bf16[1,192,512]{2,1,0:T(8,128)(2,1)S(1)} %ahead_back_1.1.refs_1_), channel_id=1, source_target_pairs={{0,2},{1,3},{2,0},{3,1},{4,6},{5,7},{6,4},{7,5},{8,10},{9,11},{10,... | collective-permute-start | bytes 589832 | tf_op jit(solution)/shard_map/ppermute | solution.py:221
  111.7 32.7 %collective-permute-start.28 = (bf16[2,192,512]{2,1,0:T(8,128)(2,1)S(1)}, bf16[2,192,512]{2,1,0:T(8,128)(2,1)S(1)}, u32[]{:S(2)}, u32[]{:S(2)}) collective-permute-start(bf16[2,192,512]{2,1,0:T(8,128)(2,1)S(1)} %behind_first_1.1.refs_6_.refs_2_), channel_id=1, source_target_pairs={{0,0},{1,1},{2,4},{3,5},{4,2},{5,3},{6,6},{7,7},{8,8},{9,9},{10,12... | collective-permute-start | bytes 1179656 | tf_op jit(solution)/shard_map/ppermute | solution.py:221
  118.8 23.3 %collective-permute-start.33 = (bf16[192,896]{1,0:T(8,128)(2,1)S(1)}, bf16[192,896]{1,0:T(8,128)(2,1)S(1)}, u32[]{:S(2)}, u32[]{:S(2)}) collective-permute-start(bf16[192,896]{1,0:T(8,128)(2,1)S(1)} %get-tuple-element.10.refs_1_), channel_id=1, source_target_pairs={{8,1},{9,0},{10,3},{11,2},{12,5},{13,4},{14,7},{15,6},{16,9},{17,8... | collective-permute-start | bytes 1032200 | tf_op jit(solution)/shard_map/ppermute | solution.py:239
  133.2 11.1 %collective-permute-start.34 = (bf16[192,896]{1,0:T(8,128)(2,1)S(1)}, bf16[192,896]{1,0:T(8,128)(2,1)S(1)}, u32[]{:S(2)}, u32[]{:S(2)}) collective-permute-start(bf16[192,896]{1,0:T(8,128)(2,1)S(1)} %get-tuple-element.16), channel_id=1, source_target_pairs={{8,0},{9,1},{10,2},{11,3},{12,4},{13,5},{14,6},{15,7},{16,8},{17,9... | collective-permute-start | bytes 1032200 | tf_op jit(solution)/shard_map/ppermute | solution.py:239
  135.5 14.6 %collective-permute-start.27 = (bf16[1,192,512]{2,1,0:T(8,128)(2,1)S(1)}, bf16[1,192,512]{2,1,0:T(8,128)(2,1)S(1)}, u32[]{:S(2)}, u32[]{:S(2)}) collective-permute-start(bf16[1,192,512]{2,1,0:T(8,128)(2,1)S(1)} %ahead_first_1.1.refs_7_.refs_2_), channel_id=1, source_target_pairs={{0,0},{1,1},{2,4},{3,5},{4,2},{5,3},{6,6},{7,7},{8,8},{9,9},{10,12... | collective-permute-start | bytes 589832 | tf_op jit(solution)/shard_map/ppermute | solution.py:221
  138.5 10.4 %collective-permute-start.25 = (bf16[192,896]{1,0:T(8,128)(2,1)S(1)}, bf16[192,896]{1,0:T(8,128)(2,1)S(1)}, u32[]{:S(2)}, u32[]{:S(2)}) collective-permute-start(bf16[192,896]{1,0:T(8,128)(2,1)S(1)} %get-tuple-element.11.refs_1_), channel_id=1, source_target_pairs={{0,9},{1,8},{2,11},{3,10},{4,13},{5,12},{6,15},{7,14},{8,17},{9,16... | collective-permute-start | bytes 1032200 | tf_op jit(solution)/shard_map/ppermute | solution.py:239
  144.4 13.5 %collective-permute-start.30 = (bf16[2,192,512]{2,1,0:T(8,128)(2,1)S(1)}, bf16[2,192,512]{2,1,0:T(8,128)(2,1)S(1)}, u32[]{:S(2)}, u32[]{:S(2)}) collective-permute-start(bf16[2,192,512]{2,1,0:T(8,128)(2,1)S(1)} %behind_back_2.1.refs_1_), channel_id=1, source_target_pairs={{0,2},{1,3},{2,0},{3,1},{4,6},{5,7},{6,4},{7,5},{8,10},{9,11},{10,... | collective-permute-start | bytes 1179656 | tf_op jit(solution)/shard_map/ppermute | solution.py:221
  150.1 17.7 %collective-permute-start.29 = (bf16[1,192,512]{2,1,0:T(8,128)(2,1)S(1)}, bf16[1,192,512]{2,1,0:T(8,128)(2,1)S(1)}, u32[]{:S(2)}, u32[]{:S(2)}) collective-permute-start(bf16[1,192,512]{2,1,0:T(8,128)(2,1)S(1)} %ahead_back_2.1.refs_6_), channel_id=1, source_target_pairs={{0,2},{1,3},{2,0},{3,1},{4,6},{5,7},{6,4},{7,5},{8,10},{9,11},{10,... | collective-permute-start | bytes 589832 | tf_op jit(solution)/shard_map/ppermute | solution.py:221
  161.3 14.3 %collective-permute-start.35 = (bf16[192,896]{1,0:T(8,128)(2,1)S(1)}, bf16[192,896]{1,0:T(8,128)(2,1)S(1)}, u32[]{:S(2)}, u32[]{:S(2)}) collective-permute-start(bf16[192,896]{1,0:T(8,128)(2,1)S(1)} %get-tuple-element.13.refs_7_), channel_id=1, source_target_pairs={{8,1},{9,0},{10,3},{11,2},{12,5},{13,4},{14,7},{15,6},{16,9},{17,8... | collective-permute-start | bytes 1032200 | tf_op jit(solution)/shard_map/ppermute | solution.py:239
  (35 other events, 233.9 us)

commit v7 on v6

--- a/solution.py
+++ b/solution.py
@@ -12,7 +12,7 @@
 F32 = jnp.float32
 MIB = 1024 * 1024
 PIECES = 2
-ROWS, SMALL, ACT, FIRST, AHEAD_OUT, BEHIND_OUT = 20, 1.6, 10, 5.2, 12, 20
+ROWS, SMALL, ACT, FIRST, AHEAD_OUT, BEHIND_OUT = 20, 6, 10, 5.2, 3, 20
 
 
 def shift(shard, axis, by):
@@ -55,21 +55,42 @@
     out[...] = rows[...]
 
 
+def touch_kernel(out):
+    out[...] = jnp.zeros_like(out)
+
+
 def cut_first_kernel(value, out):
     out[...] = value[: out.shape[0]]
 
 
-def first_kernel(width, where, own, partner, tile, out, joined):
-    @pl.when((pl.program_id(0) == 0) & (pl.program_id(1) == 0))
-    def _():
-        at = pl.multiple_of(where[1] * width, 128)
-        other = pl.multiple_of((1 - where[1]) * width, 128)
-        joined[:, pl.ds(at, width)] = own[...]
-        joined[:, pl.ds(other, width)] = partner[...]
-
-    out[0] = lax.dot_general(
-        joined[...], tile[0], (((1,), (1,)), ((), ())), preferred_element_type=F32
-    ).astype(BF16)
+def first_kernel(width, far, where, own, partner, weights, out, joined, tiles, sems):
+    parts, slots, half = out.shape
+    tile = tiles.shape[1]
+    steps = half // tile
+    side = 1 - where[0] if far else where[0]
+    copies = []
+    for k in range(parts):
+        for j in range(steps):
+            at = pl.multiple_of((side * steps + j) * tile, tile)
+            copy = pltpu.make_async_copy(
+                weights.at[k, pl.ds(at, tile)], tiles.at[k * steps + j], sems.at[k * steps + j]
+            )
+            copy.start()
+            copies.append(copy)
+    at = pl.multiple_of(where[1] * width, 128)
+    other = pl.multiple_of((1 - where[1]) * width, 128)
+    joined[:slots, pl.ds(at, width)] = own[...]
+    joined[:slots, pl.ds(other, width)] = partner[...]
+    for k in range(parts):
+        for j in range(steps):
+            copies[k * steps + j].wait()
+            product = lax.dot_general(
+                tiles[k * steps + j],
+                joined[...],
+                (((1,), (1,)), ((), ())),
+                preferred_element_type=F32,
+            )
+            out[k, :, j * tile : (j + 1) * tile] = product.T[:slots].astype(BF16)
 
 
 def first_product(name, where, far, rows, weights, after):
@@ -78,21 +99,19 @@
     half = units // 2
     tile = min(256, half)
     steps = half // tile
-
-    def tile_at(k, j, w):
-        return (k, ((1 - w[0]) if far else w[0]) * steps + j, 0)
-
     return call(
-        functools.partial(first_kernel, width),
+        functools.partial(first_kernel, width, far),
         FIRST * parts,
         (*rows, weights),
         after,
         jax.ShapeDtypeStruct((parts, slots, half), BF16),
         scalars=(where,),
-        grid=(parts, steps),
-        in_specs=[*[whole(r) for r in rows], pl.BlockSpec((1, tile, features), tile_at)],
-        out_specs=pl.BlockSpec((1, slots, tile), lambda k, j, w: (k, 0, j)),
-        scratch=[pltpu.VMEM((slots, features), BF16)],
+        in_specs=[*[whole(r) for r in rows], pl.BlockSpec(memory_space=pltpu.HBM)],
+        scratch=[
+            pltpu.VMEM((-(-slots // 128) * 128, features), BF16),
+            pltpu.VMEM((parts * steps, tile, features), BF16),
+            pltpu.SemaphoreType.DMA((parts * steps,)),
+        ],
         name=name,
     )
 
@@ -141,8 +160,17 @@
 
 def second_kernel(scaled, where, act, one, two, three, *refs):
     scale, refs = (refs[0], refs[1:]) if scaled else (None, refs)
-    tile, give, keep, joined = refs
+    weights, give, keep, joined, tiles, sems = refs
     kinds, _, half = act.shape
+    _, _, units, width = tiles.shape
+    copies = []
+    for own in range(2):
+        at = pl.multiple_of((where[1] if own else 1 - where[1]) * width, 128)
+        copy = pltpu.make_async_copy(
+            weights.at[:, :, pl.ds(at, width)], tiles.at[own], sems.at[own]
+        )
+        copy.start()
+        copies.append(copy)
 
     def place(near, far):
         for kind in range(kinds):
@@ -151,40 +179,28 @@
             joined[:, pl.ds(at, half)] = near[kind]
             joined[:, pl.ds(other, half)] = far[kind]
 
-    first = pl.program_id(0) == 0
-
-    @pl.when(first & (where[2] == 1))
+    @pl.when(where[2] == 1)
     def _():
         place(act, three)
 
-    @pl.when(first & (where[2] == 0))
+    @pl.when(where[2] == 0)
     def _():
         place(one, two)
 
-    kinds, units, width = tile.shape
-    share = jnp.dot(
-        joined[...], tile[...].reshape(kinds * units, width), preferred_element_type=F32
-    )
-    if scaled:
-        share = share * scale[...]
-
-    @pl.when(first)
-    def _():
-        give[...] = share.astype(BF16)
-
-    @pl.when(pl.program_id(0) == 1)
-    def _():
-        keep[...] = share.astype(BF16)
+    for own, out in enumerate((give, keep)):
+        copies[own].wait()
+        share = jnp.dot(
+            joined[...], tiles[own].reshape(kinds * units, width), preferred_element_type=F32
+        )
+        if scaled:
+            share = share * scale[...]
+        out[...] = share.astype(BF16)
 
 
 def second_product(name, where, values, scale, weights, after):
     kinds, units, features = weights.shape
     slots = values[0].shape[1]
     width = features // 2
-
-    def tile_at(own, w):
-        return (0, 0, jnp.where(own == 0, 1 - w[1], w[1]))
-
     operands = [*values] + ([] if scale is None else [scale])
     share = jax.ShapeDtypeStruct((slots, width), BF16)
     return call(
@@ -194,9 +210,12 @@
         after,
         (share, share),
         scalars=(where,),
-        grid=(2,),
-        in_specs=[*[whole(v) for v in operands], pl.BlockSpec((kinds, units, width), tile_at)],
-        scratch=[pltpu.VMEM((slots, kinds * units), BF16)],
+        in_specs=[*[whole(v) for v in operands], pl.BlockSpec(memory_space=pltpu.HBM)],
+        scratch=[
+            pltpu.VMEM((slots, kinds * units), BF16),
+            pltpu.VMEM((2, kinds, units, width), BF16),
+            pltpu.SemaphoreType.DMA((2,)),
+        ],
         name=name,
     )
 
@@ -370,46 +389,58 @@
         ]
         return jnp.concatenate(sums)[None]
 
-    chains = (behind, grad, ahead)
-    last = PIECES - 1
-    for chain in chains:
+    for chain in (behind, grad, ahead):
         chain.fetch(0)
-    for chain in chains:
-        chain.product(0, True)
-        chain.outer_sum(0)
-        chain.product(0, False)
-        if chain is not ahead:
-            chain.fetch(1)
-    for c in range(PIECES):
-        for chain in chains:
-            chain.middle_sum(c)
-            if chain is grad and c > 0:
-                activate_behind(c - 1)
-            if chain is ahead and c > 0:
-                activate_ahead(c - 1)
-            if c == 0 and chain is behind:
-                ahead.fetch(1)
-            if c < last:
-                chain.product(c + 1, True)
-        for chain in chains:
-            chain.outer_sum(c + 1)
-            if c < last:
-                chain.product(c + 1, False)
-    for c in range(PIECES):
-        behind.middle_pass(c)
-        if c == 0:
-            activate_behind(last)
-        else:
-            finish(behind, c - 1)
-        ahead.middle_pass(c)
-        if c == 0:
-            activate_ahead(last)
-        else:
-            finish(ahead, c - 1)
-        behind.outer_pass(c + 1)
-        ahead.outer_pass(c + 1)
-    finish(behind, last)
-    finish(ahead, last)
+    touched = call(
+        touch_kernel, ROWS, (), [*recent, gates, downs], jax.ShapeDtypeStruct((8, 128), F32), name="touch"
+    )
+    recent[:] = [touched]
+    behind.product(0, True)
+    behind.outer_sum(0)
+    behind.fetch(1)
+    grad.product(0, True)
+    grad.outer_sum(0)
+    behind.product(0, False)
+    behind.middle_sum(0)
+    grad.fetch(1)
+    ahead.product(0, True)
+    ahead.outer_sum(0)
+    grad.middle_sum(0)
+    grad.product(0, False)
+    behind.product(1, True)
+    behind.outer_sum(1)
+    ahead.fetch(1)
+    ahead.product(0, False)
+    ahead.middle_sum(0)
+    grad.product(1, True)
+    grad.outer_sum(1)
+    behind.product(1, False)
+    behind.middle_sum(1)
+    ahead.product(1, True)
+    ahead.outer_sum(1)
+    grad.middle_sum(1)
+    activate_behind(0)
+    grad.product(1, False)
+    behind.outer_sum(2)
+    ahead.product(1, False)
+    ahead.middle_sum(1)
+    activate_ahead(0)
+    grad.outer_sum(2)
+    behind.middle_pass(0)
+    ahead.outer_sum(2)
+    activate_behind(1)
+    behind.outer_pass(1)
+    ahead.middle_pass(0)
+    activate_ahead(1)
+    ahead.outer_pass(1)
+    behind.middle_pass(1)
+    finish(behind, 0)
+    ahead.middle_pass(1)
+    behind.outer_pass(2)
+    ahead.outer_pass(2)
+    finish(ahead, 0)
+    finish(behind, 1)
+    finish(ahead, 1)
     return result(True), result(False)
 
 

time: 184 us -> 180 us (0.978)
  Pallas kernels: 46 us -> 64.5 us
  waiting for transfers between devices: 30.4 us -> 13.8 us
  local copies, waits for them, and re-layouts: 12.2 us -> 7.89 us
    ppermute x23, waiting for transfers between devices: 18.9 us -> 0.29 us  [between(): return lax.ppermute(value, 'expert', pairs)]
    pallas_call x45 -> x46, Pallas kernels: 46 us -> 64.5 us  [call(): pl.pallas_call(run, compiler_params=pltpu.CompilerParams(vmem_limit_bytes...]
    ppermute x8, waiting for transfers between devices: 6.03 us -> 11.7 us  [to_section(): return lax.ppermute(value, ('section', 'expert'), pairs)]
    unnamed x44 -> x26, local copies, waits for them, and re-layouts: 11.1 us -> 7.33 us
    ppermute x6, waiting for transfers between devices: 5.48 us -> 1.83 us  [swapped(): return lax.ppermute(value, 'expert', [(i, i ^ 1) for i in range(devices)])]
  transfers between devices with their start and end apart: 37 -> 37, of which waited for: 8 -> 6; matrix products, arithmetic and copies ran while one was open for 1% -> 1% of each run, Pallas kernels for 25% -> 36%
where the time goes in v7:
time: 180 us; the launch traced here: 179 us
  starting transfers between devices  89.2 us (50%)
  Pallas kernels  64.5 us (36%)
  waiting for transfers between devices  13.8 us (8%)
  local copies, waits for them, and re-layouts  7.89 us (4%)
  other arithmetic  2.29 us (1%)
    pallas_call x46, Pallas kernels, call(): pl.pallas_call(run, compiler_params=pltpu.CompilerParams(vmem_limit_bytes...  64.5 us
    ppermute x23, starting transfers between devices, between(): return lax.ppermute(value, 'expert', pairs)  48 us
    ppermute x8, starting transfers between devices, to_section(): return lax.ppermute(value, ('section', 'expert'), pairs)  34.1 us
    ppermute x8, waiting for transfers between devices, to_section(): return lax.ppermute(value, ('section', 'expert'), pairs)  11.7 us
    unnamed x26, local copies, waits for them, and re-layouts  7.33 us
    ppermute x6, starting transfers between devices, swapped(): return lax.ppermute(value, 'expert', [(i, i ^ 1) for i in range(devices)])  7.1 us
  transfers between devices with their start and end apart: 37, of which 6 were waited for; matrix products, arithmetic and copies ran while one was open for 1% of the time, Pallas kernels for 36%

profile of v7, /device:TPU:1, one launch (start us, length us, event | category | flops | bytes accessed | tf_op | source)
XLA Modules:
  0.0 179.1 jit_solution(3542178783027696455)
XLA Ops:
  11.8 3.1 %copy-done = bf16[1,1,2,1024,1792]{4,3,2,1,0:T(8,128)(2,1)S(1)} copy-done((bf16[1,1,2,1024,1792]{4,3,2,1,0:T(8,128)(2,1)S(1)}, bf16[1,1,2,1024,1792]{4,3,2,1,0:T(8,128)(2,1)}, u32[]{:S(2)}) %copy-start) | copy-done | bytes 7340056
  14.9 5.7 %behind_far_0.1.refs_1_.refs_0_ = bf16[2,192,512]{2,1,0:T(8,128)(2,1)S(1)} custom-call(s32[3]{0:T(128)S(1)} %pad_add_fusion.refs_0_, bf16[192,896]{1,0:T(8,128)(2,1)S(1)} %behind_rows_0.1.refs_1_, bf16[192,896]{1,0:T(8,128)(2,1)} %collective-permute-done.1.refs_2_, bf16[2,1024,1792]{2,1,0:T(8,128)(2,1)S(1)} %bitcast.26, f32[8,128]{1,0:T(8,128)S(1)} %touch.1.refs_4_), custom_call_target="tpu_custom_call" | custom-call | flops 10400000000 | bytes 1024 | tf_op jit(solution)/shard_map/behind_far_0/pallas_call | solution.py:38
  26.4 5.4 %behind_near_0.1.refs_2_.refs_0_ = bf16[2,192,512]{2,1,0:T(8,128)(2,1)S(1)} custom-call(s32[3]{0:T(128)S(1)} %pad_add_fusion.refs_0_, bf16[192,896]{1,0:T(8,128)(2,1)S(1)} %behind_rows_0.1.refs_1_, bf16[192,896]{1,0:T(8,128)(2,1)} %collective-permute-done.1.refs_2_, bf16[2,1024,1792]{2,1,0:T(8,128)(2,1)S(1)} %bitcast.29, ...), custom_call_target="tpu_custom_call" | custom-call | flops 10400000000 | bytes 1024 | tf_op jit(solution)/shard_map/behind_near_0/pallas_call | solution.py:38
  33.9 4.4 %ahead_far_0.1.refs_2_.refs_0_ = bf16[2,192,512]{2,1,0:T(8,128)(2,1)S(1)} custom-call(s32[3]{0:T(128)S(1)} %pad_add_fusion.refs_0_, bf16[192,896]{1,0:T(8,128)(2,1)S(1)} %ahead_rows_0.1.refs_0_.refs_1_, bf16[192,896]{1,0:T(8,128)(2,1)S(1)} %collective-permute-done.refs_2_, bf16[2,1024,1792]{2,1,0:T(8,128)(2,1)S(1)} %bitcast.30, ...), custom_call_target="tpu_custom_call" | custom-call | flops 10400000000 | bytes 1024 | tf_op jit(solution)/shard_map/ahead_far_0/pallas_call | solution.py:38
  38.4 3.9 %collective-permute-start.10 = (bf16[2,192,512]{2,1,0:T(8,128)(2,1)S(1)}, bf16[2,192,512]{2,1,0:T(8,128)(2,1)S(1)}, u32[]{:S(2)}, u32[]{:S(2)}) collective-permute-start(bf16[2,192,512]{2,1,0:T(8,128)(2,1)S(1)} %ahead_far_0.1.refs_2_.refs_0_), channel_id=1, source_target_pairs={{0,2},{1,3},{2,0},{3,1},{4,6},{5,7},{6,4},{7,5},{8,10},{9,11},{10,... | collective-permute-start | bytes 1179656 | tf_op jit(solution)/shard_map/ppermute | solution.py:240
  45.5 4.4 %behind_far_1.1.refs_1_.refs_4_.refs_0_ = bf16[2,192,512]{2,1,0:T(8,128)(2,1)S(1)} custom-call(s32[3]{0:T(128)S(1)} %pad_add_fusion.refs_0_, bf16[192,896]{1,0:T(8,128)(2,1)S(1)} %behind_rows_1.1.refs_4_.refs_1_, bf16[192,896]{1,0:T(8,128)(2,1)S(1)} %collective-permute-done.2.refs_2_, bf16[2,1024,1792]{2,1,0:T(8,128)(2,1)S(1)} %bitcast.31, ...), custom_call_target="tpu_custom_call" | custom-call | flops 10400000000 | bytes 1024 | tf_op jit(solution)/shard_map/behind_far_1/pallas_call | solution.py:38
  52.2 4.4 %ahead_near_0.1.refs_2_.refs_0_ = bf16[2,192,512]{2,1,0:T(8,128)(2,1)S(1)} custom-call(s32[3]{0:T(128)S(1)} %pad_add_fusion.refs_0_, bf16[192,896]{1,0:T(8,128)(2,1)S(1)} %ahead_rows_0.1.refs_0_.refs_1_, bf16[192,896]{1,0:T(8,128)(2,1)S(1)} %collective-permute-done.refs_2_, bf16[2,1024,1792]{2,1,0:T(8,128)(2,1)S(1)} %bitcast.32, ...), custom_call_target="tpu_custom_call" | custom-call | flops 10400000000 | bytes 1024 | tf_op jit(solution)/shard_map/ahead_near_0/pallas_call | solution.py:38
  60.8 2.9 %collective-permute-start.14 = (bf16[1,192,512]{2,1,0:T(8,128)(2,1)S(1)}, bf16[1,192,512]{2,1,0:T(8,128)(2,1)S(1)}, u32[]{:S(2)}, u32[]{:S(2)}) collective-permute-start(bf16[1,192,512]{2,1,0:T(8,128)(2,1)S(1)} %grad_outer_1.1.refs_4_), channel_id=1, source_target_pairs={{0,2},{1,3},{2,0},{3,1},{4,6},{5,7},{6,4},{7,5},{8,10},{9,11},{10,... | collective-permute-start | bytes 589832 | tf_op jit(solution)/shard_map/ppermute | solution.py:240
  63.6 4.4 %behind_near_1.1.refs_2_.refs_0_ = bf16[2,192,512]{2,1,0:T(8,128)(2,1)S(1)} custom-call(s32[3]{0:T(128)S(1)} %pad_add_fusion.refs_0_, bf16[192,896]{1,0:T(8,128)(2,1)S(1)} %behind_rows_1.1.refs_4_.refs_1_, bf16[192,896]{1,0:T(8,128)(2,1)S(1)} %collective-permute-done.2.refs_2_, bf16[2,1024,1792]{2,1,0:T(8,128)(2,1)S(1)} %bitcast.33, ...), custom_call_target="tpu_custom_call" | custom-call | flops 10400000000 | bytes 1024 | tf_op jit(solution)/shard_map/behind_near_1/pallas_call | solution.py:38
  68.9 4.4 %ahead_far_1.1.refs_1_.refs_4_.refs_0_ = bf16[2,192,512]{2,1,0:T(8,128)(2,1)S(1)} custom-call(s32[3]{0:T(128)S(1)} %pad_add_fusion.refs_0_, bf16[192,896]{1,0:T(8,128)(2,1)S(1)} %ahead_rows_1.1.refs_4_.refs_1_, bf16[192,896]{1,0:T(8,128)(2,1)S(1)} %collective-permute-done.7.refs_2_, bf16[2,1024,1792]{2,1,0:T(8,128)(2,1)S(1)} %bitcast.34, ...), custom_call_target="tpu_custom_call" | custom-call | flops 10400000000 | bytes 1024 | tf_op jit(solution)/shard_map/ahead_far_1/pallas_call | solution.py:38
  79.6 2.7 %collective-permute-start.19 = (bf16[2,192,512]{2,1,0:T(8,128)(2,1)S(1)}, bf16[2,192,512]{2,1,0:T(8,128)(2,1)S(1)}, u32[]{:S(2)}, u32[]{:S(2)}) collective-permute-start(bf16[2,192,512]{2,1,0:T(8,128)(2,1)S(1)} %behind_outer_2.1.refs_4_), channel_id=1, source_target_pairs={{0,2},{1,3},{2,0},{3,1},{4,6},{5,7},{6,4},{7,5},{8,10},{9,11},{10,... | collective-permute-start | bytes 1179656 | tf_op jit(solution)/shard_map/ppermute | solution.py:240
  82.3 4.4 %ahead_near_1.1.refs_2_.refs_0_ = bf16[2,192,512]{2,1,0:T(8,128)(2,1)S(1)} custom-call(s32[3]{0:T(128)S(1)} %pad_add_fusion.refs_0_, bf16[192,896]{1,0:T(8,128)(2,1)S(1)} %ahead_rows_1.1.refs_4_.refs_1_, bf16[192,896]{1,0:T(8,128)(2,1)S(1)} %collective-permute-done.7.refs_2_, bf16[2,1024,1792]{2,1,0:T(8,128)(2,1)S(1)} %bitcast.35, ...), custom_call_target="tpu_custom_call" | custom-call | flops 10400000000 | bytes 1024 | tf_op jit(solution)/shard_map/ahead_near_1/pallas_call | solution.py:38
  89.8 6.6 %collective-permute-start.18 = (bf16[2,192,512]{2,1,0:T(8,128)(2,1)S(1)}, bf16[2,192,512]{2,1,0:T(8,128)(2,1)S(1)}, u32[]{:S(2)}, u32[]{:S(2)}) collective-permute-start(bf16[2,192,512]{2,1,0:T(8,128)(2,1)S(1)} %ahead_outer_2.1.refs_5_), channel_id=1, source_target_pairs={{0,2},{1,3},{2,0},{3,1},{4,6},{5,7},{6,4},{7,5},{8,10},{9,11},{10,... | collective-permute-start | bytes 1179656 | tf_op jit(solution)/shard_map/ppermute | solution.py:240
  98.0 7.8 %collective-permute-start.24 = (bf16[2,192,512]{2,1,0:T(8,128)(2,1)S(1)}, bf16[2,192,512]{2,1,0:T(8,128)(2,1)S(1)}, u32[]{:S(2)}, u32[]{:S(2)}) collective-permute-start(bf16[2,192,512]{2,1,0:T(8,128)(2,1)S(1)} %behind_back_1.1.refs_1_), channel_id=1, source_target_pairs={{0,2},{1,3},{2,0},{3,1},{4,6},{5,7},{6,4},{7,5},{8,10},{9,11},{10,... | collective-permute-start | bytes 1179656 | tf_op jit(solution)/shard_map/ppermute | solution.py:240
  107.2 7.9 %collective-permute-start.23 = (bf16[1,192,512]{2,1,0:T(8,128)(2,1)S(1)}, bf16[1,192,512]{2,1,0:T(8,128)(2,1)S(1)}, u32[]{:S(2)}, u32[]{:S(2)}) collective-permute-start(bf16[1,192,512]{2,1,0:T(8,128)(2,1)S(1)} %ahead_back_1.1.refs_1_), channel_id=1, source_target_pairs={{0,2},{1,3},{2,0},{3,1},{4,6},{5,7},{6,4},{7,5},{8,10},{9,11},{10,... | collective-permute-start | bytes 589832 | tf_op jit(solution)/shard_map/ppermute | solution.py:240
  115.9 3.2 %behind_out_0.1 = (bf16[192,896]{1,0:T(8,128)(2,1)S(1)}, bf16[192,896]{1,0:T(8,128)(2,1)S(1)}) custom-call(s32[3]{0:T(128)S(1)} %pad_add_fusion.refs_0_, bf16[2,192,512]{2,1,0:T(8,128)(2,1)S(1)} %behind_act_0.1.refs_4_.refs_1_, bf16[2,192,512]{2,1,0:T(8,128)(2,1)S(1)} %collective-permute-done.19.refs_1_.refs_2_, ...), custom_call_target="tpu_custom_call" | custom-call | flops 20000000000 | bytes 1024 | tf_op jit(solution)/shard_map/behind_out_0/pallas_call | solution.py:38
  119.1 13.6 %collective-permute-start.33 = (bf16[192,896]{1,0:T(8,128)(2,1)S(1)}, bf16[192,896]{1,0:T(8,128)(2,1)S(1)}, u32[]{:S(2)}, u32[]{:S(2)}) collective-permute-start(bf16[192,896]{1,0:T(8,128)(2,1)S(1)} %get-tuple-element.10.refs_1_), channel_id=1, source_target_pairs={{8,1},{9,0},{10,3},{11,2},{12,5},{13,4},{14,7},{15,6},{16,9},{17,8... | collective-permute-start | bytes 1032200 | tf_op jit(solution)/shard_map/ppermute | solution.py:258
  135.4 5.2 %collective-permute-done.33 = bf16[192,896]{1,0:T(8,128)(2,1)S(1)} collective-permute-done((bf16[192,896]{1,0:T(8,128)(2,1)S(1)}, bf16[192,896]{1,0:T(8,128)(2,1)S(1)}, u32[]{:S(2)}, u32[]{:S(2)}) %collective-permute-start.33) | collective-permute-done | bytes 344096 | tf_op jit(solution)/shard_map/ppermute | solution.py:258
  142.2 3.1 %collective-permute-start.30 = (bf16[2,192,512]{2,1,0:T(8,128)(2,1)S(1)}, bf16[2,192,512]{2,1,0:T(8,128)(2,1)S(1)}, u32[]{:S(2)}, u32[]{:S(2)}) collective-permute-start(bf16[2,192,512]{2,1,0:T(8,128)(2,1)S(1)} %behind_back_2.1.refs_1_), channel_id=1, source_target_pairs={{0,2},{1,3},{2,0},{3,1},{4,6},{5,7},{6,4},{7,5},{8,10},{9,11},{10,... | collective-permute-start | bytes 1179656 | tf_op jit(solution)/shard_map/ppermute | solution.py:240
  147.6 4.8 %collective-permute-start.27 = (bf16[192,896]{1,0:T(8,128)(2,1)S(1)}, bf16[192,896]{1,0:T(8,128)(2,1)S(1)}, u32[]{:S(2)}, u32[]{:S(2)}) collective-permute-start(bf16[192,896]{1,0:T(8,128)(2,1)S(1)} %get-tuple-element.11.refs_6_), channel_id=1, source_target_pairs={{0,9},{1,8},{2,11},{3,10},{4,13},{5,12},{6,15},{7,14},{8,17},{9,16... | collective-permute-start | bytes 1032200 | tf_op jit(solution)/shard_map/ppermute | solution.py:258
  154.5 3.4 %behind_out_1.1 = (bf16[192,896]{1,0:T(8,128)(2,1)S(1)}, bf16[192,896]{1,0:T(8,128)(2,1)S(1)}) custom-call(s32[3]{0:T(128)S(1)} %pad_add_fusion.refs_0_, bf16[2,192,512]{2,1,0:T(8,128)(2,1)S(1)} %behind_act_1.1.refs_1_.refs_3_, bf16[2,192,512]{2,1,0:T(8,128)(2,1)S(1)} %behind_first_1.1.refs_6_.refs_2_, ...), custom_call_target="tpu_custom_call" | custom-call | flops 20000000000 | bytes 1024 | tf_op jit(solution)/shard_map/behind_out_1/pallas_call | solution.py:38
  157.9 3.9 %collective-permute-start.35 = (bf16[192,896]{1,0:T(8,128)(2,1)S(1)}, bf16[192,896]{1,0:T(8,128)(2,1)S(1)}, u32[]{:S(2)}, u32[]{:S(2)}) collective-permute-start(bf16[192,896]{1,0:T(8,128)(2,1)S(1)} %get-tuple-element.13.refs_7_), channel_id=1, source_target_pairs={{8,1},{9,0},{10,3},{11,2},{12,5},{13,4},{14,7},{15,6},{16,9},{17,8... | collective-permute-start | bytes 1032200 | tf_op jit(solution)/shard_map/ppermute | solution.py:258
  166.0 4.2 %collective-permute-start.31 = (bf16[192,896]{1,0:T(8,128)(2,1)S(1)}, bf16[192,896]{1,0:T(8,128)(2,1)S(1)}, u32[]{:S(2)}, u32[]{:S(2)}) collective-permute-start(bf16[192,896]{1,0:T(8,128)(2,1)S(1)} %get-tuple-element.14), channel_id=1, source_target_pairs={{0,9},{1,8},{2,11},{3,10},{4,13},{5,12},{6,15},{7,14},{8,17},{9,16... | collective-permute-start | bytes 1032200 | tf_op jit(solution)/shard_map/ppermute | solution.py:258
  174.6 3.4 %collective-permute-done.32 = bf16[192,896]{1,0:T(8,128)(2,1)S(1)} collective-permute-done((bf16[192,896]{1,0:T(8,128)(2,1)S(1)}, bf16[192,896]{1,0:T(8,128)(2,1)S(1)}, u32[]{:S(2)}, u32[]{:S(2)}) %collective-permute-start.32) | collective-permute-done | bytes 344096 | tf_op jit(solution)/shard_map/ppermute | solution.py:258
  (137 shorter events, 60.4 us)
Async XLA Ops:
  3.9 19.2 %collective-permute-start.3 = (bf16[192,896]{1,0:T(8,128)(2,1)S(1)}, bf16[192,896]{1,0:T(8,128)(2,1)S(1)}, u32[]{:S(2)}, u32[]{:S(2)}) collective-permute-start(bf16[192,896]{1,0:T(8,128)(2,1)S(1)} %grad_rows_0.1.refs_1_), channel_id=1, source_target_pairs={{0,1},{1,0},{2,3},{3,2},{4,5},{5,4},{6,7},{7,6},{8,9},{9,8},{10,11... | collective-permute-start | bytes 1032200 | tf_op jit(solution)/shard_map/ppermute | solution.py:249
  5.0 28.9 %collective-permute-start = (bf16[192,896]{1,0:T(8,128)(2,1)S(1)}, bf16[192,896]{1,0:T(8,128)(2,1)S(1)}, u32[]{:S(2)}, u32[]{:S(2)}) collective-permute-start(bf16[192,896]{1,0:T(8,128)(2,1)S(1)} %ahead_rows_0.1.refs_0_.refs_1_), channel_id=1, source_target_pairs={{0,1},{1,0},{2,3},{3,2},{4,5},{5,4},{6,7},{7,6},{8,9},{9,8},{10,11... | collective-permute-start | bytes 1032200 | tf_op jit(solution)/shard_map/ppermute | solution.py:249
  21.9 23.7 %collective-permute-start.2 = (bf16[192,896]{1,0:T(8,128)(2,1)S(1)}, bf16[192,896]{1,0:T(8,128)(2,1)S(1)}, u32[]{:S(2)}, u32[]{:S(2)}) collective-permute-start(bf16[192,896]{1,0:T(8,128)(2,1)S(1)} %behind_rows_1.1.refs_4_.refs_1_), channel_id=1, source_target_pairs={{0,1},{1,0},{2,3},{3,2},{4,5},{5,4},{6,7},{7,6},{8,9},{9,8},{10,11... | collective-permute-start | bytes 1032200 | tf_op jit(solution)/shard_map/ppermute | solution.py:249
  25.7 16.6 %collective-permute-start.4 = (bf16[1,192,512]{2,1,0:T(8,128)(2,1)S(1)}, bf16[1,192,512]{2,1,0:T(8,128)(2,1)S(1)}, u32[]{:S(2)}, u32[]{:S(2)}) collective-permute-start(bf16[1,192,512]{2,1,0:T(8,128)(2,1)S(1)} %grad_far_0.1.refs_4_.refs_0_), channel_id=1, source_target_pairs={{0,2},{1,3},{2,0},{3,1},{4,6},{5,7},{6,4},{7,5},{8,10},{9,11},{10,... | collective-permute-start | bytes 589832 | tf_op jit(solution)/shard_map/ppermute | solution.py:240
  31.9 18.1 %collective-permute-start.6 = (bf16[2,192,512]{2,1,0:T(8,128)(2,1)S(1)}, bf16[2,192,512]{2,1,0:T(8,128)(2,1)S(1)}, u32[]{:S(2)}, u32[]{:S(2)}) collective-permute-start(bf16[2,192,512]{2,1,0:T(8,128)(2,1)S(1)} %behind_middle_0.1.refs_1_), channel_id=1, source_target_pairs={{0,0},{1,1},{2,4},{3,5},{4,2},{5,3},{6,6},{7,7},{8,8},{9,9},{10,12... | collective-permute-start | bytes 1179656 | tf_op jit(solution)/shard_map/ppermute | solution.py:240
  32.6 24.9 %collective-permute-start.9 = (bf16[192,896]{1,0:T(8,128)(2,1)S(1)}, bf16[192,896]{1,0:T(8,128)(2,1)S(1)}, u32[]{:S(2)}, u32[]{:S(2)}) collective-permute-start(bf16[192,896]{1,0:T(8,128)(2,1)S(1)} %grad_rows_1.1.refs_4_.refs_1_), channel_id=1, source_target_pairs={{0,1},{1,0},{2,3},{3,2},{4,5},{5,4},{6,7},{7,6},{8,9},{9,8},{10,11... | collective-permute-start | bytes 1032200 | tf_op jit(solution)/shard_map/ppermute | solution.py:249
  38.4 18.3 %collective-permute-start.10 = (bf16[2,192,512]{2,1,0:T(8,128)(2,1)S(1)}, bf16[2,192,512]{2,1,0:T(8,128)(2,1)S(1)}, u32[]{:S(2)}, u32[]{:S(2)}) collective-permute-start(bf16[2,192,512]{2,1,0:T(8,128)(2,1)S(1)} %ahead_far_0.1.refs_2_.refs_0_), channel_id=1, source_target_pairs={{0,2},{1,3},{2,0},{3,1},{4,6},{5,7},{6,4},{7,5},{8,10},{9,11},{10,... | collective-permute-start | bytes 1179656 | tf_op jit(solution)/shard_map/ppermute | solution.py:240
  42.3 17.7 %collective-permute-start.11 = (bf16[1,192,512]{2,1,0:T(8,128)(2,1)S(1)}, bf16[1,192,512]{2,1,0:T(8,128)(2,1)S(1)}, u32[]{:S(2)}, u32[]{:S(2)}) collective-permute-start(bf16[1,192,512]{2,1,0:T(8,128)(2,1)S(1)} %grad_middle_0.1.refs_4_), channel_id=1, source_target_pairs={{0,0},{1,1},{2,4},{3,5},{4,2},{5,3},{6,6},{7,7},{8,8},{9,9},{10,12... | collective-permute-start | bytes 589832 | tf_op jit(solution)/shard_map/ppermute | solution.py:240
  50.6 17.5 %collective-permute-start.8 = (bf16[2,192,512]{2,1,0:T(8,128)(2,1)S(1)}, bf16[2,192,512]{2,1,0:T(8,128)(2,1)S(1)}, u32[]{:S(2)}, u32[]{:S(2)}) collective-permute-start(bf16[2,192,512]{2,1,0:T(8,128)(2,1)S(1)} %behind_outer_1.1.refs_1_), channel_id=1, source_target_pairs={{0,2},{1,3},{2,0},{3,1},{4,6},{5,7},{6,4},{7,5},{8,10},{9,11},{10,... | collective-permute-start | bytes 1179656 | tf_op jit(solution)/shard_map/ppermute | solution.py:240
  52.0 16.9 %collective-permute-start.7 = (bf16[192,896]{1,0:T(8,128)(2,1)S(1)}, bf16[192,896]{1,0:T(8,128)(2,1)S(1)}, u32[]{:S(2)}, u32[]{:S(2)}) collective-permute-start(bf16[192,896]{1,0:T(8,128)(2,1)S(1)} %ahead_rows_1.1.refs_4_.refs_1_), channel_id=1, source_target_pairs={{0,1},{1,0},{2,3},{3,2},{4,5},{5,4},{6,7},{7,6},{8,9},{9,8},{10,11... | collective-permute-start | bytes 1032200 | tf_op jit(solution)/shard_map/ppermute | solution.py:249
  56.8 16.5 %collective-permute-start.12 = (bf16[2,192,512]{2,1,0:T(8,128)(2,1)S(1)}, bf16[2,192,512]{2,1,0:T(8,128)(2,1)S(1)}, u32[]{:S(2)}, u32[]{:S(2)}) collective-permute-start(bf16[2,192,512]{2,1,0:T(8,128)(2,1)S(1)} %ahead_middle_0.1.refs_4_), channel_id=1, source_target_pairs={{0,0},{1,1},{2,4},{3,5},{4,2},{5,3},{6,6},{7,7},{8,8},{9,9},{10,12... | collective-permute-start | bytes 1179656 | tf_op jit(solution)/shard_map/ppermute | solution.py:240
  60.8 14.6 %collective-permute-start.14 = (bf16[1,192,512]{2,1,0:T(8,128)(2,1)S(1)}, bf16[1,192,512]{2,1,0:T(8,128)(2,1)S(1)}, u32[]{:S(2)}, u32[]{:S(2)}) collective-permute-start(bf16[1,192,512]{2,1,0:T(8,128)(2,1)S(1)} %grad_outer_1.1.refs_4_), channel_id=1, source_target_pairs={{0,2},{1,3},{2,0},{3,1},{4,6},{5,7},{6,4},{7,5},{8,10},{9,11},{10,... | collective-permute-start | bytes 589832 | tf_op jit(solution)/shard_map/ppermute | solution.py:240
  73.9 12.8 %collective-permute-start.13 = (bf16[2,192,512]{2,1,0:T(8,128)(2,1)S(1)}, bf16[2,192,512]{2,1,0:T(8,128)(2,1)S(1)}, u32[]{:S(2)}, u32[]{:S(2)}) collective-permute-start(bf16[2,192,512]{2,1,0:T(8,128)(2,1)S(1)} %ahead_outer_1.1.refs_2_), channel_id=1, source_target_pairs={{0,2},{1,3},{2,0},{3,1},{4,6},{5,7},{6,4},{7,5},{8,10},{9,11},{10,... | collective-permute-start | bytes 1179656 | tf_op jit(solution)/shard_map/ppermute | solution.py:240
  75.5 12.2 %collective-permute-start.17 = (bf16[1,192,512]{2,1,0:T(8,128)(2,1)S(1)}, bf16[1,192,512]{2,1,0:T(8,128)(2,1)S(1)}, u32[]{:S(2)}, u32[]{:S(2)}) collective-permute-start(bf16[1,192,512]{2,1,0:T(8,128)(2,1)S(1)} %grad_middle_1.1.refs_5_), channel_id=1, source_target_pairs={{0,0},{1,1},{2,4},{3,5},{4,2},{5,3},{6,6},{7,7},{8,8},{9,9},{10,12... | collective-permute-start | bytes 589832 | tf_op jit(solution)/shard_map/ppermute | solution.py:240
  79.6 16.8 %collective-permute-start.19 = (bf16[2,192,512]{2,1,0:T(8,128)(2,1)S(1)}, bf16[2,192,512]{2,1,0:T(8,128)(2,1)S(1)}, u32[]{:S(2)}, u32[]{:S(2)}) collective-permute-start(bf16[2,192,512]{2,1,0:T(8,128)(2,1)S(1)} %behind_outer_2.1.refs_4_), channel_id=1, source_target_pairs={{0,2},{1,3},{2,0},{3,1},{4,6},{5,7},{6,4},{7,5},{8,10},{9,11},{10,... | collective-permute-start | bytes 1179656 | tf_op jit(solution)/shard_map/ppermute | solution.py:240
  89.8 16.0 %collective-permute-start.18 = (bf16[2,192,512]{2,1,0:T(8,128)(2,1)S(1)}, bf16[2,192,512]{2,1,0:T(8,128)(2,1)S(1)}, u32[]{:S(2)}, u32[]{:S(2)}) collective-permute-start(bf16[2,192,512]{2,1,0:T(8,128)(2,1)S(1)} %ahead_outer_2.1.refs_5_), channel_id=1, source_target_pairs={{0,2},{1,3},{2,0},{3,1},{4,6},{5,7},{6,4},{7,5},{8,10},{9,11},{10,... | collective-permute-start | bytes 1179656 | tf_op jit(solution)/shard_map/ppermute | solution.py:240
  98.0 17.1 %collective-permute-start.24 = (bf16[2,192,512]{2,1,0:T(8,128)(2,1)S(1)}, bf16[2,192,512]{2,1,0:T(8,128)(2,1)S(1)}, u32[]{:S(2)}, u32[]{:S(2)}) collective-permute-start(bf16[2,192,512]{2,1,0:T(8,128)(2,1)S(1)} %behind_back_1.1.refs_1_), channel_id=1, source_target_pairs={{0,2},{1,3},{2,0},{3,1},{4,6},{5,7},{6,4},{7,5},{8,10},{9,11},{10,... | collective-permute-start | bytes 1179656 | tf_op jit(solution)/shard_map/ppermute | solution.py:240
  107.2 27.4 %collective-permute-start.23 = (bf16[1,192,512]{2,1,0:T(8,128)(2,1)S(1)}, bf16[1,192,512]{2,1,0:T(8,128)(2,1)S(1)}, u32[]{:S(2)}, u32[]{:S(2)}) collective-permute-start(bf16[1,192,512]{2,1,0:T(8,128)(2,1)S(1)} %ahead_back_1.1.refs_1_), channel_id=1, source_target_pairs={{0,2},{1,3},{2,0},{3,1},{4,6},{5,7},{6,4},{7,5},{8,10},{9,11},{10,... | collective-permute-start | bytes 589832 | tf_op jit(solution)/shard_map/ppermute | solution.py:240
  115.2 27.0 %collective-permute-start.26 = (bf16[2,192,512]{2,1,0:T(8,128)(2,1)S(1)}, bf16[2,192,512]{2,1,0:T(8,128)(2,1)S(1)}, u32[]{:S(2)}, u32[]{:S(2)}) collective-permute-start(bf16[2,192,512]{2,1,0:T(8,128)(2,1)S(1)} %behind_first_1.1.refs_6_.refs_2_), channel_id=1, source_target_pairs={{0,0},{1,1},{2,4},{3,5},{4,2},{5,3},{6,6},{7,7},{8,8},{9,9},{10,12... | collective-permute-start | bytes 1179656 | tf_op jit(solution)/shard_map/ppermute | solution.py:240
  119.1 21.5 %collective-permute-start.33 = (bf16[192,896]{1,0:T(8,128)(2,1)S(1)}, bf16[192,896]{1,0:T(8,128)(2,1)S(1)}, u32[]{:S(2)}, u32[]{:S(2)}) collective-permute-start(bf16[192,896]{1,0:T(8,128)(2,1)S(1)} %get-tuple-element.10.refs_1_), channel_id=1, source_target_pairs={{8,1},{9,0},{10,3},{11,2},{12,5},{13,4},{14,7},{15,6},{16,9},{17,8... | collective-permute-start | bytes 1032200 | tf_op jit(solution)/shard_map/ppermute | solution.py:258
  142.2 12.2 %collective-permute-start.30 = (bf16[2,192,512]{2,1,0:T(8,128)(2,1)S(1)}, bf16[2,192,512]{2,1,0:T(8,128)(2,1)S(1)}, u32[]{:S(2)}, u32[]{:S(2)}) collective-permute-start(bf16[2,192,512]{2,1,0:T(8,128)(2,1)S(1)} %behind_back_2.1.refs_1_), channel_id=1, source_target_pairs={{0,2},{1,3},{2,0},{3,1},{4,6},{5,7},{6,4},{7,5},{8,10},{9,11},{10,... | collective-permute-start | bytes 1179656 | tf_op jit(solution)/shard_map/ppermute | solution.py:240
  145.4 18.5 %collective-permute-start.29 = (bf16[1,192,512]{2,1,0:T(8,128)(2,1)S(1)}, bf16[1,192,512]{2,1,0:T(8,128)(2,1)S(1)}, u32[]{:S(2)}, u32[]{:S(2)}) collective-permute-start(bf16[1,192,512]{2,1,0:T(8,128)(2,1)S(1)} %ahead_back_2.1.refs_7_), channel_id=1, source_target_pairs={{0,2},{1,3},{2,0},{3,1},{4,6},{5,7},{6,4},{7,5},{8,10},{9,11},{10,... | collective-permute-start | bytes 589832 | tf_op jit(solution)/shard_map/ppermute | solution.py:240
  147.6 16.2 %collective-permute-start.27 = (bf16[192,896]{1,0:T(8,128)(2,1)S(1)}, bf16[192,896]{1,0:T(8,128)(2,1)S(1)}, u32[]{:S(2)}, u32[]{:S(2)}) collective-permute-start(bf16[192,896]{1,0:T(8,128)(2,1)S(1)} %get-tuple-element.11.refs_6_), channel_id=1, source_target_pairs={{0,9},{1,8},{2,11},{3,10},{4,13},{5,12},{6,15},{7,14},{8,17},{9,16... | collective-permute-start | bytes 1032200 | tf_op jit(solution)/shard_map/ppermute | solution.py:258
  157.9 14.2 %collective-permute-start.35 = (bf16[192,896]{1,0:T(8,128)(2,1)S(1)}, bf16[192,896]{1,0:T(8,128)(2,1)S(1)}, u32[]{:S(2)}, u32[]{:S(2)}) collective-permute-start(bf16[192,896]{1,0:T(8,128)(2,1)S(1)} %get-tuple-element.13.refs_7_), channel_id=1, source_target_pairs={{8,1},{9,0},{10,3},{11,2},{12,5},{13,4},{14,7},{15,6},{16,9},{17,8... | collective-permute-start | bytes 1032200 | tf_op jit(solution)/shard_map/ppermute | solution.py:258
  (26 other events, 148.0 us)

commit v8 on v7

--- a/solution.py
+++ b/solution.py
@@ -55,42 +55,21 @@
     out[...] = rows[...]
 
 
-def touch_kernel(out):
-    out[...] = jnp.zeros_like(out)
-
-
 def cut_first_kernel(value, out):
     out[...] = value[: out.shape[0]]
 
 
-def first_kernel(width, far, where, own, partner, weights, out, joined, tiles, sems):
-    parts, slots, half = out.shape
-    tile = tiles.shape[1]
-    steps = half // tile
-    side = 1 - where[0] if far else where[0]
-    copies = []
-    for k in range(parts):
-        for j in range(steps):
-            at = pl.multiple_of((side * steps + j) * tile, tile)
-            copy = pltpu.make_async_copy(
-                weights.at[k, pl.ds(at, tile)], tiles.at[k * steps + j], sems.at[k * steps + j]
-            )
-            copy.start()
-            copies.append(copy)
-    at = pl.multiple_of(where[1] * width, 128)
-    other = pl.multiple_of((1 - where[1]) * width, 128)
-    joined[:slots, pl.ds(at, width)] = own[...]
-    joined[:slots, pl.ds(other, width)] = partner[...]
-    for k in range(parts):
-        for j in range(steps):
-            copies[k * steps + j].wait()
-            product = lax.dot_general(
-                tiles[k * steps + j],
-                joined[...],
-                (((1,), (1,)), ((), ())),
-                preferred_element_type=F32,
-            )
-            out[k, :, j * tile : (j + 1) * tile] = product.T[:slots].astype(BF16)
+def first_kernel(width, where, own, partner, tile, out, joined):
+    @pl.when((pl.program_id(0) == 0) & (pl.program_id(1) == 0))
+    def _():
+        at = pl.multiple_of(where[1] * width, 128)
+        other = pl.multiple_of((1 - where[1]) * width, 128)
+        joined[:, pl.ds(at, width)] = own[...]
+        joined[:, pl.ds(other, width)] = partner[...]
+
+    out[0] = lax.dot_general(
+        joined[...], tile[0], (((1,), (1,)), ((), ())), preferred_element_type=F32
+    ).astype(BF16)
 
 
 def first_product(name, where, far, rows, weights, after):
@@ -99,19 +78,21 @@
     half = units // 2
     tile = min(256, half)
     steps = half // tile
+
+    def tile_at(k, j, w):
+        return (k, ((1 - w[0]) if far else w[0]) * steps + j, 0)
+
     return call(
-        functools.partial(first_kernel, width, far),
+        functools.partial(first_kernel, width),
         FIRST * parts,
         (*rows, weights),
         after,
         jax.ShapeDtypeStruct((parts, slots, half), BF16),
         scalars=(where,),
-        in_specs=[*[whole(r) for r in rows], pl.BlockSpec(memory_space=pltpu.HBM)],
-        scratch=[
-            pltpu.VMEM((-(-slots // 128) * 128, features), BF16),
-            pltpu.VMEM((parts * steps, tile, features), BF16),
-            pltpu.SemaphoreType.DMA((parts * steps,)),
-        ],
+        grid=(parts, steps),
+        in_specs=[*[whole(r) for r in rows], pl.BlockSpec((1, tile, features), tile_at)],
+        out_specs=pl.BlockSpec((1, slots, tile), lambda k, j, w: (k, 0, j)),
+        scratch=[pltpu.VMEM((slots, features), BF16)],
         name=name,
     )
 
@@ -156,6 +137,16 @@
     sig = jax.nn.sigmoid(gate)
     out[0] = (expanded * up * sig * (1.0 + gate * (1.0 - sig))).astype(BF16)
     out[1] = (expanded * gate * sig).astype(BF16)
+
+
+def shares_kernel(one, two, out):
+    out[...] = (one[...].astype(F32) + two[...].astype(F32)).astype(BF16)
+
+
+def result_kernel(first, one, two, out):
+    size = first.shape[0]
+    out[:size] = first[...]
+    out[size:] = (one[...].astype(F32) + two[...].astype(F32)).astype(BF16)
 
 
 def second_kernel(scaled, where, act, one, two, three, *refs):
@@ -382,19 +373,18 @@
         by = 1 if forward else -1
         sent[forward, c] = to_section(give, by, 1), to_section(keep, by, 0)
 
-    def result(forward):
-        sums = [
-            (a.astype(F32) + b.astype(F32)).astype(BF16)
-            for a, b in (sent[forward, c] for c in range(PIECES))
-        ]
-        return jnp.concatenate(sums)[None]
+    def shares(chain):
+        pieces = sent[chain is ahead, 0]
+        shape = pieces[0].shape
+        sent[chain is ahead, 0] = kernel_call(f"{chain.name}_shares", shares_kernel, SMALL, pieces, shape)
+
+    def result(chain):
+        operands = (sent[chain is ahead, 0], *sent[chain is ahead, 1])
+        shape = (height, operands[0].shape[1])
+        return kernel_call(f"{chain.name}_result", result_kernel, SMALL, operands, shape)[None]
 
     for chain in (behind, grad, ahead):
         chain.fetch(0)
-    touched = call(
-        touch_kernel, ROWS, (), [*recent, gates, downs], jax.ShapeDtypeStruct((8, 128), F32), name="touch"
-    )
-    recent[:] = [touched]
     behind.product(0, True)
     behind.outer_sum(0)
     behind.fetch(1)
@@ -438,10 +428,14 @@
     ahead.middle_pass(1)
     behind.outer_pass(2)
     ahead.outer_pass(2)
+    shares(behind)
     finish(ahead, 0)
     finish(behind, 1)
     finish(ahead, 1)
-    return result(True), result(False)
+    shares(ahead)
+    behind_sent = result(behind)
+    ahead_sent = result(ahead)
+    return ahead_sent, behind_sent
 
 
 def body(ahead_rows, behind_rows, behind_grad, route_scores, route_counts, gate_up, down_proj):

time: 180 us -> 169 us (0.939)
  Pallas kernels: 64.5 us -> 47.9 us
  starting transfers between devices: 89.2 us -> 101 us
  waiting for transfers between devices: 13.8 us -> 11.2 us
  other arithmetic: 2.29 us -> 0.15 us
  local copies, waits for them, and re-layouts: 7.89 us -> 5.87 us
    pallas_call x46 -> x49, Pallas kernels: 64.5 us -> 47.9 us  [call(): pl.pallas_call(run, compiler_params=pltpu.CompilerParams(vmem_limit_bytes...]
    ppermute x23, starting transfers between devices: 48 us -> 57.8 us  [between(): return lax.ppermute(value, 'expert', pairs)]
    ppermute x8, waiting for transfers between devices: 11.7 us -> 4.9 us  [to_section(): return lax.ppermute(value, ('section', 'expert'), pairs)]
    ppermute x6, waiting for transfers between devices: 1.83 us -> 4.95 us  [swapped(): return lax.ppermute(value, 'expert', [(i, i ^ 1) for i in range(devices)])]
    ppermute x8, starting transfers between devices: 34.1 us -> 36.5 us  [to_section(): return lax.ppermute(value, ('section', 'expert'), pairs)]
    unnamed x26 -> x22, local copies, waits for them, and re-layouts: 7.33 us -> 5.31 us
    broadcast_in_dim x2 -> x0, other arithmetic: 1.81 us -> none  [result(): return jnp.concatenate(sums)[None]]
  transfers between devices with their start and end apart: 37 -> 37, of which waited for: 6 -> 5; matrix products, arithmetic and copies ran while one was open for 1% -> 0% of each run, Pallas kernels for 36% -> 28%
where the time goes in v8:
time: 169 us; the launch traced here: 168 us
  starting transfers between devices  101 us (60%)
  Pallas kernels  47.9 us (28%)
  waiting for transfers between devices  11.2 us (7%)
  local copies, waits for them, and re-layouts  5.87 us (3%)
    ppermute x23, starting transfers between devices, between(): return lax.ppermute(value, 'expert', pairs)  57.8 us
    pallas_call x49, Pallas kernels, call(): pl.pallas_call(run, compiler_params=pltpu.CompilerParams(vmem_limit_bytes...  47.9 us
    ppermute x8, starting transfers between devices, to_section(): return lax.ppermute(value, ('section', 'expert'), pairs)  36.5 us
    ppermute x6, starting transfers between devices, swapped(): return lax.ppermute(value, 'expert', [(i, i ^ 1) for i in range(devices)])  7.08 us
    unnamed x22, local copies, waits for them, and re-layouts  5.31 us
    ppermute x6, waiting for transfers between devices, swapped(): return lax.ppermute(value, 'expert', [(i, i ^ 1) for i in range(devices)])  4.95 us
    ppermute x8, waiting for transfers between devices, to_section(): return lax.ppermute(value, ('section', 'expert'), pairs)  4.9 us
  transfers between devices with their start and end apart: 37, of which 5 were waited for; matrix products, arithmetic and copies ran while one was open for 0% of the time, Pallas kernels for 28%

profile of v8, /device:TPU:1, one launch (start us, length us, event | category | flops | bytes accessed | tf_op | source)
XLA Modules:
  0.0 167.8 jit_solution(17946457137319302579)
XLA Ops:
  6.9 4.9 %collective-permute-done.1.refs_2_ = bf16[192,896]{1,0:T(8,128)(2,1)} collective-permute-done((bf16[192,896]{1,0:T(8,128)(2,1)S(1)}, bf16[192,896]{1,0:T(8,128)(2,1)}, u32[]{:S(2)}, u32[]{:S(2)}) %collective-permute-start.1) | collective-permute-done | bytes 344096 | tf_op jit(solution)/shard_map/ppermute | solution.py:240
  11.8 3.1 %copy-done = bf16[1,1,2,1024,1792]{4,3,2,1,0:T(8,128)(2,1)S(1)} copy-done((bf16[1,1,2,1024,1792]{4,3,2,1,0:T(8,128)(2,1)S(1)}, bf16[1,1,2,1024,1792]{4,3,2,1,0:T(8,128)(2,1)}, u32[]{:S(2)}) %copy-start) | copy-done | bytes 7340056
  14.9 3.9 %behind_far_0.1.refs_1_.refs_0_ = bf16[2,192,512]{2,1,0:T(8,128)(2,1)S(1)} custom-call(s32[3]{0:T(128)S(1)} %pad_add_fusion.refs_0_, bf16[192,896]{1,0:T(8,128)(2,1)S(1)} %behind_rows_0.1.refs_1_, bf16[192,896]{1,0:T(8,128)(2,1)} %collective-permute-done.1.refs_2_, bf16[2,1024,1792]{2,1,0:T(8,128)(2,1)S(1)} %bitcast.21, ...), custom_call_target="tpu_custom_call" | custom-call | flops 10400000000 | bytes 1024 | tf_op jit(solution)/shard_map/behind_far_0/pallas_call | solution.py:38
  23.7 3.6 %behind_near_0.1.refs_2_.refs_0_ = bf16[2,192,512]{2,1,0:T(8,128)(2,1)S(1)} custom-call(s32[3]{0:T(128)S(1)} %pad_add_fusion.refs_0_, bf16[192,896]{1,0:T(8,128)(2,1)S(1)} %behind_rows_0.1.refs_1_, bf16[192,896]{1,0:T(8,128)(2,1)} %collective-permute-done.1.refs_2_, bf16[2,1024,1792]{2,1,0:T(8,128)(2,1)S(1)} %bitcast.24, ...), custom_call_target="tpu_custom_call" | custom-call | flops 10400000000 | bytes 1024 | tf_op jit(solution)/shard_map/behind_near_0/pallas_call | solution.py:38
  29.4 2.6 %ahead_far_0.1.refs_2_.refs_0_ = bf16[2,192,512]{2,1,0:T(8,128)(2,1)S(1)} custom-call(s32[3]{0:T(128)S(1)} %pad_add_fusion.refs_0_, bf16[192,896]{1,0:T(8,128)(2,1)S(1)} %ahead_rows_0.1.refs_4_.refs_1_, bf16[192,896]{1,0:T(8,128)(2,1)S(1)} %collective-permute-done.refs_2_, bf16[2,1024,1792]{2,1,0:T(8,128)(2,1)S(1)} %bitcast.25, ...), custom_call_target="tpu_custom_call" | custom-call | flops 10400000000 | bytes 1024 | tf_op jit(solution)/shard_map/ahead_far_0/pallas_call | solution.py:38
  32.0 3.9 %collective-permute-start.10 = (bf16[2,192,512]{2,1,0:T(8,128)(2,1)S(1)}, bf16[2,192,512]{2,1,0:T(8,128)(2,1)S(1)}, u32[]{:S(2)}, u32[]{:S(2)}) collective-permute-start(bf16[2,192,512]{2,1,0:T(8,128)(2,1)S(1)} %ahead_far_0.1.refs_2_.refs_0_), channel_id=1, source_target_pairs={{0,2},{1,3},{2,0},{3,1},{4,6},{5,7},{6,4},{7,5},{8,10},{9,11},{10,... | collective-permute-start | bytes 1179656 | tf_op jit(solution)/shard_map/ppermute | solution.py:231
  38.3 2.6 %behind_far_1.1.refs_1_.refs_4_.refs_0_ = bf16[2,192,512]{2,1,0:T(8,128)(2,1)S(1)} custom-call(s32[3]{0:T(128)S(1)} %pad_add_fusion.refs_0_, bf16[192,896]{1,0:T(8,128)(2,1)S(1)} %behind_rows_1.1.refs_4_.refs_1_, bf16[192,896]{1,0:T(8,128)(2,1)S(1)} %collective-permute-done.2.refs_2_, bf16[2,1024,1792]{2,1,0:T(8,128)(2,1)S(1)} %bitcast.26, ...), custom_call_target="tpu_custom_call" | custom-call | flops 10400000000 | bytes 1024 | tf_op jit(solution)/shard_map/behind_far_1/pallas_call | solution.py:38
  48.8 2.9 %collective-permute-start.14 = (bf16[1,192,512]{2,1,0:T(8,128)(2,1)S(1)}, bf16[1,192,512]{2,1,0:T(8,128)(2,1)S(1)}, u32[]{:S(2)}, u32[]{:S(2)}) collective-permute-start(bf16[1,192,512]{2,1,0:T(8,128)(2,1)S(1)} %grad_outer_1.1.refs_4_), channel_id=1, source_target_pairs={{0,2},{1,3},{2,0},{3,1},{4,6},{5,7},{6,4},{7,5},{8,10},{9,11},{10,... | collective-permute-start | bytes 589832 | tf_op jit(solution)/shard_map/ppermute | solution.py:231
  51.6 2.6 %behind_near_1.1.refs_2_.refs_0_ = bf16[2,192,512]{2,1,0:T(8,128)(2,1)S(1)} custom-call(s32[3]{0:T(128)S(1)} %pad_add_fusion.refs_0_, bf16[192,896]{1,0:T(8,128)(2,1)S(1)} %behind_rows_1.1.refs_4_.refs_1_, bf16[192,896]{1,0:T(8,128)(2,1)S(1)} %collective-permute-done.2.refs_2_, bf16[2,1024,1792]{2,1,0:T(8,128)(2,1)S(1)} %bitcast.28, ...), custom_call_target="tpu_custom_call" | custom-call | flops 10400000000 | bytes 1024 | tf_op jit(solution)/shard_map/behind_near_1/pallas_call | solution.py:38
  55.1 2.6 %ahead_far_1.1.refs_1_.refs_4_.refs_0_ = bf16[2,192,512]{2,1,0:T(8,128)(2,1)S(1)} custom-call(s32[3]{0:T(128)S(1)} %pad_add_fusion.refs_0_, bf16[192,896]{1,0:T(8,128)(2,1)S(1)} %ahead_rows_1.1.refs_4_.refs_1_, bf16[192,896]{1,0:T(8,128)(2,1)S(1)} %collective-permute-done.7.refs_2_, bf16[2,1024,1792]{2,1,0:T(8,128)(2,1)S(1)} %bitcast.29, ...), custom_call_target="tpu_custom_call" | custom-call | flops 10400000000 | bytes 1024 | tf_op jit(solution)/shard_map/ahead_far_1/pallas_call | solution.py:38
  63.0 4.2 %collective-permute-start.19 = (bf16[2,192,512]{2,1,0:T(8,128)(2,1)S(1)}, bf16[2,192,512]{2,1,0:T(8,128)(2,1)S(1)}, u32[]{:S(2)}, u32[]{:S(2)}) collective-permute-start(bf16[2,192,512]{2,1,0:T(8,128)(2,1)S(1)} %behind_outer_2.1.refs_4_), channel_id=1, source_target_pairs={{0,2},{1,3},{2,0},{3,1},{4,6},{5,7},{6,4},{7,5},{8,10},{9,11},{10,... | collective-permute-start | bytes 1179656 | tf_op jit(solution)/shard_map/ppermute | solution.py:231
  67.2 2.6 %ahead_near_1.1.refs_2_.refs_0_ = bf16[2,192,512]{2,1,0:T(8,128)(2,1)S(1)} custom-call(s32[3]{0:T(128)S(1)} %pad_add_fusion.refs_0_, bf16[192,896]{1,0:T(8,128)(2,1)S(1)} %ahead_rows_1.1.refs_4_.refs_1_, bf16[192,896]{1,0:T(8,128)(2,1)S(1)} %collective-permute-done.7.refs_2_, bf16[2,1024,1792]{2,1,0:T(8,128)(2,1)S(1)} %bitcast.30, ...), custom_call_target="tpu_custom_call" | custom-call | flops 10400000000 | bytes 1024 | tf_op jit(solution)/shard_map/ahead_near_1/pallas_call | solution.py:38
  73.7 5.9 %collective-permute-start.18 = (bf16[2,192,512]{2,1,0:T(8,128)(2,1)S(1)}, bf16[2,192,512]{2,1,0:T(8,128)(2,1)S(1)}, u32[]{:S(2)}, u32[]{:S(2)}) collective-permute-start(bf16[2,192,512]{2,1,0:T(8,128)(2,1)S(1)} %ahead_outer_2.1.refs_5_), channel_id=1, source_target_pairs={{0,2},{1,3},{2,0},{3,1},{4,6},{5,7},{6,4},{7,5},{8,10},{9,11},{10,... | collective-permute-start | bytes 1179656 | tf_op jit(solution)/shard_map/ppermute | solution.py:231
  82.0 11.2 %collective-permute-start.24 = (bf16[2,192,512]{2,1,0:T(8,128)(2,1)S(1)}, bf16[2,192,512]{2,1,0:T(8,128)(2,1)S(1)}, u32[]{:S(2)}, u32[]{:S(2)}) collective-permute-start(bf16[2,192,512]{2,1,0:T(8,128)(2,1)S(1)} %behind_back_1.1.refs_1_), channel_id=1, source_target_pairs={{0,2},{1,3},{2,0},{3,1},{4,6},{5,7},{6,4},{7,5},{8,10},{9,11},{10,... | collective-permute-start | bytes 1179656 | tf_op jit(solution)/shard_map/ppermute | solution.py:231
  94.7 7.2 %collective-permute-start.23 = (bf16[1,192,512]{2,1,0:T(8,128)(2,1)S(1)}, bf16[1,192,512]{2,1,0:T(8,128)(2,1)S(1)}, u32[]{:S(2)}, u32[]{:S(2)}) collective-permute-start(bf16[1,192,512]{2,1,0:T(8,128)(2,1)S(1)} %ahead_back_1.1.refs_1_), channel_id=1, source_target_pairs={{0,2},{1,3},{2,0},{3,1},{4,6},{5,7},{6,4},{7,5},{8,10},{9,11},{10,... | collective-permute-start | bytes 589832 | tf_op jit(solution)/shard_map/ppermute | solution.py:231
  103.1 3.2 %behind_out_0.1 = (bf16[192,896]{1,0:T(8,128)(2,1)S(1)}, bf16[192,896]{1,0:T(8,128)(2,1)S(1)}) custom-call(s32[3]{0:T(128)S(1)} %pad_add_fusion.refs_0_, bf16[2,192,512]{2,1,0:T(8,128)(2,1)S(1)} %behind_act_0.1.refs_4_.refs_1_, bf16[2,192,512]{2,1,0:T(8,128)(2,1)S(1)} %collective-permute-done.19.refs_1_.refs_2_, ...), custom_call_target="tpu_custom_call" | custom-call | flops 20000000000 | bytes 1024 | tf_op jit(solution)/shard_map/behind_out_0/pallas_call | solution.py:38
  106.3 16.2 %collective-permute-start.25 = (bf16[192,896]{1,0:T(8,128)(2,1)S(1)}, bf16[192,896]{1,0:T(8,128)(2,1)S(1)}, u32[]{:S(2)}, u32[]{:S(2)}) collective-permute-start(bf16[192,896]{1,0:T(8,128)(2,1)S(1)} %get-tuple-element.10.refs_1_), channel_id=1, source_target_pairs={{8,1},{9,0},{10,3},{11,2},{12,5},{13,4},{14,7},{15,6},{16,9},{17,8... | collective-permute-start | bytes 1032200 | tf_op jit(solution)/shard_map/ppermute | solution.py:249
  125.4 4.0 %collective-permute-start.32 = (bf16[2,192,512]{2,1,0:T(8,128)(2,1)S(1)}, bf16[2,192,512]{2,1,0:T(8,128)(2,1)S(1)}, u32[]{:S(2)}, u32[]{:S(2)}) collective-permute-start(bf16[2,192,512]{2,1,0:T(8,128)(2,1)S(1)} %behind_back_2.1.refs_1_), channel_id=1, source_target_pairs={{0,2},{1,3},{2,0},{3,1},{4,6},{5,7},{6,4},{7,5},{8,10},{9,11},{10,... | collective-permute-start | bytes 1179656 | tf_op jit(solution)/shard_map/ppermute | solution.py:231
  129.4 4.4 %collective-permute-start.31 = (bf16[1,192,512]{2,1,0:T(8,128)(2,1)S(1)}, bf16[1,192,512]{2,1,0:T(8,128)(2,1)S(1)}, u32[]{:S(2)}, u32[]{:S(2)}) collective-permute-start(bf16[1,192,512]{2,1,0:T(8,128)(2,1)S(1)} %ahead_back_2.1.refs_2_), channel_id=1, source_target_pairs={{0,2},{1,3},{2,0},{3,1},{4,6},{5,7},{6,4},{7,5},{8,10},{9,11},{10,... | collective-permute-start | bytes 589832 | tf_op jit(solution)/shard_map/ppermute | solution.py:231
  136.1 5.4 %collective-permute-start.29 = (bf16[192,896]{1,0:T(8,128)(2,1)S(1)}, bf16[192,896]{1,0:T(8,128)(2,1)S(1)}, u32[]{:S(2)}, u32[]{:S(2)}) collective-permute-start(bf16[192,896]{1,0:T(8,128)(2,1)S(1)} %get-tuple-element.12.refs_6_), channel_id=1, source_target_pairs={{0,9},{1,8},{2,11},{3,10},{4,13},{5,12},{6,15},{7,14},{8,17},{9,16... | collective-permute-start | bytes 1032200 | tf_op jit(solution)/shard_map/ppermute | solution.py:249
  143.4 3.2 %behind_out_1.1 = (bf16[192,896]{1,0:T(8,128)(2,1)S(1)}, bf16[192,896]{1,0:T(8,128)(2,1)S(1)}) custom-call(s32[3]{0:T(128)S(1)} %pad_add_fusion.refs_0_, bf16[2,192,512]{2,1,0:T(8,128)(2,1)S(1)} %behind_act_1.1.refs_1_.refs_3_, bf16[2,192,512]{2,1,0:T(8,128)(2,1)S(1)} %behind_first_1.1.refs_6_.refs_2_, ...), custom_call_target="tpu_custom_call" | custom-call | flops 20000000000 | bytes 1024 | tf_op jit(solution)/shard_map/behind_out_1/pallas_call | solution.py:38
  146.7 3.0 %collective-permute-start.35 = (bf16[192,896]{1,0:T(8,128)(2,1)S(1)}, bf16[192,896]{1,0:T(8,128)(2,1)S(1)}, u32[]{:S(2)}, u32[]{:S(2)}) collective-permute-start(bf16[192,896]{1,0:T(8,128)(2,1)S(1)} %get-tuple-element.14.refs_7_), channel_id=1, source_target_pairs={{8,1},{9,0},{10,3},{11,2},{12,5},{13,4},{14,7},{15,6},{16,9},{17,8... | collective-permute-start | bytes 1032200 | tf_op jit(solution)/shard_map/ppermute | solution.py:249
  153.8 4.1 %collective-permute-start.33 = (bf16[192,896]{1,0:T(8,128)(2,1)S(1)}, bf16[192,896]{1,0:T(8,128)(2,1)S(1)}, u32[]{:S(2)}, u32[]{:S(2)}) collective-permute-start(bf16[192,896]{1,0:T(8,128)(2,1)S(1)} %get-tuple-element.15.refs_2_), channel_id=1, source_target_pairs={{0,9},{1,8},{2,11},{3,10},{4,13},{5,12},{6,15},{7,14},{8,17},{9,16... | collective-permute-start | bytes 1032200 | tf_op jit(solution)/shard_map/ppermute | solution.py:249
  162.4 3.3 %collective-permute-done.34.refs_2_ = bf16[192,896]{1,0:T(8,128)(2,1)S(1)} collective-permute-done((bf16[192,896]{1,0:T(8,128)(2,1)S(1)}, bf16[192,896]{1,0:T(8,128)(2,1)S(1)}, u32[]{:S(2)}, u32[]{:S(2)}) %collective-permute-start.34) | collective-permute-done | bytes 344096 | tf_op jit(solution)/shard_map/ppermute | solution.py:249
  (129 shorter events, 55.7 us)
Async XLA Ops:
  3.9 17.4 %collective-permute-start.3 = (bf16[192,896]{1,0:T(8,128)(2,1)S(1)}, bf16[192,896]{1,0:T(8,128)(2,1)S(1)}, u32[]{:S(2)}, u32[]{:S(2)}) collective-permute-start(bf16[192,896]{1,0:T(8,128)(2,1)S(1)} %grad_rows_0.1.refs_1_), channel_id=1, source_target_pairs={{0,1},{1,0},{2,3},{3,2},{4,5},{5,4},{6,7},{7,6},{8,9},{9,8},{10,11... | collective-permute-start | bytes 1032200 | tf_op jit(solution)/shard_map/ppermute | solution.py:240
  5.0 24.4 %collective-permute-start = (bf16[192,896]{1,0:T(8,128)(2,1)S(1)}, bf16[192,896]{1,0:T(8,128)(2,1)S(1)}, u32[]{:S(2)}, u32[]{:S(2)}) collective-permute-start(bf16[192,896]{1,0:T(8,128)(2,1)S(1)} %ahead_rows_0.1.refs_4_.refs_1_), channel_id=1, source_target_pairs={{0,1},{1,0},{2,3},{3,2},{4,5},{5,4},{6,7},{7,6},{8,9},{9,8},{10,11... | collective-permute-start | bytes 1032200 | tf_op jit(solution)/shard_map/ppermute | solution.py:240
  20.1 18.2 %collective-permute-start.2 = (bf16[192,896]{1,0:T(8,128)(2,1)S(1)}, bf16[192,896]{1,0:T(8,128)(2,1)S(1)}, u32[]{:S(2)}, u32[]{:S(2)}) collective-permute-start(bf16[192,896]{1,0:T(8,128)(2,1)S(1)} %behind_rows_1.1.refs_4_.refs_1_), channel_id=1, source_target_pairs={{0,1},{1,0},{2,3},{3,2},{4,5},{5,4},{6,7},{7,6},{8,9},{9,8},{10,11... | collective-permute-start | bytes 1032200 | tf_op jit(solution)/shard_map/ppermute | solution.py:240
  23.0 12.9 %collective-permute-start.4 = (bf16[1,192,512]{2,1,0:T(8,128)(2,1)S(1)}, bf16[1,192,512]{2,1,0:T(8,128)(2,1)S(1)}, u32[]{:S(2)}, u32[]{:S(2)}) collective-permute-start(bf16[1,192,512]{2,1,0:T(8,128)(2,1)S(1)} %grad_far_0.1.refs_4_.refs_0_), channel_id=1, source_target_pairs={{0,2},{1,3},{2,0},{3,1},{4,6},{5,7},{6,4},{7,5},{8,10},{9,11},{10,... | collective-permute-start | bytes 589832 | tf_op jit(solution)/shard_map/ppermute | solution.py:231
  27.4 13.5 %collective-permute-start.6 = (bf16[2,192,512]{2,1,0:T(8,128)(2,1)S(1)}, bf16[2,192,512]{2,1,0:T(8,128)(2,1)S(1)}, u32[]{:S(2)}, u32[]{:S(2)}) collective-permute-start(bf16[2,192,512]{2,1,0:T(8,128)(2,1)S(1)} %behind_middle_0.1.refs_1_), channel_id=1, source_target_pairs={{0,0},{1,1},{2,4},{3,5},{4,2},{5,3},{6,6},{7,7},{8,8},{9,9},{10,12... | collective-permute-start | bytes 1179656 | tf_op jit(solution)/shard_map/ppermute | solution.py:231
  28.1 18.5 %collective-permute-start.9 = (bf16[192,896]{1,0:T(8,128)(2,1)S(1)}, bf16[192,896]{1,0:T(8,128)(2,1)S(1)}, u32[]{:S(2)}, u32[]{:S(2)}) collective-permute-start(bf16[192,896]{1,0:T(8,128)(2,1)S(1)} %grad_rows_1.1.refs_4_.refs_1_), channel_id=1, source_target_pairs={{0,1},{1,0},{2,3},{3,2},{4,5},{5,4},{6,7},{7,6},{8,9},{9,8},{10,11... | collective-permute-start | bytes 1032200 | tf_op jit(solution)/shard_map/ppermute | solution.py:240
  32.0 13.7 %collective-permute-start.10 = (bf16[2,192,512]{2,1,0:T(8,128)(2,1)S(1)}, bf16[2,192,512]{2,1,0:T(8,128)(2,1)S(1)}, u32[]{:S(2)}, u32[]{:S(2)}) collective-permute-start(bf16[2,192,512]{2,1,0:T(8,128)(2,1)S(1)} %ahead_far_0.1.refs_2_.refs_0_), channel_id=1, source_target_pairs={{0,2},{1,3},{2,0},{3,1},{4,6},{5,7},{6,4},{7,5},{8,10},{9,11},{10,... | collective-permute-start | bytes 1179656 | tf_op jit(solution)/shard_map/ppermute | solution.py:231
  36.0 12.2 %collective-permute-start.11 = (bf16[1,192,512]{2,1,0:T(8,128)(2,1)S(1)}, bf16[1,192,512]{2,1,0:T(8,128)(2,1)S(1)}, u32[]{:S(2)}, u32[]{:S(2)}) collective-permute-start(bf16[1,192,512]{2,1,0:T(8,128)(2,1)S(1)} %grad_middle_0.1.refs_4_), channel_id=1, source_target_pairs={{0,0},{1,1},{2,4},{3,5},{4,2},{5,3},{6,6},{7,7},{8,8},{9,9},{10,12... | collective-permute-start | bytes 589832 | tf_op jit(solution)/shard_map/ppermute | solution.py:231
  41.5 12.7 %collective-permute-start.8 = (bf16[2,192,512]{2,1,0:T(8,128)(2,1)S(1)}, bf16[2,192,512]{2,1,0:T(8,128)(2,1)S(1)}, u32[]{:S(2)}, u32[]{:S(2)}) collective-permute-start(bf16[2,192,512]{2,1,0:T(8,128)(2,1)S(1)} %behind_outer_1.1.refs_1_), channel_id=1, source_target_pairs={{0,2},{1,3},{2,0},{3,1},{4,6},{5,7},{6,4},{7,5},{8,10},{9,11},{10,... | collective-permute-start | bytes 1179656 | tf_op jit(solution)/shard_map/ppermute | solution.py:231
  42.9 12.1 %collective-permute-start.7 = (bf16[192,896]{1,0:T(8,128)(2,1)S(1)}, bf16[192,896]{1,0:T(8,128)(2,1)S(1)}, u32[]{:S(2)}, u32[]{:S(2)}) collective-permute-start(bf16[192,896]{1,0:T(8,128)(2,1)S(1)} %ahead_rows_1.1.refs_4_.refs_1_), channel_id=1, source_target_pairs={{0,1},{1,0},{2,3},{3,2},{4,5},{5,4},{6,7},{7,6},{8,9},{9,8},{10,11... | collective-permute-start | bytes 1032200 | tf_op jit(solution)/shard_map/ppermute | solution.py:240
  45.9 11.8 %collective-permute-start.12 = (bf16[2,192,512]{2,1,0:T(8,128)(2,1)S(1)}, bf16[2,192,512]{2,1,0:T(8,128)(2,1)S(1)}, u32[]{:S(2)}, u32[]{:S(2)}) collective-permute-start(bf16[2,192,512]{2,1,0:T(8,128)(2,1)S(1)} %ahead_middle_0.1.refs_4_), channel_id=1, source_target_pairs={{0,0},{1,1},{2,4},{3,5},{4,2},{5,3},{6,6},{7,7},{8,8},{9,9},{10,12... | collective-permute-start | bytes 1179656 | tf_op jit(solution)/shard_map/ppermute | solution.py:231
  58.3 11.6 %collective-permute-start.13 = (bf16[2,192,512]{2,1,0:T(8,128)(2,1)S(1)}, bf16[2,192,512]{2,1,0:T(8,128)(2,1)S(1)}, u32[]{:S(2)}, u32[]{:S(2)}) collective-permute-start(bf16[2,192,512]{2,1,0:T(8,128)(2,1)S(1)} %ahead_outer_1.1.refs_2_), channel_id=1, source_target_pairs={{0,2},{1,3},{2,0},{3,1},{4,6},{5,7},{6,4},{7,5},{8,10},{9,11},{10,... | collective-permute-start | bytes 1179656 | tf_op jit(solution)/shard_map/ppermute | solution.py:231
  63.0 16.6 %collective-permute-start.19 = (bf16[2,192,512]{2,1,0:T(8,128)(2,1)S(1)}, bf16[2,192,512]{2,1,0:T(8,128)(2,1)S(1)}, u32[]{:S(2)}, u32[]{:S(2)}) collective-permute-start(bf16[2,192,512]{2,1,0:T(8,128)(2,1)S(1)} %behind_outer_2.1.refs_4_), channel_id=1, source_target_pairs={{0,2},{1,3},{2,0},{3,1},{4,6},{5,7},{6,4},{7,5},{8,10},{9,11},{10,... | collective-permute-start | bytes 1179656 | tf_op jit(solution)/shard_map/ppermute | solution.py:231
  73.7 19.6 %collective-permute-start.18 = (bf16[2,192,512]{2,1,0:T(8,128)(2,1)S(1)}, bf16[2,192,512]{2,1,0:T(8,128)(2,1)S(1)}, u32[]{:S(2)}, u32[]{:S(2)}) collective-permute-start(bf16[2,192,512]{2,1,0:T(8,128)(2,1)S(1)} %ahead_outer_2.1.refs_5_), channel_id=1, source_target_pairs={{0,2},{1,3},{2,0},{3,1},{4,6},{5,7},{6,4},{7,5},{8,10},{9,11},{10,... | collective-permute-start | bytes 1179656 | tf_op jit(solution)/shard_map/ppermute | solution.py:231
  82.0 20.3 %collective-permute-start.24 = (bf16[2,192,512]{2,1,0:T(8,128)(2,1)S(1)}, bf16[2,192,512]{2,1,0:T(8,128)(2,1)S(1)}, u32[]{:S(2)}, u32[]{:S(2)}) collective-permute-start(bf16[2,192,512]{2,1,0:T(8,128)(2,1)S(1)} %behind_back_1.1.refs_1_), channel_id=1, source_target_pairs={{0,2},{1,3},{2,0},{3,1},{4,6},{5,7},{6,4},{7,5},{8,10},{9,11},{10,... | collective-permute-start | bytes 1179656 | tf_op jit(solution)/shard_map/ppermute | solution.py:231
  94.7 29.8 %collective-permute-start.23 = (bf16[1,192,512]{2,1,0:T(8,128)(2,1)S(1)}, bf16[1,192,512]{2,1,0:T(8,128)(2,1)S(1)}, u32[]{:S(2)}, u32[]{:S(2)}) collective-permute-start(bf16[1,192,512]{2,1,0:T(8,128)(2,1)S(1)} %ahead_back_1.1.refs_1_), channel_id=1, source_target_pairs={{0,2},{1,3},{2,0},{3,1},{4,6},{5,7},{6,4},{7,5},{8,10},{9,11},{10,... | collective-permute-start | bytes 589832 | tf_op jit(solution)/shard_map/ppermute | solution.py:231
  102.4 23.0 %collective-permute-start.28 = (bf16[2,192,512]{2,1,0:T(8,128)(2,1)S(1)}, bf16[2,192,512]{2,1,0:T(8,128)(2,1)S(1)}, u32[]{:S(2)}, u32[]{:S(2)}) collective-permute-start(bf16[2,192,512]{2,1,0:T(8,128)(2,1)S(1)} %behind_first_1.1.refs_6_.refs_2_), channel_id=1, source_target_pairs={{0,0},{1,1},{2,4},{3,5},{4,2},{5,3},{6,6},{7,7},{8,8},{9,9},{10,12... | collective-permute-start | bytes 1179656 | tf_op jit(solution)/shard_map/ppermute | solution.py:231
  106.3 27.6 %collective-permute-start.25 = (bf16[192,896]{1,0:T(8,128)(2,1)S(1)}, bf16[192,896]{1,0:T(8,128)(2,1)S(1)}, u32[]{:S(2)}, u32[]{:S(2)}) collective-permute-start(bf16[192,896]{1,0:T(8,128)(2,1)S(1)} %get-tuple-element.10.refs_1_), channel_id=1, source_target_pairs={{8,1},{9,0},{10,3},{11,2},{12,5},{13,4},{14,7},{15,6},{16,9},{17,8... | collective-permute-start | bytes 1032200 | tf_op jit(solution)/shard_map/ppermute | solution.py:249
  122.5 11.3 %collective-permute-start.26 = (bf16[192,896]{1,0:T(8,128)(2,1)S(1)}, bf16[192,896]{1,0:T(8,128)(2,1)S(1)}, u32[]{:S(2)}, u32[]{:S(2)}) collective-permute-start(bf16[192,896]{1,0:T(8,128)(2,1)S(1)} %get-tuple-element.11), channel_id=1, source_target_pairs={{8,0},{9,1},{10,2},{11,3},{12,4},{13,5},{14,6},{15,7},{16,8},{17,9... | collective-permute-start | bytes 1032200 | tf_op jit(solution)/shard_map/ppermute | solution.py:249
  125.4 18.0 %collective-permute-start.32 = (bf16[2,192,512]{2,1,0:T(8,128)(2,1)S(1)}, bf16[2,192,512]{2,1,0:T(8,128)(2,1)S(1)}, u32[]{:S(2)}, u32[]{:S(2)}) collective-permute-start(bf16[2,192,512]{2,1,0:T(8,128)(2,1)S(1)} %behind_back_2.1.refs_1_), channel_id=1, source_target_pairs={{0,2},{1,3},{2,0},{3,1},{4,6},{5,7},{6,4},{7,5},{8,10},{9,11},{10,... | collective-permute-start | bytes 1179656 | tf_op jit(solution)/shard_map/ppermute | solution.py:231
  129.4 22.2 %collective-permute-start.31 = (bf16[1,192,512]{2,1,0:T(8,128)(2,1)S(1)}, bf16[1,192,512]{2,1,0:T(8,128)(2,1)S(1)}, u32[]{:S(2)}, u32[]{:S(2)}) collective-permute-start(bf16[1,192,512]{2,1,0:T(8,128)(2,1)S(1)} %ahead_back_2.1.refs_2_), channel_id=1, source_target_pairs={{0,2},{1,3},{2,0},{3,1},{4,6},{5,7},{6,4},{7,5},{8,10},{9,11},{10,... | collective-permute-start | bytes 589832 | tf_op jit(solution)/shard_map/ppermute | solution.py:231
  136.1 21.8 %collective-permute-start.29 = (bf16[192,896]{1,0:T(8,128)(2,1)S(1)}, bf16[192,896]{1,0:T(8,128)(2,1)S(1)}, u32[]{:S(2)}, u32[]{:S(2)}) collective-permute-start(bf16[192,896]{1,0:T(8,128)(2,1)S(1)} %get-tuple-element.12.refs_6_), channel_id=1, source_target_pairs={{0,9},{1,8},{2,11},{3,10},{4,13},{5,12},{6,15},{7,14},{8,17},{9,16... | collective-permute-start | bytes 1032200 | tf_op jit(solution)/shard_map/ppermute | solution.py:249
  141.5 18.3 %collective-permute-start.30 = (bf16[192,896]{1,0:T(8,128)(2,1)S(1)}, bf16[192,896]{1,0:T(8,128)(2,1)S(1)}, u32[]{:S(2)}, u32[]{:S(2)}) collective-permute-start(bf16[192,896]{1,0:T(8,128)(2,1)S(1)} %get-tuple-element.13), channel_id=1, source_target_pairs={{0,8},{1,9},{2,10},{3,11},{4,12},{5,13},{6,14},{7,15},{8,16},{9,17... | collective-permute-start | bytes 1032200 | tf_op jit(solution)/shard_map/ppermute | solution.py:249
  146.7 13.2 %collective-permute-start.35 = (bf16[192,896]{1,0:T(8,128)(2,1)S(1)}, bf16[192,896]{1,0:T(8,128)(2,1)S(1)}, u32[]{:S(2)}, u32[]{:S(2)}) collective-permute-start(bf16[192,896]{1,0:T(8,128)(2,1)S(1)} %get-tuple-element.14.refs_7_), channel_id=1, source_target_pairs={{8,1},{9,0},{10,3},{11,2},{12,5},{13,4},{14,7},{15,6},{16,9},{17,8... | collective-permute-start | bytes 1032200 | tf_op jit(solution)/shard_map/ppermute | solution.py:249
  (24 other events, 128.5 us)

commit v9 on v8

--- a/solution.py
+++ b/solution.py
@@ -137,10 +137,6 @@
     sig = jax.nn.sigmoid(gate)
     out[0] = (expanded * up * sig * (1.0 + gate * (1.0 - sig))).astype(BF16)
     out[1] = (expanded * gate * sig).astype(BF16)
-
-
-def shares_kernel(one, two, out):
-    out[...] = (one[...].astype(F32) + two[...].astype(F32)).astype(BF16)
 
 
 def result_kernel(first, one, two, out):
@@ -319,9 +315,8 @@
 
         def middle_pass(self, c):
             value = self.out[PIECES] if c == 0 else self.back[c]
-            if value.shape[0] > self.spreads or c > 0:
-                shape = (self.spreads, *value.shape[1:])
-                value = kernel_call(f"{self.name}_first_{c}", cut_first_kernel, SMALL, (value,), shape)
+            shape = (self.spreads, *value.shape[1:])
+            value = kernel_call(f"{self.name}_first_{c}", cut_first_kernel, SMALL, (value,), shape)
             self.one[c] = value
             self.mid[PIECES + c] = middle(value)
 
@@ -364,22 +359,34 @@
         operands = (near, behind.out[c + 1], grad.near[c], grad.out[c + 1], cut(scales[1], c))
         behind.act[c] = kernel_call(f"behind_act_{c}", behind_act_kernel, ACT, operands, near.shape)
 
-    def finish(chain, c):
+    def output(chain, c):
         forward = chain is ahead
         scale = cut(scales[0], c) if forward else None
         weights = downs if forward else gates
-        give, keep = second_product(f"{chain.name}_out_{c}", where, chain.activated(c), scale, weights, list(recent))
+        give, keep = second_product(
+            f"{chain.name}_out_{c}", where, chain.activated(c), scale, weights, list(recent)
+        )
         recent[:] = [give]
-        by = 1 if forward else -1
-        sent[forward, c] = to_section(give, by, 1), to_section(keep, by, 0)
-
-    def shares(chain):
-        pieces = sent[chain is ahead, 0]
-        shape = pieces[0].shape
-        sent[chain is ahead, 0] = kernel_call(f"{chain.name}_shares", shares_kernel, SMALL, pieces, shape)
+        return give, keep
+
+    def finish_first(chain):
+        give, keep = output(chain, 0)
+        sent[chain, 0] = swapped(give), keep
+
+    def send_first(chain):
+        share, keep = sent[chain, 0]
+        total = kernel_call(
+            f"{chain.name}_shares", sum_kernel, SMALL, (keep, share), keep.shape
+        )
+        sent[chain, 0] = to_section(total, 1 if chain is ahead else -1, 0)
+
+    def finish_last(chain):
+        give, keep = output(chain, 1)
+        by = 1 if chain is ahead else -1
+        sent[chain, 1] = to_section(give, by, 1), to_section(keep, by, 0)
 
     def result(chain):
-        operands = (sent[chain is ahead, 0], *sent[chain is ahead, 1])
+        operands = (sent[chain, 0], *sent[chain, 1])
         shape = (height, operands[0].shape[1])
         return kernel_call(f"{chain.name}_result", result_kernel, SMALL, operands, shape)[None]
 
@@ -424,15 +431,15 @@
     activate_ahead(1)
     ahead.outer_pass(1)
     behind.middle_pass(1)
-    finish(behind, 0)
+    finish_first(behind)
     ahead.middle_pass(1)
     behind.outer_pass(2)
+    finish_first(ahead)
     ahead.outer_pass(2)
-    shares(behind)
-    finish(ahead, 0)
-    finish(behind, 1)
-    finish(ahead, 1)
-    shares(ahead)
+    send_first(behind)
+    finish_last(behind)
+    send_first(ahead)
+    finish_last(ahead)
     behind_sent = result(behind)
     ahead_sent = result(ahead)
     return ahead_sent, behind_sent

time: 169 us -> 156 us (0.923)
  starting transfers between devices: 101 us -> 85.5 us
  waiting for transfers between devices: 11.2 us -> 14.4 us
    ppermute x23, starting transfers between devices: 57.8 us -> 47.6 us  [between(): return lax.ppermute(value, 'expert', pairs)]
    ppermute x8 -> x6, starting transfers between devices: 36.5 us -> 28.7 us  [to_section(): return lax.ppermute(value, ('section', 'expert'), pairs)]
    ppermute x23, waiting for transfers between devices: 1.37 us -> 4.41 us  [between(): return lax.ppermute(value, 'expert', pairs)]
    ppermute x6 -> x8, starting transfers between devices: 7.08 us -> 9.18 us  [swapped(): return lax.ppermute(value, 'expert', [(i, i ^ 1) for i in range(devices)])]
    pallas_call x49 -> x50, Pallas kernels: 47.9 us -> 48.1 us  [call(): pl.pallas_call(run, compiler_params=pltpu.CompilerParams(vmem_limit_bytes...]
    ppermute x8 -> x6, waiting for transfers between devices: 4.9 us -> 5 us  [to_section(): return lax.ppermute(value, ('section', 'expert'), pairs)]
    ppermute x6 -> x8, waiting for transfers between devices: 4.95 us -> 4.96 us  [swapped(): return lax.ppermute(value, 'expert', [(i, i ^ 1) for i in range(devices)])]
  transfers between devices with their start and end apart: 37 -> 37, of which waited for: 5 -> 5; matrix products, arithmetic and copies ran while one was open for 0% -> 0% of each run, Pallas kernels for 28% -> 30%
where the time goes in v9:
time: 156 us; the launch traced here: 155 us
  starting transfers between devices  85.5 us (55%)
  Pallas kernels  48.1 us (31%)
  waiting for transfers between devices  14.4 us (9%)
  local copies, waits for them, and re-layouts  5.87 us (4%)
    pallas_call x50, Pallas kernels, call(): pl.pallas_call(run, compiler_params=pltpu.CompilerParams(vmem_limit_bytes...  48.1 us
    ppermute x23, starting transfers between devices, between(): return lax.ppermute(value, 'expert', pairs)  47.6 us
    ppermute x6, starting transfers between devices, to_section(): return lax.ppermute(value, ('section', 'expert'), pairs)  28.7 us
    ppermute x8, starting transfers between devices, swapped(): return lax.ppermute(value, 'expert', [(i, i ^ 1) for i in range(devices)])  9.18 us
    unnamed x22, local copies, waits for them, and re-layouts  5.31 us
    ppermute x6, waiting for transfers between devices, to_section(): return lax.ppermute(value, ('section', 'expert'), pairs)  5 us
    ppermute x8, waiting for transfers between devices, swapped(): return lax.ppermute(value, 'expert', [(i, i ^ 1) for i in range(devices)])  4.96 us
    ppermute x23, waiting for transfers between devices, between(): return lax.ppermute(value, 'expert', pairs)  4.41 us
  transfers between devices with their start and end apart: 37, of which 5 were waited for; matrix products, arithmetic and copies ran while one was open for 0% of the time, Pallas kernels for 30%

profile of v9, /device:TPU:1, one launch (start us, length us, event | category | flops | bytes accessed | tf_op | source)
XLA Modules:
  0.0 155.3 jit_solution(1254206567220722851)
XLA Ops:
  6.9 4.9 %collective-permute-done.1.refs_2_ = bf16[192,896]{1,0:T(8,128)(2,1)} collective-permute-done((bf16[192,896]{1,0:T(8,128)(2,1)S(1)}, bf16[192,896]{1,0:T(8,128)(2,1)}, u32[]{:S(2)}, u32[]{:S(2)}) %collective-permute-start.1) | collective-permute-done | bytes 344096 | tf_op jit(solution)/shard_map/ppermute | solution.py:236
  11.8 3.1 %copy-done = bf16[1,1,2,1024,1792]{4,3,2,1,0:T(8,128)(2,1)S(1)} copy-done((bf16[1,1,2,1024,1792]{4,3,2,1,0:T(8,128)(2,1)S(1)}, bf16[1,1,2,1024,1792]{4,3,2,1,0:T(8,128)(2,1)}, u32[]{:S(2)}) %copy-start) | copy-done | bytes 7340056
  14.9 3.9 %behind_far_0.1.refs_1_.refs_0_ = bf16[2,192,512]{2,1,0:T(8,128)(2,1)S(1)} custom-call(s32[3]{0:T(128)S(1)} %pad_add_fusion.refs_0_, bf16[192,896]{1,0:T(8,128)(2,1)S(1)} %behind_rows_0.1.refs_1_, bf16[192,896]{1,0:T(8,128)(2,1)} %collective-permute-done.1.refs_2_, bf16[2,1024,1792]{2,1,0:T(8,128)(2,1)S(1)} %bitcast.21, ...), custom_call_target="tpu_custom_call" | custom-call | flops 10400000000 | bytes 1024 | tf_op jit(solution)/shard_map/behind_far_0/pallas_call | solution.py:38
  23.7 3.6 %behind_near_0.1.refs_2_.refs_0_ = bf16[2,192,512]{2,1,0:T(8,128)(2,1)S(1)} custom-call(s32[3]{0:T(128)S(1)} %pad_add_fusion.refs_0_, bf16[192,896]{1,0:T(8,128)(2,1)S(1)} %behind_rows_0.1.refs_1_, bf16[192,896]{1,0:T(8,128)(2,1)} %collective-permute-done.1.refs_2_, bf16[2,1024,1792]{2,1,0:T(8,128)(2,1)S(1)} %bitcast.24, ...), custom_call_target="tpu_custom_call" | custom-call | flops 10400000000 | bytes 1024 | tf_op jit(solution)/shard_map/behind_near_0/pallas_call | solution.py:38
  29.4 2.6 %ahead_far_0.1.refs_2_.refs_0_ = bf16[2,192,512]{2,1,0:T(8,128)(2,1)S(1)} custom-call(s32[3]{0:T(128)S(1)} %pad_add_fusion.refs_0_, bf16[192,896]{1,0:T(8,128)(2,1)S(1)} %ahead_rows_0.1.refs_4_.refs_1_, bf16[192,896]{1,0:T(8,128)(2,1)S(1)} %collective-permute-done.refs_2_, bf16[2,1024,1792]{2,1,0:T(8,128)(2,1)S(1)} %bitcast.25, ...), custom_call_target="tpu_custom_call" | custom-call | flops 10400000000 | bytes 1024 | tf_op jit(solution)/shard_map/ahead_far_0/pallas_call | solution.py:38
  32.0 3.9 %collective-permute-start.10 = (bf16[2,192,512]{2,1,0:T(8,128)(2,1)S(1)}, bf16[2,192,512]{2,1,0:T(8,128)(2,1)S(1)}, u32[]{:S(2)}, u32[]{:S(2)}) collective-permute-start(bf16[2,192,512]{2,1,0:T(8,128)(2,1)S(1)} %ahead_far_0.1.refs_2_.refs_0_), channel_id=1, source_target_pairs={{0,2},{1,3},{2,0},{3,1},{4,6},{5,7},{6,4},{7,5},{8,10},{9,11},{10,... | collective-permute-start | bytes 1179656 | tf_op jit(solution)/shard_map/ppermute | solution.py:227
  38.3 2.6 %behind_far_1.1.refs_1_.refs_4_.refs_0_ = bf16[2,192,512]{2,1,0:T(8,128)(2,1)S(1)} custom-call(s32[3]{0:T(128)S(1)} %pad_add_fusion.refs_0_, bf16[192,896]{1,0:T(8,128)(2,1)S(1)} %behind_rows_1.1.refs_4_.refs_1_, bf16[192,896]{1,0:T(8,128)(2,1)S(1)} %collective-permute-done.2.refs_2_, bf16[2,1024,1792]{2,1,0:T(8,128)(2,1)S(1)} %bitcast.26, ...), custom_call_target="tpu_custom_call" | custom-call | flops 10400000000 | bytes 1024 | tf_op jit(solution)/shard_map/behind_far_1/pallas_call | solution.py:38
  43.2 2.6 %ahead_near_0.1.refs_2_.refs_0_ = bf16[2,192,512]{2,1,0:T(8,128)(2,1)S(1)} custom-call(s32[3]{0:T(128)S(1)} %pad_add_fusion.refs_0_, bf16[192,896]{1,0:T(8,128)(2,1)S(1)} %ahead_rows_0.1.refs_4_.refs_1_, bf16[192,896]{1,0:T(8,128)(2,1)S(1)} %collective-permute-done.refs_2_, bf16[2,1024,1792]{2,1,0:T(8,128)(2,1)S(1)} %bitcast.27, ...), custom_call_target="tpu_custom_call" | custom-call | flops 10400000000 | bytes 1024 | tf_op jit(solution)/shard_map/ahead_near_0/pallas_call | solution.py:38
  48.8 2.9 %collective-permute-start.14 = (bf16[1,192,512]{2,1,0:T(8,128)(2,1)S(1)}, bf16[1,192,512]{2,1,0:T(8,128)(2,1)S(1)}, u32[]{:S(2)}, u32[]{:S(2)}) collective-permute-start(bf16[1,192,512]{2,1,0:T(8,128)(2,1)S(1)} %grad_outer_1.1.refs_4_), channel_id=1, source_target_pairs={{0,2},{1,3},{2,0},{3,1},{4,6},{5,7},{6,4},{7,5},{8,10},{9,11},{10,... | collective-permute-start | bytes 589832 | tf_op jit(solution)/shard_map/ppermute | solution.py:227
  51.6 2.6 %behind_near_1.1.refs_2_.refs_0_ = bf16[2,192,512]{2,1,0:T(8,128)(2,1)S(1)} custom-call(s32[3]{0:T(128)S(1)} %pad_add_fusion.refs_0_, bf16[192,896]{1,0:T(8,128)(2,1)S(1)} %behind_rows_1.1.refs_4_.refs_1_, bf16[192,896]{1,0:T(8,128)(2,1)S(1)} %collective-permute-done.2.refs_2_, bf16[2,1024,1792]{2,1,0:T(8,128)(2,1)S(1)} %bitcast.28, ...), custom_call_target="tpu_custom_call" | custom-call | flops 10400000000 | bytes 1024 | tf_op jit(solution)/shard_map/behind_near_1/pallas_call | solution.py:38
  55.1 2.6 %ahead_far_1.1.refs_1_.refs_4_.refs_0_ = bf16[2,192,512]{2,1,0:T(8,128)(2,1)S(1)} custom-call(s32[3]{0:T(128)S(1)} %pad_add_fusion.refs_0_, bf16[192,896]{1,0:T(8,128)(2,1)S(1)} %ahead_rows_1.1.refs_4_.refs_1_, bf16[192,896]{1,0:T(8,128)(2,1)S(1)} %collective-permute-done.7.refs_2_, bf16[2,1024,1792]{2,1,0:T(8,128)(2,1)S(1)} %bitcast.29, ...), custom_call_target="tpu_custom_call" | custom-call | flops 10400000000 | bytes 1024 | tf_op jit(solution)/shard_map/ahead_far_1/pallas_call | solution.py:38
  63.0 4.2 %collective-permute-start.17 = (bf16[2,192,512]{2,1,0:T(8,128)(2,1)S(1)}, bf16[2,192,512]{2,1,0:T(8,128)(2,1)S(1)}, u32[]{:S(2)}, u32[]{:S(2)}) collective-permute-start(bf16[2,192,512]{2,1,0:T(8,128)(2,1)S(1)} %behind_outer_2.1.refs_4_), channel_id=1, source_target_pairs={{0,2},{1,3},{2,0},{3,1},{4,6},{5,7},{6,4},{7,5},{8,10},{9,11},{10,... | collective-permute-start | bytes 1179656 | tf_op jit(solution)/shard_map/ppermute | solution.py:227
  67.2 2.6 %ahead_near_1.1.refs_2_.refs_0_ = bf16[2,192,512]{2,1,0:T(8,128)(2,1)S(1)} custom-call(s32[3]{0:T(128)S(1)} %pad_add_fusion.refs_0_, bf16[192,896]{1,0:T(8,128)(2,1)S(1)} %ahead_rows_1.1.refs_4_.refs_1_, bf16[192,896]{1,0:T(8,128)(2,1)S(1)} %collective-permute-done.7.refs_2_, bf16[2,1024,1792]{2,1,0:T(8,128)(2,1)S(1)} %bitcast.30, ...), custom_call_target="tpu_custom_call" | custom-call | flops 10400000000 | bytes 1024 | tf_op jit(solution)/shard_map/ahead_near_1/pallas_call | solution.py:38
  73.1 3.8 %collective-permute-done.17.refs_0_.refs_1_ = bf16[2,192,512]{2,1,0:T(8,128)(2,1)S(1)} collective-permute-done((bf16[2,192,512]{2,1,0:T(8,128)(2,1)S(1)}, bf16[2,192,512]{2,1,0:T(8,128)(2,1)S(1)}, u32[]{:S(2)}, u32[]{:S(2)}) %collective-permute-start.17) | collective-permute-done | bytes 393248 | tf_op jit(solution)/shard_map/ppermute | solution.py:227
  78.2 3.5 %collective-permute-start.19 = (bf16[2,192,512]{2,1,0:T(8,128)(2,1)S(1)}, bf16[2,192,512]{2,1,0:T(8,128)(2,1)S(1)}, u32[]{:S(2)}, u32[]{:S(2)}) collective-permute-start(bf16[2,192,512]{2,1,0:T(8,128)(2,1)S(1)} %ahead_outer_2.1.refs_5_), channel_id=1, source_target_pairs={{0,2},{1,3},{2,0},{3,1},{4,6},{5,7},{6,4},{7,5},{8,10},{9,11},{10,... | collective-permute-start | bytes 1179656 | tf_op jit(solution)/shard_map/ppermute | solution.py:227
  82.6 7.6 %collective-permute-start.24 = (bf16[2,192,512]{2,1,0:T(8,128)(2,1)S(1)}, bf16[2,192,512]{2,1,0:T(8,128)(2,1)S(1)}, u32[]{:S(2)}, u32[]{:S(2)}) collective-permute-start(bf16[2,192,512]{2,1,0:T(8,128)(2,1)S(1)} %behind_back_1.1.refs_1_), channel_id=1, source_target_pairs={{0,2},{1,3},{2,0},{3,1},{4,6},{5,7},{6,4},{7,5},{8,10},{9,11},{10,... | collective-permute-start | bytes 1179656 | tf_op jit(solution)/shard_map/ppermute | solution.py:227
  91.7 6.7 %collective-permute-start.23 = (bf16[1,192,512]{2,1,0:T(8,128)(2,1)S(1)}, bf16[1,192,512]{2,1,0:T(8,128)(2,1)S(1)}, u32[]{:S(2)}, u32[]{:S(2)}) collective-permute-start(bf16[1,192,512]{2,1,0:T(8,128)(2,1)S(1)} %ahead_back_1.1.refs_1_), channel_id=1, source_target_pairs={{0,2},{1,3},{2,0},{3,1},{4,6},{5,7},{6,4},{7,5},{8,10},{9,11},{10,... | collective-permute-start | bytes 589832 | tf_op jit(solution)/shard_map/ppermute | solution.py:227
  99.1 3.2 %behind_out_0.1 = (bf16[192,896]{1,0:T(8,128)(2,1)S(1)}, bf16[192,896]{1,0:T(8,128)(2,1)S(1)}) custom-call(s32[3]{0:T(128)S(1)} %pad_add_fusion.refs_0_, bf16[2,192,512]{2,1,0:T(8,128)(2,1)S(1)} %behind_act_0.1.refs_4_.refs_1_, bf16[2,192,512]{2,1,0:T(8,128)(2,1)S(1)} %behind_first_0.1.refs_4_.refs_2_, ...), custom_call_target="tpu_custom_call" | custom-call | flops 20000000000 | bytes 1024 | tf_op jit(solution)/shard_map/behind_out_0/pallas_call | solution.py:38
  104.6 3.9 %collective-permute-start.27 = (bf16[2,192,512]{2,1,0:T(8,128)(2,1)S(1)}, bf16[2,192,512]{2,1,0:T(8,128)(2,1)S(1)}, u32[]{:S(2)}, u32[]{:S(2)}) collective-permute-start(bf16[2,192,512]{2,1,0:T(8,128)(2,1)S(1)} %behind_back_2.1.refs_7_), channel_id=1, source_target_pairs={{0,2},{1,3},{2,0},{3,1},{4,6},{5,7},{6,4},{7,5},{8,10},{9,11},{10,... | collective-permute-start | bytes 1179656 | tf_op jit(solution)/shard_map/ppermute | solution.py:227
  113.1 15.9 %collective-permute-start.34 = (bf16[192,896]{1,0:T(8,128)(2,1)S(1)}, bf16[192,896]{1,0:T(8,128)(2,1)S(1)}, u32[]{:S(2)}, u32[]{:S(2)}) collective-permute-start(bf16[192,896]{1,0:T(8,128)(2,1)S(1)} %behind_shares.1.refs_6_), channel_id=1, source_target_pairs={{8,0},{9,1},{10,2},{11,3},{12,4},{13,5},{14,6},{15,7},{16,8},{17,9... | collective-permute-start | bytes 1032200 | tf_op jit(solution)/shard_map/ppermute | solution.py:245
  129.1 3.2 %behind_out_1.1 = (bf16[192,896]{1,0:T(8,128)(2,1)S(1)}, bf16[192,896]{1,0:T(8,128)(2,1)S(1)}) custom-call(s32[3]{0:T(128)S(1)} %pad_add_fusion.refs_0_, bf16[2,192,512]{2,1,0:T(8,128)(2,1)S(1)} %behind_act_1.1.refs_1_.refs_3_, bf16[2,192,512]{2,1,0:T(8,128)(2,1)S(1)} %behind_first_1.1.refs_6_.refs_2_, ...), custom_call_target="tpu_custom_call" | custom-call | flops 20000000000 | bytes 1024 | tf_op jit(solution)/shard_map/behind_out_1/pallas_call | solution.py:38
  136.5 3.6 %collective-permute-start.30 = (bf16[192,896]{1,0:T(8,128)(2,1)S(1)}, bf16[192,896]{1,0:T(8,128)(2,1)S(1)}, u32[]{:S(2)}, u32[]{:S(2)}) collective-permute-start(bf16[192,896]{1,0:T(8,128)(2,1)S(1)} %ahead_shares.1.refs_7_), channel_id=1, source_target_pairs={{0,8},{1,9},{2,10},{3,11},{4,12},{5,13},{6,14},{7,15},{8,16},{9,17... | collective-permute-start | bytes 1032200 | tf_op jit(solution)/shard_map/ppermute | solution.py:245
  142.3 3.1 %collective-permute-start.32 = (bf16[192,896]{1,0:T(8,128)(2,1)S(1)}, bf16[192,896]{1,0:T(8,128)(2,1)S(1)}, u32[]{:S(2)}, u32[]{:S(2)}) collective-permute-start(bf16[192,896]{1,0:T(8,128)(2,1)S(1)} %get-tuple-element.15.refs_3_), channel_id=1, source_target_pairs={{0,9},{1,8},{2,11},{3,10},{4,13},{5,12},{6,15},{7,14},{8,17},{9,16... | collective-permute-start | bytes 1032200 | tf_op jit(solution)/shard_map/ppermute | solution.py:245
  148.3 2.6 %collective-permute-done.32.refs_1_ = bf16[192,896]{1,0:T(8,128)(2,1)S(1)} collective-permute-done((bf16[192,896]{1,0:T(8,128)(2,1)S(1)}, bf16[192,896]{1,0:T(8,128)(2,1)S(1)}, u32[]{:S(2)}, u32[]{:S(2)}) %collective-permute-start.32) | collective-permute-done | bytes 344096 | tf_op jit(solution)/shard_map/ppermute | solution.py:245
  (130 shorter events, 54.7 us)
Async XLA Ops:
  3.9 17.4 %collective-permute-start.3 = (bf16[192,896]{1,0:T(8,128)(2,1)S(1)}, bf16[192,896]{1,0:T(8,128)(2,1)S(1)}, u32[]{:S(2)}, u32[]{:S(2)}) collective-permute-start(bf16[192,896]{1,0:T(8,128)(2,1)S(1)} %grad_rows_0.1.refs_1_), channel_id=1, source_target_pairs={{0,1},{1,0},{2,3},{3,2},{4,5},{5,4},{6,7},{7,6},{8,9},{9,8},{10,11... | collective-permute-start | bytes 1032200 | tf_op jit(solution)/shard_map/ppermute | solution.py:236
  5.0 24.4 %collective-permute-start = (bf16[192,896]{1,0:T(8,128)(2,1)S(1)}, bf16[192,896]{1,0:T(8,128)(2,1)S(1)}, u32[]{:S(2)}, u32[]{:S(2)}) collective-permute-start(bf16[192,896]{1,0:T(8,128)(2,1)S(1)} %ahead_rows_0.1.refs_4_.refs_1_), channel_id=1, source_target_pairs={{0,1},{1,0},{2,3},{3,2},{4,5},{5,4},{6,7},{7,6},{8,9},{9,8},{10,11... | collective-permute-start | bytes 1032200 | tf_op jit(solution)/shard_map/ppermute | solution.py:236
  20.1 18.2 %collective-permute-start.2 = (bf16[192,896]{1,0:T(8,128)(2,1)S(1)}, bf16[192,896]{1,0:T(8,128)(2,1)S(1)}, u32[]{:S(2)}, u32[]{:S(2)}) collective-permute-start(bf16[192,896]{1,0:T(8,128)(2,1)S(1)} %behind_rows_1.1.refs_4_.refs_1_), channel_id=1, source_target_pairs={{0,1},{1,0},{2,3},{3,2},{4,5},{5,4},{6,7},{7,6},{8,9},{9,8},{10,11... | collective-permute-start | bytes 1032200 | tf_op jit(solution)/shard_map/ppermute | solution.py:236
  23.0 12.9 %collective-permute-start.4 = (bf16[1,192,512]{2,1,0:T(8,128)(2,1)S(1)}, bf16[1,192,512]{2,1,0:T(8,128)(2,1)S(1)}, u32[]{:S(2)}, u32[]{:S(2)}) collective-permute-start(bf16[1,192,512]{2,1,0:T(8,128)(2,1)S(1)} %grad_far_0.1.refs_4_.refs_0_), channel_id=1, source_target_pairs={{0,2},{1,3},{2,0},{3,1},{4,6},{5,7},{6,4},{7,5},{8,10},{9,11},{10,... | collective-permute-start | bytes 589832 | tf_op jit(solution)/shard_map/ppermute | solution.py:227
  27.4 13.5 %collective-permute-start.6 = (bf16[2,192,512]{2,1,0:T(8,128)(2,1)S(1)}, bf16[2,192,512]{2,1,0:T(8,128)(2,1)S(1)}, u32[]{:S(2)}, u32[]{:S(2)}) collective-permute-start(bf16[2,192,512]{2,1,0:T(8,128)(2,1)S(1)} %behind_middle_0.1.refs_1_), channel_id=1, source_target_pairs={{0,0},{1,1},{2,4},{3,5},{4,2},{5,3},{6,6},{7,7},{8,8},{9,9},{10,12... | collective-permute-start | bytes 1179656 | tf_op jit(solution)/shard_map/ppermute | solution.py:227
  28.1 18.5 %collective-permute-start.9 = (bf16[192,896]{1,0:T(8,128)(2,1)S(1)}, bf16[192,896]{1,0:T(8,128)(2,1)S(1)}, u32[]{:S(2)}, u32[]{:S(2)}) collective-permute-start(bf16[192,896]{1,0:T(8,128)(2,1)S(1)} %grad_rows_1.1.refs_4_.refs_1_), channel_id=1, source_target_pairs={{0,1},{1,0},{2,3},{3,2},{4,5},{5,4},{6,7},{7,6},{8,9},{9,8},{10,11... | collective-permute-start | bytes 1032200 | tf_op jit(solution)/shard_map/ppermute | solution.py:236
  32.0 13.7 %collective-permute-start.10 = (bf16[2,192,512]{2,1,0:T(8,128)(2,1)S(1)}, bf16[2,192,512]{2,1,0:T(8,128)(2,1)S(1)}, u32[]{:S(2)}, u32[]{:S(2)}) collective-permute-start(bf16[2,192,512]{2,1,0:T(8,128)(2,1)S(1)} %ahead_far_0.1.refs_2_.refs_0_), channel_id=1, source_target_pairs={{0,2},{1,3},{2,0},{3,1},{4,6},{5,7},{6,4},{7,5},{8,10},{9,11},{10,... | collective-permute-start | bytes 1179656 | tf_op jit(solution)/shard_map/ppermute | solution.py:227
  36.0 12.2 %collective-permute-start.11 = (bf16[1,192,512]{2,1,0:T(8,128)(2,1)S(1)}, bf16[1,192,512]{2,1,0:T(8,128)(2,1)S(1)}, u32[]{:S(2)}, u32[]{:S(2)}) collective-permute-start(bf16[1,192,512]{2,1,0:T(8,128)(2,1)S(1)} %grad_middle_0.1.refs_4_), channel_id=1, source_target_pairs={{0,0},{1,1},{2,4},{3,5},{4,2},{5,3},{6,6},{7,7},{8,8},{9,9},{10,12... | collective-permute-start | bytes 589832 | tf_op jit(solution)/shard_map/ppermute | solution.py:227
  41.5 12.7 %collective-permute-start.8 = (bf16[2,192,512]{2,1,0:T(8,128)(2,1)S(1)}, bf16[2,192,512]{2,1,0:T(8,128)(2,1)S(1)}, u32[]{:S(2)}, u32[]{:S(2)}) collective-permute-start(bf16[2,192,512]{2,1,0:T(8,128)(2,1)S(1)} %behind_outer_1.1.refs_1_), channel_id=1, source_target_pairs={{0,2},{1,3},{2,0},{3,1},{4,6},{5,7},{6,4},{7,5},{8,10},{9,11},{10,... | collective-permute-start | bytes 1179656 | tf_op jit(solution)/shard_map/ppermute | solution.py:227
  42.9 12.1 %collective-permute-start.7 = (bf16[192,896]{1,0:T(8,128)(2,1)S(1)}, bf16[192,896]{1,0:T(8,128)(2,1)S(1)}, u32[]{:S(2)}, u32[]{:S(2)}) collective-permute-start(bf16[192,896]{1,0:T(8,128)(2,1)S(1)} %ahead_rows_1.1.refs_4_.refs_1_), channel_id=1, source_target_pairs={{0,1},{1,0},{2,3},{3,2},{4,5},{5,4},{6,7},{7,6},{8,9},{9,8},{10,11... | collective-permute-start | bytes 1032200 | tf_op jit(solution)/shard_map/ppermute | solution.py:236
  45.9 11.8 %collective-permute-start.12 = (bf16[2,192,512]{2,1,0:T(8,128)(2,1)S(1)}, bf16[2,192,512]{2,1,0:T(8,128)(2,1)S(1)}, u32[]{:S(2)}, u32[]{:S(2)}) collective-permute-start(bf16[2,192,512]{2,1,0:T(8,128)(2,1)S(1)} %ahead_middle_0.1.refs_4_), channel_id=1, source_target_pairs={{0,0},{1,1},{2,4},{3,5},{4,2},{5,3},{6,6},{7,7},{8,8},{9,9},{10,12... | collective-permute-start | bytes 1179656 | tf_op jit(solution)/shard_map/ppermute | solution.py:227
  48.8 11.0 %collective-permute-start.14 = (bf16[1,192,512]{2,1,0:T(8,128)(2,1)S(1)}, bf16[1,192,512]{2,1,0:T(8,128)(2,1)S(1)}, u32[]{:S(2)}, u32[]{:S(2)}) collective-permute-start(bf16[1,192,512]{2,1,0:T(8,128)(2,1)S(1)} %grad_outer_1.1.refs_4_), channel_id=1, source_target_pairs={{0,2},{1,3},{2,0},{3,1},{4,6},{5,7},{6,4},{7,5},{8,10},{9,11},{10,... | collective-permute-start | bytes 589832 | tf_op jit(solution)/shard_map/ppermute | solution.py:227
  58.3 11.6 %collective-permute-start.13 = (bf16[2,192,512]{2,1,0:T(8,128)(2,1)S(1)}, bf16[2,192,512]{2,1,0:T(8,128)(2,1)S(1)}, u32[]{:S(2)}, u32[]{:S(2)}) collective-permute-start(bf16[2,192,512]{2,1,0:T(8,128)(2,1)S(1)} %ahead_outer_1.1.refs_2_), channel_id=1, source_target_pairs={{0,2},{1,3},{2,0},{3,1},{4,6},{5,7},{6,4},{7,5},{8,10},{9,11},{10,... | collective-permute-start | bytes 1179656 | tf_op jit(solution)/shard_map/ppermute | solution.py:227
  63.0 13.9 %collective-permute-start.17 = (bf16[2,192,512]{2,1,0:T(8,128)(2,1)S(1)}, bf16[2,192,512]{2,1,0:T(8,128)(2,1)S(1)}, u32[]{:S(2)}, u32[]{:S(2)}) collective-permute-start(bf16[2,192,512]{2,1,0:T(8,128)(2,1)S(1)} %behind_outer_2.1.refs_4_), channel_id=1, source_target_pairs={{0,2},{1,3},{2,0},{3,1},{4,6},{5,7},{6,4},{7,5},{8,10},{9,11},{10,... | collective-permute-start | bytes 1179656 | tf_op jit(solution)/shard_map/ppermute | solution.py:227
  78.2 12.0 %collective-permute-start.19 = (bf16[2,192,512]{2,1,0:T(8,128)(2,1)S(1)}, bf16[2,192,512]{2,1,0:T(8,128)(2,1)S(1)}, u32[]{:S(2)}, u32[]{:S(2)}) collective-permute-start(bf16[2,192,512]{2,1,0:T(8,128)(2,1)S(1)} %ahead_outer_2.1.refs_5_), channel_id=1, source_target_pairs={{0,2},{1,3},{2,0},{3,1},{4,6},{5,7},{6,4},{7,5},{8,10},{9,11},{10,... | collective-permute-start | bytes 1179656 | tf_op jit(solution)/shard_map/ppermute | solution.py:227
  82.6 15.8 %collective-permute-start.24 = (bf16[2,192,512]{2,1,0:T(8,128)(2,1)S(1)}, bf16[2,192,512]{2,1,0:T(8,128)(2,1)S(1)}, u32[]{:S(2)}, u32[]{:S(2)}) collective-permute-start(bf16[2,192,512]{2,1,0:T(8,128)(2,1)S(1)} %behind_back_1.1.refs_1_), channel_id=1, source_target_pairs={{0,2},{1,3},{2,0},{3,1},{4,6},{5,7},{6,4},{7,5},{8,10},{9,11},{10,... | collective-permute-start | bytes 1179656 | tf_op jit(solution)/shard_map/ppermute | solution.py:227
  91.7 12.2 %collective-permute-start.23 = (bf16[1,192,512]{2,1,0:T(8,128)(2,1)S(1)}, bf16[1,192,512]{2,1,0:T(8,128)(2,1)S(1)}, u32[]{:S(2)}, u32[]{:S(2)}) collective-permute-start(bf16[1,192,512]{2,1,0:T(8,128)(2,1)S(1)} %ahead_back_1.1.refs_1_), channel_id=1, source_target_pairs={{0,2},{1,3},{2,0},{3,1},{4,6},{5,7},{6,4},{7,5},{8,10},{9,11},{10,... | collective-permute-start | bytes 589832 | tf_op jit(solution)/shard_map/ppermute | solution.py:227
  104.6 24.4 %collective-permute-start.27 = (bf16[2,192,512]{2,1,0:T(8,128)(2,1)S(1)}, bf16[2,192,512]{2,1,0:T(8,128)(2,1)S(1)}, u32[]{:S(2)}, u32[]{:S(2)}) collective-permute-start(bf16[2,192,512]{2,1,0:T(8,128)(2,1)S(1)} %behind_back_2.1.refs_7_), channel_id=1, source_target_pairs={{0,2},{1,3},{2,0},{3,1},{4,6},{5,7},{6,4},{7,5},{8,10},{9,11},{10,... | collective-permute-start | bytes 1179656 | tf_op jit(solution)/shard_map/ppermute | solution.py:227
  110.9 25.6 %collective-permute-start.26 = (bf16[192,896]{1,0:T(8,128)(2,1)S(1)}, bf16[192,896]{1,0:T(8,128)(2,1)S(1)}, u32[]{:S(2)}, u32[]{:S(2)}) collective-permute-start(bf16[192,896]{1,0:T(8,128)(2,1)S(1)} %get-tuple-element.12.refs_1_), channel_id=1, source_target_pairs={{0,1},{1,0},{2,3},{3,2},{4,5},{5,4},{6,7},{7,6},{8,9},{9,8},{10,11... | collective-permute-start | bytes 1032200 | tf_op jit(solution)/shard_map/ppermute | solution.py:236
  111.9 28.3 %collective-permute-start.31 = (bf16[1,192,512]{2,1,0:T(8,128)(2,1)S(1)}, bf16[1,192,512]{2,1,0:T(8,128)(2,1)S(1)}, u32[]{:S(2)}, u32[]{:S(2)}) collective-permute-start(bf16[1,192,512]{2,1,0:T(8,128)(2,1)S(1)} %ahead_back_2.1.refs_2_), channel_id=1, source_target_pairs={{0,2},{1,3},{2,0},{3,1},{4,6},{5,7},{6,4},{7,5},{8,10},{9,11},{10,... | collective-permute-start | bytes 589832 | tf_op jit(solution)/shard_map/ppermute | solution.py:227
  113.1 32.2 %collective-permute-start.34 = (bf16[192,896]{1,0:T(8,128)(2,1)S(1)}, bf16[192,896]{1,0:T(8,128)(2,1)S(1)}, u32[]{:S(2)}, u32[]{:S(2)}) collective-permute-start(bf16[192,896]{1,0:T(8,128)(2,1)S(1)} %behind_shares.1.refs_6_), channel_id=1, source_target_pairs={{8,0},{9,1},{10,2},{11,3},{12,4},{13,5},{14,6},{15,7},{16,8},{17,9... | collective-permute-start | bytes 1032200 | tf_op jit(solution)/shard_map/ppermute | solution.py:245
  132.3 15.0 %collective-permute-start.35 = (bf16[192,896]{1,0:T(8,128)(2,1)S(1)}, bf16[192,896]{1,0:T(8,128)(2,1)S(1)}, u32[]{:S(2)}, u32[]{:S(2)}) collective-permute-start(bf16[192,896]{1,0:T(8,128)(2,1)S(1)} %get-tuple-element.14.refs_2_), channel_id=1, source_target_pairs={{8,1},{9,0},{10,3},{11,2},{12,5},{13,4},{14,7},{15,6},{16,9},{17,8... | collective-permute-start | bytes 1032200 | tf_op jit(solution)/shard_map/ppermute | solution.py:245
  134.5 12.8 %collective-permute-start.36 = (bf16[192,896]{1,0:T(8,128)(2,1)S(1)}, bf16[192,896]{1,0:T(8,128)(2,1)S(1)}, u32[]{:S(2)}, u32[]{:S(2)}) collective-permute-start(bf16[192,896]{1,0:T(8,128)(2,1)S(1)} %get-tuple-element.17), channel_id=1, source_target_pairs={{8,0},{9,1},{10,2},{11,3},{12,4},{13,5},{14,6},{15,7},{16,8},{17,9... | collective-permute-start | bytes 1032200 | tf_op jit(solution)/shard_map/ppermute | solution.py:245
  136.5 16.7 %collective-permute-start.30 = (bf16[192,896]{1,0:T(8,128)(2,1)S(1)}, bf16[192,896]{1,0:T(8,128)(2,1)S(1)}, u32[]{:S(2)}, u32[]{:S(2)}) collective-permute-start(bf16[192,896]{1,0:T(8,128)(2,1)S(1)} %ahead_shares.1.refs_7_), channel_id=1, source_target_pairs={{0,8},{1,9},{2,10},{3,11},{4,12},{5,13},{6,14},{7,15},{8,16},{9,17... | collective-permute-start | bytes 1032200 | tf_op jit(solution)/shard_map/ppermute | solution.py:245
  (24 other events, 135.6 us)

commit v10 on v9

--- a/solution.py
+++ b/solution.py
@@ -25,7 +25,7 @@
     return pl.BlockSpec(array.shape, functools.partial(lambda n, *_: (0,) * n, array.ndim))
 
 
-def call(kernel, micros, operands, after, out_shape, scalars=(), grid=(1,), in_specs=None, out_specs=None, scratch=(), limit=24, name=None):
+def call(kernel, micros, operands, after, out_shape, scalars=(), grid=(1,), in_specs=None, out_specs=None, scratch=(), limit=16, name=None):
     count, unread = len(scalars) + len(operands), len(after)
 
     def run(*refs):
@@ -390,56 +390,56 @@
         shape = (height, operands[0].shape[1])
         return kernel_call(f"{chain.name}_result", result_kernel, SMALL, operands, shape)[None]
 
-    for chain in (behind, grad, ahead):
+    for chain in (behind, ahead, grad):
         chain.fetch(0)
     behind.product(0, True)
     behind.outer_sum(0)
     behind.fetch(1)
+    ahead.product(0, True)
+    ahead.outer_sum(0)
     grad.product(0, True)
     grad.outer_sum(0)
+    behind.middle_sum(0)
+    ahead.fetch(1)
+    behind.product(1, True)
     behind.product(0, False)
-    behind.middle_sum(0)
+    behind.outer_sum(1)
+    ahead.middle_sum(0)
     grad.fetch(1)
-    ahead.product(0, True)
-    ahead.outer_sum(0)
     grad.middle_sum(0)
     grad.product(0, False)
-    behind.product(1, True)
-    behind.outer_sum(1)
-    ahead.fetch(1)
+    grad.product(1, True)
+    behind.middle_sum(1)
+    grad.outer_sum(1)
+    ahead.product(1, True)
     ahead.product(0, False)
-    ahead.middle_sum(0)
-    grad.product(1, True)
-    grad.outer_sum(1)
+    ahead.outer_sum(1)
     behind.product(1, False)
-    behind.middle_sum(1)
-    ahead.product(1, True)
-    ahead.outer_sum(1)
+    activate_behind(0)
+    behind.outer_sum(2)
     grad.middle_sum(1)
-    activate_behind(0)
     grad.product(1, False)
-    behind.outer_sum(2)
     ahead.product(1, False)
     ahead.middle_sum(1)
     activate_ahead(0)
     grad.outer_sum(2)
     behind.middle_pass(0)
+    activate_behind(1)
     ahead.outer_sum(2)
-    activate_behind(1)
     behind.outer_pass(1)
     ahead.middle_pass(0)
     activate_ahead(1)
+    behind.middle_pass(1)
     ahead.outer_pass(1)
-    behind.middle_pass(1)
     finish_first(behind)
+    behind.outer_pass(2)
     ahead.middle_pass(1)
-    behind.outer_pass(2)
     finish_first(ahead)
     ahead.outer_pass(2)
     send_first(behind)
     finish_last(behind)
+    finish_last(ahead)
     send_first(ahead)
-    finish_last(ahead)
     behind_sent = result(behind)
     ahead_sent = result(ahead)
     return ahead_sent, behind_sent

time: 156 us -> 161 us (1.032)
  waiting for transfers between devices: 14.4 us -> 27.3 us
  starting transfers between devices: 85.5 us -> 74.5 us
  local copies, waits for them, and re-layouts: 5.87 us -> 8.95 us
    ppermute x23, waiting for transfers between devices: 4.41 us -> 10.9 us  [between(): return lax.ppermute(value, 'expert', pairs)]
    ppermute x23, starting transfers between devices: 47.6 us -> 41.1 us  [between(): return lax.ppermute(value, 'expert', pairs)]
    ppermute x8, waiting for transfers between devices: 4.96 us -> 10.3 us  [swapped(): return lax.ppermute(value, 'expert', [(i, i ^ 1) for i in range(devices)])]
    ppermute x6, starting transfers between devices: 28.7 us -> 23.6 us  [to_section(): return lax.ppermute(value, ('section', 'expert'), pairs)]
    unnamed x22 -> x24, local copies, waits for them, and re-layouts: 5.31 us -> 8.39 us
  transfers between devices with their start and end apart: 37 -> 37, of which waited for: 5 -> 7; matrix products, arithmetic and copies ran while one was open for 0% -> 0% of each run, Pallas kernels for 30% -> 29%
where the time goes in v10:
time: 161 us; the launch traced here: 160 us
  starting transfers between devices  74.5 us (46%)
  Pallas kernels  47.9 us (30%)
  waiting for transfers between devices  27.3 us (17%)
  local copies, waits for them, and re-layouts  8.95 us (6%)
    pallas_call x50, Pallas kernels, call(): pl.pallas_call(run, compiler_params=pltpu.CompilerParams(vmem_limit_bytes...  47.9 us
    ppermute x23, starting transfers between devices, between(): return lax.ppermute(value, 'expert', pairs)  41.1 us
    ppermute x6, starting transfers between devices, to_section(): return lax.ppermute(value, ('section', 'expert'), pairs)  23.6 us
    ppermute x23, waiting for transfers between devices, between(): return lax.ppermute(value, 'expert', pairs)  10.9 us
    ppermute x8, waiting for transfers between devices, swapped(): return lax.ppermute(value, 'expert', [(i, i ^ 1) for i in range(devices)])  10.3 us
    ppermute x8, starting transfers between devices, swapped(): return lax.ppermute(value, 'expert', [(i, i ^ 1) for i in range(devices)])  9.78 us
    unnamed x24, local copies, waits for them, and re-layouts  8.39 us
    ppermute x6, waiting for transfers between devices, to_section(): return lax.ppermute(value, ('section', 'expert'), pairs)  6.04 us
  transfers between devices with their start and end apart: 37, of which 7 were waited for; matrix products, arithmetic and copies ran while one was open for 0% of the time, Pallas kernels for 29%

profile of v10, /device:TPU:1, one launch (start us, length us, event | category | flops | bytes accessed | tf_op | source)
XLA Modules:
  0.0 160.0 jit_solution(8593321133213886891)
XLA Ops:
  6.9 4.9 %collective-permute-done.1.refs_2_ = bf16[192,896]{1,0:T(8,128)(2,1)} collective-permute-done((bf16[192,896]{1,0:T(8,128)(2,1)S(1)}, bf16[192,896]{1,0:T(8,128)(2,1)}, u32[]{:S(2)}, u32[]{:S(2)}) %collective-permute-start.1) | collective-permute-done | bytes 344096 | tf_op jit(solution)/shard_map/ppermute | solution.py:236
  11.8 3.1 %copy-done = bf16[1,1,2,1024,1792]{4,3,2,1,0:T(8,128)(2,1)S(1)} copy-done((bf16[1,1,2,1024,1792]{4,3,2,1,0:T(8,128)(2,1)S(1)}, bf16[1,1,2,1024,1792]{4,3,2,1,0:T(8,128)(2,1)}, u32[]{:S(2)}) %copy-start) | copy-done | bytes 7340056
  14.9 3.6 %behind_far_0.1.refs_1_.refs_0_ = bf16[2,192,512]{2,1,0:T(8,128)(2,1)S(1)} custom-call(s32[3]{0:T(128)S(1)} %pad_add_fusion.refs_0_, bf16[192,896]{1,0:T(8,128)(2,1)S(1)} %behind_rows_0.1.refs_1_, bf16[192,896]{1,0:T(8,128)(2,1)} %collective-permute-done.1.refs_2_, bf16[2,1024,1792]{2,1,0:T(8,128)(2,1)S(1)} %bitcast.21, ...), custom_call_target="tpu_custom_call" | custom-call | flops 10400000000 | bytes 1024 | tf_op jit(solution)/shard_map/behind_far_0/pallas_call | solution.py:38
  21.1 3.1 %copy-done.1 = bf16[1,1,2,1024,1792]{4,3,2,1,0:T(8,128)(2,1)S(1)} copy-done((bf16[1,1,2,1024,1792]{4,3,2,1,0:T(8,128)(2,1)S(1)}, bf16[1,1,2,1024,1792]{4,3,2,1,0:T(8,128)(2,1)}, u32[]{:S(2)}) %copy-start.1) | copy-done | bytes 7340056
  24.2 2.6 %ahead_far_0.1.refs_4_.refs_0_ = bf16[2,192,512]{2,1,0:T(8,128)(2,1)S(1)} custom-call(s32[3]{0:T(128)S(1)} %pad_add_fusion.refs_0_, bf16[192,896]{1,0:T(8,128)(2,1)S(1)} %ahead_rows_0.1.refs_1_, bf16[192,896]{1,0:T(8,128)(2,1)S(1)} %collective-permute-done.refs_2_, bf16[2,1024,1792]{2,1,0:T(8,128)(2,1)S(1)} %bitcast.22, ...), custom_call_target="tpu_custom_call" | custom-call | flops 10400000000 | bytes 1024 | tf_op jit(solution)/shard_map/ahead_far_0/pallas_call | solution.py:38
  33.8 2.6 %behind_far_1.1.refs_4_.refs_1_.refs_0_ = bf16[2,192,512]{2,1,0:T(8,128)(2,1)S(1)} custom-call(s32[3]{0:T(128)S(1)} %pad_add_fusion.refs_0_, bf16[192,896]{1,0:T(8,128)(2,1)S(1)} %behind_rows_1.1.refs_4_.refs_1_, bf16[192,896]{1,0:T(8,128)(2,1)S(1)} %collective-permute-done.6.refs_2_, bf16[2,1024,1792]{2,1,0:T(8,128)(2,1)S(1)} %bitcast.25, ...), custom_call_target="tpu_custom_call" | custom-call | flops 10400000000 | bytes 1024 | tf_op jit(solution)/shard_map/behind_far_1/pallas_call | solution.py:38
  36.4 3.6 %behind_near_0.1.refs_2_.refs_4_.refs_0_ = bf16[2,192,512]{2,1,0:T(8,128)(2,1)S(1)} custom-call(s32[3]{0:T(128)S(1)} %pad_add_fusion.refs_0_, bf16[192,896]{1,0:T(8,128)(2,1)S(1)} %behind_rows_0.1.refs_1_, bf16[192,896]{1,0:T(8,128)(2,1)} %collective-permute-done.1.refs_2_, bf16[2,1024,1792]{2,1,0:T(8,128)(2,1)S(1)} %bitcast.26, ...), custom_call_target="tpu_custom_call" | custom-call | flops 10400000000 | bytes 1024 | tf_op jit(solution)/shard_map/behind_near_0/pallas_call | solution.py:38
  46.6 3.2 %collective-permute-done.8.refs_2_ = bf16[192,896]{1,0:T(8,128)(2,1)S(1)} collective-permute-done((bf16[192,896]{1,0:T(8,128)(2,1)S(1)}, bf16[192,896]{1,0:T(8,128)(2,1)S(1)}, u32[]{:S(2)}, u32[]{:S(2)}) %collective-permute-start.8) | collective-permute-done | bytes 344096 | tf_op jit(solution)/shard_map/ppermute | solution.py:236
  52.8 4.5 %collective-permute-start.14 = (bf16[1,192,512]{2,1,0:T(8,128)(2,1)S(1)}, bf16[1,192,512]{2,1,0:T(8,128)(2,1)S(1)}, u32[]{:S(2)}, u32[]{:S(2)}) collective-permute-start(bf16[1,192,512]{2,1,0:T(8,128)(2,1)S(1)} %grad_outer_1.1.refs_4_), channel_id=1, source_target_pairs={{0,2},{1,3},{2,0},{3,1},{4,6},{5,7},{6,4},{7,5},{8,10},{9,11},{10,... | collective-permute-start | bytes 589832 | tf_op jit(solution)/shard_map/ppermute | solution.py:227
  57.3 2.6 %ahead_far_1.1.refs_4_.refs_1_.refs_0_ = bf16[2,192,512]{2,1,0:T(8,128)(2,1)S(1)} custom-call(s32[3]{0:T(128)S(1)} %pad_add_fusion.refs_0_, bf16[192,896]{1,0:T(8,128)(2,1)S(1)} %ahead_rows_1.1.refs_4_.refs_1_, bf16[192,896]{1,0:T(8,128)(2,1)S(1)} %collective-permute-done.4.refs_2_, bf16[2,1024,1792]{2,1,0:T(8,128)(2,1)S(1)} %bitcast.27, ...), custom_call_target="tpu_custom_call" | custom-call | flops 10400000000 | bytes 1024 | tf_op jit(solution)/shard_map/ahead_far_1/pallas_call | solution.py:38
  60.0 2.6 %ahead_near_0.1.refs_2_.refs_4_.refs_0_ = bf16[2,192,512]{2,1,0:T(8,128)(2,1)S(1)} custom-call(s32[3]{0:T(128)S(1)} %pad_add_fusion.refs_0_, bf16[192,896]{1,0:T(8,128)(2,1)S(1)} %ahead_rows_0.1.refs_1_, bf16[192,896]{1,0:T(8,128)(2,1)S(1)} %collective-permute-done.refs_2_, bf16[2,1024,1792]{2,1,0:T(8,128)(2,1)S(1)} %bitcast.28, ...), custom_call_target="tpu_custom_call" | custom-call | flops 10400000000 | bytes 1024 | tf_op jit(solution)/shard_map/ahead_near_0/pallas_call | solution.py:38
  63.3 2.6 %behind_near_1.1.refs_5_.refs_2_.refs_0_ = bf16[2,192,512]{2,1,0:T(8,128)(2,1)S(1)} custom-call(s32[3]{0:T(128)S(1)} %pad_add_fusion.refs_0_, bf16[192,896]{1,0:T(8,128)(2,1)S(1)} %behind_rows_1.1.refs_4_.refs_1_, bf16[192,896]{1,0:T(8,128)(2,1)S(1)} %collective-permute-done.6.refs_2_, bf16[2,1024,1792]{2,1,0:T(8,128)(2,1)S(1)} %bitcast.29, ...), custom_call_target="tpu_custom_call" | custom-call | flops 10400000000 | bytes 1024 | tf_op jit(solution)/shard_map/behind_near_1/pallas_call | solution.py:38
  70.7 2.6 %ahead_near_1.1.refs_2_.refs_0_ = bf16[2,192,512]{2,1,0:T(8,128)(2,1)S(1)} custom-call(s32[3]{0:T(128)S(1)} %pad_add_fusion.refs_0_, bf16[192,896]{1,0:T(8,128)(2,1)S(1)} %ahead_rows_1.1.refs_4_.refs_1_, bf16[192,896]{1,0:T(8,128)(2,1)S(1)} %collective-permute-done.4.refs_2_, bf16[2,1024,1792]{2,1,0:T(8,128)(2,1)S(1)} %bitcast.30, ...), custom_call_target="tpu_custom_call" | custom-call | flops 10400000000 | bytes 1024 | tf_op jit(solution)/shard_map/ahead_near_1/pallas_call | solution.py:38
  74.3 4.3 %collective-permute-start.19 = (bf16[1,192,512]{2,1,0:T(8,128)(2,1)S(1)}, bf16[1,192,512]{2,1,0:T(8,128)(2,1)S(1)}, u32[]{:S(2)}, u32[]{:S(2)}) collective-permute-start(bf16[1,192,512]{2,1,0:T(8,128)(2,1)S(1)} %grad_outer_2.1.refs_1_), channel_id=1, source_target_pairs={{0,2},{1,3},{2,0},{3,1},{4,6},{5,7},{6,4},{7,5},{8,10},{9,11},{10,... | collective-permute-start | bytes 589832 | tf_op jit(solution)/shard_map/ppermute | solution.py:227
  79.4 4.8 %collective-permute-done.19.refs_3_ = bf16[1,192,512]{2,1,0:T(8,128)(2,1)S(1)} collective-permute-done((bf16[1,192,512]{2,1,0:T(8,128)(2,1)S(1)}, bf16[1,192,512]{2,1,0:T(8,128)(2,1)S(1)}, u32[]{:S(2)}, u32[]{:S(2)}) %collective-permute-start.19) | collective-permute-done | bytes 196640 | tf_op jit(solution)/shard_map/ppermute | solution.py:227
  88.0 5.7 %collective-permute-start.23 = (bf16[2,192,512]{2,1,0:T(8,128)(2,1)S(1)}, bf16[2,192,512]{2,1,0:T(8,128)(2,1)S(1)}, u32[]{:S(2)}, u32[]{:S(2)}) collective-permute-start(bf16[2,192,512]{2,1,0:T(8,128)(2,1)S(1)} %behind_back_1.1.refs_1_), channel_id=1, source_target_pairs={{0,2},{1,3},{2,0},{3,1},{4,6},{5,7},{6,4},{7,5},{8,10},{9,11},{10,... | collective-permute-start | bytes 1179656 | tf_op jit(solution)/shard_map/ppermute | solution.py:227
  94.6 6.1 %collective-permute-done.23.refs_0_.refs_4_ = bf16[2,192,512]{2,1,0:T(8,128)(2,1)S(1)} collective-permute-done((bf16[2,192,512]{2,1,0:T(8,128)(2,1)S(1)}, bf16[2,192,512]{2,1,0:T(8,128)(2,1)S(1)}, u32[]{:S(2)}, u32[]{:S(2)}) %collective-permute-start.23) | collective-permute-done | bytes 393248 | tf_op jit(solution)/shard_map/ppermute | solution.py:227
  102.0 4.9 %collective-permute-start.24 = (bf16[1,192,512]{2,1,0:T(8,128)(2,1)S(1)}, bf16[1,192,512]{2,1,0:T(8,128)(2,1)S(1)}, u32[]{:S(2)}, u32[]{:S(2)}) collective-permute-start(bf16[1,192,512]{2,1,0:T(8,128)(2,1)S(1)} %ahead_back_1.1.refs_6_), channel_id=1, source_target_pairs={{0,2},{1,3},{2,0},{3,1},{4,6},{5,7},{6,4},{7,5},{8,10},{9,11},{10,... | collective-permute-start | bytes 589832 | tf_op jit(solution)/shard_map/ppermute | solution.py:227
  106.9 3.2 %behind_out_0.1 = (bf16[192,896]{1,0:T(8,128)(2,1)S(1)}, bf16[192,896]{1,0:T(8,128)(2,1)S(1)}) custom-call(s32[3]{0:T(128)S(1)} %pad_add_fusion.refs_0_, bf16[2,192,512]{2,1,0:T(8,128)(2,1)S(1)} %behind_act_0.1.refs_1_.refs_4_, bf16[2,192,512]{2,1,0:T(8,128)(2,1)S(1)} %behind_first_0.1.refs_5_.refs_2_, ...), custom_call_target="tpu_custom_call" | custom-call | flops 20000000000 | bytes 1024 | tf_op jit(solution)/shard_map/behind_out_0/pallas_call | solution.py:38
  117.4 4.3 %collective-permute-start.28 = (bf16[1,192,512]{2,1,0:T(8,128)(2,1)S(1)}, bf16[1,192,512]{2,1,0:T(8,128)(2,1)S(1)}, u32[]{:S(2)}, u32[]{:S(2)}) collective-permute-start(bf16[1,192,512]{2,1,0:T(8,128)(2,1)S(1)} %ahead_back_2.1.refs_2_), channel_id=1, source_target_pairs={{0,2},{1,3},{2,0},{3,1},{4,6},{5,7},{6,4},{7,5},{8,10},{9,11},{10,... | collective-permute-start | bytes 589832 | tf_op jit(solution)/shard_map/ppermute | solution.py:227
  121.9 10.7 %collective-permute-start.34 = (bf16[192,896]{1,0:T(8,128)(2,1)S(1)}, bf16[192,896]{1,0:T(8,128)(2,1)S(1)}, u32[]{:S(2)}, u32[]{:S(2)}) collective-permute-start(bf16[192,896]{1,0:T(8,128)(2,1)S(1)} %behind_shares.1.refs_6_), channel_id=1, source_target_pairs={{8,0},{9,1},{10,2},{11,3},{12,4},{13,5},{14,6},{15,7},{16,8},{17,9... | collective-permute-start | bytes 1032200 | tf_op jit(solution)/shard_map/ppermute | solution.py:245
  132.5 3.2 %behind_out_1.1 = (bf16[192,896]{1,0:T(8,128)(2,1)S(1)}, bf16[192,896]{1,0:T(8,128)(2,1)S(1)}) custom-call(s32[3]{0:T(128)S(1)} %pad_add_fusion.refs_0_, bf16[2,192,512]{2,1,0:T(8,128)(2,1)S(1)} %behind_act_1.1.refs_4_.refs_1_, bf16[2,192,512]{2,1,0:T(8,128)(2,1)S(1)} %behind_first_1.1.refs_3_.refs_2_, ...), custom_call_target="tpu_custom_call" | custom-call | flops 20000000000 | bytes 1024 | tf_op jit(solution)/shard_map/behind_out_1/pallas_call | solution.py:38
  142.2 4.1 %collective-permute-start.32 = (bf16[192,896]{1,0:T(8,128)(2,1)S(1)}, bf16[192,896]{1,0:T(8,128)(2,1)S(1)}, u32[]{:S(2)}, u32[]{:S(2)}) collective-permute-start(bf16[192,896]{1,0:T(8,128)(2,1)S(1)} %get-tuple-element.15.refs_2_), channel_id=1, source_target_pairs={{0,9},{1,8},{2,11},{3,10},{4,13},{5,12},{6,15},{7,14},{8,17},{9,16... | collective-permute-start | bytes 1032200 | tf_op jit(solution)/shard_map/ppermute | solution.py:245
  154.3 3.7 %collective-permute-done.33.refs_2_ = bf16[192,896]{1,0:T(8,128)(2,1)S(1)} collective-permute-done((bf16[192,896]{1,0:T(8,128)(2,1)S(1)}, bf16[192,896]{1,0:T(8,128)(2,1)S(1)}, u32[]{:S(2)}, u32[]{:S(2)}) %collective-permute-start.33) | collective-permute-done | bytes 344096 | tf_op jit(solution)/shard_map/ppermute | solution.py:245
  (132 shorter events, 62.1 us)
Async XLA Ops:
  3.9 17.1 %collective-permute-start = (bf16[192,896]{1,0:T(8,128)(2,1)S(1)}, bf16[192,896]{1,0:T(8,128)(2,1)S(1)}, u32[]{:S(2)}, u32[]{:S(2)}) collective-permute-start(bf16[192,896]{1,0:T(8,128)(2,1)S(1)} %ahead_rows_0.1.refs_1_), channel_id=1, source_target_pairs={{0,1},{1,0},{2,3},{3,2},{4,5},{5,4},{6,7},{7,6},{8,9},{9,8},{10,11... | collective-permute-start | bytes 1032200 | tf_op jit(solution)/shard_map/ppermute | solution.py:236
  5.0 22.0 %collective-permute-start.3 = (bf16[192,896]{1,0:T(8,128)(2,1)S(1)}, bf16[192,896]{1,0:T(8,128)(2,1)S(1)}, u32[]{:S(2)}, u32[]{:S(2)}) collective-permute-start(bf16[192,896]{1,0:T(8,128)(2,1)S(1)} %grad_rows_0.1.refs_4_.refs_1_), channel_id=1, source_target_pairs={{0,1},{1,0},{2,3},{3,2},{4,5},{5,4},{6,7},{7,6},{8,9},{9,8},{10,11... | collective-permute-start | bytes 1032200 | tf_op jit(solution)/shard_map/ppermute | solution.py:236
  18.5 11.5 %collective-permute-start.2 = (bf16[2,192,512]{2,1,0:T(8,128)(2,1)S(1)}, bf16[2,192,512]{2,1,0:T(8,128)(2,1)S(1)}, u32[]{:S(2)}, u32[]{:S(2)}) collective-permute-start(bf16[2,192,512]{2,1,0:T(8,128)(2,1)S(1)} %behind_far_0.1.refs_1_.refs_0_), channel_id=1, source_target_pairs={{0,2},{1,3},{2,0},{3,1},{4,6},{5,7},{6,4},{7,5},{8,10},{9,11},{10,... | collective-permute-start | bytes 1179656 | tf_op jit(solution)/shard_map/ppermute | solution.py:227
  19.8 14.0 %collective-permute-start.6 = (bf16[192,896]{1,0:T(8,128)(2,1)S(1)}, bf16[192,896]{1,0:T(8,128)(2,1)S(1)}, u32[]{:S(2)}, u32[]{:S(2)}) collective-permute-start(bf16[192,896]{1,0:T(8,128)(2,1)S(1)} %behind_rows_1.1.refs_4_.refs_1_), channel_id=1, source_target_pairs={{0,1},{1,0},{2,3},{3,2},{4,5},{5,4},{6,7},{7,6},{8,9},{9,8},{10,11... | collective-permute-start | bytes 1032200 | tf_op jit(solution)/shard_map/ppermute | solution.py:236
  26.8 15.8 %collective-permute-start.5 = (bf16[2,192,512]{2,1,0:T(8,128)(2,1)S(1)}, bf16[2,192,512]{2,1,0:T(8,128)(2,1)S(1)}, u32[]{:S(2)}, u32[]{:S(2)}) collective-permute-start(bf16[2,192,512]{2,1,0:T(8,128)(2,1)S(1)} %ahead_far_0.1.refs_4_.refs_0_), channel_id=1, source_target_pairs={{0,2},{1,3},{2,0},{3,1},{4,6},{5,7},{6,4},{7,5},{8,10},{9,11},{10,... | collective-permute-start | bytes 1179656 | tf_op jit(solution)/shard_map/ppermute | solution.py:227
  28.6 15.7 %collective-permute-start.9 = (bf16[1,192,512]{2,1,0:T(8,128)(2,1)S(1)}, bf16[1,192,512]{2,1,0:T(8,128)(2,1)S(1)}, u32[]{:S(2)}, u32[]{:S(2)}) collective-permute-start(bf16[1,192,512]{2,1,0:T(8,128)(2,1)S(1)} %grad_far_0.1.refs_2_.refs_0_), channel_id=1, source_target_pairs={{0,2},{1,3},{2,0},{3,1},{4,6},{5,7},{6,4},{7,5},{8,10},{9,11},{10,... | collective-permute-start | bytes 589832 | tf_op jit(solution)/shard_map/ppermute | solution.py:227
  30.9 26.4 %collective-permute-start.4 = (bf16[192,896]{1,0:T(8,128)(2,1)S(1)}, bf16[192,896]{1,0:T(8,128)(2,1)S(1)}, u32[]{:S(2)}, u32[]{:S(2)}) collective-permute-start(bf16[192,896]{1,0:T(8,128)(2,1)S(1)} %ahead_rows_1.1.refs_4_.refs_1_), channel_id=1, source_target_pairs={{0,1},{1,0},{2,3},{3,2},{4,5},{5,4},{6,7},{7,6},{8,9},{9,8},{10,11... | collective-permute-start | bytes 1032200 | tf_op jit(solution)/shard_map/ppermute | solution.py:236
  40.6 10.8 %collective-permute-start.11 = (bf16[2,192,512]{2,1,0:T(8,128)(2,1)S(1)}, bf16[2,192,512]{2,1,0:T(8,128)(2,1)S(1)}, u32[]{:S(2)}, u32[]{:S(2)}) collective-permute-start(bf16[2,192,512]{2,1,0:T(8,128)(2,1)S(1)} %behind_outer_1.1.refs_2_), channel_id=1, source_target_pairs={{0,2},{1,3},{2,0},{3,1},{4,6},{5,7},{6,4},{7,5},{8,10},{9,11},{10,... | collective-permute-start | bytes 1179656 | tf_op jit(solution)/shard_map/ppermute | solution.py:227
  42.6 19.9 %collective-permute-start.12 = (bf16[2,192,512]{2,1,0:T(8,128)(2,1)S(1)}, bf16[2,192,512]{2,1,0:T(8,128)(2,1)S(1)}, u32[]{:S(2)}, u32[]{:S(2)}) collective-permute-start(bf16[2,192,512]{2,1,0:T(8,128)(2,1)S(1)} %ahead_middle_0.1.refs_1_), channel_id=1, source_target_pairs={{0,0},{1,1},{2,4},{3,5},{4,2},{5,3},{6,6},{7,7},{8,8},{9,9},{10,12... | collective-permute-start | bytes 1179656 | tf_op jit(solution)/shard_map/ppermute | solution.py:227
  51.5 14.7 %collective-permute-start.15 = (bf16[2,192,512]{2,1,0:T(8,128)(2,1)S(1)}, bf16[2,192,512]{2,1,0:T(8,128)(2,1)S(1)}, u32[]{:S(2)}, u32[]{:S(2)}) collective-permute-start(bf16[2,192,512]{2,1,0:T(8,128)(2,1)S(1)} %behind_middle_1.1.refs_4_), channel_id=1, source_target_pairs={{0,0},{1,1},{2,4},{3,5},{4,2},{5,3},{6,6},{7,7},{8,8},{9,9},{10,12... | collective-permute-start | bytes 1179656 | tf_op jit(solution)/shard_map/ppermute | solution.py:227
  52.8 13.1 %collective-permute-start.14 = (bf16[1,192,512]{2,1,0:T(8,128)(2,1)S(1)}, bf16[1,192,512]{2,1,0:T(8,128)(2,1)S(1)}, u32[]{:S(2)}, u32[]{:S(2)}) collective-permute-start(bf16[1,192,512]{2,1,0:T(8,128)(2,1)S(1)} %grad_outer_1.1.refs_4_), channel_id=1, source_target_pairs={{0,2},{1,3},{2,0},{3,1},{4,6},{5,7},{6,4},{7,5},{8,10},{9,11},{10,... | collective-permute-start | bytes 589832 | tf_op jit(solution)/shard_map/ppermute | solution.py:227
  66.9 11.8 %collective-permute-start.17 = (bf16[2,192,512]{2,1,0:T(8,128)(2,1)S(1)}, bf16[2,192,512]{2,1,0:T(8,128)(2,1)S(1)}, u32[]{:S(2)}, u32[]{:S(2)}) collective-permute-start(bf16[2,192,512]{2,1,0:T(8,128)(2,1)S(1)} %behind_outer_2.1.refs_2_), channel_id=1, source_target_pairs={{0,2},{1,3},{2,0},{3,1},{4,6},{5,7},{6,4},{7,5},{8,10},{9,11},{10,... | collective-permute-start | bytes 1179656 | tf_op jit(solution)/shard_map/ppermute | solution.py:227
  73.4 11.0 %collective-permute-start.16 = (bf16[2,192,512]{2,1,0:T(8,128)(2,1)S(1)}, bf16[2,192,512]{2,1,0:T(8,128)(2,1)S(1)}, u32[]{:S(2)}, u32[]{:S(2)}) collective-permute-start(bf16[2,192,512]{2,1,0:T(8,128)(2,1)S(1)} %ahead_middle_1.1.refs_2_), channel_id=1, source_target_pairs={{0,0},{1,1},{2,4},{3,5},{4,2},{5,3},{6,6},{7,7},{8,8},{9,9},{10,12... | collective-permute-start | bytes 1179656 | tf_op jit(solution)/shard_map/ppermute | solution.py:227
  88.0 12.7 %collective-permute-start.23 = (bf16[2,192,512]{2,1,0:T(8,128)(2,1)S(1)}, bf16[2,192,512]{2,1,0:T(8,128)(2,1)S(1)}, u32[]{:S(2)}, u32[]{:S(2)}) collective-permute-start(bf16[2,192,512]{2,1,0:T(8,128)(2,1)S(1)} %behind_back_1.1.refs_1_), channel_id=1, source_target_pairs={{0,2},{1,3},{2,0},{3,1},{4,6},{5,7},{6,4},{7,5},{8,10},{9,11},{10,... | collective-permute-start | bytes 1179656 | tf_op jit(solution)/shard_map/ppermute | solution.py:227
  100.7 10.8 %collective-permute-start.25 = (bf16[2,192,512]{2,1,0:T(8,128)(2,1)S(1)}, bf16[2,192,512]{2,1,0:T(8,128)(2,1)S(1)}, u32[]{:S(2)}, u32[]{:S(2)}) collective-permute-start(bf16[2,192,512]{2,1,0:T(8,128)(2,1)S(1)} %behind_first_1.1.refs_3_.refs_2_), channel_id=1, source_target_pairs={{0,0},{1,1},{2,4},{3,5},{4,2},{5,3},{6,6},{7,7},{8,8},{9,9},{10,12... | collective-permute-start | bytes 1179656 | tf_op jit(solution)/shard_map/ppermute | solution.py:227
  102.0 11.1 %collective-permute-start.24 = (bf16[1,192,512]{2,1,0:T(8,128)(2,1)S(1)}, bf16[1,192,512]{2,1,0:T(8,128)(2,1)S(1)}, u32[]{:S(2)}, u32[]{:S(2)}) collective-permute-start(bf16[1,192,512]{2,1,0:T(8,128)(2,1)S(1)} %ahead_back_1.1.refs_6_), channel_id=1, source_target_pairs={{0,2},{1,3},{2,0},{3,1},{4,6},{5,7},{6,4},{7,5},{8,10},{9,11},{10,... | collective-permute-start | bytes 589832 | tf_op jit(solution)/shard_map/ppermute | solution.py:227
  110.2 11.6 %collective-permute-start.30 = (bf16[192,896]{1,0:T(8,128)(2,1)S(1)}, bf16[192,896]{1,0:T(8,128)(2,1)S(1)}, u32[]{:S(2)}, u32[]{:S(2)}) collective-permute-start(bf16[192,896]{1,0:T(8,128)(2,1)S(1)} %get-tuple-element.10.refs_1_), channel_id=1, source_target_pairs={{0,1},{1,0},{2,3},{3,2},{4,5},{5,4},{6,7},{7,6},{8,9},{9,8},{10,11... | collective-permute-start | bytes 1032200 | tf_op jit(solution)/shard_map/ppermute | solution.py:236
  111.5 21.0 %collective-permute-start.29 = (bf16[2,192,512]{2,1,0:T(8,128)(2,1)S(1)}, bf16[2,192,512]{2,1,0:T(8,128)(2,1)S(1)}, u32[]{:S(2)}, u32[]{:S(2)}) collective-permute-start(bf16[2,192,512]{2,1,0:T(8,128)(2,1)S(1)} %behind_back_2.1.refs_1_), channel_id=1, source_target_pairs={{0,2},{1,3},{2,0},{3,1},{4,6},{5,7},{6,4},{7,5},{8,10},{9,11},{10,... | collective-permute-start | bytes 1179656 | tf_op jit(solution)/shard_map/ppermute | solution.py:227
  116.1 30.2 %collective-permute-start.26 = (bf16[192,896]{1,0:T(8,128)(2,1)S(1)}, bf16[192,896]{1,0:T(8,128)(2,1)S(1)}, u32[]{:S(2)}, u32[]{:S(2)}) collective-permute-start(bf16[192,896]{1,0:T(8,128)(2,1)S(1)} %get-tuple-element.12.refs_1_), channel_id=1, source_target_pairs={{0,1},{1,0},{2,3},{3,2},{4,5},{5,4},{6,7},{7,6},{8,9},{9,8},{10,11... | collective-permute-start | bytes 1032200 | tf_op jit(solution)/shard_map/ppermute | solution.py:236
  117.4 22.7 %collective-permute-start.28 = (bf16[1,192,512]{2,1,0:T(8,128)(2,1)S(1)}, bf16[1,192,512]{2,1,0:T(8,128)(2,1)S(1)}, u32[]{:S(2)}, u32[]{:S(2)}) collective-permute-start(bf16[1,192,512]{2,1,0:T(8,128)(2,1)S(1)} %ahead_back_2.1.refs_2_), channel_id=1, source_target_pairs={{0,2},{1,3},{2,0},{3,1},{4,6},{5,7},{6,4},{7,5},{8,10},{9,11},{10,... | collective-permute-start | bytes 589832 | tf_op jit(solution)/shard_map/ppermute | solution.py:227
  121.9 27.1 %collective-permute-start.34 = (bf16[192,896]{1,0:T(8,128)(2,1)S(1)}, bf16[192,896]{1,0:T(8,128)(2,1)S(1)}, u32[]{:S(2)}, u32[]{:S(2)}) collective-permute-start(bf16[192,896]{1,0:T(8,128)(2,1)S(1)} %behind_shares.1.refs_6_), channel_id=1, source_target_pairs={{8,0},{9,1},{10,2},{11,3},{12,4},{13,5},{14,6},{15,7},{16,8},{17,9... | collective-permute-start | bytes 1032200 | tf_op jit(solution)/shard_map/ppermute | solution.py:245
  135.8 15.2 %collective-permute-start.35 = (bf16[192,896]{1,0:T(8,128)(2,1)S(1)}, bf16[192,896]{1,0:T(8,128)(2,1)S(1)}, u32[]{:S(2)}, u32[]{:S(2)}) collective-permute-start(bf16[192,896]{1,0:T(8,128)(2,1)S(1)} %get-tuple-element.14.refs_7_), channel_id=1, source_target_pairs={{8,1},{9,0},{10,3},{11,2},{12,5},{13,4},{14,7},{15,6},{16,9},{17,8... | collective-permute-start | bytes 1032200 | tf_op jit(solution)/shard_map/ppermute | solution.py:245
  138.2 12.8 %collective-permute-start.36 = (bf16[192,896]{1,0:T(8,128)(2,1)S(1)}, bf16[192,896]{1,0:T(8,128)(2,1)S(1)}, u32[]{:S(2)}, u32[]{:S(2)}) collective-permute-start(bf16[192,896]{1,0:T(8,128)(2,1)S(1)} %get-tuple-element.17), channel_id=1, source_target_pairs={{8,0},{9,1},{10,2},{11,3},{12,4},{13,5},{14,6},{15,7},{16,8},{17,9... | collective-permute-start | bytes 1032200 | tf_op jit(solution)/shard_map/ppermute | solution.py:245
  142.2 12.0 %collective-permute-start.32 = (bf16[192,896]{1,0:T(8,128)(2,1)S(1)}, bf16[192,896]{1,0:T(8,128)(2,1)S(1)}, u32[]{:S(2)}, u32[]{:S(2)}) collective-permute-start(bf16[192,896]{1,0:T(8,128)(2,1)S(1)} %get-tuple-element.15.refs_2_), channel_id=1, source_target_pairs={{0,9},{1,8},{2,11},{3,10},{4,13},{5,12},{6,15},{7,14},{8,17},{9,16... | collective-permute-start | bytes 1032200 | tf_op jit(solution)/shard_map/ppermute | solution.py:245
  (25 other events, 139.8 us)

commit v11 on v10

--- a/solution.py
+++ b/solution.py
@@ -25,7 +25,12 @@
     return pl.BlockSpec(array.shape, functools.partial(lambda n, *_: (0,) * n, array.ndim))
 
 
-def call(kernel, micros, operands, after, out_shape, scalars=(), grid=(1,), in_specs=None, out_specs=None, scratch=(), limit=16, name=None):
+def row_piece(array, c):
+    parts, slots, half = array.shape
+    return pl.BlockSpec((parts, slots // PIECES, half), lambda *_: (0, c, 0))
+
+
+def call(kernel, micros, operands, after, out_shape, scalars=(), grid=(1,), in_specs=None, out_specs=None, scratch=(), limit=24, name=None):
     count, unread = len(scalars) + len(operands), len(after)
 
     def run(*refs):
@@ -59,13 +64,18 @@
     out[...] = value[: out.shape[0]]
 
 
-def first_kernel(width, where, own, partner, tile, out, joined):
+def first_kernel(width, where, *refs):
+    rows, (tile, out, joined) = refs[:-3], refs[-3:]
+
     @pl.when((pl.program_id(0) == 0) & (pl.program_id(1) == 0))
     def _():
         at = pl.multiple_of(where[1] * width, 128)
         other = pl.multiple_of((1 - where[1]) * width, 128)
-        joined[:, pl.ds(at, width)] = own[...]
-        joined[:, pl.ds(other, width)] = partner[...]
+        slots = rows[0].shape[0]
+        for piece in range(len(rows) // 2):
+            here = pl.ds(piece * slots, slots)
+            joined[here, pl.ds(at, width)] = rows[2 * piece][...]
+            joined[here, pl.ds(other, width)] = rows[2 * piece + 1][...]
 
     out[0] = lax.dot_general(
         joined[...], tile[0], (((1,), (1,)), ((), ())), preferred_element_type=F32
@@ -74,6 +84,7 @@
 
 def first_product(name, where, far, rows, weights, after):
     slots, width = rows[0].shape
+    slots *= len(rows) // 2
     parts, units, features = weights.shape
     half = units // 2
     tile = min(256, half)
@@ -223,11 +234,17 @@
     scales = jnp.where(live, route_scores[0], 0.0)[:, :, None]
 
     def between(value, to):
-        pairs = [(q * 2 + f, to[q] * 2 + f) for q in range(DBLOCKS) for f in range(2)]
+        pairs = [(q * 2 + f, to[q] * 2 + f) for q in range(DBLOCKS) for f in range(2) if to[q] is not None]
         return lax.ppermute(value, "expert", pairs)
 
     def outer(value):
         return between(value, (1, 0, 3, 2))
+
+    def inward(value):
+        return between(value, (1, None, None, 2))
+
+    def outward(value):
+        return between(value, (None, 0, 3, None))
 
     def middle(value):
         return between(value, (0, 2, 1, 3))
@@ -247,8 +264,20 @@
     recent = []
 
     def kernel_call(name, kernel, micros, operands, shape, scalars=()):
+        specs, arrays = [], []
+        for operand in operands:
+            array, c = operand if isinstance(operand, tuple) else (operand, None)
+            arrays.append(array)
+            specs.append(whole(array) if c is None else row_piece(array, c))
         made = call(
-            kernel, micros, operands, list(recent), jax.ShapeDtypeStruct(shape, BF16), scalars, name=name
+            kernel,
+            micros,
+            arrays,
+            list(recent),
+            jax.ShapeDtypeStruct(shape, BF16),
+            scalars,
+            in_specs=specs,
+            name=name,
         )
         recent[:] = [made]
         return made
@@ -259,7 +288,7 @@
             self.rows, self.weights = rows, weights
             self.spreads = spreads
             self.pairs, self.far, self.near, self.act = {}, {}, {}, {}
-            self.out, self.mid, self.one, self.back = {}, {}, {}, {}
+            self.out, self.mid, self.one, self.back, self.third = {}, {}, {}, {}, {}
 
         def fetch(self, c):
             size, width = height // PIECES, self.rows.shape[1]
@@ -275,35 +304,38 @@
             recent[:] = [rows]
             self.pairs[c] = rows, swapped(rows)
 
-        def product(self, c, far):
-            made = first_product(f"{self.name}_{'far' if far else 'near'}_{c}", where, far, self.pairs[c], self.weights, list(recent))
+        def far_product(self, c):
+            name = f"{self.name}_far_{c}"
+            made = first_product(name, where, True, self.pairs[c], self.weights, list(recent))
             recent[:] = [made]
-            (self.far if far else self.near)[c] = made
-
-        def products(self, c):
-            self.product(c, True)
-            self.product(c, False)
-
-        def outer_sum(self, c):
-            if c == 0:
-                value = self.far[0]
-            else:
-                mine = self.near[c - 1]
-                first = self.far[c] if c < PIECES else self.act.get(0)
-                if first is None:
-                    value = kernel_call(
-                        f"{self.name}_outer_{c}", sum_kernel, SMALL, (mine, self.mid[c - 1]), mine.shape
-                    )
-                else:
-                    value = kernel_call(
-                        f"{self.name}_outer_{c}",
-                        end_or_sum_kernel,
-                        SMALL,
-                        (first, mine, self.mid[c - 1]),
-                        mine.shape,
-                        (where,),
-                    )
-            self.out[c] = outer(value)
+            self.far[c] = made
+
+        def near_products(self):
+            rows = [row for c in range(PIECES) for row in self.pairs[c]]
+            made = first_product(f"{self.name}_near", where, False, rows, self.weights, list(recent))
+            recent[:] = [made]
+            self.near = {c: (made, c) for c in range(PIECES)}
+
+        def near_sum(self, c):
+            operands = (self.near[c], self.mid[c])
+            return kernel_call(f"{self.name}_third_{c}", sum_kernel, SMALL, operands, self.far[c].shape)
+
+        def first_hop(self, c):
+            self.out[c] = outer(self.far[c]) if c == 0 else inward(self.far[c])
+
+        def third_hop(self, c):
+            self.third[c] = outward(self.near_sum(c))
+
+        def merged_hop(self, c, first):
+            operands = (first, self.near[c - 1], self.mid[c - 1])
+            shape = self.far[0].shape
+            self.out[c] = outer(
+                kernel_call(f"{self.name}_outer_{c}", end_or_sum_kernel, SMALL, operands, shape, (where,))
+            )
+            self.third[c - 1] = self.out[c]
+
+        def last_third_hop(self):
+            self.third[PIECES - 1] = outer(self.near_sum(PIECES - 1))
 
         def middle_sum(self, c):
             mine = self.far[c]
@@ -351,13 +383,13 @@
 
     def activate_ahead(c):
         near = ahead.near[c]
-        operands = (near, ahead.out[c + 1])
-        ahead.act[c] = kernel_call(f"ahead_act_{c}", ahead_act_kernel, ACT, operands, (1, *near.shape[1:]))
+        operands = (near, ahead.third[c])
+        ahead.act[c] = kernel_call(f"ahead_act_{c}", ahead_act_kernel, ACT, operands, (1, *ahead.far[c].shape[1:]))
 
     def activate_behind(c):
         near = behind.near[c]
-        operands = (near, behind.out[c + 1], grad.near[c], grad.out[c + 1], cut(scales[1], c))
-        behind.act[c] = kernel_call(f"behind_act_{c}", behind_act_kernel, ACT, operands, near.shape)
+        operands = (near, behind.third[c], grad.near[c], grad.third[c], cut(scales[1], c))
+        behind.act[c] = kernel_call(f"behind_act_{c}", behind_act_kernel, ACT, operands, behind.far[c].shape)
 
     def output(chain, c):
         forward = chain is ahead
@@ -390,42 +422,41 @@
         shape = (height, operands[0].shape[1])
         return kernel_call(f"{chain.name}_result", result_kernel, SMALL, operands, shape)[None]
 
-    for chain in (behind, ahead, grad):
+    for chain in (behind, grad, ahead):
         chain.fetch(0)
-    behind.product(0, True)
-    behind.outer_sum(0)
+    behind.far_product(0)
+    behind.first_hop(0)
     behind.fetch(1)
-    ahead.product(0, True)
-    ahead.outer_sum(0)
-    grad.product(0, True)
-    grad.outer_sum(0)
+    grad.far_product(0)
+    grad.first_hop(0)
+    ahead.far_product(0)
+    ahead.first_hop(0)
     behind.middle_sum(0)
+    grad.fetch(1)
+    behind.far_product(1)
+    behind.first_hop(1)
+    grad.middle_sum(0)
+    behind.near_products()
+    behind.third_hop(0)
     ahead.fetch(1)
-    behind.product(1, True)
-    behind.product(0, False)
-    behind.outer_sum(1)
+    behind.middle_sum(1)
+    grad.far_product(1)
+    grad.near_products()
+    grad.merged_hop(1, grad.far[1])
     ahead.middle_sum(0)
-    grad.fetch(1)
-    grad.middle_sum(0)
-    grad.product(0, False)
-    grad.product(1, True)
-    behind.middle_sum(1)
-    grad.outer_sum(1)
-    ahead.product(1, True)
-    ahead.product(0, False)
-    ahead.outer_sum(1)
-    behind.product(1, False)
+    ahead.far_product(1)
+    ahead.first_hop(1)
+    ahead.near_products()
+    ahead.third_hop(0)
     activate_behind(0)
-    behind.outer_sum(2)
+    behind.merged_hop(2, behind.act[0])
     grad.middle_sum(1)
-    grad.product(1, False)
-    ahead.product(1, False)
     ahead.middle_sum(1)
     activate_ahead(0)
-    grad.outer_sum(2)
     behind.middle_pass(0)
+    grad.last_third_hop()
+    ahead.merged_hop(2, ahead.act[0])
     activate_behind(1)
-    ahead.outer_sum(2)
     behind.outer_pass(1)
     ahead.middle_pass(0)
     activate_ahead(1)

time: 161 us -> 165 us (1.025)
  waiting for transfers between devices: 27.3 us -> 37.9 us
  Pallas kernels: 47.9 us -> 41.4 us
  local copies, waits for them, and re-layouts: 8.95 us -> 5.87 us
  starting transfers between devices: 74.5 us -> 77.2 us
    ppermute x23 -> x25, waiting for transfers between devices: 10.9 us -> 22.8 us  [between(): return lax.ppermute(value, 'expert', pairs)]
    ppermute x23 -> x25, starting transfers between devices: 41.1 us -> 47.9 us  [between(): return lax.ppermute(value, 'expert', pairs)]
    pallas_call x50 -> x47, Pallas kernels: 47.9 us -> 41.4 us  [call(): pl.pallas_call(run, compiler_params=pltpu.CompilerParams(vmem_limit_bytes...]
    unnamed x24 -> x22, local copies, waits for them, and re-layouts: 8.39 us -> 5.31 us
    ppermute x6, starting transfers between devices: 23.6 us -> 20.5 us  [to_section(): return lax.ppermute(value, ('section', 'expert'), pairs)]
  transfers between devices with their start and end apart: 37 -> 39, of which waited for: 7 -> 10; matrix products, arithmetic and copies ran while one was open for 0% -> 0% of each run, Pallas kernels for 29% -> 25%
where the time goes in v11:
time: 165 us; the launch traced here: 164 us
  starting transfers between devices  77.2 us (47%)
  Pallas kernels  41.4 us (25%)
  waiting for transfers between devices  37.9 us (23%)
  local copies, waits for them, and re-layouts  5.87 us (4%)
    ppermute x25, starting transfers between devices, between(): return lax.ppermute(value, 'expert', pairs)  47.9 us
    pallas_call x47, Pallas kernels, call(): pl.pallas_call(run, compiler_params=pltpu.CompilerParams(vmem_limit_bytes...  41.4 us
    ppermute x25, waiting for transfers between devices, between(): return lax.ppermute(value, 'expert', pairs)  22.8 us
    ppermute x6, starting transfers between devices, to_section(): return lax.ppermute(value, ('section', 'expert'), pairs)  20.5 us
    ppermute x8, waiting for transfers between devices, swapped(): return lax.ppermute(value, 'expert', [(i, i ^ 1) for i in range(devices)])  9.08 us
    ppermute x8, starting transfers between devices, swapped(): return lax.ppermute(value, 'expert', [(i, i ^ 1) for i in range(devices)])  8.79 us
    ppermute x6, waiting for transfers between devices, to_section(): return lax.ppermute(value, ('section', 'expert'), pairs)  5.98 us
    unnamed x22, local copies, waits for them, and re-layouts  5.31 us
  transfers between devices with their start and end apart: 39, of which 10 were waited for; matrix products, arithmetic and copies ran while one was open for 0% of the time, Pallas kernels for 25%

profile of v11, /device:TPU:1, one launch (start us, length us, event | category | flops | bytes accessed | tf_op | source)
XLA Modules:
  0.0 163.8 jit_solution(4258068612690031281)
XLA Ops:
  6.9 4.9 %collective-permute-done.1.refs_2_ = bf16[192,896]{1,0:T(8,128)(2,1)} collective-permute-done((bf16[192,896]{1,0:T(8,128)(2,1)S(1)}, bf16[192,896]{1,0:T(8,128)(2,1)}, u32[]{:S(2)}, u32[]{:S(2)}) %collective-permute-start.1) | collective-permute-done | bytes 344096 | tf_op jit(solution)/shard_map/ppermute | solution.py:253
  11.8 3.1 %copy-done = bf16[1,1,2,1024,1792]{4,3,2,1,0:T(8,128)(2,1)S(1)} copy-done((bf16[1,1,2,1024,1792]{4,3,2,1,0:T(8,128)(2,1)S(1)}, bf16[1,1,2,1024,1792]{4,3,2,1,0:T(8,128)(2,1)}, u32[]{:S(2)}) %copy-start) | copy-done | bytes 7340056
  14.9 3.9 %behind_far_0.1.refs_1_.refs_0_ = bf16[2,192,512]{2,1,0:T(8,128)(2,1)S(1)} custom-call(s32[3]{0:T(128)S(1)} %pad_add_fusion.refs_0_, bf16[192,896]{1,0:T(8,128)(2,1)S(1)} %behind_rows_0.1.refs_1_, bf16[192,896]{1,0:T(8,128)(2,1)} %collective-permute-done.1.refs_2_, bf16[2,1024,1792]{2,1,0:T(8,128)(2,1)S(1)} %bitcast.21, ...), custom_call_target="tpu_custom_call" | custom-call | flops 10400000000 | bytes 1024 | tf_op jit(solution)/shard_map/behind_far_0/pallas_call | solution.py:43
  23.7 2.8 %collective-permute-done.refs_2_ = bf16[192,896]{1,0:T(8,128)(2,1)S(1)} collective-permute-done((bf16[192,896]{1,0:T(8,128)(2,1)S(1)}, bf16[192,896]{1,0:T(8,128)(2,1)S(1)}, u32[]{:S(2)}, u32[]{:S(2)}) %collective-permute-start) | collective-permute-done | bytes 344096 | tf_op jit(solution)/shard_map/ppermute | solution.py:253
  26.4 2.6 %ahead_far_0.1.refs_2_.refs_0_ = bf16[2,192,512]{2,1,0:T(8,128)(2,1)S(1)} custom-call(s32[3]{0:T(128)S(1)} %pad_add_fusion.refs_0_, bf16[192,896]{1,0:T(8,128)(2,1)S(1)} %ahead_rows_0.1.refs_4_.refs_1_, bf16[192,896]{1,0:T(8,128)(2,1)S(1)} %collective-permute-done.refs_2_, bf16[2,1024,1792]{2,1,0:T(8,128)(2,1)S(1)} %bitcast.24, ...), custom_call_target="tpu_custom_call" | custom-call | flops 10400000000 | bytes 1024 | tf_op jit(solution)/shard_map/ahead_far_0/pallas_call | solution.py:43
  33.8 2.6 %behind_far_1.1.refs_2_.refs_0_ = bf16[2,192,512]{2,1,0:T(8,128)(2,1)S(1)} custom-call(s32[3]{0:T(128)S(1)} %pad_add_fusion.refs_0_, bf16[192,896]{1,0:T(8,128)(2,1)S(1)} %behind_rows_1.1.refs_4_.refs_1_.refs_3_, bf16[192,896]{1,0:T(8,128)(2,1)S(1)} %collective-permute-done.2.refs_2_.refs_4_, bf16[2,1024,1792]{2,1,0:T(8,128)(2,1)S(1)} %bitcast.25, ...), custom_call_target="tpu_custom_call" | custom-call | flops 10400000000 | bytes 1024 | tf_op jit(solution)/shard_map/behind_far_1/pallas_call | solution.py:43
  36.4 4.4 %collective-permute-start.10 = (bf16[2,192,512]{2,1,0:T(8,128)(2,1)S(1)}, bf16[2,192,512]{2,1,0:T(8,128)(2,1)S(1)}, u32[]{:S(2)}, u32[]{:S(2)}) collective-permute-start(bf16[2,192,512]{2,1,0:T(8,128)(2,1)S(1)} %behind_far_1.1.refs_2_.refs_0_), channel_id=1, source_target_pairs={{0,2},{1,3},{6,4},{7,5},{8,10},{9,11},{14,12},{15,13},{16,18},{17,... | collective-permute-start | bytes 1179656 | tf_op jit(solution)/shard_map/ppermute | solution.py:238
  41.6 4.0 %behind_near.1.refs_0_.refs_2_ = bf16[2,384,512]{2,1,0:T(8,128)(2,1)S(1)} custom-call(s32[3]{0:T(128)S(1)} %pad_add_fusion.refs_0_, bf16[192,896]{1,0:T(8,128)(2,1)S(1)} %behind_rows_0.1.refs_1_, bf16[192,896]{1,0:T(8,128)(2,1)} %collective-permute-done.1.refs_2_, bf16[192,896]{1,0:T(8,128)(2,1)S(1)} %behind_rows_1.1.refs_4_.refs_1_.refs_3_, ...), custom_call_target="tpu_custom_call" | custom-call | flops 10400000000 | bytes 1024 | tf_op jit(solution)/shard_map/behind_near/pallas_call | solution.py:43
  53.4 6.0 %collective-permute-start.15 = (bf16[1,192,512]{2,1,0:T(8,128)(2,1)S(1)}, bf16[1,192,512]{2,1,0:T(8,128)(2,1)S(1)}, u32[]{:S(2)}, u32[]{:S(2)}) collective-permute-start(bf16[1,192,512]{2,1,0:T(8,128)(2,1)S(1)} %grad_outer_1.1.refs_2_), channel_id=1, source_target_pairs={{0,2},{1,3},{2,0},{3,1},{4,6},{5,7},{6,4},{7,5},{8,10},{9,11},{10,... | collective-permute-start | bytes 589832 | tf_op jit(solution)/shard_map/ppermute | solution.py:238
  60.2 2.6 %ahead_far_1.1.refs_6_.refs_0_ = bf16[2,192,512]{2,1,0:T(8,128)(2,1)S(1)} custom-call(s32[3]{0:T(128)S(1)} %pad_add_fusion.refs_0_, bf16[192,896]{1,0:T(8,128)(2,1)S(1)} %ahead_rows_1.1.refs_2_.refs_1_.refs_3_, bf16[192,896]{1,0:T(8,128)(2,1)S(1)} %collective-permute-done.7.refs_2_.refs_4_, bf16[2,1024,1792]{2,1,0:T(8,128)(2,1)S(1)} %bitcast.27, ...), custom_call_target="tpu_custom_call" | custom-call | flops 10400000000 | bytes 1024 | tf_op jit(solution)/shard_map/ahead_far_1/pallas_call | solution.py:43
  62.8 3.2 %collective-permute-start.14 = (bf16[2,192,512]{2,1,0:T(8,128)(2,1)S(1)}, bf16[2,192,512]{2,1,0:T(8,128)(2,1)S(1)}, u32[]{:S(2)}, u32[]{:S(2)}) collective-permute-start(bf16[2,192,512]{2,1,0:T(8,128)(2,1)S(1)} %ahead_far_1.1.refs_6_.refs_0_), channel_id=1, source_target_pairs={{0,2},{1,3},{6,4},{7,5},{8,10},{9,11},{14,12},{15,13},{16,18},{17,... | collective-permute-start | bytes 1179656 | tf_op jit(solution)/shard_map/ppermute | solution.py:238
  66.0 3.0 %ahead_near.1.refs_0_.refs_2_ = bf16[2,384,512]{2,1,0:T(8,128)(2,1)S(1)} custom-call(s32[3]{0:T(128)S(1)} %pad_add_fusion.refs_0_, bf16[192,896]{1,0:T(8,128)(2,1)S(1)} %ahead_rows_0.1.refs_4_.refs_1_, bf16[192,896]{1,0:T(8,128)(2,1)S(1)} %collective-permute-done.refs_2_, bf16[192,896]{1,0:T(8,128)(2,1)S(1)} %ahead_rows_1.1.refs_2_.refs_1_.refs_3_, ...), custom_call_target="tpu_custom_call" | custom-call | flops 10400000000 | bytes 1024 | tf_op jit(solution)/shard_map/ahead_near/pallas_call | solution.py:43
  75.2 3.3 %collective-permute-done.13.refs_1_ = bf16[2,192,512]{2,1,0:T(8,128)(2,1)S(1)} collective-permute-done((bf16[2,192,512]{2,1,0:T(8,128)(2,1)S(1)}, bf16[2,192,512]{2,1,0:T(8,128)(2,1)S(1)}, u32[]{:S(2)}, u32[]{:S(2)}) %collective-permute-start.13) | collective-permute-done | bytes 393248 | tf_op jit(solution)/shard_map/ppermute | solution.py:238
  78.6 8.3 %collective-permute-done.20.refs_0_.refs_1_ = bf16[2,192,512]{2,1,0:T(8,128)(2,1)S(1)} collective-permute-done((bf16[2,192,512]{2,1,0:T(8,128)(2,1)S(1)}, bf16[2,192,512]{2,1,0:T(8,128)(2,1)S(1)}, u32[]{:S(2)}, u32[]{:S(2)}) %collective-permute-start.20) | collective-permute-done | bytes 393248 | tf_op jit(solution)/shard_map/ppermute | solution.py:238
  93.9 4.5 %collective-permute-start.25 = (bf16[2,192,512]{2,1,0:T(8,128)(2,1)S(1)}, bf16[2,192,512]{2,1,0:T(8,128)(2,1)S(1)}, u32[]{:S(2)}, u32[]{:S(2)}) collective-permute-start(bf16[2,192,512]{2,1,0:T(8,128)(2,1)S(1)} %behind_back_1.1.refs_1_), channel_id=1, source_target_pairs={{0,2},{1,3},{2,0},{3,1},{4,6},{5,7},{6,4},{7,5},{8,10},{9,11},{10,... | collective-permute-start | bytes 1179656 | tf_op jit(solution)/shard_map/ppermute | solution.py:238
  100.3 7.8 %collective-permute-done.25.refs_0_.refs_4_ = bf16[2,192,512]{2,1,0:T(8,128)(2,1)S(1)} collective-permute-done((bf16[2,192,512]{2,1,0:T(8,128)(2,1)S(1)}, bf16[2,192,512]{2,1,0:T(8,128)(2,1)S(1)}, u32[]{:S(2)}, u32[]{:S(2)}) %collective-permute-start.25) | collective-permute-done | bytes 393248 | tf_op jit(solution)/shard_map/ppermute | solution.py:238
  109.4 2.8 %collective-permute-start.26 = (bf16[1,192,512]{2,1,0:T(8,128)(2,1)S(1)}, bf16[1,192,512]{2,1,0:T(8,128)(2,1)S(1)}, u32[]{:S(2)}, u32[]{:S(2)}) collective-permute-start(bf16[1,192,512]{2,1,0:T(8,128)(2,1)S(1)} %ahead_back_1.1.refs_6_), channel_id=1, source_target_pairs={{0,2},{1,3},{2,0},{3,1},{4,6},{5,7},{6,4},{7,5},{8,10},{9,11},{10,... | collective-permute-start | bytes 589832 | tf_op jit(solution)/shard_map/ppermute | solution.py:238
  112.2 3.2 %behind_out_0.1 = (bf16[192,896]{1,0:T(8,128)(2,1)S(1)}, bf16[192,896]{1,0:T(8,128)(2,1)S(1)}) custom-call(s32[3]{0:T(128)S(1)} %pad_add_fusion.refs_0_, bf16[2,192,512]{2,1,0:T(8,128)(2,1)S(1)} %behind_act_0.1.refs_1_.refs_4_, bf16[2,192,512]{2,1,0:T(8,128)(2,1)S(1)} %behind_first_0.1.refs_2_, ...), custom_call_target="tpu_custom_call" | custom-call | flops 20000000000 | bytes 1024 | tf_op jit(solution)/shard_map/behind_out_0/pallas_call | solution.py:43
  115.5 6.3 %collective-permute-start.31 = (bf16[2,192,512]{2,1,0:T(8,128)(2,1)S(1)}, bf16[2,192,512]{2,1,0:T(8,128)(2,1)S(1)}, u32[]{:S(2)}, u32[]{:S(2)}) collective-permute-start(bf16[2,192,512]{2,1,0:T(8,128)(2,1)S(1)} %behind_back_2.1.refs_1_), channel_id=1, source_target_pairs={{0,2},{1,3},{2,0},{3,1},{4,6},{5,7},{6,4},{7,5},{8,10},{9,11},{10,... | collective-permute-start | bytes 1179656 | tf_op jit(solution)/shard_map/ppermute | solution.py:238
  125.2 3.5 %collective-permute-start.30 = (bf16[1,192,512]{2,1,0:T(8,128)(2,1)S(1)}, bf16[1,192,512]{2,1,0:T(8,128)(2,1)S(1)}, u32[]{:S(2)}, u32[]{:S(2)}) collective-permute-start(bf16[1,192,512]{2,1,0:T(8,128)(2,1)S(1)} %ahead_back_2.1.refs_2_), channel_id=1, source_target_pairs={{0,2},{1,3},{2,0},{3,1},{4,6},{5,7},{6,4},{7,5},{8,10},{9,11},{10,... | collective-permute-start | bytes 589832 | tf_op jit(solution)/shard_map/ppermute | solution.py:238
  128.8 7.6 %collective-permute-start.36 = (bf16[192,896]{1,0:T(8,128)(2,1)S(1)}, bf16[192,896]{1,0:T(8,128)(2,1)S(1)}, u32[]{:S(2)}, u32[]{:S(2)}) collective-permute-start(bf16[192,896]{1,0:T(8,128)(2,1)S(1)} %behind_shares.1.refs_6_), channel_id=1, source_target_pairs={{8,0},{9,1},{10,2},{11,3},{12,4},{13,5},{14,6},{15,7},{16,8},{17,9... | collective-permute-start | bytes 1032200 | tf_op jit(solution)/shard_map/ppermute | solution.py:262
  136.4 3.2 %behind_out_1.1 = (bf16[192,896]{1,0:T(8,128)(2,1)S(1)}, bf16[192,896]{1,0:T(8,128)(2,1)S(1)}) custom-call(s32[3]{0:T(128)S(1)} %pad_add_fusion.refs_0_, bf16[2,192,512]{2,1,0:T(8,128)(2,1)S(1)} %behind_act_1.1.refs_1_.refs_3_, bf16[2,192,512]{2,1,0:T(8,128)(2,1)S(1)} %behind_first_1.1.refs_3_.refs_2_, ...), custom_call_target="tpu_custom_call" | custom-call | flops 20000000000 | bytes 1024 | tf_op jit(solution)/shard_map/behind_out_1/pallas_call | solution.py:43
  145.7 4.5 %collective-permute-start.34 = (bf16[192,896]{1,0:T(8,128)(2,1)S(1)}, bf16[192,896]{1,0:T(8,128)(2,1)S(1)}, u32[]{:S(2)}, u32[]{:S(2)}) collective-permute-start(bf16[192,896]{1,0:T(8,128)(2,1)S(1)} %get-tuple-element.15.refs_2_), channel_id=1, source_target_pairs={{0,9},{1,8},{2,11},{3,10},{4,13},{5,12},{6,15},{7,14},{8,17},{9,16... | collective-permute-start | bytes 1032200 | tf_op jit(solution)/shard_map/ppermute | solution.py:262
  158.1 3.7 %collective-permute-done.35.refs_2_ = bf16[192,896]{1,0:T(8,128)(2,1)S(1)} collective-permute-done((bf16[192,896]{1,0:T(8,128)(2,1)S(1)}, bf16[192,896]{1,0:T(8,128)(2,1)S(1)}, u32[]{:S(2)}, u32[]{:S(2)}) %collective-permute-start.35) | collective-permute-done | bytes 344096 | tf_op jit(solution)/shard_map/ppermute | solution.py:262
  (131 shorter events, 60.7 us)
Async XLA Ops:
  3.9 17.4 %collective-permute-start.3 = (bf16[192,896]{1,0:T(8,128)(2,1)S(1)}, bf16[192,896]{1,0:T(8,128)(2,1)S(1)}, u32[]{:S(2)}, u32[]{:S(2)}) collective-permute-start(bf16[192,896]{1,0:T(8,128)(2,1)S(1)} %grad_rows_0.1.refs_1_), channel_id=1, source_target_pairs={{0,1},{1,0},{2,3},{3,2},{4,5},{5,4},{6,7},{7,6},{8,9},{9,8},{10,11... | collective-permute-start | bytes 1032200 | tf_op jit(solution)/shard_map/ppermute | solution.py:253
  5.0 21.4 %collective-permute-start = (bf16[192,896]{1,0:T(8,128)(2,1)S(1)}, bf16[192,896]{1,0:T(8,128)(2,1)S(1)}, u32[]{:S(2)}, u32[]{:S(2)}) collective-permute-start(bf16[192,896]{1,0:T(8,128)(2,1)S(1)} %ahead_rows_0.1.refs_4_.refs_1_), channel_id=1, source_target_pairs={{0,1},{1,0},{2,3},{3,2},{4,5},{5,4},{6,7},{7,6},{8,9},{9,8},{10,11... | collective-permute-start | bytes 1032200 | tf_op jit(solution)/shard_map/ppermute | solution.py:253
  20.1 13.7 %collective-permute-start.2 = (bf16[192,896]{1,0:T(8,128)(2,1)S(1)}, bf16[192,896]{1,0:T(8,128)(2,1)S(1)}, u32[]{:S(2)}, u32[]{:S(2)}) collective-permute-start(bf16[192,896]{1,0:T(8,128)(2,1)S(1)} %behind_rows_1.1.refs_4_.refs_1_.refs_3_), channel_id=1, source_target_pairs={{0,1},{1,0},{2,3},{3,2},{4,5},{5,4},{6,7},{7,6},{8,9},{9,8},{10,11... | collective-permute-start | bytes 1032200 | tf_op jit(solution)/shard_map/ppermute | solution.py:253
  23.0 17.8 %collective-permute-start.4 = (bf16[1,192,512]{2,1,0:T(8,128)(2,1)S(1)}, bf16[1,192,512]{2,1,0:T(8,128)(2,1)S(1)}, u32[]{:S(2)}, u32[]{:S(2)}) collective-permute-start(bf16[1,192,512]{2,1,0:T(8,128)(2,1)S(1)} %grad_far_0.1.refs_4_.refs_0_), channel_id=1, source_target_pairs={{0,2},{1,3},{2,0},{3,1},{4,6},{5,7},{6,4},{7,5},{8,10},{9,11},{10,... | collective-permute-start | bytes 589832 | tf_op jit(solution)/shard_map/ppermute | solution.py:238
  29.1 30.3 %collective-permute-start.8 = (bf16[2,192,512]{2,1,0:T(8,128)(2,1)S(1)}, bf16[2,192,512]{2,1,0:T(8,128)(2,1)S(1)}, u32[]{:S(2)}, u32[]{:S(2)}) collective-permute-start(bf16[2,192,512]{2,1,0:T(8,128)(2,1)S(1)} %ahead_far_0.1.refs_2_.refs_0_), channel_id=1, source_target_pairs={{0,2},{1,3},{2,0},{3,1},{4,6},{5,7},{6,4},{7,5},{8,10},{9,11},{10,... | collective-permute-start | bytes 1179656 | tf_op jit(solution)/shard_map/ppermute | solution.py:238
  30.4 15.2 %collective-permute-start.6 = (bf16[2,192,512]{2,1,0:T(8,128)(2,1)S(1)}, bf16[2,192,512]{2,1,0:T(8,128)(2,1)S(1)}, u32[]{:S(2)}, u32[]{:S(2)}) collective-permute-start(bf16[2,192,512]{2,1,0:T(8,128)(2,1)S(1)} %behind_middle_0.1.refs_1_), channel_id=1, source_target_pairs={{0,0},{1,1},{2,4},{3,5},{4,2},{5,3},{6,6},{7,7},{8,8},{9,9},{10,12... | collective-permute-start | bytes 1179656 | tf_op jit(solution)/shard_map/ppermute | solution.py:238
  31.1 17.5 %collective-permute-start.9 = (bf16[192,896]{1,0:T(8,128)(2,1)S(1)}, bf16[192,896]{1,0:T(8,128)(2,1)S(1)}, u32[]{:S(2)}, u32[]{:S(2)}) collective-permute-start(bf16[192,896]{1,0:T(8,128)(2,1)S(1)} %grad_rows_1.1.refs_4_.refs_1_.refs_3_), channel_id=1, source_target_pairs={{0,1},{1,0},{2,3},{3,2},{4,5},{5,4},{6,7},{7,6},{8,9},{9,8},{10,11... | collective-permute-start | bytes 1032200 | tf_op jit(solution)/shard_map/ppermute | solution.py:253
  45.7 24.8 %collective-permute-start.16 = (bf16[2,192,512]{2,1,0:T(8,128)(2,1)S(1)}, bf16[2,192,512]{2,1,0:T(8,128)(2,1)S(1)}, u32[]{:S(2)}, u32[]{:S(2)}) collective-permute-start(bf16[2,192,512]{2,1,0:T(8,128)(2,1)S(1)} %behind_third_0.1.refs_1_), channel_id=1, source_target_pairs={{2,0},{3,1},{4,6},{5,7},{10,8},{11,9},{12,14},{13,15},{18,16},{19,... | collective-permute-start | bytes 1179656 | tf_op jit(solution)/shard_map/ppermute | solution.py:238
  47.0 13.2 %collective-permute-start.7 = (bf16[192,896]{1,0:T(8,128)(2,1)S(1)}, bf16[192,896]{1,0:T(8,128)(2,1)S(1)}, u32[]{:S(2)}, u32[]{:S(2)}) collective-permute-start(bf16[192,896]{1,0:T(8,128)(2,1)S(1)} %ahead_rows_1.1.refs_2_.refs_1_.refs_3_), channel_id=1, source_target_pairs={{0,1},{1,0},{2,3},{3,2},{4,5},{5,4},{6,7},{7,6},{8,9},{9,8},{10,11... | collective-permute-start | bytes 1032200 | tf_op jit(solution)/shard_map/ppermute | solution.py:253
  48.7 22.1 %collective-permute-start.17 = (bf16[2,192,512]{2,1,0:T(8,128)(2,1)S(1)}, bf16[2,192,512]{2,1,0:T(8,128)(2,1)S(1)}, u32[]{:S(2)}, u32[]{:S(2)}) collective-permute-start(bf16[2,192,512]{2,1,0:T(8,128)(2,1)S(1)} %behind_middle_1.1.refs_4_), channel_id=1, source_target_pairs={{0,0},{1,1},{2,4},{3,5},{4,2},{5,3},{6,6},{7,7},{8,8},{9,9},{10,12... | collective-permute-start | bytes 1179656 | tf_op jit(solution)/shard_map/ppermute | solution.py:238
  53.4 17.1 %collective-permute-start.15 = (bf16[1,192,512]{2,1,0:T(8,128)(2,1)S(1)}, bf16[1,192,512]{2,1,0:T(8,128)(2,1)S(1)}, u32[]{:S(2)}, u32[]{:S(2)}) collective-permute-start(bf16[1,192,512]{2,1,0:T(8,128)(2,1)S(1)} %grad_outer_1.1.refs_2_), channel_id=1, source_target_pairs={{0,2},{1,3},{2,0},{3,1},{4,6},{5,7},{6,4},{7,5},{8,10},{9,11},{10,... | collective-permute-start | bytes 589832 | tf_op jit(solution)/shard_map/ppermute | solution.py:238
  71.4 15.5 %collective-permute-start.20 = (bf16[2,192,512]{2,1,0:T(8,128)(2,1)S(1)}, bf16[2,192,512]{2,1,0:T(8,128)(2,1)S(1)}, u32[]{:S(2)}, u32[]{:S(2)}) collective-permute-start(bf16[2,192,512]{2,1,0:T(8,128)(2,1)S(1)} %behind_outer_2.1.refs_2_), channel_id=1, source_target_pairs={{0,2},{1,3},{2,0},{3,1},{4,6},{5,7},{6,4},{7,5},{8,10},{9,11},{10,... | collective-permute-start | bytes 1179656 | tf_op jit(solution)/shard_map/ppermute | solution.py:238
  73.7 13.9 %collective-permute-start.19 = (bf16[1,192,512]{2,1,0:T(8,128)(2,1)S(1)}, bf16[1,192,512]{2,1,0:T(8,128)(2,1)S(1)}, u32[]{:S(2)}, u32[]{:S(2)}) collective-permute-start(bf16[1,192,512]{2,1,0:T(8,128)(2,1)S(1)} %grad_middle_1.1.refs_2_), channel_id=1, source_target_pairs={{0,0},{1,1},{2,4},{3,5},{4,2},{5,3},{6,6},{7,7},{8,8},{9,9},{10,12... | collective-permute-start | bytes 589832 | tf_op jit(solution)/shard_map/ppermute | solution.py:238
  74.5 15.4 %collective-permute-start.18 = (bf16[2,192,512]{2,1,0:T(8,128)(2,1)S(1)}, bf16[2,192,512]{2,1,0:T(8,128)(2,1)S(1)}, u32[]{:S(2)}, u32[]{:S(2)}) collective-permute-start(bf16[2,192,512]{2,1,0:T(8,128)(2,1)S(1)} %ahead_middle_1.1.refs_2_), channel_id=1, source_target_pairs={{0,0},{1,1},{2,4},{3,5},{4,2},{5,3},{6,6},{7,7},{8,8},{9,9},{10,12... | collective-permute-start | bytes 1179656 | tf_op jit(solution)/shard_map/ppermute | solution.py:238
  93.9 14.2 %collective-permute-start.25 = (bf16[2,192,512]{2,1,0:T(8,128)(2,1)S(1)}, bf16[2,192,512]{2,1,0:T(8,128)(2,1)S(1)}, u32[]{:S(2)}, u32[]{:S(2)}) collective-permute-start(bf16[2,192,512]{2,1,0:T(8,128)(2,1)S(1)} %behind_back_1.1.refs_1_), channel_id=1, source_target_pairs={{0,2},{1,3},{2,0},{3,1},{4,6},{5,7},{6,4},{7,5},{8,10},{9,11},{10,... | collective-permute-start | bytes 1179656 | tf_op jit(solution)/shard_map/ppermute | solution.py:238
  109.4 12.5 %collective-permute-start.26 = (bf16[1,192,512]{2,1,0:T(8,128)(2,1)S(1)}, bf16[1,192,512]{2,1,0:T(8,128)(2,1)S(1)}, u32[]{:S(2)}, u32[]{:S(2)}) collective-permute-start(bf16[1,192,512]{2,1,0:T(8,128)(2,1)S(1)} %ahead_back_1.1.refs_6_), channel_id=1, source_target_pairs={{0,2},{1,3},{2,0},{3,1},{4,6},{5,7},{6,4},{7,5},{8,10},{9,11},{10,... | collective-permute-start | bytes 589832 | tf_op jit(solution)/shard_map/ppermute | solution.py:238
  115.4 13.3 %collective-permute-start.32 = (bf16[192,896]{1,0:T(8,128)(2,1)S(1)}, bf16[192,896]{1,0:T(8,128)(2,1)S(1)}, u32[]{:S(2)}, u32[]{:S(2)}) collective-permute-start(bf16[192,896]{1,0:T(8,128)(2,1)S(1)} %get-tuple-element.10.refs_1_), channel_id=1, source_target_pairs={{0,1},{1,0},{2,3},{3,2},{4,5},{5,4},{6,7},{7,6},{8,9},{9,8},{10,11... | collective-permute-start | bytes 1032200 | tf_op jit(solution)/shard_map/ppermute | solution.py:253
  115.5 20.9 %collective-permute-start.31 = (bf16[2,192,512]{2,1,0:T(8,128)(2,1)S(1)}, bf16[2,192,512]{2,1,0:T(8,128)(2,1)S(1)}, u32[]{:S(2)}, u32[]{:S(2)}) collective-permute-start(bf16[2,192,512]{2,1,0:T(8,128)(2,1)S(1)} %behind_back_2.1.refs_1_), channel_id=1, source_target_pairs={{0,2},{1,3},{2,0},{3,1},{4,6},{5,7},{6,4},{7,5},{8,10},{9,11},{10,... | collective-permute-start | bytes 1179656 | tf_op jit(solution)/shard_map/ppermute | solution.py:238
  124.9 25.3 %collective-permute-start.28 = (bf16[192,896]{1,0:T(8,128)(2,1)S(1)}, bf16[192,896]{1,0:T(8,128)(2,1)S(1)}, u32[]{:S(2)}, u32[]{:S(2)}) collective-permute-start(bf16[192,896]{1,0:T(8,128)(2,1)S(1)} %get-tuple-element.12.refs_1_), channel_id=1, source_target_pairs={{0,1},{1,0},{2,3},{3,2},{4,5},{5,4},{6,7},{7,6},{8,9},{9,8},{10,11... | collective-permute-start | bytes 1032200 | tf_op jit(solution)/shard_map/ppermute | solution.py:253
  125.2 18.4 %collective-permute-start.30 = (bf16[1,192,512]{2,1,0:T(8,128)(2,1)S(1)}, bf16[1,192,512]{2,1,0:T(8,128)(2,1)S(1)}, u32[]{:S(2)}, u32[]{:S(2)}) collective-permute-start(bf16[1,192,512]{2,1,0:T(8,128)(2,1)S(1)} %ahead_back_2.1.refs_2_), channel_id=1, source_target_pairs={{0,2},{1,3},{2,0},{3,1},{4,6},{5,7},{6,4},{7,5},{8,10},{9,11},{10,... | collective-permute-start | bytes 589832 | tf_op jit(solution)/shard_map/ppermute | solution.py:238
  128.8 24.1 %collective-permute-start.36 = (bf16[192,896]{1,0:T(8,128)(2,1)S(1)}, bf16[192,896]{1,0:T(8,128)(2,1)S(1)}, u32[]{:S(2)}, u32[]{:S(2)}) collective-permute-start(bf16[192,896]{1,0:T(8,128)(2,1)S(1)} %behind_shares.1.refs_6_), channel_id=1, source_target_pairs={{8,0},{9,1},{10,2},{11,3},{12,4},{13,5},{14,6},{15,7},{16,8},{17,9... | collective-permute-start | bytes 1032200 | tf_op jit(solution)/shard_map/ppermute | solution.py:262
  139.7 15.2 %collective-permute-start.37 = (bf16[192,896]{1,0:T(8,128)(2,1)S(1)}, bf16[192,896]{1,0:T(8,128)(2,1)S(1)}, u32[]{:S(2)}, u32[]{:S(2)}) collective-permute-start(bf16[192,896]{1,0:T(8,128)(2,1)S(1)} %get-tuple-element.14.refs_7_), channel_id=1, source_target_pairs={{8,1},{9,0},{10,3},{11,2},{12,5},{13,4},{14,7},{15,6},{16,9},{17,8... | collective-permute-start | bytes 1032200 | tf_op jit(solution)/shard_map/ppermute | solution.py:262
  141.6 13.2 %collective-permute-start.38 = (bf16[192,896]{1,0:T(8,128)(2,1)S(1)}, bf16[192,896]{1,0:T(8,128)(2,1)S(1)}, u32[]{:S(2)}, u32[]{:S(2)}) collective-permute-start(bf16[192,896]{1,0:T(8,128)(2,1)S(1)} %get-tuple-element.17), channel_id=1, source_target_pairs={{8,0},{9,1},{10,2},{11,3},{12,4},{13,5},{14,6},{15,7},{16,8},{17,9... | collective-permute-start | bytes 1032200 | tf_op jit(solution)/shard_map/ppermute | solution.py:262
  145.7 12.4 %collective-permute-start.34 = (bf16[192,896]{1,0:T(8,128)(2,1)S(1)}, bf16[192,896]{1,0:T(8,128)(2,1)S(1)}, u32[]{:S(2)}, u32[]{:S(2)}) collective-permute-start(bf16[192,896]{1,0:T(8,128)(2,1)S(1)} %get-tuple-element.15.refs_2_), channel_id=1, source_target_pairs={{0,9},{1,8},{2,11},{3,10},{4,13},{5,12},{6,15},{7,14},{8,17},{9,16... | collective-permute-start | bytes 1032200 | tf_op jit(solution)/shard_map/ppermute | solution.py:262
  (26 other events, 169.5 us)

commit v12 on v11

--- a/solution.py
+++ b/solution.py
@@ -30,8 +30,8 @@
     return pl.BlockSpec((parts, slots // PIECES, half), lambda *_: (0, c, 0))
 
 
-def call(kernel, micros, operands, after, out_shape, scalars=(), grid=(1,), in_specs=None, out_specs=None, scratch=(), limit=24, name=None):
-    count, unread = len(scalars) + len(operands), len(after)
+def call(kernel, micros, operands, after, out_shape, grid=(1,), in_specs=None, out_specs=None, scratch=(), limit=24, name=None):
+    count, unread = len(operands), len(after)
 
     def run(*refs):
         kernel(*refs[:count], *refs[count + unread :])
@@ -46,14 +46,11 @@
         cost_estimate=pl.CostEstimate(flops=int(micros * 1e9), bytes_accessed=1024, transcendentals=0),
         out_shape=out_shape,
         name=name,
-        grid_spec=pltpu.PrefetchScalarGridSpec(
-            num_scalar_prefetch=len(scalars),
-            grid=grid,
-            in_specs=[*in_specs, *[pl.BlockSpec(memory_space=pl.ANY)] * unread],
-            out_specs=out_specs,
-            scratch_shapes=list(scratch),
-        ),
-    )(*scalars, *operands, *after)
+        grid=grid,
+        in_specs=[*in_specs, *[pl.BlockSpec(memory_space=pl.ANY)] * unread],
+        out_specs=out_specs,
+        scratch_shapes=list(scratch),
+    )(*operands, *after)
 
 
 def cut_kernel(rows, out):
@@ -64,46 +61,63 @@
     out[...] = value[: out.shape[0]]
 
 
-def first_kernel(width, where, *refs):
-    rows, (tile, out, joined) = refs[:-3], refs[-3:]
-
-    @pl.when((pl.program_id(0) == 0) & (pl.program_id(1) == 0))
-    def _():
-        at = pl.multiple_of(where[1] * width, 128)
-        other = pl.multiple_of((1 - where[1]) * width, 128)
-        slots = rows[0].shape[0]
-        for piece in range(len(rows) // 2):
-            here = pl.ds(piece * slots, slots)
-            joined[here, pl.ds(at, width)] = rows[2 * piece][...]
-            joined[here, pl.ds(other, width)] = rows[2 * piece + 1][...]
-
-    out[0] = lax.dot_general(
-        joined[...], tile[0], (((1,), (1,)), ((), ())), preferred_element_type=F32
-    ).astype(BF16)
-
-
-def first_product(name, where, far, rows, weights, after):
+def position():
+    own = lax.axis_index("expert")
+    block = own // 2
+    near = jnp.where(block >= DBLOCKS // 2, 1, 0)
+    return near, own % 2, (block == 0) | (block == DBLOCKS - 1)
+
+
+def first_kernel(far, *refs):
+    rows, (weights, out, joined, tiles, sems) = refs[:-5], refs[-5:]
+    near, group, _ = position()
+    side = 1 - near if far else near
+    parts, _, half = out.shape
+    tile = tiles.shape[1]
+    steps = half // tile
+    copies = []
+    for k in range(parts):
+        for j in range(steps):
+            n = k * steps + j
+            at = pl.multiple_of((side * steps + j) * tile, tile)
+            copy = pltpu.make_async_copy(weights.at[k, pl.ds(at, tile)], tiles.at[n], sems.at[n])
+            copy.start()
+            copies.append(copy)
+    slots, width = rows[0].shape
+    at = pl.multiple_of(group * width, 128)
+    other = pl.multiple_of((1 - group) * width, 128)
+    for piece in range(len(rows) // 2):
+        here = pl.ds(piece * slots, slots)
+        joined[here, pl.ds(at, width)] = rows[2 * piece][...]
+        joined[here, pl.ds(other, width)] = rows[2 * piece + 1][...]
+    for k in range(parts):
+        for j in range(steps):
+            n = k * steps + j
+            copies[n].wait()
+            out[k, :, j * tile : (j + 1) * tile] = lax.dot_general(
+                joined[...], tiles[n], (((1,), (1,)), ((), ())), preferred_element_type=F32
+            ).astype(BF16)
+
+
+def first_product(name, far, rows, weights, after):
     slots, width = rows[0].shape
     slots *= len(rows) // 2
     parts, units, features = weights.shape
     half = units // 2
     tile = min(256, half)
     steps = half // tile
-
-    def tile_at(k, j, w):
-        return (k, ((1 - w[0]) if far else w[0]) * steps + j, 0)
-
     return call(
-        functools.partial(first_kernel, width),
+        functools.partial(first_kernel, far),
         FIRST * parts,
         (*rows, weights),
         after,
         jax.ShapeDtypeStruct((parts, slots, half), BF16),
-        scalars=(where,),
-        grid=(parts, steps),
-        in_specs=[*[whole(r) for r in rows], pl.BlockSpec((1, tile, features), tile_at)],
-        out_specs=pl.BlockSpec((1, slots, tile), lambda k, j, w: (k, 0, j)),
-        scratch=[pltpu.VMEM((slots, features), BF16)],
+        in_specs=[*[whole(r) for r in rows], pl.BlockSpec(memory_space=pl.ANY)],
+        scratch=[
+            pltpu.VMEM((slots, features), BF16),
+            pltpu.VMEM((parts * steps, tile, features), BF16),
+            pltpu.SemaphoreType.DMA((parts * steps,)),
+        ],
         name=name,
     )
 
@@ -112,25 +126,29 @@
     out[...] = (mine[...].astype(F32) + arrived[...].astype(F32)).astype(BF16)
 
 
-def end_or_sum_kernel(where, at_end, mine, arrived, out):
-    @pl.when(where[2] == 1)
+def end_or_sum_kernel(at_end, mine, arrived, out):
+    _, _, end = position()
+
+    @pl.when(end)
     def _():
         parts = at_end.shape[0]
         out[:parts] = at_end[...]
         if parts < out.shape[0]:
             out[parts:] = jnp.zeros_like(out[parts:])
 
-    @pl.when(where[2] == 0)
+    @pl.when(jnp.logical_not(end))
     def _():
         out[...] = (mine[...].astype(F32) + arrived[...].astype(F32)).astype(BF16)
 
 
-def end_or_pass_kernel(where, at_end, passed, out):
-    @pl.when(where[2] == 1)
+def end_or_pass_kernel(at_end, passed, out):
+    _, _, end = position()
+
+    @pl.when(end)
     def _():
         out[...] = at_end[...]
 
-    @pl.when(where[2] == 0)
+    @pl.when(jnp.logical_not(end))
     def _():
         out[...] = passed[...]
 
@@ -156,14 +174,15 @@
     out[size:] = (one[...].astype(F32) + two[...].astype(F32)).astype(BF16)
 
 
-def second_kernel(scaled, where, act, one, two, three, *refs):
+def second_kernel(scaled, act, one, two, three, *refs):
     scale, refs = (refs[0], refs[1:]) if scaled else (None, refs)
     weights, give, keep, joined, tiles, sems = refs
+    near_half, group, end = position()
     kinds, _, half = act.shape
     _, _, units, width = tiles.shape
     copies = []
     for own in range(2):
-        at = pl.multiple_of((where[1] if own else 1 - where[1]) * width, 128)
+        at = pl.multiple_of((group if own else 1 - group) * width, 128)
         copy = pltpu.make_async_copy(
             weights.at[:, :, pl.ds(at, width)], tiles.at[own], sems.at[own]
         )
@@ -172,16 +191,16 @@
 
     def place(near, far):
         for kind in range(kinds):
-            at = pl.multiple_of((2 * kind + where[0]) * half, 128)
-            other = pl.multiple_of((2 * kind + 1 - where[0]) * half, 128)
+            at = pl.multiple_of((2 * kind + near_half) * half, 128)
+            other = pl.multiple_of((2 * kind + 1 - near_half) * half, 128)
             joined[:, pl.ds(at, half)] = near[kind]
             joined[:, pl.ds(other, half)] = far[kind]
 
-    @pl.when(where[2] == 1)
+    @pl.when(end)
     def _():
         place(act, three)
 
-    @pl.when(where[2] == 0)
+    @pl.when(jnp.logical_not(end))
     def _():
         place(one, two)
 
@@ -195,7 +214,7 @@
         out[...] = share.astype(BF16)
 
 
-def second_product(name, where, values, scale, weights, after):
+def second_product(name, values, scale, weights, after):
     kinds, units, features = weights.shape
     slots = values[0].shape[1]
     width = features // 2
@@ -207,8 +226,7 @@
         (*operands, weights),
         after,
         (share, share),
-        scalars=(where,),
-        in_specs=[*[whole(v) for v in operands], pl.BlockSpec(memory_space=pltpu.HBM)],
+        in_specs=[*[whole(v) for v in operands], pl.BlockSpec(memory_space=pl.ANY)],
         scratch=[
             pltpu.VMEM((slots, kinds * units), BF16),
             pltpu.VMEM((2, kinds, units, width), BF16),
@@ -222,13 +240,8 @@
     height = ahead_rows.shape[1]
     gates = gate_up[0, 0]
     downs = down_proj[0]
-    own = lax.axis_index("expert")
     sections = lax.axis_size("section")
     devices = 2 * DBLOCKS
-    block, group = own // 2, own % 2
-    near_half = (block >= DBLOCKS // 2).astype(jnp.int32)
-    at_end = ((block == 0) | (block == DBLOCKS - 1)).astype(jnp.int32)
-    where = jnp.stack([near_half, group, at_end])
     slot_ids = jnp.arange(height, dtype=jnp.int32)[None]
     live = slot_ids < route_counts[0][:, None]
     scales = jnp.where(live, route_scores[0], 0.0)[:, :, None]
@@ -263,7 +276,7 @@
 
     recent = []
 
-    def kernel_call(name, kernel, micros, operands, shape, scalars=()):
+    def kernel_call(name, kernel, micros, operands, shape):
         specs, arrays = [], []
         for operand in operands:
             array, c = operand if isinstance(operand, tuple) else (operand, None)
@@ -275,7 +288,6 @@
             arrays,
             list(recent),
             jax.ShapeDtypeStruct(shape, BF16),
-            scalars,
             in_specs=specs,
             name=name,
         )
@@ -306,13 +318,13 @@
 
         def far_product(self, c):
             name = f"{self.name}_far_{c}"
-            made = first_product(name, where, True, self.pairs[c], self.weights, list(recent))
+            made = first_product(name, True, self.pairs[c], self.weights, list(recent))
             recent[:] = [made]
             self.far[c] = made
 
         def near_products(self):
             rows = [row for c in range(PIECES) for row in self.pairs[c]]
-            made = first_product(f"{self.name}_near", where, False, rows, self.weights, list(recent))
+            made = first_product(f"{self.name}_near", False, rows, self.weights, list(recent))
             recent[:] = [made]
             self.near = {c: (made, c) for c in range(PIECES)}
 
@@ -330,7 +342,7 @@
             operands = (first, self.near[c - 1], self.mid[c - 1])
             shape = self.far[0].shape
             self.out[c] = outer(
-                kernel_call(f"{self.name}_outer_{c}", end_or_sum_kernel, SMALL, operands, shape, (where,))
+                kernel_call(f"{self.name}_outer_{c}", end_or_sum_kernel, SMALL, operands, shape)
             )
             self.third[c - 1] = self.out[c]
 
@@ -365,7 +377,6 @@
                     SMALL,
                     (self.act[c], value),
                     value.shape,
-                    (where,),
                 )
             self.back[c] = outer(value)
 
@@ -396,7 +407,7 @@
         scale = cut(scales[0], c) if forward else None
         weights = downs if forward else gates
         give, keep = second_product(
-            f"{chain.name}_out_{c}", where, chain.activated(c), scale, weights, list(recent)
+            f"{chain.name}_out_{c}", chain.activated(c), scale, weights, list(recent)
         )
         recent[:] = [give]
         return give, keep
@@ -433,28 +444,26 @@
     ahead.first_hop(0)
     behind.middle_sum(0)
     grad.fetch(1)
+    grad.middle_sum(0)
     behind.far_product(1)
-    behind.first_hop(1)
-    grad.middle_sum(0)
     behind.near_products()
-    behind.third_hop(0)
+    behind.merged_hop(1, behind.far[1])
     ahead.fetch(1)
-    behind.middle_sum(1)
+    ahead.middle_sum(0)
     grad.far_product(1)
     grad.near_products()
     grad.merged_hop(1, grad.far[1])
-    ahead.middle_sum(0)
     ahead.far_product(1)
-    ahead.first_hop(1)
+    behind.middle_sum(1)
     ahead.near_products()
-    ahead.third_hop(0)
+    ahead.merged_hop(1, ahead.far[1])
+    grad.middle_sum(1)
     activate_behind(0)
     behind.merged_hop(2, behind.act[0])
-    grad.middle_sum(1)
     ahead.middle_sum(1)
     activate_ahead(0)
+    grad.last_third_hop()
     behind.middle_pass(0)
-    grad.last_third_hop()
     ahead.merged_hop(2, ahead.act[0])
     activate_behind(1)
     behind.outer_pass(1)

time: 165 us -> 161 us (0.976)
  waiting for transfers between devices: 37.9 us -> 23.9 us
  starting transfers between devices: 77.2 us -> 84.6 us
  Pallas kernels: 41.4 us -> 44.2 us
    ppermute x25 -> x23, waiting for transfers between devices: 22.8 us -> 11.1 us  [between(): return lax.ppermute(value, 'expert', pairs)]
    ppermute x6, starting transfers between devices: 20.5 us -> 28.2 us  [to_section(): return lax.ppermute(value, ('section', 'expert'), pairs)]
    pallas_call x47, Pallas kernels: 41.4 us -> 44.2 us  [call(): pl.pallas_call(run, compiler_params=pltpu.CompilerParams(vmem_limit_bytes...]
    ppermute x8, waiting for transfers between devices: 9.08 us -> 6.74 us  [swapped(): return lax.ppermute(value, 'expert', [(i, i ^ 1) for i in range(devices)])]
    ppermute x25 -> x23, starting transfers between devices: 47.9 us -> 46.6 us  [between(): return lax.ppermute(value, 'expert', pairs)]
  transfers between devices with their start and end apart: 39 -> 37, of which waited for: 10 -> 9; matrix products, arithmetic and copies ran while one was open for 0% -> 0% of each run, Pallas kernels for 25% -> 27%
where the time goes in v12:
time: 161 us; the launch traced here: 160 us
  starting transfers between devices  84.6 us (53%)
  Pallas kernels  44.2 us (27%)
  waiting for transfers between devices  23.9 us (15%)
  local copies, waits for them, and re-layouts  5.87 us (4%)
    ppermute x23, starting transfers between devices, between(): return lax.ppermute(value, 'expert', pairs)  46.6 us
    pallas_call x47, Pallas kernels, call(): pl.pallas_call(run, compiler_params=pltpu.CompilerParams(vmem_limit_bytes...  44.2 us
    ppermute x6, starting transfers between devices, to_section(): return lax.ppermute(value, ('section', 'expert'), pairs)  28.2 us
    ppermute x23, waiting for transfers between devices, between(): return lax.ppermute(value, 'expert', pairs)  11.1 us
    ppermute x8, starting transfers between devices, swapped(): return lax.ppermute(value, 'expert', [(i, i ^ 1) for i in range(devices)])  9.77 us
    ppermute x8, waiting for transfers between devices, swapped(): return lax.ppermute(value, 'expert', [(i, i ^ 1) for i in range(devices)])  6.74 us
    ppermute x6, waiting for transfers between devices, to_section(): return lax.ppermute(value, ('section', 'expert'), pairs)  6.04 us
    unnamed x22, local copies, waits for them, and re-layouts  5.31 us
  transfers between devices with their start and end apart: 37, of which 9 were waited for; matrix products, arithmetic and copies ran while one was open for 0% of the time, Pallas kernels for 27%

profile of v12, /device:TPU:1, one launch (start us, length us, event | category | flops | bytes accessed | tf_op | source)
XLA Modules:
  0.0 159.9 jit_solution(7723640662249499204)
XLA Ops:
  6.8 5.0 %collective-permute-done.1.refs_1_ = bf16[192,896]{1,0:T(8,128)(2,1)} collective-permute-done((bf16[192,896]{1,0:T(8,128)(2,1)S(1)}, bf16[192,896]{1,0:T(8,128)(2,1)}, u32[]{:S(2)}, u32[]{:S(2)}) %collective-permute-start.1) | collective-permute-done | bytes 344096 | tf_op jit(solution)/shard_map/ppermute | solution.py:266
  11.8 3.1 %copy-done = bf16[1,1,2,1024,1792]{4,3,2,1,0:T(8,128)(2,1)S(1)} copy-done((bf16[1,1,2,1024,1792]{4,3,2,1,0:T(8,128)(2,1)S(1)}, bf16[1,1,2,1024,1792]{4,3,2,1,0:T(8,128)(2,1)}, u32[]{:S(2)}) %copy-start) | copy-done | bytes 7340056
  14.9 4.7 %behind_far_0.1.refs_1_.refs_0_ = bf16[2,192,512]{2,1,0:T(8,128)(2,1)S(1)} custom-call(bf16[192,896]{1,0:T(8,128)(2,1)S(1)} %behind_rows_0.1.refs_1_.refs_0_, bf16[192,896]{1,0:T(8,128)(2,1)} %collective-permute-done.1.refs_1_, bf16[2,1024,1792]{2,1,0:T(8,128)(2,1)S(1)} %bitcast.18, bf16[192,896]{1,0:T(8,128)(2,1)S(1)} %ahead_rows_0.1.refs_3_.refs_0_), custom_call_target="tpu_custom_call" | custom-call | flops 10400000000 | bytes 1024 | tf_op jit(solution)/shard_map/behind_far_0/pallas_call | solution.py:43
  26.4 3.6 %ahead_far_0.1.refs_2_.refs_0_ = bf16[2,192,512]{2,1,0:T(8,128)(2,1)S(1)} custom-call(bf16[192,896]{1,0:T(8,128)(2,1)S(1)} %ahead_rows_0.1.refs_3_.refs_0_, bf16[192,896]{1,0:T(8,128)(2,1)S(1)} %collective-permute-done.refs_1_, bf16[2,1024,1792]{2,1,0:T(8,128)(2,1)S(1)} %bitcast.21, bf16[1,192,512]{2,1,0:T(8,128)(2,1)S(1)} %grad_far_0.1.refs_3_.refs_0_), custom_call_target="tpu_custom_call" | custom-call | flops 10400000000 | bytes 1024 | tf_op jit(solution)/shard_map/ahead_far_0/pallas_call | solution.py:43
  34.2 3.6 %behind_far_1.1.refs_5_.refs_0_ = bf16[2,192,512]{2,1,0:T(8,128)(2,1)S(1)} custom-call(bf16[192,896]{1,0:T(8,128)(2,1)S(1)} %behind_rows_1.1.refs_3_.refs_0_.refs_2_, bf16[192,896]{1,0:T(8,128)(2,1)S(1)} %collective-permute-done.2.refs_1_.refs_3_, bf16[2,1024,1792]{2,1,0:T(8,128)(2,1)S(1)} %bitcast.22, bf16[1,192,512]{2,1,0:T(8,128)(2,1)S(1)} %grad_middle_0.1.refs_3_), custom_call_target="tpu_custom_call" | custom-call | flops 10400000000 | bytes 1024 | tf_op jit(solution)/shard_map/behind_far_1/pallas_call | solution.py:43
  37.8 5.6 %behind_near.1.refs_1_.refs_3_.refs_0_ = bf16[2,384,512]{2,1,0:T(8,128)(2,1)S(1)} custom-call(bf16[192,896]{1,0:T(8,128)(2,1)S(1)} %behind_rows_0.1.refs_1_.refs_0_, bf16[192,896]{1,0:T(8,128)(2,1)} %collective-permute-done.1.refs_1_, bf16[192,896]{1,0:T(8,128)(2,1)S(1)} %behind_rows_1.1.refs_3_.refs_0_.refs_2_, ...), custom_call_target="tpu_custom_call" | custom-call | flops 10400000000 | bytes 1024 | tf_op jit(solution)/shard_map/behind_near/pallas_call | solution.py:43
  43.4 5.2 %collective-permute-start.8 = (bf16[2,192,512]{2,1,0:T(8,128)(2,1)S(1)}, bf16[2,192,512]{2,1,0:T(8,128)(2,1)S(1)}, u32[]{:S(2)}, u32[]{:S(2)}) collective-permute-start(bf16[2,192,512]{2,1,0:T(8,128)(2,1)S(1)} %behind_outer_1.1.refs_1_), channel_id=1, source_target_pairs={{0,2},{1,3},{2,0},{3,1},{4,6},{5,7},{6,4},{7,5},{8,10},{9,11},{10,... | collective-permute-start | bytes 1179656 | tf_op jit(solution)/shard_map/ppermute | solution.py:251
  54.0 2.8 %collective-permute-start.14 = (bf16[1,192,512]{2,1,0:T(8,128)(2,1)S(1)}, bf16[1,192,512]{2,1,0:T(8,128)(2,1)S(1)}, u32[]{:S(2)}, u32[]{:S(2)}) collective-permute-start(bf16[1,192,512]{2,1,0:T(8,128)(2,1)S(1)} %grad_outer_1.1.refs_3_), channel_id=1, source_target_pairs={{0,2},{1,3},{2,0},{3,1},{4,6},{5,7},{6,4},{7,5},{8,10},{9,11},{10,... | collective-permute-start | bytes 589832 | tf_op jit(solution)/shard_map/ppermute | solution.py:251
  56.8 3.6 %ahead_far_1.1.refs_2_.refs_0_ = bf16[2,192,512]{2,1,0:T(8,128)(2,1)S(1)} custom-call(bf16[192,896]{1,0:T(8,128)(2,1)S(1)} %ahead_rows_1.1.refs_2_.refs_0_, bf16[192,896]{1,0:T(8,128)(2,1)S(1)} %collective-permute-done.7.refs_1_.refs_3_, bf16[2,1024,1792]{2,1,0:T(8,128)(2,1)S(1)} %bitcast.24, bf16[1,192,512]{2,1,0:T(8,128)(2,1)S(1)} %grad_outer_1.1.refs_3_), custom_call_target="tpu_custom_call" | custom-call | flops 10400000000 | bytes 1024 | tf_op jit(solution)/shard_map/ahead_far_1/pallas_call | solution.py:43
  61.4 4.6 %ahead_near.1.refs_1_.refs_3_.refs_0_ = bf16[2,384,512]{2,1,0:T(8,128)(2,1)S(1)} custom-call(bf16[192,896]{1,0:T(8,128)(2,1)S(1)} %ahead_rows_0.1.refs_3_.refs_0_, bf16[192,896]{1,0:T(8,128)(2,1)S(1)} %collective-permute-done.refs_1_, bf16[192,896]{1,0:T(8,128)(2,1)S(1)} %ahead_rows_1.1.refs_2_.refs_0_, ...), custom_call_target="tpu_custom_call" | custom-call | flops 10400000000 | bytes 1024 | tf_op jit(solution)/shard_map/ahead_near/pallas_call | solution.py:43
  68.8 2.7 %collective-permute-start.17 = (bf16[2,192,512]{2,1,0:T(8,128)(2,1)S(1)}, bf16[2,192,512]{2,1,0:T(8,128)(2,1)S(1)}, u32[]{:S(2)}, u32[]{:S(2)}) collective-permute-start(bf16[2,192,512]{2,1,0:T(8,128)(2,1)S(1)} %behind_outer_2.1.refs_2_), channel_id=1, source_target_pairs={{0,2},{1,3},{2,0},{3,1},{4,6},{5,7},{6,4},{7,5},{8,10},{9,11},{10,... | collective-permute-start | bytes 1179656 | tf_op jit(solution)/shard_map/ppermute | solution.py:251
  73.8 4.1 %collective-permute-start.20 = (bf16[1,192,512]{2,1,0:T(8,128)(2,1)S(1)}, bf16[1,192,512]{2,1,0:T(8,128)(2,1)S(1)}, u32[]{:S(2)}, u32[]{:S(2)}) collective-permute-start(bf16[1,192,512]{2,1,0:T(8,128)(2,1)S(1)} %grad_third_1.1.refs_1_), channel_id=1, source_target_pairs={{0,2},{1,3},{2,0},{3,1},{4,6},{5,7},{6,4},{7,5},{8,10},{9,11},{10,... | collective-permute-start | bytes 589832 | tf_op jit(solution)/shard_map/ppermute | solution.py:251
  77.9 2.7 %collective-permute-done.17.refs_0_.refs_1_ = bf16[2,192,512]{2,1,0:T(8,128)(2,1)S(1)} collective-permute-done((bf16[2,192,512]{2,1,0:T(8,128)(2,1)S(1)}, bf16[2,192,512]{2,1,0:T(8,128)(2,1)S(1)}, u32[]{:S(2)}, u32[]{:S(2)}) %collective-permute-start.17) | collective-permute-done | bytes 393248 | tf_op jit(solution)/shard_map/ppermute | solution.py:251
  81.4 4.1 %collective-permute-start.19 = (bf16[2,192,512]{2,1,0:T(8,128)(2,1)S(1)}, bf16[2,192,512]{2,1,0:T(8,128)(2,1)S(1)}, u32[]{:S(2)}, u32[]{:S(2)}) collective-permute-start(bf16[2,192,512]{2,1,0:T(8,128)(2,1)S(1)} %ahead_outer_2.1.refs_5_), channel_id=1, source_target_pairs={{0,2},{1,3},{2,0},{3,1},{4,6},{5,7},{6,4},{7,5},{8,10},{9,11},{10,... | collective-permute-start | bytes 1179656 | tf_op jit(solution)/shard_map/ppermute | solution.py:251
  85.9 5.9 %collective-permute-start.23 = (bf16[2,192,512]{2,1,0:T(8,128)(2,1)S(1)}, bf16[2,192,512]{2,1,0:T(8,128)(2,1)S(1)}, u32[]{:S(2)}, u32[]{:S(2)}) collective-permute-start(bf16[2,192,512]{2,1,0:T(8,128)(2,1)S(1)} %behind_back_1.1.refs_1_), channel_id=1, source_target_pairs={{0,2},{1,3},{2,0},{3,1},{4,6},{5,7},{6,4},{7,5},{8,10},{9,11},{10,... | collective-permute-start | bytes 1179656 | tf_op jit(solution)/shard_map/ppermute | solution.py:251
  94.8 4.7 %collective-permute-done.23.refs_0_.refs_3_ = bf16[2,192,512]{2,1,0:T(8,128)(2,1)S(1)} collective-permute-done((bf16[2,192,512]{2,1,0:T(8,128)(2,1)S(1)}, bf16[2,192,512]{2,1,0:T(8,128)(2,1)S(1)}, u32[]{:S(2)}, u32[]{:S(2)}) %collective-permute-start.23) | collective-permute-done | bytes 393248 | tf_op jit(solution)/shard_map/ppermute | solution.py:251
  100.2 3.9 %collective-permute-start.24 = (bf16[1,192,512]{2,1,0:T(8,128)(2,1)S(1)}, bf16[1,192,512]{2,1,0:T(8,128)(2,1)S(1)}, u32[]{:S(2)}, u32[]{:S(2)}) collective-permute-start(bf16[1,192,512]{2,1,0:T(8,128)(2,1)S(1)} %ahead_back_1.1.refs_5_), channel_id=1, source_target_pairs={{0,2},{1,3},{2,0},{3,1},{4,6},{5,7},{6,4},{7,5},{8,10},{9,11},{10,... | collective-permute-start | bytes 589832 | tf_op jit(solution)/shard_map/ppermute | solution.py:251
  104.2 2.7 %behind_out_0.1 = (bf16[192,896]{1,0:T(8,128)(2,1)S(1)}, bf16[192,896]{1,0:T(8,128)(2,1)S(1)}) custom-call(bf16[2,192,512]{2,1,0:T(8,128)(2,1)S(1)} %behind_act_0.1.refs_0_.refs_3_, bf16[2,192,512]{2,1,0:T(8,128)(2,1)S(1)} %behind_first_0.1.refs_3_.refs_1_, bf16[2,192,512]{2,1,0:T(8,128)(2,1)S(1)} %collective-permute-done.21.refs_1_.refs_2_, ...), custom_call_target="tpu_custom_call" | custom-call | flops 20000000000 | bytes 1024 | tf_op jit(solution)/shard_map/behind_out_0/pallas_call | solution.py:43
  113.3 4.8 %collective-permute-start.28 = (bf16[1,192,512]{2,1,0:T(8,128)(2,1)S(1)}, bf16[1,192,512]{2,1,0:T(8,128)(2,1)S(1)}, u32[]{:S(2)}, u32[]{:S(2)}) collective-permute-start(bf16[1,192,512]{2,1,0:T(8,128)(2,1)S(1)} %ahead_back_2.1.refs_2_), channel_id=1, source_target_pairs={{0,2},{1,3},{2,0},{3,1},{4,6},{5,7},{6,4},{7,5},{8,10},{9,11},{10,... | collective-permute-start | bytes 589832 | tf_op jit(solution)/shard_map/ppermute | solution.py:251
  118.2 15.3 %collective-permute-start.34 = (bf16[192,896]{1,0:T(8,128)(2,1)S(1)}, bf16[192,896]{1,0:T(8,128)(2,1)S(1)}, u32[]{:S(2)}, u32[]{:S(2)}) collective-permute-start(bf16[192,896]{1,0:T(8,128)(2,1)S(1)} %behind_shares.1.refs_5_), channel_id=1, source_target_pairs={{8,0},{9,1},{10,2},{11,3},{12,4},{13,5},{14,6},{15,7},{16,8},{17,9... | collective-permute-start | bytes 1032200 | tf_op jit(solution)/shard_map/ppermute | solution.py:275
  133.5 2.7 %behind_out_1.1 = (bf16[192,896]{1,0:T(8,128)(2,1)S(1)}, bf16[192,896]{1,0:T(8,128)(2,1)S(1)}) custom-call(bf16[2,192,512]{2,1,0:T(8,128)(2,1)S(1)} %behind_act_1.1.refs_0_.refs_2_, bf16[2,192,512]{2,1,0:T(8,128)(2,1)S(1)} %behind_first_1.1.refs_2_.refs_1_, bf16[2,192,512]{2,1,0:T(8,128)(2,1)S(1)} %collective-permute-done.25.refs_0_.refs_2_, ...), custom_call_target="tpu_custom_call" | custom-call | flops 20000000000 | bytes 1024 | tf_op jit(solution)/shard_map/behind_out_1/pallas_call | solution.py:43
  142.1 4.1 %collective-permute-start.32 = (bf16[192,896]{1,0:T(8,128)(2,1)S(1)}, bf16[192,896]{1,0:T(8,128)(2,1)S(1)}, u32[]{:S(2)}, u32[]{:S(2)}) collective-permute-start(bf16[192,896]{1,0:T(8,128)(2,1)S(1)} %get-tuple-element.15.refs_2_), channel_id=1, source_target_pairs={{0,9},{1,8},{2,11},{3,10},{4,13},{5,12},{6,15},{7,14},{8,17},{9,16... | collective-permute-start | bytes 1032200 | tf_op jit(solution)/shard_map/ppermute | solution.py:275
  146.4 2.5 %collective-permute-start.31 = (bf16[192,896]{1,0:T(8,128)(2,1)S(1)}, bf16[192,896]{1,0:T(8,128)(2,1)S(1)}, u32[]{:S(2)}, u32[]{:S(2)}) collective-permute-start(bf16[192,896]{1,0:T(8,128)(2,1)S(1)} %ahead_shares.1.refs_3_), channel_id=1, source_target_pairs={{0,8},{1,9},{2,10},{3,11},{4,12},{5,13},{6,14},{7,15},{8,16},{9,17... | collective-permute-start | bytes 1032200 | tf_op jit(solution)/shard_map/ppermute | solution.py:275
  154.2 3.7 %collective-permute-done.33.refs_2_ = bf16[192,896]{1,0:T(8,128)(2,1)S(1)} collective-permute-done((bf16[192,896]{1,0:T(8,128)(2,1)S(1)}, bf16[192,896]{1,0:T(8,128)(2,1)S(1)}, u32[]{:S(2)}, u32[]{:S(2)}) %collective-permute-start.33) | collective-permute-done | bytes 344096 | tf_op jit(solution)/shard_map/ppermute | solution.py:275
  (126 shorter events, 53.1 us)
Async XLA Ops:
  1.8 10.0 %collective-permute-start.1 = (bf16[192,896]{1,0:T(8,128)(2,1)S(1)}, bf16[192,896]{1,0:T(8,128)(2,1)}, u32[]{:S(2)}, u32[]{:S(2)}) collective-permute-start(bf16[192,896]{1,0:T(8,128)(2,1)S(1)} %behind_rows_0.1.refs_1_.refs_0_), channel_id=1, source_target_pairs={{0,1},{1,0},{2,3},{3,2},{4,5},{5,4},{6,7},{7,6},{8,9},{9,8},{10,11... | collective-permute-start | bytes 1032200 | tf_op jit(solution)/shard_map/ppermute | solution.py:266
  3.9 18.3 %collective-permute-start.3 = (bf16[192,896]{1,0:T(8,128)(2,1)S(1)}, bf16[192,896]{1,0:T(8,128)(2,1)S(1)}, u32[]{:S(2)}, u32[]{:S(2)}) collective-permute-start(bf16[192,896]{1,0:T(8,128)(2,1)S(1)} %grad_rows_0.1.refs_1_.refs_0_), channel_id=1, source_target_pairs={{0,1},{1,0},{2,3},{3,2},{4,5},{5,4},{6,7},{7,6},{8,9},{9,8},{10,11... | collective-permute-start | bytes 1032200 | tf_op jit(solution)/shard_map/ppermute | solution.py:266
  5.0 21.4 %collective-permute-start = (bf16[192,896]{1,0:T(8,128)(2,1)S(1)}, bf16[192,896]{1,0:T(8,128)(2,1)S(1)}, u32[]{:S(2)}, u32[]{:S(2)}) collective-permute-start(bf16[192,896]{1,0:T(8,128)(2,1)S(1)} %ahead_rows_0.1.refs_3_.refs_0_), channel_id=1, source_target_pairs={{0,1},{1,0},{2,3},{3,2},{4,5},{5,4},{6,7},{7,6},{8,9},{9,8},{10,11... | collective-permute-start | bytes 1032200 | tf_op jit(solution)/shard_map/ppermute | solution.py:266
  19.6 11.7 %collective-permute-start.5 = (bf16[2,192,512]{2,1,0:T(8,128)(2,1)S(1)}, bf16[2,192,512]{2,1,0:T(8,128)(2,1)S(1)}, u32[]{:S(2)}, u32[]{:S(2)}) collective-permute-start(bf16[2,192,512]{2,1,0:T(8,128)(2,1)S(1)} %behind_far_0.1.refs_1_.refs_0_), channel_id=1, source_target_pairs={{0,2},{1,3},{2,0},{3,1},{4,6},{5,7},{6,4},{7,5},{8,10},{9,11},{10,... | collective-permute-start | bytes 1179656 | tf_op jit(solution)/shard_map/ppermute | solution.py:251
  20.9 13.2 %collective-permute-start.2 = (bf16[192,896]{1,0:T(8,128)(2,1)S(1)}, bf16[192,896]{1,0:T(8,128)(2,1)S(1)}, u32[]{:S(2)}, u32[]{:S(2)}) collective-permute-start(bf16[192,896]{1,0:T(8,128)(2,1)S(1)} %behind_rows_1.1.refs_3_.refs_0_.refs_2_), channel_id=1, source_target_pairs={{0,1},{1,0},{2,3},{3,2},{4,5},{5,4},{6,7},{7,6},{8,9},{9,8},{10,11... | collective-permute-start | bytes 1032200 | tf_op jit(solution)/shard_map/ppermute | solution.py:266
  30.0 18.9 %collective-permute-start.10 = (bf16[2,192,512]{2,1,0:T(8,128)(2,1)S(1)}, bf16[2,192,512]{2,1,0:T(8,128)(2,1)S(1)}, u32[]{:S(2)}, u32[]{:S(2)}) collective-permute-start(bf16[2,192,512]{2,1,0:T(8,128)(2,1)S(1)} %ahead_far_0.1.refs_2_.refs_0_), channel_id=1, source_target_pairs={{0,2},{1,3},{2,0},{3,1},{4,6},{5,7},{6,4},{7,5},{8,10},{9,11},{10,... | collective-permute-start | bytes 1179656 | tf_op jit(solution)/shard_map/ppermute | solution.py:251
  31.4 11.9 %collective-permute-start.6 = (bf16[2,192,512]{2,1,0:T(8,128)(2,1)S(1)}, bf16[2,192,512]{2,1,0:T(8,128)(2,1)S(1)}, u32[]{:S(2)}, u32[]{:S(2)}) collective-permute-start(bf16[2,192,512]{2,1,0:T(8,128)(2,1)S(1)} %behind_middle_0.1.refs_1_), channel_id=1, source_target_pairs={{0,0},{1,1},{2,4},{3,5},{4,2},{5,3},{6,6},{7,7},{8,8},{9,9},{10,12... | collective-permute-start | bytes 1179656 | tf_op jit(solution)/shard_map/ppermute | solution.py:251
  32.1 17.6 %collective-permute-start.9 = (bf16[192,896]{1,0:T(8,128)(2,1)S(1)}, bf16[192,896]{1,0:T(8,128)(2,1)S(1)}, u32[]{:S(2)}, u32[]{:S(2)}) collective-permute-start(bf16[192,896]{1,0:T(8,128)(2,1)S(1)} %grad_rows_1.1.refs_2_.refs_0_), channel_id=1, source_target_pairs={{0,1},{1,0},{2,3},{3,2},{4,5},{5,4},{6,7},{7,6},{8,9},{9,8},{10,11... | collective-permute-start | bytes 1032200 | tf_op jit(solution)/shard_map/ppermute | solution.py:266
  33.5 20.5 %collective-permute-start.11 = (bf16[1,192,512]{2,1,0:T(8,128)(2,1)S(1)}, bf16[1,192,512]{2,1,0:T(8,128)(2,1)S(1)}, u32[]{:S(2)}, u32[]{:S(2)}) collective-permute-start(bf16[1,192,512]{2,1,0:T(8,128)(2,1)S(1)} %grad_middle_0.1.refs_3_), channel_id=1, source_target_pairs={{0,0},{1,1},{2,4},{3,5},{4,2},{5,3},{6,6},{7,7},{8,8},{9,9},{10,12... | collective-permute-start | bytes 589832 | tf_op jit(solution)/shard_map/ppermute | solution.py:251
  43.4 17.0 %collective-permute-start.8 = (bf16[2,192,512]{2,1,0:T(8,128)(2,1)S(1)}, bf16[2,192,512]{2,1,0:T(8,128)(2,1)S(1)}, u32[]{:S(2)}, u32[]{:S(2)}) collective-permute-start(bf16[2,192,512]{2,1,0:T(8,128)(2,1)S(1)} %behind_outer_1.1.refs_1_), channel_id=1, source_target_pairs={{0,2},{1,3},{2,0},{3,1},{4,6},{5,7},{6,4},{7,5},{8,10},{9,11},{10,... | collective-permute-start | bytes 1179656 | tf_op jit(solution)/shard_map/ppermute | solution.py:251
  49.1 17.0 %collective-permute-start.12 = (bf16[2,192,512]{2,1,0:T(8,128)(2,1)S(1)}, bf16[2,192,512]{2,1,0:T(8,128)(2,1)S(1)}, u32[]{:S(2)}, u32[]{:S(2)}) collective-permute-start(bf16[2,192,512]{2,1,0:T(8,128)(2,1)S(1)} %ahead_middle_0.1.refs_3_), channel_id=1, source_target_pairs={{0,0},{1,1},{2,4},{3,5},{4,2},{5,3},{6,6},{7,7},{8,8},{9,9},{10,12... | collective-permute-start | bytes 1179656 | tf_op jit(solution)/shard_map/ppermute | solution.py:251
  54.0 13.6 %collective-permute-start.14 = (bf16[1,192,512]{2,1,0:T(8,128)(2,1)S(1)}, bf16[1,192,512]{2,1,0:T(8,128)(2,1)S(1)}, u32[]{:S(2)}, u32[]{:S(2)}) collective-permute-start(bf16[1,192,512]{2,1,0:T(8,128)(2,1)S(1)} %grad_outer_1.1.refs_3_), channel_id=1, source_target_pairs={{0,2},{1,3},{2,0},{3,1},{4,6},{5,7},{6,4},{7,5},{8,10},{9,11},{10,... | collective-permute-start | bytes 589832 | tf_op jit(solution)/shard_map/ppermute | solution.py:251
  68.8 11.8 %collective-permute-start.17 = (bf16[2,192,512]{2,1,0:T(8,128)(2,1)S(1)}, bf16[2,192,512]{2,1,0:T(8,128)(2,1)S(1)}, u32[]{:S(2)}, u32[]{:S(2)}) collective-permute-start(bf16[2,192,512]{2,1,0:T(8,128)(2,1)S(1)} %behind_outer_2.1.refs_2_), channel_id=1, source_target_pairs={{0,2},{1,3},{2,0},{3,1},{4,6},{5,7},{6,4},{7,5},{8,10},{9,11},{10,... | collective-permute-start | bytes 1179656 | tf_op jit(solution)/shard_map/ppermute | solution.py:251
  73.8 11.7 %collective-permute-start.20 = (bf16[1,192,512]{2,1,0:T(8,128)(2,1)S(1)}, bf16[1,192,512]{2,1,0:T(8,128)(2,1)S(1)}, u32[]{:S(2)}, u32[]{:S(2)}) collective-permute-start(bf16[1,192,512]{2,1,0:T(8,128)(2,1)S(1)} %grad_third_1.1.refs_1_), channel_id=1, source_target_pairs={{0,2},{1,3},{2,0},{3,1},{4,6},{5,7},{6,4},{7,5},{8,10},{9,11},{10,... | collective-permute-start | bytes 589832 | tf_op jit(solution)/shard_map/ppermute | solution.py:251
  81.4 12.6 %collective-permute-start.19 = (bf16[2,192,512]{2,1,0:T(8,128)(2,1)S(1)}, bf16[2,192,512]{2,1,0:T(8,128)(2,1)S(1)}, u32[]{:S(2)}, u32[]{:S(2)}) collective-permute-start(bf16[2,192,512]{2,1,0:T(8,128)(2,1)S(1)} %ahead_outer_2.1.refs_5_), channel_id=1, source_target_pairs={{0,2},{1,3},{2,0},{3,1},{4,6},{5,7},{6,4},{7,5},{8,10},{9,11},{10,... | collective-permute-start | bytes 1179656 | tf_op jit(solution)/shard_map/ppermute | solution.py:251
  85.9 13.6 %collective-permute-start.23 = (bf16[2,192,512]{2,1,0:T(8,128)(2,1)S(1)}, bf16[2,192,512]{2,1,0:T(8,128)(2,1)S(1)}, u32[]{:S(2)}, u32[]{:S(2)}) collective-permute-start(bf16[2,192,512]{2,1,0:T(8,128)(2,1)S(1)} %behind_back_1.1.refs_1_), channel_id=1, source_target_pairs={{0,2},{1,3},{2,0},{3,1},{4,6},{5,7},{6,4},{7,5},{8,10},{9,11},{10,... | collective-permute-start | bytes 1179656 | tf_op jit(solution)/shard_map/ppermute | solution.py:251
  106.8 11.2 %collective-permute-start.30 = (bf16[192,896]{1,0:T(8,128)(2,1)S(1)}, bf16[192,896]{1,0:T(8,128)(2,1)S(1)}, u32[]{:S(2)}, u32[]{:S(2)}) collective-permute-start(bf16[192,896]{1,0:T(8,128)(2,1)S(1)} %get-tuple-element.10.refs_1_), channel_id=1, source_target_pairs={{0,1},{1,0},{2,3},{3,2},{4,5},{5,4},{6,7},{7,6},{8,9},{9,8},{10,11... | collective-permute-start | bytes 1032200 | tf_op jit(solution)/shard_map/ppermute | solution.py:266
  108.2 25.3 %collective-permute-start.29 = (bf16[2,192,512]{2,1,0:T(8,128)(2,1)S(1)}, bf16[2,192,512]{2,1,0:T(8,128)(2,1)S(1)}, u32[]{:S(2)}, u32[]{:S(2)}) collective-permute-start(bf16[2,192,512]{2,1,0:T(8,128)(2,1)S(1)} %behind_back_2.1.refs_1_), channel_id=1, source_target_pairs={{0,2},{1,3},{2,0},{3,1},{4,6},{5,7},{6,4},{7,5},{8,10},{9,11},{10,... | collective-permute-start | bytes 1179656 | tf_op jit(solution)/shard_map/ppermute | solution.py:251
  112.0 34.3 %collective-permute-start.26 = (bf16[192,896]{1,0:T(8,128)(2,1)S(1)}, bf16[192,896]{1,0:T(8,128)(2,1)S(1)}, u32[]{:S(2)}, u32[]{:S(2)}) collective-permute-start(bf16[192,896]{1,0:T(8,128)(2,1)S(1)} %get-tuple-element.12.refs_1_), channel_id=1, source_target_pairs={{0,1},{1,0},{2,3},{3,2},{4,5},{5,4},{6,7},{7,6},{8,9},{9,8},{10,11... | collective-permute-start | bytes 1032200 | tf_op jit(solution)/shard_map/ppermute | solution.py:266
  113.3 27.3 %collective-permute-start.28 = (bf16[1,192,512]{2,1,0:T(8,128)(2,1)S(1)}, bf16[1,192,512]{2,1,0:T(8,128)(2,1)S(1)}, u32[]{:S(2)}, u32[]{:S(2)}) collective-permute-start(bf16[1,192,512]{2,1,0:T(8,128)(2,1)S(1)} %ahead_back_2.1.refs_2_), channel_id=1, source_target_pairs={{0,2},{1,3},{2,0},{3,1},{4,6},{5,7},{6,4},{7,5},{8,10},{9,11},{10,... | collective-permute-start | bytes 589832 | tf_op jit(solution)/shard_map/ppermute | solution.py:251
  118.2 30.7 %collective-permute-start.34 = (bf16[192,896]{1,0:T(8,128)(2,1)S(1)}, bf16[192,896]{1,0:T(8,128)(2,1)S(1)}, u32[]{:S(2)}, u32[]{:S(2)}) collective-permute-start(bf16[192,896]{1,0:T(8,128)(2,1)S(1)} %behind_shares.1.refs_5_), channel_id=1, source_target_pairs={{8,0},{9,1},{10,2},{11,3},{12,4},{13,5},{14,6},{15,7},{16,8},{17,9... | collective-permute-start | bytes 1032200 | tf_op jit(solution)/shard_map/ppermute | solution.py:275
  136.2 14.6 %collective-permute-start.35 = (bf16[192,896]{1,0:T(8,128)(2,1)S(1)}, bf16[192,896]{1,0:T(8,128)(2,1)S(1)}, u32[]{:S(2)}, u32[]{:S(2)}) collective-permute-start(bf16[192,896]{1,0:T(8,128)(2,1)S(1)} %get-tuple-element.14.refs_6_), channel_id=1, source_target_pairs={{8,1},{9,0},{10,3},{11,2},{12,5},{13,4},{14,7},{15,6},{16,9},{17,8... | collective-permute-start | bytes 1032200 | tf_op jit(solution)/shard_map/ppermute | solution.py:275
  138.6 12.2 %collective-permute-start.36 = (bf16[192,896]{1,0:T(8,128)(2,1)S(1)}, bf16[192,896]{1,0:T(8,128)(2,1)S(1)}, u32[]{:S(2)}, u32[]{:S(2)}) collective-permute-start(bf16[192,896]{1,0:T(8,128)(2,1)S(1)} %get-tuple-element.17), channel_id=1, source_target_pairs={{8,0},{9,1},{10,2},{11,3},{12,4},{13,5},{14,6},{15,7},{16,8},{17,9... | collective-permute-start | bytes 1032200 | tf_op jit(solution)/shard_map/ppermute | solution.py:275
  142.1 12.0 %collective-permute-start.32 = (bf16[192,896]{1,0:T(8,128)(2,1)S(1)}, bf16[192,896]{1,0:T(8,128)(2,1)S(1)}, u32[]{:S(2)}, u32[]{:S(2)}) collective-permute-start(bf16[192,896]{1,0:T(8,128)(2,1)S(1)} %get-tuple-element.15.refs_2_), channel_id=1, source_target_pairs={{0,9},{1,8},{2,11},{3,10},{4,13},{5,12},{6,15},{7,14},{8,17},{9,16... | collective-permute-start | bytes 1032200 | tf_op jit(solution)/shard_map/ppermute | solution.py:275
  (24 other events, 134.4 us)

commit v13 on v12

--- a/solution.py
+++ b/solution.py
@@ -69,20 +69,10 @@
 
 
 def first_kernel(far, *refs):
-    rows, (weights, out, joined, tiles, sems) = refs[:-5], refs[-5:]
+    rows, (weights, out, joined) = refs[:-3], refs[-3:]
     near, group, _ = position()
     side = 1 - near if far else near
     parts, _, half = out.shape
-    tile = tiles.shape[1]
-    steps = half // tile
-    copies = []
-    for k in range(parts):
-        for j in range(steps):
-            n = k * steps + j
-            at = pl.multiple_of((side * steps + j) * tile, tile)
-            copy = pltpu.make_async_copy(weights.at[k, pl.ds(at, tile)], tiles.at[n], sems.at[n])
-            copy.start()
-            copies.append(copy)
     slots, width = rows[0].shape
     at = pl.multiple_of(group * width, 128)
     other = pl.multiple_of((1 - group) * width, 128)
@@ -90,34 +80,29 @@
         here = pl.ds(piece * slots, slots)
         joined[here, pl.ds(at, width)] = rows[2 * piece][...]
         joined[here, pl.ds(other, width)] = rows[2 * piece + 1][...]
+    tile = min(256, half)
     for k in range(parts):
-        for j in range(steps):
-            n = k * steps + j
-            copies[n].wait()
+        for j in range(half // tile):
+            at = pl.multiple_of(side * half + j * tile, tile)
             out[k, :, j * tile : (j + 1) * tile] = lax.dot_general(
-                joined[...], tiles[n], (((1,), (1,)), ((), ())), preferred_element_type=F32
+                joined[...],
+                weights[k, pl.ds(at, tile)],
+                (((1,), (1,)), ((), ())),
+                preferred_element_type=F32,
             ).astype(BF16)
 
 
 def first_product(name, far, rows, weights, after):
-    slots, width = rows[0].shape
-    slots *= len(rows) // 2
+    slots = rows[0].shape[0] * len(rows) // 2
     parts, units, features = weights.shape
-    half = units // 2
-    tile = min(256, half)
-    steps = half // tile
     return call(
         functools.partial(first_kernel, far),
         FIRST * parts,
         (*rows, weights),
         after,
-        jax.ShapeDtypeStruct((parts, slots, half), BF16),
-        in_specs=[*[whole(r) for r in rows], pl.BlockSpec(memory_space=pl.ANY)],
-        scratch=[
-            pltpu.VMEM((slots, features), BF16),
-            pltpu.VMEM((parts * steps, tile, features), BF16),
-            pltpu.SemaphoreType.DMA((parts * steps,)),
-        ],
+        jax.ShapeDtypeStruct((parts, slots, units // 2), BF16),
+        in_specs=[*[whole(r) for r in rows], pl.BlockSpec(memory_space=pltpu.VMEM)],
+        scratch=[pltpu.VMEM((slots, features), BF16)],
         name=name,
     )
 
@@ -176,18 +161,11 @@
 
 def second_kernel(scaled, act, one, two, three, *refs):
     scale, refs = (refs[0], refs[1:]) if scaled else (None, refs)
-    weights, give, keep, joined, tiles, sems = refs
+    weights, give, keep, joined = refs
     near_half, group, end = position()
     kinds, _, half = act.shape
-    _, _, units, width = tiles.shape
-    copies = []
-    for own in range(2):
-        at = pl.multiple_of((group if own else 1 - group) * width, 128)
-        copy = pltpu.make_async_copy(
-            weights.at[:, :, pl.ds(at, width)], tiles.at[own], sems.at[own]
-        )
-        copy.start()
-        copies.append(copy)
+    units = weights.shape[1]
+    width = give.shape[1]
 
     def place(near, far):
         for kind in range(kinds):
@@ -204,11 +182,10 @@
     def _():
         place(one, two)
 
-    for own, out in enumerate((give, keep)):
-        copies[own].wait()
-        share = jnp.dot(
-            joined[...], tiles[own].reshape(kinds * units, width), preferred_element_type=F32
-        )
+    for side, out in ((1 - group, give), (group, keep)):
+        at = pl.multiple_of(side * width, 128)
+        tile = weights[:, :, pl.ds(at, width)].reshape(kinds * units, width)
+        share = jnp.dot(joined[...], tile, preferred_element_type=F32)
         if scaled:
             share = share * scale[...]
         out[...] = share.astype(BF16)
@@ -217,21 +194,16 @@
 def second_product(name, values, scale, weights, after):
     kinds, units, features = weights.shape
     slots = values[0].shape[1]
-    width = features // 2
     operands = [*values] + ([] if scale is None else [scale])
-    share = jax.ShapeDtypeStruct((slots, width), BF16)
+    share = jax.ShapeDtypeStruct((slots, features // 2), BF16)
     return call(
         functools.partial(second_kernel, scale is not None),
         AHEAD_OUT if kinds == 1 else BEHIND_OUT,
         (*operands, weights),
         after,
         (share, share),
-        in_specs=[*[whole(v) for v in operands], pl.BlockSpec(memory_space=pl.ANY)],
-        scratch=[
-            pltpu.VMEM((slots, kinds * units), BF16),
-            pltpu.VMEM((2, kinds, units, width), BF16),
-            pltpu.SemaphoreType.DMA((2,)),
-        ],
+        in_specs=[*[whole(v) for v in operands], pl.BlockSpec(memory_space=pltpu.VMEM)],
+        scratch=[pltpu.VMEM((slots, kinds * units), BF16)],
         name=name,
     )
 

time: 161 us -> 149 us (0.925)
  Pallas kernels: 44.2 us -> 23.2 us
  waiting for transfers between devices: 23.9 us -> 32 us
  starting transfers between devices: 84.6 us -> 86.3 us
    pallas_call x47, Pallas kernels: 44.2 us -> 23.2 us  [call(): pl.pallas_call(run, compiler_params=pltpu.CompilerParams(vmem_limit_bytes...]
    ppermute x23, starting transfers between devices: 46.6 us -> 58.9 us  [between(): return lax.ppermute(value, 'expert', pairs)]
    ppermute x6, starting transfers between devices: 28.2 us -> 19.9 us  [to_section(): return lax.ppermute(value, ('section', 'expert'), pairs)]
    ppermute x8, waiting for transfers between devices: 6.74 us -> 12.7 us  [swapped(): return lax.ppermute(value, 'expert', [(i, i ^ 1) for i in range(devices)])]
    ppermute x8, starting transfers between devices: 9.77 us -> 7.52 us  [swapped(): return lax.ppermute(value, 'expert', [(i, i ^ 1) for i in range(devices)])]
    ppermute x23, waiting for transfers between devices: 11.1 us -> 13.3 us  [between(): return lax.ppermute(value, 'expert', pairs)]
  transfers between devices with their start and end apart: 37 -> 37, of which waited for: 9 -> 8; matrix products, arithmetic and copies ran while one was open for 0% -> 0% of each run, Pallas kernels for 27% -> 15%
where the time goes in v13:
time: 149 us
  starting transfers between devices  86.3 us (58%)
  waiting for transfers between devices  32 us (21%)
  Pallas kernels  23.2 us (16%)
  local copies, waits for them, and re-layouts  5.87 us (4%)
    ppermute x23, starting transfers between devices, between(): return lax.ppermute(value, 'expert', pairs)  58.9 us
    pallas_call x47, Pallas kernels, call(): pl.pallas_call(run, compiler_params=pltpu.CompilerParams(vmem_limit_bytes...  23.2 us
    ppermute x6, starting transfers between devices, to_section(): return lax.ppermute(value, ('section', 'expert'), pairs)  19.9 us
    ppermute x23, waiting for transfers between devices, between(): return lax.ppermute(value, 'expert', pairs)  13.3 us
    ppermute x8, waiting for transfers between devices, swapped(): return lax.ppermute(value, 'expert', [(i, i ^ 1) for i in range(devices)])  12.7 us
    ppermute x8, starting transfers between devices, swapped(): return lax.ppermute(value, 'expert', [(i, i ^ 1) for i in range(devices)])  7.52 us
    ppermute x6, waiting for transfers between devices, to_section(): return lax.ppermute(value, ('section', 'expert'), pairs)  5.98 us
    unnamed x22, local copies, waits for them, and re-layouts  5.31 us
  transfers between devices with their start and end apart: 37, of which 8 were waited for; matrix products, arithmetic and copies ran while one was open for 0% of the time, Pallas kernels for 15%

profile of v13, /device:TPU:1, one launch (start us, length us, event | category | flops | bytes accessed | tf_op | source)
XLA Modules:
  0.0 148.6 jit_solution(15311015529544176312)
XLA Ops:
  1.8 2.1 %collective-permute-start.1 = (bf16[192,896]{1,0:T(8,128)(2,1)S(1)}, bf16[192,896]{1,0:T(8,128)(2,1)}, u32[]{:S(2)}, u32[]{:S(2)}) collective-permute-start(bf16[192,896]{1,0:T(8,128)(2,1)S(1)} %behind_rows_0.1.refs_1_.refs_0_), channel_id=1, source_target_pairs={{0,1},{1,0},{2,3},{3,2},{4,5},{5,4},{6,7},{7,6},{8,9},{9,8},{10,11... | collective-permute-start | bytes 1032200 | tf_op jit(solution)/shard_map/ppermute | solution.py:238
  6.8 5.0 %collective-permute-done.1.refs_1_ = bf16[192,896]{1,0:T(8,128)(2,1)} collective-permute-done((bf16[192,896]{1,0:T(8,128)(2,1)S(1)}, bf16[192,896]{1,0:T(8,128)(2,1)}, u32[]{:S(2)}, u32[]{:S(2)}) %collective-permute-start.1) | collective-permute-done | bytes 344096 | tf_op jit(solution)/shard_map/ppermute | solution.py:238
  11.8 3.1 %copy-done = bf16[1,1,2,1024,1792]{4,3,2,1,0:T(8,128)(2,1)S(1)} copy-done((bf16[1,1,2,1024,1792]{4,3,2,1,0:T(8,128)(2,1)S(1)}, bf16[1,1,2,1024,1792]{4,3,2,1,0:T(8,128)(2,1)}, u32[]{:S(2)}) %copy-start) | copy-done | bytes 7340056
  14.9 2.4 %behind_far_0.1.refs_1_.refs_0_ = bf16[2,192,512]{2,1,0:T(8,128)(2,1)S(1)} custom-call(bf16[192,896]{1,0:T(8,128)(2,1)S(1)} %behind_rows_0.1.refs_1_.refs_0_, bf16[192,896]{1,0:T(8,128)(2,1)} %collective-permute-done.1.refs_1_, bf16[2,1024,1792]{2,1,0:T(8,128)(2,1)S(1)} %bitcast.18, bf16[192,896]{1,0:T(8,128)(2,1)S(1)} %ahead_rows_0.1.refs_3_.refs_0_), custom_call_target="tpu_custom_call" | custom-call | flops 10400000000 | bytes 1024 | tf_op jit(solution)/shard_map/behind_far_0/pallas_call | solution.py:43
  21.4 5.1 %collective-permute-done.refs_1_ = bf16[192,896]{1,0:T(8,128)(2,1)S(1)} collective-permute-done((bf16[192,896]{1,0:T(8,128)(2,1)S(1)}, bf16[192,896]{1,0:T(8,128)(2,1)S(1)}, u32[]{:S(2)}, u32[]{:S(2)}) %collective-permute-start) | collective-permute-done | bytes 344096 | tf_op jit(solution)/shard_map/ppermute | solution.py:238
  35.1 2.6 %behind_near.1.refs_1_.refs_3_.refs_0_ = bf16[2,384,512]{2,1,0:T(8,128)(2,1)S(1)} custom-call(bf16[192,896]{1,0:T(8,128)(2,1)S(1)} %behind_rows_0.1.refs_1_.refs_0_, bf16[192,896]{1,0:T(8,128)(2,1)} %collective-permute-done.1.refs_1_, bf16[192,896]{1,0:T(8,128)(2,1)S(1)} %behind_rows_1.1.refs_3_.refs_0_.refs_2_, ...), custom_call_target="tpu_custom_call" | custom-call | flops 10400000000 | bytes 1024 | tf_op jit(solution)/shard_map/behind_near/pallas_call | solution.py:43
  37.8 3.3 %collective-permute-start.8 = (bf16[2,192,512]{2,1,0:T(8,128)(2,1)S(1)}, bf16[2,192,512]{2,1,0:T(8,128)(2,1)S(1)}, u32[]{:S(2)}, u32[]{:S(2)}) collective-permute-start(bf16[2,192,512]{2,1,0:T(8,128)(2,1)S(1)} %behind_outer_1.1.refs_1_), channel_id=1, source_target_pairs={{0,2},{1,3},{2,0},{3,1},{4,6},{5,7},{6,4},{7,5},{8,10},{9,11},{10,... | collective-permute-start | bytes 1179656 | tf_op jit(solution)/shard_map/ppermute | solution.py:223
  44.2 2.7 %collective-permute-start.14 = (bf16[1,192,512]{2,1,0:T(8,128)(2,1)S(1)}, bf16[1,192,512]{2,1,0:T(8,128)(2,1)S(1)}, u32[]{:S(2)}, u32[]{:S(2)}) collective-permute-start(bf16[1,192,512]{2,1,0:T(8,128)(2,1)S(1)} %grad_outer_1.1.refs_3_), channel_id=1, source_target_pairs={{0,2},{1,3},{2,0},{3,1},{4,6},{5,7},{6,4},{7,5},{8,10},{9,11},{10,... | collective-permute-start | bytes 589832 | tf_op jit(solution)/shard_map/ppermute | solution.py:223
  51.4 2.8 %collective-permute-start.13 = (bf16[2,192,512]{2,1,0:T(8,128)(2,1)S(1)}, bf16[2,192,512]{2,1,0:T(8,128)(2,1)S(1)}, u32[]{:S(2)}, u32[]{:S(2)}) collective-permute-start(bf16[2,192,512]{2,1,0:T(8,128)(2,1)S(1)} %ahead_outer_1.1.refs_2_), channel_id=1, source_target_pairs={{0,2},{1,3},{2,0},{3,1},{4,6},{5,7},{6,4},{7,5},{8,10},{9,11},{10,... | collective-permute-start | bytes 1179656 | tf_op jit(solution)/shard_map/ppermute | solution.py:223
  55.4 6.2 %collective-permute-start.17 = (bf16[2,192,512]{2,1,0:T(8,128)(2,1)S(1)}, bf16[2,192,512]{2,1,0:T(8,128)(2,1)S(1)}, u32[]{:S(2)}, u32[]{:S(2)}) collective-permute-start(bf16[2,192,512]{2,1,0:T(8,128)(2,1)S(1)} %behind_outer_2.1.refs_2_), channel_id=1, source_target_pairs={{0,2},{1,3},{2,0},{3,1},{4,6},{5,7},{6,4},{7,5},{8,10},{9,11},{10,... | collective-permute-start | bytes 1179656 | tf_op jit(solution)/shard_map/ppermute | solution.py:223
  62.5 3.5 %collective-permute-start.20 = (bf16[1,192,512]{2,1,0:T(8,128)(2,1)S(1)}, bf16[1,192,512]{2,1,0:T(8,128)(2,1)S(1)}, u32[]{:S(2)}, u32[]{:S(2)}) collective-permute-start(bf16[1,192,512]{2,1,0:T(8,128)(2,1)S(1)} %grad_third_1.1.refs_1_), channel_id=1, source_target_pairs={{0,2},{1,3},{2,0},{3,1},{4,6},{5,7},{6,4},{7,5},{8,10},{9,11},{10,... | collective-permute-start | bytes 589832 | tf_op jit(solution)/shard_map/ppermute | solution.py:223
  66.0 5.2 %collective-permute-done.17.refs_0_.refs_1_ = bf16[2,192,512]{2,1,0:T(8,128)(2,1)S(1)} collective-permute-done((bf16[2,192,512]{2,1,0:T(8,128)(2,1)S(1)}, bf16[2,192,512]{2,1,0:T(8,128)(2,1)S(1)}, u32[]{:S(2)}, u32[]{:S(2)}) %collective-permute-start.17) | collective-permute-done | bytes 393248 | tf_op jit(solution)/shard_map/ppermute | solution.py:223
  72.0 4.9 %collective-permute-start.19 = (bf16[2,192,512]{2,1,0:T(8,128)(2,1)S(1)}, bf16[2,192,512]{2,1,0:T(8,128)(2,1)S(1)}, u32[]{:S(2)}, u32[]{:S(2)}) collective-permute-start(bf16[2,192,512]{2,1,0:T(8,128)(2,1)S(1)} %ahead_outer_2.1.refs_5_), channel_id=1, source_target_pairs={{0,2},{1,3},{2,0},{3,1},{4,6},{5,7},{6,4},{7,5},{8,10},{9,11},{10,... | collective-permute-start | bytes 1179656 | tf_op jit(solution)/shard_map/ppermute | solution.py:223
  77.3 9.1 %collective-permute-start.23 = (bf16[2,192,512]{2,1,0:T(8,128)(2,1)S(1)}, bf16[2,192,512]{2,1,0:T(8,128)(2,1)S(1)}, u32[]{:S(2)}, u32[]{:S(2)}) collective-permute-start(bf16[2,192,512]{2,1,0:T(8,128)(2,1)S(1)} %behind_back_1.1.refs_1_), channel_id=1, source_target_pairs={{0,2},{1,3},{2,0},{3,1},{4,6},{5,7},{6,4},{7,5},{8,10},{9,11},{10,... | collective-permute-start | bytes 1179656 | tf_op jit(solution)/shard_map/ppermute | solution.py:223
  87.2 8.0 %collective-permute-done.23.refs_0_.refs_3_ = bf16[2,192,512]{2,1,0:T(8,128)(2,1)S(1)} collective-permute-done((bf16[2,192,512]{2,1,0:T(8,128)(2,1)S(1)}, bf16[2,192,512]{2,1,0:T(8,128)(2,1)S(1)}, u32[]{:S(2)}, u32[]{:S(2)}) %collective-permute-start.23) | collective-permute-done | bytes 393248 | tf_op jit(solution)/shard_map/ppermute | solution.py:223
  96.0 5.0 %collective-permute-start.24 = (bf16[1,192,512]{2,1,0:T(8,128)(2,1)S(1)}, bf16[1,192,512]{2,1,0:T(8,128)(2,1)S(1)}, u32[]{:S(2)}, u32[]{:S(2)}) collective-permute-start(bf16[1,192,512]{2,1,0:T(8,128)(2,1)S(1)} %ahead_back_1.1.refs_5_), channel_id=1, source_target_pairs={{0,2},{1,3},{2,0},{3,1},{4,6},{5,7},{6,4},{7,5},{8,10},{9,11},{10,... | collective-permute-start | bytes 589832 | tf_op jit(solution)/shard_map/ppermute | solution.py:223
  101.0 2.1 %behind_out_0.1 = (bf16[192,896]{1,0:T(8,128)(2,1)S(1)}, bf16[192,896]{1,0:T(8,128)(2,1)S(1)}) custom-call(bf16[2,192,512]{2,1,0:T(8,128)(2,1)S(1)} %behind_act_0.1.refs_0_.refs_3_, bf16[2,192,512]{2,1,0:T(8,128)(2,1)S(1)} %behind_first_0.1.refs_3_.refs_1_, bf16[2,192,512]{2,1,0:T(8,128)(2,1)S(1)} %collective-permute-done.21.refs_1_.refs_2_, ...), custom_call_target="tpu_custom_call" | custom-call | flops 20000000000 | bytes 1024 | tf_op jit(solution)/shard_map/behind_out_0/pallas_call | solution.py:43
  103.2 6.5 %collective-permute-start.29 = (bf16[2,192,512]{2,1,0:T(8,128)(2,1)S(1)}, bf16[2,192,512]{2,1,0:T(8,128)(2,1)S(1)}, u32[]{:S(2)}, u32[]{:S(2)}) collective-permute-start(bf16[2,192,512]{2,1,0:T(8,128)(2,1)S(1)} %behind_back_2.1.refs_1_), channel_id=1, source_target_pairs={{0,2},{1,3},{2,0},{3,1},{4,6},{5,7},{6,4},{7,5},{8,10},{9,11},{10,... | collective-permute-start | bytes 1179656 | tf_op jit(solution)/shard_map/ppermute | solution.py:223
  111.6 5.0 %collective-permute-start.28 = (bf16[1,192,512]{2,1,0:T(8,128)(2,1)S(1)}, bf16[1,192,512]{2,1,0:T(8,128)(2,1)S(1)}, u32[]{:S(2)}, u32[]{:S(2)}) collective-permute-start(bf16[1,192,512]{2,1,0:T(8,128)(2,1)S(1)} %ahead_back_2.1.refs_2_), channel_id=1, source_target_pairs={{0,2},{1,3},{2,0},{3,1},{4,6},{5,7},{6,4},{7,5},{8,10},{9,11},{10,... | collective-permute-start | bytes 589832 | tf_op jit(solution)/shard_map/ppermute | solution.py:223
  116.6 7.0 %collective-permute-start.34 = (bf16[192,896]{1,0:T(8,128)(2,1)S(1)}, bf16[192,896]{1,0:T(8,128)(2,1)S(1)}, u32[]{:S(2)}, u32[]{:S(2)}) collective-permute-start(bf16[192,896]{1,0:T(8,128)(2,1)S(1)} %behind_shares.1.refs_5_), channel_id=1, source_target_pairs={{8,0},{9,1},{10,2},{11,3},{12,4},{13,5},{14,6},{15,7},{16,8},{17,9... | collective-permute-start | bytes 1032200 | tf_op jit(solution)/shard_map/ppermute | solution.py:247
  130.5 4.5 %collective-permute-start.32 = (bf16[192,896]{1,0:T(8,128)(2,1)S(1)}, bf16[192,896]{1,0:T(8,128)(2,1)S(1)}, u32[]{:S(2)}, u32[]{:S(2)}) collective-permute-start(bf16[192,896]{1,0:T(8,128)(2,1)S(1)} %get-tuple-element.15.refs_2_), channel_id=1, source_target_pairs={{0,9},{1,8},{2,11},{3,10},{4,13},{5,12},{6,15},{7,14},{8,17},{9,16... | collective-permute-start | bytes 1032200 | tf_op jit(solution)/shard_map/ppermute | solution.py:247
  135.1 2.6 %collective-permute-start.31 = (bf16[192,896]{1,0:T(8,128)(2,1)S(1)}, bf16[192,896]{1,0:T(8,128)(2,1)S(1)}, u32[]{:S(2)}, u32[]{:S(2)}) collective-permute-start(bf16[192,896]{1,0:T(8,128)(2,1)S(1)} %ahead_shares.1.refs_3_), channel_id=1, source_target_pairs={{0,8},{1,9},{2,10},{3,11},{4,12},{5,13},{6,14},{7,15},{8,16},{9,17... | collective-permute-start | bytes 1032200 | tf_op jit(solution)/shard_map/ppermute | solution.py:247
  140.6 2.3 %collective-permute-done.31.refs_0_ = bf16[192,896]{1,0:T(8,128)(2,1)S(1)} collective-permute-done((bf16[192,896]{1,0:T(8,128)(2,1)S(1)}, bf16[192,896]{1,0:T(8,128)(2,1)S(1)}, u32[]{:S(2)}, u32[]{:S(2)}) %collective-permute-start.31) | collective-permute-done | bytes 344096 | tf_op jit(solution)/shard_map/ppermute | solution.py:247
  142.9 3.7 %collective-permute-done.33.refs_2_ = bf16[192,896]{1,0:T(8,128)(2,1)S(1)} collective-permute-done((bf16[192,896]{1,0:T(8,128)(2,1)S(1)}, bf16[192,896]{1,0:T(8,128)(2,1)S(1)}, u32[]{:S(2)}, u32[]{:S(2)}) %collective-permute-start.33) | collective-permute-done | bytes 344096 | tf_op jit(solution)/shard_map/ppermute | solution.py:247
  (126 shorter events, 42.7 us)
Async XLA Ops:
  3.9 16.0 %collective-permute-start.3 = (bf16[192,896]{1,0:T(8,128)(2,1)S(1)}, bf16[192,896]{1,0:T(8,128)(2,1)S(1)}, u32[]{:S(2)}, u32[]{:S(2)}) collective-permute-start(bf16[192,896]{1,0:T(8,128)(2,1)S(1)} %grad_rows_0.1.refs_1_.refs_0_), channel_id=1, source_target_pairs={{0,1},{1,0},{2,3},{3,2},{4,5},{5,4},{6,7},{7,6},{8,9},{9,8},{10,11... | collective-permute-start | bytes 1032200 | tf_op jit(solution)/shard_map/ppermute | solution.py:238
  5.0 21.4 %collective-permute-start = (bf16[192,896]{1,0:T(8,128)(2,1)S(1)}, bf16[192,896]{1,0:T(8,128)(2,1)S(1)}, u32[]{:S(2)}, u32[]{:S(2)}) collective-permute-start(bf16[192,896]{1,0:T(8,128)(2,1)S(1)} %ahead_rows_0.1.refs_3_.refs_0_), channel_id=1, source_target_pairs={{0,1},{1,0},{2,3},{3,2},{4,5},{5,4},{6,7},{7,6},{8,9},{9,8},{10,11... | collective-permute-start | bytes 1032200 | tf_op jit(solution)/shard_map/ppermute | solution.py:238
  17.4 11.7 %collective-permute-start.5 = (bf16[2,192,512]{2,1,0:T(8,128)(2,1)S(1)}, bf16[2,192,512]{2,1,0:T(8,128)(2,1)S(1)}, u32[]{:S(2)}, u32[]{:S(2)}) collective-permute-start(bf16[2,192,512]{2,1,0:T(8,128)(2,1)S(1)} %behind_far_0.1.refs_1_.refs_0_), channel_id=1, source_target_pairs={{0,2},{1,3},{2,0},{3,1},{4,6},{5,7},{6,4},{7,5},{8,10},{9,11},{10,... | collective-permute-start | bytes 1179656 | tf_op jit(solution)/shard_map/ppermute | solution.py:223
  18.6 15.2 %collective-permute-start.2 = (bf16[192,896]{1,0:T(8,128)(2,1)S(1)}, bf16[192,896]{1,0:T(8,128)(2,1)S(1)}, u32[]{:S(2)}, u32[]{:S(2)}) collective-permute-start(bf16[192,896]{1,0:T(8,128)(2,1)S(1)} %behind_rows_1.1.refs_3_.refs_0_.refs_2_), channel_id=1, source_target_pairs={{0,1},{1,0},{2,3},{3,2},{4,5},{5,4},{6,7},{7,6},{8,9},{9,8},{10,11... | collective-permute-start | bytes 1032200 | tf_op jit(solution)/shard_map/ppermute | solution.py:238
  20.7 10.5 %collective-permute-start.4 = (bf16[1,192,512]{2,1,0:T(8,128)(2,1)S(1)}, bf16[1,192,512]{2,1,0:T(8,128)(2,1)S(1)}, u32[]{:S(2)}, u32[]{:S(2)}) collective-permute-start(bf16[1,192,512]{2,1,0:T(8,128)(2,1)S(1)} %grad_far_0.1.refs_3_.refs_0_), channel_id=1, source_target_pairs={{0,2},{1,3},{2,0},{3,1},{4,6},{5,7},{6,4},{7,5},{8,10},{9,11},{10,... | collective-permute-start | bytes 589832 | tf_op jit(solution)/shard_map/ppermute | solution.py:223
  27.8 13.9 %collective-permute-start.10 = (bf16[2,192,512]{2,1,0:T(8,128)(2,1)S(1)}, bf16[2,192,512]{2,1,0:T(8,128)(2,1)S(1)}, u32[]{:S(2)}, u32[]{:S(2)}) collective-permute-start(bf16[2,192,512]{2,1,0:T(8,128)(2,1)S(1)} %ahead_far_0.1.refs_2_.refs_0_), channel_id=1, source_target_pairs={{0,2},{1,3},{2,0},{3,1},{4,6},{5,7},{6,4},{7,5},{8,10},{9,11},{10,... | collective-permute-start | bytes 1179656 | tf_op jit(solution)/shard_map/ppermute | solution.py:223
  29.9 12.5 %collective-permute-start.9 = (bf16[192,896]{1,0:T(8,128)(2,1)S(1)}, bf16[192,896]{1,0:T(8,128)(2,1)S(1)}, u32[]{:S(2)}, u32[]{:S(2)}) collective-permute-start(bf16[192,896]{1,0:T(8,128)(2,1)S(1)} %grad_rows_1.1.refs_2_.refs_0_), channel_id=1, source_target_pairs={{0,1},{1,0},{2,3},{3,2},{4,5},{5,4},{6,7},{7,6},{8,9},{9,8},{10,11... | collective-permute-start | bytes 1032200 | tf_op jit(solution)/shard_map/ppermute | solution.py:238
  31.2 12.9 %collective-permute-start.11 = (bf16[1,192,512]{2,1,0:T(8,128)(2,1)S(1)}, bf16[1,192,512]{2,1,0:T(8,128)(2,1)S(1)}, u32[]{:S(2)}, u32[]{:S(2)}) collective-permute-start(bf16[1,192,512]{2,1,0:T(8,128)(2,1)S(1)} %grad_middle_0.1.refs_3_), channel_id=1, source_target_pairs={{0,0},{1,1},{2,4},{3,5},{4,2},{5,3},{6,6},{7,7},{8,8},{9,9},{10,12... | collective-permute-start | bytes 589832 | tf_op jit(solution)/shard_map/ppermute | solution.py:223
  37.8 11.1 %collective-permute-start.8 = (bf16[2,192,512]{2,1,0:T(8,128)(2,1)S(1)}, bf16[2,192,512]{2,1,0:T(8,128)(2,1)S(1)}, u32[]{:S(2)}, u32[]{:S(2)}) collective-permute-start(bf16[2,192,512]{2,1,0:T(8,128)(2,1)S(1)} %behind_outer_1.1.refs_1_), channel_id=1, source_target_pairs={{0,2},{1,3},{2,0},{3,1},{4,6},{5,7},{6,4},{7,5},{8,10},{9,11},{10,... | collective-permute-start | bytes 1179656 | tf_op jit(solution)/shard_map/ppermute | solution.py:223
  44.2 10.1 %collective-permute-start.14 = (bf16[1,192,512]{2,1,0:T(8,128)(2,1)S(1)}, bf16[1,192,512]{2,1,0:T(8,128)(2,1)S(1)}, u32[]{:S(2)}, u32[]{:S(2)}) collective-permute-start(bf16[1,192,512]{2,1,0:T(8,128)(2,1)S(1)} %grad_outer_1.1.refs_3_), channel_id=1, source_target_pairs={{0,2},{1,3},{2,0},{3,1},{4,6},{5,7},{6,4},{7,5},{8,10},{9,11},{10,... | collective-permute-start | bytes 589832 | tf_op jit(solution)/shard_map/ppermute | solution.py:223
  55.4 15.8 %collective-permute-start.17 = (bf16[2,192,512]{2,1,0:T(8,128)(2,1)S(1)}, bf16[2,192,512]{2,1,0:T(8,128)(2,1)S(1)}, u32[]{:S(2)}, u32[]{:S(2)}) collective-permute-start(bf16[2,192,512]{2,1,0:T(8,128)(2,1)S(1)} %behind_outer_2.1.refs_2_), channel_id=1, source_target_pairs={{0,2},{1,3},{2,0},{3,1},{4,6},{5,7},{6,4},{7,5},{8,10},{9,11},{10,... | collective-permute-start | bytes 1179656 | tf_op jit(solution)/shard_map/ppermute | solution.py:223
  61.6 10.3 %collective-permute-start.16 = (bf16[2,192,512]{2,1,0:T(8,128)(2,1)S(1)}, bf16[2,192,512]{2,1,0:T(8,128)(2,1)S(1)}, u32[]{:S(2)}, u32[]{:S(2)}) collective-permute-start(bf16[2,192,512]{2,1,0:T(8,128)(2,1)S(1)} %ahead_middle_1.1.refs_2_), channel_id=1, source_target_pairs={{0,0},{1,1},{2,4},{3,5},{4,2},{5,3},{6,6},{7,7},{8,8},{9,9},{10,12... | collective-permute-start | bytes 1179656 | tf_op jit(solution)/shard_map/ppermute | solution.py:223
  62.5 14.4 %collective-permute-start.20 = (bf16[1,192,512]{2,1,0:T(8,128)(2,1)S(1)}, bf16[1,192,512]{2,1,0:T(8,128)(2,1)S(1)}, u32[]{:S(2)}, u32[]{:S(2)}) collective-permute-start(bf16[1,192,512]{2,1,0:T(8,128)(2,1)S(1)} %grad_third_1.1.refs_1_), channel_id=1, source_target_pairs={{0,2},{1,3},{2,0},{3,1},{4,6},{5,7},{6,4},{7,5},{8,10},{9,11},{10,... | collective-permute-start | bytes 589832 | tf_op jit(solution)/shard_map/ppermute | solution.py:223
  72.0 14.3 %collective-permute-start.19 = (bf16[2,192,512]{2,1,0:T(8,128)(2,1)S(1)}, bf16[2,192,512]{2,1,0:T(8,128)(2,1)S(1)}, u32[]{:S(2)}, u32[]{:S(2)}) collective-permute-start(bf16[2,192,512]{2,1,0:T(8,128)(2,1)S(1)} %ahead_outer_2.1.refs_5_), channel_id=1, source_target_pairs={{0,2},{1,3},{2,0},{3,1},{4,6},{5,7},{6,4},{7,5},{8,10},{9,11},{10,... | collective-permute-start | bytes 1179656 | tf_op jit(solution)/shard_map/ppermute | solution.py:223
  77.3 17.9 %collective-permute-start.23 = (bf16[2,192,512]{2,1,0:T(8,128)(2,1)S(1)}, bf16[2,192,512]{2,1,0:T(8,128)(2,1)S(1)}, u32[]{:S(2)}, u32[]{:S(2)}) collective-permute-start(bf16[2,192,512]{2,1,0:T(8,128)(2,1)S(1)} %behind_back_1.1.refs_1_), channel_id=1, source_target_pairs={{0,2},{1,3},{2,0},{3,1},{4,6},{5,7},{6,4},{7,5},{8,10},{9,11},{10,... | collective-permute-start | bytes 1179656 | tf_op jit(solution)/shard_map/ppermute | solution.py:223
  96.0 13.7 %collective-permute-start.24 = (bf16[1,192,512]{2,1,0:T(8,128)(2,1)S(1)}, bf16[1,192,512]{2,1,0:T(8,128)(2,1)S(1)}, u32[]{:S(2)}, u32[]{:S(2)}) collective-permute-start(bf16[1,192,512]{2,1,0:T(8,128)(2,1)S(1)} %ahead_back_1.1.refs_5_), channel_id=1, source_target_pairs={{0,2},{1,3},{2,0},{3,1},{4,6},{5,7},{6,4},{7,5},{8,10},{9,11},{10,... | collective-permute-start | bytes 589832 | tf_op jit(solution)/shard_map/ppermute | solution.py:223
  103.0 13.5 %collective-permute-start.30 = (bf16[192,896]{1,0:T(8,128)(2,1)S(1)}, bf16[192,896]{1,0:T(8,128)(2,1)S(1)}, u32[]{:S(2)}, u32[]{:S(2)}) collective-permute-start(bf16[192,896]{1,0:T(8,128)(2,1)S(1)} %get-tuple-element.10.refs_1_), channel_id=1, source_target_pairs={{0,1},{1,0},{2,3},{3,2},{4,5},{5,4},{6,7},{7,6},{8,9},{9,8},{10,11... | collective-permute-start | bytes 1032200 | tf_op jit(solution)/shard_map/ppermute | solution.py:238
  103.2 20.4 %collective-permute-start.29 = (bf16[2,192,512]{2,1,0:T(8,128)(2,1)S(1)}, bf16[2,192,512]{2,1,0:T(8,128)(2,1)S(1)}, u32[]{:S(2)}, u32[]{:S(2)}) collective-permute-start(bf16[2,192,512]{2,1,0:T(8,128)(2,1)S(1)} %behind_back_2.1.refs_1_), channel_id=1, source_target_pairs={{0,2},{1,3},{2,0},{3,1},{4,6},{5,7},{6,4},{7,5},{8,10},{9,11},{10,... | collective-permute-start | bytes 1179656 | tf_op jit(solution)/shard_map/ppermute | solution.py:223
  111.5 23.5 %collective-permute-start.26 = (bf16[192,896]{1,0:T(8,128)(2,1)S(1)}, bf16[192,896]{1,0:T(8,128)(2,1)S(1)}, u32[]{:S(2)}, u32[]{:S(2)}) collective-permute-start(bf16[192,896]{1,0:T(8,128)(2,1)S(1)} %get-tuple-element.12.refs_1_), channel_id=1, source_target_pairs={{0,1},{1,0},{2,3},{3,2},{4,5},{5,4},{6,7},{7,6},{8,9},{9,8},{10,11... | collective-permute-start | bytes 1032200 | tf_op jit(solution)/shard_map/ppermute | solution.py:238
  111.6 17.8 %collective-permute-start.28 = (bf16[1,192,512]{2,1,0:T(8,128)(2,1)S(1)}, bf16[1,192,512]{2,1,0:T(8,128)(2,1)S(1)}, u32[]{:S(2)}, u32[]{:S(2)}) collective-permute-start(bf16[1,192,512]{2,1,0:T(8,128)(2,1)S(1)} %ahead_back_2.1.refs_2_), channel_id=1, source_target_pairs={{0,2},{1,3},{2,0},{3,1},{4,6},{5,7},{6,4},{7,5},{8,10},{9,11},{10,... | collective-permute-start | bytes 589832 | tf_op jit(solution)/shard_map/ppermute | solution.py:223
  116.6 21.1 %collective-permute-start.34 = (bf16[192,896]{1,0:T(8,128)(2,1)S(1)}, bf16[192,896]{1,0:T(8,128)(2,1)S(1)}, u32[]{:S(2)}, u32[]{:S(2)}) collective-permute-start(bf16[192,896]{1,0:T(8,128)(2,1)S(1)} %behind_shares.1.refs_5_), channel_id=1, source_target_pairs={{8,0},{9,1},{10,2},{11,3},{12,4},{13,5},{14,6},{15,7},{16,8},{17,9... | collective-permute-start | bytes 1032200 | tf_op jit(solution)/shard_map/ppermute | solution.py:247
  125.5 14.1 %collective-permute-start.35 = (bf16[192,896]{1,0:T(8,128)(2,1)S(1)}, bf16[192,896]{1,0:T(8,128)(2,1)S(1)}, u32[]{:S(2)}, u32[]{:S(2)}) collective-permute-start(bf16[192,896]{1,0:T(8,128)(2,1)S(1)} %get-tuple-element.14.refs_6_), channel_id=1, source_target_pairs={{8,1},{9,0},{10,3},{11,2},{12,5},{13,4},{14,7},{15,6},{16,9},{17,8... | collective-permute-start | bytes 1032200 | tf_op jit(solution)/shard_map/ppermute | solution.py:247
  127.5 12.2 %collective-permute-start.36 = (bf16[192,896]{1,0:T(8,128)(2,1)S(1)}, bf16[192,896]{1,0:T(8,128)(2,1)S(1)}, u32[]{:S(2)}, u32[]{:S(2)}) collective-permute-start(bf16[192,896]{1,0:T(8,128)(2,1)S(1)} %get-tuple-element.17), channel_id=1, source_target_pairs={{8,0},{9,1},{10,2},{11,3},{12,4},{13,5},{14,6},{15,7},{16,8},{17,9... | collective-permute-start | bytes 1032200 | tf_op jit(solution)/shard_map/ppermute | solution.py:247
  130.5 12.5 %collective-permute-start.32 = (bf16[192,896]{1,0:T(8,128)(2,1)S(1)}, bf16[192,896]{1,0:T(8,128)(2,1)S(1)}, u32[]{:S(2)}, u32[]{:S(2)}) collective-permute-start(bf16[192,896]{1,0:T(8,128)(2,1)S(1)} %get-tuple-element.15.refs_2_), channel_id=1, source_target_pairs={{0,9},{1,8},{2,11},{3,10},{4,13},{5,12},{6,15},{7,14},{8,17},{9,16... | collective-permute-start | bytes 1032200 | tf_op jit(solution)/shard_map/ppermute | solution.py:247
  (24 other events, 138.9 us)

commit v14 on v13

--- a/solution.py
+++ b/solution.py
@@ -55,6 +55,10 @@
 
 def cut_kernel(rows, out):
     out[...] = rows[...]
+
+
+def touch_kernel(gates, downs, out):
+    out[...] = gates[0, :16, :128] + downs[0, :16, :128]
 
 
 def cut_first_kernel(value, out):
@@ -276,6 +280,10 @@
 
         def fetch(self, c):
             size, width = height // PIECES, self.rows.shape[1]
+            if c == 0 and self.name == "behind":
+                rows = self.rows[:size]
+                self.pairs[c] = rows, swapped(rows)
+                return
             rows = call(
                 cut_kernel,
                 SMALL if c else ROWS,
@@ -405,53 +413,64 @@
         shape = (height, operands[0].shape[1])
         return kernel_call(f"{chain.name}_result", result_kernel, SMALL, operands, shape)[None]
 
-    for chain in (behind, grad, ahead):
+    for chain in (behind, ahead, grad):
         chain.fetch(0)
+    weights_spec = pl.BlockSpec(memory_space=pltpu.VMEM)
+    touched = call(
+        touch_kernel,
+        ROWS,
+        (gates, downs),
+        list(recent),
+        jax.ShapeDtypeStruct((16, 128), BF16),
+        in_specs=[weights_spec, weights_spec],
+        name="touch",
+    )
+    recent[:] = [touched]
     behind.far_product(0)
     behind.first_hop(0)
     behind.fetch(1)
+    ahead.far_product(0)
+    ahead.first_hop(0)
     grad.far_product(0)
     grad.first_hop(0)
-    ahead.far_product(0)
-    ahead.first_hop(0)
     behind.middle_sum(0)
+    ahead.fetch(1)
+    behind.far_product(1)
+    behind.near_products()
+    ahead.middle_sum(0)
+    behind.merged_hop(1, behind.far[1])
     grad.fetch(1)
     grad.middle_sum(0)
-    behind.far_product(1)
-    behind.near_products()
-    behind.merged_hop(1, behind.far[1])
-    ahead.fetch(1)
-    ahead.middle_sum(0)
+    ahead.far_product(1)
+    ahead.near_products()
+    ahead.merged_hop(1, ahead.far[1])
+    behind.middle_sum(1)
     grad.far_product(1)
     grad.near_products()
     grad.merged_hop(1, grad.far[1])
-    ahead.far_product(1)
-    behind.middle_sum(1)
-    ahead.near_products()
-    ahead.merged_hop(1, ahead.far[1])
+    ahead.middle_sum(1)
     grad.middle_sum(1)
     activate_behind(0)
     behind.merged_hop(2, behind.act[0])
-    ahead.middle_sum(1)
     activate_ahead(0)
+    ahead.merged_hop(2, ahead.act[0])
     grad.last_third_hop()
     behind.middle_pass(0)
-    ahead.merged_hop(2, ahead.act[0])
+    ahead.middle_pass(0)
+    activate_ahead(1)
     activate_behind(1)
     behind.outer_pass(1)
-    ahead.middle_pass(0)
-    activate_ahead(1)
+    ahead.outer_pass(1)
     behind.middle_pass(1)
-    ahead.outer_pass(1)
+    ahead.middle_pass(1)
     finish_first(behind)
+    finish_first(ahead)
     behind.outer_pass(2)
-    ahead.middle_pass(1)
-    finish_first(ahead)
     ahead.outer_pass(2)
     send_first(behind)
+    send_first(ahead)
     finish_last(behind)
     finish_last(ahead)
-    send_first(ahead)
     behind_sent = result(behind)
     ahead_sent = result(ahead)
     return ahead_sent, behind_sent

time: 149 us -> 144 us (0.966)
  local copies, waits for them, and re-layouts: 5.87 us -> 17.2 us
  starting transfers between devices: 86.3 us -> 76.4 us
  waiting for transfers between devices: 32 us -> 26.4 us
  Pallas kernels: 23.2 us -> 21 us
    ppermute x23, starting transfers between devices: 58.9 us -> 43 us  [between(): return lax.ppermute(value, 'expert', pairs)]
    unnamed x22 -> x34, local copies, waits for them, and re-layouts: 5.31 us -> 15.1 us
    ppermute x8, waiting for transfers between devices: 12.7 us -> 5.39 us  [swapped(): return lax.ppermute(value, 'expert', [(i, i ^ 1) for i in range(devices)])]
    ppermute x6, starting transfers between devices: 19.9 us -> 25.3 us  [to_section(): return lax.ppermute(value, ('section', 'expert'), pairs)]
    ppermute x23, waiting for transfers between devices: 13.3 us -> 16 us  [between(): return lax.ppermute(value, 'expert', pairs)]
    pallas_call x47, Pallas kernels: 23.2 us -> 21 us  [call(): pl.pallas_call(run, compiler_params=pltpu.CompilerParams(vmem_limit_bytes...]
  transfers between devices with their start and end apart: 37 -> 37, of which waited for: 8 -> 12; matrix products, arithmetic and copies ran while one was open for 0% -> 1% of each run, Pallas kernels for 15% -> 14%
where the time goes in v14:
time: 144 us; the launch traced here: 142 us
  starting transfers between devices  76.4 us (53%)
  waiting for transfers between devices  26.4 us (18%)
  Pallas kernels  21 us (15%)
  local copies, waits for them, and re-layouts  17.2 us (12%)
    ppermute x23, starting transfers between devices, between(): return lax.ppermute(value, 'expert', pairs)  43 us
    ppermute x6, starting transfers between devices, to_section(): return lax.ppermute(value, ('section', 'expert'), pairs)  25.3 us
    pallas_call x47, Pallas kernels, call(): pl.pallas_call(run, compiler_params=pltpu.CompilerParams(vmem_limit_bytes...  21 us
    ppermute x23, waiting for transfers between devices, between(): return lax.ppermute(value, 'expert', pairs)  16 us
    unnamed x34, local copies, waits for them, and re-layouts  15.1 us
    ppermute x8, starting transfers between devices, swapped(): return lax.ppermute(value, 'expert', [(i, i ^ 1) for i in range(devices)])  8.19 us
    ppermute x8, waiting for transfers between devices, swapped(): return lax.ppermute(value, 'expert', [(i, i ^ 1) for i in range(devices)])  5.39 us
    ppermute x6, waiting for transfers between devices, to_section(): return lax.ppermute(value, ('section', 'expert'), pairs)  4.99 us
  transfers between devices with their start and end apart: 37, of which 12 were waited for; matrix products, arithmetic and copies ran while one was open for 1% of the time, Pallas kernels for 14%

profile of v14, /device:TPU:1, one launch (start us, length us, event | category | flops | bytes accessed | tf_op | source)
XLA Modules:
  0.0 142.3 jit_solution(2005618190982115814)
XLA Ops:
  1.6 2.1 %collective-permute-start.1 = (bf16[192,896]{1,0:T(8,128)(2,1)S(1)}, bf16[192,896]{1,0:T(8,128)(2,1)S(1)}, u32[]{:S(2)}, u32[]{:S(2)}) collective-permute-start(bf16[192,896]{1,0:T(8,128)(2,1)S(1)} %slice_bitcast_fusion.refs_0_), channel_id=1, source_target_pairs={{0,1},{1,0},{2,3},{3,2},{4,5},{5,4},{6,7},{7,6},{8,9},{9,8},{10,11... | collective-permute-start | bytes 1032200 | tf_op jit(solution)/shard_map/ppermute | solution.py:242
  11.6 3.1 %copy-done.1 = bf16[1,1,2,1024,1792]{4,3,2,1,0:T(8,128)(2,1)S(1)} copy-done((bf16[1,1,2,1024,1792]{4,3,2,1,0:T(8,128)(2,1)S(1)}, bf16[1,1,2,1024,1792]{4,3,2,1,0:T(8,128)(2,1)}, u32[]{:S(2)}) %copy-start.1) | copy-done | bytes 7340056
  18.9 3.1 %copy-done.2 = bf16[1,1,2,1024,1792]{4,3,2,1,0:T(8,128)(2,1)S(1)} copy-done((bf16[1,1,2,1024,1792]{4,3,2,1,0:T(8,128)(2,1)S(1)}, bf16[1,1,2,1024,1792]{4,3,2,1,0:T(8,128)(2,1)}, u32[]{:S(2)}) %copy-start.2) | copy-done | bytes 7340056
  30.6 3.0 %collective-permute-done.6.refs_1_.refs_3_ = bf16[192,896]{1,0:T(8,128)(2,1)S(1)} collective-permute-done((bf16[192,896]{1,0:T(8,128)(2,1)S(1)}, bf16[192,896]{1,0:T(8,128)(2,1)S(1)}, u32[]{:S(2)}, u32[]{:S(2)}) %collective-permute-start.6) | collective-permute-done | bytes 344096 | tf_op jit(solution)/shard_map/ppermute | solution.py:242
  37.6 3.8 %collective-permute-start.11 = (bf16[2,192,512]{2,1,0:T(8,128)(2,1)S(1)}, bf16[2,192,512]{2,1,0:T(8,128)(2,1)S(1)}, u32[]{:S(2)}, u32[]{:S(2)}) collective-permute-start(bf16[2,192,512]{2,1,0:T(8,128)(2,1)S(1)} %behind_outer_1.1.refs_1_), channel_id=1, source_target_pairs={{0,2},{1,3},{2,0},{3,1},{4,6},{5,7},{6,4},{7,5},{8,10},{9,11},{10,... | collective-permute-start | bytes 1179656 | tf_op jit(solution)/shard_map/ppermute | solution.py:227
  50.8 3.3 %collective-permute-start.14 = (bf16[1,192,512]{2,1,0:T(8,128)(2,1)S(1)}, bf16[1,192,512]{2,1,0:T(8,128)(2,1)S(1)}, u32[]{:S(2)}, u32[]{:S(2)}) collective-permute-start(bf16[1,192,512]{2,1,0:T(8,128)(2,1)S(1)} %grad_outer_1.1.refs_2_), channel_id=1, source_target_pairs={{0,2},{1,3},{2,0},{3,1},{4,6},{5,7},{6,4},{7,5},{8,10},{9,11},{10,... | collective-permute-start | bytes 589832 | tf_op jit(solution)/shard_map/ppermute | solution.py:227
  55.8 3.7 %collective-permute-done.14.refs_1_.refs_3_ = bf16[1,192,512]{2,1,0:T(8,128)(2,1)S(1)} collective-permute-done((bf16[1,192,512]{2,1,0:T(8,128)(2,1)S(1)}, bf16[1,192,512]{2,1,0:T(8,128)(2,1)S(1)}, u32[]{:S(2)}, u32[]{:S(2)}) %collective-permute-start.14) | collective-permute-done | bytes 196640 | tf_op jit(solution)/shard_map/ppermute | solution.py:227
  60.6 2.6 %collective-permute-start.18 = (bf16[2,192,512]{2,1,0:T(8,128)(2,1)S(1)}, bf16[2,192,512]{2,1,0:T(8,128)(2,1)S(1)}, u32[]{:S(2)}, u32[]{:S(2)}) collective-permute-start(bf16[2,192,512]{2,1,0:T(8,128)(2,1)S(1)} %behind_outer_2.1.refs_2_), channel_id=1, source_target_pairs={{0,2},{1,3},{2,0},{3,1},{4,6},{5,7},{6,4},{7,5},{8,10},{9,11},{10,... | collective-permute-start | bytes 1179656 | tf_op jit(solution)/shard_map/ppermute | solution.py:227
  63.4 4.7 %collective-permute-start.17 = (bf16[2,192,512]{2,1,0:T(8,128)(2,1)S(1)}, bf16[2,192,512]{2,1,0:T(8,128)(2,1)S(1)}, u32[]{:S(2)}, u32[]{:S(2)}) collective-permute-start(bf16[2,192,512]{2,1,0:T(8,128)(2,1)S(1)} %ahead_outer_2.1.refs_2_), channel_id=1, source_target_pairs={{0,2},{1,3},{2,0},{3,1},{4,6},{5,7},{6,4},{7,5},{8,10},{9,11},{10,... | collective-permute-start | bytes 1179656 | tf_op jit(solution)/shard_map/ppermute | solution.py:227
  68.2 4.0 %collective-permute-start.21 = (bf16[1,192,512]{2,1,0:T(8,128)(2,1)S(1)}, bf16[1,192,512]{2,1,0:T(8,128)(2,1)S(1)}, u32[]{:S(2)}, u32[]{:S(2)}) collective-permute-start(bf16[1,192,512]{2,1,0:T(8,128)(2,1)S(1)} %grad_third_1.1.refs_1_), channel_id=1, source_target_pairs={{0,2},{1,3},{2,0},{3,1},{4,6},{5,7},{6,4},{7,5},{8,10},{9,11},{10,... | collective-permute-start | bytes 589832 | tf_op jit(solution)/shard_map/ppermute | solution.py:227
  73.0 2.7 %collective-permute-done.17.refs_0_.refs_1_ = bf16[2,192,512]{2,1,0:T(8,128)(2,1)S(1)} collective-permute-done((bf16[2,192,512]{2,1,0:T(8,128)(2,1)S(1)}, bf16[2,192,512]{2,1,0:T(8,128)(2,1)S(1)}, u32[]{:S(2)}, u32[]{:S(2)}) %collective-permute-start.17) | collective-permute-done | bytes 393248 | tf_op jit(solution)/shard_map/ppermute | solution.py:227
  76.5 3.4 %collective-permute-done.21.refs_3_ = bf16[1,192,512]{2,1,0:T(8,128)(2,1)S(1)} collective-permute-done((bf16[1,192,512]{2,1,0:T(8,128)(2,1)S(1)}, bf16[1,192,512]{2,1,0:T(8,128)(2,1)S(1)}, u32[]{:S(2)}, u32[]{:S(2)}) %collective-permute-start.21) | collective-permute-done | bytes 196640 | tf_op jit(solution)/shard_map/ppermute | solution.py:227
  80.2 3.1 %collective-permute-start.24 = (bf16[2,192,512]{2,1,0:T(8,128)(2,1)S(1)}, bf16[2,192,512]{2,1,0:T(8,128)(2,1)S(1)}, u32[]{:S(2)}, u32[]{:S(2)}) collective-permute-start(bf16[2,192,512]{2,1,0:T(8,128)(2,1)S(1)} %behind_back_1.1.refs_2_), channel_id=1, source_target_pairs={{0,2},{1,3},{2,0},{3,1},{4,6},{5,7},{6,4},{7,5},{8,10},{9,11},{10,... | collective-permute-start | bytes 1179656 | tf_op jit(solution)/shard_map/ppermute | solution.py:227
  83.4 2.8 %collective-permute-start.23 = (bf16[1,192,512]{2,1,0:T(8,128)(2,1)S(1)}, bf16[1,192,512]{2,1,0:T(8,128)(2,1)S(1)}, u32[]{:S(2)}, u32[]{:S(2)}) collective-permute-start(bf16[1,192,512]{2,1,0:T(8,128)(2,1)S(1)} %ahead_back_1.1.refs_1_), channel_id=1, source_target_pairs={{0,2},{1,3},{2,0},{3,1},{4,6},{5,7},{6,4},{7,5},{8,10},{9,11},{10,... | collective-permute-start | bytes 589832 | tf_op jit(solution)/shard_map/ppermute | solution.py:227
  86.2 4.0 %collective-permute-done.24.refs_0_.refs_3_ = bf16[2,192,512]{2,1,0:T(8,128)(2,1)S(1)} collective-permute-done((bf16[2,192,512]{2,1,0:T(8,128)(2,1)S(1)}, bf16[2,192,512]{2,1,0:T(8,128)(2,1)S(1)}, u32[]{:S(2)}, u32[]{:S(2)}) %collective-permute-start.24) | collective-permute-done | bytes 393248 | tf_op jit(solution)/shard_map/ppermute | solution.py:227
  93.0 2.1 %behind_out_0.1 = (bf16[192,896]{1,0:T(8,128)(2,1)S(1)}, bf16[192,896]{1,0:T(8,128)(2,1)S(1)}) custom-call(bf16[2,192,512]{2,1,0:T(8,128)(2,1)S(1)} %behind_act_0.1.refs_0_.refs_3_, bf16[2,192,512]{2,1,0:T(8,128)(2,1)S(1)} %behind_first_0.1.refs_1_, bf16[2,192,512]{2,1,0:T(8,128)(2,1)S(1)} %collective-permute-done.22.refs_1_.refs_2_, ...), custom_call_target="tpu_custom_call" | custom-call | flops 20000000000 | bytes 1024 | tf_op jit(solution)/shard_map/behind_out_0/pallas_call | solution.py:43
  97.7 5.8 %collective-permute-start.31 = (bf16[2,192,512]{2,1,0:T(8,128)(2,1)S(1)}, bf16[2,192,512]{2,1,0:T(8,128)(2,1)S(1)}, u32[]{:S(2)}, u32[]{:S(2)}) collective-permute-start(bf16[2,192,512]{2,1,0:T(8,128)(2,1)S(1)} %behind_back_2.1.refs_1_), channel_id=1, source_target_pairs={{0,2},{1,3},{2,0},{3,1},{4,6},{5,7},{6,4},{7,5},{8,10},{9,11},{10,... | collective-permute-start | bytes 1179656 | tf_op jit(solution)/shard_map/ppermute | solution.py:227
  103.7 9.8 %collective-permute-start.34 = (bf16[192,896]{1,0:T(8,128)(2,1)S(1)}, bf16[192,896]{1,0:T(8,128)(2,1)S(1)}, u32[]{:S(2)}, u32[]{:S(2)}) collective-permute-start(bf16[192,896]{1,0:T(8,128)(2,1)S(1)} %behind_shares.1.refs_2_), channel_id=1, source_target_pairs={{8,0},{9,1},{10,2},{11,3},{12,4},{13,5},{14,6},{15,7},{16,8},{17,9... | collective-permute-start | bytes 1032200 | tf_op jit(solution)/shard_map/ppermute | solution.py:251
  115.6 6.0 %collective-permute-start.35 = (bf16[192,896]{1,0:T(8,128)(2,1)S(1)}, bf16[192,896]{1,0:T(8,128)(2,1)S(1)}, u32[]{:S(2)}, u32[]{:S(2)}) collective-permute-start(bf16[192,896]{1,0:T(8,128)(2,1)S(1)} %get-tuple-element.14.refs_6_), channel_id=1, source_target_pairs={{8,1},{9,0},{10,3},{11,2},{12,5},{13,4},{14,7},{15,6},{16,9},{17,8... | collective-permute-start | bytes 1032200 | tf_op jit(solution)/shard_map/ppermute | solution.py:251
  121.6 1.9 %collective-permute-start.36 = (bf16[192,896]{1,0:T(8,128)(2,1)S(1)}, bf16[192,896]{1,0:T(8,128)(2,1)S(1)}, u32[]{:S(2)}, u32[]{:S(2)}) collective-permute-start(bf16[192,896]{1,0:T(8,128)(2,1)S(1)} %get-tuple-element.17), channel_id=1, source_target_pairs={{8,0},{9,1},{10,2},{11,3},{12,4},{13,5},{14,6},{15,7},{16,8},{17,9... | collective-permute-start | bytes 1032200 | tf_op jit(solution)/shard_map/ppermute | solution.py:251
  123.7 3.6 %collective-permute-start.29 = (bf16[192,896]{1,0:T(8,128)(2,1)S(1)}, bf16[192,896]{1,0:T(8,128)(2,1)S(1)}, u32[]{:S(2)}, u32[]{:S(2)}) collective-permute-start(bf16[192,896]{1,0:T(8,128)(2,1)S(1)} %ahead_shares.1.refs_5_), channel_id=1, source_target_pairs={{0,8},{1,9},{2,10},{3,11},{4,12},{5,13},{6,14},{7,15},{8,16},{9,17... | collective-permute-start | bytes 1032200 | tf_op jit(solution)/shard_map/ppermute | solution.py:251
  127.4 2.0 %copy-done.5 = bf16[1,1,1024,1792]{3,2,1,0:T(8,128)(2,1)S(1)} copy-done((bf16[1,1,1024,1792]{3,2,1,0:T(8,128)(2,1)S(1)}, bf16[1,1,1024,1792]{3,2,1,0:T(8,128)(2,1)}, u32[]{:S(2)}) %copy-start.5) | copy-done | bytes 3670040
  132.4 1.9 %collective-permute-start.33 = (bf16[192,896]{1,0:T(8,128)(2,1)S(1)}, bf16[192,896]{1,0:T(8,128)(2,1)S(1)}, u32[]{:S(2)}, u32[]{:S(2)}) collective-permute-start(bf16[192,896]{1,0:T(8,128)(2,1)S(1)} %get-tuple-element.16), channel_id=1, source_target_pairs={{0,8},{1,9},{2,10},{3,11},{4,12},{5,13},{6,14},{7,15},{8,16},{9,17... | collective-permute-start | bytes 1032200 | tf_op jit(solution)/shard_map/ppermute | solution.py:251
  135.3 3.7 %collective-permute-done.32.refs_1_ = bf16[192,896]{1,0:T(8,128)(2,1)S(1)} collective-permute-done((bf16[192,896]{1,0:T(8,128)(2,1)S(1)}, bf16[192,896]{1,0:T(8,128)(2,1)S(1)}, u32[]{:S(2)}, u32[]{:S(2)}) %collective-permute-start.32) | collective-permute-done | bytes 344096 | tf_op jit(solution)/shard_map/ppermute | solution.py:251
  (140 shorter events, 54.5 us)
Async XLA Ops:
  1.6 9.9 %collective-permute-start.1 = (bf16[192,896]{1,0:T(8,128)(2,1)S(1)}, bf16[192,896]{1,0:T(8,128)(2,1)S(1)}, u32[]{:S(2)}, u32[]{:S(2)}) collective-permute-start(bf16[192,896]{1,0:T(8,128)(2,1)S(1)} %slice_bitcast_fusion.refs_0_), channel_id=1, source_target_pairs={{0,1},{1,0},{2,3},{3,2},{4,5},{5,4},{6,7},{7,6},{8,9},{9,8},{10,11... | collective-permute-start | bytes 1032200 | tf_op jit(solution)/shard_map/ppermute | solution.py:242
  4.9 14.0 %collective-permute-start = (bf16[192,896]{1,0:T(8,128)(2,1)S(1)}, bf16[192,896]{1,0:T(8,128)(2,1)S(1)}, u32[]{:S(2)}, u32[]{:S(2)}) collective-permute-start(bf16[192,896]{1,0:T(8,128)(2,1)S(1)} %ahead_rows_0.1.refs_1_.refs_0_), channel_id=1, source_target_pairs={{0,1},{1,0},{2,3},{3,2},{4,5},{5,4},{6,7},{7,6},{8,9},{9,8},{10,11... | collective-permute-start | bytes 1032200 | tf_op jit(solution)/shard_map/ppermute | solution.py:242
  6.0 20.3 %collective-permute-start.3 = (bf16[192,896]{1,0:T(8,128)(2,1)S(1)}, bf16[192,896]{1,0:T(8,128)(2,1)S(1)}, u32[]{:S(2)}, u32[]{:S(2)}) collective-permute-start(bf16[192,896]{1,0:T(8,128)(2,1)S(1)} %grad_rows_0.1.refs_2_.refs_0_), channel_id=1, source_target_pairs={{0,1},{1,0},{2,3},{3,2},{4,5},{5,4},{6,7},{7,6},{8,9},{9,8},{10,11... | collective-permute-start | bytes 1032200 | tf_op jit(solution)/shard_map/ppermute | solution.py:242
  16.0 12.4 %collective-permute-start.2 = (bf16[2,192,512]{2,1,0:T(8,128)(2,1)S(1)}, bf16[2,192,512]{2,1,0:T(8,128)(2,1)S(1)}, u32[]{:S(2)}, u32[]{:S(2)}) collective-permute-start(bf16[2,192,512]{2,1,0:T(8,128)(2,1)S(1)} %behind_far_0.1.refs_1_.refs_0_), channel_id=1, source_target_pairs={{0,2},{1,3},{2,0},{3,1},{4,6},{5,7},{6,4},{7,5},{8,10},{9,11},{10,... | collective-permute-start | bytes 1179656 | tf_op jit(solution)/shard_map/ppermute | solution.py:227
  17.3 16.4 %collective-permute-start.6 = (bf16[192,896]{1,0:T(8,128)(2,1)S(1)}, bf16[192,896]{1,0:T(8,128)(2,1)S(1)}, u32[]{:S(2)}, u32[]{:S(2)}) collective-permute-start(bf16[192,896]{1,0:T(8,128)(2,1)S(1)} %behind_rows_1.1.refs_3_.refs_0_.refs_2_), channel_id=1, source_target_pairs={{0,1},{1,0},{2,3},{3,2},{4,5},{5,4},{6,7},{7,6},{8,9},{9,8},{10,11... | collective-permute-start | bytes 1032200 | tf_op jit(solution)/shard_map/ppermute | solution.py:242
  23.3 13.3 %collective-permute-start.8 = (bf16[2,192,512]{2,1,0:T(8,128)(2,1)S(1)}, bf16[2,192,512]{2,1,0:T(8,128)(2,1)S(1)}, u32[]{:S(2)}, u32[]{:S(2)}) collective-permute-start(bf16[2,192,512]{2,1,0:T(8,128)(2,1)S(1)} %ahead_far_0.1.refs_3_.refs_0_), channel_id=1, source_target_pairs={{0,2},{1,3},{2,0},{3,1},{4,6},{5,7},{6,4},{7,5},{8,10},{9,11},{10,... | collective-permute-start | bytes 1179656 | tf_op jit(solution)/shard_map/ppermute | solution.py:227
  27.1 15.6 %collective-permute-start.5 = (bf16[1,192,512]{2,1,0:T(8,128)(2,1)S(1)}, bf16[1,192,512]{2,1,0:T(8,128)(2,1)S(1)}, u32[]{:S(2)}, u32[]{:S(2)}) collective-permute-start(bf16[1,192,512]{2,1,0:T(8,128)(2,1)S(1)} %grad_far_0.1.refs_2_.refs_0_), channel_id=1, source_target_pairs={{0,2},{1,3},{2,0},{3,1},{4,6},{5,7},{6,4},{7,5},{8,10},{9,11},{10,... | collective-permute-start | bytes 589832 | tf_op jit(solution)/shard_map/ppermute | solution.py:227
  28.4 9.0 %collective-permute-start.7 = (bf16[2,192,512]{2,1,0:T(8,128)(2,1)S(1)}, bf16[2,192,512]{2,1,0:T(8,128)(2,1)S(1)}, u32[]{:S(2)}, u32[]{:S(2)}) collective-permute-start(bf16[2,192,512]{2,1,0:T(8,128)(2,1)S(1)} %behind_middle_0.1.refs_1_), channel_id=1, source_target_pairs={{0,0},{1,1},{2,4},{3,5},{4,2},{5,3},{6,6},{7,7},{8,8},{9,9},{10,12... | collective-permute-start | bytes 1179656 | tf_op jit(solution)/shard_map/ppermute | solution.py:227
  29.3 14.1 %collective-permute-start.4 = (bf16[192,896]{1,0:T(8,128)(2,1)S(1)}, bf16[192,896]{1,0:T(8,128)(2,1)S(1)}, u32[]{:S(2)}, u32[]{:S(2)}) collective-permute-start(bf16[192,896]{1,0:T(8,128)(2,1)S(1)} %ahead_rows_1.1.refs_3_.refs_0_.refs_2_), channel_id=1, source_target_pairs={{0,1},{1,0},{2,3},{3,2},{4,5},{5,4},{6,7},{7,6},{8,9},{9,8},{10,11... | collective-permute-start | bytes 1032200 | tf_op jit(solution)/shard_map/ppermute | solution.py:242
  36.8 9.6 %collective-permute-start.9 = (bf16[2,192,512]{2,1,0:T(8,128)(2,1)S(1)}, bf16[2,192,512]{2,1,0:T(8,128)(2,1)S(1)}, u32[]{:S(2)}, u32[]{:S(2)}) collective-permute-start(bf16[2,192,512]{2,1,0:T(8,128)(2,1)S(1)} %ahead_middle_0.1.refs_3_), channel_id=1, source_target_pairs={{0,0},{1,1},{2,4},{3,5},{4,2},{5,3},{6,6},{7,7},{8,8},{9,9},{10,12... | collective-permute-start | bytes 1179656 | tf_op jit(solution)/shard_map/ppermute | solution.py:227
  37.6 10.7 %collective-permute-start.11 = (bf16[2,192,512]{2,1,0:T(8,128)(2,1)S(1)}, bf16[2,192,512]{2,1,0:T(8,128)(2,1)S(1)}, u32[]{:S(2)}, u32[]{:S(2)}) collective-permute-start(bf16[2,192,512]{2,1,0:T(8,128)(2,1)S(1)} %behind_outer_1.1.refs_1_), channel_id=1, source_target_pairs={{0,2},{1,3},{2,0},{3,1},{4,6},{5,7},{6,4},{7,5},{8,10},{9,11},{10,... | collective-permute-start | bytes 1179656 | tf_op jit(solution)/shard_map/ppermute | solution.py:227
  48.4 12.1 %collective-permute-start.15 = (bf16[2,192,512]{2,1,0:T(8,128)(2,1)S(1)}, bf16[2,192,512]{2,1,0:T(8,128)(2,1)S(1)}, u32[]{:S(2)}, u32[]{:S(2)}) collective-permute-start(bf16[2,192,512]{2,1,0:T(8,128)(2,1)S(1)} %behind_middle_1.1.refs_3_), channel_id=1, source_target_pairs={{0,0},{1,1},{2,4},{3,5},{4,2},{5,3},{6,6},{7,7},{8,8},{9,9},{10,12... | collective-permute-start | bytes 1179656 | tf_op jit(solution)/shard_map/ppermute | solution.py:227
  60.6 11.6 %collective-permute-start.18 = (bf16[2,192,512]{2,1,0:T(8,128)(2,1)S(1)}, bf16[2,192,512]{2,1,0:T(8,128)(2,1)S(1)}, u32[]{:S(2)}, u32[]{:S(2)}) collective-permute-start(bf16[2,192,512]{2,1,0:T(8,128)(2,1)S(1)} %behind_outer_2.1.refs_2_), channel_id=1, source_target_pairs={{0,2},{1,3},{2,0},{3,1},{4,6},{5,7},{6,4},{7,5},{8,10},{9,11},{10,... | collective-permute-start | bytes 1179656 | tf_op jit(solution)/shard_map/ppermute | solution.py:227
  63.4 12.2 %collective-permute-start.17 = (bf16[2,192,512]{2,1,0:T(8,128)(2,1)S(1)}, bf16[2,192,512]{2,1,0:T(8,128)(2,1)S(1)}, u32[]{:S(2)}, u32[]{:S(2)}) collective-permute-start(bf16[2,192,512]{2,1,0:T(8,128)(2,1)S(1)} %ahead_outer_2.1.refs_2_), channel_id=1, source_target_pairs={{0,2},{1,3},{2,0},{3,1},{4,6},{5,7},{6,4},{7,5},{8,10},{9,11},{10,... | collective-permute-start | bytes 1179656 | tf_op jit(solution)/shard_map/ppermute | solution.py:227
  68.2 11.7 %collective-permute-start.21 = (bf16[1,192,512]{2,1,0:T(8,128)(2,1)S(1)}, bf16[1,192,512]{2,1,0:T(8,128)(2,1)S(1)}, u32[]{:S(2)}, u32[]{:S(2)}) collective-permute-start(bf16[1,192,512]{2,1,0:T(8,128)(2,1)S(1)} %grad_third_1.1.refs_1_), channel_id=1, source_target_pairs={{0,2},{1,3},{2,0},{3,1},{4,6},{5,7},{6,4},{7,5},{8,10},{9,11},{10,... | collective-permute-start | bytes 589832 | tf_op jit(solution)/shard_map/ppermute | solution.py:227
  80.2 9.9 %collective-permute-start.24 = (bf16[2,192,512]{2,1,0:T(8,128)(2,1)S(1)}, bf16[2,192,512]{2,1,0:T(8,128)(2,1)S(1)}, u32[]{:S(2)}, u32[]{:S(2)}) collective-permute-start(bf16[2,192,512]{2,1,0:T(8,128)(2,1)S(1)} %behind_back_1.1.refs_2_), channel_id=1, source_target_pairs={{0,2},{1,3},{2,0},{3,1},{4,6},{5,7},{6,4},{7,5},{8,10},{9,11},{10,... | collective-permute-start | bytes 1179656 | tf_op jit(solution)/shard_map/ppermute | solution.py:227
  92.3 11.2 %collective-permute-start.27 = (bf16[1,192,512]{2,1,0:T(8,128)(2,1)S(1)}, bf16[1,192,512]{2,1,0:T(8,128)(2,1)S(1)}, u32[]{:S(2)}, u32[]{:S(2)}) collective-permute-start(bf16[1,192,512]{2,1,0:T(8,128)(2,1)S(1)} %ahead_first_1.1.refs_5_.refs_1_), channel_id=1, source_target_pairs={{0,0},{1,1},{2,4},{3,5},{4,2},{5,3},{6,6},{7,7},{8,8},{9,9},{10,12... | collective-permute-start | bytes 589832 | tf_op jit(solution)/shard_map/ppermute | solution.py:227
  97.4 16.1 %collective-permute-start.25 = (bf16[192,896]{1,0:T(8,128)(2,1)S(1)}, bf16[192,896]{1,0:T(8,128)(2,1)S(1)}, u32[]{:S(2)}, u32[]{:S(2)}) collective-permute-start(bf16[192,896]{1,0:T(8,128)(2,1)S(1)} %get-tuple-element.12.refs_1_), channel_id=1, source_target_pairs={{0,1},{1,0},{2,3},{3,2},{4,5},{5,4},{6,7},{7,6},{8,9},{9,8},{10,11... | collective-permute-start | bytes 1032200 | tf_op jit(solution)/shard_map/ppermute | solution.py:242
  97.7 15.9 %collective-permute-start.31 = (bf16[2,192,512]{2,1,0:T(8,128)(2,1)S(1)}, bf16[2,192,512]{2,1,0:T(8,128)(2,1)S(1)}, u32[]{:S(2)}, u32[]{:S(2)}) collective-permute-start(bf16[2,192,512]{2,1,0:T(8,128)(2,1)S(1)} %behind_back_2.1.refs_1_), channel_id=1, source_target_pairs={{0,2},{1,3},{2,0},{3,1},{4,6},{5,7},{6,4},{7,5},{8,10},{9,11},{10,... | collective-permute-start | bytes 1179656 | tf_op jit(solution)/shard_map/ppermute | solution.py:227
  103.6 23.8 %collective-permute-start.30 = (bf16[1,192,512]{2,1,0:T(8,128)(2,1)S(1)}, bf16[1,192,512]{2,1,0:T(8,128)(2,1)S(1)}, u32[]{:S(2)}, u32[]{:S(2)}) collective-permute-start(bf16[1,192,512]{2,1,0:T(8,128)(2,1)S(1)} %ahead_back_2.1.refs_2_), channel_id=1, source_target_pairs={{0,2},{1,3},{2,0},{3,1},{4,6},{5,7},{6,4},{7,5},{8,10},{9,11},{10,... | collective-permute-start | bytes 589832 | tf_op jit(solution)/shard_map/ppermute | solution.py:227
  103.7 28.6 %collective-permute-start.34 = (bf16[192,896]{1,0:T(8,128)(2,1)S(1)}, bf16[192,896]{1,0:T(8,128)(2,1)S(1)}, u32[]{:S(2)}, u32[]{:S(2)}) collective-permute-start(bf16[192,896]{1,0:T(8,128)(2,1)S(1)} %behind_shares.1.refs_2_), channel_id=1, source_target_pairs={{8,0},{9,1},{10,2},{11,3},{12,4},{13,5},{14,6},{15,7},{16,8},{17,9... | collective-permute-start | bytes 1032200 | tf_op jit(solution)/shard_map/ppermute | solution.py:251
  115.6 18.7 %collective-permute-start.35 = (bf16[192,896]{1,0:T(8,128)(2,1)S(1)}, bf16[192,896]{1,0:T(8,128)(2,1)S(1)}, u32[]{:S(2)}, u32[]{:S(2)}) collective-permute-start(bf16[192,896]{1,0:T(8,128)(2,1)S(1)} %get-tuple-element.14.refs_6_), channel_id=1, source_target_pairs={{8,1},{9,0},{10,3},{11,2},{12,5},{13,4},{14,7},{15,6},{16,9},{17,8... | collective-permute-start | bytes 1032200 | tf_op jit(solution)/shard_map/ppermute | solution.py:251
  121.6 12.7 %collective-permute-start.36 = (bf16[192,896]{1,0:T(8,128)(2,1)S(1)}, bf16[192,896]{1,0:T(8,128)(2,1)S(1)}, u32[]{:S(2)}, u32[]{:S(2)}) collective-permute-start(bf16[192,896]{1,0:T(8,128)(2,1)S(1)} %get-tuple-element.17), channel_id=1, source_target_pairs={{8,0},{9,1},{10,2},{11,3},{12,4},{13,5},{14,6},{15,7},{16,8},{17,9... | collective-permute-start | bytes 1032200 | tf_op jit(solution)/shard_map/ppermute | solution.py:251
  123.7 11.6 %collective-permute-start.29 = (bf16[192,896]{1,0:T(8,128)(2,1)S(1)}, bf16[192,896]{1,0:T(8,128)(2,1)S(1)}, u32[]{:S(2)}, u32[]{:S(2)}) collective-permute-start(bf16[192,896]{1,0:T(8,128)(2,1)S(1)} %ahead_shares.1.refs_5_), channel_id=1, source_target_pairs={{0,8},{1,9},{2,10},{3,11},{4,12},{5,13},{6,14},{7,15},{8,16},{9,17... | collective-permute-start | bytes 1032200 | tf_op jit(solution)/shard_map/ppermute | solution.py:251
  (30 other events, 165.9 us)

commit v15 on v14

--- a/solution.py
+++ b/solution.py
@@ -12,7 +12,8 @@
 F32 = jnp.float32
 MIB = 1024 * 1024
 PIECES = 2
-ROWS, SMALL, ACT, FIRST, AHEAD_OUT, BEHIND_OUT = 20, 6, 10, 5.2, 3, 20
+ROWS, SMALL, ACT, FIRST = 20, 6, 10, 5.2
+OUT = {(True, 0): 3, (False, 0): 20, (True, 1): 3, (False, 1): 20}
 
 
 def shift(shard, axis, by):
@@ -30,7 +31,7 @@
     return pl.BlockSpec((parts, slots // PIECES, half), lambda *_: (0, c, 0))
 
 
-def call(kernel, micros, operands, after, out_shape, grid=(1,), in_specs=None, out_specs=None, scratch=(), limit=24, name=None):
+def call(kernel, micros, operands, after, out_shape, grid=(1,), in_specs=None, out_specs=None, scratch=(), limit=16, name=None):
     count, unread = len(operands), len(after)
 
     def run(*refs):
@@ -55,10 +56,6 @@
 
 def cut_kernel(rows, out):
     out[...] = rows[...]
-
-
-def touch_kernel(gates, downs, out):
-    out[...] = gates[0, :16, :128] + downs[0, :16, :128]
 
 
 def cut_first_kernel(value, out):
@@ -195,14 +192,14 @@
         out[...] = share.astype(BF16)
 
 
-def second_product(name, values, scale, weights, after):
+def second_product(name, micros, values, scale, weights, after):
     kinds, units, features = weights.shape
     slots = values[0].shape[1]
     operands = [*values] + ([] if scale is None else [scale])
     share = jax.ShapeDtypeStruct((slots, features // 2), BF16)
     return call(
         functools.partial(second_kernel, scale is not None),
-        AHEAD_OUT if kinds == 1 else BEHIND_OUT,
+        micros,
         (*operands, weights),
         after,
         (share, share),
@@ -387,7 +384,7 @@
         scale = cut(scales[0], c) if forward else None
         weights = downs if forward else gates
         give, keep = second_product(
-            f"{chain.name}_out_{c}", chain.activated(c), scale, weights, list(recent)
+            f"{chain.name}_out_{c}", OUT[forward, c], chain.activated(c), scale, weights, list(recent)
         )
         recent[:] = [give]
         return give, keep
@@ -404,6 +401,8 @@
         sent[chain, 0] = to_section(total, 1 if chain is ahead else -1, 0)
 
     def finish_last(chain):
+        if chain is ahead:
+            recent.append(sent[chain, 0])
         give, keep = output(chain, 1)
         by = 1 if chain is ahead else -1
         sent[chain, 1] = to_section(give, by, 1), to_section(keep, by, 0)
@@ -415,17 +414,6 @@
 
     for chain in (behind, ahead, grad):
         chain.fetch(0)
-    weights_spec = pl.BlockSpec(memory_space=pltpu.VMEM)
-    touched = call(
-        touch_kernel,
-        ROWS,
-        (gates, downs),
-        list(recent),
-        jax.ShapeDtypeStruct((16, 128), BF16),
-        in_specs=[weights_spec, weights_spec],
-        name="touch",
-    )
-    recent[:] = [touched]
     behind.far_product(0)
     behind.first_hop(0)
     behind.fetch(1)
@@ -449,9 +437,9 @@
     grad.near_products()
     grad.merged_hop(1, grad.far[1])
     ahead.middle_sum(1)
-    grad.middle_sum(1)
     activate_behind(0)
     behind.merged_hop(2, behind.act[0])
+    grad.middle_sum(1)
     activate_ahead(0)
     ahead.merged_hop(2, ahead.act[0])
     grad.last_third_hop()
@@ -462,9 +450,9 @@
     behind.outer_pass(1)
     ahead.outer_pass(1)
     behind.middle_pass(1)
-    ahead.middle_pass(1)
     finish_first(behind)
     finish_first(ahead)
+    ahead.middle_pass(1)
     behind.outer_pass(2)
     ahead.outer_pass(2)
     send_first(behind)

time: 144 us -> 147 us (1.021)
  waiting for transfers between devices: 26.4 us -> 30.8 us
  local copies, waits for them, and re-layouts: 17.2 us -> 12.9 us
  starting transfers between devices: 76.4 us -> 79.2 us
    ppermute x8, waiting for transfers between devices: 5.39 us -> 11.7 us  [swapped(): return lax.ppermute(value, 'expert', [(i, i ^ 1) for i in range(devices)])]
    ppermute x23, starting transfers between devices: 43 us -> 48.4 us  [between(): return lax.ppermute(value, 'expert', pairs)]
    unnamed x34 -> x28, local copies, waits for them, and re-layouts: 15.1 us -> 10.8 us
    ppermute x6, starting transfers between devices: 25.3 us -> 22.6 us  [to_section(): return lax.ppermute(value, ('section', 'expert'), pairs)]
    pallas_call x47 -> x46, Pallas kernels: 21 us -> 21.7 us  [call(): pl.pallas_call(run, compiler_params=pltpu.CompilerParams(vmem_limit_bytes...]
  transfers between devices with their start and end apart: 37 -> 37, of which waited for: 12 -> 11; matrix products, arithmetic and copies ran while one was open for 1% -> 1% of each run, Pallas kernels for 14% -> 14%
where the time goes in v15:
time: 147 us; the launch traced here: 146 us
  starting transfers between devices  79.2 us (54%)
  waiting for transfers between devices  30.8 us (21%)
  Pallas kernels  21.7 us (15%)
  local copies, waits for them, and re-layouts  12.9 us (9%)
    ppermute x23, starting transfers between devices, between(): return lax.ppermute(value, 'expert', pairs)  48.4 us
    ppermute x6, starting transfers between devices, to_section(): return lax.ppermute(value, ('section', 'expert'), pairs)  22.6 us
    pallas_call x46, Pallas kernels, call(): pl.pallas_call(run, compiler_params=pltpu.CompilerParams(vmem_limit_bytes...  21.7 us
    ppermute x23, waiting for transfers between devices, between(): return lax.ppermute(value, 'expert', pairs)  14.7 us
    ppermute x8, waiting for transfers between devices, swapped(): return lax.ppermute(value, 'expert', [(i, i ^ 1) for i in range(devices)])  11.7 us
    unnamed x28, local copies, waits for them, and re-layouts  10.8 us
    ppermute x8, starting transfers between devices, swapped(): return lax.ppermute(value, 'expert', [(i, i ^ 1) for i in range(devices)])  8.19 us
    ppermute x6, waiting for transfers between devices, to_section(): return lax.ppermute(value, ('section', 'expert'), pairs)  4.42 us
  transfers between devices with their start and end apart: 37, of which 11 were waited for; matrix products, arithmetic and copies ran while one was open for 1% of the time, Pallas kernels for 14%

profile of v15, /device:TPU:1, one launch (start us, length us, event | category | flops | bytes accessed | tf_op | source)
XLA Modules:
  0.0 145.9 jit_solution(13700098398077426648)
XLA Ops:
  1.6 2.1 %collective-permute-start.1 = (bf16[192,896]{1,0:T(8,128)(2,1)S(1)}, bf16[192,896]{1,0:T(8,128)(2,1)S(1)}, u32[]{:S(2)}, u32[]{:S(2)}) collective-permute-start(bf16[192,896]{1,0:T(8,128)(2,1)S(1)} %slice_bitcast_fusion.refs_0_), channel_id=1, source_target_pairs={{0,1},{1,0},{2,3},{3,2},{4,5},{5,4},{6,7},{7,6},{8,9},{9,8},{10,11... | collective-permute-start | bytes 1032200 | tf_op jit(solution)/shard_map/ppermute | solution.py:239
  7.7 3.8 %collective-permute-done.1.refs_1_ = bf16[192,896]{1,0:T(8,128)(2,1)S(1)} collective-permute-done((bf16[192,896]{1,0:T(8,128)(2,1)S(1)}, bf16[192,896]{1,0:T(8,128)(2,1)S(1)}, u32[]{:S(2)}, u32[]{:S(2)}) %collective-permute-start.1) | collective-permute-done | bytes 344096 | tf_op jit(solution)/shard_map/ppermute | solution.py:239
  11.6 3.1 %copy-done.1 = bf16[1,1,2,1024,1792]{4,3,2,1,0:T(8,128)(2,1)S(1)} copy-done((bf16[1,1,2,1024,1792]{4,3,2,1,0:T(8,128)(2,1)S(1)}, bf16[1,1,2,1024,1792]{4,3,2,1,0:T(8,128)(2,1)}, u32[]{:S(2)}) %copy-start.1) | copy-done | bytes 7340056
  22.0 4.4 %collective-permute-done.3.refs_1_ = bf16[192,896]{1,0:T(8,128)(2,1)S(1)} collective-permute-done((bf16[192,896]{1,0:T(8,128)(2,1)S(1)}, bf16[192,896]{1,0:T(8,128)(2,1)S(1)}, u32[]{:S(2)}, u32[]{:S(2)}) %collective-permute-start.3) | collective-permute-done | bytes 344096 | tf_op jit(solution)/shard_map/ppermute | solution.py:239
  30.5 3.2 %collective-permute-done.6.refs_1_.refs_3_ = bf16[192,896]{1,0:T(8,128)(2,1)S(1)} collective-permute-done((bf16[192,896]{1,0:T(8,128)(2,1)S(1)}, bf16[192,896]{1,0:T(8,128)(2,1)S(1)}, u32[]{:S(2)}, u32[]{:S(2)}) %collective-permute-start.6) | collective-permute-done | bytes 344096 | tf_op jit(solution)/shard_map/ppermute | solution.py:239
  37.6 3.8 %collective-permute-start.12 = (bf16[2,192,512]{2,1,0:T(8,128)(2,1)S(1)}, bf16[2,192,512]{2,1,0:T(8,128)(2,1)S(1)}, u32[]{:S(2)}, u32[]{:S(2)}) collective-permute-start(bf16[2,192,512]{2,1,0:T(8,128)(2,1)S(1)} %behind_outer_1.1.refs_1_), channel_id=1, source_target_pairs={{0,2},{1,3},{2,0},{3,1},{4,6},{5,7},{6,4},{7,5},{8,10},{9,11},{10,... | collective-permute-start | bytes 1179656 | tf_op jit(solution)/shard_map/ppermute | solution.py:224
  50.6 2.9 %collective-permute-start.14 = (bf16[1,192,512]{2,1,0:T(8,128)(2,1)S(1)}, bf16[1,192,512]{2,1,0:T(8,128)(2,1)S(1)}, u32[]{:S(2)}, u32[]{:S(2)}) collective-permute-start(bf16[1,192,512]{2,1,0:T(8,128)(2,1)S(1)} %grad_outer_1.1.refs_2_), channel_id=1, source_target_pairs={{0,2},{1,3},{2,0},{3,1},{4,6},{5,7},{6,4},{7,5},{8,10},{9,11},{10,... | collective-permute-start | bytes 589832 | tf_op jit(solution)/shard_map/ppermute | solution.py:224
  56.2 3.4 %collective-permute-done.14.refs_3_.refs_1_ = bf16[1,192,512]{2,1,0:T(8,128)(2,1)S(1)} collective-permute-done((bf16[1,192,512]{2,1,0:T(8,128)(2,1)S(1)}, bf16[1,192,512]{2,1,0:T(8,128)(2,1)S(1)}, u32[]{:S(2)}, u32[]{:S(2)}) %collective-permute-start.14) | collective-permute-done | bytes 196640 | tf_op jit(solution)/shard_map/ppermute | solution.py:224
  62.2 5.9 %collective-permute-start.17 = (bf16[2,192,512]{2,1,0:T(8,128)(2,1)S(1)}, bf16[2,192,512]{2,1,0:T(8,128)(2,1)S(1)}, u32[]{:S(2)}, u32[]{:S(2)}) collective-permute-start(bf16[2,192,512]{2,1,0:T(8,128)(2,1)S(1)} %ahead_outer_2.1.refs_2_), channel_id=1, source_target_pairs={{0,2},{1,3},{2,0},{3,1},{4,6},{5,7},{6,4},{7,5},{8,10},{9,11},{10,... | collective-permute-start | bytes 1179656 | tf_op jit(solution)/shard_map/ppermute | solution.py:224
  68.2 3.9 %collective-permute-start.21 = (bf16[1,192,512]{2,1,0:T(8,128)(2,1)S(1)}, bf16[1,192,512]{2,1,0:T(8,128)(2,1)S(1)}, u32[]{:S(2)}, u32[]{:S(2)}) collective-permute-start(bf16[1,192,512]{2,1,0:T(8,128)(2,1)S(1)} %grad_third_1.1.refs_1_), channel_id=1, source_target_pairs={{0,2},{1,3},{2,0},{3,1},{4,6},{5,7},{6,4},{7,5},{8,10},{9,11},{10,... | collective-permute-start | bytes 589832 | tf_op jit(solution)/shard_map/ppermute | solution.py:224
  72.8 4.7 %collective-permute-done.17.refs_0_.refs_1_ = bf16[2,192,512]{2,1,0:T(8,128)(2,1)S(1)} collective-permute-done((bf16[2,192,512]{2,1,0:T(8,128)(2,1)S(1)}, bf16[2,192,512]{2,1,0:T(8,128)(2,1)S(1)}, u32[]{:S(2)}, u32[]{:S(2)}) %collective-permute-start.17) | collective-permute-done | bytes 393248 | tf_op jit(solution)/shard_map/ppermute | solution.py:224
  78.4 3.4 %collective-permute-done.21.refs_3_ = bf16[1,192,512]{2,1,0:T(8,128)(2,1)S(1)} collective-permute-done((bf16[1,192,512]{2,1,0:T(8,128)(2,1)S(1)}, bf16[1,192,512]{2,1,0:T(8,128)(2,1)S(1)}, u32[]{:S(2)}, u32[]{:S(2)}) %collective-permute-start.21) | collective-permute-done | bytes 196640 | tf_op jit(solution)/shard_map/ppermute | solution.py:224
  83.8 4.3 %collective-permute-start.23 = (bf16[1,192,512]{2,1,0:T(8,128)(2,1)S(1)}, bf16[1,192,512]{2,1,0:T(8,128)(2,1)S(1)}, u32[]{:S(2)}, u32[]{:S(2)}) collective-permute-start(bf16[1,192,512]{2,1,0:T(8,128)(2,1)S(1)} %ahead_back_1.1.refs_1_), channel_id=1, source_target_pairs={{0,2},{1,3},{2,0},{3,1},{4,6},{5,7},{6,4},{7,5},{8,10},{9,11},{10,... | collective-permute-start | bytes 589832 | tf_op jit(solution)/shard_map/ppermute | solution.py:224
  90.1 2.1 %behind_out_0.1 = (bf16[192,896]{1,0:T(8,128)(2,1)S(1)}, bf16[192,896]{1,0:T(8,128)(2,1)S(1)}) custom-call(bf16[2,192,512]{2,1,0:T(8,128)(2,1)S(1)} %behind_act_0.1.refs_0_.refs_3_, bf16[2,192,512]{2,1,0:T(8,128)(2,1)S(1)} %behind_first_0.1.refs_1_, bf16[2,192,512]{2,1,0:T(8,128)(2,1)S(1)} %collective-permute-done.22.refs_1_.refs_2_, ...), custom_call_target="tpu_custom_call" | custom-call | flops 20000000000 | bytes 1024 | tf_op jit(solution)/shard_map/behind_out_0/pallas_call | solution.py:44
  95.6 6.5 %collective-permute-start.31 = (bf16[2,192,512]{2,1,0:T(8,128)(2,1)S(1)}, bf16[2,192,512]{2,1,0:T(8,128)(2,1)S(1)}, u32[]{:S(2)}, u32[]{:S(2)}) collective-permute-start(bf16[2,192,512]{2,1,0:T(8,128)(2,1)S(1)} %behind_back_2.1.refs_1_), channel_id=1, source_target_pairs={{0,2},{1,3},{2,0},{3,1},{4,6},{5,7},{6,4},{7,5},{8,10},{9,11},{10,... | collective-permute-start | bytes 1179656 | tf_op jit(solution)/shard_map/ppermute | solution.py:224
  102.8 6.7 %collective-permute-start.30 = (bf16[1,192,512]{2,1,0:T(8,128)(2,1)}, bf16[1,192,512]{2,1,0:T(8,128)(2,1)S(1)}, u32[]{:S(2)}, u32[]{:S(2)}) collective-permute-start(bf16[1,192,512]{2,1,0:T(8,128)(2,1)} %ahead_back_2.1.refs_2_), channel_id=1, source_target_pairs={{0,2},{1,3},{2,0},{3,1},{4,6},{5,7},{6,4},{7,5},{8,10},{9,11},{10,... | collective-permute-start | bytes 589832 | tf_op jit(solution)/shard_map/ppermute | solution.py:224
  109.7 8.5 %collective-permute-start.34 = (bf16[192,896]{1,0:T(8,128)(2,1)S(1)}, bf16[192,896]{1,0:T(8,128)(2,1)S(1)}, u32[]{:S(2)}, u32[]{:S(2)}) collective-permute-start(bf16[192,896]{1,0:T(8,128)(2,1)S(1)} %behind_shares.1.refs_2_), channel_id=1, source_target_pairs={{8,0},{9,1},{10,2},{11,3},{12,4},{13,5},{14,6},{15,7},{16,8},{17,9... | collective-permute-start | bytes 1032200 | tf_op jit(solution)/shard_map/ppermute | solution.py:248
  118.3 3.1 %collective-permute-start.29 = (bf16[192,896]{1,0:T(8,128)(2,1)S(1)}, bf16[192,896]{1,0:T(8,128)(2,1)S(1)}, u32[]{:S(2)}, u32[]{:S(2)}) collective-permute-start(bf16[192,896]{1,0:T(8,128)(2,1)S(1)} %ahead_shares.1.refs_5_), channel_id=1, source_target_pairs={{0,8},{1,9},{2,10},{3,11},{4,12},{5,13},{6,14},{7,15},{8,16},{9,17... | collective-permute-start | bytes 1032200 | tf_op jit(solution)/shard_map/ppermute | solution.py:248
  123.3 2.4 %collective-permute-start.35 = (bf16[192,896]{1,0:T(8,128)(2,1)S(1)}, bf16[192,896]{1,0:T(8,128)(2,1)S(1)}, u32[]{:S(2)}, u32[]{:S(2)}) collective-permute-start(bf16[192,896]{1,0:T(8,128)(2,1)S(1)} %get-tuple-element.14.refs_6_), channel_id=1, source_target_pairs={{8,1},{9,0},{10,3},{11,2},{12,5},{13,4},{14,7},{15,6},{16,9},{17,8... | collective-permute-start | bytes 1032200 | tf_op jit(solution)/shard_map/ppermute | solution.py:248
  125.7 1.9 %collective-permute-start.36 = (bf16[192,896]{1,0:T(8,128)(2,1)S(1)}, bf16[192,896]{1,0:T(8,128)(2,1)S(1)}, u32[]{:S(2)}, u32[]{:S(2)}) collective-permute-start(bf16[192,896]{1,0:T(8,128)(2,1)S(1)} %get-tuple-element.17), channel_id=1, source_target_pairs={{8,0},{9,1},{10,2},{11,3},{12,4},{13,5},{14,6},{15,7},{16,8},{17,9... | collective-permute-start | bytes 1032200 | tf_op jit(solution)/shard_map/ppermute | solution.py:248
  127.8 2.0 %copy-done.4 = bf16[1,1,1024,1792]{3,2,1,0:T(8,128)(2,1)S(1)} copy-done((bf16[1,1,1024,1792]{3,2,1,0:T(8,128)(2,1)S(1)}, bf16[1,1,1024,1792]{3,2,1,0:T(8,128)(2,1)}, u32[]{:S(2)}) %copy-start.4) | copy-done | bytes 3670040
  131.8 4.1 %collective-permute-start.32 = (bf16[192,896]{1,0:T(8,128)(2,1)S(1)}, bf16[192,896]{1,0:T(8,128)(2,1)S(1)}, u32[]{:S(2)}, u32[]{:S(2)}) collective-permute-start(bf16[192,896]{1,0:T(8,128)(2,1)S(1)} %get-tuple-element.15.refs_3_), channel_id=1, source_target_pairs={{0,9},{1,8},{2,11},{3,10},{4,13},{5,12},{6,15},{7,14},{8,17},{9,16... | collective-permute-start | bytes 1032200 | tf_op jit(solution)/shard_map/ppermute | solution.py:248
  135.9 2.5 %collective-permute-start.33 = (bf16[192,896]{1,0:T(8,128)(2,1)S(1)}, bf16[192,896]{1,0:T(8,128)(2,1)S(1)}, u32[]{:S(2)}, u32[]{:S(2)}) collective-permute-start(bf16[192,896]{1,0:T(8,128)(2,1)S(1)} %get-tuple-element.16), channel_id=1, source_target_pairs={{0,8},{1,9},{2,10},{3,11},{4,12},{5,13},{6,14},{7,15},{8,16},{9,17... | collective-permute-start | bytes 1032200 | tf_op jit(solution)/shard_map/ppermute | solution.py:248
  140.4 3.5 %collective-permute-done.33.refs_2_ = bf16[192,896]{1,0:T(8,128)(2,1)S(1)} collective-permute-done((bf16[192,896]{1,0:T(8,128)(2,1)S(1)}, bf16[192,896]{1,0:T(8,128)(2,1)S(1)}, u32[]{:S(2)}, u32[]{:S(2)}) %collective-permute-start.33) | collective-permute-done | bytes 344096 | tf_op jit(solution)/shard_map/ppermute | solution.py:248
  (131 shorter events, 52.3 us)
Async XLA Ops:
  1.6 9.9 %collective-permute-start.1 = (bf16[192,896]{1,0:T(8,128)(2,1)S(1)}, bf16[192,896]{1,0:T(8,128)(2,1)S(1)}, u32[]{:S(2)}, u32[]{:S(2)}) collective-permute-start(bf16[192,896]{1,0:T(8,128)(2,1)S(1)} %slice_bitcast_fusion.refs_0_), channel_id=1, source_target_pairs={{0,1},{1,0},{2,3},{3,2},{4,5},{5,4},{6,7},{7,6},{8,9},{9,8},{10,11... | collective-permute-start | bytes 1032200 | tf_op jit(solution)/shard_map/ppermute | solution.py:239
  4.9 14.0 %collective-permute-start = (bf16[192,896]{1,0:T(8,128)(2,1)S(1)}, bf16[192,896]{1,0:T(8,128)(2,1)S(1)}, u32[]{:S(2)}, u32[]{:S(2)}) collective-permute-start(bf16[192,896]{1,0:T(8,128)(2,1)S(1)} %ahead_rows_0.1.refs_1_.refs_0_), channel_id=1, source_target_pairs={{0,1},{1,0},{2,3},{3,2},{4,5},{5,4},{6,7},{7,6},{8,9},{9,8},{10,11... | collective-permute-start | bytes 1032200 | tf_op jit(solution)/shard_map/ppermute | solution.py:239
  6.0 20.3 %collective-permute-start.3 = (bf16[192,896]{1,0:T(8,128)(2,1)S(1)}, bf16[192,896]{1,0:T(8,128)(2,1)S(1)}, u32[]{:S(2)}, u32[]{:S(2)}) collective-permute-start(bf16[192,896]{1,0:T(8,128)(2,1)S(1)} %grad_rows_0.1.refs_3_.refs_0_), channel_id=1, source_target_pairs={{0,1},{1,0},{2,3},{3,2},{4,5},{5,4},{6,7},{7,6},{8,9},{9,8},{10,11... | collective-permute-start | bytes 1032200 | tf_op jit(solution)/shard_map/ppermute | solution.py:239
  16.0 12.4 %collective-permute-start.2 = (bf16[2,192,512]{2,1,0:T(8,128)(2,1)S(1)}, bf16[2,192,512]{2,1,0:T(8,128)(2,1)S(1)}, u32[]{:S(2)}, u32[]{:S(2)}) collective-permute-start(bf16[2,192,512]{2,1,0:T(8,128)(2,1)S(1)} %behind_far_0.1.refs_1_.refs_0_), channel_id=1, source_target_pairs={{0,2},{1,3},{2,0},{3,1},{4,6},{5,7},{6,4},{7,5},{8,10},{9,11},{10,... | collective-permute-start | bytes 1179656 | tf_op jit(solution)/shard_map/ppermute | solution.py:224
  17.3 16.4 %collective-permute-start.6 = (bf16[192,896]{1,0:T(8,128)(2,1)S(1)}, bf16[192,896]{1,0:T(8,128)(2,1)S(1)}, u32[]{:S(2)}, u32[]{:S(2)}) collective-permute-start(bf16[192,896]{1,0:T(8,128)(2,1)S(1)} %behind_rows_1.1.refs_3_.refs_0_.refs_2_), channel_id=1, source_target_pairs={{0,1},{1,0},{2,3},{3,2},{4,5},{5,4},{6,7},{7,6},{8,9},{9,8},{10,11... | collective-permute-start | bytes 1032200 | tf_op jit(solution)/shard_map/ppermute | solution.py:239
  21.7 15.0 %collective-permute-start.8 = (bf16[2,192,512]{2,1,0:T(8,128)(2,1)S(1)}, bf16[2,192,512]{2,1,0:T(8,128)(2,1)S(1)}, u32[]{:S(2)}, u32[]{:S(2)}) collective-permute-start(bf16[2,192,512]{2,1,0:T(8,128)(2,1)S(1)} %ahead_far_0.1.refs_3_.refs_0_), channel_id=1, source_target_pairs={{0,2},{1,3},{2,0},{3,1},{4,6},{5,7},{6,4},{7,5},{8,10},{9,11},{10,... | collective-permute-start | bytes 1179656 | tf_op jit(solution)/shard_map/ppermute | solution.py:224
  27.1 15.6 %collective-permute-start.5 = (bf16[1,192,512]{2,1,0:T(8,128)(2,1)S(1)}, bf16[1,192,512]{2,1,0:T(8,128)(2,1)S(1)}, u32[]{:S(2)}, u32[]{:S(2)}) collective-permute-start(bf16[1,192,512]{2,1,0:T(8,128)(2,1)S(1)} %grad_far_0.1.refs_2_.refs_0_), channel_id=1, source_target_pairs={{0,2},{1,3},{2,0},{3,1},{4,6},{5,7},{6,4},{7,5},{8,10},{9,11},{10,... | collective-permute-start | bytes 589832 | tf_op jit(solution)/shard_map/ppermute | solution.py:224
  29.2 14.2 %collective-permute-start.4 = (bf16[192,896]{1,0:T(8,128)(2,1)S(1)}, bf16[192,896]{1,0:T(8,128)(2,1)S(1)}, u32[]{:S(2)}, u32[]{:S(2)}) collective-permute-start(bf16[192,896]{1,0:T(8,128)(2,1)S(1)} %ahead_rows_1.1.refs_3_.refs_0_.refs_2_), channel_id=1, source_target_pairs={{0,1},{1,0},{2,3},{3,2},{4,5},{5,4},{6,7},{7,6},{8,9},{9,8},{10,11... | collective-permute-start | bytes 1032200 | tf_op jit(solution)/shard_map/ppermute | solution.py:239
  36.8 9.6 %collective-permute-start.9 = (bf16[2,192,512]{2,1,0:T(8,128)(2,1)S(1)}, bf16[2,192,512]{2,1,0:T(8,128)(2,1)S(1)}, u32[]{:S(2)}, u32[]{:S(2)}) collective-permute-start(bf16[2,192,512]{2,1,0:T(8,128)(2,1)S(1)} %ahead_middle_0.1.refs_3_), channel_id=1, source_target_pairs={{0,0},{1,1},{2,4},{3,5},{4,2},{5,3},{6,6},{7,7},{8,8},{9,9},{10,12... | collective-permute-start | bytes 1179656 | tf_op jit(solution)/shard_map/ppermute | solution.py:224
  37.6 10.5 %collective-permute-start.12 = (bf16[2,192,512]{2,1,0:T(8,128)(2,1)S(1)}, bf16[2,192,512]{2,1,0:T(8,128)(2,1)S(1)}, u32[]{:S(2)}, u32[]{:S(2)}) collective-permute-start(bf16[2,192,512]{2,1,0:T(8,128)(2,1)S(1)} %behind_outer_1.1.refs_1_), channel_id=1, source_target_pairs={{0,2},{1,3},{2,0},{3,1},{4,6},{5,7},{6,4},{7,5},{8,10},{9,11},{10,... | collective-permute-start | bytes 1179656 | tf_op jit(solution)/shard_map/ppermute | solution.py:224
  48.2 11.7 %collective-permute-start.15 = (bf16[2,192,512]{2,1,0:T(8,128)(2,1)S(1)}, bf16[2,192,512]{2,1,0:T(8,128)(2,1)S(1)}, u32[]{:S(2)}, u32[]{:S(2)}) collective-permute-start(bf16[2,192,512]{2,1,0:T(8,128)(2,1)S(1)} %behind_middle_1.1.refs_3_), channel_id=1, source_target_pairs={{0,0},{1,1},{2,4},{3,5},{4,2},{5,3},{6,6},{7,7},{8,8},{9,9},{10,12... | collective-permute-start | bytes 1179656 | tf_op jit(solution)/shard_map/ppermute | solution.py:224
  60.0 12.1 %collective-permute-start.18 = (bf16[2,192,512]{2,1,0:T(8,128)(2,1)S(1)}, bf16[2,192,512]{2,1,0:T(8,128)(2,1)S(1)}, u32[]{:S(2)}, u32[]{:S(2)}) collective-permute-start(bf16[2,192,512]{2,1,0:T(8,128)(2,1)S(1)} %behind_outer_2.1.refs_2_), channel_id=1, source_target_pairs={{0,2},{1,3},{2,0},{3,1},{4,6},{5,7},{6,4},{7,5},{8,10},{9,11},{10,... | collective-permute-start | bytes 1179656 | tf_op jit(solution)/shard_map/ppermute | solution.py:224
  62.2 15.3 %collective-permute-start.17 = (bf16[2,192,512]{2,1,0:T(8,128)(2,1)S(1)}, bf16[2,192,512]{2,1,0:T(8,128)(2,1)S(1)}, u32[]{:S(2)}, u32[]{:S(2)}) collective-permute-start(bf16[2,192,512]{2,1,0:T(8,128)(2,1)S(1)} %ahead_outer_2.1.refs_2_), channel_id=1, source_target_pairs={{0,2},{1,3},{2,0},{3,1},{4,6},{5,7},{6,4},{7,5},{8,10},{9,11},{10,... | collective-permute-start | bytes 1179656 | tf_op jit(solution)/shard_map/ppermute | solution.py:224
  68.2 13.6 %collective-permute-start.21 = (bf16[1,192,512]{2,1,0:T(8,128)(2,1)S(1)}, bf16[1,192,512]{2,1,0:T(8,128)(2,1)S(1)}, u32[]{:S(2)}, u32[]{:S(2)}) collective-permute-start(bf16[1,192,512]{2,1,0:T(8,128)(2,1)S(1)} %grad_third_1.1.refs_1_), channel_id=1, source_target_pairs={{0,2},{1,3},{2,0},{3,1},{4,6},{5,7},{6,4},{7,5},{8,10},{9,11},{10,... | collective-permute-start | bytes 589832 | tf_op jit(solution)/shard_map/ppermute | solution.py:224
  72.1 9.9 %collective-permute-start.22 = (bf16[2,192,512]{2,1,0:T(8,128)(2,1)S(1)}, bf16[2,192,512]{2,1,0:T(8,128)(2,1)S(1)}, u32[]{:S(2)}, u32[]{:S(2)}) collective-permute-start(bf16[2,192,512]{2,1,0:T(8,128)(2,1)S(1)} %behind_first_0.1.refs_1_), channel_id=1, source_target_pairs={{0,0},{1,1},{2,4},{3,5},{4,2},{5,3},{6,6},{7,7},{8,8},{9,9},{10,12... | collective-permute-start | bytes 1179656 | tf_op jit(solution)/shard_map/ppermute | solution.py:224
  83.8 9.7 %collective-permute-start.23 = (bf16[1,192,512]{2,1,0:T(8,128)(2,1)S(1)}, bf16[1,192,512]{2,1,0:T(8,128)(2,1)S(1)}, u32[]{:S(2)}, u32[]{:S(2)}) collective-permute-start(bf16[1,192,512]{2,1,0:T(8,128)(2,1)S(1)} %ahead_back_1.1.refs_1_), channel_id=1, source_target_pairs={{0,2},{1,3},{2,0},{3,1},{4,6},{5,7},{6,4},{7,5},{8,10},{9,11},{10,... | collective-permute-start | bytes 589832 | tf_op jit(solution)/shard_map/ppermute | solution.py:224
  92.2 17.3 %collective-permute-start.26 = (bf16[192,896]{1,0:T(8,128)(2,1)S(1)}, bf16[192,896]{1,0:T(8,128)(2,1)S(1)}, u32[]{:S(2)}, u32[]{:S(2)}) collective-permute-start(bf16[192,896]{1,0:T(8,128)(2,1)S(1)} %get-tuple-element.10.refs_6_), channel_id=1, source_target_pairs={{0,1},{1,0},{2,3},{3,2},{4,5},{5,4},{6,7},{7,6},{8,9},{9,8},{10,11... | collective-permute-start | bytes 1032200 | tf_op jit(solution)/shard_map/ppermute | solution.py:239
  94.6 23.6 %collective-permute-start.25 = (bf16[192,896]{1,0:T(8,128)(2,1)S(1)}, bf16[192,896]{1,0:T(8,128)(2,1)S(1)}, u32[]{:S(2)}, u32[]{:S(2)}) collective-permute-start(bf16[192,896]{1,0:T(8,128)(2,1)S(1)} %get-tuple-element.12.refs_1_), channel_id=1, source_target_pairs={{0,1},{1,0},{2,3},{3,2},{4,5},{5,4},{6,7},{7,6},{8,9},{9,8},{10,11... | collective-permute-start | bytes 1032200 | tf_op jit(solution)/shard_map/ppermute | solution.py:239
  95.6 25.8 %collective-permute-start.31 = (bf16[2,192,512]{2,1,0:T(8,128)(2,1)S(1)}, bf16[2,192,512]{2,1,0:T(8,128)(2,1)S(1)}, u32[]{:S(2)}, u32[]{:S(2)}) collective-permute-start(bf16[2,192,512]{2,1,0:T(8,128)(2,1)S(1)} %behind_back_2.1.refs_1_), channel_id=1, source_target_pairs={{0,2},{1,3},{2,0},{3,1},{4,6},{5,7},{6,4},{7,5},{8,10},{9,11},{10,... | collective-permute-start | bytes 1179656 | tf_op jit(solution)/shard_map/ppermute | solution.py:224
  102.8 25.0 %collective-permute-start.30 = (bf16[1,192,512]{2,1,0:T(8,128)(2,1)}, bf16[1,192,512]{2,1,0:T(8,128)(2,1)S(1)}, u32[]{:S(2)}, u32[]{:S(2)}) collective-permute-start(bf16[1,192,512]{2,1,0:T(8,128)(2,1)} %ahead_back_2.1.refs_2_), channel_id=1, source_target_pairs={{0,2},{1,3},{2,0},{3,1},{4,6},{5,7},{6,4},{7,5},{8,10},{9,11},{10,... | collective-permute-start | bytes 589832 | tf_op jit(solution)/shard_map/ppermute | solution.py:224
  109.7 28.8 %collective-permute-start.34 = (bf16[192,896]{1,0:T(8,128)(2,1)S(1)}, bf16[192,896]{1,0:T(8,128)(2,1)S(1)}, u32[]{:S(2)}, u32[]{:S(2)}) collective-permute-start(bf16[192,896]{1,0:T(8,128)(2,1)S(1)} %behind_shares.1.refs_2_), channel_id=1, source_target_pairs={{8,0},{9,1},{10,2},{11,3},{12,4},{13,5},{14,6},{15,7},{16,8},{17,9... | collective-permute-start | bytes 1032200 | tf_op jit(solution)/shard_map/ppermute | solution.py:248
  118.3 9.5 %collective-permute-start.29 = (bf16[192,896]{1,0:T(8,128)(2,1)S(1)}, bf16[192,896]{1,0:T(8,128)(2,1)S(1)}, u32[]{:S(2)}, u32[]{:S(2)}) collective-permute-start(bf16[192,896]{1,0:T(8,128)(2,1)S(1)} %ahead_shares.1.refs_5_), channel_id=1, source_target_pairs={{0,8},{1,9},{2,10},{3,11},{4,12},{5,13},{6,14},{7,15},{8,16},{9,17... | collective-permute-start | bytes 1032200 | tf_op jit(solution)/shard_map/ppermute | solution.py:248
  123.3 15.2 %collective-permute-start.35 = (bf16[192,896]{1,0:T(8,128)(2,1)S(1)}, bf16[192,896]{1,0:T(8,128)(2,1)S(1)}, u32[]{:S(2)}, u32[]{:S(2)}) collective-permute-start(bf16[192,896]{1,0:T(8,128)(2,1)S(1)} %get-tuple-element.14.refs_6_), channel_id=1, source_target_pairs={{8,1},{9,0},{10,3},{11,2},{12,5},{13,4},{14,7},{15,6},{16,9},{17,8... | collective-permute-start | bytes 1032200 | tf_op jit(solution)/shard_map/ppermute | solution.py:248
  125.7 12.7 %collective-permute-start.36 = (bf16[192,896]{1,0:T(8,128)(2,1)S(1)}, bf16[192,896]{1,0:T(8,128)(2,1)S(1)}, u32[]{:S(2)}, u32[]{:S(2)}) collective-permute-start(bf16[192,896]{1,0:T(8,128)(2,1)S(1)} %get-tuple-element.17), channel_id=1, source_target_pairs={{8,0},{9,1},{10,2},{11,3},{12,4},{13,5},{14,6},{15,7},{16,8},{17,9... | collective-permute-start | bytes 1032200 | tf_op jit(solution)/shard_map/ppermute | solution.py:248
  (27 other events, 141.5 us)

commit v16 on v15

--- a/solution.py
+++ b/solution.py
@@ -72,7 +72,7 @@
 def first_kernel(far, *refs):
     rows, (weights, out, joined) = refs[:-3], refs[-3:]
     near, group, _ = position()
-    side = 1 - near if far else near
+    side = 0 if far else near
     parts, _, half = out.shape
     slots, width = rows[0].shape
     at = pl.multiple_of(group * width, 128)
@@ -96,12 +96,13 @@
 def first_product(name, far, rows, weights, after):
     slots = rows[0].shape[0] * len(rows) // 2
     parts, units, features = weights.shape
+    half = units if far else units // 2
     return call(
         functools.partial(first_kernel, far),
         FIRST * parts,
         (*rows, weights),
         after,
-        jax.ShapeDtypeStruct((parts, slots, units // 2), BF16),
+        jax.ShapeDtypeStruct((parts, slots, half), BF16),
         in_specs=[*[whole(r) for r in rows], pl.BlockSpec(memory_space=pltpu.VMEM)],
         scratch=[pltpu.VMEM((slots, features), BF16)],
         name=name,
@@ -154,10 +155,14 @@
     out[1] = (expanded * gate * sig).astype(BF16)
 
 
-def result_kernel(first, one, two, out):
-    size = first.shape[0]
-    out[:size] = first[...]
-    out[size:] = (one[...].astype(F32) + two[...].astype(F32)).astype(BF16)
+def result_kernel(count, *refs):
+    shares, out = refs[:-1], refs[-1]
+    size = shares[0].shape[0]
+    for at, terms in ((0, shares[:count]), (size, shares[count:])):
+        total = terms[0][...].astype(F32)
+        for term in terms[1:]:
+            total += term[...].astype(F32)
+        out[at : at + size] = total.astype(BF16)
 
 
 def second_kernel(scaled, act, one, two, three, *refs):
@@ -192,19 +197,65 @@
         out[...] = share.astype(BF16)
 
 
+def copying_second_kernel(scaled, act, one, two, three, *refs):
+    scale, refs = (refs[0], refs[1:]) if scaled else (None, refs)
+    weights, give, keep, joined, tiles, sems = refs
+    near_half, group, end = position()
+    kinds, _, half = act.shape
+    _, _, units, width = tiles.shape
+    copies = []
+    for own in range(2):
+        at = pl.multiple_of((group if own else 1 - group) * width, 128)
+        copy = pltpu.make_async_copy(
+            weights.at[:, :, pl.ds(at, width)], tiles.at[own], sems.at[own]
+        )
+        copy.start()
+        copies.append(copy)
+
+    def place(near, far):
+        for kind in range(kinds):
+            at = pl.multiple_of((2 * kind + near_half) * half, 128)
+            other = pl.multiple_of((2 * kind + 1 - near_half) * half, 128)
+            joined[:, pl.ds(at, half)] = near[kind]
+            joined[:, pl.ds(other, half)] = far[kind]
+
+    @pl.when(end)
+    def _():
+        place(act, three)
+
+    @pl.when(jnp.logical_not(end))
+    def _():
+        place(one, two)
+
+    for own, out in enumerate((give, keep)):
+        copies[own].wait()
+        share = jnp.dot(
+            joined[...], tiles[own].reshape(kinds * units, width), preferred_element_type=F32
+        )
+        if scaled:
+            share = share * scale[...]
+        out[...] = share.astype(BF16)
+
+
 def second_product(name, micros, values, scale, weights, after):
     kinds, units, features = weights.shape
     slots = values[0].shape[1]
     operands = [*values] + ([] if scale is None else [scale])
     share = jax.ShapeDtypeStruct((slots, features // 2), BF16)
+    kernel, space = second_kernel, pltpu.VMEM
+    scratch = [pltpu.VMEM((slots, kinds * units), BF16)]
+    if kinds == 1:
+        kernel, space = copying_second_kernel, pl.ANY
+        scratch.append(pltpu.VMEM((2, kinds, units, features // 2), BF16))
+        scratch.append(pltpu.SemaphoreType.DMA((2,)))
     return call(
-        functools.partial(second_kernel, scale is not None),
+        functools.partial(kernel, scale is not None),
         micros,
         (*operands, weights),
         after,
         (share, share),
-        in_specs=[*[whole(v) for v in operands], pl.BlockSpec(memory_space=pltpu.VMEM)],
-        scratch=[pltpu.VMEM((slots, kinds * units), BF16)],
+        in_specs=[*[whole(v) for v in operands], pl.BlockSpec(memory_space=space)],
+        scratch=scratch,
         name=name,
     )
 
@@ -267,10 +318,17 @@
         recent[:] = [made]
         return made
 
+    def far_half(weights):
+        parts, units, features = weights.shape
+        start = jnp.where(lax.axis_index("expert") // 2 >= DBLOCKS // 2, 0, units // 2)
+        return lax.dynamic_slice(weights, (0, start, 0), (parts, units // 2, features))
+
+    gates_far, downs_far = far_half(gates), far_half(downs)
+
     class Chain:
-        def __init__(self, name, rows, weights, spreads):
+        def __init__(self, name, rows, weights, far_weights, spreads):
             self.name = name
-            self.rows, self.weights = rows, weights
+            self.rows, self.weights, self.far_weights = rows, weights, far_weights
             self.spreads = spreads
             self.pairs, self.far, self.near, self.act = {}, {}, {}, {}
             self.out, self.mid, self.one, self.back, self.third = {}, {}, {}, {}, {}
@@ -295,7 +353,7 @@
 
         def far_product(self, c):
             name = f"{self.name}_far_{c}"
-            made = first_product(name, True, self.pairs[c], self.weights, list(recent))
+            made = first_product(name, True, self.pairs[c], self.far_weights, list(recent))
             recent[:] = [made]
             self.far[c] = made
 
@@ -360,9 +418,9 @@
         def activated(self, c):
             return self.act[c], self.one[c], self.mid[PIECES + c], self.back[c + 1]
 
-    ahead = Chain("ahead", ahead_rows[0], gates, 1)
-    behind = Chain("behind", behind_rows[0], gates, 2)
-    grad = Chain("grad", behind_grad[0], downs, 0)
+    ahead = Chain("ahead", ahead_rows[0], gates, gates_far, 1)
+    behind = Chain("behind", behind_rows[0], gates, gates_far, 2)
+    grad = Chain("grad", behind_grad[0], downs, downs_far, 0)
     sent = {}
 
     def cut(array, c):
@@ -389,28 +447,29 @@
         recent[:] = [give]
         return give, keep
 
-    def finish_first(chain):
-        give, keep = output(chain, 0)
-        sent[chain, 0] = swapped(give), keep
-
-    def send_first(chain):
-        share, keep = sent[chain, 0]
-        total = kernel_call(
-            f"{chain.name}_shares", sum_kernel, SMALL, (keep, share), keep.shape
-        )
-        sent[chain, 0] = to_section(total, 1 if chain is ahead else -1, 0)
-
-    def finish_last(chain):
-        if chain is ahead:
-            recent.append(sent[chain, 0])
-        give, keep = output(chain, 1)
+    def finish_swapped(chain, c):
+        give, keep = output(chain, c)
+        sent[chain, c] = swapped(give), keep
+
+    def send_swapped(chain, c):
+        share, keep = sent[chain, c]
+        total = kernel_call(f"{chain.name}_shares", sum_kernel, SMALL, (keep, share), keep.shape)
+        sent[chain, c] = (to_section(total, 1 if chain is ahead else -1, 0),)
+
+    def finish_straight(chain, c):
+        give, keep = output(chain, c)
         by = 1 if chain is ahead else -1
-        sent[chain, 1] = to_section(give, by, 1), to_section(keep, by, 0)
+        sent[chain, c] = to_section(give, by, 1), to_section(keep, by, 0)
 
     def result(chain):
-        operands = (sent[chain, 0], *sent[chain, 1])
-        shape = (height, operands[0].shape[1])
-        return kernel_call(f"{chain.name}_result", result_kernel, SMALL, operands, shape)[None]
+        first, second = sent[chain, 0], sent[chain, 1]
+        return kernel_call(
+            f"{chain.name}_result",
+            functools.partial(result_kernel, len(first)),
+            SMALL,
+            (*first, *second),
+            (height, first[0].shape[1]),
+        )[None]
 
     for chain in (behind, ahead, grad):
         chain.fetch(0)
@@ -450,15 +509,15 @@
     behind.outer_pass(1)
     ahead.outer_pass(1)
     behind.middle_pass(1)
-    finish_first(behind)
-    finish_first(ahead)
     ahead.middle_pass(1)
+    finish_swapped(behind, 0)
+    finish_swapped(ahead, 0)
     behind.outer_pass(2)
     ahead.outer_pass(2)
-    send_first(behind)
-    send_first(ahead)
-    finish_last(behind)
-    finish_last(ahead)
+    send_swapped(behind, 0)
+    finish_straight(behind, 1)
+    send_swapped(ahead, 0)
+    finish_straight(ahead, 1)
     behind_sent = result(behind)
     ahead_sent = result(ahead)
     return ahead_sent, behind_sent

time: 147 us -> 144 us (0.980)
  Pallas kernels: 21.7 us -> 29.9 us
  starting transfers between devices: 79.2 us -> 72.6 us
  local copies, waits for them, and re-layouts: 12.9 us -> 8.61 us
    ppermute x23, starting transfers between devices: 48.4 us -> 37.6 us  [between(): return lax.ppermute(value, 'expert', pairs)]
    pallas_call x46, Pallas kernels: 21.7 us -> 29.9 us  [call(): pl.pallas_call(run, compiler_params=pltpu.CompilerParams(vmem_limit_bytes...]
    unnamed x28 -> x20, local copies, waits for them, and re-layouts: 10.8 us -> 3.14 us
    dynamic_slice x0 -> x2, local copies, waits for them, and re-layouts: none -> 3.9 us  [far_half(): lax.dynamic_slice(weights, (0, start, 0), (parts, units // 2, features))]
    ppermute x8, waiting for transfers between devices: 11.7 us -> 7.97 us  [swapped(): return lax.ppermute(value, 'expert', [(i, i ^ 1) for i in range(devices)])]
    ppermute x6, starting transfers between devices: 22.6 us -> 26.3 us  [to_section(): return lax.ppermute(value, ('section', 'expert'), pairs)]
    ppermute x23, waiting for transfers between devices: 14.7 us -> 16.8 us  [between(): return lax.ppermute(value, 'expert', pairs)]
  transfers between devices with their start and end apart: 37 -> 37, of which waited for: 11 -> 10; matrix products, arithmetic and copies ran while one was open for 1% -> 3% of each run, Pallas kernels for 14% -> 20%
where the time goes in v16:
time: 144 us; the launch traced here: 142 us
  starting transfers between devices  72.6 us (50%)
  waiting for transfers between devices  30 us (21%)
  Pallas kernels  29.9 us (21%)
  local copies, waits for them, and re-layouts  8.61 us (6%)
    ppermute x23, starting transfers between devices, between(): return lax.ppermute(value, 'expert', pairs)  37.6 us
    pallas_call x46, Pallas kernels, call(): pl.pallas_call(run, compiler_params=pltpu.CompilerParams(vmem_limit_bytes...  29.9 us
    ppermute x6, starting transfers between devices, to_section(): return lax.ppermute(value, ('section', 'expert'), pairs)  26.3 us
    ppermute x23, waiting for transfers between devices, between(): return lax.ppermute(value, 'expert', pairs)  16.8 us
    ppermute x8, starting transfers between devices, swapped(): return lax.ppermute(value, 'expert', [(i, i ^ 1) for i in range(devices)])  8.74 us
    ppermute x8, waiting for transfers between devices, swapped(): return lax.ppermute(value, 'expert', [(i, i ^ 1) for i in range(devices)])  7.97 us
    ppermute x6, waiting for transfers between devices, to_section(): return lax.ppermute(value, ('section', 'expert'), pairs)  5.18 us
    dynamic_slice x2, local copies, waits for them, and re-layouts, far_half(): lax.dynamic_slice(weights, (0, start, 0), (parts, units // 2, features))  3.9 us
  transfers between devices with their start and end apart: 37, of which 10 were waited for; matrix products, arithmetic and copies ran while one was open for 3% of the time, Pallas kernels for 20%

profile of v16, /device:TPU:1, one launch (start us, length us, event | category | flops | bytes accessed | tf_op | source)
XLA Modules:
  0.0 142.5 jit_solution(2716262481721674575)
XLA Ops:
  1.6 2.1 %collective-permute-start.1 = (bf16[192,896]{1,0:T(8,128)(2,1)S(1)}, bf16[192,896]{1,0:T(8,128)(2,1)}, u32[]{:S(2)}, u32[]{:S(2)}) collective-permute-start(bf16[192,896]{1,0:T(8,128)(2,1)S(1)} %slice_bitcast_fusion.refs_0_), channel_id=1, source_target_pairs={{0,1},{1,0},{2,3},{3,2},{4,5},{5,4},{6,7},{7,6},{8,9},{9,8},{10,11... | collective-permute-start | bytes 1032200 | tf_op jit(solution)/shard_map/ppermute | solution.py:290
  10.2 2.3 %dynamic-slice_bitcast_fusion.refs_2_ = bf16[2,512,1792]{2,1,0:T(8,128)(2,1)S(1)} fusion(bf16[1,1,2,1024,1792]{4,3,2,1,0:T(8,128)(2,1)} %param.12, s32[]{:T(128)S(6)} %select_n.18), kind=kLoop, calls=%fused_computation | loop fusion | bytes 7340036 | tf_op jit(solution)/shard_map/dynamic_slice | solution.py:324
  12.5 2.4 %behind_far_0.1.refs_1_.refs_0_ = bf16[2,192,512]{2,1,0:T(8,128)(2,1)S(1)} custom-call(bf16[192,896]{1,0:T(8,128)(2,1)S(1)} %slice_bitcast_fusion.refs_0_, bf16[192,896]{1,0:T(8,128)(2,1)} %collective-permute-done.1.refs_1_, bf16[2,512,1792]{2,1,0:T(8,128)(2,1)S(1)} %dynamic-slice_bitcast_fusion.refs_2_, bf16[192,896]{1,0:T(8,128)(2,1)} %grad_rows_0.1.refs_3_.refs_0_), custom_call_target="tpu_custom_call" | custom-call | flops 10400000000 | bytes 1024 | tf_op jit(solution)/shard_map/behind_far_0/pallas_call | solution.py:44
  16.8 2.3 %collective-permute-done.refs_1_ = bf16[192,896]{1,0:T(8,128)(2,1)} collective-permute-done((bf16[192,896]{1,0:T(8,128)(2,1)}, bf16[192,896]{1,0:T(8,128)(2,1)}, u32[]{:S(2)}, u32[]{:S(2)}) %collective-permute-start) | collective-permute-done | bytes 344096 | tf_op jit(solution)/shard_map/ppermute | solution.py:290
  19.0 2.4 %ahead_far_0.1.refs_3_.refs_0_ = bf16[2,192,512]{2,1,0:T(8,128)(2,1)S(1)} custom-call(bf16[192,896]{1,0:T(8,128)(2,1)} %ahead_rows_0.1.refs_1_.refs_0_, bf16[192,896]{1,0:T(8,128)(2,1)} %collective-permute-done.refs_1_, bf16[2,512,1792]{2,1,0:T(8,128)(2,1)S(1)} %dynamic-slice_bitcast_fusion.refs_2_, bf16[192,896]{1,0:T(8,128)(2,1)S(1)} %behind_rows_1.1.refs_3_.refs_0_.refs_2_), custom_call_target="tpu_custom_call" | custom-call | flops 10400000000 | bytes 1024 | tf_op jit(solution)/shard_map/ahead_far_0/pallas_call | solution.py:44
  22.7 3.7 %collective-permute-done.3.refs_1_ = bf16[192,896]{1,0:T(8,128)(2,1)} collective-permute-done((bf16[192,896]{1,0:T(8,128)(2,1)}, bf16[192,896]{1,0:T(8,128)(2,1)}, u32[]{:S(2)}, u32[]{:S(2)}) %collective-permute-start.3) | collective-permute-done | bytes 344096 | tf_op jit(solution)/shard_map/ppermute | solution.py:290
  35.0 2.6 %behind_near.1.refs_2_.refs_1_.refs_0_ = bf16[2,384,512]{2,1,0:T(8,128)(2,1)S(1)} custom-call(bf16[192,896]{1,0:T(8,128)(2,1)S(1)} %slice_bitcast_fusion.refs_0_, bf16[192,896]{1,0:T(8,128)(2,1)} %collective-permute-done.1.refs_1_, bf16[192,896]{1,0:T(8,128)(2,1)S(1)} %behind_rows_1.1.refs_3_.refs_0_.refs_2_, ...), custom_call_target="tpu_custom_call" | custom-call | flops 10400000000 | bytes 1024 | tf_op jit(solution)/shard_map/behind_near/pallas_call | solution.py:44
  38.6 3.8 %collective-permute-start.12 = (bf16[2,192,512]{2,1,0:T(8,128)(2,1)S(1)}, bf16[2,192,512]{2,1,0:T(8,128)(2,1)S(1)}, u32[]{:S(2)}, u32[]{:S(2)}) collective-permute-start(bf16[2,192,512]{2,1,0:T(8,128)(2,1)S(1)} %behind_outer_1.1.refs_1_), channel_id=1, source_target_pairs={{0,2},{1,3},{2,0},{3,1},{4,6},{5,7},{6,4},{7,5},{8,10},{9,11},{10,... | collective-permute-start | bytes 1179656 | tf_op jit(solution)/shard_map/ppermute | solution.py:275
  45.7 2.7 %ahead_near.1.refs_1_.refs_3_.refs_0_ = bf16[2,384,512]{2,1,0:T(8,128)(2,1)S(1)} custom-call(bf16[192,896]{1,0:T(8,128)(2,1)} %ahead_rows_0.1.refs_1_.refs_0_, bf16[192,896]{1,0:T(8,128)(2,1)} %collective-permute-done.refs_1_, bf16[192,896]{1,0:T(8,128)(2,1)S(1)} %ahead_rows_1.1.refs_3_.refs_0_.refs_2_, ...), custom_call_target="tpu_custom_call" | custom-call | flops 10400000000 | bytes 1024 | tf_op jit(solution)/shard_map/ahead_near/pallas_call | solution.py:44
  48.6 2.7 %collective-permute-start.10 = (bf16[2,192,512]{2,1,0:T(8,128)(2,1)S(1)}, bf16[2,192,512]{2,1,0:T(8,128)(2,1)S(1)}, u32[]{:S(2)}, u32[]{:S(2)}) collective-permute-start(bf16[2,192,512]{2,1,0:T(8,128)(2,1)S(1)} %ahead_outer_1.1.refs_2_), channel_id=1, source_target_pairs={{0,2},{1,3},{2,0},{3,1},{4,6},{5,7},{6,4},{7,5},{8,10},{9,11},{10,... | collective-permute-start | bytes 1179656 | tf_op jit(solution)/shard_map/ppermute | solution.py:275
  53.4 2.0 %grad_near.1.refs_1_.refs_3_.refs_2_.refs_0_ = bf16[1,384,512]{2,1,0:T(8,128)(2,1)S(1)} custom-call(bf16[192,896]{1,0:T(8,128)(2,1)} %grad_rows_0.1.refs_3_.refs_0_, bf16[192,896]{1,0:T(8,128)(2,1)} %collective-permute-done.3.refs_1_, bf16[192,896]{1,0:T(8,128)(2,1)S(1)} %grad_rows_1.1.refs_2_.refs_0_, ...), custom_call_target="tpu_custom_call" | custom-call | flops 5200000000 | bytes 1024 | tf_op jit(solution)/shard_map/grad_near/pallas_call | solution.py:44
  57.5 4.9 %collective-permute-done.14.refs_3_.refs_1_ = bf16[1,192,512]{2,1,0:T(8,128)(2,1)S(1)} collective-permute-done((bf16[1,192,512]{2,1,0:T(8,128)(2,1)S(1)}, bf16[1,192,512]{2,1,0:T(8,128)(2,1)S(1)}, u32[]{:S(2)}, u32[]{:S(2)}) %collective-permute-start.14) | collective-permute-done | bytes 196640 | tf_op jit(solution)/shard_map/ppermute | solution.py:275
  65.0 4.8 %collective-permute-start.17 = (bf16[2,192,512]{2,1,0:T(8,128)(2,1)S(1)}, bf16[2,192,512]{2,1,0:T(8,128)(2,1)S(1)}, u32[]{:S(2)}, u32[]{:S(2)}) collective-permute-start(bf16[2,192,512]{2,1,0:T(8,128)(2,1)S(1)} %ahead_outer_2.1.refs_2_), channel_id=1, source_target_pairs={{0,2},{1,3},{2,0},{3,1},{4,6},{5,7},{6,4},{7,5},{8,10},{9,11},{10,... | collective-permute-start | bytes 1179656 | tf_op jit(solution)/shard_map/ppermute | solution.py:275
  69.9 3.4 %collective-permute-start.21 = (bf16[1,192,512]{2,1,0:T(8,128)(2,1)S(1)}, bf16[1,192,512]{2,1,0:T(8,128)(2,1)S(1)}, u32[]{:S(2)}, u32[]{:S(2)}) collective-permute-start(bf16[1,192,512]{2,1,0:T(8,128)(2,1)S(1)} %grad_third_1.1.refs_1_), channel_id=1, source_target_pairs={{0,2},{1,3},{2,0},{3,1},{4,6},{5,7},{6,4},{7,5},{8,10},{9,11},{10,... | collective-permute-start | bytes 589832 | tf_op jit(solution)/shard_map/ppermute | solution.py:275
  74.0 5.4 %collective-permute-done.17.refs_0_.refs_1_ = bf16[2,192,512]{2,1,0:T(8,128)(2,1)S(1)} collective-permute-done((bf16[2,192,512]{2,1,0:T(8,128)(2,1)S(1)}, bf16[2,192,512]{2,1,0:T(8,128)(2,1)S(1)}, u32[]{:S(2)}, u32[]{:S(2)}) %collective-permute-start.17) | collective-permute-done | bytes 393248 | tf_op jit(solution)/shard_map/ppermute | solution.py:275
  80.3 3.4 %collective-permute-done.21.refs_3_ = bf16[1,192,512]{2,1,0:T(8,128)(2,1)S(1)} collective-permute-done((bf16[1,192,512]{2,1,0:T(8,128)(2,1)S(1)}, bf16[1,192,512]{2,1,0:T(8,128)(2,1)S(1)}, u32[]{:S(2)}, u32[]{:S(2)}) %collective-permute-start.21) | collective-permute-done | bytes 196640 | tf_op jit(solution)/shard_map/ppermute | solution.py:275
  85.6 3.9 %collective-permute-start.23 = (bf16[1,192,512]{2,1,0:T(8,128)(2,1)S(1)}, bf16[1,192,512]{2,1,0:T(8,128)(2,1)S(1)}, u32[]{:S(2)}, u32[]{:S(2)}) collective-permute-start(bf16[1,192,512]{2,1,0:T(8,128)(2,1)S(1)} %ahead_back_1.1.refs_1_), channel_id=1, source_target_pairs={{0,2},{1,3},{2,0},{3,1},{4,6},{5,7},{6,4},{7,5},{8,10},{9,11},{10,... | collective-permute-start | bytes 589832 | tf_op jit(solution)/shard_map/ppermute | solution.py:275
  94.1 2.1 %behind_out_0.1 = (bf16[192,896]{1,0:T(8,128)(2,1)S(1)}, bf16[192,896]{1,0:T(8,128)(2,1)S(1)}) custom-call(bf16[2,192,512]{2,1,0:T(8,128)(2,1)S(1)} %behind_act_0.1.refs_0_.refs_3_, bf16[2,192,512]{2,1,0:T(8,128)(2,1)S(1)} %behind_first_0.1.refs_1_, bf16[2,192,512]{2,1,0:T(8,128)(2,1)S(1)} %collective-permute-done.22.refs_1_.refs_2_, ...), custom_call_target="tpu_custom_call" | custom-call | flops 20000000000 | bytes 1024 | tf_op jit(solution)/shard_map/behind_out_0/pallas_call | solution.py:44
  96.2 2.4 %collective-permute-start.28 = (bf16[192,896]{1,0:T(8,128)(2,1)S(1)}, bf16[192,896]{1,0:T(8,128)(2,1)S(1)}, u32[]{:S(2)}, u32[]{:S(2)}) collective-permute-start(bf16[192,896]{1,0:T(8,128)(2,1)S(1)} %get-tuple-element.10.refs_6_), channel_id=1, source_target_pairs={{0,1},{1,0},{2,3},{3,2},{4,5},{5,4},{6,7},{7,6},{8,9},{9,8},{10,11... | collective-permute-start | bytes 1032200 | tf_op jit(solution)/shard_map/ppermute | solution.py:290
  100.3 3.9 %collective-permute-start.27 = (bf16[2,192,512]{2,1,0:T(8,128)(2,1)S(1)}, bf16[2,192,512]{2,1,0:T(8,128)(2,1)S(1)}, u32[]{:S(2)}, u32[]{:S(2)}) collective-permute-start(bf16[2,192,512]{2,1,0:T(8,128)(2,1)S(1)} %behind_back_2.1.refs_1_), channel_id=1, source_target_pairs={{0,2},{1,3},{2,0},{3,1},{4,6},{5,7},{6,4},{7,5},{8,10},{9,11},{10,... | collective-permute-start | bytes 1179656 | tf_op jit(solution)/shard_map/ppermute | solution.py:275
  104.3 10.1 %collective-permute-start.34 = (bf16[192,896]{1,0:T(8,128)(2,1)S(1)}, bf16[192,896]{1,0:T(8,128)(2,1)S(1)}, u32[]{:S(2)}, u32[]{:S(2)}) collective-permute-start(bf16[192,896]{1,0:T(8,128)(2,1)S(1)} %behind_shares.1.refs_5_), channel_id=1, source_target_pairs={{8,0},{9,1},{10,2},{11,3},{12,4},{13,5},{14,6},{15,7},{16,8},{17,9... | collective-permute-start | bytes 1032200 | tf_op jit(solution)/shard_map/ppermute | solution.py:299
  116.3 6.8 %collective-permute-start.35 = (bf16[192,896]{1,0:T(8,128)(2,1)S(1)}, bf16[192,896]{1,0:T(8,128)(2,1)S(1)}, u32[]{:S(2)}, u32[]{:S(2)}) collective-permute-start(bf16[192,896]{1,0:T(8,128)(2,1)S(1)} %get-tuple-element.14.refs_2_), channel_id=1, source_target_pairs={{8,1},{9,0},{10,3},{11,2},{12,5},{13,4},{14,7},{15,6},{16,9},{17,8... | collective-permute-start | bytes 1032200 | tf_op jit(solution)/shard_map/ppermute | solution.py:299
  125.2 3.6 %collective-permute-start.30 = (bf16[192,896]{1,0:T(8,128)(2,1)S(1)}, bf16[192,896]{1,0:T(8,128)(2,1)S(1)}, u32[]{:S(2)}, u32[]{:S(2)}) collective-permute-start(bf16[192,896]{1,0:T(8,128)(2,1)S(1)} %ahead_shares.1.refs_6_), channel_id=1, source_target_pairs={{0,8},{1,9},{2,10},{3,11},{4,12},{5,13},{6,14},{7,15},{8,16},{9,17... | collective-permute-start | bytes 1032200 | tf_op jit(solution)/shard_map/ppermute | solution.py:299
  135.3 3.7 %collective-permute-done.32.refs_1_ = bf16[192,896]{1,0:T(8,128)(2,1)S(1)} collective-permute-done((bf16[192,896]{1,0:T(8,128)(2,1)S(1)}, bf16[192,896]{1,0:T(8,128)(2,1)S(1)}, u32[]{:S(2)}, u32[]{:S(2)}) %collective-permute-start.32) | collective-permute-done | bytes 344096 | tf_op jit(solution)/shard_map/ppermute | solution.py:299
  (126 shorter events, 53.7 us)
Async XLA Ops:
  1.6 10.8 %collective-permute-start.1 = (bf16[192,896]{1,0:T(8,128)(2,1)S(1)}, bf16[192,896]{1,0:T(8,128)(2,1)}, u32[]{:S(2)}, u32[]{:S(2)}) collective-permute-start(bf16[192,896]{1,0:T(8,128)(2,1)S(1)} %slice_bitcast_fusion.refs_0_), channel_id=1, source_target_pairs={{0,1},{1,0},{2,3},{3,2},{4,5},{5,4},{6,7},{7,6},{8,9},{9,8},{10,11... | collective-permute-start | bytes 1032200 | tf_op jit(solution)/shard_map/ppermute | solution.py:290
  5.6 13.4 %collective-permute-start = (bf16[192,896]{1,0:T(8,128)(2,1)}, bf16[192,896]{1,0:T(8,128)(2,1)}, u32[]{:S(2)}, u32[]{:S(2)}) collective-permute-start(bf16[192,896]{1,0:T(8,128)(2,1)} %ahead_rows_0.1.refs_1_.refs_0_), channel_id=1, source_target_pairs={{0,1},{1,0},{2,3},{3,2},{4,5},{5,4},{6,7},{7,6},{8,9},{9,8},{10,11... | collective-permute-start | bytes 1032200 | tf_op jit(solution)/shard_map/ppermute | solution.py:290
  6.9 19.6 %collective-permute-start.3 = (bf16[192,896]{1,0:T(8,128)(2,1)}, bf16[192,896]{1,0:T(8,128)(2,1)}, u32[]{:S(2)}, u32[]{:S(2)}) collective-permute-start(bf16[192,896]{1,0:T(8,128)(2,1)} %grad_rows_0.1.refs_3_.refs_0_), channel_id=1, source_target_pairs={{0,1},{1,0},{2,3},{3,2},{4,5},{5,4},{6,7},{7,6},{8,9},{9,8},{10,11... | collective-permute-start | bytes 1032200 | tf_op jit(solution)/shard_map/ppermute | solution.py:290
  14.9 14.7 %collective-permute-start.2 = (bf16[2,192,512]{2,1,0:T(8,128)(2,1)S(1)}, bf16[2,192,512]{2,1,0:T(8,128)(2,1)S(1)}, u32[]{:S(2)}, u32[]{:S(2)}) collective-permute-start(bf16[2,192,512]{2,1,0:T(8,128)(2,1)S(1)} %behind_far_0.1.refs_1_.refs_0_), channel_id=1, source_target_pairs={{0,2},{1,3},{2,0},{3,1},{4,6},{5,7},{6,4},{7,5},{8,10},{9,11},{10,... | collective-permute-start | bytes 1179656 | tf_op jit(solution)/shard_map/ppermute | solution.py:275
  16.2 17.4 %collective-permute-start.6 = (bf16[192,896]{1,0:T(8,128)(2,1)S(1)}, bf16[192,896]{1,0:T(8,128)(2,1)S(1)}, u32[]{:S(2)}, u32[]{:S(2)}) collective-permute-start(bf16[192,896]{1,0:T(8,128)(2,1)S(1)} %behind_rows_1.1.refs_3_.refs_0_.refs_2_), channel_id=1, source_target_pairs={{0,1},{1,0},{2,3},{3,2},{4,5},{5,4},{6,7},{7,6},{8,9},{9,8},{10,11... | collective-permute-start | bytes 1032200 | tf_op jit(solution)/shard_map/ppermute | solution.py:290
  21.5 16.2 %collective-permute-start.8 = (bf16[2,192,512]{2,1,0:T(8,128)(2,1)S(1)}, bf16[2,192,512]{2,1,0:T(8,128)(2,1)S(1)}, u32[]{:S(2)}, u32[]{:S(2)}) collective-permute-start(bf16[2,192,512]{2,1,0:T(8,128)(2,1)S(1)} %ahead_far_0.1.refs_3_.refs_0_), channel_id=1, source_target_pairs={{0,2},{1,3},{2,0},{3,1},{4,6},{5,7},{6,4},{7,5},{8,10},{9,11},{10,... | collective-permute-start | bytes 1179656 | tf_op jit(solution)/shard_map/ppermute | solution.py:275
  28.2 15.4 %collective-permute-start.5 = (bf16[1,192,512]{2,1,0:T(8,128)(2,1)S(1)}, bf16[1,192,512]{2,1,0:T(8,128)(2,1)S(1)}, u32[]{:S(2)}, u32[]{:S(2)}) collective-permute-start(bf16[1,192,512]{2,1,0:T(8,128)(2,1)S(1)} %grad_far_0.1.refs_2_.refs_0_), channel_id=1, source_target_pairs={{0,2},{1,3},{2,0},{3,1},{4,6},{5,7},{6,4},{7,5},{8,10},{9,11},{10,... | collective-permute-start | bytes 589832 | tf_op jit(solution)/shard_map/ppermute | solution.py:275
  30.4 14.0 %collective-permute-start.4 = (bf16[192,896]{1,0:T(8,128)(2,1)S(1)}, bf16[192,896]{1,0:T(8,128)(2,1)S(1)}, u32[]{:S(2)}, u32[]{:S(2)}) collective-permute-start(bf16[192,896]{1,0:T(8,128)(2,1)S(1)} %ahead_rows_1.1.refs_3_.refs_0_.refs_2_), channel_id=1, source_target_pairs={{0,1},{1,0},{2,3},{3,2},{4,5},{5,4},{6,7},{7,6},{8,9},{9,8},{10,11... | collective-permute-start | bytes 1032200 | tf_op jit(solution)/shard_map/ppermute | solution.py:290
  37.8 10.7 %collective-permute-start.9 = (bf16[2,192,512]{2,1,0:T(8,128)(2,1)S(1)}, bf16[2,192,512]{2,1,0:T(8,128)(2,1)S(1)}, u32[]{:S(2)}, u32[]{:S(2)}) collective-permute-start(bf16[2,192,512]{2,1,0:T(8,128)(2,1)S(1)} %ahead_middle_0.1.refs_3_), channel_id=1, source_target_pairs={{0,0},{1,1},{2,4},{3,5},{4,2},{5,3},{6,6},{7,7},{8,8},{9,9},{10,12... | collective-permute-start | bytes 1179656 | tf_op jit(solution)/shard_map/ppermute | solution.py:275
  38.6 12.7 %collective-permute-start.12 = (bf16[2,192,512]{2,1,0:T(8,128)(2,1)S(1)}, bf16[2,192,512]{2,1,0:T(8,128)(2,1)S(1)}, u32[]{:S(2)}, u32[]{:S(2)}) collective-permute-start(bf16[2,192,512]{2,1,0:T(8,128)(2,1)S(1)} %behind_outer_1.1.refs_1_), channel_id=1, source_target_pairs={{0,2},{1,3},{2,0},{3,1},{4,6},{5,7},{6,4},{7,5},{8,10},{9,11},{10,... | collective-permute-start | bytes 1179656 | tf_op jit(solution)/shard_map/ppermute | solution.py:275
  43.7 11.7 %collective-permute-start.13 = (bf16[1,192,512]{2,1,0:T(8,128)(2,1)S(1)}, bf16[1,192,512]{2,1,0:T(8,128)(2,1)S(1)}, u32[]{:S(2)}, u32[]{:S(2)}) collective-permute-start(bf16[1,192,512]{2,1,0:T(8,128)(2,1)S(1)} %grad_middle_0.1.refs_3_), channel_id=1, source_target_pairs={{0,0},{1,1},{2,4},{3,5},{4,2},{5,3},{6,6},{7,7},{8,8},{9,9},{10,12... | collective-permute-start | bytes 589832 | tf_op jit(solution)/shard_map/ppermute | solution.py:275
  51.4 11.4 %collective-permute-start.15 = (bf16[2,192,512]{2,1,0:T(8,128)(2,1)S(1)}, bf16[2,192,512]{2,1,0:T(8,128)(2,1)S(1)}, u32[]{:S(2)}, u32[]{:S(2)}) collective-permute-start(bf16[2,192,512]{2,1,0:T(8,128)(2,1)S(1)} %behind_middle_1.1.refs_3_), channel_id=1, source_target_pairs={{0,0},{1,1},{2,4},{3,5},{4,2},{5,3},{6,6},{7,7},{8,8},{9,9},{10,12... | collective-permute-start | bytes 1179656 | tf_op jit(solution)/shard_map/ppermute | solution.py:275
  62.8 10.5 %collective-permute-start.18 = (bf16[2,192,512]{2,1,0:T(8,128)(2,1)S(1)}, bf16[2,192,512]{2,1,0:T(8,128)(2,1)S(1)}, u32[]{:S(2)}, u32[]{:S(2)}) collective-permute-start(bf16[2,192,512]{2,1,0:T(8,128)(2,1)S(1)} %behind_outer_2.1.refs_2_), channel_id=1, source_target_pairs={{0,2},{1,3},{2,0},{3,1},{4,6},{5,7},{6,4},{7,5},{8,10},{9,11},{10,... | collective-permute-start | bytes 1179656 | tf_op jit(solution)/shard_map/ppermute | solution.py:275
  65.0 14.4 %collective-permute-start.17 = (bf16[2,192,512]{2,1,0:T(8,128)(2,1)S(1)}, bf16[2,192,512]{2,1,0:T(8,128)(2,1)S(1)}, u32[]{:S(2)}, u32[]{:S(2)}) collective-permute-start(bf16[2,192,512]{2,1,0:T(8,128)(2,1)S(1)} %ahead_outer_2.1.refs_2_), channel_id=1, source_target_pairs={{0,2},{1,3},{2,0},{3,1},{4,6},{5,7},{6,4},{7,5},{8,10},{9,11},{10,... | collective-permute-start | bytes 1179656 | tf_op jit(solution)/shard_map/ppermute | solution.py:275
  69.9 13.8 %collective-permute-start.21 = (bf16[1,192,512]{2,1,0:T(8,128)(2,1)S(1)}, bf16[1,192,512]{2,1,0:T(8,128)(2,1)S(1)}, u32[]{:S(2)}, u32[]{:S(2)}) collective-permute-start(bf16[1,192,512]{2,1,0:T(8,128)(2,1)S(1)} %grad_third_1.1.refs_1_), channel_id=1, source_target_pairs={{0,2},{1,3},{2,0},{3,1},{4,6},{5,7},{6,4},{7,5},{8,10},{9,11},{10,... | collective-permute-start | bytes 589832 | tf_op jit(solution)/shard_map/ppermute | solution.py:275
  73.3 10.6 %collective-permute-start.22 = (bf16[2,192,512]{2,1,0:T(8,128)(2,1)S(1)}, bf16[2,192,512]{2,1,0:T(8,128)(2,1)S(1)}, u32[]{:S(2)}, u32[]{:S(2)}) collective-permute-start(bf16[2,192,512]{2,1,0:T(8,128)(2,1)S(1)} %behind_first_0.1.refs_1_), channel_id=1, source_target_pairs={{0,0},{1,1},{2,4},{3,5},{4,2},{5,3},{6,6},{7,7},{8,8},{9,9},{10,12... | collective-permute-start | bytes 1179656 | tf_op jit(solution)/shard_map/ppermute | solution.py:275
  93.4 10.7 %collective-permute-start.29 = (bf16[1,192,512]{2,1,0:T(8,128)(2,1)S(1)}, bf16[1,192,512]{2,1,0:T(8,128)(2,1)S(1)}, u32[]{:S(2)}, u32[]{:S(2)}) collective-permute-start(bf16[1,192,512]{2,1,0:T(8,128)(2,1)S(1)} %ahead_first_1.1.refs_5_.refs_1_), channel_id=1, source_target_pairs={{0,0},{1,1},{2,4},{3,5},{4,2},{5,3},{6,6},{7,7},{8,8},{9,9},{10,12... | collective-permute-start | bytes 589832 | tf_op jit(solution)/shard_map/ppermute | solution.py:275
  100.2 24.9 %collective-permute-start.25 = (bf16[192,896]{1,0:T(8,128)(2,1)S(1)}, bf16[192,896]{1,0:T(8,128)(2,1)S(1)}, u32[]{:S(2)}, u32[]{:S(2)}) collective-permute-start(bf16[192,896]{1,0:T(8,128)(2,1)S(1)} %get-tuple-element.12.refs_1_), channel_id=1, source_target_pairs={{0,1},{1,0},{2,3},{3,2},{4,5},{5,4},{6,7},{7,6},{8,9},{9,8},{10,11... | collective-permute-start | bytes 1032200 | tf_op jit(solution)/shard_map/ppermute | solution.py:290
  100.3 14.1 %collective-permute-start.27 = (bf16[2,192,512]{2,1,0:T(8,128)(2,1)S(1)}, bf16[2,192,512]{2,1,0:T(8,128)(2,1)S(1)}, u32[]{:S(2)}, u32[]{:S(2)}) collective-permute-start(bf16[2,192,512]{2,1,0:T(8,128)(2,1)S(1)} %behind_back_2.1.refs_1_), channel_id=1, source_target_pairs={{0,2},{1,3},{2,0},{3,1},{4,6},{5,7},{6,4},{7,5},{8,10},{9,11},{10,... | collective-permute-start | bytes 1179656 | tf_op jit(solution)/shard_map/ppermute | solution.py:275
  104.2 24.7 %collective-permute-start.31 = (bf16[1,192,512]{2,1,0:T(8,128)(2,1)S(1)}, bf16[1,192,512]{2,1,0:T(8,128)(2,1)S(1)}, u32[]{:S(2)}, u32[]{:S(2)}) collective-permute-start(bf16[1,192,512]{2,1,0:T(8,128)(2,1)S(1)} %ahead_back_2.1.refs_2_), channel_id=1, source_target_pairs={{0,2},{1,3},{2,0},{3,1},{4,6},{5,7},{6,4},{7,5},{8,10},{9,11},{10,... | collective-permute-start | bytes 589832 | tf_op jit(solution)/shard_map/ppermute | solution.py:275
  104.3 28.0 %collective-permute-start.34 = (bf16[192,896]{1,0:T(8,128)(2,1)S(1)}, bf16[192,896]{1,0:T(8,128)(2,1)S(1)}, u32[]{:S(2)}, u32[]{:S(2)}) collective-permute-start(bf16[192,896]{1,0:T(8,128)(2,1)S(1)} %behind_shares.1.refs_5_), channel_id=1, source_target_pairs={{8,0},{9,1},{10,2},{11,3},{12,4},{13,5},{14,6},{15,7},{16,8},{17,9... | collective-permute-start | bytes 1032200 | tf_op jit(solution)/shard_map/ppermute | solution.py:299
  116.3 17.9 %collective-permute-start.35 = (bf16[192,896]{1,0:T(8,128)(2,1)S(1)}, bf16[192,896]{1,0:T(8,128)(2,1)S(1)}, u32[]{:S(2)}, u32[]{:S(2)}) collective-permute-start(bf16[192,896]{1,0:T(8,128)(2,1)S(1)} %get-tuple-element.14.refs_2_), channel_id=1, source_target_pairs={{8,1},{9,0},{10,3},{11,2},{12,5},{13,4},{14,7},{15,6},{16,9},{17,8... | collective-permute-start | bytes 1032200 | tf_op jit(solution)/shard_map/ppermute | solution.py:299
  123.2 11.1 %collective-permute-start.36 = (bf16[192,896]{1,0:T(8,128)(2,1)S(1)}, bf16[192,896]{1,0:T(8,128)(2,1)S(1)}, u32[]{:S(2)}, u32[]{:S(2)}) collective-permute-start(bf16[192,896]{1,0:T(8,128)(2,1)S(1)} %get-tuple-element.17), channel_id=1, source_target_pairs={{8,0},{9,1},{10,2},{11,3},{12,4},{13,5},{14,6},{15,7},{16,8},{17,9... | collective-permute-start | bytes 1032200 | tf_op jit(solution)/shard_map/ppermute | solution.py:299
  125.2 15.2 %collective-permute-start.30 = (bf16[192,896]{1,0:T(8,128)(2,1)S(1)}, bf16[192,896]{1,0:T(8,128)(2,1)S(1)}, u32[]{:S(2)}, u32[]{:S(2)}) collective-permute-start(bf16[192,896]{1,0:T(8,128)(2,1)S(1)} %ahead_shares.1.refs_6_), channel_id=1, source_target_pairs={{0,8},{1,9},{2,10},{3,11},{4,12},{5,13},{6,14},{7,15},{8,16},{9,17... | collective-permute-start | bytes 1032200 | tf_op jit(solution)/shard_map/ppermute | solution.py:299
  (23 other events, 128.4 us)

commit v17 on v16

--- a/solution.py
+++ b/solution.py
@@ -457,6 +457,8 @@
         sent[chain, c] = (to_section(total, 1 if chain is ahead else -1, 0),)
 
     def finish_straight(chain, c):
+        if chain is ahead:
+            recent.extend(sent[chain, 0])
         give, keep = output(chain, c)
         by = 1 if chain is ahead else -1
         sent[chain, c] = to_section(give, by, 1), to_section(keep, by, 0)
@@ -478,9 +480,9 @@
     behind.fetch(1)
     ahead.far_product(0)
     ahead.first_hop(0)
+    behind.middle_sum(0)
     grad.far_product(0)
     grad.first_hop(0)
-    behind.middle_sum(0)
     ahead.fetch(1)
     behind.far_product(1)
     behind.near_products()
@@ -501,8 +503,8 @@
     grad.middle_sum(1)
     activate_ahead(0)
     ahead.merged_hop(2, ahead.act[0])
+    behind.middle_pass(0)
     grad.last_third_hop()
-    behind.middle_pass(0)
     ahead.middle_pass(0)
     activate_ahead(1)
     activate_behind(1)
@@ -510,13 +512,13 @@
     ahead.outer_pass(1)
     behind.middle_pass(1)
     ahead.middle_pass(1)
+    finish_swapped(ahead, 0)
     finish_swapped(behind, 0)
-    finish_swapped(ahead, 0)
     behind.outer_pass(2)
     ahead.outer_pass(2)
+    send_swapped(ahead, 0)
+    finish_straight(behind, 1)
     send_swapped(behind, 0)
-    finish_straight(behind, 1)
-    send_swapped(ahead, 0)
     finish_straight(ahead, 1)
     behind_sent = result(behind)
     ahead_sent = result(ahead)

time: 144 us -> 147 us (1.021)
  local copies, waits for them, and re-layouts: 8.61 us -> 12.2 us
  starting transfers between devices: 72.6 us -> 71 us
    unnamed x20 -> x28, local copies, waits for them, and re-layouts: 3.14 us -> 6.11 us
    ppermute x23, waiting for transfers between devices: 16.8 us -> 19.6 us  [between(): return lax.ppermute(value, 'expert', pairs)]
  transfers between devices with their start and end apart: 37 -> 37, of which waited for: 10 -> 12; matrix products, arithmetic and copies ran while one was open for 3% -> 4% of each run, Pallas kernels for 20% -> 20%
where the time goes in v17:
time: 147 us; the launch traced here: 145 us
  starting transfers between devices  71 us (48%)
  waiting for transfers between devices  30.9 us (21%)
  Pallas kernels  29.4 us (20%)
  local copies, waits for them, and re-layouts  12.2 us (8%)
    ppermute x23, starting transfers between devices, between(): return lax.ppermute(value, 'expert', pairs)  37.2 us
    pallas_call x46, Pallas kernels, call(): pl.pallas_call(run, compiler_params=pltpu.CompilerParams(vmem_limit_bytes...  29.4 us
    ppermute x6, starting transfers between devices, to_section(): return lax.ppermute(value, ('section', 'expert'), pairs)  25.8 us
    ppermute x23, waiting for transfers between devices, between(): return lax.ppermute(value, 'expert', pairs)  19.6 us
    ppermute x8, starting transfers between devices, swapped(): return lax.ppermute(value, 'expert', [(i, i ^ 1) for i in range(devices)])  8.01 us
    ppermute x8, waiting for transfers between devices, swapped(): return lax.ppermute(value, 'expert', [(i, i ^ 1) for i in range(devices)])  6.92 us
    unnamed x28, local copies, waits for them, and re-layouts  6.11 us
    ppermute x6, waiting for transfers between devices, to_section(): return lax.ppermute(value, ('section', 'expert'), pairs)  4.33 us
  transfers between devices with their start and end apart: 37, of which 12 were waited for; matrix products, arithmetic and copies ran while one was open for 4% of the time, Pallas kernels for 20%

profile of v17, /device:TPU:1, one launch (start us, length us, event | category | flops | bytes accessed | tf_op | source)
XLA Modules:
  0.0 144.8 jit_solution(16656375954216111497)
XLA Ops:
  1.6 2.1 %collective-permute-start.2 = (bf16[192,896]{1,0:T(8,128)(2,1)S(1)}, bf16[192,896]{1,0:T(8,128)(2,1)}, u32[]{:S(2)}, u32[]{:S(2)}) collective-permute-start(bf16[192,896]{1,0:T(8,128)(2,1)S(1)} %slice_bitcast_fusion.refs_0_), channel_id=1, source_target_pairs={{0,1},{1,0},{2,3},{3,2},{4,5},{5,4},{6,7},{7,6},{8,9},{9,8},{10,11... | collective-permute-start | bytes 1032200 | tf_op jit(solution)/shard_map/ppermute | solution.py:290
  10.0 2.3 %dynamic-slice_bitcast_fusion.refs_2_ = bf16[2,512,1792]{2,1,0:T(8,128)(2,1)S(1)} fusion(bf16[1,1,2,1024,1792]{4,3,2,1,0:T(8,128)(2,1)} %param.12, s32[]{:T(128)S(6)} %select_n.18), kind=kLoop, calls=%fused_computation | loop fusion | bytes 7340036 | tf_op jit(solution)/shard_map/dynamic_slice | solution.py:324
  12.3 2.4 %behind_far_0.1.refs_1_.refs_0_ = bf16[2,192,512]{2,1,0:T(8,128)(2,1)S(1)} custom-call(bf16[192,896]{1,0:T(8,128)(2,1)S(1)} %slice_bitcast_fusion.refs_0_, bf16[192,896]{1,0:T(8,128)(2,1)} %collective-permute-done.2.refs_1_, bf16[2,512,1792]{2,1,0:T(8,128)(2,1)S(1)} %dynamic-slice_bitcast_fusion.refs_2_, bf16[192,896]{1,0:T(8,128)(2,1)S(1)} %grad_rows_0.1.refs_3_.refs_0_), custom_call_target="tpu_custom_call" | custom-call | flops 10400000000 | bytes 1024 | tf_op jit(solution)/shard_map/behind_far_0/pallas_call | solution.py:44
  16.6 2.4 %collective-permute-done.refs_1_ = bf16[192,896]{1,0:T(8,128)(2,1)} collective-permute-done((bf16[192,896]{1,0:T(8,128)(2,1)}, bf16[192,896]{1,0:T(8,128)(2,1)}, u32[]{:S(2)}, u32[]{:S(2)}) %collective-permute-start) | collective-permute-done | bytes 344096 | tf_op jit(solution)/shard_map/ppermute | solution.py:290
  19.0 2.4 %ahead_far_0.1.refs_2_.refs_0_ = bf16[2,192,512]{2,1,0:T(8,128)(2,1)S(1)} custom-call(bf16[192,896]{1,0:T(8,128)(2,1)} %ahead_rows_0.1.refs_1_.refs_0_, bf16[192,896]{1,0:T(8,128)(2,1)} %collective-permute-done.refs_1_, bf16[2,512,1792]{2,1,0:T(8,128)(2,1)S(1)} %dynamic-slice_bitcast_fusion.refs_2_, bf16[192,896]{1,0:T(8,128)(2,1)S(1)} %behind_rows_1.1.refs_3_.refs_0_.refs_2_), custom_call_target="tpu_custom_call" | custom-call | flops 10400000000 | bytes 1024 | tf_op jit(solution)/shard_map/ahead_far_0/pallas_call | solution.py:44
  30.8 2.9 %collective-permute-done.6.refs_1_.refs_3_ = bf16[192,896]{1,0:T(8,128)(2,1)S(1)} collective-permute-done((bf16[192,896]{1,0:T(8,128)(2,1)S(1)}, bf16[192,896]{1,0:T(8,128)(2,1)S(1)}, u32[]{:S(2)}, u32[]{:S(2)}) %collective-permute-start.6) | collective-permute-done | bytes 344096 | tf_op jit(solution)/shard_map/ppermute | solution.py:290
  35.0 2.6 %behind_near.1.refs_2_.refs_1_.refs_0_ = bf16[2,384,512]{2,1,0:T(8,128)(2,1)S(1)} custom-call(bf16[192,896]{1,0:T(8,128)(2,1)S(1)} %slice_bitcast_fusion.refs_0_, bf16[192,896]{1,0:T(8,128)(2,1)} %collective-permute-done.2.refs_1_, bf16[192,896]{1,0:T(8,128)(2,1)S(1)} %behind_rows_1.1.refs_3_.refs_0_.refs_2_, ...), custom_call_target="tpu_custom_call" | custom-call | flops 10400000000 | bytes 1024 | tf_op jit(solution)/shard_map/behind_near/pallas_call | solution.py:44
  38.6 3.8 %collective-permute-start.12 = (bf16[2,192,512]{2,1,0:T(8,128)(2,1)S(1)}, bf16[2,192,512]{2,1,0:T(8,128)(2,1)S(1)}, u32[]{:S(2)}, u32[]{:S(2)}) collective-permute-start(bf16[2,192,512]{2,1,0:T(8,128)(2,1)S(1)} %behind_outer_1.1.refs_1_), channel_id=1, source_target_pairs={{0,2},{1,3},{2,0},{3,1},{4,6},{5,7},{6,4},{7,5},{8,10},{9,11},{10,... | collective-permute-start | bytes 1179656 | tf_op jit(solution)/shard_map/ppermute | solution.py:275
  45.7 2.7 %ahead_near.1.refs_1_.refs_3_.refs_0_ = bf16[2,384,512]{2,1,0:T(8,128)(2,1)S(1)} custom-call(bf16[192,896]{1,0:T(8,128)(2,1)} %ahead_rows_0.1.refs_1_.refs_0_, bf16[192,896]{1,0:T(8,128)(2,1)} %collective-permute-done.refs_1_, bf16[192,896]{1,0:T(8,128)(2,1)S(1)} %ahead_rows_1.1.refs_3_.refs_0_.refs_2_, ...), custom_call_target="tpu_custom_call" | custom-call | flops 10400000000 | bytes 1024 | tf_op jit(solution)/shard_map/ahead_near/pallas_call | solution.py:44
  54.2 2.3 %collective-permute-start.14 = (bf16[1,192,512]{2,1,0:T(8,128)(2,1)S(1)}, bf16[1,192,512]{2,1,0:T(8,128)(2,1)S(1)}, u32[]{:S(2)}, u32[]{:S(2)}) collective-permute-start(bf16[1,192,512]{2,1,0:T(8,128)(2,1)S(1)} %grad_outer_1.1.refs_2_), channel_id=1, source_target_pairs={{0,2},{1,3},{2,0},{3,1},{4,6},{5,7},{6,4},{7,5},{8,10},{9,11},{10,... | collective-permute-start | bytes 589832 | tf_op jit(solution)/shard_map/ppermute | solution.py:275
  57.4 4.7 %collective-permute-done.14.refs_3_.refs_1_ = bf16[1,192,512]{2,1,0:T(8,128)(2,1)S(1)} collective-permute-done((bf16[1,192,512]{2,1,0:T(8,128)(2,1)S(1)}, bf16[1,192,512]{2,1,0:T(8,128)(2,1)S(1)}, u32[]{:S(2)}, u32[]{:S(2)}) %collective-permute-start.14) | collective-permute-done | bytes 196640 | tf_op jit(solution)/shard_map/ppermute | solution.py:275
  65.0 3.7 %collective-permute-start.17 = (bf16[2,192,512]{2,1,0:T(8,128)(2,1)S(1)}, bf16[2,192,512]{2,1,0:T(8,128)(2,1)S(1)}, u32[]{:S(2)}, u32[]{:S(2)}) collective-permute-start(bf16[2,192,512]{2,1,0:T(8,128)(2,1)S(1)} %ahead_outer_2.1.refs_1_), channel_id=1, source_target_pairs={{0,2},{1,3},{2,0},{3,1},{4,6},{5,7},{6,4},{7,5},{8,10},{9,11},{10,... | collective-permute-start | bytes 1179656 | tf_op jit(solution)/shard_map/ppermute | solution.py:275
  70.0 3.9 %collective-permute-start.21 = (bf16[1,192,512]{2,1,0:T(8,128)(2,1)S(1)}, bf16[1,192,512]{2,1,0:T(8,128)(2,1)S(1)}, u32[]{:S(2)}, u32[]{:S(2)}) collective-permute-start(bf16[1,192,512]{2,1,0:T(8,128)(2,1)S(1)} %grad_third_1.1.refs_1_), channel_id=1, source_target_pairs={{0,2},{1,3},{2,0},{3,1},{4,6},{5,7},{6,4},{7,5},{8,10},{9,11},{10,... | collective-permute-start | bytes 589832 | tf_op jit(solution)/shard_map/ppermute | solution.py:275
  73.9 4.4 %collective-permute-done.17.refs_0_.refs_1_ = bf16[2,192,512]{2,1,0:T(8,128)(2,1)S(1)} collective-permute-done((bf16[2,192,512]{2,1,0:T(8,128)(2,1)S(1)}, bf16[2,192,512]{2,1,0:T(8,128)(2,1)S(1)}, u32[]{:S(2)}, u32[]{:S(2)}) %collective-permute-start.17) | collective-permute-done | bytes 393248 | tf_op jit(solution)/shard_map/ppermute | solution.py:275
  79.2 3.4 %collective-permute-done.21.refs_3_ = bf16[1,192,512]{2,1,0:T(8,128)(2,1)S(1)} collective-permute-done((bf16[1,192,512]{2,1,0:T(8,128)(2,1)S(1)}, bf16[1,192,512]{2,1,0:T(8,128)(2,1)S(1)}, u32[]{:S(2)}, u32[]{:S(2)}) %collective-permute-start.21) | collective-permute-done | bytes 196640 | tf_op jit(solution)/shard_map/ppermute | solution.py:275
  84.2 3.3 %collective-permute-start.23 = (bf16[1,192,512]{2,1,0:T(8,128)(2,1)S(1)}, bf16[1,192,512]{2,1,0:T(8,128)(2,1)S(1)}, u32[]{:S(2)}, u32[]{:S(2)}) collective-permute-start(bf16[1,192,512]{2,1,0:T(8,128)(2,1)S(1)} %ahead_back_1.1.refs_1_), channel_id=1, source_target_pairs={{0,2},{1,3},{2,0},{3,1},{4,6},{5,7},{6,4},{7,5},{8,10},{9,11},{10,... | collective-permute-start | bytes 589832 | tf_op jit(solution)/shard_map/ppermute | solution.py:275
  87.5 3.3 %collective-permute-done.24.refs_0_.refs_3_ = bf16[2,192,512]{2,1,0:T(8,128)(2,1)S(1)} collective-permute-done((bf16[2,192,512]{2,1,0:T(8,128)(2,1)S(1)}, bf16[2,192,512]{2,1,0:T(8,128)(2,1)S(1)}, u32[]{:S(2)}, u32[]{:S(2)}) %collective-permute-start.24) | collective-permute-done | bytes 393248 | tf_op jit(solution)/shard_map/ppermute | solution.py:275
  96.1 2.2 %collective-permute-start.25 = (bf16[192,896]{1,0:T(8,128)(2,1)S(1)}, bf16[192,896]{1,0:T(8,128)(2,1)S(1)}, u32[]{:S(2)}, u32[]{:S(2)}) collective-permute-start(bf16[192,896]{1,0:T(8,128)(2,1)S(1)} %get-tuple-element.11.refs_5_), channel_id=1, source_target_pairs={{0,1},{1,0},{2,3},{3,2},{4,5},{5,4},{6,7},{7,6},{8,9},{9,8},{10,11... | collective-permute-start | bytes 1032200 | tf_op jit(solution)/shard_map/ppermute | solution.py:290
  100.3 3.8 %collective-permute-start.31 = (bf16[2,192,512]{2,1,0:T(8,128)(2,1)S(1)}, bf16[2,192,512]{2,1,0:T(8,128)(2,1)S(1)}, u32[]{:S(2)}, u32[]{:S(2)}) collective-permute-start(bf16[2,192,512]{2,1,0:T(8,128)(2,1)S(1)} %behind_back_2.1.refs_1_), channel_id=1, source_target_pairs={{0,2},{1,3},{2,0},{3,1},{4,6},{5,7},{6,4},{7,5},{8,10},{9,11},{10,... | collective-permute-start | bytes 1179656 | tf_op jit(solution)/shard_map/ppermute | solution.py:275
  104.9 10.8 %collective-permute-start.28 = (bf16[192,896]{1,0:T(8,128)(2,1)S(1)}, bf16[192,896]{1,0:T(8,128)(2,1)S(1)}, u32[]{:S(2)}, u32[]{:S(2)}) collective-permute-start(bf16[192,896]{1,0:T(8,128)(2,1)S(1)} %ahead_shares.1.refs_5_), channel_id=1, source_target_pairs={{0,8},{1,9},{2,10},{3,11},{4,12},{5,13},{6,14},{7,15},{8,16},{9,17... | collective-permute-start | bytes 1032200 | tf_op jit(solution)/shard_map/ppermute | solution.py:299
  117.7 5.4 %collective-permute-start.35 = (bf16[192,896]{1,0:T(8,128)(2,1)S(1)}, bf16[192,896]{1,0:T(8,128)(2,1)S(1)}, u32[]{:S(2)}, u32[]{:S(2)}) collective-permute-start(bf16[192,896]{1,0:T(8,128)(2,1)S(1)} %get-tuple-element.14.refs_2_), channel_id=1, source_target_pairs={{8,1},{9,0},{10,3},{11,2},{12,5},{13,4},{14,7},{15,6},{16,9},{17,8... | collective-permute-start | bytes 1032200 | tf_op jit(solution)/shard_map/ppermute | solution.py:299
  131.7 3.1 %collective-permute-start.32 = (bf16[192,896]{1,0:T(8,128)(2,1)S(1)}, bf16[192,896]{1,0:T(8,128)(2,1)S(1)}, u32[]{:S(2)}, u32[]{:S(2)}) collective-permute-start(bf16[192,896]{1,0:T(8,128)(2,1)S(1)} %get-tuple-element.15.refs_3_), channel_id=1, source_target_pairs={{0,9},{1,8},{2,11},{3,10},{4,13},{5,12},{6,15},{7,14},{8,17},{9,16... | collective-permute-start | bytes 1032200 | tf_op jit(solution)/shard_map/ppermute | solution.py:299
  134.9 2.6 %collective-permute-start.33 = (bf16[192,896]{1,0:T(8,128)(2,1)S(1)}, bf16[192,896]{1,0:T(8,128)(2,1)S(1)}, u32[]{:S(2)}, u32[]{:S(2)}) collective-permute-start(bf16[192,896]{1,0:T(8,128)(2,1)S(1)} %get-tuple-element.16), channel_id=1, source_target_pairs={{0,8},{1,9},{2,10},{3,11},{4,12},{5,13},{6,14},{7,15},{8,16},{9,17... | collective-permute-start | bytes 1032200 | tf_op jit(solution)/shard_map/ppermute | solution.py:299
  140.3 2.5 %collective-permute-done.33.refs_2_ = bf16[192,896]{1,0:T(8,128)(2,1)S(1)} collective-permute-done((bf16[192,896]{1,0:T(8,128)(2,1)S(1)}, bf16[192,896]{1,0:T(8,128)(2,1)S(1)}, u32[]{:S(2)}, u32[]{:S(2)}) %collective-permute-start.33) | collective-permute-done | bytes 344096 | tf_op jit(solution)/shard_map/ppermute | solution.py:299
  (134 shorter events, 60.3 us)
Async XLA Ops:
  1.6 10.6 %collective-permute-start.2 = (bf16[192,896]{1,0:T(8,128)(2,1)S(1)}, bf16[192,896]{1,0:T(8,128)(2,1)}, u32[]{:S(2)}, u32[]{:S(2)}) collective-permute-start(bf16[192,896]{1,0:T(8,128)(2,1)S(1)} %slice_bitcast_fusion.refs_0_), channel_id=1, source_target_pairs={{0,1},{1,0},{2,3},{3,2},{4,5},{5,4},{6,7},{7,6},{8,9},{9,8},{10,11... | collective-permute-start | bytes 1032200 | tf_op jit(solution)/shard_map/ppermute | solution.py:290
  5.6 13.4 %collective-permute-start = (bf16[192,896]{1,0:T(8,128)(2,1)}, bf16[192,896]{1,0:T(8,128)(2,1)}, u32[]{:S(2)}, u32[]{:S(2)}) collective-permute-start(bf16[192,896]{1,0:T(8,128)(2,1)} %ahead_rows_0.1.refs_1_.refs_0_), channel_id=1, source_target_pairs={{0,1},{1,0},{2,3},{3,2},{4,5},{5,4},{6,7},{7,6},{8,9},{9,8},{10,11... | collective-permute-start | bytes 1032200 | tf_op jit(solution)/shard_map/ppermute | solution.py:290
  6.2 20.3 %collective-permute-start.1 = (bf16[192,896]{1,0:T(8,128)(2,1)S(1)}, bf16[192,896]{1,0:T(8,128)(2,1)}, u32[]{:S(2)}, u32[]{:S(2)}) collective-permute-start(bf16[192,896]{1,0:T(8,128)(2,1)S(1)} %grad_rows_0.1.refs_3_.refs_0_), channel_id=1, source_target_pairs={{0,1},{1,0},{2,3},{3,2},{4,5},{5,4},{6,7},{7,6},{8,9},{9,8},{10,11... | collective-permute-start | bytes 1032200 | tf_op jit(solution)/shard_map/ppermute | solution.py:290
  16.0 17.6 %collective-permute-start.6 = (bf16[192,896]{1,0:T(8,128)(2,1)S(1)}, bf16[192,896]{1,0:T(8,128)(2,1)S(1)}, u32[]{:S(2)}, u32[]{:S(2)}) collective-permute-start(bf16[192,896]{1,0:T(8,128)(2,1)S(1)} %behind_rows_1.1.refs_3_.refs_0_.refs_2_), channel_id=1, source_target_pairs={{0,1},{1,0},{2,3},{3,2},{4,5},{5,4},{6,7},{7,6},{8,9},{9,8},{10,11... | collective-permute-start | bytes 1032200 | tf_op jit(solution)/shard_map/ppermute | solution.py:290
  21.5 16.2 %collective-permute-start.8 = (bf16[2,192,512]{2,1,0:T(8,128)(2,1)S(1)}, bf16[2,192,512]{2,1,0:T(8,128)(2,1)S(1)}, u32[]{:S(2)}, u32[]{:S(2)}) collective-permute-start(bf16[2,192,512]{2,1,0:T(8,128)(2,1)S(1)} %ahead_far_0.1.refs_2_.refs_0_), channel_id=1, source_target_pairs={{0,2},{1,3},{2,0},{3,1},{4,6},{5,7},{6,4},{7,5},{8,10},{9,11},{10,... | collective-permute-start | bytes 1179656 | tf_op jit(solution)/shard_map/ppermute | solution.py:275
  24.0 14.4 %collective-permute-start.7 = (bf16[2,192,512]{2,1,0:T(8,128)(2,1)S(1)}, bf16[2,192,512]{2,1,0:T(8,128)(2,1)S(1)}, u32[]{:S(2)}, u32[]{:S(2)}) collective-permute-start(bf16[2,192,512]{2,1,0:T(8,128)(2,1)S(1)} %behind_middle_0.1.refs_3_), channel_id=1, source_target_pairs={{0,0},{1,1},{2,4},{3,5},{4,2},{5,3},{6,6},{7,7},{8,8},{9,9},{10,12... | collective-permute-start | bytes 1179656 | tf_op jit(solution)/shard_map/ppermute | solution.py:275
  28.1 15.5 %collective-permute-start.5 = (bf16[1,192,512]{2,1,0:T(8,128)(2,1)S(1)}, bf16[1,192,512]{2,1,0:T(8,128)(2,1)S(1)}, u32[]{:S(2)}, u32[]{:S(2)}) collective-permute-start(bf16[1,192,512]{2,1,0:T(8,128)(2,1)S(1)} %grad_far_0.1.refs_1_.refs_0_), channel_id=1, source_target_pairs={{0,2},{1,3},{2,0},{3,1},{4,6},{5,7},{6,4},{7,5},{8,10},{9,11},{10,... | collective-permute-start | bytes 589832 | tf_op jit(solution)/shard_map/ppermute | solution.py:275
  30.1 14.3 %collective-permute-start.4 = (bf16[192,896]{1,0:T(8,128)(2,1)S(1)}, bf16[192,896]{1,0:T(8,128)(2,1)S(1)}, u32[]{:S(2)}, u32[]{:S(2)}) collective-permute-start(bf16[192,896]{1,0:T(8,128)(2,1)S(1)} %ahead_rows_1.1.refs_3_.refs_0_.refs_2_), channel_id=1, source_target_pairs={{0,1},{1,0},{2,3},{3,2},{4,5},{5,4},{6,7},{7,6},{8,9},{9,8},{10,11... | collective-permute-start | bytes 1032200 | tf_op jit(solution)/shard_map/ppermute | solution.py:290
  37.8 10.7 %collective-permute-start.9 = (bf16[2,192,512]{2,1,0:T(8,128)(2,1)S(1)}, bf16[2,192,512]{2,1,0:T(8,128)(2,1)S(1)}, u32[]{:S(2)}, u32[]{:S(2)}) collective-permute-start(bf16[2,192,512]{2,1,0:T(8,128)(2,1)S(1)} %ahead_middle_0.1.refs_3_), channel_id=1, source_target_pairs={{0,0},{1,1},{2,4},{3,5},{4,2},{5,3},{6,6},{7,7},{8,8},{9,9},{10,12... | collective-permute-start | bytes 1179656 | tf_op jit(solution)/shard_map/ppermute | solution.py:275
  38.6 11.6 %collective-permute-start.12 = (bf16[2,192,512]{2,1,0:T(8,128)(2,1)S(1)}, bf16[2,192,512]{2,1,0:T(8,128)(2,1)S(1)}, u32[]{:S(2)}, u32[]{:S(2)}) collective-permute-start(bf16[2,192,512]{2,1,0:T(8,128)(2,1)S(1)} %behind_outer_1.1.refs_1_), channel_id=1, source_target_pairs={{0,2},{1,3},{2,0},{3,1},{4,6},{5,7},{6,4},{7,5},{8,10},{9,11},{10,... | collective-permute-start | bytes 1179656 | tf_op jit(solution)/shard_map/ppermute | solution.py:275
  43.7 10.5 %collective-permute-start.13 = (bf16[1,192,512]{2,1,0:T(8,128)(2,1)S(1)}, bf16[1,192,512]{2,1,0:T(8,128)(2,1)S(1)}, u32[]{:S(2)}, u32[]{:S(2)}) collective-permute-start(bf16[1,192,512]{2,1,0:T(8,128)(2,1)S(1)} %grad_middle_0.1.refs_3_), channel_id=1, source_target_pairs={{0,0},{1,1},{2,4},{3,5},{4,2},{5,3},{6,6},{7,7},{8,8},{9,9},{10,12... | collective-permute-start | bytes 589832 | tf_op jit(solution)/shard_map/ppermute | solution.py:275
  50.3 12.1 %collective-permute-start.15 = (bf16[2,192,512]{2,1,0:T(8,128)(2,1)S(1)}, bf16[2,192,512]{2,1,0:T(8,128)(2,1)S(1)}, u32[]{:S(2)}, u32[]{:S(2)}) collective-permute-start(bf16[2,192,512]{2,1,0:T(8,128)(2,1)S(1)} %behind_middle_1.1.refs_3_), channel_id=1, source_target_pairs={{0,0},{1,1},{2,4},{3,5},{4,2},{5,3},{6,6},{7,7},{8,8},{9,9},{10,12... | collective-permute-start | bytes 1179656 | tf_op jit(solution)/shard_map/ppermute | solution.py:275
  65.0 13.3 %collective-permute-start.17 = (bf16[2,192,512]{2,1,0:T(8,128)(2,1)S(1)}, bf16[2,192,512]{2,1,0:T(8,128)(2,1)S(1)}, u32[]{:S(2)}, u32[]{:S(2)}) collective-permute-start(bf16[2,192,512]{2,1,0:T(8,128)(2,1)S(1)} %ahead_outer_2.1.refs_1_), channel_id=1, source_target_pairs={{0,2},{1,3},{2,0},{3,1},{4,6},{5,7},{6,4},{7,5},{8,10},{9,11},{10,... | collective-permute-start | bytes 1179656 | tf_op jit(solution)/shard_map/ppermute | solution.py:275
  69.2 13.6 %collective-permute-start.22 = (bf16[2,192,512]{2,1,0:T(8,128)(2,1)S(1)}, bf16[2,192,512]{2,1,0:T(8,128)(2,1)S(1)}, u32[]{:S(2)}, u32[]{:S(2)}) collective-permute-start(bf16[2,192,512]{2,1,0:T(8,128)(2,1)S(1)} %behind_first_0.1.refs_2_.refs_1_), channel_id=1, source_target_pairs={{0,0},{1,1},{2,4},{3,5},{4,2},{5,3},{6,6},{7,7},{8,8},{9,9},{10,12... | collective-permute-start | bytes 1179656 | tf_op jit(solution)/shard_map/ppermute | solution.py:275
  70.0 12.5 %collective-permute-start.21 = (bf16[1,192,512]{2,1,0:T(8,128)(2,1)S(1)}, bf16[1,192,512]{2,1,0:T(8,128)(2,1)S(1)}, u32[]{:S(2)}, u32[]{:S(2)}) collective-permute-start(bf16[1,192,512]{2,1,0:T(8,128)(2,1)S(1)} %grad_third_1.1.refs_1_), channel_id=1, source_target_pairs={{0,2},{1,3},{2,0},{3,1},{4,6},{5,7},{6,4},{7,5},{8,10},{9,11},{10,... | collective-permute-start | bytes 589832 | tf_op jit(solution)/shard_map/ppermute | solution.py:275
  84.2 9.4 %collective-permute-start.23 = (bf16[1,192,512]{2,1,0:T(8,128)(2,1)S(1)}, bf16[1,192,512]{2,1,0:T(8,128)(2,1)S(1)}, u32[]{:S(2)}, u32[]{:S(2)}) collective-permute-start(bf16[1,192,512]{2,1,0:T(8,128)(2,1)S(1)} %ahead_back_1.1.refs_1_), channel_id=1, source_target_pairs={{0,2},{1,3},{2,0},{3,1},{4,6},{5,7},{6,4},{7,5},{8,10},{9,11},{10,... | collective-permute-start | bytes 589832 | tf_op jit(solution)/shard_map/ppermute | solution.py:275
  93.7 10.4 %collective-permute-start.26 = (bf16[1,192,512]{2,1,0:T(8,128)(2,1)S(1)}, bf16[1,192,512]{2,1,0:T(8,128)(2,1)S(1)}, u32[]{:S(2)}, u32[]{:S(2)}) collective-permute-start(bf16[1,192,512]{2,1,0:T(8,128)(2,1)S(1)} %ahead_first_1.1.refs_6_.refs_1_), channel_id=1, source_target_pairs={{0,0},{1,1},{2,4},{3,5},{4,2},{5,3},{6,6},{7,7},{8,8},{9,9},{10,12... | collective-permute-start | bytes 589832 | tf_op jit(solution)/shard_map/ppermute | solution.py:275
  100.2 22.9 %collective-permute-start.30 = (bf16[192,896]{1,0:T(8,128)(2,1)S(1)}, bf16[192,896]{1,0:T(8,128)(2,1)S(1)}, u32[]{:S(2)}, u32[]{:S(2)}) collective-permute-start(bf16[192,896]{1,0:T(8,128)(2,1)S(1)} %get-tuple-element.12.refs_1_), channel_id=1, source_target_pairs={{0,1},{1,0},{2,3},{3,2},{4,5},{5,4},{6,7},{7,6},{8,9},{9,8},{10,11... | collective-permute-start | bytes 1032200 | tf_op jit(solution)/shard_map/ppermute | solution.py:290
  100.3 15.5 %collective-permute-start.31 = (bf16[2,192,512]{2,1,0:T(8,128)(2,1)S(1)}, bf16[2,192,512]{2,1,0:T(8,128)(2,1)S(1)}, u32[]{:S(2)}, u32[]{:S(2)}) collective-permute-start(bf16[2,192,512]{2,1,0:T(8,128)(2,1)S(1)} %behind_back_2.1.refs_1_), channel_id=1, source_target_pairs={{0,2},{1,3},{2,0},{3,1},{4,6},{5,7},{6,4},{7,5},{8,10},{9,11},{10,... | collective-permute-start | bytes 1179656 | tf_op jit(solution)/shard_map/ppermute | solution.py:275
  104.8 22.4 %collective-permute-start.29 = (bf16[1,192,512]{2,1,0:T(8,128)(2,1)}, bf16[1,192,512]{2,1,0:T(8,128)(2,1)S(1)}, u32[]{:S(2)}, u32[]{:S(2)}) collective-permute-start(bf16[1,192,512]{2,1,0:T(8,128)(2,1)} %ahead_back_2.1.refs_2_), channel_id=1, source_target_pairs={{0,2},{1,3},{2,0},{3,1},{4,6},{5,7},{6,4},{7,5},{8,10},{9,11},{10,... | collective-permute-start | bytes 589832 | tf_op jit(solution)/shard_map/ppermute | solution.py:275
  104.9 22.3 %collective-permute-start.28 = (bf16[192,896]{1,0:T(8,128)(2,1)S(1)}, bf16[192,896]{1,0:T(8,128)(2,1)S(1)}, u32[]{:S(2)}, u32[]{:S(2)}) collective-permute-start(bf16[192,896]{1,0:T(8,128)(2,1)S(1)} %ahead_shares.1.refs_5_), channel_id=1, source_target_pairs={{0,8},{1,9},{2,10},{3,11},{4,12},{5,13},{6,14},{7,15},{8,16},{9,17... | collective-permute-start | bytes 1032200 | tf_op jit(solution)/shard_map/ppermute | solution.py:299
  117.7 19.8 %collective-permute-start.35 = (bf16[192,896]{1,0:T(8,128)(2,1)S(1)}, bf16[192,896]{1,0:T(8,128)(2,1)S(1)}, u32[]{:S(2)}, u32[]{:S(2)}) collective-permute-start(bf16[192,896]{1,0:T(8,128)(2,1)S(1)} %get-tuple-element.14.refs_2_), channel_id=1, source_target_pairs={{8,1},{9,0},{10,3},{11,2},{12,5},{13,4},{14,7},{15,6},{16,9},{17,8... | collective-permute-start | bytes 1032200 | tf_op jit(solution)/shard_map/ppermute | solution.py:299
  123.2 14.2 %collective-permute-start.34 = (bf16[192,896]{1,0:T(8,128)(2,1)S(1)}, bf16[192,896]{1,0:T(8,128)(2,1)S(1)}, u32[]{:S(2)}, u32[]{:S(2)}) collective-permute-start(bf16[192,896]{1,0:T(8,128)(2,1)S(1)} %behind_shares.1.refs_6_), channel_id=1, source_target_pairs={{8,0},{9,1},{10,2},{11,3},{12,4},{13,5},{14,6},{15,7},{16,8},{17,9... | collective-permute-start | bytes 1032200 | tf_op jit(solution)/shard_map/ppermute | solution.py:299
  125.1 12.3 %collective-permute-start.36 = (bf16[192,896]{1,0:T(8,128)(2,1)S(1)}, bf16[192,896]{1,0:T(8,128)(2,1)S(1)}, u32[]{:S(2)}, u32[]{:S(2)}) collective-permute-start(bf16[192,896]{1,0:T(8,128)(2,1)S(1)} %get-tuple-element.17), channel_id=1, source_target_pairs={{8,0},{9,1},{10,2},{11,3},{12,4},{13,5},{14,6},{15,7},{16,8},{17,9... | collective-permute-start | bytes 1032200 | tf_op jit(solution)/shard_map/ppermute | solution.py:299
  (27 other events, 145.7 us)

commit v18 on v16

--- a/solution.py
+++ b/solution.py
@@ -478,20 +478,20 @@
     behind.fetch(1)
     ahead.far_product(0)
     ahead.first_hop(0)
+    behind.middle_sum(0)
     grad.far_product(0)
     grad.first_hop(0)
-    behind.middle_sum(0)
     ahead.fetch(1)
     behind.far_product(1)
     behind.near_products()
+    behind.merged_hop(1, behind.far[1])
     ahead.middle_sum(0)
-    behind.merged_hop(1, behind.far[1])
     grad.fetch(1)
     grad.middle_sum(0)
     ahead.far_product(1)
+    behind.middle_sum(1)
     ahead.near_products()
     ahead.merged_hop(1, ahead.far[1])
-    behind.middle_sum(1)
     grad.far_product(1)
     grad.near_products()
     grad.merged_hop(1, grad.far[1])
@@ -501,8 +501,8 @@
     grad.middle_sum(1)
     activate_ahead(0)
     ahead.merged_hop(2, ahead.act[0])
+    behind.middle_pass(0)
     grad.last_third_hop()
-    behind.middle_pass(0)
     ahead.middle_pass(0)
     activate_ahead(1)
     activate_behind(1)

time: 144 us -> 146 us (1.014)
  waiting for transfers between devices: 30 us -> 35.4 us
  starting transfers between devices: 72.6 us -> 70.1 us
    ppermute x23, waiting for transfers between devices: 16.8 us -> 24 us  [between(): return lax.ppermute(value, 'expert', pairs)]
    ppermute x8, starting transfers between devices: 8.74 us -> 6.85 us  [swapped(): return lax.ppermute(value, 'expert', [(i, i ^ 1) for i in range(devices)])]
    ppermute x8, waiting for transfers between devices: 7.97 us -> 6.48 us  [swapped(): return lax.ppermute(value, 'expert', [(i, i ^ 1) for i in range(devices)])]
  transfers between devices with their start and end apart: 37 -> 37, of which waited for: 10 -> 14; matrix products, arithmetic and copies ran while one was open for 3% -> 3% of each run, Pallas kernels for 20% -> 20%
where the time goes in v18:
time: 146 us; the launch traced here: 145 us
  starting transfers between devices  70.1 us (48%)
  waiting for transfers between devices  35.4 us (24%)
  Pallas kernels  29.8 us (20%)
  local copies, waits for them, and re-layouts  8.16 us (6%)
    ppermute x23, starting transfers between devices, between(): return lax.ppermute(value, 'expert', pairs)  36.2 us
    pallas_call x46, Pallas kernels, call(): pl.pallas_call(run, compiler_params=pltpu.CompilerParams(vmem_limit_bytes...  29.8 us
    ppermute x6, starting transfers between devices, to_section(): return lax.ppermute(value, ('section', 'expert'), pairs)  27 us
    ppermute x23, waiting for transfers between devices, between(): return lax.ppermute(value, 'expert', pairs)  24 us
    ppermute x8, starting transfers between devices, swapped(): return lax.ppermute(value, 'expert', [(i, i ^ 1) for i in range(devices)])  6.85 us
    ppermute x8, waiting for transfers between devices, swapped(): return lax.ppermute(value, 'expert', [(i, i ^ 1) for i in range(devices)])  6.48 us
    ppermute x6, waiting for transfers between devices, to_section(): return lax.ppermute(value, ('section', 'expert'), pairs)  5 us
    dynamic_slice x2, local copies, waits for them, and re-layouts, far_half(): lax.dynamic_slice(weights, (0, start, 0), (parts, units // 2, features))  3.9 us
  transfers between devices with their start and end apart: 37, of which 14 were waited for; matrix products, arithmetic and copies ran while one was open for 3% of the time, Pallas kernels for 20%

profile of v18, /device:TPU:1, one launch (start us, length us, event | category | flops | bytes accessed | tf_op | source)
XLA Modules:
  0.0 144.9 jit_solution(18248308654554201151)
XLA Ops:
  1.6 2.1 %collective-permute-start.2 = (bf16[192,896]{1,0:T(8,128)(2,1)S(1)}, bf16[192,896]{1,0:T(8,128)(2,1)}, u32[]{:S(2)}, u32[]{:S(2)}) collective-permute-start(bf16[192,896]{1,0:T(8,128)(2,1)S(1)} %slice_bitcast_fusion.refs_0_), channel_id=1, source_target_pairs={{0,1},{1,0},{2,3},{3,2},{4,5},{5,4},{6,7},{7,6},{8,9},{9,8},{10,11... | collective-permute-start | bytes 1032200 | tf_op jit(solution)/shard_map/ppermute | solution.py:290
  10.2 2.3 %dynamic-slice_bitcast_fusion.refs_2_ = bf16[2,512,1792]{2,1,0:T(8,128)(2,1)S(1)} fusion(bf16[1,1,2,1024,1792]{4,3,2,1,0:T(8,128)(2,1)} %param.12, s32[]{:T(128)S(6)} %select_n.18), kind=kLoop, calls=%fused_computation | loop fusion | bytes 7340036 | tf_op jit(solution)/shard_map/dynamic_slice | solution.py:324
  12.5 2.4 %behind_far_0.1.refs_1_.refs_0_ = bf16[2,192,512]{2,1,0:T(8,128)(2,1)S(1)} custom-call(bf16[192,896]{1,0:T(8,128)(2,1)S(1)} %slice_bitcast_fusion.refs_0_, bf16[192,896]{1,0:T(8,128)(2,1)} %collective-permute-done.2.refs_1_, bf16[2,512,1792]{2,1,0:T(8,128)(2,1)S(1)} %dynamic-slice_bitcast_fusion.refs_2_, bf16[192,896]{1,0:T(8,128)(2,1)} %grad_rows_0.1.refs_3_.refs_0_), custom_call_target="tpu_custom_call" | custom-call | flops 10400000000 | bytes 1024 | tf_op jit(solution)/shard_map/behind_far_0/pallas_call | solution.py:44
  16.8 2.3 %collective-permute-done.refs_1_ = bf16[192,896]{1,0:T(8,128)(2,1)} collective-permute-done((bf16[192,896]{1,0:T(8,128)(2,1)}, bf16[192,896]{1,0:T(8,128)(2,1)}, u32[]{:S(2)}, u32[]{:S(2)}) %collective-permute-start) | collective-permute-done | bytes 344096 | tf_op jit(solution)/shard_map/ppermute | solution.py:290
  19.0 2.4 %ahead_far_0.1.refs_2_.refs_0_ = bf16[2,192,512]{2,1,0:T(8,128)(2,1)S(1)} custom-call(bf16[192,896]{1,0:T(8,128)(2,1)} %ahead_rows_0.1.refs_1_.refs_0_, bf16[192,896]{1,0:T(8,128)(2,1)} %collective-permute-done.refs_1_, bf16[2,512,1792]{2,1,0:T(8,128)(2,1)S(1)} %dynamic-slice_bitcast_fusion.refs_2_, bf16[192,896]{1,0:T(8,128)(2,1)S(1)} %behind_rows_1.1.refs_3_.refs_0_.refs_2_), custom_call_target="tpu_custom_call" | custom-call | flops 10400000000 | bytes 1024 | tf_op jit(solution)/shard_map/ahead_far_0/pallas_call | solution.py:44
  28.2 2.3 %collective-permute-start.8 = (bf16[1,192,512]{2,1,0:T(8,128)(2,1)S(1)}, bf16[1,192,512]{2,1,0:T(8,128)(2,1)S(1)}, u32[]{:S(2)}, u32[]{:S(2)}) collective-permute-start(bf16[1,192,512]{2,1,0:T(8,128)(2,1)S(1)} %grad_far_0.1.refs_1_.refs_0_), channel_id=1, source_target_pairs={{0,2},{1,3},{2,0},{3,1},{4,6},{5,7},{6,4},{7,5},{8,10},{9,11},{10,... | collective-permute-start | bytes 589832 | tf_op jit(solution)/shard_map/ppermute | solution.py:275
  30.9 2.8 %collective-permute-done.5.refs_1_.refs_3_ = bf16[192,896]{1,0:T(8,128)(2,1)S(1)} collective-permute-done((bf16[192,896]{1,0:T(8,128)(2,1)S(1)}, bf16[192,896]{1,0:T(8,128)(2,1)S(1)}, u32[]{:S(2)}, u32[]{:S(2)}) %collective-permute-start.5) | collective-permute-done | bytes 344096 | tf_op jit(solution)/shard_map/ppermute | solution.py:290
  35.0 2.6 %behind_near.1.refs_1_.refs_3_.refs_0_ = bf16[2,384,512]{2,1,0:T(8,128)(2,1)S(1)} custom-call(bf16[192,896]{1,0:T(8,128)(2,1)S(1)} %slice_bitcast_fusion.refs_0_, bf16[192,896]{1,0:T(8,128)(2,1)} %collective-permute-done.2.refs_1_, bf16[192,896]{1,0:T(8,128)(2,1)S(1)} %behind_rows_1.1.refs_3_.refs_0_.refs_2_, ...), custom_call_target="tpu_custom_call" | custom-call | flops 10400000000 | bytes 1024 | tf_op jit(solution)/shard_map/behind_near/pallas_call | solution.py:44
  45.6 2.7 %ahead_near.1.refs_1_.refs_3_.refs_0_ = bf16[2,384,512]{2,1,0:T(8,128)(2,1)S(1)} custom-call(bf16[192,896]{1,0:T(8,128)(2,1)} %ahead_rows_0.1.refs_1_.refs_0_, bf16[192,896]{1,0:T(8,128)(2,1)} %collective-permute-done.refs_1_, bf16[192,896]{1,0:T(8,128)(2,1)S(1)} %ahead_rows_1.1.refs_3_.refs_0_.refs_2_, ...), custom_call_target="tpu_custom_call" | custom-call | flops 10400000000 | bytes 1024 | tf_op jit(solution)/shard_map/ahead_near/pallas_call | solution.py:44
  48.4 6.3 %collective-permute-start.11 = (bf16[2,192,512]{2,1,0:T(8,128)(2,1)S(1)}, bf16[2,192,512]{2,1,0:T(8,128)(2,1)S(1)}, u32[]{:S(2)}, u32[]{:S(2)}) collective-permute-start(bf16[2,192,512]{2,1,0:T(8,128)(2,1)S(1)} %ahead_outer_1.1.refs_3_), channel_id=1, source_target_pairs={{0,2},{1,3},{2,0},{3,1},{4,6},{5,7},{6,4},{7,5},{8,10},{9,11},{10,... | collective-permute-start | bytes 1179656 | tf_op jit(solution)/shard_map/ppermute | solution.py:275
  60.6 3.8 %collective-permute-done.14.refs_3_.refs_1_ = bf16[1,192,512]{2,1,0:T(8,128)(2,1)S(1)} collective-permute-done((bf16[1,192,512]{2,1,0:T(8,128)(2,1)S(1)}, bf16[1,192,512]{2,1,0:T(8,128)(2,1)S(1)}, u32[]{:S(2)}, u32[]{:S(2)}) %collective-permute-start.14) | collective-permute-done | bytes 196640 | tf_op jit(solution)/shard_map/ppermute | solution.py:275
  66.8 3.9 %collective-permute-start.17 = (bf16[2,192,512]{2,1,0:T(8,128)(2,1)S(1)}, bf16[2,192,512]{2,1,0:T(8,128)(2,1)S(1)}, u32[]{:S(2)}, u32[]{:S(2)}) collective-permute-start(bf16[2,192,512]{2,1,0:T(8,128)(2,1)S(1)} %ahead_outer_2.1.refs_1_), channel_id=1, source_target_pairs={{0,2},{1,3},{2,0},{3,1},{4,6},{5,7},{6,4},{7,5},{8,10},{9,11},{10,... | collective-permute-start | bytes 1179656 | tf_op jit(solution)/shard_map/ppermute | solution.py:275
  73.4 3.0 %collective-permute-start.21 = (bf16[1,192,512]{2,1,0:T(8,128)(2,1)S(1)}, bf16[1,192,512]{2,1,0:T(8,128)(2,1)S(1)}, u32[]{:S(2)}, u32[]{:S(2)}) collective-permute-start(bf16[1,192,512]{2,1,0:T(8,128)(2,1)S(1)} %grad_third_1.1.refs_1_), channel_id=1, source_target_pairs={{0,2},{1,3},{2,0},{3,1},{4,6},{5,7},{6,4},{7,5},{8,10},{9,11},{10,... | collective-permute-start | bytes 589832 | tf_op jit(solution)/shard_map/ppermute | solution.py:275
  76.3 4.0 %collective-permute-done.17.refs_0_.refs_1_ = bf16[2,192,512]{2,1,0:T(8,128)(2,1)S(1)} collective-permute-done((bf16[2,192,512]{2,1,0:T(8,128)(2,1)S(1)}, bf16[2,192,512]{2,1,0:T(8,128)(2,1)S(1)}, u32[]{:S(2)}, u32[]{:S(2)}) %collective-permute-start.17) | collective-permute-done | bytes 393248 | tf_op jit(solution)/shard_map/ppermute | solution.py:275
  81.2 3.4 %collective-permute-done.21.refs_3_ = bf16[1,192,512]{2,1,0:T(8,128)(2,1)S(1)} collective-permute-done((bf16[1,192,512]{2,1,0:T(8,128)(2,1)S(1)}, bf16[1,192,512]{2,1,0:T(8,128)(2,1)S(1)}, u32[]{:S(2)}, u32[]{:S(2)}) %collective-permute-start.21) | collective-permute-done | bytes 196640 | tf_op jit(solution)/shard_map/ppermute | solution.py:275
  86.0 2.1 %collective-permute-start.23 = (bf16[1,192,512]{2,1,0:T(8,128)(2,1)S(1)}, bf16[1,192,512]{2,1,0:T(8,128)(2,1)S(1)}, u32[]{:S(2)}, u32[]{:S(2)}) collective-permute-start(bf16[1,192,512]{2,1,0:T(8,128)(2,1)S(1)} %ahead_back_1.1.refs_1_), channel_id=1, source_target_pairs={{0,2},{1,3},{2,0},{3,1},{4,6},{5,7},{6,4},{7,5},{8,10},{9,11},{10,... | collective-permute-start | bytes 589832 | tf_op jit(solution)/shard_map/ppermute | solution.py:275
  88.2 5.5 %collective-permute-done.24.refs_0_.refs_3_ = bf16[2,192,512]{2,1,0:T(8,128)(2,1)S(1)} collective-permute-done((bf16[2,192,512]{2,1,0:T(8,128)(2,1)S(1)}, bf16[2,192,512]{2,1,0:T(8,128)(2,1)S(1)}, u32[]{:S(2)}, u32[]{:S(2)}) %collective-permute-start.24) | collective-permute-done | bytes 393248 | tf_op jit(solution)/shard_map/ppermute | solution.py:275
  101.8 4.2 %collective-permute-start.27 = (bf16[2,192,512]{2,1,0:T(8,128)(2,1)S(1)}, bf16[2,192,512]{2,1,0:T(8,128)(2,1)S(1)}, u32[]{:S(2)}, u32[]{:S(2)}) collective-permute-start(bf16[2,192,512]{2,1,0:T(8,128)(2,1)S(1)} %behind_back_2.1.refs_1_), channel_id=1, source_target_pairs={{0,2},{1,3},{2,0},{3,1},{4,6},{5,7},{6,4},{7,5},{8,10},{9,11},{10,... | collective-permute-start | bytes 1179656 | tf_op jit(solution)/shard_map/ppermute | solution.py:275
  106.2 11.0 %collective-permute-start.34 = (bf16[192,896]{1,0:T(8,128)(2,1)S(1)}, bf16[192,896]{1,0:T(8,128)(2,1)S(1)}, u32[]{:S(2)}, u32[]{:S(2)}) collective-permute-start(bf16[192,896]{1,0:T(8,128)(2,1)S(1)} %behind_shares.1.refs_5_), channel_id=1, source_target_pairs={{8,0},{9,1},{10,2},{11,3},{12,4},{13,5},{14,6},{15,7},{16,8},{17,9... | collective-permute-start | bytes 1032200 | tf_op jit(solution)/shard_map/ppermute | solution.py:299
  119.1 5.5 %collective-permute-start.35 = (bf16[192,896]{1,0:T(8,128)(2,1)S(1)}, bf16[192,896]{1,0:T(8,128)(2,1)S(1)}, u32[]{:S(2)}, u32[]{:S(2)}) collective-permute-start(bf16[192,896]{1,0:T(8,128)(2,1)S(1)} %get-tuple-element.14.refs_2_), channel_id=1, source_target_pairs={{8,1},{9,0},{10,3},{11,2},{12,5},{13,4},{14,7},{15,6},{16,9},{17,8... | collective-permute-start | bytes 1032200 | tf_op jit(solution)/shard_map/ppermute | solution.py:299
  126.7 3.6 %collective-permute-start.30 = (bf16[192,896]{1,0:T(8,128)(2,1)S(1)}, bf16[192,896]{1,0:T(8,128)(2,1)S(1)}, u32[]{:S(2)}, u32[]{:S(2)}) collective-permute-start(bf16[192,896]{1,0:T(8,128)(2,1)S(1)} %ahead_shares.1.refs_6_), channel_id=1, source_target_pairs={{0,8},{1,9},{2,10},{3,11},{4,12},{5,13},{6,14},{7,15},{8,16},{9,17... | collective-permute-start | bytes 1032200 | tf_op jit(solution)/shard_map/ppermute | solution.py:299
  131.9 3.0 %collective-permute-start.32 = (bf16[192,896]{1,0:T(8,128)(2,1)S(1)}, bf16[192,896]{1,0:T(8,128)(2,1)S(1)}, u32[]{:S(2)}, u32[]{:S(2)}) collective-permute-start(bf16[192,896]{1,0:T(8,128)(2,1)S(1)} %get-tuple-element.15.refs_3_), channel_id=1, source_target_pairs={{0,9},{1,8},{2,11},{3,10},{4,13},{5,12},{6,15},{7,14},{8,17},{9,16... | collective-permute-start | bytes 1032200 | tf_op jit(solution)/shard_map/ppermute | solution.py:299
  137.8 2.6 %collective-permute-done.32.refs_1_ = bf16[192,896]{1,0:T(8,128)(2,1)S(1)} collective-permute-done((bf16[192,896]{1,0:T(8,128)(2,1)S(1)}, bf16[192,896]{1,0:T(8,128)(2,1)S(1)}, u32[]{:S(2)}, u32[]{:S(2)}) %collective-permute-start.32) | collective-permute-done | bytes 344096 | tf_op jit(solution)/shard_map/ppermute | solution.py:299
  140.5 2.4 %collective-permute-done.33.refs_2_ = bf16[192,896]{1,0:T(8,128)(2,1)S(1)} collective-permute-done((bf16[192,896]{1,0:T(8,128)(2,1)S(1)}, bf16[192,896]{1,0:T(8,128)(2,1)S(1)}, u32[]{:S(2)}, u32[]{:S(2)}) %collective-permute-start.33) | collective-permute-done | bytes 344096 | tf_op jit(solution)/shard_map/ppermute | solution.py:299
  (126 shorter events, 57.3 us)
Async XLA Ops:
  1.6 10.8 %collective-permute-start.2 = (bf16[192,896]{1,0:T(8,128)(2,1)S(1)}, bf16[192,896]{1,0:T(8,128)(2,1)}, u32[]{:S(2)}, u32[]{:S(2)}) collective-permute-start(bf16[192,896]{1,0:T(8,128)(2,1)S(1)} %slice_bitcast_fusion.refs_0_), channel_id=1, source_target_pairs={{0,1},{1,0},{2,3},{3,2},{4,5},{5,4},{6,7},{7,6},{8,9},{9,8},{10,11... | collective-permute-start | bytes 1032200 | tf_op jit(solution)/shard_map/ppermute | solution.py:290
  5.6 13.4 %collective-permute-start = (bf16[192,896]{1,0:T(8,128)(2,1)}, bf16[192,896]{1,0:T(8,128)(2,1)}, u32[]{:S(2)}, u32[]{:S(2)}) collective-permute-start(bf16[192,896]{1,0:T(8,128)(2,1)} %ahead_rows_0.1.refs_1_.refs_0_), channel_id=1, source_target_pairs={{0,1},{1,0},{2,3},{3,2},{4,5},{5,4},{6,7},{7,6},{8,9},{9,8},{10,11... | collective-permute-start | bytes 1032200 | tf_op jit(solution)/shard_map/ppermute | solution.py:290
  6.9 19.6 %collective-permute-start.1 = (bf16[192,896]{1,0:T(8,128)(2,1)}, bf16[192,896]{1,0:T(8,128)(2,1)}, u32[]{:S(2)}, u32[]{:S(2)}) collective-permute-start(bf16[192,896]{1,0:T(8,128)(2,1)} %grad_rows_0.1.refs_3_.refs_0_), channel_id=1, source_target_pairs={{0,1},{1,0},{2,3},{3,2},{4,5},{5,4},{6,7},{7,6},{8,9},{9,8},{10,11... | collective-permute-start | bytes 1032200 | tf_op jit(solution)/shard_map/ppermute | solution.py:290
  16.2 17.4 %collective-permute-start.5 = (bf16[192,896]{1,0:T(8,128)(2,1)S(1)}, bf16[192,896]{1,0:T(8,128)(2,1)S(1)}, u32[]{:S(2)}, u32[]{:S(2)}) collective-permute-start(bf16[192,896]{1,0:T(8,128)(2,1)S(1)} %behind_rows_1.1.refs_3_.refs_0_.refs_2_), channel_id=1, source_target_pairs={{0,1},{1,0},{2,3},{3,2},{4,5},{5,4},{6,7},{7,6},{8,9},{9,8},{10,11... | collective-permute-start | bytes 1032200 | tf_op jit(solution)/shard_map/ppermute | solution.py:290
  21.5 17.6 %collective-permute-start.9 = (bf16[2,192,512]{2,1,0:T(8,128)(2,1)S(1)}, bf16[2,192,512]{2,1,0:T(8,128)(2,1)S(1)}, u32[]{:S(2)}, u32[]{:S(2)}) collective-permute-start(bf16[2,192,512]{2,1,0:T(8,128)(2,1)S(1)} %ahead_far_0.1.refs_2_.refs_0_), channel_id=1, source_target_pairs={{0,2},{1,3},{2,0},{3,1},{4,6},{5,7},{6,4},{7,5},{8,10},{9,11},{10,... | collective-permute-start | bytes 1179656 | tf_op jit(solution)/shard_map/ppermute | solution.py:275
  24.2 13.4 %collective-permute-start.6 = (bf16[2,192,512]{2,1,0:T(8,128)(2,1)S(1)}, bf16[2,192,512]{2,1,0:T(8,128)(2,1)S(1)}, u32[]{:S(2)}, u32[]{:S(2)}) collective-permute-start(bf16[2,192,512]{2,1,0:T(8,128)(2,1)S(1)} %behind_middle_0.1.refs_3_), channel_id=1, source_target_pairs={{0,0},{1,1},{2,4},{3,5},{4,2},{5,3},{6,6},{7,7},{8,8},{9,9},{10,12... | collective-permute-start | bytes 1179656 | tf_op jit(solution)/shard_map/ppermute | solution.py:275
  28.2 13.0 %collective-permute-start.8 = (bf16[1,192,512]{2,1,0:T(8,128)(2,1)S(1)}, bf16[1,192,512]{2,1,0:T(8,128)(2,1)S(1)}, u32[]{:S(2)}, u32[]{:S(2)}) collective-permute-start(bf16[1,192,512]{2,1,0:T(8,128)(2,1)S(1)} %grad_far_0.1.refs_1_.refs_0_), channel_id=1, source_target_pairs={{0,2},{1,3},{2,0},{3,1},{4,6},{5,7},{6,4},{7,5},{8,10},{9,11},{10,... | collective-permute-start | bytes 589832 | tf_op jit(solution)/shard_map/ppermute | solution.py:275
  30.6 11.3 %collective-permute-start.4 = (bf16[192,896]{1,0:T(8,128)(2,1)S(1)}, bf16[192,896]{1,0:T(8,128)(2,1)S(1)}, u32[]{:S(2)}, u32[]{:S(2)}) collective-permute-start(bf16[192,896]{1,0:T(8,128)(2,1)S(1)} %ahead_rows_1.1.refs_3_.refs_0_.refs_2_), channel_id=1, source_target_pairs={{0,1},{1,0},{2,3},{3,2},{4,5},{5,4},{6,7},{7,6},{8,9},{9,8},{10,11... | collective-permute-start | bytes 1032200 | tf_op jit(solution)/shard_map/ppermute | solution.py:290
  39.9 14.8 %collective-permute-start.12 = (bf16[192,896]{1,0:T(8,128)(2,1)S(1)}, bf16[192,896]{1,0:T(8,128)(2,1)S(1)}, u32[]{:S(2)}, u32[]{:S(2)}) collective-permute-start(bf16[192,896]{1,0:T(8,128)(2,1)S(1)} %grad_rows_1.1.refs_2_.refs_0_), channel_id=1, source_target_pairs={{0,1},{1,0},{2,3},{3,2},{4,5},{5,4},{6,7},{7,6},{8,9},{9,8},{10,11... | collective-permute-start | bytes 1032200 | tf_op jit(solution)/shard_map/ppermute | solution.py:290
  41.2 16.2 %collective-permute-start.13 = (bf16[1,192,512]{2,1,0:T(8,128)(2,1)S(1)}, bf16[1,192,512]{2,1,0:T(8,128)(2,1)S(1)}, u32[]{:S(2)}, u32[]{:S(2)}) collective-permute-start(bf16[1,192,512]{2,1,0:T(8,128)(2,1)S(1)} %grad_middle_0.1.refs_3_), channel_id=1, source_target_pairs={{0,0},{1,1},{2,4},{3,5},{4,2},{5,3},{6,6},{7,7},{8,8},{9,9},{10,12... | collective-permute-start | bytes 589832 | tf_op jit(solution)/shard_map/ppermute | solution.py:275
  44.9 19.9 %collective-permute-start.15 = (bf16[2,192,512]{2,1,0:T(8,128)(2,1)S(1)}, bf16[2,192,512]{2,1,0:T(8,128)(2,1)S(1)}, u32[]{:S(2)}, u32[]{:S(2)}) collective-permute-start(bf16[2,192,512]{2,1,0:T(8,128)(2,1)S(1)} %behind_middle_1.1.refs_5_), channel_id=1, source_target_pairs={{0,0},{1,1},{2,4},{3,5},{4,2},{5,3},{6,6},{7,7},{8,8},{9,9},{10,12... | collective-permute-start | bytes 1179656 | tf_op jit(solution)/shard_map/ppermute | solution.py:275
  48.4 11.5 %collective-permute-start.11 = (bf16[2,192,512]{2,1,0:T(8,128)(2,1)S(1)}, bf16[2,192,512]{2,1,0:T(8,128)(2,1)S(1)}, u32[]{:S(2)}, u32[]{:S(2)}) collective-permute-start(bf16[2,192,512]{2,1,0:T(8,128)(2,1)S(1)} %ahead_outer_1.1.refs_3_), channel_id=1, source_target_pairs={{0,2},{1,3},{2,0},{3,1},{4,6},{5,7},{6,4},{7,5},{8,10},{9,11},{10,... | collective-permute-start | bytes 1179656 | tf_op jit(solution)/shard_map/ppermute | solution.py:275
  66.8 13.5 %collective-permute-start.17 = (bf16[2,192,512]{2,1,0:T(8,128)(2,1)S(1)}, bf16[2,192,512]{2,1,0:T(8,128)(2,1)S(1)}, u32[]{:S(2)}, u32[]{:S(2)}) collective-permute-start(bf16[2,192,512]{2,1,0:T(8,128)(2,1)S(1)} %ahead_outer_2.1.refs_1_), channel_id=1, source_target_pairs={{0,2},{1,3},{2,0},{3,1},{4,6},{5,7},{6,4},{7,5},{8,10},{9,11},{10,... | collective-permute-start | bytes 1179656 | tf_op jit(solution)/shard_map/ppermute | solution.py:275
  72.6 12.3 %collective-permute-start.22 = (bf16[2,192,512]{2,1,0:T(8,128)(2,1)S(1)}, bf16[2,192,512]{2,1,0:T(8,128)(2,1)S(1)}, u32[]{:S(2)}, u32[]{:S(2)}) collective-permute-start(bf16[2,192,512]{2,1,0:T(8,128)(2,1)S(1)} %behind_first_0.1.refs_2_.refs_1_), channel_id=1, source_target_pairs={{0,0},{1,1},{2,4},{3,5},{4,2},{5,3},{6,6},{7,7},{8,8},{9,9},{10,12... | collective-permute-start | bytes 1179656 | tf_op jit(solution)/shard_map/ppermute | solution.py:275
  73.4 11.2 %collective-permute-start.21 = (bf16[1,192,512]{2,1,0:T(8,128)(2,1)S(1)}, bf16[1,192,512]{2,1,0:T(8,128)(2,1)S(1)}, u32[]{:S(2)}, u32[]{:S(2)}) collective-permute-start(bf16[1,192,512]{2,1,0:T(8,128)(2,1)S(1)} %grad_third_1.1.refs_1_), channel_id=1, source_target_pairs={{0,2},{1,3},{2,0},{3,1},{4,6},{5,7},{6,4},{7,5},{8,10},{9,11},{10,... | collective-permute-start | bytes 589832 | tf_op jit(solution)/shard_map/ppermute | solution.py:275
  86.0 9.8 %collective-permute-start.23 = (bf16[1,192,512]{2,1,0:T(8,128)(2,1)S(1)}, bf16[1,192,512]{2,1,0:T(8,128)(2,1)S(1)}, u32[]{:S(2)}, u32[]{:S(2)}) collective-permute-start(bf16[1,192,512]{2,1,0:T(8,128)(2,1)S(1)} %ahead_back_1.1.refs_1_), channel_id=1, source_target_pairs={{0,2},{1,3},{2,0},{3,1},{4,6},{5,7},{6,4},{7,5},{8,10},{9,11},{10,... | collective-permute-start | bytes 589832 | tf_op jit(solution)/shard_map/ppermute | solution.py:275
  95.9 10.1 %collective-permute-start.29 = (bf16[1,192,512]{2,1,0:T(8,128)(2,1)S(1)}, bf16[1,192,512]{2,1,0:T(8,128)(2,1)S(1)}, u32[]{:S(2)}, u32[]{:S(2)}) collective-permute-start(bf16[1,192,512]{2,1,0:T(8,128)(2,1)S(1)} %ahead_first_1.1.refs_5_.refs_1_), channel_id=1, source_target_pairs={{0,0},{1,1},{2,4},{3,5},{4,2},{5,3},{6,6},{7,7},{8,8},{9,9},{10,12... | collective-permute-start | bytes 589832 | tf_op jit(solution)/shard_map/ppermute | solution.py:275
  100.4 26.1 %collective-permute-start.25 = (bf16[192,896]{1,0:T(8,128)(2,1)S(1)}, bf16[192,896]{1,0:T(8,128)(2,1)S(1)}, u32[]{:S(2)}, u32[]{:S(2)}) collective-permute-start(bf16[192,896]{1,0:T(8,128)(2,1)S(1)} %get-tuple-element.12.refs_1_), channel_id=1, source_target_pairs={{0,1},{1,0},{2,3},{3,2},{4,5},{5,4},{6,7},{7,6},{8,9},{9,8},{10,11... | collective-permute-start | bytes 1032200 | tf_op jit(solution)/shard_map/ppermute | solution.py:290
  101.8 15.4 %collective-permute-start.27 = (bf16[2,192,512]{2,1,0:T(8,128)(2,1)S(1)}, bf16[2,192,512]{2,1,0:T(8,128)(2,1)S(1)}, u32[]{:S(2)}, u32[]{:S(2)}) collective-permute-start(bf16[2,192,512]{2,1,0:T(8,128)(2,1)S(1)} %behind_back_2.1.refs_1_), channel_id=1, source_target_pairs={{0,2},{1,3},{2,0},{3,1},{4,6},{5,7},{6,4},{7,5},{8,10},{9,11},{10,... | collective-permute-start | bytes 1179656 | tf_op jit(solution)/shard_map/ppermute | solution.py:275
  106.0 24.3 %collective-permute-start.31 = (bf16[1,192,512]{2,1,0:T(8,128)(2,1)S(1)}, bf16[1,192,512]{2,1,0:T(8,128)(2,1)S(1)}, u32[]{:S(2)}, u32[]{:S(2)}) collective-permute-start(bf16[1,192,512]{2,1,0:T(8,128)(2,1)S(1)} %ahead_back_2.1.refs_2_), channel_id=1, source_target_pairs={{0,2},{1,3},{2,0},{3,1},{4,6},{5,7},{6,4},{7,5},{8,10},{9,11},{10,... | collective-permute-start | bytes 589832 | tf_op jit(solution)/shard_map/ppermute | solution.py:275
  106.2 28.7 %collective-permute-start.34 = (bf16[192,896]{1,0:T(8,128)(2,1)S(1)}, bf16[192,896]{1,0:T(8,128)(2,1)S(1)}, u32[]{:S(2)}, u32[]{:S(2)}) collective-permute-start(bf16[192,896]{1,0:T(8,128)(2,1)S(1)} %behind_shares.1.refs_5_), channel_id=1, source_target_pairs={{8,0},{9,1},{10,2},{11,3},{12,4},{13,5},{14,6},{15,7},{16,8},{17,9... | collective-permute-start | bytes 1032200 | tf_op jit(solution)/shard_map/ppermute | solution.py:299
  119.1 17.7 %collective-permute-start.35 = (bf16[192,896]{1,0:T(8,128)(2,1)S(1)}, bf16[192,896]{1,0:T(8,128)(2,1)S(1)}, u32[]{:S(2)}, u32[]{:S(2)}) collective-permute-start(bf16[192,896]{1,0:T(8,128)(2,1)S(1)} %get-tuple-element.14.refs_2_), channel_id=1, source_target_pairs={{8,1},{9,0},{10,3},{11,2},{12,5},{13,4},{14,7},{15,6},{16,9},{17,8... | collective-permute-start | bytes 1032200 | tf_op jit(solution)/shard_map/ppermute | solution.py:299
  124.6 12.2 %collective-permute-start.36 = (bf16[192,896]{1,0:T(8,128)(2,1)S(1)}, bf16[192,896]{1,0:T(8,128)(2,1)S(1)}, u32[]{:S(2)}, u32[]{:S(2)}) collective-permute-start(bf16[192,896]{1,0:T(8,128)(2,1)S(1)} %get-tuple-element.17), channel_id=1, source_target_pairs={{8,0},{9,1},{10,2},{11,3},{12,4},{13,5},{14,6},{15,7},{16,8},{17,9... | collective-permute-start | bytes 1032200 | tf_op jit(solution)/shard_map/ppermute | solution.py:299
  126.7 16.1 %collective-permute-start.30 = (bf16[192,896]{1,0:T(8,128)(2,1)S(1)}, bf16[192,896]{1,0:T(8,128)(2,1)S(1)}, u32[]{:S(2)}, u32[]{:S(2)}) collective-permute-start(bf16[192,896]{1,0:T(8,128)(2,1)S(1)} %ahead_shares.1.refs_6_), channel_id=1, source_target_pairs={{0,8},{1,9},{2,10},{3,11},{4,12},{5,13},{6,14},{7,15},{8,16},{9,17... | collective-permute-start | bytes 1032200 | tf_op jit(solution)/shard_map/ppermute | solution.py:299
  (23 other events, 135.4 us)

commit v19 on v18

--- a/solution.py
+++ b/solution.py
@@ -72,7 +72,7 @@
 def first_kernel(far, *refs):
     rows, (weights, out, joined) = refs[:-3], refs[-3:]
     near, group, _ = position()
-    side = 0 if far else near
+    side = 1 - near if far else near
     parts, _, half = out.shape
     slots, width = rows[0].shape
     at = pl.multiple_of(group * width, 128)
@@ -96,7 +96,7 @@
 def first_product(name, far, rows, weights, after):
     slots = rows[0].shape[0] * len(rows) // 2
     parts, units, features = weights.shape
-    half = units if far else units // 2
+    half = units // 2
     return call(
         functools.partial(first_kernel, far),
         FIRST * parts,
@@ -318,17 +318,10 @@
         recent[:] = [made]
         return made
 
-    def far_half(weights):
-        parts, units, features = weights.shape
-        start = jnp.where(lax.axis_index("expert") // 2 >= DBLOCKS // 2, 0, units // 2)
-        return lax.dynamic_slice(weights, (0, start, 0), (parts, units // 2, features))
-
-    gates_far, downs_far = far_half(gates), far_half(downs)
-
     class Chain:
-        def __init__(self, name, rows, weights, far_weights, spreads):
+        def __init__(self, name, rows, weights, spreads):
             self.name = name
-            self.rows, self.weights, self.far_weights = rows, weights, far_weights
+            self.rows, self.weights = rows, weights
             self.spreads = spreads
             self.pairs, self.far, self.near, self.act = {}, {}, {}, {}
             self.out, self.mid, self.one, self.back, self.third = {}, {}, {}, {}, {}
@@ -353,7 +346,7 @@
 
         def far_product(self, c):
             name = f"{self.name}_far_{c}"
-            made = first_product(name, True, self.pairs[c], self.far_weights, list(recent))
+            made = first_product(name, True, self.pairs[c], self.weights, list(recent))
             recent[:] = [made]
             self.far[c] = made
 
@@ -418,9 +411,9 @@
         def activated(self, c):
             return self.act[c], self.one[c], self.mid[PIECES + c], self.back[c + 1]
 
-    ahead = Chain("ahead", ahead_rows[0], gates, gates_far, 1)
-    behind = Chain("behind", behind_rows[0], gates, gates_far, 2)
-    grad = Chain("grad", behind_grad[0], downs, downs_far, 0)
+    ahead = Chain("ahead", ahead_rows[0], gates, 1)
+    behind = Chain("behind", behind_rows[0], gates, 2)
+    grad = Chain("grad", behind_grad[0], downs, 0)
     sent = {}
 
     def cut(array, c):
@@ -478,26 +471,26 @@
     behind.fetch(1)
     ahead.far_product(0)
     ahead.first_hop(0)
+    grad.fetch(1)
     behind.middle_sum(0)
     grad.far_product(0)
     grad.first_hop(0)
+    behind.far_product(1)
     ahead.fetch(1)
-    behind.far_product(1)
     behind.near_products()
     behind.merged_hop(1, behind.far[1])
     ahead.middle_sum(0)
-    grad.fetch(1)
     grad.middle_sum(0)
+    grad.far_product(1)
+    grad.near_products()
+    behind.middle_sum(1)
     ahead.far_product(1)
-    behind.middle_sum(1)
+    grad.merged_hop(1, grad.far[1])
     ahead.near_products()
     ahead.merged_hop(1, ahead.far[1])
-    grad.far_product(1)
-    grad.near_products()
-    grad.merged_hop(1, grad.far[1])
-    ahead.middle_sum(1)
     activate_behind(0)
     behind.merged_hop(2, behind.act[0])
+    ahead.middle_sum(1)
     grad.middle_sum(1)
     activate_ahead(0)
     ahead.merged_hop(2, ahead.act[0])

time: 146 us -> 158 us (1.082)
  starting transfers between devices: 70.1 us -> 86.7 us
  Pallas kernels: 29.8 us -> 22 us
  waiting for transfers between devices: 35.4 us -> 37.3 us
    ppermute x23, starting transfers between devices: 36.2 us -> 44.9 us  [between(): return lax.ppermute(value, 'expert', pairs)]
    pallas_call x46, Pallas kernels: 29.8 us -> 22 us  [call(): pl.pallas_call(run, compiler_params=pltpu.CompilerParams(vmem_limit_bytes...]
    ppermute x6, starting transfers between devices: 27 us -> 33.8 us  [to_section(): return lax.ppermute(value, ('section', 'expert'), pairs)]
    ppermute x8, waiting for transfers between devices: 6.48 us -> 12.1 us  [swapped(): return lax.ppermute(value, 'expert', [(i, i ^ 1) for i in range(devices)])]
    unnamed x20, local copies, waits for them, and re-layouts: 2.69 us -> 7.8 us
    dynamic_slice x2 -> x0, local copies, waits for them, and re-layouts: 3.9 us -> none  [far_half(): lax.dynamic_slice(weights, (0, start, 0), (parts, units // 2, features))]
    ppermute x23, waiting for transfers between devices: 24 us -> 20.2 us  [between(): return lax.ppermute(value, 'expert', pairs)]
  transfers between devices with their start and end apart: 37 -> 37, of which waited for: 14 -> 15; matrix products, arithmetic and copies ran while one was open for 3% -> 0% of each run, Pallas kernels for 20% -> 13%
where the time goes in v19:
time: 158 us; the launch traced here: 157 us
  starting transfers between devices  86.7 us (55%)
  waiting for transfers between devices  37.3 us (24%)
  Pallas kernels  22 us (14%)
  local copies, waits for them, and re-layouts  9.37 us (6%)
    ppermute x23, starting transfers between devices, between(): return lax.ppermute(value, 'expert', pairs)  44.9 us
    ppermute x6, starting transfers between devices, to_section(): return lax.ppermute(value, ('section', 'expert'), pairs)  33.8 us
    pallas_call x46, Pallas kernels, call(): pl.pallas_call(run, compiler_params=pltpu.CompilerParams(vmem_limit_bytes...  22 us
    ppermute x23, waiting for transfers between devices, between(): return lax.ppermute(value, 'expert', pairs)  20.2 us
    ppermute x8, waiting for transfers between devices, swapped(): return lax.ppermute(value, 'expert', [(i, i ^ 1) for i in range(devices)])  12.1 us
    ppermute x8, starting transfers between devices, swapped(): return lax.ppermute(value, 'expert', [(i, i ^ 1) for i in range(devices)])  8.09 us
    unnamed x20, local copies, waits for them, and re-layouts  7.8 us
    ppermute x6, waiting for transfers between devices, to_section(): return lax.ppermute(value, ('section', 'expert'), pairs)  5 us
  transfers between devices with their start and end apart: 37, of which 15 were waited for; matrix products, arithmetic and copies ran while one was open for 0% of the time, Pallas kernels for 13%

profile of v19, /device:TPU:1, one launch (start us, length us, event | category | flops | bytes accessed | tf_op | source)
XLA Modules:
  0.0 156.6 jit_solution(16860565594827141565)
XLA Ops:
  1.6 2.1 %collective-permute-start.1 = (bf16[192,896]{1,0:T(8,128)(2,1)S(1)}, bf16[192,896]{1,0:T(8,128)(2,1)S(1)}, u32[]{:S(2)}, u32[]{:S(2)}) collective-permute-start(bf16[192,896]{1,0:T(8,128)(2,1)S(1)} %slice_bitcast_fusion.refs_0_), channel_id=1, source_target_pairs={{0,1},{1,0},{2,3},{3,2},{4,5},{5,4},{6,7},{7,6},{8,9},{9,8},{10,11... | collective-permute-start | bytes 1032200 | tf_op jit(solution)/shard_map/ppermute | solution.py:290
  7.3 4.2 %collective-permute-done.1.refs_1_ = bf16[192,896]{1,0:T(8,128)(2,1)S(1)} collective-permute-done((bf16[192,896]{1,0:T(8,128)(2,1)S(1)}, bf16[192,896]{1,0:T(8,128)(2,1)S(1)}, u32[]{:S(2)}, u32[]{:S(2)}) %collective-permute-start.1) | collective-permute-done | bytes 344096 | tf_op jit(solution)/shard_map/ppermute | solution.py:290
  11.6 3.1 %copy-done.1 = bf16[1,1,2,1024,1792]{4,3,2,1,0:T(8,128)(2,1)S(1)} copy-done((bf16[1,1,2,1024,1792]{4,3,2,1,0:T(8,128)(2,1)S(1)}, bf16[1,1,2,1024,1792]{4,3,2,1,0:T(8,128)(2,1)}, u32[]{:S(2)}) %copy-start.1) | copy-done | bytes 7340056
  27.1 2.3 %collective-permute-start.7 = (bf16[1,192,512]{2,1,0:T(8,128)(2,1)S(1)}, bf16[1,192,512]{2,1,0:T(8,128)(2,1)S(1)}, u32[]{:S(2)}, u32[]{:S(2)}) collective-permute-start(bf16[1,192,512]{2,1,0:T(8,128)(2,1)S(1)} %grad_far_0.1.refs_3_.refs_0_), channel_id=1, source_target_pairs={{0,2},{1,3},{2,0},{3,1},{4,6},{5,7},{6,4},{7,5},{8,10},{9,11},{10,... | collective-permute-start | bytes 589832 | tf_op jit(solution)/shard_map/ppermute | solution.py:275
  29.3 4.3 %collective-permute-done.2.refs_1_.refs_3_ = bf16[192,896]{1,0:T(8,128)(2,1)S(1)} collective-permute-done((bf16[192,896]{1,0:T(8,128)(2,1)S(1)}, bf16[192,896]{1,0:T(8,128)(2,1)S(1)}, u32[]{:S(2)}, u32[]{:S(2)}) %collective-permute-start.2) | collective-permute-done | bytes 344096 | tf_op jit(solution)/shard_map/ppermute | solution.py:290
  42.8 2.9 %collective-permute-done.11.refs_1_ = bf16[2,192,512]{2,1,0:T(8,128)(2,1)S(1)} collective-permute-done((bf16[2,192,512]{2,1,0:T(8,128)(2,1)S(1)}, bf16[2,192,512]{2,1,0:T(8,128)(2,1)S(1)}, u32[]{:S(2)}, u32[]{:S(2)}) %collective-permute-start.11) | collective-permute-done | bytes 393248 | tf_op jit(solution)/shard_map/ppermute | solution.py:275
  46.5 2.0 %collective-permute-done.5.refs_1_.refs_3_ = bf16[192,896]{1,0:T(8,128)(2,1)S(1)} collective-permute-done((bf16[192,896]{1,0:T(8,128)(2,1)S(1)}, bf16[192,896]{1,0:T(8,128)(2,1)S(1)}, u32[]{:S(2)}, u32[]{:S(2)}) %collective-permute-start.5) | collective-permute-done | bytes 344096 | tf_op jit(solution)/shard_map/ppermute | solution.py:290
  49.8 4.6 %collective-permute-start.14 = (bf16[1,192,512]{2,1,0:T(8,128)(2,1)S(1)}, bf16[1,192,512]{2,1,0:T(8,128)(2,1)S(1)}, u32[]{:S(2)}, u32[]{:S(2)}) collective-permute-start(bf16[1,192,512]{2,1,0:T(8,128)(2,1)S(1)} %grad_outer_1.1.refs_5_), channel_id=1, source_target_pairs={{0,2},{1,3},{2,0},{3,1},{4,6},{5,7},{6,4},{7,5},{8,10},{9,11},{10,... | collective-permute-start | bytes 589832 | tf_op jit(solution)/shard_map/ppermute | solution.py:275
  57.9 5.1 %collective-permute-start.19 = (bf16[2,192,512]{2,1,0:T(8,128)(2,1)S(1)}, bf16[2,192,512]{2,1,0:T(8,128)(2,1)S(1)}, u32[]{:S(2)}, u32[]{:S(2)}) collective-permute-start(bf16[2,192,512]{2,1,0:T(8,128)(2,1)S(1)} %behind_outer_2.1.refs_2_), channel_id=1, source_target_pairs={{0,2},{1,3},{2,0},{3,1},{4,6},{5,7},{6,4},{7,5},{8,10},{9,11},{10,... | collective-permute-start | bytes 1179656 | tf_op jit(solution)/shard_map/ppermute | solution.py:275
  64.7 7.9 %collective-permute-start.17 = (bf16[2,192,512]{2,1,0:T(8,128)(2,1)S(1)}, bf16[2,192,512]{2,1,0:T(8,128)(2,1)S(1)}, u32[]{:S(2)}, u32[]{:S(2)}) collective-permute-start(bf16[2,192,512]{2,1,0:T(8,128)(2,1)S(1)} %ahead_outer_2.1.refs_1_), channel_id=1, source_target_pairs={{0,2},{1,3},{2,0},{3,1},{4,6},{5,7},{6,4},{7,5},{8,10},{9,11},{10,... | collective-permute-start | bytes 1179656 | tf_op jit(solution)/shard_map/ppermute | solution.py:275
  73.4 4.0 %collective-permute-start.21 = (bf16[1,192,512]{2,1,0:T(8,128)(2,1)S(1)}, bf16[1,192,512]{2,1,0:T(8,128)(2,1)S(1)}, u32[]{:S(2)}, u32[]{:S(2)}) collective-permute-start(bf16[1,192,512]{2,1,0:T(8,128)(2,1)S(1)} %grad_third_1.1.refs_1_), channel_id=1, source_target_pairs={{0,2},{1,3},{2,0},{3,1},{4,6},{5,7},{6,4},{7,5},{8,10},{9,11},{10,... | collective-permute-start | bytes 589832 | tf_op jit(solution)/shard_map/ppermute | solution.py:275
  77.3 4.7 %collective-permute-done.17.refs_0_.refs_1_ = bf16[2,192,512]{2,1,0:T(8,128)(2,1)S(1)} collective-permute-done((bf16[2,192,512]{2,1,0:T(8,128)(2,1)S(1)}, bf16[2,192,512]{2,1,0:T(8,128)(2,1)S(1)}, u32[]{:S(2)}, u32[]{:S(2)}) %collective-permute-start.17) | collective-permute-done | bytes 393248 | tf_op jit(solution)/shard_map/ppermute | solution.py:275
  84.3 3.1 %collective-permute-start.24 = (bf16[2,192,512]{2,1,0:T(8,128)(2,1)S(1)}, bf16[2,192,512]{2,1,0:T(8,128)(2,1)S(1)}, u32[]{:S(2)}, u32[]{:S(2)}) collective-permute-start(bf16[2,192,512]{2,1,0:T(8,128)(2,1)S(1)} %behind_back_1.1.refs_2_), channel_id=1, source_target_pairs={{0,2},{1,3},{2,0},{3,1},{4,6},{5,7},{6,4},{7,5},{8,10},{9,11},{10,... | collective-permute-start | bytes 1179656 | tf_op jit(solution)/shard_map/ppermute | solution.py:275
  87.5 3.9 %collective-permute-start.23 = (bf16[1,192,512]{2,1,0:T(8,128)(2,1)S(1)}, bf16[1,192,512]{2,1,0:T(8,128)(2,1)S(1)}, u32[]{:S(2)}, u32[]{:S(2)}) collective-permute-start(bf16[1,192,512]{2,1,0:T(8,128)(2,1)S(1)} %ahead_back_1.1.refs_1_), channel_id=1, source_target_pairs={{0,2},{1,3},{2,0},{3,1},{4,6},{5,7},{6,4},{7,5},{8,10},{9,11},{10,... | collective-permute-start | bytes 589832 | tf_op jit(solution)/shard_map/ppermute | solution.py:275
  91.4 5.5 %collective-permute-done.24.refs_0_.refs_3_ = bf16[2,192,512]{2,1,0:T(8,128)(2,1)S(1)} collective-permute-done((bf16[2,192,512]{2,1,0:T(8,128)(2,1)S(1)}, bf16[2,192,512]{2,1,0:T(8,128)(2,1)S(1)}, u32[]{:S(2)}, u32[]{:S(2)}) %collective-permute-start.24) | collective-permute-done | bytes 393248 | tf_op jit(solution)/shard_map/ppermute | solution.py:275
  97.6 3.5 %collective-permute-done.23.refs_0_.refs_3_ = bf16[1,192,512]{2,1,0:T(8,128)(2,1)S(1)} collective-permute-done((bf16[1,192,512]{2,1,0:T(8,128)(2,1)S(1)}, bf16[1,192,512]{2,1,0:T(8,128)(2,1)S(1)}, u32[]{:S(2)}, u32[]{:S(2)}) %collective-permute-start.23) | collective-permute-done | bytes 196640 | tf_op jit(solution)/shard_map/ppermute | solution.py:275
  101.8 2.1 %behind_out_0.1 = (bf16[192,896]{1,0:T(8,128)(2,1)S(1)}, bf16[192,896]{1,0:T(8,128)(2,1)S(1)}) custom-call(bf16[2,192,512]{2,1,0:T(8,128)(2,1)S(1)} %behind_act_0.1.refs_0_.refs_3_, bf16[2,192,512]{2,1,0:T(8,128)(2,1)S(1)} %behind_first_0.1.refs_2_.refs_1_, bf16[2,192,512]{2,1,0:T(8,128)(2,1)S(1)} %collective-permute-done.22.refs_1_.refs_2_, ...), custom_call_target="tpu_custom_call" | custom-call | flops 20000000000 | bytes 1024 | tf_op jit(solution)/shard_map/behind_out_0/pallas_call | solution.py:44
  107.0 2.6 %collective-permute-start.27 = (bf16[2,192,512]{2,1,0:T(8,128)(2,1)S(1)}, bf16[2,192,512]{2,1,0:T(8,128)(2,1)S(1)}, u32[]{:S(2)}, u32[]{:S(2)}) collective-permute-start(bf16[2,192,512]{2,1,0:T(8,128)(2,1)S(1)} %behind_back_2.1.refs_1_), channel_id=1, source_target_pairs={{0,2},{1,3},{2,0},{3,1},{4,6},{5,7},{6,4},{7,5},{8,10},{9,11},{10,... | collective-permute-start | bytes 1179656 | tf_op jit(solution)/shard_map/ppermute | solution.py:275
  111.2 17.8 %collective-permute-start.34 = (bf16[192,896]{1,0:T(8,128)(2,1)S(1)}, bf16[192,896]{1,0:T(8,128)(2,1)S(1)}, u32[]{:S(2)}, u32[]{:S(2)}) collective-permute-start(bf16[192,896]{1,0:T(8,128)(2,1)S(1)} %behind_shares.1.refs_5_), channel_id=1, source_target_pairs={{8,0},{9,1},{10,2},{11,3},{12,4},{13,5},{14,6},{15,7},{16,8},{17,9... | collective-permute-start | bytes 1032200 | tf_op jit(solution)/shard_map/ppermute | solution.py:299
  130.9 5.6 %collective-permute-start.35 = (bf16[192,896]{1,0:T(8,128)(2,1)S(1)}, bf16[192,896]{1,0:T(8,128)(2,1)S(1)}, u32[]{:S(2)}, u32[]{:S(2)}) collective-permute-start(bf16[192,896]{1,0:T(8,128)(2,1)S(1)} %get-tuple-element.14.refs_2_), channel_id=1, source_target_pairs={{8,1},{9,0},{10,3},{11,2},{12,5},{13,4},{14,7},{15,6},{16,9},{17,8... | collective-permute-start | bytes 1032200 | tf_op jit(solution)/shard_map/ppermute | solution.py:299
  138.6 3.6 %collective-permute-start.30 = (bf16[192,896]{1,0:T(8,128)(2,1)S(1)}, bf16[192,896]{1,0:T(8,128)(2,1)S(1)}, u32[]{:S(2)}, u32[]{:S(2)}) collective-permute-start(bf16[192,896]{1,0:T(8,128)(2,1)S(1)} %ahead_shares.1.refs_6_), channel_id=1, source_target_pairs={{0,8},{1,9},{2,10},{3,11},{4,12},{5,13},{6,14},{7,15},{8,16},{9,17... | collective-permute-start | bytes 1032200 | tf_op jit(solution)/shard_map/ppermute | solution.py:299
  143.8 2.9 %collective-permute-start.32 = (bf16[192,896]{1,0:T(8,128)(2,1)S(1)}, bf16[192,896]{1,0:T(8,128)(2,1)S(1)}, u32[]{:S(2)}, u32[]{:S(2)}) collective-permute-start(bf16[192,896]{1,0:T(8,128)(2,1)S(1)} %get-tuple-element.15.refs_3_), channel_id=1, source_target_pairs={{0,9},{1,8},{2,11},{3,10},{4,13},{5,12},{6,15},{7,14},{8,17},{9,16... | collective-permute-start | bytes 1032200 | tf_op jit(solution)/shard_map/ppermute | solution.py:299
  149.6 2.8 %collective-permute-done.32.refs_1_ = bf16[192,896]{1,0:T(8,128)(2,1)S(1)} collective-permute-done((bf16[192,896]{1,0:T(8,128)(2,1)S(1)}, bf16[192,896]{1,0:T(8,128)(2,1)S(1)}, u32[]{:S(2)}, u32[]{:S(2)}) %collective-permute-start.32) | collective-permute-done | bytes 344096 | tf_op jit(solution)/shard_map/ppermute | solution.py:299
  152.4 2.2 %collective-permute-done.33.refs_2_ = bf16[192,896]{1,0:T(8,128)(2,1)S(1)} collective-permute-done((bf16[192,896]{1,0:T(8,128)(2,1)S(1)}, bf16[192,896]{1,0:T(8,128)(2,1)S(1)}, u32[]{:S(2)}, u32[]{:S(2)}) %collective-permute-start.33) | collective-permute-done | bytes 344096 | tf_op jit(solution)/shard_map/ppermute | solution.py:299
  (123 shorter events, 52.7 us)
Async XLA Ops:
  4.9 14.0 %collective-permute-start = (bf16[192,896]{1,0:T(8,128)(2,1)S(1)}, bf16[192,896]{1,0:T(8,128)(2,1)S(1)}, u32[]{:S(2)}, u32[]{:S(2)}) collective-permute-start(bf16[192,896]{1,0:T(8,128)(2,1)S(1)} %ahead_rows_0.1.refs_1_.refs_0_), channel_id=1, source_target_pairs={{0,1},{1,0},{2,3},{3,2},{4,5},{5,4},{6,7},{7,6},{8,9},{9,8},{10,11... | collective-permute-start | bytes 1032200 | tf_op jit(solution)/shard_map/ppermute | solution.py:290
  6.0 20.3 %collective-permute-start.3 = (bf16[192,896]{1,0:T(8,128)(2,1)S(1)}, bf16[192,896]{1,0:T(8,128)(2,1)S(1)}, u32[]{:S(2)}, u32[]{:S(2)}) collective-permute-start(bf16[192,896]{1,0:T(8,128)(2,1)S(1)} %grad_rows_0.1.refs_3_.refs_0_), channel_id=1, source_target_pairs={{0,1},{1,0},{2,3},{3,2},{4,5},{5,4},{6,7},{7,6},{8,9},{9,8},{10,11... | collective-permute-start | bytes 1032200 | tf_op jit(solution)/shard_map/ppermute | solution.py:290
  17.3 16.4 %collective-permute-start.2 = (bf16[192,896]{1,0:T(8,128)(2,1)S(1)}, bf16[192,896]{1,0:T(8,128)(2,1)S(1)}, u32[]{:S(2)}, u32[]{:S(2)}) collective-permute-start(bf16[192,896]{1,0:T(8,128)(2,1)S(1)} %behind_rows_1.1.refs_3_.refs_0_.refs_2_), channel_id=1, source_target_pairs={{0,1},{1,0},{2,3},{3,2},{4,5},{5,4},{6,7},{7,6},{8,9},{9,8},{10,11... | collective-permute-start | bytes 1032200 | tf_op jit(solution)/shard_map/ppermute | solution.py:290
  21.7 17.7 %collective-permute-start.8 = (bf16[2,192,512]{2,1,0:T(8,128)(2,1)S(1)}, bf16[2,192,512]{2,1,0:T(8,128)(2,1)S(1)}, u32[]{:S(2)}, u32[]{:S(2)}) collective-permute-start(bf16[2,192,512]{2,1,0:T(8,128)(2,1)S(1)} %ahead_far_0.1.refs_1_.refs_0_), channel_id=1, source_target_pairs={{0,2},{1,3},{2,0},{3,1},{4,6},{5,7},{6,4},{7,5},{8,10},{9,11},{10,... | collective-permute-start | bytes 1179656 | tf_op jit(solution)/shard_map/ppermute | solution.py:275
  22.0 19.1 %collective-permute-start.6 = (bf16[192,896]{1,0:T(8,128)(2,1)S(1)}, bf16[192,896]{1,0:T(8,128)(2,1)S(1)}, u32[]{:S(2)}, u32[]{:S(2)}) collective-permute-start(bf16[192,896]{1,0:T(8,128)(2,1)S(1)} %grad_rows_1.1.refs_2_.refs_0_), channel_id=1, source_target_pairs={{0,1},{1,0},{2,3},{3,2},{4,5},{5,4},{6,7},{7,6},{8,9},{9,8},{10,11... | collective-permute-start | bytes 1032200 | tf_op jit(solution)/shard_map/ppermute | solution.py:290
  24.6 13.3 %collective-permute-start.9 = (bf16[2,192,512]{2,1,0:T(8,128)(2,1)S(1)}, bf16[2,192,512]{2,1,0:T(8,128)(2,1)S(1)}, u32[]{:S(2)}, u32[]{:S(2)}) collective-permute-start(bf16[2,192,512]{2,1,0:T(8,128)(2,1)S(1)} %behind_middle_0.1.refs_3_), channel_id=1, source_target_pairs={{0,0},{1,1},{2,4},{3,5},{4,2},{5,3},{6,6},{7,7},{8,8},{9,9},{10,12... | collective-permute-start | bytes 1179656 | tf_op jit(solution)/shard_map/ppermute | solution.py:275
  27.1 13.1 %collective-permute-start.7 = (bf16[1,192,512]{2,1,0:T(8,128)(2,1)S(1)}, bf16[1,192,512]{2,1,0:T(8,128)(2,1)S(1)}, u32[]{:S(2)}, u32[]{:S(2)}) collective-permute-start(bf16[1,192,512]{2,1,0:T(8,128)(2,1)S(1)} %grad_far_0.1.refs_3_.refs_0_), channel_id=1, source_target_pairs={{0,2},{1,3},{2,0},{3,1},{4,6},{5,7},{6,4},{7,5},{8,10},{9,11},{10,... | collective-permute-start | bytes 589832 | tf_op jit(solution)/shard_map/ppermute | solution.py:275
  35.1 13.4 %collective-permute-start.5 = (bf16[192,896]{1,0:T(8,128)(2,1)S(1)}, bf16[192,896]{1,0:T(8,128)(2,1)S(1)}, u32[]{:S(2)}, u32[]{:S(2)}) collective-permute-start(bf16[192,896]{1,0:T(8,128)(2,1)S(1)} %ahead_rows_1.1.refs_5_.refs_0_.refs_2_), channel_id=1, source_target_pairs={{0,1},{1,0},{2,3},{3,2},{4,5},{5,4},{6,7},{7,6},{8,9},{9,8},{10,11... | collective-permute-start | bytes 1032200 | tf_op jit(solution)/shard_map/ppermute | solution.py:290
  39.5 16.6 %collective-permute-start.12 = (bf16[2,192,512]{2,1,0:T(8,128)(2,1)S(1)}, bf16[2,192,512]{2,1,0:T(8,128)(2,1)S(1)}, u32[]{:S(2)}, u32[]{:S(2)}) collective-permute-start(bf16[2,192,512]{2,1,0:T(8,128)(2,1)S(1)} %ahead_middle_0.1.refs_2_), channel_id=1, source_target_pairs={{0,0},{1,1},{2,4},{3,5},{4,2},{5,3},{6,6},{7,7},{8,8},{9,9},{10,12... | collective-permute-start | bytes 1179656 | tf_op jit(solution)/shard_map/ppermute | solution.py:275
  45.8 12.0 %collective-permute-start.15 = (bf16[2,192,512]{2,1,0:T(8,128)(2,1)S(1)}, bf16[2,192,512]{2,1,0:T(8,128)(2,1)S(1)}, u32[]{:S(2)}, u32[]{:S(2)}) collective-permute-start(bf16[2,192,512]{2,1,0:T(8,128)(2,1)S(1)} %behind_middle_1.1.refs_3_), channel_id=1, source_target_pairs={{0,0},{1,1},{2,4},{3,5},{4,2},{5,3},{6,6},{7,7},{8,8},{9,9},{10,12... | collective-permute-start | bytes 1179656 | tf_op jit(solution)/shard_map/ppermute | solution.py:275
  57.9 14.7 %collective-permute-start.19 = (bf16[2,192,512]{2,1,0:T(8,128)(2,1)S(1)}, bf16[2,192,512]{2,1,0:T(8,128)(2,1)S(1)}, u32[]{:S(2)}, u32[]{:S(2)}) collective-permute-start(bf16[2,192,512]{2,1,0:T(8,128)(2,1)S(1)} %behind_outer_2.1.refs_2_), channel_id=1, source_target_pairs={{0,2},{1,3},{2,0},{3,1},{4,6},{5,7},{6,4},{7,5},{8,10},{9,11},{10,... | collective-permute-start | bytes 1179656 | tf_op jit(solution)/shard_map/ppermute | solution.py:275
  64.7 17.3 %collective-permute-start.17 = (bf16[2,192,512]{2,1,0:T(8,128)(2,1)S(1)}, bf16[2,192,512]{2,1,0:T(8,128)(2,1)S(1)}, u32[]{:S(2)}, u32[]{:S(2)}) collective-permute-start(bf16[2,192,512]{2,1,0:T(8,128)(2,1)S(1)} %ahead_outer_2.1.refs_1_), channel_id=1, source_target_pairs={{0,2},{1,3},{2,0},{3,1},{4,6},{5,7},{6,4},{7,5},{8,10},{9,11},{10,... | collective-permute-start | bytes 1179656 | tf_op jit(solution)/shard_map/ppermute | solution.py:275
  72.6 11.7 %collective-permute-start.22 = (bf16[2,192,512]{2,1,0:T(8,128)(2,1)S(1)}, bf16[2,192,512]{2,1,0:T(8,128)(2,1)S(1)}, u32[]{:S(2)}, u32[]{:S(2)}) collective-permute-start(bf16[2,192,512]{2,1,0:T(8,128)(2,1)S(1)} %behind_first_0.1.refs_2_.refs_1_), channel_id=1, source_target_pairs={{0,0},{1,1},{2,4},{3,5},{4,2},{5,3},{6,6},{7,7},{8,8},{9,9},{10,12... | collective-permute-start | bytes 1179656 | tf_op jit(solution)/shard_map/ppermute | solution.py:275
  73.4 10.6 %collective-permute-start.21 = (bf16[1,192,512]{2,1,0:T(8,128)(2,1)S(1)}, bf16[1,192,512]{2,1,0:T(8,128)(2,1)S(1)}, u32[]{:S(2)}, u32[]{:S(2)}) collective-permute-start(bf16[1,192,512]{2,1,0:T(8,128)(2,1)S(1)} %grad_third_1.1.refs_1_), channel_id=1, source_target_pairs={{0,2},{1,3},{2,0},{3,1},{4,6},{5,7},{6,4},{7,5},{8,10},{9,11},{10,... | collective-permute-start | bytes 589832 | tf_op jit(solution)/shard_map/ppermute | solution.py:275
  84.3 12.5 %collective-permute-start.24 = (bf16[2,192,512]{2,1,0:T(8,128)(2,1)S(1)}, bf16[2,192,512]{2,1,0:T(8,128)(2,1)S(1)}, u32[]{:S(2)}, u32[]{:S(2)}) collective-permute-start(bf16[2,192,512]{2,1,0:T(8,128)(2,1)S(1)} %behind_back_1.1.refs_2_), channel_id=1, source_target_pairs={{0,2},{1,3},{2,0},{3,1},{4,6},{5,7},{6,4},{7,5},{8,10},{9,11},{10,... | collective-permute-start | bytes 1179656 | tf_op jit(solution)/shard_map/ppermute | solution.py:275
  87.5 13.6 %collective-permute-start.23 = (bf16[1,192,512]{2,1,0:T(8,128)(2,1)S(1)}, bf16[1,192,512]{2,1,0:T(8,128)(2,1)S(1)}, u32[]{:S(2)}, u32[]{:S(2)}) collective-permute-start(bf16[1,192,512]{2,1,0:T(8,128)(2,1)S(1)} %ahead_back_1.1.refs_1_), channel_id=1, source_target_pairs={{0,2},{1,3},{2,0},{3,1},{4,6},{5,7},{6,4},{7,5},{8,10},{9,11},{10,... | collective-permute-start | bytes 589832 | tf_op jit(solution)/shard_map/ppermute | solution.py:275
  96.9 10.1 %collective-permute-start.26 = (bf16[2,192,512]{2,1,0:T(8,128)(2,1)S(1)}, bf16[2,192,512]{2,1,0:T(8,128)(2,1)S(1)}, u32[]{:S(2)}, u32[]{:S(2)}) collective-permute-start(bf16[2,192,512]{2,1,0:T(8,128)(2,1)S(1)} %behind_first_1.1.refs_1_), channel_id=1, source_target_pairs={{0,0},{1,1},{2,4},{3,5},{4,2},{5,3},{6,6},{7,7},{8,8},{9,9},{10,12... | collective-permute-start | bytes 1179656 | tf_op jit(solution)/shard_map/ppermute | solution.py:275
  105.7 32.8 %collective-permute-start.25 = (bf16[192,896]{1,0:T(8,128)(2,1)S(1)}, bf16[192,896]{1,0:T(8,128)(2,1)S(1)}, u32[]{:S(2)}, u32[]{:S(2)}) collective-permute-start(bf16[192,896]{1,0:T(8,128)(2,1)S(1)} %get-tuple-element.12.refs_1_), channel_id=1, source_target_pairs={{0,1},{1,0},{2,3},{3,2},{4,5},{5,4},{6,7},{7,6},{8,9},{9,8},{10,11... | collective-permute-start | bytes 1032200 | tf_op jit(solution)/shard_map/ppermute | solution.py:290
  107.0 22.0 %collective-permute-start.27 = (bf16[2,192,512]{2,1,0:T(8,128)(2,1)S(1)}, bf16[2,192,512]{2,1,0:T(8,128)(2,1)S(1)}, u32[]{:S(2)}, u32[]{:S(2)}) collective-permute-start(bf16[2,192,512]{2,1,0:T(8,128)(2,1)S(1)} %behind_back_2.1.refs_1_), channel_id=1, source_target_pairs={{0,2},{1,3},{2,0},{3,1},{4,6},{5,7},{6,4},{7,5},{8,10},{9,11},{10,... | collective-permute-start | bytes 1179656 | tf_op jit(solution)/shard_map/ppermute | solution.py:275
  109.6 32.6 %collective-permute-start.31 = (bf16[1,192,512]{2,1,0:T(8,128)(2,1)S(1)}, bf16[1,192,512]{2,1,0:T(8,128)(2,1)S(1)}, u32[]{:S(2)}, u32[]{:S(2)}) collective-permute-start(bf16[1,192,512]{2,1,0:T(8,128)(2,1)S(1)} %ahead_back_2.1.refs_2_), channel_id=1, source_target_pairs={{0,2},{1,3},{2,0},{3,1},{4,6},{5,7},{6,4},{7,5},{8,10},{9,11},{10,... | collective-permute-start | bytes 589832 | tf_op jit(solution)/shard_map/ppermute | solution.py:275
  111.2 35.5 %collective-permute-start.34 = (bf16[192,896]{1,0:T(8,128)(2,1)S(1)}, bf16[192,896]{1,0:T(8,128)(2,1)S(1)}, u32[]{:S(2)}, u32[]{:S(2)}) collective-permute-start(bf16[192,896]{1,0:T(8,128)(2,1)S(1)} %behind_shares.1.refs_5_), channel_id=1, source_target_pairs={{8,0},{9,1},{10,2},{11,3},{12,4},{13,5},{14,6},{15,7},{16,8},{17,9... | collective-permute-start | bytes 1032200 | tf_op jit(solution)/shard_map/ppermute | solution.py:299
  130.9 17.7 %collective-permute-start.35 = (bf16[192,896]{1,0:T(8,128)(2,1)S(1)}, bf16[192,896]{1,0:T(8,128)(2,1)S(1)}, u32[]{:S(2)}, u32[]{:S(2)}) collective-permute-start(bf16[192,896]{1,0:T(8,128)(2,1)S(1)} %get-tuple-element.14.refs_2_), channel_id=1, source_target_pairs={{8,1},{9,0},{10,3},{11,2},{12,5},{13,4},{14,7},{15,6},{16,9},{17,8... | collective-permute-start | bytes 1032200 | tf_op jit(solution)/shard_map/ppermute | solution.py:299
  136.5 12.1 %collective-permute-start.36 = (bf16[192,896]{1,0:T(8,128)(2,1)S(1)}, bf16[192,896]{1,0:T(8,128)(2,1)S(1)}, u32[]{:S(2)}, u32[]{:S(2)}) collective-permute-start(bf16[192,896]{1,0:T(8,128)(2,1)S(1)} %get-tuple-element.17), channel_id=1, source_target_pairs={{8,0},{9,1},{10,2},{11,3},{12,4},{13,5},{14,6},{15,7},{16,8},{17,9... | collective-permute-start | bytes 1032200 | tf_op jit(solution)/shard_map/ppermute | solution.py:299
  138.6 16.0 %collective-permute-start.30 = (bf16[192,896]{1,0:T(8,128)(2,1)S(1)}, bf16[192,896]{1,0:T(8,128)(2,1)S(1)}, u32[]{:S(2)}, u32[]{:S(2)}) collective-permute-start(bf16[192,896]{1,0:T(8,128)(2,1)S(1)} %ahead_shares.1.refs_6_), channel_id=1, source_target_pairs={{0,8},{1,9},{2,10},{3,11},{4,12},{5,13},{6,14},{7,15},{8,16},{9,17... | collective-permute-start | bytes 1032200 | tf_op jit(solution)/shard_map/ppermute | solution.py:299
  (23 other events, 124.7 us)

commit v20 on v14

--- a/solution.py
+++ b/solution.py
@@ -55,10 +55,6 @@
 
 def cut_kernel(rows, out):
     out[...] = rows[...]
-
-
-def touch_kernel(gates, downs, out):
-    out[...] = gates[0, :16, :128] + downs[0, :16, :128]
 
 
 def cut_first_kernel(value, out):
@@ -195,19 +191,65 @@
         out[...] = share.astype(BF16)
 
 
+def copying_second_kernel(scaled, act, one, two, three, *refs):
+    scale, refs = (refs[0], refs[1:]) if scaled else (None, refs)
+    weights, give, keep, joined, tiles, sems = refs
+    near_half, group, end = position()
+    kinds, _, half = act.shape
+    _, _, units, width = tiles.shape
+    copies = []
+    for own in range(2):
+        at = pl.multiple_of((group if own else 1 - group) * width, 128)
+        copy = pltpu.make_async_copy(
+            weights.at[:, :, pl.ds(at, width)], tiles.at[own], sems.at[own]
+        )
+        copy.start()
+        copies.append(copy)
+
+    def place(near, far):
+        for kind in range(kinds):
+            at = pl.multiple_of((2 * kind + near_half) * half, 128)
+            other = pl.multiple_of((2 * kind + 1 - near_half) * half, 128)
+            joined[:, pl.ds(at, half)] = near[kind]
+            joined[:, pl.ds(other, half)] = far[kind]
+
+    @pl.when(end)
+    def _():
+        place(act, three)
+
+    @pl.when(jnp.logical_not(end))
+    def _():
+        place(one, two)
+
+    for own, out in enumerate((give, keep)):
+        copies[own].wait()
+        share = jnp.dot(
+            joined[...], tiles[own].reshape(kinds * units, width), preferred_element_type=F32
+        )
+        if scaled:
+            share = share * scale[...]
+        out[...] = share.astype(BF16)
+
+
 def second_product(name, values, scale, weights, after):
     kinds, units, features = weights.shape
     slots = values[0].shape[1]
     operands = [*values] + ([] if scale is None else [scale])
     share = jax.ShapeDtypeStruct((slots, features // 2), BF16)
+    kernel, space = second_kernel, pltpu.VMEM
+    scratch = [pltpu.VMEM((slots, kinds * units), BF16)]
+    if kinds == 1:
+        kernel, space = copying_second_kernel, pl.ANY
+        scratch.append(pltpu.VMEM((2, kinds, units, features // 2), BF16))
+        scratch.append(pltpu.SemaphoreType.DMA((2,)))
     return call(
-        functools.partial(second_kernel, scale is not None),
+        functools.partial(kernel, scale is not None),
         AHEAD_OUT if kinds == 1 else BEHIND_OUT,
         (*operands, weights),
         after,
         (share, share),
-        in_specs=[*[whole(v) for v in operands], pl.BlockSpec(memory_space=pltpu.VMEM)],
-        scratch=[pltpu.VMEM((slots, kinds * units), BF16)],
+        in_specs=[*[whole(v) for v in operands], pl.BlockSpec(memory_space=space)],
+        scratch=scratch,
         name=name,
     )
 
@@ -415,17 +457,6 @@
 
     for chain in (behind, ahead, grad):
         chain.fetch(0)
-    weights_spec = pl.BlockSpec(memory_space=pltpu.VMEM)
-    touched = call(
-        touch_kernel,
-        ROWS,
-        (gates, downs),
-        list(recent),
-        jax.ShapeDtypeStruct((16, 128), BF16),
-        in_specs=[weights_spec, weights_spec],
-        name="touch",
-    )
-    recent[:] = [touched]
     behind.far_product(0)
     behind.first_hop(0)
     behind.fetch(1)
@@ -468,8 +499,8 @@
     behind.outer_pass(2)
     ahead.outer_pass(2)
     send_first(behind)
+    finish_last(behind)
     send_first(ahead)
-    finish_last(behind)
     finish_last(ahead)
     behind_sent = result(behind)
     ahead_sent = result(ahead)

time: 144 us -> 142 us (0.986)
  waiting for transfers between devices: 26.4 us -> 35 us
  local copies, waits for them, and re-layouts: 17.2 us -> 9.37 us
  starting transfers between devices: 76.4 us -> 73.5 us
    unnamed x34 -> x20, local copies, waits for them, and re-layouts: 15.1 us -> 7.8 us
    ppermute x8, waiting for transfers between devices: 5.39 us -> 12.1 us  [swapped(): return lax.ppermute(value, 'expert', [(i, i ^ 1) for i in range(devices)])]
    ppermute x23, starting transfers between devices: 43 us -> 39.1 us  [between(): return lax.ppermute(value, 'expert', pairs)]
    ppermute x23, waiting for transfers between devices: 16 us -> 17.8 us  [between(): return lax.ppermute(value, 'expert', pairs)]
    pallas_call x47 -> x46, Pallas kernels: 21 us -> 22 us  [call(): pl.pallas_call(run, compiler_params=pltpu.CompilerParams(vmem_limit_bytes...]
  transfers between devices with their start and end apart: 37 -> 37, of which waited for: 12 -> 12; matrix products, arithmetic and copies ran while one was open for 1% -> 0% of each run, Pallas kernels for 14% -> 15%
where the time goes in v20:
time: 142 us; the launch traced here: 141 us
  starting transfers between devices  73.5 us (52%)
  waiting for transfers between devices  35 us (25%)
  Pallas kernels  22 us (15%)
  local copies, waits for them, and re-layouts  9.37 us (7%)
    ppermute x23, starting transfers between devices, between(): return lax.ppermute(value, 'expert', pairs)  39.1 us
    ppermute x6, starting transfers between devices, to_section(): return lax.ppermute(value, ('section', 'expert'), pairs)  26.2 us
    pallas_call x46, Pallas kernels, call(): pl.pallas_call(run, compiler_params=pltpu.CompilerParams(vmem_limit_bytes...  22 us
    ppermute x23, waiting for transfers between devices, between(): return lax.ppermute(value, 'expert', pairs)  17.8 us
    ppermute x8, waiting for transfers between devices, swapped(): return lax.ppermute(value, 'expert', [(i, i ^ 1) for i in range(devices)])  12.1 us
    ppermute x8, starting transfers between devices, swapped(): return lax.ppermute(value, 'expert', [(i, i ^ 1) for i in range(devices)])  8.2 us
    unnamed x20, local copies, waits for them, and re-layouts  7.8 us
    ppermute x6, waiting for transfers between devices, to_section(): return lax.ppermute(value, ('section', 'expert'), pairs)  5 us
  transfers between devices with their start and end apart: 37, of which 12 were waited for; matrix products, arithmetic and copies ran while one was open for 0% of the time, Pallas kernels for 15%

profile of v20, /device:TPU:1, one launch (start us, length us, event | category | flops | bytes accessed | tf_op | source)
XLA Modules:
  0.0 141.2 jit_solution(4639017763840862035)
XLA Ops:
  1.6 2.1 %collective-permute-start.1 = (bf16[192,896]{1,0:T(8,128)(2,1)S(1)}, bf16[192,896]{1,0:T(8,128)(2,1)S(1)}, u32[]{:S(2)}, u32[]{:S(2)}) collective-permute-start(bf16[192,896]{1,0:T(8,128)(2,1)S(1)} %slice_bitcast_fusion.refs_0_), channel_id=1, source_target_pairs={{0,1},{1,0},{2,3},{3,2},{4,5},{5,4},{6,7},{7,6},{8,9},{9,8},{10,11... | collective-permute-start | bytes 1032200 | tf_op jit(solution)/shard_map/ppermute | solution.py:284
  7.3 4.2 %collective-permute-done.1.refs_1_ = bf16[192,896]{1,0:T(8,128)(2,1)S(1)} collective-permute-done((bf16[192,896]{1,0:T(8,128)(2,1)S(1)}, bf16[192,896]{1,0:T(8,128)(2,1)S(1)}, u32[]{:S(2)}, u32[]{:S(2)}) %collective-permute-start.1) | collective-permute-done | bytes 344096 | tf_op jit(solution)/shard_map/ppermute | solution.py:284
  11.6 3.1 %copy-done.1 = bf16[1,1,2,1024,1792]{4,3,2,1,0:T(8,128)(2,1)S(1)} copy-done((bf16[1,1,2,1024,1792]{4,3,2,1,0:T(8,128)(2,1)S(1)}, bf16[1,1,2,1024,1792]{4,3,2,1,0:T(8,128)(2,1)}, u32[]{:S(2)}) %copy-start.1) | copy-done | bytes 7340056
  22.0 4.4 %collective-permute-done.3.refs_1_ = bf16[192,896]{1,0:T(8,128)(2,1)S(1)} collective-permute-done((bf16[192,896]{1,0:T(8,128)(2,1)S(1)}, bf16[192,896]{1,0:T(8,128)(2,1)S(1)}, u32[]{:S(2)}, u32[]{:S(2)}) %collective-permute-start.3) | collective-permute-done | bytes 344096 | tf_op jit(solution)/shard_map/ppermute | solution.py:284
  30.5 3.2 %collective-permute-done.6.refs_1_.refs_3_ = bf16[192,896]{1,0:T(8,128)(2,1)S(1)} collective-permute-done((bf16[192,896]{1,0:T(8,128)(2,1)S(1)}, bf16[192,896]{1,0:T(8,128)(2,1)S(1)}, u32[]{:S(2)}, u32[]{:S(2)}) %collective-permute-start.6) | collective-permute-done | bytes 344096 | tf_op jit(solution)/shard_map/ppermute | solution.py:284
  37.6 3.8 %collective-permute-start.11 = (bf16[2,192,512]{2,1,0:T(8,128)(2,1)S(1)}, bf16[2,192,512]{2,1,0:T(8,128)(2,1)S(1)}, u32[]{:S(2)}, u32[]{:S(2)}) collective-permute-start(bf16[2,192,512]{2,1,0:T(8,128)(2,1)S(1)} %behind_outer_1.1.refs_1_), channel_id=1, source_target_pairs={{0,2},{1,3},{2,0},{3,1},{4,6},{5,7},{6,4},{7,5},{8,10},{9,11},{10,... | collective-permute-start | bytes 1179656 | tf_op jit(solution)/shard_map/ppermute | solution.py:269
  50.6 3.0 %collective-permute-start.14 = (bf16[1,192,512]{2,1,0:T(8,128)(2,1)S(1)}, bf16[1,192,512]{2,1,0:T(8,128)(2,1)S(1)}, u32[]{:S(2)}, u32[]{:S(2)}) collective-permute-start(bf16[1,192,512]{2,1,0:T(8,128)(2,1)S(1)} %grad_outer_1.1.refs_2_), channel_id=1, source_target_pairs={{0,2},{1,3},{2,0},{3,1},{4,6},{5,7},{6,4},{7,5},{8,10},{9,11},{10,... | collective-permute-start | bytes 589832 | tf_op jit(solution)/shard_map/ppermute | solution.py:269
  56.2 3.4 %collective-permute-done.14.refs_1_.refs_3_ = bf16[1,192,512]{2,1,0:T(8,128)(2,1)S(1)} collective-permute-done((bf16[1,192,512]{2,1,0:T(8,128)(2,1)S(1)}, bf16[1,192,512]{2,1,0:T(8,128)(2,1)S(1)}, u32[]{:S(2)}, u32[]{:S(2)}) %collective-permute-start.14) | collective-permute-done | bytes 196640 | tf_op jit(solution)/shard_map/ppermute | solution.py:269
  60.7 2.5 %collective-permute-start.18 = (bf16[2,192,512]{2,1,0:T(8,128)(2,1)S(1)}, bf16[2,192,512]{2,1,0:T(8,128)(2,1)S(1)}, u32[]{:S(2)}, u32[]{:S(2)}) collective-permute-start(bf16[2,192,512]{2,1,0:T(8,128)(2,1)S(1)} %behind_outer_2.1.refs_2_), channel_id=1, source_target_pairs={{0,2},{1,3},{2,0},{3,1},{4,6},{5,7},{6,4},{7,5},{8,10},{9,11},{10,... | collective-permute-start | bytes 1179656 | tf_op jit(solution)/shard_map/ppermute | solution.py:269
  63.5 4.7 %collective-permute-start.17 = (bf16[2,192,512]{2,1,0:T(8,128)(2,1)S(1)}, bf16[2,192,512]{2,1,0:T(8,128)(2,1)S(1)}, u32[]{:S(2)}, u32[]{:S(2)}) collective-permute-start(bf16[2,192,512]{2,1,0:T(8,128)(2,1)S(1)} %ahead_outer_2.1.refs_2_), channel_id=1, source_target_pairs={{0,2},{1,3},{2,0},{3,1},{4,6},{5,7},{6,4},{7,5},{8,10},{9,11},{10,... | collective-permute-start | bytes 1179656 | tf_op jit(solution)/shard_map/ppermute | solution.py:269
  68.2 3.9 %collective-permute-start.21 = (bf16[1,192,512]{2,1,0:T(8,128)(2,1)S(1)}, bf16[1,192,512]{2,1,0:T(8,128)(2,1)S(1)}, u32[]{:S(2)}, u32[]{:S(2)}) collective-permute-start(bf16[1,192,512]{2,1,0:T(8,128)(2,1)S(1)} %grad_third_1.1.refs_1_), channel_id=1, source_target_pairs={{0,2},{1,3},{2,0},{3,1},{4,6},{5,7},{6,4},{7,5},{8,10},{9,11},{10,... | collective-permute-start | bytes 589832 | tf_op jit(solution)/shard_map/ppermute | solution.py:269
  72.9 2.9 %collective-permute-done.17.refs_0_.refs_1_ = bf16[2,192,512]{2,1,0:T(8,128)(2,1)S(1)} collective-permute-done((bf16[2,192,512]{2,1,0:T(8,128)(2,1)S(1)}, bf16[2,192,512]{2,1,0:T(8,128)(2,1)S(1)}, u32[]{:S(2)}, u32[]{:S(2)}) %collective-permute-start.17) | collective-permute-done | bytes 393248 | tf_op jit(solution)/shard_map/ppermute | solution.py:269
  76.6 3.4 %collective-permute-done.21.refs_3_ = bf16[1,192,512]{2,1,0:T(8,128)(2,1)S(1)} collective-permute-done((bf16[1,192,512]{2,1,0:T(8,128)(2,1)S(1)}, bf16[1,192,512]{2,1,0:T(8,128)(2,1)S(1)}, u32[]{:S(2)}, u32[]{:S(2)}) %collective-permute-start.21) | collective-permute-done | bytes 196640 | tf_op jit(solution)/shard_map/ppermute | solution.py:269
  80.3 2.1 %collective-permute-start.24 = (bf16[2,192,512]{2,1,0:T(8,128)(2,1)S(1)}, bf16[2,192,512]{2,1,0:T(8,128)(2,1)S(1)}, u32[]{:S(2)}, u32[]{:S(2)}) collective-permute-start(bf16[2,192,512]{2,1,0:T(8,128)(2,1)S(1)} %behind_back_1.1.refs_2_), channel_id=1, source_target_pairs={{0,2},{1,3},{2,0},{3,1},{4,6},{5,7},{6,4},{7,5},{8,10},{9,11},{10,... | collective-permute-start | bytes 1179656 | tf_op jit(solution)/shard_map/ppermute | solution.py:269
  82.4 2.8 %collective-permute-start.23 = (bf16[1,192,512]{2,1,0:T(8,128)(2,1)S(1)}, bf16[1,192,512]{2,1,0:T(8,128)(2,1)S(1)}, u32[]{:S(2)}, u32[]{:S(2)}) collective-permute-start(bf16[1,192,512]{2,1,0:T(8,128)(2,1)S(1)} %ahead_back_1.1.refs_1_), channel_id=1, source_target_pairs={{0,2},{1,3},{2,0},{3,1},{4,6},{5,7},{6,4},{7,5},{8,10},{9,11},{10,... | collective-permute-start | bytes 589832 | tf_op jit(solution)/shard_map/ppermute | solution.py:269
  85.2 4.9 %collective-permute-done.24.refs_0_.refs_3_ = bf16[2,192,512]{2,1,0:T(8,128)(2,1)S(1)} collective-permute-done((bf16[2,192,512]{2,1,0:T(8,128)(2,1)S(1)}, bf16[2,192,512]{2,1,0:T(8,128)(2,1)S(1)}, u32[]{:S(2)}, u32[]{:S(2)}) %collective-permute-start.24) | collective-permute-done | bytes 393248 | tf_op jit(solution)/shard_map/ppermute | solution.py:269
  93.0 2.1 %behind_out_0.1 = (bf16[192,896]{1,0:T(8,128)(2,1)S(1)}, bf16[192,896]{1,0:T(8,128)(2,1)S(1)}) custom-call(bf16[2,192,512]{2,1,0:T(8,128)(2,1)S(1)} %behind_act_0.1.refs_0_.refs_3_, bf16[2,192,512]{2,1,0:T(8,128)(2,1)S(1)} %behind_first_0.1.refs_1_, bf16[2,192,512]{2,1,0:T(8,128)(2,1)S(1)} %collective-permute-done.22.refs_1_.refs_2_, ...), custom_call_target="tpu_custom_call" | custom-call | flops 20000000000 | bytes 1024 | tf_op jit(solution)/shard_map/behind_out_0/pallas_call | solution.py:43
  98.2 4.9 %collective-permute-start.27 = (bf16[2,192,512]{2,1,0:T(8,128)(2,1)S(1)}, bf16[2,192,512]{2,1,0:T(8,128)(2,1)S(1)}, u32[]{:S(2)}, u32[]{:S(2)}) collective-permute-start(bf16[2,192,512]{2,1,0:T(8,128)(2,1)S(1)} %behind_back_2.1.refs_1_), channel_id=1, source_target_pairs={{0,2},{1,3},{2,0},{3,1},{4,6},{5,7},{6,4},{7,5},{8,10},{9,11},{10,... | collective-permute-start | bytes 1179656 | tf_op jit(solution)/shard_map/ppermute | solution.py:269
  103.3 10.2 %collective-permute-start.34 = (bf16[192,896]{1,0:T(8,128)(2,1)S(1)}, bf16[192,896]{1,0:T(8,128)(2,1)S(1)}, u32[]{:S(2)}, u32[]{:S(2)}) collective-permute-start(bf16[192,896]{1,0:T(8,128)(2,1)S(1)} %behind_shares.1.refs_5_), channel_id=1, source_target_pairs={{8,0},{9,1},{10,2},{11,3},{12,4},{13,5},{14,6},{15,7},{16,8},{17,9... | collective-permute-start | bytes 1032200 | tf_op jit(solution)/shard_map/ppermute | solution.py:293
  115.5 6.3 %collective-permute-start.35 = (bf16[192,896]{1,0:T(8,128)(2,1)S(1)}, bf16[192,896]{1,0:T(8,128)(2,1)S(1)}, u32[]{:S(2)}, u32[]{:S(2)}) collective-permute-start(bf16[192,896]{1,0:T(8,128)(2,1)S(1)} %get-tuple-element.14.refs_2_), channel_id=1, source_target_pairs={{8,1},{9,0},{10,3},{11,2},{12,5},{13,4},{14,7},{15,6},{16,9},{17,8... | collective-permute-start | bytes 1032200 | tf_op jit(solution)/shard_map/ppermute | solution.py:293
  121.7 1.9 %collective-permute-start.36 = (bf16[192,896]{1,0:T(8,128)(2,1)S(1)}, bf16[192,896]{1,0:T(8,128)(2,1)S(1)}, u32[]{:S(2)}, u32[]{:S(2)}) collective-permute-start(bf16[192,896]{1,0:T(8,128)(2,1)S(1)} %get-tuple-element.17), channel_id=1, source_target_pairs={{8,0},{9,1},{10,2},{11,3},{12,4},{13,5},{14,6},{15,7},{16,8},{17,9... | collective-permute-start | bytes 1032200 | tf_op jit(solution)/shard_map/ppermute | solution.py:293
  123.8 3.6 %collective-permute-start.30 = (bf16[192,896]{1,0:T(8,128)(2,1)S(1)}, bf16[192,896]{1,0:T(8,128)(2,1)S(1)}, u32[]{:S(2)}, u32[]{:S(2)}) collective-permute-start(bf16[192,896]{1,0:T(8,128)(2,1)S(1)} %ahead_shares.1.refs_6_), channel_id=1, source_target_pairs={{0,8},{1,9},{2,10},{3,11},{4,12},{5,13},{6,14},{7,15},{8,16},{9,17... | collective-permute-start | bytes 1032200 | tf_op jit(solution)/shard_map/ppermute | solution.py:293
  129.0 2.2 %collective-permute-start.32 = (bf16[192,896]{1,0:T(8,128)(2,1)S(1)}, bf16[192,896]{1,0:T(8,128)(2,1)S(1)}, u32[]{:S(2)}, u32[]{:S(2)}) collective-permute-start(bf16[192,896]{1,0:T(8,128)(2,1)S(1)} %get-tuple-element.15.refs_3_), channel_id=1, source_target_pairs={{0,9},{1,8},{2,11},{3,10},{4,13},{5,12},{6,15},{7,14},{8,17},{9,16... | collective-permute-start | bytes 1032200 | tf_op jit(solution)/shard_map/ppermute | solution.py:293
  134.2 3.4 %collective-permute-done.32.refs_1_ = bf16[192,896]{1,0:T(8,128)(2,1)S(1)} collective-permute-done((bf16[192,896]{1,0:T(8,128)(2,1)S(1)}, bf16[192,896]{1,0:T(8,128)(2,1)S(1)}, u32[]{:S(2)}, u32[]{:S(2)}) %collective-permute-start.32) | collective-permute-done | bytes 344096 | tf_op jit(solution)/shard_map/ppermute | solution.py:293
  (123 shorter events, 50.8 us)
Async XLA Ops:
  1.6 9.9 %collective-permute-start.1 = (bf16[192,896]{1,0:T(8,128)(2,1)S(1)}, bf16[192,896]{1,0:T(8,128)(2,1)S(1)}, u32[]{:S(2)}, u32[]{:S(2)}) collective-permute-start(bf16[192,896]{1,0:T(8,128)(2,1)S(1)} %slice_bitcast_fusion.refs_0_), channel_id=1, source_target_pairs={{0,1},{1,0},{2,3},{3,2},{4,5},{5,4},{6,7},{7,6},{8,9},{9,8},{10,11... | collective-permute-start | bytes 1032200 | tf_op jit(solution)/shard_map/ppermute | solution.py:284
  4.9 14.0 %collective-permute-start = (bf16[192,896]{1,0:T(8,128)(2,1)S(1)}, bf16[192,896]{1,0:T(8,128)(2,1)S(1)}, u32[]{:S(2)}, u32[]{:S(2)}) collective-permute-start(bf16[192,896]{1,0:T(8,128)(2,1)S(1)} %ahead_rows_0.1.refs_1_.refs_0_), channel_id=1, source_target_pairs={{0,1},{1,0},{2,3},{3,2},{4,5},{5,4},{6,7},{7,6},{8,9},{9,8},{10,11... | collective-permute-start | bytes 1032200 | tf_op jit(solution)/shard_map/ppermute | solution.py:284
  6.0 20.3 %collective-permute-start.3 = (bf16[192,896]{1,0:T(8,128)(2,1)S(1)}, bf16[192,896]{1,0:T(8,128)(2,1)S(1)}, u32[]{:S(2)}, u32[]{:S(2)}) collective-permute-start(bf16[192,896]{1,0:T(8,128)(2,1)S(1)} %grad_rows_0.1.refs_3_.refs_0_), channel_id=1, source_target_pairs={{0,1},{1,0},{2,3},{3,2},{4,5},{5,4},{6,7},{7,6},{8,9},{9,8},{10,11... | collective-permute-start | bytes 1032200 | tf_op jit(solution)/shard_map/ppermute | solution.py:284
  16.0 12.4 %collective-permute-start.2 = (bf16[2,192,512]{2,1,0:T(8,128)(2,1)S(1)}, bf16[2,192,512]{2,1,0:T(8,128)(2,1)S(1)}, u32[]{:S(2)}, u32[]{:S(2)}) collective-permute-start(bf16[2,192,512]{2,1,0:T(8,128)(2,1)S(1)} %behind_far_0.1.refs_1_.refs_0_), channel_id=1, source_target_pairs={{0,2},{1,3},{2,0},{3,1},{4,6},{5,7},{6,4},{7,5},{8,10},{9,11},{10,... | collective-permute-start | bytes 1179656 | tf_op jit(solution)/shard_map/ppermute | solution.py:269
  17.3 16.4 %collective-permute-start.6 = (bf16[192,896]{1,0:T(8,128)(2,1)S(1)}, bf16[192,896]{1,0:T(8,128)(2,1)S(1)}, u32[]{:S(2)}, u32[]{:S(2)}) collective-permute-start(bf16[192,896]{1,0:T(8,128)(2,1)S(1)} %behind_rows_1.1.refs_3_.refs_0_.refs_2_), channel_id=1, source_target_pairs={{0,1},{1,0},{2,3},{3,2},{4,5},{5,4},{6,7},{7,6},{8,9},{9,8},{10,11... | collective-permute-start | bytes 1032200 | tf_op jit(solution)/shard_map/ppermute | solution.py:284
  21.7 15.0 %collective-permute-start.8 = (bf16[2,192,512]{2,1,0:T(8,128)(2,1)S(1)}, bf16[2,192,512]{2,1,0:T(8,128)(2,1)S(1)}, u32[]{:S(2)}, u32[]{:S(2)}) collective-permute-start(bf16[2,192,512]{2,1,0:T(8,128)(2,1)S(1)} %ahead_far_0.1.refs_3_.refs_0_), channel_id=1, source_target_pairs={{0,2},{1,3},{2,0},{3,1},{4,6},{5,7},{6,4},{7,5},{8,10},{9,11},{10,... | collective-permute-start | bytes 1179656 | tf_op jit(solution)/shard_map/ppermute | solution.py:269
  27.1 15.6 %collective-permute-start.5 = (bf16[1,192,512]{2,1,0:T(8,128)(2,1)S(1)}, bf16[1,192,512]{2,1,0:T(8,128)(2,1)S(1)}, u32[]{:S(2)}, u32[]{:S(2)}) collective-permute-start(bf16[1,192,512]{2,1,0:T(8,128)(2,1)S(1)} %grad_far_0.1.refs_2_.refs_0_), channel_id=1, source_target_pairs={{0,2},{1,3},{2,0},{3,1},{4,6},{5,7},{6,4},{7,5},{8,10},{9,11},{10,... | collective-permute-start | bytes 589832 | tf_op jit(solution)/shard_map/ppermute | solution.py:269
  29.2 14.2 %collective-permute-start.4 = (bf16[192,896]{1,0:T(8,128)(2,1)S(1)}, bf16[192,896]{1,0:T(8,128)(2,1)S(1)}, u32[]{:S(2)}, u32[]{:S(2)}) collective-permute-start(bf16[192,896]{1,0:T(8,128)(2,1)S(1)} %ahead_rows_1.1.refs_3_.refs_0_.refs_2_), channel_id=1, source_target_pairs={{0,1},{1,0},{2,3},{3,2},{4,5},{5,4},{6,7},{7,6},{8,9},{9,8},{10,11... | collective-permute-start | bytes 1032200 | tf_op jit(solution)/shard_map/ppermute | solution.py:284
  36.8 9.6 %collective-permute-start.9 = (bf16[2,192,512]{2,1,0:T(8,128)(2,1)S(1)}, bf16[2,192,512]{2,1,0:T(8,128)(2,1)S(1)}, u32[]{:S(2)}, u32[]{:S(2)}) collective-permute-start(bf16[2,192,512]{2,1,0:T(8,128)(2,1)S(1)} %ahead_middle_0.1.refs_3_), channel_id=1, source_target_pairs={{0,0},{1,1},{2,4},{3,5},{4,2},{5,3},{6,6},{7,7},{8,8},{9,9},{10,12... | collective-permute-start | bytes 1179656 | tf_op jit(solution)/shard_map/ppermute | solution.py:269
  37.6 10.5 %collective-permute-start.11 = (bf16[2,192,512]{2,1,0:T(8,128)(2,1)S(1)}, bf16[2,192,512]{2,1,0:T(8,128)(2,1)S(1)}, u32[]{:S(2)}, u32[]{:S(2)}) collective-permute-start(bf16[2,192,512]{2,1,0:T(8,128)(2,1)S(1)} %behind_outer_1.1.refs_1_), channel_id=1, source_target_pairs={{0,2},{1,3},{2,0},{3,1},{4,6},{5,7},{6,4},{7,5},{8,10},{9,11},{10,... | collective-permute-start | bytes 1179656 | tf_op jit(solution)/shard_map/ppermute | solution.py:269
  48.1 12.5 %collective-permute-start.15 = (bf16[2,192,512]{2,1,0:T(8,128)(2,1)S(1)}, bf16[2,192,512]{2,1,0:T(8,128)(2,1)S(1)}, u32[]{:S(2)}, u32[]{:S(2)}) collective-permute-start(bf16[2,192,512]{2,1,0:T(8,128)(2,1)S(1)} %behind_middle_1.1.refs_3_), channel_id=1, source_target_pairs={{0,0},{1,1},{2,4},{3,5},{4,2},{5,3},{6,6},{7,7},{8,8},{9,9},{10,12... | collective-permute-start | bytes 1179656 | tf_op jit(solution)/shard_map/ppermute | solution.py:269
  60.7 11.4 %collective-permute-start.18 = (bf16[2,192,512]{2,1,0:T(8,128)(2,1)S(1)}, bf16[2,192,512]{2,1,0:T(8,128)(2,1)S(1)}, u32[]{:S(2)}, u32[]{:S(2)}) collective-permute-start(bf16[2,192,512]{2,1,0:T(8,128)(2,1)S(1)} %behind_outer_2.1.refs_2_), channel_id=1, source_target_pairs={{0,2},{1,3},{2,0},{3,1},{4,6},{5,7},{6,4},{7,5},{8,10},{9,11},{10,... | collective-permute-start | bytes 1179656 | tf_op jit(solution)/shard_map/ppermute | solution.py:269
  63.5 12.3 %collective-permute-start.17 = (bf16[2,192,512]{2,1,0:T(8,128)(2,1)S(1)}, bf16[2,192,512]{2,1,0:T(8,128)(2,1)S(1)}, u32[]{:S(2)}, u32[]{:S(2)}) collective-permute-start(bf16[2,192,512]{2,1,0:T(8,128)(2,1)S(1)} %ahead_outer_2.1.refs_2_), channel_id=1, source_target_pairs={{0,2},{1,3},{2,0},{3,1},{4,6},{5,7},{6,4},{7,5},{8,10},{9,11},{10,... | collective-permute-start | bytes 1179656 | tf_op jit(solution)/shard_map/ppermute | solution.py:269
  68.2 11.7 %collective-permute-start.21 = (bf16[1,192,512]{2,1,0:T(8,128)(2,1)S(1)}, bf16[1,192,512]{2,1,0:T(8,128)(2,1)S(1)}, u32[]{:S(2)}, u32[]{:S(2)}) collective-permute-start(bf16[1,192,512]{2,1,0:T(8,128)(2,1)S(1)} %grad_third_1.1.refs_1_), channel_id=1, source_target_pairs={{0,2},{1,3},{2,0},{3,1},{4,6},{5,7},{6,4},{7,5},{8,10},{9,11},{10,... | collective-permute-start | bytes 589832 | tf_op jit(solution)/shard_map/ppermute | solution.py:269
  80.3 9.9 %collective-permute-start.24 = (bf16[2,192,512]{2,1,0:T(8,128)(2,1)S(1)}, bf16[2,192,512]{2,1,0:T(8,128)(2,1)S(1)}, u32[]{:S(2)}, u32[]{:S(2)}) collective-permute-start(bf16[2,192,512]{2,1,0:T(8,128)(2,1)S(1)} %behind_back_1.1.refs_2_), channel_id=1, source_target_pairs={{0,2},{1,3},{2,0},{3,1},{4,6},{5,7},{6,4},{7,5},{8,10},{9,11},{10,... | collective-permute-start | bytes 1179656 | tf_op jit(solution)/shard_map/ppermute | solution.py:269
  82.4 9.9 %collective-permute-start.23 = (bf16[1,192,512]{2,1,0:T(8,128)(2,1)S(1)}, bf16[1,192,512]{2,1,0:T(8,128)(2,1)S(1)}, u32[]{:S(2)}, u32[]{:S(2)}) collective-permute-start(bf16[1,192,512]{2,1,0:T(8,128)(2,1)S(1)} %ahead_back_1.1.refs_1_), channel_id=1, source_target_pairs={{0,2},{1,3},{2,0},{3,1},{4,6},{5,7},{6,4},{7,5},{8,10},{9,11},{10,... | collective-permute-start | bytes 589832 | tf_op jit(solution)/shard_map/ppermute | solution.py:269
  92.3 10.8 %collective-permute-start.29 = (bf16[1,192,512]{2,1,0:T(8,128)(2,1)S(1)}, bf16[1,192,512]{2,1,0:T(8,128)(2,1)S(1)}, u32[]{:S(2)}, u32[]{:S(2)}) collective-permute-start(bf16[1,192,512]{2,1,0:T(8,128)(2,1)S(1)} %ahead_first_1.1.refs_5_.refs_1_), channel_id=1, source_target_pairs={{0,0},{1,1},{2,4},{3,5},{4,2},{5,3},{6,6},{7,7},{8,8},{9,9},{10,12... | collective-permute-start | bytes 589832 | tf_op jit(solution)/shard_map/ppermute | solution.py:269
  97.5 26.1 %collective-permute-start.25 = (bf16[192,896]{1,0:T(8,128)(2,1)S(1)}, bf16[192,896]{1,0:T(8,128)(2,1)S(1)}, u32[]{:S(2)}, u32[]{:S(2)}) collective-permute-start(bf16[192,896]{1,0:T(8,128)(2,1)S(1)} %get-tuple-element.12.refs_1_), channel_id=1, source_target_pairs={{0,1},{1,0},{2,3},{3,2},{4,5},{5,4},{6,7},{7,6},{8,9},{9,8},{10,11... | collective-permute-start | bytes 1032200 | tf_op jit(solution)/shard_map/ppermute | solution.py:284
  98.2 15.3 %collective-permute-start.27 = (bf16[2,192,512]{2,1,0:T(8,128)(2,1)S(1)}, bf16[2,192,512]{2,1,0:T(8,128)(2,1)S(1)}, u32[]{:S(2)}, u32[]{:S(2)}) collective-permute-start(bf16[2,192,512]{2,1,0:T(8,128)(2,1)S(1)} %behind_back_2.1.refs_1_), channel_id=1, source_target_pairs={{0,2},{1,3},{2,0},{3,1},{4,6},{5,7},{6,4},{7,5},{8,10},{9,11},{10,... | collective-permute-start | bytes 1179656 | tf_op jit(solution)/shard_map/ppermute | solution.py:269
  103.1 24.3 %collective-permute-start.31 = (bf16[1,192,512]{2,1,0:T(8,128)(2,1)S(1)}, bf16[1,192,512]{2,1,0:T(8,128)(2,1)S(1)}, u32[]{:S(2)}, u32[]{:S(2)}) collective-permute-start(bf16[1,192,512]{2,1,0:T(8,128)(2,1)S(1)} %ahead_back_2.1.refs_2_), channel_id=1, source_target_pairs={{0,2},{1,3},{2,0},{3,1},{4,6},{5,7},{6,4},{7,5},{8,10},{9,11},{10,... | collective-permute-start | bytes 589832 | tf_op jit(solution)/shard_map/ppermute | solution.py:269
  103.3 27.9 %collective-permute-start.34 = (bf16[192,896]{1,0:T(8,128)(2,1)S(1)}, bf16[192,896]{1,0:T(8,128)(2,1)S(1)}, u32[]{:S(2)}, u32[]{:S(2)}) collective-permute-start(bf16[192,896]{1,0:T(8,128)(2,1)S(1)} %behind_shares.1.refs_5_), channel_id=1, source_target_pairs={{8,0},{9,1},{10,2},{11,3},{12,4},{13,5},{14,6},{15,7},{16,8},{17,9... | collective-permute-start | bytes 1032200 | tf_op jit(solution)/shard_map/ppermute | solution.py:293
  115.5 17.7 %collective-permute-start.35 = (bf16[192,896]{1,0:T(8,128)(2,1)S(1)}, bf16[192,896]{1,0:T(8,128)(2,1)S(1)}, u32[]{:S(2)}, u32[]{:S(2)}) collective-permute-start(bf16[192,896]{1,0:T(8,128)(2,1)S(1)} %get-tuple-element.14.refs_2_), channel_id=1, source_target_pairs={{8,1},{9,0},{10,3},{11,2},{12,5},{13,4},{14,7},{15,6},{16,9},{17,8... | collective-permute-start | bytes 1032200 | tf_op jit(solution)/shard_map/ppermute | solution.py:293
  121.7 11.5 %collective-permute-start.36 = (bf16[192,896]{1,0:T(8,128)(2,1)S(1)}, bf16[192,896]{1,0:T(8,128)(2,1)S(1)}, u32[]{:S(2)}, u32[]{:S(2)}) collective-permute-start(bf16[192,896]{1,0:T(8,128)(2,1)S(1)} %get-tuple-element.17), channel_id=1, source_target_pairs={{8,0},{9,1},{10,2},{11,3},{12,4},{13,5},{14,6},{15,7},{16,8},{17,9... | collective-permute-start | bytes 1032200 | tf_op jit(solution)/shard_map/ppermute | solution.py:293
  123.8 15.4 %collective-permute-start.30 = (bf16[192,896]{1,0:T(8,128)(2,1)S(1)}, bf16[192,896]{1,0:T(8,128)(2,1)S(1)}, u32[]{:S(2)}, u32[]{:S(2)}) collective-permute-start(bf16[192,896]{1,0:T(8,128)(2,1)S(1)} %ahead_shares.1.refs_6_), channel_id=1, source_target_pairs={{0,8},{1,9},{2,10},{3,11},{4,12},{5,13},{6,14},{7,15},{8,16},{9,17... | collective-permute-start | bytes 1032200 | tf_op jit(solution)/shard_map/ppermute | solution.py:293
  (23 other events, 130.5 us)

commit v21 on v20

--- a/solution.py
+++ b/solution.py
@@ -480,28 +480,28 @@
     grad.near_products()
     grad.merged_hop(1, grad.far[1])
     ahead.middle_sum(1)
-    grad.middle_sum(1)
     activate_behind(0)
     behind.merged_hop(2, behind.act[0])
+    grad.middle_sum(1)
     activate_ahead(0)
     ahead.merged_hop(2, ahead.act[0])
     grad.last_third_hop()
     behind.middle_pass(0)
+    activate_behind(1)
+    behind.outer_pass(1)
     ahead.middle_pass(0)
     activate_ahead(1)
-    activate_behind(1)
-    behind.outer_pass(1)
+    behind.middle_pass(1)
     ahead.outer_pass(1)
-    behind.middle_pass(1)
+    finish_first(behind)
     ahead.middle_pass(1)
-    finish_first(behind)
+    behind.outer_pass(2)
     finish_first(ahead)
-    behind.outer_pass(2)
     ahead.outer_pass(2)
     send_first(behind)
     finish_last(behind)
+    finish_last(ahead)
     send_first(ahead)
-    finish_last(ahead)
     behind_sent = result(behind)
     ahead_sent = result(ahead)
     return ahead_sent, behind_sent

time: 142 us -> 145 us (1.021)
  waiting for transfers between devices: 35 us -> 37.3 us
    ppermute x6, starting transfers between devices: 26.2 us -> 22.8 us  [to_section(): return lax.ppermute(value, ('section', 'expert'), pairs)]
    ppermute x23, starting transfers between devices: 39.1 us -> 42.2 us  [between(): return lax.ppermute(value, 'expert', pairs)]
  transfers between devices with their start and end apart: 37 -> 37, of which waited for: 12 -> 10; matrix products, arithmetic and copies ran while one was open for 0% -> 0% of each run, Pallas kernels for 15% -> 15%
where the time goes in v21:
time: 145 us; the launch traced here: 144 us
  starting transfers between devices  74.4 us (51%)
  waiting for transfers between devices  37.3 us (26%)
  Pallas kernels  22.1 us (15%)
  local copies, waits for them, and re-layouts  9.36 us (6%)
    ppermute x23, starting transfers between devices, between(): return lax.ppermute(value, 'expert', pairs)  42.2 us
    ppermute x6, starting transfers between devices, to_section(): return lax.ppermute(value, ('section', 'expert'), pairs)  22.8 us
    pallas_call x46, Pallas kernels, call(): pl.pallas_call(run, compiler_params=pltpu.CompilerParams(vmem_limit_bytes...  22.1 us
    ppermute x23, waiting for transfers between devices, between(): return lax.ppermute(value, 'expert', pairs)  19 us
    ppermute x8, waiting for transfers between devices, swapped(): return lax.ppermute(value, 'expert', [(i, i ^ 1) for i in range(devices)])  12.1 us
    ppermute x8, starting transfers between devices, swapped(): return lax.ppermute(value, 'expert', [(i, i ^ 1) for i in range(devices)])  9.31 us
    unnamed x20, local copies, waits for them, and re-layouts  7.8 us
    ppermute x6, waiting for transfers between devices, to_section(): return lax.ppermute(value, ('section', 'expert'), pairs)  6.16 us
  transfers between devices with their start and end apart: 37, of which 10 were waited for; matrix products, arithmetic and copies ran while one was open for 0% of the time, Pallas kernels for 15%

profile of v21, /device:TPU:1, one launch (start us, length us, event | category | flops | bytes accessed | tf_op | source)
XLA Modules:
  0.0 144.4 jit_solution(2620154942526519231)
XLA Ops:
  1.6 2.1 %collective-permute-start.1 = (bf16[192,896]{1,0:T(8,128)(2,1)S(1)}, bf16[192,896]{1,0:T(8,128)(2,1)S(1)}, u32[]{:S(2)}, u32[]{:S(2)}) collective-permute-start(bf16[192,896]{1,0:T(8,128)(2,1)S(1)} %slice_bitcast_fusion.refs_0_), channel_id=1, source_target_pairs={{0,1},{1,0},{2,3},{3,2},{4,5},{5,4},{6,7},{7,6},{8,9},{9,8},{10,11... | collective-permute-start | bytes 1032200 | tf_op jit(solution)/shard_map/ppermute | solution.py:284
  7.3 4.2 %collective-permute-done.1.refs_1_ = bf16[192,896]{1,0:T(8,128)(2,1)S(1)} collective-permute-done((bf16[192,896]{1,0:T(8,128)(2,1)S(1)}, bf16[192,896]{1,0:T(8,128)(2,1)S(1)}, u32[]{:S(2)}, u32[]{:S(2)}) %collective-permute-start.1) | collective-permute-done | bytes 344096 | tf_op jit(solution)/shard_map/ppermute | solution.py:284
  11.6 3.1 %copy-done.1 = bf16[1,1,2,1024,1792]{4,3,2,1,0:T(8,128)(2,1)S(1)} copy-done((bf16[1,1,2,1024,1792]{4,3,2,1,0:T(8,128)(2,1)S(1)}, bf16[1,1,2,1024,1792]{4,3,2,1,0:T(8,128)(2,1)}, u32[]{:S(2)}) %copy-start.1) | copy-done | bytes 7340056
  22.0 4.4 %collective-permute-done.3.refs_1_ = bf16[192,896]{1,0:T(8,128)(2,1)S(1)} collective-permute-done((bf16[192,896]{1,0:T(8,128)(2,1)S(1)}, bf16[192,896]{1,0:T(8,128)(2,1)S(1)}, u32[]{:S(2)}, u32[]{:S(2)}) %collective-permute-start.3) | collective-permute-done | bytes 344096 | tf_op jit(solution)/shard_map/ppermute | solution.py:284
  30.5 3.2 %collective-permute-done.6.refs_1_.refs_3_ = bf16[192,896]{1,0:T(8,128)(2,1)S(1)} collective-permute-done((bf16[192,896]{1,0:T(8,128)(2,1)S(1)}, bf16[192,896]{1,0:T(8,128)(2,1)S(1)}, u32[]{:S(2)}, u32[]{:S(2)}) %collective-permute-start.6) | collective-permute-done | bytes 344096 | tf_op jit(solution)/shard_map/ppermute | solution.py:284
  37.6 3.8 %collective-permute-start.12 = (bf16[2,192,512]{2,1,0:T(8,128)(2,1)S(1)}, bf16[2,192,512]{2,1,0:T(8,128)(2,1)S(1)}, u32[]{:S(2)}, u32[]{:S(2)}) collective-permute-start(bf16[2,192,512]{2,1,0:T(8,128)(2,1)S(1)} %behind_outer_1.1.refs_1_), channel_id=1, source_target_pairs={{0,2},{1,3},{2,0},{3,1},{4,6},{5,7},{6,4},{7,5},{8,10},{9,11},{10,... | collective-permute-start | bytes 1179656 | tf_op jit(solution)/shard_map/ppermute | solution.py:269
  50.6 3.0 %collective-permute-start.14 = (bf16[1,192,512]{2,1,0:T(8,128)(2,1)S(1)}, bf16[1,192,512]{2,1,0:T(8,128)(2,1)S(1)}, u32[]{:S(2)}, u32[]{:S(2)}) collective-permute-start(bf16[1,192,512]{2,1,0:T(8,128)(2,1)S(1)} %grad_outer_1.1.refs_2_), channel_id=1, source_target_pairs={{0,2},{1,3},{2,0},{3,1},{4,6},{5,7},{6,4},{7,5},{8,10},{9,11},{10,... | collective-permute-start | bytes 589832 | tf_op jit(solution)/shard_map/ppermute | solution.py:269
  56.2 3.4 %collective-permute-done.14.refs_3_.refs_1_ = bf16[1,192,512]{2,1,0:T(8,128)(2,1)S(1)} collective-permute-done((bf16[1,192,512]{2,1,0:T(8,128)(2,1)S(1)}, bf16[1,192,512]{2,1,0:T(8,128)(2,1)S(1)}, u32[]{:S(2)}, u32[]{:S(2)}) %collective-permute-start.14) | collective-permute-done | bytes 196640 | tf_op jit(solution)/shard_map/ppermute | solution.py:269
  62.2 5.9 %collective-permute-start.17 = (bf16[2,192,512]{2,1,0:T(8,128)(2,1)S(1)}, bf16[2,192,512]{2,1,0:T(8,128)(2,1)S(1)}, u32[]{:S(2)}, u32[]{:S(2)}) collective-permute-start(bf16[2,192,512]{2,1,0:T(8,128)(2,1)S(1)} %ahead_outer_2.1.refs_2_), channel_id=1, source_target_pairs={{0,2},{1,3},{2,0},{3,1},{4,6},{5,7},{6,4},{7,5},{8,10},{9,11},{10,... | collective-permute-start | bytes 1179656 | tf_op jit(solution)/shard_map/ppermute | solution.py:269
  68.2 3.9 %collective-permute-start.20 = (bf16[1,192,512]{2,1,0:T(8,128)(2,1)S(1)}, bf16[1,192,512]{2,1,0:T(8,128)(2,1)S(1)}, u32[]{:S(2)}, u32[]{:S(2)}) collective-permute-start(bf16[1,192,512]{2,1,0:T(8,128)(2,1)S(1)} %grad_third_1.1.refs_1_), channel_id=1, source_target_pairs={{0,2},{1,3},{2,0},{3,1},{4,6},{5,7},{6,4},{7,5},{8,10},{9,11},{10,... | collective-permute-start | bytes 589832 | tf_op jit(solution)/shard_map/ppermute | solution.py:269
  72.9 8.9 %collective-permute-done.20.refs_3_ = bf16[1,192,512]{2,1,0:T(8,128)(2,1)S(1)} collective-permute-done((bf16[1,192,512]{2,1,0:T(8,128)(2,1)S(1)}, bf16[1,192,512]{2,1,0:T(8,128)(2,1)S(1)}, u32[]{:S(2)}, u32[]{:S(2)}) %collective-permute-start.20) | collective-permute-done | bytes 196640 | tf_op jit(solution)/shard_map/ppermute | solution.py:269
  84.7 4.8 %collective-permute-done.23.refs_0_.refs_3_ = bf16[2,192,512]{2,1,0:T(8,128)(2,1)S(1)} collective-permute-done((bf16[2,192,512]{2,1,0:T(8,128)(2,1)S(1)}, bf16[2,192,512]{2,1,0:T(8,128)(2,1)S(1)}, u32[]{:S(2)}, u32[]{:S(2)}) %collective-permute-start.23) | collective-permute-done | bytes 393248 | tf_op jit(solution)/shard_map/ppermute | solution.py:269
  90.3 4.9 %collective-permute-start.24 = (bf16[1,192,512]{2,1,0:T(8,128)(2,1)S(1)}, bf16[1,192,512]{2,1,0:T(8,128)(2,1)S(1)}, u32[]{:S(2)}, u32[]{:S(2)}) collective-permute-start(bf16[1,192,512]{2,1,0:T(8,128)(2,1)S(1)} %ahead_back_1.1.refs_5_), channel_id=1, source_target_pairs={{0,2},{1,3},{2,0},{3,1},{4,6},{5,7},{6,4},{7,5},{8,10},{9,11},{10,... | collective-permute-start | bytes 589832 | tf_op jit(solution)/shard_map/ppermute | solution.py:269
  95.2 2.1 %behind_out_0.1 = (bf16[192,896]{1,0:T(8,128)(2,1)S(1)}, bf16[192,896]{1,0:T(8,128)(2,1)S(1)}) custom-call(bf16[2,192,512]{2,1,0:T(8,128)(2,1)S(1)} %behind_act_0.1.refs_0_.refs_3_, bf16[2,192,512]{2,1,0:T(8,128)(2,1)S(1)} %behind_first_0.1.refs_5_.refs_1_, bf16[2,192,512]{2,1,0:T(8,128)(2,1)S(1)} %collective-permute-done.21.refs_1_.refs_2_, ...), custom_call_target="tpu_custom_call" | custom-call | flops 20000000000 | bytes 1024 | tf_op jit(solution)/shard_map/behind_out_0/pallas_call | solution.py:43
  99.3 2.8 %collective-permute-start.29 = (bf16[2,192,512]{2,1,0:T(8,128)(2,1)S(1)}, bf16[2,192,512]{2,1,0:T(8,128)(2,1)S(1)}, u32[]{:S(2)}, u32[]{:S(2)}) collective-permute-start(bf16[2,192,512]{2,1,0:T(8,128)(2,1)S(1)} %behind_back_2.1.refs_6_), channel_id=1, source_target_pairs={{0,2},{1,3},{2,0},{3,1},{4,6},{5,7},{6,4},{7,5},{8,10},{9,11},{10,... | collective-permute-start | bytes 1179656 | tf_op jit(solution)/shard_map/ppermute | solution.py:269
  105.0 3.6 %collective-permute-start.28 = (bf16[1,192,512]{2,1,0:T(8,128)(2,1)S(1)}, bf16[1,192,512]{2,1,0:T(8,128)(2,1)S(1)}, u32[]{:S(2)}, u32[]{:S(2)}) collective-permute-start(bf16[1,192,512]{2,1,0:T(8,128)(2,1)S(1)} %ahead_back_2.1.refs_2_), channel_id=1, source_target_pairs={{0,2},{1,3},{2,0},{3,1},{4,6},{5,7},{6,4},{7,5},{8,10},{9,11},{10,... | collective-permute-start | bytes 589832 | tf_op jit(solution)/shard_map/ppermute | solution.py:269
  108.8 9.9 %collective-permute-start.34 = (bf16[192,896]{1,0:T(8,128)(2,1)S(1)}, bf16[192,896]{1,0:T(8,128)(2,1)S(1)}, u32[]{:S(2)}, u32[]{:S(2)}) collective-permute-start(bf16[192,896]{1,0:T(8,128)(2,1)S(1)} %behind_shares.1.refs_5_), channel_id=1, source_target_pairs={{8,0},{9,1},{10,2},{11,3},{12,4},{13,5},{14,6},{15,7},{16,8},{17,9... | collective-permute-start | bytes 1032200 | tf_op jit(solution)/shard_map/ppermute | solution.py:293
  120.6 2.5 %collective-permute-start.35 = (bf16[192,896]{1,0:T(8,128)(2,1)S(1)}, bf16[192,896]{1,0:T(8,128)(2,1)S(1)}, u32[]{:S(2)}, u32[]{:S(2)}) collective-permute-start(bf16[192,896]{1,0:T(8,128)(2,1)S(1)} %get-tuple-element.14.refs_6_), channel_id=1, source_target_pairs={{8,1},{9,0},{10,3},{11,2},{12,5},{13,4},{14,7},{15,6},{16,9},{17,8... | collective-permute-start | bytes 1032200 | tf_op jit(solution)/shard_map/ppermute | solution.py:293
  123.1 1.9 %collective-permute-start.36 = (bf16[192,896]{1,0:T(8,128)(2,1)S(1)}, bf16[192,896]{1,0:T(8,128)(2,1)S(1)}, u32[]{:S(2)}, u32[]{:S(2)}) collective-permute-start(bf16[192,896]{1,0:T(8,128)(2,1)S(1)} %get-tuple-element.17), channel_id=1, source_target_pairs={{8,0},{9,1},{10,2},{11,3},{12,4},{13,5},{14,6},{15,7},{16,8},{17,9... | collective-permute-start | bytes 1032200 | tf_op jit(solution)/shard_map/ppermute | solution.py:293
  126.6 4.1 %collective-permute-start.32 = (bf16[192,896]{1,0:T(8,128)(2,1)S(1)}, bf16[192,896]{1,0:T(8,128)(2,1)S(1)}, u32[]{:S(2)}, u32[]{:S(2)}) collective-permute-start(bf16[192,896]{1,0:T(8,128)(2,1)S(1)} %get-tuple-element.15.refs_2_), channel_id=1, source_target_pairs={{0,9},{1,8},{2,11},{3,10},{4,13},{5,12},{6,15},{7,14},{8,17},{9,16... | collective-permute-start | bytes 1032200 | tf_op jit(solution)/shard_map/ppermute | solution.py:293
  130.9 2.4 %collective-permute-start.31 = (bf16[192,896]{1,0:T(8,128)(2,1)S(1)}, bf16[192,896]{1,0:T(8,128)(2,1)S(1)}, u32[]{:S(2)}, u32[]{:S(2)}) collective-permute-start(bf16[192,896]{1,0:T(8,128)(2,1)S(1)} %ahead_shares.1.refs_3_), channel_id=1, source_target_pairs={{0,8},{1,9},{2,10},{3,11},{4,12},{5,13},{6,14},{7,15},{8,16},{9,17... | collective-permute-start | bytes 1032200 | tf_op jit(solution)/shard_map/ppermute | solution.py:293
  133.3 1.9 %collective-permute-start.33 = (bf16[192,896]{1,0:T(8,128)(2,1)S(1)}, bf16[192,896]{1,0:T(8,128)(2,1)S(1)}, u32[]{:S(2)}, u32[]{:S(2)}) collective-permute-start(bf16[192,896]{1,0:T(8,128)(2,1)S(1)} %get-tuple-element.16), channel_id=1, source_target_pairs={{0,8},{1,9},{2,10},{3,11},{4,12},{5,13},{6,14},{7,15},{8,16},{9,17... | collective-permute-start | bytes 1032200 | tf_op jit(solution)/shard_map/ppermute | solution.py:293
  136.2 2.5 %collective-permute-done.31.refs_0_ = bf16[192,896]{1,0:T(8,128)(2,1)S(1)} collective-permute-done((bf16[192,896]{1,0:T(8,128)(2,1)S(1)}, bf16[192,896]{1,0:T(8,128)(2,1)S(1)}, u32[]{:S(2)}, u32[]{:S(2)}) %collective-permute-start.31) | collective-permute-done | bytes 344096 | tf_op jit(solution)/shard_map/ppermute | solution.py:293
  138.7 3.7 %collective-permute-done.33.refs_2_ = bf16[192,896]{1,0:T(8,128)(2,1)S(1)} collective-permute-done((bf16[192,896]{1,0:T(8,128)(2,1)S(1)}, bf16[192,896]{1,0:T(8,128)(2,1)S(1)}, u32[]{:S(2)}, u32[]{:S(2)}) %collective-permute-start.33) | collective-permute-done | bytes 344096 | tf_op jit(solution)/shard_map/ppermute | solution.py:293
  (123 shorter events, 50.0 us)
Async XLA Ops:
  1.6 9.9 %collective-permute-start.1 = (bf16[192,896]{1,0:T(8,128)(2,1)S(1)}, bf16[192,896]{1,0:T(8,128)(2,1)S(1)}, u32[]{:S(2)}, u32[]{:S(2)}) collective-permute-start(bf16[192,896]{1,0:T(8,128)(2,1)S(1)} %slice_bitcast_fusion.refs_0_), channel_id=1, source_target_pairs={{0,1},{1,0},{2,3},{3,2},{4,5},{5,4},{6,7},{7,6},{8,9},{9,8},{10,11... | collective-permute-start | bytes 1032200 | tf_op jit(solution)/shard_map/ppermute | solution.py:284
  4.9 14.0 %collective-permute-start = (bf16[192,896]{1,0:T(8,128)(2,1)S(1)}, bf16[192,896]{1,0:T(8,128)(2,1)S(1)}, u32[]{:S(2)}, u32[]{:S(2)}) collective-permute-start(bf16[192,896]{1,0:T(8,128)(2,1)S(1)} %ahead_rows_0.1.refs_1_.refs_0_), channel_id=1, source_target_pairs={{0,1},{1,0},{2,3},{3,2},{4,5},{5,4},{6,7},{7,6},{8,9},{9,8},{10,11... | collective-permute-start | bytes 1032200 | tf_op jit(solution)/shard_map/ppermute | solution.py:284
  6.0 20.3 %collective-permute-start.3 = (bf16[192,896]{1,0:T(8,128)(2,1)S(1)}, bf16[192,896]{1,0:T(8,128)(2,1)S(1)}, u32[]{:S(2)}, u32[]{:S(2)}) collective-permute-start(bf16[192,896]{1,0:T(8,128)(2,1)S(1)} %grad_rows_0.1.refs_3_.refs_0_), channel_id=1, source_target_pairs={{0,1},{1,0},{2,3},{3,2},{4,5},{5,4},{6,7},{7,6},{8,9},{9,8},{10,11... | collective-permute-start | bytes 1032200 | tf_op jit(solution)/shard_map/ppermute | solution.py:284
  16.0 12.4 %collective-permute-start.2 = (bf16[2,192,512]{2,1,0:T(8,128)(2,1)S(1)}, bf16[2,192,512]{2,1,0:T(8,128)(2,1)S(1)}, u32[]{:S(2)}, u32[]{:S(2)}) collective-permute-start(bf16[2,192,512]{2,1,0:T(8,128)(2,1)S(1)} %behind_far_0.1.refs_1_.refs_0_), channel_id=1, source_target_pairs={{0,2},{1,3},{2,0},{3,1},{4,6},{5,7},{6,4},{7,5},{8,10},{9,11},{10,... | collective-permute-start | bytes 1179656 | tf_op jit(solution)/shard_map/ppermute | solution.py:269
  17.3 16.4 %collective-permute-start.6 = (bf16[192,896]{1,0:T(8,128)(2,1)S(1)}, bf16[192,896]{1,0:T(8,128)(2,1)S(1)}, u32[]{:S(2)}, u32[]{:S(2)}) collective-permute-start(bf16[192,896]{1,0:T(8,128)(2,1)S(1)} %behind_rows_1.1.refs_3_.refs_0_.refs_2_), channel_id=1, source_target_pairs={{0,1},{1,0},{2,3},{3,2},{4,5},{5,4},{6,7},{7,6},{8,9},{9,8},{10,11... | collective-permute-start | bytes 1032200 | tf_op jit(solution)/shard_map/ppermute | solution.py:284
  21.7 15.0 %collective-permute-start.8 = (bf16[2,192,512]{2,1,0:T(8,128)(2,1)S(1)}, bf16[2,192,512]{2,1,0:T(8,128)(2,1)S(1)}, u32[]{:S(2)}, u32[]{:S(2)}) collective-permute-start(bf16[2,192,512]{2,1,0:T(8,128)(2,1)S(1)} %ahead_far_0.1.refs_3_.refs_0_), channel_id=1, source_target_pairs={{0,2},{1,3},{2,0},{3,1},{4,6},{5,7},{6,4},{7,5},{8,10},{9,11},{10,... | collective-permute-start | bytes 1179656 | tf_op jit(solution)/shard_map/ppermute | solution.py:269
  27.1 15.6 %collective-permute-start.5 = (bf16[1,192,512]{2,1,0:T(8,128)(2,1)S(1)}, bf16[1,192,512]{2,1,0:T(8,128)(2,1)S(1)}, u32[]{:S(2)}, u32[]{:S(2)}) collective-permute-start(bf16[1,192,512]{2,1,0:T(8,128)(2,1)S(1)} %grad_far_0.1.refs_2_.refs_0_), channel_id=1, source_target_pairs={{0,2},{1,3},{2,0},{3,1},{4,6},{5,7},{6,4},{7,5},{8,10},{9,11},{10,... | collective-permute-start | bytes 589832 | tf_op jit(solution)/shard_map/ppermute | solution.py:269
  29.2 14.2 %collective-permute-start.4 = (bf16[192,896]{1,0:T(8,128)(2,1)S(1)}, bf16[192,896]{1,0:T(8,128)(2,1)S(1)}, u32[]{:S(2)}, u32[]{:S(2)}) collective-permute-start(bf16[192,896]{1,0:T(8,128)(2,1)S(1)} %ahead_rows_1.1.refs_3_.refs_0_.refs_2_), channel_id=1, source_target_pairs={{0,1},{1,0},{2,3},{3,2},{4,5},{5,4},{6,7},{7,6},{8,9},{9,8},{10,11... | collective-permute-start | bytes 1032200 | tf_op jit(solution)/shard_map/ppermute | solution.py:284
  36.8 9.6 %collective-permute-start.9 = (bf16[2,192,512]{2,1,0:T(8,128)(2,1)S(1)}, bf16[2,192,512]{2,1,0:T(8,128)(2,1)S(1)}, u32[]{:S(2)}, u32[]{:S(2)}) collective-permute-start(bf16[2,192,512]{2,1,0:T(8,128)(2,1)S(1)} %ahead_middle_0.1.refs_3_), channel_id=1, source_target_pairs={{0,0},{1,1},{2,4},{3,5},{4,2},{5,3},{6,6},{7,7},{8,8},{9,9},{10,12... | collective-permute-start | bytes 1179656 | tf_op jit(solution)/shard_map/ppermute | solution.py:269
  37.6 10.5 %collective-permute-start.12 = (bf16[2,192,512]{2,1,0:T(8,128)(2,1)S(1)}, bf16[2,192,512]{2,1,0:T(8,128)(2,1)S(1)}, u32[]{:S(2)}, u32[]{:S(2)}) collective-permute-start(bf16[2,192,512]{2,1,0:T(8,128)(2,1)S(1)} %behind_outer_1.1.refs_1_), channel_id=1, source_target_pairs={{0,2},{1,3},{2,0},{3,1},{4,6},{5,7},{6,4},{7,5},{8,10},{9,11},{10,... | collective-permute-start | bytes 1179656 | tf_op jit(solution)/shard_map/ppermute | solution.py:269
  48.1 11.8 %collective-permute-start.15 = (bf16[2,192,512]{2,1,0:T(8,128)(2,1)S(1)}, bf16[2,192,512]{2,1,0:T(8,128)(2,1)S(1)}, u32[]{:S(2)}, u32[]{:S(2)}) collective-permute-start(bf16[2,192,512]{2,1,0:T(8,128)(2,1)S(1)} %behind_middle_1.1.refs_3_), channel_id=1, source_target_pairs={{0,0},{1,1},{2,4},{3,5},{4,2},{5,3},{6,6},{7,7},{8,8},{9,9},{10,12... | collective-permute-start | bytes 1179656 | tf_op jit(solution)/shard_map/ppermute | solution.py:269
  60.0 12.2 %collective-permute-start.18 = (bf16[2,192,512]{2,1,0:T(8,128)(2,1)S(1)}, bf16[2,192,512]{2,1,0:T(8,128)(2,1)S(1)}, u32[]{:S(2)}, u32[]{:S(2)}) collective-permute-start(bf16[2,192,512]{2,1,0:T(8,128)(2,1)S(1)} %behind_outer_2.1.refs_2_), channel_id=1, source_target_pairs={{0,2},{1,3},{2,0},{3,1},{4,6},{5,7},{6,4},{7,5},{8,10},{9,11},{10,... | collective-permute-start | bytes 1179656 | tf_op jit(solution)/shard_map/ppermute | solution.py:269
  62.2 21.6 %collective-permute-start.17 = (bf16[2,192,512]{2,1,0:T(8,128)(2,1)S(1)}, bf16[2,192,512]{2,1,0:T(8,128)(2,1)S(1)}, u32[]{:S(2)}, u32[]{:S(2)}) collective-permute-start(bf16[2,192,512]{2,1,0:T(8,128)(2,1)S(1)} %ahead_outer_2.1.refs_2_), channel_id=1, source_target_pairs={{0,2},{1,3},{2,0},{3,1},{4,6},{5,7},{6,4},{7,5},{8,10},{9,11},{10,... | collective-permute-start | bytes 1179656 | tf_op jit(solution)/shard_map/ppermute | solution.py:269
  68.2 13.6 %collective-permute-start.20 = (bf16[1,192,512]{2,1,0:T(8,128)(2,1)S(1)}, bf16[1,192,512]{2,1,0:T(8,128)(2,1)S(1)}, u32[]{:S(2)}, u32[]{:S(2)}) collective-permute-start(bf16[1,192,512]{2,1,0:T(8,128)(2,1)S(1)} %grad_third_1.1.refs_1_), channel_id=1, source_target_pairs={{0,2},{1,3},{2,0},{3,1},{4,6},{5,7},{6,4},{7,5},{8,10},{9,11},{10,... | collective-permute-start | bytes 589832 | tf_op jit(solution)/shard_map/ppermute | solution.py:269
  72.2 9.9 %collective-permute-start.21 = (bf16[2,192,512]{2,1,0:T(8,128)(2,1)S(1)}, bf16[2,192,512]{2,1,0:T(8,128)(2,1)S(1)}, u32[]{:S(2)}, u32[]{:S(2)}) collective-permute-start(bf16[2,192,512]{2,1,0:T(8,128)(2,1)S(1)} %behind_first_0.1.refs_5_.refs_1_), channel_id=1, source_target_pairs={{0,0},{1,1},{2,4},{3,5},{4,2},{5,3},{6,6},{7,7},{8,8},{9,9},{10,12... | collective-permute-start | bytes 1179656 | tf_op jit(solution)/shard_map/ppermute | solution.py:269
  89.5 9.8 %collective-permute-start.25 = (bf16[2,192,512]{2,1,0:T(8,128)(2,1)S(1)}, bf16[2,192,512]{2,1,0:T(8,128)(2,1)S(1)}, u32[]{:S(2)}, u32[]{:S(2)}) collective-permute-start(bf16[2,192,512]{2,1,0:T(8,128)(2,1)S(1)} %behind_first_1.1.refs_2_.refs_1_), channel_id=1, source_target_pairs={{0,0},{1,1},{2,4},{3,5},{4,2},{5,3},{6,6},{7,7},{8,8},{9,9},{10,12... | collective-permute-start | bytes 1179656 | tf_op jit(solution)/shard_map/ppermute | solution.py:269
  97.2 11.4 %collective-permute-start.30 = (bf16[192,896]{1,0:T(8,128)(2,1)S(1)}, bf16[192,896]{1,0:T(8,128)(2,1)S(1)}, u32[]{:S(2)}, u32[]{:S(2)}) collective-permute-start(bf16[192,896]{1,0:T(8,128)(2,1)S(1)} %get-tuple-element.10.refs_1_), channel_id=1, source_target_pairs={{0,1},{1,0},{2,3},{3,2},{4,5},{5,4},{6,7},{7,6},{8,9},{9,8},{10,11... | collective-permute-start | bytes 1032200 | tf_op jit(solution)/shard_map/ppermute | solution.py:284
  99.3 19.4 %collective-permute-start.29 = (bf16[2,192,512]{2,1,0:T(8,128)(2,1)S(1)}, bf16[2,192,512]{2,1,0:T(8,128)(2,1)S(1)}, u32[]{:S(2)}, u32[]{:S(2)}) collective-permute-start(bf16[2,192,512]{2,1,0:T(8,128)(2,1)S(1)} %behind_back_2.1.refs_6_), channel_id=1, source_target_pairs={{0,2},{1,3},{2,0},{3,1},{4,6},{5,7},{6,4},{7,5},{8,10},{9,11},{10,... | collective-permute-start | bytes 1179656 | tf_op jit(solution)/shard_map/ppermute | solution.py:269
  103.6 27.1 %collective-permute-start.26 = (bf16[192,896]{1,0:T(8,128)(2,1)S(1)}, bf16[192,896]{1,0:T(8,128)(2,1)S(1)}, u32[]{:S(2)}, u32[]{:S(2)}) collective-permute-start(bf16[192,896]{1,0:T(8,128)(2,1)S(1)} %get-tuple-element.12.refs_1_), channel_id=1, source_target_pairs={{0,1},{1,0},{2,3},{3,2},{4,5},{5,4},{6,7},{7,6},{8,9},{9,8},{10,11... | collective-permute-start | bytes 1032200 | tf_op jit(solution)/shard_map/ppermute | solution.py:284
  105.0 20.1 %collective-permute-start.28 = (bf16[1,192,512]{2,1,0:T(8,128)(2,1)S(1)}, bf16[1,192,512]{2,1,0:T(8,128)(2,1)S(1)}, u32[]{:S(2)}, u32[]{:S(2)}) collective-permute-start(bf16[1,192,512]{2,1,0:T(8,128)(2,1)S(1)} %ahead_back_2.1.refs_2_), channel_id=1, source_target_pairs={{0,2},{1,3},{2,0},{3,1},{4,6},{5,7},{6,4},{7,5},{8,10},{9,11},{10,... | collective-permute-start | bytes 589832 | tf_op jit(solution)/shard_map/ppermute | solution.py:269
  108.8 24.5 %collective-permute-start.34 = (bf16[192,896]{1,0:T(8,128)(2,1)S(1)}, bf16[192,896]{1,0:T(8,128)(2,1)S(1)}, u32[]{:S(2)}, u32[]{:S(2)}) collective-permute-start(bf16[192,896]{1,0:T(8,128)(2,1)S(1)} %behind_shares.1.refs_5_), channel_id=1, source_target_pairs={{8,0},{9,1},{10,2},{11,3},{12,4},{13,5},{14,6},{15,7},{16,8},{17,9... | collective-permute-start | bytes 1032200 | tf_op jit(solution)/shard_map/ppermute | solution.py:293
  120.6 14.6 %collective-permute-start.35 = (bf16[192,896]{1,0:T(8,128)(2,1)S(1)}, bf16[192,896]{1,0:T(8,128)(2,1)S(1)}, u32[]{:S(2)}, u32[]{:S(2)}) collective-permute-start(bf16[192,896]{1,0:T(8,128)(2,1)S(1)} %get-tuple-element.14.refs_6_), channel_id=1, source_target_pairs={{8,1},{9,0},{10,3},{11,2},{12,5},{13,4},{14,7},{15,6},{16,9},{17,8... | collective-permute-start | bytes 1032200 | tf_op jit(solution)/shard_map/ppermute | solution.py:293
  123.1 12.1 %collective-permute-start.36 = (bf16[192,896]{1,0:T(8,128)(2,1)S(1)}, bf16[192,896]{1,0:T(8,128)(2,1)S(1)}, u32[]{:S(2)}, u32[]{:S(2)}) collective-permute-start(bf16[192,896]{1,0:T(8,128)(2,1)S(1)} %get-tuple-element.17), channel_id=1, source_target_pairs={{8,0},{9,1},{10,2},{11,3},{12,4},{13,5},{14,6},{15,7},{16,8},{17,9... | collective-permute-start | bytes 1032200 | tf_op jit(solution)/shard_map/ppermute | solution.py:293
  126.6 12.0 %collective-permute-start.32 = (bf16[192,896]{1,0:T(8,128)(2,1)S(1)}, bf16[192,896]{1,0:T(8,128)(2,1)S(1)}, u32[]{:S(2)}, u32[]{:S(2)}) collective-permute-start(bf16[192,896]{1,0:T(8,128)(2,1)S(1)} %get-tuple-element.15.refs_2_), channel_id=1, source_target_pairs={{0,9},{1,8},{2,11},{3,10},{4,13},{5,12},{6,15},{7,14},{8,17},{9,16... | collective-permute-start | bytes 1032200 | tf_op jit(solution)/shard_map/ppermute | solution.py:293
  (23 other events, 125.5 us)

commit v22 on v20

--- a/solution.py
+++ b/solution.py
@@ -12,7 +12,7 @@
 F32 = jnp.float32
 MIB = 1024 * 1024
 PIECES = 2
-ROWS, SMALL, ACT, FIRST, AHEAD_OUT, BEHIND_OUT = 20, 6, 10, 5.2, 3, 20
+ROWS, SMALL, ACT, FIRST, AHEAD_OUT, BEHIND_OUT, RESULT = 20, 6, 10, 5.2, 20, 60, 60
 
 
 def shift(shard, axis, by):
@@ -453,7 +453,7 @@
     def result(chain):
         operands = (sent[chain, 0], *sent[chain, 1])
         shape = (height, operands[0].shape[1])
-        return kernel_call(f"{chain.name}_result", result_kernel, SMALL, operands, shape)[None]
+        return kernel_call(f"{chain.name}_result", result_kernel, RESULT, operands, shape)[None]
 
     for chain in (behind, ahead, grad):
         chain.fetch(0)
@@ -480,9 +480,9 @@
     grad.near_products()
     grad.merged_hop(1, grad.far[1])
     ahead.middle_sum(1)
-    grad.middle_sum(1)
     activate_behind(0)
     behind.merged_hop(2, behind.act[0])
+    grad.middle_sum(1)
     activate_ahead(0)
     ahead.merged_hop(2, ahead.act[0])
     grad.last_third_hop()
@@ -494,13 +494,13 @@
     ahead.outer_pass(1)
     behind.middle_pass(1)
     ahead.middle_pass(1)
+    finish_first(ahead)
     finish_first(behind)
-    finish_first(ahead)
     behind.outer_pass(2)
     ahead.outer_pass(2)
+    send_first(ahead)
+    finish_last(behind)
     send_first(behind)
-    finish_last(behind)
-    send_first(ahead)
     finish_last(ahead)
     behind_sent = result(behind)
     ahead_sent = result(ahead)

time: 142 us -> 144 us (1.014)
  waiting for transfers between devices: 35 us -> 32.5 us
  Pallas kernels: 22 us -> 23.6 us
  starting transfers between devices: 73.5 us -> 75.1 us
    ppermute x23, waiting for transfers between devices: 17.8 us -> 16 us  [between(): return lax.ppermute(value, 'expert', pairs)]
    ppermute x23, starting transfers between devices: 39.1 us -> 40.7 us  [between(): return lax.ppermute(value, 'expert', pairs)]
    pallas_call x46, Pallas kernels: 22 us -> 23.6 us  [call(): pl.pallas_call(run, compiler_params=pltpu.CompilerParams(vmem_limit_bytes...]
    unnamed x20 -> x28, local copies, waits for them, and re-layouts: 7.8 us -> 7.82 us
  transfers between devices with their start and end apart: 37 -> 37, of which waited for: 12 -> 13; matrix products, arithmetic and copies ran while one was open for 0% -> 0% of each run, Pallas kernels for 15% -> 15%
where the time goes in v22:
time: 144 us; the launch traced here: 142 us
  starting transfers between devices  75.1 us (52%)
  waiting for transfers between devices  32.5 us (23%)
  Pallas kernels  23.6 us (16%)
  local copies, waits for them, and re-layouts  9.39 us (7%)
    ppermute x23, starting transfers between devices, between(): return lax.ppermute(value, 'expert', pairs)  40.7 us
    ppermute x6, starting transfers between devices, to_section(): return lax.ppermute(value, ('section', 'expert'), pairs)  26 us
    pallas_call x46, Pallas kernels, call(): pl.pallas_call(run, compiler_params=pltpu.CompilerParams(vmem_limit_bytes...  23.6 us
    ppermute x23, waiting for transfers between devices, between(): return lax.ppermute(value, 'expert', pairs)  16 us
    ppermute x8, waiting for transfers between devices, swapped(): return lax.ppermute(value, 'expert', [(i, i ^ 1) for i in range(devices)])  12.1 us
    ppermute x8, starting transfers between devices, swapped(): return lax.ppermute(value, 'expert', [(i, i ^ 1) for i in range(devices)])  8.48 us
    unnamed x28, local copies, waits for them, and re-layouts  7.82 us
    ppermute x6, waiting for transfers between devices, to_section(): return lax.ppermute(value, ('section', 'expert'), pairs)  4.33 us
  transfers between devices with their start and end apart: 37, of which 13 were waited for; matrix products, arithmetic and copies ran while one was open for 0% of the time, Pallas kernels for 15%

profile of v22, /device:TPU:1, one launch (start us, length us, event | category | flops | bytes accessed | tf_op | source)
XLA Modules:
  0.0 141.9 jit_solution(9892978677057139784)
XLA Ops:
  1.6 2.1 %collective-permute-start.1 = (bf16[192,896]{1,0:T(8,128)(2,1)S(1)}, bf16[192,896]{1,0:T(8,128)(2,1)S(1)}, u32[]{:S(2)}, u32[]{:S(2)}) collective-permute-start(bf16[192,896]{1,0:T(8,128)(2,1)S(1)} %slice_bitcast_fusion.refs_0_), channel_id=1, source_target_pairs={{0,1},{1,0},{2,3},{3,2},{4,5},{5,4},{6,7},{7,6},{8,9},{9,8},{10,11... | collective-permute-start | bytes 1032200 | tf_op jit(solution)/shard_map/ppermute | solution.py:284
  7.3 4.2 %collective-permute-done.1.refs_1_ = bf16[192,896]{1,0:T(8,128)(2,1)S(1)} collective-permute-done((bf16[192,896]{1,0:T(8,128)(2,1)S(1)}, bf16[192,896]{1,0:T(8,128)(2,1)S(1)}, u32[]{:S(2)}, u32[]{:S(2)}) %collective-permute-start.1) | collective-permute-done | bytes 344096 | tf_op jit(solution)/shard_map/ppermute | solution.py:284
  11.6 3.1 %copy-done.1 = bf16[1,1,2,1024,1792]{4,3,2,1,0:T(8,128)(2,1)S(1)} copy-done((bf16[1,1,2,1024,1792]{4,3,2,1,0:T(8,128)(2,1)S(1)}, bf16[1,1,2,1024,1792]{4,3,2,1,0:T(8,128)(2,1)}, u32[]{:S(2)}) %copy-start.1) | copy-done | bytes 7340056
  22.0 4.4 %collective-permute-done.3.refs_1_ = bf16[192,896]{1,0:T(8,128)(2,1)S(1)} collective-permute-done((bf16[192,896]{1,0:T(8,128)(2,1)S(1)}, bf16[192,896]{1,0:T(8,128)(2,1)S(1)}, u32[]{:S(2)}, u32[]{:S(2)}) %collective-permute-start.3) | collective-permute-done | bytes 344096 | tf_op jit(solution)/shard_map/ppermute | solution.py:284
  30.5 3.2 %collective-permute-done.6.refs_1_.refs_3_ = bf16[192,896]{1,0:T(8,128)(2,1)S(1)} collective-permute-done((bf16[192,896]{1,0:T(8,128)(2,1)S(1)}, bf16[192,896]{1,0:T(8,128)(2,1)S(1)}, u32[]{:S(2)}, u32[]{:S(2)}) %collective-permute-start.6) | collective-permute-done | bytes 344096 | tf_op jit(solution)/shard_map/ppermute | solution.py:284
  37.6 3.8 %collective-permute-start.12 = (bf16[2,192,512]{2,1,0:T(8,128)(2,1)S(1)}, bf16[2,192,512]{2,1,0:T(8,128)(2,1)S(1)}, u32[]{:S(2)}, u32[]{:S(2)}) collective-permute-start(bf16[2,192,512]{2,1,0:T(8,128)(2,1)S(1)} %behind_outer_1.1.refs_1_), channel_id=1, source_target_pairs={{0,2},{1,3},{2,0},{3,1},{4,6},{5,7},{6,4},{7,5},{8,10},{9,11},{10,... | collective-permute-start | bytes 1179656 | tf_op jit(solution)/shard_map/ppermute | solution.py:269
  50.6 2.9 %collective-permute-start.14 = (bf16[1,192,512]{2,1,0:T(8,128)(2,1)S(1)}, bf16[1,192,512]{2,1,0:T(8,128)(2,1)S(1)}, u32[]{:S(2)}, u32[]{:S(2)}) collective-permute-start(bf16[1,192,512]{2,1,0:T(8,128)(2,1)S(1)} %grad_outer_1.1.refs_2_), channel_id=1, source_target_pairs={{0,2},{1,3},{2,0},{3,1},{4,6},{5,7},{6,4},{7,5},{8,10},{9,11},{10,... | collective-permute-start | bytes 589832 | tf_op jit(solution)/shard_map/ppermute | solution.py:269
  56.2 3.4 %collective-permute-done.14.refs_3_.refs_1_ = bf16[1,192,512]{2,1,0:T(8,128)(2,1)S(1)} collective-permute-done((bf16[1,192,512]{2,1,0:T(8,128)(2,1)S(1)}, bf16[1,192,512]{2,1,0:T(8,128)(2,1)S(1)}, u32[]{:S(2)}, u32[]{:S(2)}) %collective-permute-start.14) | collective-permute-done | bytes 196640 | tf_op jit(solution)/shard_map/ppermute | solution.py:269
  62.2 5.9 %collective-permute-start.17 = (bf16[2,192,512]{2,1,0:T(8,128)(2,1)S(1)}, bf16[2,192,512]{2,1,0:T(8,128)(2,1)S(1)}, u32[]{:S(2)}, u32[]{:S(2)}) collective-permute-start(bf16[2,192,512]{2,1,0:T(8,128)(2,1)S(1)} %ahead_outer_2.1.refs_2_), channel_id=1, source_target_pairs={{0,2},{1,3},{2,0},{3,1},{4,6},{5,7},{6,4},{7,5},{8,10},{9,11},{10,... | collective-permute-start | bytes 1179656 | tf_op jit(solution)/shard_map/ppermute | solution.py:269
  68.2 3.9 %collective-permute-start.21 = (bf16[1,192,512]{2,1,0:T(8,128)(2,1)S(1)}, bf16[1,192,512]{2,1,0:T(8,128)(2,1)S(1)}, u32[]{:S(2)}, u32[]{:S(2)}) collective-permute-start(bf16[1,192,512]{2,1,0:T(8,128)(2,1)S(1)} %grad_third_1.1.refs_1_), channel_id=1, source_target_pairs={{0,2},{1,3},{2,0},{3,1},{4,6},{5,7},{6,4},{7,5},{8,10},{9,11},{10,... | collective-permute-start | bytes 589832 | tf_op jit(solution)/shard_map/ppermute | solution.py:269
  72.8 4.7 %collective-permute-done.17.refs_0_.refs_1_ = bf16[2,192,512]{2,1,0:T(8,128)(2,1)S(1)} collective-permute-done((bf16[2,192,512]{2,1,0:T(8,128)(2,1)S(1)}, bf16[2,192,512]{2,1,0:T(8,128)(2,1)S(1)}, u32[]{:S(2)}, u32[]{:S(2)}) %collective-permute-start.17) | collective-permute-done | bytes 393248 | tf_op jit(solution)/shard_map/ppermute | solution.py:269
  78.4 3.4 %collective-permute-done.21.refs_3_ = bf16[1,192,512]{2,1,0:T(8,128)(2,1)S(1)} collective-permute-done((bf16[1,192,512]{2,1,0:T(8,128)(2,1)S(1)}, bf16[1,192,512]{2,1,0:T(8,128)(2,1)S(1)}, u32[]{:S(2)}, u32[]{:S(2)}) %collective-permute-start.21) | collective-permute-done | bytes 196640 | tf_op jit(solution)/shard_map/ppermute | solution.py:269
  83.8 4.3 %collective-permute-start.23 = (bf16[1,192,512]{2,1,0:T(8,128)(2,1)S(1)}, bf16[1,192,512]{2,1,0:T(8,128)(2,1)S(1)}, u32[]{:S(2)}, u32[]{:S(2)}) collective-permute-start(bf16[1,192,512]{2,1,0:T(8,128)(2,1)S(1)} %ahead_back_1.1.refs_1_), channel_id=1, source_target_pairs={{0,2},{1,3},{2,0},{3,1},{4,6},{5,7},{6,4},{7,5},{8,10},{9,11},{10,... | collective-permute-start | bytes 589832 | tf_op jit(solution)/shard_map/ppermute | solution.py:269
  95.4 1.9 %behind_out_0.1 = (bf16[192,896]{1,0:T(8,128)(2,1)S(1)}, bf16[192,896]{1,0:T(8,128)(2,1)S(1)}) custom-call(bf16[2,192,512]{2,1,0:T(8,128)(2,1)S(1)} %behind_act_0.1.refs_0_.refs_3_, bf16[2,192,512]{2,1,0:T(8,128)(2,1)S(1)} %behind_first_0.1.refs_1_, bf16[2,192,512]{2,1,0:T(8,128)(2,1)S(1)} %collective-permute-done.22.refs_1_.refs_2_, ...), custom_call_target="tpu_custom_call" | custom-call | flops 60000002048 | bytes 1024 | tf_op jit(solution)/shard_map/behind_out_0/pallas_call | solution.py:43
  97.9 5.1 %collective-permute-start.31 = (bf16[2,192,512]{2,1,0:T(8,128)(2,1)S(1)}, bf16[2,192,512]{2,1,0:T(8,128)(2,1)S(1)}, u32[]{:S(2)}, u32[]{:S(2)}) collective-permute-start(bf16[2,192,512]{2,1,0:T(8,128)(2,1)S(1)} %behind_back_2.1.refs_1_), channel_id=1, source_target_pairs={{0,2},{1,3},{2,0},{3,1},{4,6},{5,7},{6,4},{7,5},{8,10},{9,11},{10,... | collective-permute-start | bytes 1179656 | tf_op jit(solution)/shard_map/ppermute | solution.py:269
  104.0 11.2 %collective-permute-start.28 = (bf16[192,896]{1,0:T(8,128)(2,1)}, bf16[192,896]{1,0:T(8,128)(2,1)}, u32[]{:S(2)}, u32[]{:S(2)}) collective-permute-start(bf16[192,896]{1,0:T(8,128)(2,1)} %ahead_shares.1.refs_5_), channel_id=1, source_target_pairs={{0,8},{1,9},{2,10},{3,11},{4,12},{5,13},{6,14},{7,15},{8,16},{9,17... | collective-permute-start | bytes 1032200 | tf_op jit(solution)/shard_map/ppermute | solution.py:293
  115.2 1.9 %behind_out_1.1 = (bf16[192,896]{1,0:T(8,128)(2,1)S(1)}, bf16[192,896]{1,0:T(8,128)(2,1)S(1)}) custom-call(bf16[2,192,512]{2,1,0:T(8,128)(2,1)S(1)} %behind_act_1.1.refs_0_.refs_2_, bf16[2,192,512]{2,1,0:T(8,128)(2,1)S(1)} %behind_first_1.1.refs_1_, bf16[2,192,512]{2,1,0:T(8,128)(2,1)S(1)} %collective-permute-done.27.refs_0_.refs_2_, ...), custom_call_target="tpu_custom_call" | custom-call | flops 60000002048 | bytes 1024 | tf_op jit(solution)/shard_map/behind_out_1/pallas_call | solution.py:43
  117.1 4.8 %collective-permute-start.35 = (bf16[192,896]{1,0:T(8,128)(2,1)S(1)}, bf16[192,896]{1,0:T(8,128)(2,1)S(1)}, u32[]{:S(2)}, u32[]{:S(2)}) collective-permute-start(bf16[192,896]{1,0:T(8,128)(2,1)S(1)} %get-tuple-element.14.refs_2_), channel_id=1, source_target_pairs={{8,1},{9,0},{10,3},{11,2},{12,5},{13,4},{14,7},{15,6},{16,9},{17,8... | collective-permute-start | bytes 1032200 | tf_op jit(solution)/shard_map/ppermute | solution.py:293
  122.0 1.9 %collective-permute-start.34 = (bf16[192,896]{1,0:T(8,128)(2,1)S(1)}, bf16[192,896]{1,0:T(8,128)(2,1)S(1)}, u32[]{:S(2)}, u32[]{:S(2)}) collective-permute-start(bf16[192,896]{1,0:T(8,128)(2,1)S(1)} %behind_shares.1.refs_6_), channel_id=1, source_target_pairs={{8,0},{9,1},{10,2},{11,3},{12,4},{13,5},{14,6},{15,7},{16,8},{17,9... | collective-permute-start | bytes 1032200 | tf_op jit(solution)/shard_map/ppermute | solution.py:293
  124.0 1.9 %collective-permute-start.36 = (bf16[192,896]{1,0:T(8,128)(2,1)S(1)}, bf16[192,896]{1,0:T(8,128)(2,1)S(1)}, u32[]{:S(2)}, u32[]{:S(2)}) collective-permute-start(bf16[192,896]{1,0:T(8,128)(2,1)S(1)} %get-tuple-element.17), channel_id=1, source_target_pairs={{8,0},{9,1},{10,2},{11,3},{12,4},{13,5},{14,6},{15,7},{16,8},{17,9... | collective-permute-start | bytes 1032200 | tf_op jit(solution)/shard_map/ppermute | solution.py:293
  127.5 3.5 %collective-permute-start.32 = (bf16[192,896]{1,0:T(8,128)(2,1)S(1)}, bf16[192,896]{1,0:T(8,128)(2,1)S(1)}, u32[]{:S(2)}, u32[]{:S(2)}) collective-permute-start(bf16[192,896]{1,0:T(8,128)(2,1)S(1)} %get-tuple-element.15.refs_3_), channel_id=1, source_target_pairs={{0,9},{1,8},{2,11},{3,10},{4,13},{5,12},{6,15},{7,14},{8,17},{9,16... | collective-permute-start | bytes 1032200 | tf_op jit(solution)/shard_map/ppermute | solution.py:293
  131.0 2.6 %collective-permute-start.33 = (bf16[192,896]{1,0:T(8,128)(2,1)S(1)}, bf16[192,896]{1,0:T(8,128)(2,1)S(1)}, u32[]{:S(2)}, u32[]{:S(2)}) collective-permute-start(bf16[192,896]{1,0:T(8,128)(2,1)S(1)} %get-tuple-element.16), channel_id=1, source_target_pairs={{0,8},{1,9},{2,10},{3,11},{4,12},{5,13},{6,14},{7,15},{8,16},{9,17... | collective-permute-start | bytes 1032200 | tf_op jit(solution)/shard_map/ppermute | solution.py:293
  136.0 2.9 %collective-permute-done.33.refs_2_ = bf16[192,896]{1,0:T(8,128)(2,1)S(1)} collective-permute-done((bf16[192,896]{1,0:T(8,128)(2,1)S(1)}, bf16[192,896]{1,0:T(8,128)(2,1)S(1)}, u32[]{:S(2)}, u32[]{:S(2)}) %collective-permute-start.33) | collective-permute-done | bytes 344096 | tf_op jit(solution)/shard_map/ppermute | solution.py:293
  140.0 1.9 %ahead_result.1 = bf16[384,896]{1,0:T(8,128)(2,1)} custom-call(bf16[192,896]{1,0:T(8,128)(2,1)} %collective-permute-done.28.refs_0_, bf16[192,896]{1,0:T(8,128)(2,1)S(1)} %collective-permute-done.32.refs_1_, bf16[192,896]{1,0:T(8,128)(2,1)S(1)} %collective-permute-done.33.refs_2_, bf16[384,896]{1,0:T(8,128)(2,1)S(1)} %copy-done.7), custom_call_target="tpu_custom_call" | custom-call | flops 60000002048 | bytes 1024 | tf_op jit(solution)/shard_map/ahead_result/pallas_call | solution.py:43
  (132 shorter events, 51.7 us)
Async XLA Ops:
  1.6 9.9 %collective-permute-start.1 = (bf16[192,896]{1,0:T(8,128)(2,1)S(1)}, bf16[192,896]{1,0:T(8,128)(2,1)S(1)}, u32[]{:S(2)}, u32[]{:S(2)}) collective-permute-start(bf16[192,896]{1,0:T(8,128)(2,1)S(1)} %slice_bitcast_fusion.refs_0_), channel_id=1, source_target_pairs={{0,1},{1,0},{2,3},{3,2},{4,5},{5,4},{6,7},{7,6},{8,9},{9,8},{10,11... | collective-permute-start | bytes 1032200 | tf_op jit(solution)/shard_map/ppermute | solution.py:284
  4.9 14.0 %collective-permute-start = (bf16[192,896]{1,0:T(8,128)(2,1)S(1)}, bf16[192,896]{1,0:T(8,128)(2,1)S(1)}, u32[]{:S(2)}, u32[]{:S(2)}) collective-permute-start(bf16[192,896]{1,0:T(8,128)(2,1)S(1)} %ahead_rows_0.1.refs_1_.refs_0_), channel_id=1, source_target_pairs={{0,1},{1,0},{2,3},{3,2},{4,5},{5,4},{6,7},{7,6},{8,9},{9,8},{10,11... | collective-permute-start | bytes 1032200 | tf_op jit(solution)/shard_map/ppermute | solution.py:284
  6.0 20.3 %collective-permute-start.3 = (bf16[192,896]{1,0:T(8,128)(2,1)S(1)}, bf16[192,896]{1,0:T(8,128)(2,1)S(1)}, u32[]{:S(2)}, u32[]{:S(2)}) collective-permute-start(bf16[192,896]{1,0:T(8,128)(2,1)S(1)} %grad_rows_0.1.refs_3_.refs_0_), channel_id=1, source_target_pairs={{0,1},{1,0},{2,3},{3,2},{4,5},{5,4},{6,7},{7,6},{8,9},{9,8},{10,11... | collective-permute-start | bytes 1032200 | tf_op jit(solution)/shard_map/ppermute | solution.py:284
  16.0 12.4 %collective-permute-start.2 = (bf16[2,192,512]{2,1,0:T(8,128)(2,1)S(1)}, bf16[2,192,512]{2,1,0:T(8,128)(2,1)S(1)}, u32[]{:S(2)}, u32[]{:S(2)}) collective-permute-start(bf16[2,192,512]{2,1,0:T(8,128)(2,1)S(1)} %behind_far_0.1.refs_1_.refs_0_), channel_id=1, source_target_pairs={{0,2},{1,3},{2,0},{3,1},{4,6},{5,7},{6,4},{7,5},{8,10},{9,11},{10,... | collective-permute-start | bytes 1179656 | tf_op jit(solution)/shard_map/ppermute | solution.py:269
  17.3 16.4 %collective-permute-start.6 = (bf16[192,896]{1,0:T(8,128)(2,1)S(1)}, bf16[192,896]{1,0:T(8,128)(2,1)S(1)}, u32[]{:S(2)}, u32[]{:S(2)}) collective-permute-start(bf16[192,896]{1,0:T(8,128)(2,1)S(1)} %behind_rows_1.1.refs_3_.refs_0_.refs_2_), channel_id=1, source_target_pairs={{0,1},{1,0},{2,3},{3,2},{4,5},{5,4},{6,7},{7,6},{8,9},{9,8},{10,11... | collective-permute-start | bytes 1032200 | tf_op jit(solution)/shard_map/ppermute | solution.py:284
  21.7 15.0 %collective-permute-start.8 = (bf16[2,192,512]{2,1,0:T(8,128)(2,1)S(1)}, bf16[2,192,512]{2,1,0:T(8,128)(2,1)S(1)}, u32[]{:S(2)}, u32[]{:S(2)}) collective-permute-start(bf16[2,192,512]{2,1,0:T(8,128)(2,1)S(1)} %ahead_far_0.1.refs_3_.refs_0_), channel_id=1, source_target_pairs={{0,2},{1,3},{2,0},{3,1},{4,6},{5,7},{6,4},{7,5},{8,10},{9,11},{10,... | collective-permute-start | bytes 1179656 | tf_op jit(solution)/shard_map/ppermute | solution.py:269
  27.1 15.6 %collective-permute-start.5 = (bf16[1,192,512]{2,1,0:T(8,128)(2,1)S(1)}, bf16[1,192,512]{2,1,0:T(8,128)(2,1)S(1)}, u32[]{:S(2)}, u32[]{:S(2)}) collective-permute-start(bf16[1,192,512]{2,1,0:T(8,128)(2,1)S(1)} %grad_far_0.1.refs_2_.refs_0_), channel_id=1, source_target_pairs={{0,2},{1,3},{2,0},{3,1},{4,6},{5,7},{6,4},{7,5},{8,10},{9,11},{10,... | collective-permute-start | bytes 589832 | tf_op jit(solution)/shard_map/ppermute | solution.py:269
  28.4 9.0 %collective-permute-start.7 = (bf16[2,192,512]{2,1,0:T(8,128)(2,1)S(1)}, bf16[2,192,512]{2,1,0:T(8,128)(2,1)S(1)}, u32[]{:S(2)}, u32[]{:S(2)}) collective-permute-start(bf16[2,192,512]{2,1,0:T(8,128)(2,1)S(1)} %behind_middle_0.1.refs_1_), channel_id=1, source_target_pairs={{0,0},{1,1},{2,4},{3,5},{4,2},{5,3},{6,6},{7,7},{8,8},{9,9},{10,12... | collective-permute-start | bytes 1179656 | tf_op jit(solution)/shard_map/ppermute | solution.py:269
  29.2 14.2 %collective-permute-start.4 = (bf16[192,896]{1,0:T(8,128)(2,1)S(1)}, bf16[192,896]{1,0:T(8,128)(2,1)S(1)}, u32[]{:S(2)}, u32[]{:S(2)}) collective-permute-start(bf16[192,896]{1,0:T(8,128)(2,1)S(1)} %ahead_rows_1.1.refs_3_.refs_0_.refs_2_), channel_id=1, source_target_pairs={{0,1},{1,0},{2,3},{3,2},{4,5},{5,4},{6,7},{7,6},{8,9},{9,8},{10,11... | collective-permute-start | bytes 1032200 | tf_op jit(solution)/shard_map/ppermute | solution.py:284
  36.8 9.6 %collective-permute-start.9 = (bf16[2,192,512]{2,1,0:T(8,128)(2,1)S(1)}, bf16[2,192,512]{2,1,0:T(8,128)(2,1)S(1)}, u32[]{:S(2)}, u32[]{:S(2)}) collective-permute-start(bf16[2,192,512]{2,1,0:T(8,128)(2,1)S(1)} %ahead_middle_0.1.refs_3_), channel_id=1, source_target_pairs={{0,0},{1,1},{2,4},{3,5},{4,2},{5,3},{6,6},{7,7},{8,8},{9,9},{10,12... | collective-permute-start | bytes 1179656 | tf_op jit(solution)/shard_map/ppermute | solution.py:269
  37.6 10.5 %collective-permute-start.12 = (bf16[2,192,512]{2,1,0:T(8,128)(2,1)S(1)}, bf16[2,192,512]{2,1,0:T(8,128)(2,1)S(1)}, u32[]{:S(2)}, u32[]{:S(2)}) collective-permute-start(bf16[2,192,512]{2,1,0:T(8,128)(2,1)S(1)} %behind_outer_1.1.refs_1_), channel_id=1, source_target_pairs={{0,2},{1,3},{2,0},{3,1},{4,6},{5,7},{6,4},{7,5},{8,10},{9,11},{10,... | collective-permute-start | bytes 1179656 | tf_op jit(solution)/shard_map/ppermute | solution.py:269
  48.2 11.7 %collective-permute-start.15 = (bf16[2,192,512]{2,1,0:T(8,128)(2,1)S(1)}, bf16[2,192,512]{2,1,0:T(8,128)(2,1)S(1)}, u32[]{:S(2)}, u32[]{:S(2)}) collective-permute-start(bf16[2,192,512]{2,1,0:T(8,128)(2,1)S(1)} %behind_middle_1.1.refs_3_), channel_id=1, source_target_pairs={{0,0},{1,1},{2,4},{3,5},{4,2},{5,3},{6,6},{7,7},{8,8},{9,9},{10,12... | collective-permute-start | bytes 1179656 | tf_op jit(solution)/shard_map/ppermute | solution.py:269
  60.0 12.1 %collective-permute-start.18 = (bf16[2,192,512]{2,1,0:T(8,128)(2,1)S(1)}, bf16[2,192,512]{2,1,0:T(8,128)(2,1)S(1)}, u32[]{:S(2)}, u32[]{:S(2)}) collective-permute-start(bf16[2,192,512]{2,1,0:T(8,128)(2,1)S(1)} %behind_outer_2.1.refs_2_), channel_id=1, source_target_pairs={{0,2},{1,3},{2,0},{3,1},{4,6},{5,7},{6,4},{7,5},{8,10},{9,11},{10,... | collective-permute-start | bytes 1179656 | tf_op jit(solution)/shard_map/ppermute | solution.py:269
  62.2 15.3 %collective-permute-start.17 = (bf16[2,192,512]{2,1,0:T(8,128)(2,1)S(1)}, bf16[2,192,512]{2,1,0:T(8,128)(2,1)S(1)}, u32[]{:S(2)}, u32[]{:S(2)}) collective-permute-start(bf16[2,192,512]{2,1,0:T(8,128)(2,1)S(1)} %ahead_outer_2.1.refs_2_), channel_id=1, source_target_pairs={{0,2},{1,3},{2,0},{3,1},{4,6},{5,7},{6,4},{7,5},{8,10},{9,11},{10,... | collective-permute-start | bytes 1179656 | tf_op jit(solution)/shard_map/ppermute | solution.py:269
  68.2 13.6 %collective-permute-start.21 = (bf16[1,192,512]{2,1,0:T(8,128)(2,1)S(1)}, bf16[1,192,512]{2,1,0:T(8,128)(2,1)S(1)}, u32[]{:S(2)}, u32[]{:S(2)}) collective-permute-start(bf16[1,192,512]{2,1,0:T(8,128)(2,1)S(1)} %grad_third_1.1.refs_1_), channel_id=1, source_target_pairs={{0,2},{1,3},{2,0},{3,1},{4,6},{5,7},{6,4},{7,5},{8,10},{9,11},{10,... | collective-permute-start | bytes 589832 | tf_op jit(solution)/shard_map/ppermute | solution.py:269
  72.1 9.9 %collective-permute-start.22 = (bf16[2,192,512]{2,1,0:T(8,128)(2,1)S(1)}, bf16[2,192,512]{2,1,0:T(8,128)(2,1)S(1)}, u32[]{:S(2)}, u32[]{:S(2)}) collective-permute-start(bf16[2,192,512]{2,1,0:T(8,128)(2,1)S(1)} %behind_first_0.1.refs_1_), channel_id=1, source_target_pairs={{0,0},{1,1},{2,4},{3,5},{4,2},{5,3},{6,6},{7,7},{8,8},{9,9},{10,12... | collective-permute-start | bytes 1179656 | tf_op jit(solution)/shard_map/ppermute | solution.py:269
  91.6 11.5 %collective-permute-start.26 = (bf16[1,192,512]{2,1,0:T(8,128)(2,1)S(1)}, bf16[1,192,512]{2,1,0:T(8,128)(2,1)S(1)}, u32[]{:S(2)}, u32[]{:S(2)}) collective-permute-start(bf16[1,192,512]{2,1,0:T(8,128)(2,1)S(1)} %ahead_first_1.1.refs_6_.refs_1_), channel_id=1, source_target_pairs={{0,0},{1,1},{2,4},{3,5},{4,2},{5,3},{6,6},{7,7},{8,8},{9,9},{10,12... | collective-permute-start | bytes 589832 | tf_op jit(solution)/shard_map/ppermute | solution.py:269
  94.1 9.1 %collective-permute-start.25 = (bf16[192,896]{1,0:T(8,128)(2,1)S(1)}, bf16[192,896]{1,0:T(8,128)(2,1)S(1)}, u32[]{:S(2)}, u32[]{:S(2)}) collective-permute-start(bf16[192,896]{1,0:T(8,128)(2,1)S(1)} %get-tuple-element.11.refs_5_), channel_id=1, source_target_pairs={{0,1},{1,0},{2,3},{3,2},{4,5},{5,4},{6,7},{7,6},{8,9},{9,8},{10,11... | collective-permute-start | bytes 1032200 | tf_op jit(solution)/shard_map/ppermute | solution.py:284
  97.3 24.6 %collective-permute-start.30 = (bf16[192,896]{1,0:T(8,128)(2,1)S(1)}, bf16[192,896]{1,0:T(8,128)(2,1)S(1)}, u32[]{:S(2)}, u32[]{:S(2)}) collective-permute-start(bf16[192,896]{1,0:T(8,128)(2,1)S(1)} %get-tuple-element.12.refs_1_), channel_id=1, source_target_pairs={{0,1},{1,0},{2,3},{3,2},{4,5},{5,4},{6,7},{7,6},{8,9},{9,8},{10,11... | collective-permute-start | bytes 1032200 | tf_op jit(solution)/shard_map/ppermute | solution.py:284
  97.9 17.2 %collective-permute-start.31 = (bf16[2,192,512]{2,1,0:T(8,128)(2,1)S(1)}, bf16[2,192,512]{2,1,0:T(8,128)(2,1)S(1)}, u32[]{:S(2)}, u32[]{:S(2)}) collective-permute-start(bf16[2,192,512]{2,1,0:T(8,128)(2,1)S(1)} %behind_back_2.1.refs_1_), channel_id=1, source_target_pairs={{0,2},{1,3},{2,0},{3,1},{4,6},{5,7},{6,4},{7,5},{8,10},{9,11},{10,... | collective-permute-start | bytes 1179656 | tf_op jit(solution)/shard_map/ppermute | solution.py:269
  103.1 22.8 %collective-permute-start.29 = (bf16[1,192,512]{2,1,0:T(8,128)(2,1)S(1)}, bf16[1,192,512]{2,1,0:T(8,128)(2,1)S(1)}, u32[]{:S(2)}, u32[]{:S(2)}) collective-permute-start(bf16[1,192,512]{2,1,0:T(8,128)(2,1)S(1)} %ahead_back_2.1.refs_2_), channel_id=1, source_target_pairs={{0,2},{1,3},{2,0},{3,1},{4,6},{5,7},{6,4},{7,5},{8,10},{9,11},{10,... | collective-permute-start | bytes 589832 | tf_op jit(solution)/shard_map/ppermute | solution.py:269
  104.0 31.3 %collective-permute-start.28 = (bf16[192,896]{1,0:T(8,128)(2,1)}, bf16[192,896]{1,0:T(8,128)(2,1)}, u32[]{:S(2)}, u32[]{:S(2)}) collective-permute-start(bf16[192,896]{1,0:T(8,128)(2,1)} %ahead_shares.1.refs_5_), channel_id=1, source_target_pairs={{0,8},{1,9},{2,10},{3,11},{4,12},{5,13},{6,14},{7,15},{8,16},{9,17... | collective-permute-start | bytes 1032200 | tf_op jit(solution)/shard_map/ppermute | solution.py:293
  117.1 16.5 %collective-permute-start.35 = (bf16[192,896]{1,0:T(8,128)(2,1)S(1)}, bf16[192,896]{1,0:T(8,128)(2,1)S(1)}, u32[]{:S(2)}, u32[]{:S(2)}) collective-permute-start(bf16[192,896]{1,0:T(8,128)(2,1)S(1)} %get-tuple-element.14.refs_2_), channel_id=1, source_target_pairs={{8,1},{9,0},{10,3},{11,2},{12,5},{13,4},{14,7},{15,6},{16,9},{17,8... | collective-permute-start | bytes 1032200 | tf_op jit(solution)/shard_map/ppermute | solution.py:293
  124.0 10.3 %collective-permute-start.36 = (bf16[192,896]{1,0:T(8,128)(2,1)S(1)}, bf16[192,896]{1,0:T(8,128)(2,1)S(1)}, u32[]{:S(2)}, u32[]{:S(2)}) collective-permute-start(bf16[192,896]{1,0:T(8,128)(2,1)S(1)} %get-tuple-element.17), channel_id=1, source_target_pairs={{8,0},{9,1},{10,2},{11,3},{12,4},{13,5},{14,6},{15,7},{16,8},{17,9... | collective-permute-start | bytes 1032200 | tf_op jit(solution)/shard_map/ppermute | solution.py:293
  (27 other events, 143.7 us)

commit v23 on v20

--- a/solution.py
+++ b/solution.py
@@ -460,6 +460,7 @@
     behind.far_product(0)
     behind.first_hop(0)
     behind.fetch(1)
+    recent.append(behind.out[0])
     ahead.far_product(0)
     ahead.first_hop(0)
     grad.far_product(0)

time: 142 us -> 142 us (level)
    ppermute x23, waiting for transfers between devices: 17.8 us -> 23.4 us  [between(): return lax.ppermute(value, 'expert', pairs)]
    ppermute x8, waiting for transfers between devices: 12.1 us -> 7.8 us  [swapped(): return lax.ppermute(value, 'expert', [(i, i ^ 1) for i in range(devices)])]
where the time goes in v23:
time: 142 us; the launch traced here: 141 us
  starting transfers between devices  73.7 us (52%)
  waiting for transfers between devices  36.2 us (25%)
  Pallas kernels  22 us (15%)
  local copies, waits for them, and re-layouts  7.98 us (6%)
    ppermute x23, starting transfers between devices, between(): return lax.ppermute(value, 'expert', pairs)  39.3 us
    ppermute x6, starting transfers between devices, to_section(): return lax.ppermute(value, ('section', 'expert'), pairs)  26.2 us
    ppermute x23, waiting for transfers between devices, between(): return lax.ppermute(value, 'expert', pairs)  23.4 us
    pallas_call x46, Pallas kernels, call(): pl.pallas_call(run, compiler_params=pltpu.CompilerParams(vmem_limit_bytes...  22 us
    ppermute x8, starting transfers between devices, swapped(): return lax.ppermute(value, 'expert', [(i, i ^ 1) for i in range(devices)])  8.2 us
    ppermute x8, waiting for transfers between devices, swapped(): return lax.ppermute(value, 'expert', [(i, i ^ 1) for i in range(devices)])  7.8 us
    unnamed x20, local copies, waits for them, and re-layouts  6.41 us
    ppermute x6, waiting for transfers between devices, to_section(): return lax.ppermute(value, ('section', 'expert'), pairs)  5 us
  transfers between devices with their start and end apart: 37, of which 12 were waited for; matrix products, arithmetic and copies ran while one was open for 0% of the time, Pallas kernels for 15%

profile of v23, /device:TPU:1, one launch (start us, length us, event | category | flops | bytes accessed | tf_op | source)
XLA Modules:
  0.0 141.2 jit_solution(18045108957107148899)
XLA Ops:
  1.6 2.1 %collective-permute-start.1 = (bf16[192,896]{1,0:T(8,128)(2,1)S(1)}, bf16[192,896]{1,0:T(8,128)(2,1)S(1)}, u32[]{:S(2)}, u32[]{:S(2)}) collective-permute-start(bf16[192,896]{1,0:T(8,128)(2,1)S(1)} %slice_bitcast_fusion.refs_0_), channel_id=1, source_target_pairs={{0,1},{1,0},{2,3},{3,2},{4,5},{5,4},{6,7},{7,6},{8,9},{9,8},{10,11... | collective-permute-start | bytes 1032200 | tf_op jit(solution)/shard_map/ppermute | solution.py:284
  7.3 4.2 %collective-permute-done.1.refs_1_ = bf16[192,896]{1,0:T(8,128)(2,1)S(1)} collective-permute-done((bf16[192,896]{1,0:T(8,128)(2,1)S(1)}, bf16[192,896]{1,0:T(8,128)(2,1)S(1)}, u32[]{:S(2)}, u32[]{:S(2)}) %collective-permute-start.1) | collective-permute-done | bytes 344096 | tf_op jit(solution)/shard_map/ppermute | solution.py:284
  11.6 3.1 %copy-done.1 = bf16[1,1,2,1024,1792]{4,3,2,1,0:T(8,128)(2,1)S(1)} copy-done((bf16[1,1,2,1024,1792]{4,3,2,1,0:T(8,128)(2,1)S(1)}, bf16[1,1,2,1024,1792]{4,3,2,1,0:T(8,128)(2,1)}, u32[]{:S(2)}) %copy-start.1) | copy-done | bytes 7340056
  18.9 5.5 %collective-permute-done.2.refs_4_.refs_1_ = bf16[2,192,512]{2,1,0:T(8,128)(2,1)S(1)} collective-permute-done((bf16[2,192,512]{2,1,0:T(8,128)(2,1)S(1)}, bf16[2,192,512]{2,1,0:T(8,128)(2,1)S(1)}, u32[]{:S(2)}, u32[]{:S(2)}) %collective-permute-start.2) | collective-permute-done | bytes 393248 | tf_op jit(solution)/shard_map/ppermute | solution.py:269
  30.5 3.2 %collective-permute-done.6.refs_1_.refs_3_ = bf16[192,896]{1,0:T(8,128)(2,1)S(1)} collective-permute-done((bf16[192,896]{1,0:T(8,128)(2,1)S(1)}, bf16[192,896]{1,0:T(8,128)(2,1)S(1)}, u32[]{:S(2)}, u32[]{:S(2)}) %collective-permute-start.6) | collective-permute-done | bytes 344096 | tf_op jit(solution)/shard_map/ppermute | solution.py:284
  37.6 3.8 %collective-permute-start.11 = (bf16[2,192,512]{2,1,0:T(8,128)(2,1)S(1)}, bf16[2,192,512]{2,1,0:T(8,128)(2,1)S(1)}, u32[]{:S(2)}, u32[]{:S(2)}) collective-permute-start(bf16[2,192,512]{2,1,0:T(8,128)(2,1)S(1)} %behind_outer_1.1.refs_1_), channel_id=1, source_target_pairs={{0,2},{1,3},{2,0},{3,1},{4,6},{5,7},{6,4},{7,5},{8,10},{9,11},{10,... | collective-permute-start | bytes 1179656 | tf_op jit(solution)/shard_map/ppermute | solution.py:269
  50.6 2.9 %collective-permute-start.14 = (bf16[1,192,512]{2,1,0:T(8,128)(2,1)S(1)}, bf16[1,192,512]{2,1,0:T(8,128)(2,1)S(1)}, u32[]{:S(2)}, u32[]{:S(2)}) collective-permute-start(bf16[1,192,512]{2,1,0:T(8,128)(2,1)S(1)} %grad_outer_1.1.refs_2_), channel_id=1, source_target_pairs={{0,2},{1,3},{2,0},{3,1},{4,6},{5,7},{6,4},{7,5},{8,10},{9,11},{10,... | collective-permute-start | bytes 589832 | tf_op jit(solution)/shard_map/ppermute | solution.py:269
  56.2 3.4 %collective-permute-done.14.refs_1_.refs_3_ = bf16[1,192,512]{2,1,0:T(8,128)(2,1)S(1)} collective-permute-done((bf16[1,192,512]{2,1,0:T(8,128)(2,1)S(1)}, bf16[1,192,512]{2,1,0:T(8,128)(2,1)S(1)}, u32[]{:S(2)}, u32[]{:S(2)}) %collective-permute-start.14) | collective-permute-done | bytes 196640 | tf_op jit(solution)/shard_map/ppermute | solution.py:269
  60.7 2.6 %collective-permute-start.18 = (bf16[2,192,512]{2,1,0:T(8,128)(2,1)S(1)}, bf16[2,192,512]{2,1,0:T(8,128)(2,1)S(1)}, u32[]{:S(2)}, u32[]{:S(2)}) collective-permute-start(bf16[2,192,512]{2,1,0:T(8,128)(2,1)S(1)} %behind_outer_2.1.refs_2_), channel_id=1, source_target_pairs={{0,2},{1,3},{2,0},{3,1},{4,6},{5,7},{6,4},{7,5},{8,10},{9,11},{10,... | collective-permute-start | bytes 1179656 | tf_op jit(solution)/shard_map/ppermute | solution.py:269
  63.5 4.7 %collective-permute-start.17 = (bf16[2,192,512]{2,1,0:T(8,128)(2,1)S(1)}, bf16[2,192,512]{2,1,0:T(8,128)(2,1)S(1)}, u32[]{:S(2)}, u32[]{:S(2)}) collective-permute-start(bf16[2,192,512]{2,1,0:T(8,128)(2,1)S(1)} %ahead_outer_2.1.refs_2_), channel_id=1, source_target_pairs={{0,2},{1,3},{2,0},{3,1},{4,6},{5,7},{6,4},{7,5},{8,10},{9,11},{10,... | collective-permute-start | bytes 1179656 | tf_op jit(solution)/shard_map/ppermute | solution.py:269
  68.2 3.9 %collective-permute-start.21 = (bf16[1,192,512]{2,1,0:T(8,128)(2,1)S(1)}, bf16[1,192,512]{2,1,0:T(8,128)(2,1)S(1)}, u32[]{:S(2)}, u32[]{:S(2)}) collective-permute-start(bf16[1,192,512]{2,1,0:T(8,128)(2,1)S(1)} %grad_third_1.1.refs_1_), channel_id=1, source_target_pairs={{0,2},{1,3},{2,0},{3,1},{4,6},{5,7},{6,4},{7,5},{8,10},{9,11},{10,... | collective-permute-start | bytes 589832 | tf_op jit(solution)/shard_map/ppermute | solution.py:269
  72.9 2.9 %collective-permute-done.17.refs_0_.refs_1_ = bf16[2,192,512]{2,1,0:T(8,128)(2,1)S(1)} collective-permute-done((bf16[2,192,512]{2,1,0:T(8,128)(2,1)S(1)}, bf16[2,192,512]{2,1,0:T(8,128)(2,1)S(1)}, u32[]{:S(2)}, u32[]{:S(2)}) %collective-permute-start.17) | collective-permute-done | bytes 393248 | tf_op jit(solution)/shard_map/ppermute | solution.py:269
  76.6 3.4 %collective-permute-done.21.refs_3_ = bf16[1,192,512]{2,1,0:T(8,128)(2,1)S(1)} collective-permute-done((bf16[1,192,512]{2,1,0:T(8,128)(2,1)S(1)}, bf16[1,192,512]{2,1,0:T(8,128)(2,1)S(1)}, u32[]{:S(2)}, u32[]{:S(2)}) %collective-permute-start.21) | collective-permute-done | bytes 196640 | tf_op jit(solution)/shard_map/ppermute | solution.py:269
  80.3 2.1 %collective-permute-start.24 = (bf16[2,192,512]{2,1,0:T(8,128)(2,1)S(1)}, bf16[2,192,512]{2,1,0:T(8,128)(2,1)S(1)}, u32[]{:S(2)}, u32[]{:S(2)}) collective-permute-start(bf16[2,192,512]{2,1,0:T(8,128)(2,1)S(1)} %behind_back_1.1.refs_2_), channel_id=1, source_target_pairs={{0,2},{1,3},{2,0},{3,1},{4,6},{5,7},{6,4},{7,5},{8,10},{9,11},{10,... | collective-permute-start | bytes 1179656 | tf_op jit(solution)/shard_map/ppermute | solution.py:269
  82.4 2.8 %collective-permute-start.23 = (bf16[1,192,512]{2,1,0:T(8,128)(2,1)S(1)}, bf16[1,192,512]{2,1,0:T(8,128)(2,1)S(1)}, u32[]{:S(2)}, u32[]{:S(2)}) collective-permute-start(bf16[1,192,512]{2,1,0:T(8,128)(2,1)S(1)} %ahead_back_1.1.refs_1_), channel_id=1, source_target_pairs={{0,2},{1,3},{2,0},{3,1},{4,6},{5,7},{6,4},{7,5},{8,10},{9,11},{10,... | collective-permute-start | bytes 589832 | tf_op jit(solution)/shard_map/ppermute | solution.py:269
  85.2 5.0 %collective-permute-done.24.refs_0_.refs_3_ = bf16[2,192,512]{2,1,0:T(8,128)(2,1)S(1)} collective-permute-done((bf16[2,192,512]{2,1,0:T(8,128)(2,1)S(1)}, bf16[2,192,512]{2,1,0:T(8,128)(2,1)S(1)}, u32[]{:S(2)}, u32[]{:S(2)}) %collective-permute-start.24) | collective-permute-done | bytes 393248 | tf_op jit(solution)/shard_map/ppermute | solution.py:269
  93.0 2.1 %behind_out_0.1 = (bf16[192,896]{1,0:T(8,128)(2,1)S(1)}, bf16[192,896]{1,0:T(8,128)(2,1)S(1)}) custom-call(bf16[2,192,512]{2,1,0:T(8,128)(2,1)S(1)} %behind_act_0.1.refs_0_.refs_3_, bf16[2,192,512]{2,1,0:T(8,128)(2,1)S(1)} %behind_first_0.1.refs_1_, bf16[2,192,512]{2,1,0:T(8,128)(2,1)S(1)} %collective-permute-done.22.refs_1_.refs_2_, ...), custom_call_target="tpu_custom_call" | custom-call | flops 20000000000 | bytes 1024 | tf_op jit(solution)/shard_map/behind_out_0/pallas_call | solution.py:43
  98.2 4.9 %collective-permute-start.27 = (bf16[2,192,512]{2,1,0:T(8,128)(2,1)S(1)}, bf16[2,192,512]{2,1,0:T(8,128)(2,1)S(1)}, u32[]{:S(2)}, u32[]{:S(2)}) collective-permute-start(bf16[2,192,512]{2,1,0:T(8,128)(2,1)S(1)} %behind_back_2.1.refs_1_), channel_id=1, source_target_pairs={{0,2},{1,3},{2,0},{3,1},{4,6},{5,7},{6,4},{7,5},{8,10},{9,11},{10,... | collective-permute-start | bytes 1179656 | tf_op jit(solution)/shard_map/ppermute | solution.py:269
  103.3 10.2 %collective-permute-start.34 = (bf16[192,896]{1,0:T(8,128)(2,1)S(1)}, bf16[192,896]{1,0:T(8,128)(2,1)S(1)}, u32[]{:S(2)}, u32[]{:S(2)}) collective-permute-start(bf16[192,896]{1,0:T(8,128)(2,1)S(1)} %behind_shares.1.refs_5_), channel_id=1, source_target_pairs={{8,0},{9,1},{10,2},{11,3},{12,4},{13,5},{14,6},{15,7},{16,8},{17,9... | collective-permute-start | bytes 1032200 | tf_op jit(solution)/shard_map/ppermute | solution.py:293
  115.5 6.3 %collective-permute-start.35 = (bf16[192,896]{1,0:T(8,128)(2,1)S(1)}, bf16[192,896]{1,0:T(8,128)(2,1)S(1)}, u32[]{:S(2)}, u32[]{:S(2)}) collective-permute-start(bf16[192,896]{1,0:T(8,128)(2,1)S(1)} %get-tuple-element.14.refs_2_), channel_id=1, source_target_pairs={{8,1},{9,0},{10,3},{11,2},{12,5},{13,4},{14,7},{15,6},{16,9},{17,8... | collective-permute-start | bytes 1032200 | tf_op jit(solution)/shard_map/ppermute | solution.py:293
  121.8 1.9 %collective-permute-start.36 = (bf16[192,896]{1,0:T(8,128)(2,1)S(1)}, bf16[192,896]{1,0:T(8,128)(2,1)S(1)}, u32[]{:S(2)}, u32[]{:S(2)}) collective-permute-start(bf16[192,896]{1,0:T(8,128)(2,1)S(1)} %get-tuple-element.17), channel_id=1, source_target_pairs={{8,0},{9,1},{10,2},{11,3},{12,4},{13,5},{14,6},{15,7},{16,8},{17,9... | collective-permute-start | bytes 1032200 | tf_op jit(solution)/shard_map/ppermute | solution.py:293
  123.8 3.6 %collective-permute-start.30 = (bf16[192,896]{1,0:T(8,128)(2,1)S(1)}, bf16[192,896]{1,0:T(8,128)(2,1)S(1)}, u32[]{:S(2)}, u32[]{:S(2)}) collective-permute-start(bf16[192,896]{1,0:T(8,128)(2,1)S(1)} %ahead_shares.1.refs_6_), channel_id=1, source_target_pairs={{0,8},{1,9},{2,10},{3,11},{4,12},{5,13},{6,14},{7,15},{8,16},{9,17... | collective-permute-start | bytes 1032200 | tf_op jit(solution)/shard_map/ppermute | solution.py:293
  129.1 2.2 %collective-permute-start.32 = (bf16[192,896]{1,0:T(8,128)(2,1)S(1)}, bf16[192,896]{1,0:T(8,128)(2,1)S(1)}, u32[]{:S(2)}, u32[]{:S(2)}) collective-permute-start(bf16[192,896]{1,0:T(8,128)(2,1)S(1)} %get-tuple-element.15.refs_3_), channel_id=1, source_target_pairs={{0,9},{1,8},{2,11},{3,10},{4,13},{5,12},{6,15},{7,14},{8,17},{9,16... | collective-permute-start | bytes 1032200 | tf_op jit(solution)/shard_map/ppermute | solution.py:293
  134.2 3.5 %collective-permute-done.32.refs_1_ = bf16[192,896]{1,0:T(8,128)(2,1)S(1)} collective-permute-done((bf16[192,896]{1,0:T(8,128)(2,1)S(1)}, bf16[192,896]{1,0:T(8,128)(2,1)S(1)}, u32[]{:S(2)}, u32[]{:S(2)}) %collective-permute-start.32) | collective-permute-done | bytes 344096 | tf_op jit(solution)/shard_map/ppermute | solution.py:293
  (123 shorter events, 49.6 us)
Async XLA Ops:
  1.6 9.9 %collective-permute-start.1 = (bf16[192,896]{1,0:T(8,128)(2,1)S(1)}, bf16[192,896]{1,0:T(8,128)(2,1)S(1)}, u32[]{:S(2)}, u32[]{:S(2)}) collective-permute-start(bf16[192,896]{1,0:T(8,128)(2,1)S(1)} %slice_bitcast_fusion.refs_0_), channel_id=1, source_target_pairs={{0,1},{1,0},{2,3},{3,2},{4,5},{5,4},{6,7},{7,6},{8,9},{9,8},{10,11... | collective-permute-start | bytes 1032200 | tf_op jit(solution)/shard_map/ppermute | solution.py:284
  4.9 14.0 %collective-permute-start = (bf16[192,896]{1,0:T(8,128)(2,1)S(1)}, bf16[192,896]{1,0:T(8,128)(2,1)S(1)}, u32[]{:S(2)}, u32[]{:S(2)}) collective-permute-start(bf16[192,896]{1,0:T(8,128)(2,1)S(1)} %ahead_rows_0.1.refs_1_.refs_0_), channel_id=1, source_target_pairs={{0,1},{1,0},{2,3},{3,2},{4,5},{5,4},{6,7},{7,6},{8,9},{9,8},{10,11... | collective-permute-start | bytes 1032200 | tf_op jit(solution)/shard_map/ppermute | solution.py:284
  6.0 20.6 %collective-permute-start.3 = (bf16[192,896]{1,0:T(8,128)(2,1)S(1)}, bf16[192,896]{1,0:T(8,128)(2,1)S(1)}, u32[]{:S(2)}, u32[]{:S(2)}) collective-permute-start(bf16[192,896]{1,0:T(8,128)(2,1)S(1)} %grad_rows_0.1.refs_3_.refs_0_), channel_id=1, source_target_pairs={{0,1},{1,0},{2,3},{3,2},{4,5},{5,4},{6,7},{7,6},{8,9},{9,8},{10,11... | collective-permute-start | bytes 1032200 | tf_op jit(solution)/shard_map/ppermute | solution.py:284
  17.3 16.4 %collective-permute-start.6 = (bf16[192,896]{1,0:T(8,128)(2,1)S(1)}, bf16[192,896]{1,0:T(8,128)(2,1)S(1)}, u32[]{:S(2)}, u32[]{:S(2)}) collective-permute-start(bf16[192,896]{1,0:T(8,128)(2,1)S(1)} %behind_rows_1.1.refs_3_.refs_0_.refs_2_), channel_id=1, source_target_pairs={{0,1},{1,0},{2,3},{3,2},{4,5},{5,4},{6,7},{7,6},{8,9},{9,8},{10,11... | collective-permute-start | bytes 1032200 | tf_op jit(solution)/shard_map/ppermute | solution.py:284
  25.8 10.9 %collective-permute-start.8 = (bf16[2,192,512]{2,1,0:T(8,128)(2,1)S(1)}, bf16[2,192,512]{2,1,0:T(8,128)(2,1)S(1)}, u32[]{:S(2)}, u32[]{:S(2)}) collective-permute-start(bf16[2,192,512]{2,1,0:T(8,128)(2,1)S(1)} %ahead_far_0.1.refs_3_.refs_0_), channel_id=1, source_target_pairs={{0,2},{1,3},{2,0},{3,1},{4,6},{5,7},{6,4},{7,5},{8,10},{9,11},{10,... | collective-permute-start | bytes 1179656 | tf_op jit(solution)/shard_map/ppermute | solution.py:269
  27.3 15.3 %collective-permute-start.5 = (bf16[1,192,512]{2,1,0:T(8,128)(2,1)S(1)}, bf16[1,192,512]{2,1,0:T(8,128)(2,1)S(1)}, u32[]{:S(2)}, u32[]{:S(2)}) collective-permute-start(bf16[1,192,512]{2,1,0:T(8,128)(2,1)S(1)} %grad_far_0.1.refs_2_.refs_0_), channel_id=1, source_target_pairs={{0,2},{1,3},{2,0},{3,1},{4,6},{5,7},{6,4},{7,5},{8,10},{9,11},{10,... | collective-permute-start | bytes 589832 | tf_op jit(solution)/shard_map/ppermute | solution.py:269
  28.4 9.0 %collective-permute-start.7 = (bf16[2,192,512]{2,1,0:T(8,128)(2,1)S(1)}, bf16[2,192,512]{2,1,0:T(8,128)(2,1)S(1)}, u32[]{:S(2)}, u32[]{:S(2)}) collective-permute-start(bf16[2,192,512]{2,1,0:T(8,128)(2,1)S(1)} %behind_middle_0.1.refs_1_), channel_id=1, source_target_pairs={{0,0},{1,1},{2,4},{3,5},{4,2},{5,3},{6,6},{7,7},{8,8},{9,9},{10,12... | collective-permute-start | bytes 1179656 | tf_op jit(solution)/shard_map/ppermute | solution.py:269
  29.2 14.2 %collective-permute-start.4 = (bf16[192,896]{1,0:T(8,128)(2,1)S(1)}, bf16[192,896]{1,0:T(8,128)(2,1)S(1)}, u32[]{:S(2)}, u32[]{:S(2)}) collective-permute-start(bf16[192,896]{1,0:T(8,128)(2,1)S(1)} %ahead_rows_1.1.refs_3_.refs_0_.refs_2_), channel_id=1, source_target_pairs={{0,1},{1,0},{2,3},{3,2},{4,5},{5,4},{6,7},{7,6},{8,9},{9,8},{10,11... | collective-permute-start | bytes 1032200 | tf_op jit(solution)/shard_map/ppermute | solution.py:284
  36.8 9.6 %collective-permute-start.9 = (bf16[2,192,512]{2,1,0:T(8,128)(2,1)S(1)}, bf16[2,192,512]{2,1,0:T(8,128)(2,1)S(1)}, u32[]{:S(2)}, u32[]{:S(2)}) collective-permute-start(bf16[2,192,512]{2,1,0:T(8,128)(2,1)S(1)} %ahead_middle_0.1.refs_3_), channel_id=1, source_target_pairs={{0,0},{1,1},{2,4},{3,5},{4,2},{5,3},{6,6},{7,7},{8,8},{9,9},{10,12... | collective-permute-start | bytes 1179656 | tf_op jit(solution)/shard_map/ppermute | solution.py:269
  37.6 10.5 %collective-permute-start.11 = (bf16[2,192,512]{2,1,0:T(8,128)(2,1)S(1)}, bf16[2,192,512]{2,1,0:T(8,128)(2,1)S(1)}, u32[]{:S(2)}, u32[]{:S(2)}) collective-permute-start(bf16[2,192,512]{2,1,0:T(8,128)(2,1)S(1)} %behind_outer_1.1.refs_1_), channel_id=1, source_target_pairs={{0,2},{1,3},{2,0},{3,1},{4,6},{5,7},{6,4},{7,5},{8,10},{9,11},{10,... | collective-permute-start | bytes 1179656 | tf_op jit(solution)/shard_map/ppermute | solution.py:269
  48.1 12.5 %collective-permute-start.15 = (bf16[2,192,512]{2,1,0:T(8,128)(2,1)S(1)}, bf16[2,192,512]{2,1,0:T(8,128)(2,1)S(1)}, u32[]{:S(2)}, u32[]{:S(2)}) collective-permute-start(bf16[2,192,512]{2,1,0:T(8,128)(2,1)S(1)} %behind_middle_1.1.refs_3_), channel_id=1, source_target_pairs={{0,0},{1,1},{2,4},{3,5},{4,2},{5,3},{6,6},{7,7},{8,8},{9,9},{10,12... | collective-permute-start | bytes 1179656 | tf_op jit(solution)/shard_map/ppermute | solution.py:269
  60.7 11.4 %collective-permute-start.18 = (bf16[2,192,512]{2,1,0:T(8,128)(2,1)S(1)}, bf16[2,192,512]{2,1,0:T(8,128)(2,1)S(1)}, u32[]{:S(2)}, u32[]{:S(2)}) collective-permute-start(bf16[2,192,512]{2,1,0:T(8,128)(2,1)S(1)} %behind_outer_2.1.refs_2_), channel_id=1, source_target_pairs={{0,2},{1,3},{2,0},{3,1},{4,6},{5,7},{6,4},{7,5},{8,10},{9,11},{10,... | collective-permute-start | bytes 1179656 | tf_op jit(solution)/shard_map/ppermute | solution.py:269
  63.5 12.3 %collective-permute-start.17 = (bf16[2,192,512]{2,1,0:T(8,128)(2,1)S(1)}, bf16[2,192,512]{2,1,0:T(8,128)(2,1)S(1)}, u32[]{:S(2)}, u32[]{:S(2)}) collective-permute-start(bf16[2,192,512]{2,1,0:T(8,128)(2,1)S(1)} %ahead_outer_2.1.refs_2_), channel_id=1, source_target_pairs={{0,2},{1,3},{2,0},{3,1},{4,6},{5,7},{6,4},{7,5},{8,10},{9,11},{10,... | collective-permute-start | bytes 1179656 | tf_op jit(solution)/shard_map/ppermute | solution.py:269
  68.2 11.7 %collective-permute-start.21 = (bf16[1,192,512]{2,1,0:T(8,128)(2,1)S(1)}, bf16[1,192,512]{2,1,0:T(8,128)(2,1)S(1)}, u32[]{:S(2)}, u32[]{:S(2)}) collective-permute-start(bf16[1,192,512]{2,1,0:T(8,128)(2,1)S(1)} %grad_third_1.1.refs_1_), channel_id=1, source_target_pairs={{0,2},{1,3},{2,0},{3,1},{4,6},{5,7},{6,4},{7,5},{8,10},{9,11},{10,... | collective-permute-start | bytes 589832 | tf_op jit(solution)/shard_map/ppermute | solution.py:269
  80.3 9.9 %collective-permute-start.24 = (bf16[2,192,512]{2,1,0:T(8,128)(2,1)S(1)}, bf16[2,192,512]{2,1,0:T(8,128)(2,1)S(1)}, u32[]{:S(2)}, u32[]{:S(2)}) collective-permute-start(bf16[2,192,512]{2,1,0:T(8,128)(2,1)S(1)} %behind_back_1.1.refs_2_), channel_id=1, source_target_pairs={{0,2},{1,3},{2,0},{3,1},{4,6},{5,7},{6,4},{7,5},{8,10},{9,11},{10,... | collective-permute-start | bytes 1179656 | tf_op jit(solution)/shard_map/ppermute | solution.py:269
  82.4 9.9 %collective-permute-start.23 = (bf16[1,192,512]{2,1,0:T(8,128)(2,1)S(1)}, bf16[1,192,512]{2,1,0:T(8,128)(2,1)S(1)}, u32[]{:S(2)}, u32[]{:S(2)}) collective-permute-start(bf16[1,192,512]{2,1,0:T(8,128)(2,1)S(1)} %ahead_back_1.1.refs_1_), channel_id=1, source_target_pairs={{0,2},{1,3},{2,0},{3,1},{4,6},{5,7},{6,4},{7,5},{8,10},{9,11},{10,... | collective-permute-start | bytes 589832 | tf_op jit(solution)/shard_map/ppermute | solution.py:269
  92.3 10.8 %collective-permute-start.29 = (bf16[1,192,512]{2,1,0:T(8,128)(2,1)S(1)}, bf16[1,192,512]{2,1,0:T(8,128)(2,1)S(1)}, u32[]{:S(2)}, u32[]{:S(2)}) collective-permute-start(bf16[1,192,512]{2,1,0:T(8,128)(2,1)S(1)} %ahead_first_1.1.refs_5_.refs_1_), channel_id=1, source_target_pairs={{0,0},{1,1},{2,4},{3,5},{4,2},{5,3},{6,6},{7,7},{8,8},{9,9},{10,12... | collective-permute-start | bytes 589832 | tf_op jit(solution)/shard_map/ppermute | solution.py:269
  97.6 26.1 %collective-permute-start.25 = (bf16[192,896]{1,0:T(8,128)(2,1)S(1)}, bf16[192,896]{1,0:T(8,128)(2,1)S(1)}, u32[]{:S(2)}, u32[]{:S(2)}) collective-permute-start(bf16[192,896]{1,0:T(8,128)(2,1)S(1)} %get-tuple-element.12.refs_1_), channel_id=1, source_target_pairs={{0,1},{1,0},{2,3},{3,2},{4,5},{5,4},{6,7},{7,6},{8,9},{9,8},{10,11... | collective-permute-start | bytes 1032200 | tf_op jit(solution)/shard_map/ppermute | solution.py:284
  98.2 15.3 %collective-permute-start.27 = (bf16[2,192,512]{2,1,0:T(8,128)(2,1)S(1)}, bf16[2,192,512]{2,1,0:T(8,128)(2,1)S(1)}, u32[]{:S(2)}, u32[]{:S(2)}) collective-permute-start(bf16[2,192,512]{2,1,0:T(8,128)(2,1)S(1)} %behind_back_2.1.refs_1_), channel_id=1, source_target_pairs={{0,2},{1,3},{2,0},{3,1},{4,6},{5,7},{6,4},{7,5},{8,10},{9,11},{10,... | collective-permute-start | bytes 1179656 | tf_op jit(solution)/shard_map/ppermute | solution.py:269
  103.1 24.4 %collective-permute-start.31 = (bf16[1,192,512]{2,1,0:T(8,128)(2,1)S(1)}, bf16[1,192,512]{2,1,0:T(8,128)(2,1)S(1)}, u32[]{:S(2)}, u32[]{:S(2)}) collective-permute-start(bf16[1,192,512]{2,1,0:T(8,128)(2,1)S(1)} %ahead_back_2.1.refs_2_), channel_id=1, source_target_pairs={{0,2},{1,3},{2,0},{3,1},{4,6},{5,7},{6,4},{7,5},{8,10},{9,11},{10,... | collective-permute-start | bytes 589832 | tf_op jit(solution)/shard_map/ppermute | solution.py:269
  103.3 27.9 %collective-permute-start.34 = (bf16[192,896]{1,0:T(8,128)(2,1)S(1)}, bf16[192,896]{1,0:T(8,128)(2,1)S(1)}, u32[]{:S(2)}, u32[]{:S(2)}) collective-permute-start(bf16[192,896]{1,0:T(8,128)(2,1)S(1)} %behind_shares.1.refs_5_), channel_id=1, source_target_pairs={{8,0},{9,1},{10,2},{11,3},{12,4},{13,5},{14,6},{15,7},{16,8},{17,9... | collective-permute-start | bytes 1032200 | tf_op jit(solution)/shard_map/ppermute | solution.py:293
  115.5 17.7 %collective-permute-start.35 = (bf16[192,896]{1,0:T(8,128)(2,1)S(1)}, bf16[192,896]{1,0:T(8,128)(2,1)S(1)}, u32[]{:S(2)}, u32[]{:S(2)}) collective-permute-start(bf16[192,896]{1,0:T(8,128)(2,1)S(1)} %get-tuple-element.14.refs_2_), channel_id=1, source_target_pairs={{8,1},{9,0},{10,3},{11,2},{12,5},{13,4},{14,7},{15,6},{16,9},{17,8... | collective-permute-start | bytes 1032200 | tf_op jit(solution)/shard_map/ppermute | solution.py:293
  121.8 11.4 %collective-permute-start.36 = (bf16[192,896]{1,0:T(8,128)(2,1)S(1)}, bf16[192,896]{1,0:T(8,128)(2,1)S(1)}, u32[]{:S(2)}, u32[]{:S(2)}) collective-permute-start(bf16[192,896]{1,0:T(8,128)(2,1)S(1)} %get-tuple-element.17), channel_id=1, source_target_pairs={{8,0},{9,1},{10,2},{11,3},{12,4},{13,5},{14,6},{15,7},{16,8},{17,9... | collective-permute-start | bytes 1032200 | tf_op jit(solution)/shard_map/ppermute | solution.py:293
  123.8 15.3 %collective-permute-start.30 = (bf16[192,896]{1,0:T(8,128)(2,1)S(1)}, bf16[192,896]{1,0:T(8,128)(2,1)S(1)}, u32[]{:S(2)}, u32[]{:S(2)}) collective-permute-start(bf16[192,896]{1,0:T(8,128)(2,1)S(1)} %ahead_shares.1.refs_6_), channel_id=1, source_target_pairs={{0,8},{1,9},{2,10},{3,11},{4,12},{5,13},{6,14},{7,15},{8,16},{9,17... | collective-permute-start | bytes 1032200 | tf_op jit(solution)/shard_map/ppermute | solution.py:293
  (23 other events, 134.1 us)

commit v24 on v23

--- a/solution.py
+++ b/solution.py
@@ -463,9 +463,9 @@
     recent.append(behind.out[0])
     ahead.far_product(0)
     ahead.first_hop(0)
+    behind.middle_sum(0)
     grad.far_product(0)
     grad.first_hop(0)
-    behind.middle_sum(0)
     ahead.fetch(1)
     behind.far_product(1)
     behind.near_products()

time: 142 us -> 143 us (level)
  starting transfers between devices: 73.7 us -> 75.4 us
  waiting for transfers between devices: 36.2 us -> 34.5 us
    ppermute x8, waiting for transfers between devices: 7.8 us -> 4.93 us  [swapped(): return lax.ppermute(value, 'expert', [(i, i ^ 1) for i in range(devices)])]
where the time goes in v24:
time: 143 us; the launch traced here: 142 us
  starting transfers between devices  75.4 us (53%)
  waiting for transfers between devices  34.5 us (24%)
  Pallas kernels  22 us (15%)
  local copies, waits for them, and re-layouts  8.3 us (6%)
    ppermute x23, starting transfers between devices, between(): return lax.ppermute(value, 'expert', pairs)  39.9 us
    ppermute x6, starting transfers between devices, to_section(): return lax.ppermute(value, ('section', 'expert'), pairs)  27.3 us
    ppermute x23, waiting for transfers between devices, between(): return lax.ppermute(value, 'expert', pairs)  24.6 us
    pallas_call x46, Pallas kernels, call(): pl.pallas_call(run, compiler_params=pltpu.CompilerParams(vmem_limit_bytes...  22 us
    ppermute x8, starting transfers between devices, swapped(): return lax.ppermute(value, 'expert', [(i, i ^ 1) for i in range(devices)])  8.23 us
    unnamed x20, local copies, waits for them, and re-layouts  6.73 us
    ppermute x6, waiting for transfers between devices, to_section(): return lax.ppermute(value, ('section', 'expert'), pairs)  5 us
    ppermute x8, waiting for transfers between devices, swapped(): return lax.ppermute(value, 'expert', [(i, i ^ 1) for i in range(devices)])  4.93 us
  transfers between devices with their start and end apart: 37, of which 12 were waited for; matrix products, arithmetic and copies ran while one was open for 0% of the time, Pallas kernels for 15%

profile of v24, /device:TPU:1, one launch (start us, length us, event | category | flops | bytes accessed | tf_op | source)
XLA Modules:
  0.0 141.5 jit_solution(9377931798903248291)
XLA Ops:
  1.6 2.1 %collective-permute-start.2 = (bf16[192,896]{1,0:T(8,128)(2,1)S(1)}, bf16[192,896]{1,0:T(8,128)(2,1)S(1)}, u32[]{:S(2)}, u32[]{:S(2)}) collective-permute-start(bf16[192,896]{1,0:T(8,128)(2,1)S(1)} %slice_bitcast_fusion.refs_0_), channel_id=1, source_target_pairs={{0,1},{1,0},{2,3},{3,2},{4,5},{5,4},{6,7},{7,6},{8,9},{9,8},{10,11... | collective-permute-start | bytes 1032200 | tf_op jit(solution)/shard_map/ppermute | solution.py:284
  7.3 4.2 %collective-permute-done.2.refs_1_ = bf16[192,896]{1,0:T(8,128)(2,1)S(1)} collective-permute-done((bf16[192,896]{1,0:T(8,128)(2,1)S(1)}, bf16[192,896]{1,0:T(8,128)(2,1)S(1)}, u32[]{:S(2)}, u32[]{:S(2)}) %collective-permute-start.2) | collective-permute-done | bytes 344096 | tf_op jit(solution)/shard_map/ppermute | solution.py:284
  11.6 3.1 %copy-done.1 = bf16[1,1,2,1024,1792]{4,3,2,1,0:T(8,128)(2,1)S(1)} copy-done((bf16[1,1,2,1024,1792]{4,3,2,1,0:T(8,128)(2,1)S(1)}, bf16[1,1,2,1024,1792]{4,3,2,1,0:T(8,128)(2,1)}, u32[]{:S(2)}) %copy-start.1) | copy-done | bytes 7340056
  18.9 5.5 %collective-permute-done.3.refs_4_.refs_1_ = bf16[2,192,512]{2,1,0:T(8,128)(2,1)S(1)} collective-permute-done((bf16[2,192,512]{2,1,0:T(8,128)(2,1)S(1)}, bf16[2,192,512]{2,1,0:T(8,128)(2,1)S(1)}, u32[]{:S(2)}, u32[]{:S(2)}) %collective-permute-start.3) | collective-permute-done | bytes 393248 | tf_op jit(solution)/shard_map/ppermute | solution.py:269
  28.6 3.4 %collective-permute-start.5 = (bf16[1,192,512]{2,1,0:T(8,128)(2,1)S(1)}, bf16[1,192,512]{2,1,0:T(8,128)(2,1)S(1)}, u32[]{:S(2)}, u32[]{:S(2)}) collective-permute-start(bf16[1,192,512]{2,1,0:T(8,128)(2,1)S(1)} %grad_far_0.1.refs_1_.refs_0_), channel_id=1, source_target_pairs={{0,2},{1,3},{2,0},{3,1},{4,6},{5,7},{6,4},{7,5},{8,10},{9,11},{10,... | collective-permute-start | bytes 589832 | tf_op jit(solution)/shard_map/ppermute | solution.py:269
  37.6 3.8 %collective-permute-start.11 = (bf16[2,192,512]{2,1,0:T(8,128)(2,1)S(1)}, bf16[2,192,512]{2,1,0:T(8,128)(2,1)S(1)}, u32[]{:S(2)}, u32[]{:S(2)}) collective-permute-start(bf16[2,192,512]{2,1,0:T(8,128)(2,1)S(1)} %behind_outer_1.1.refs_1_), channel_id=1, source_target_pairs={{0,2},{1,3},{2,0},{3,1},{4,6},{5,7},{6,4},{7,5},{8,10},{9,11},{10,... | collective-permute-start | bytes 1179656 | tf_op jit(solution)/shard_map/ppermute | solution.py:269
  50.6 2.6 %collective-permute-start.14 = (bf16[1,192,512]{2,1,0:T(8,128)(2,1)S(1)}, bf16[1,192,512]{2,1,0:T(8,128)(2,1)S(1)}, u32[]{:S(2)}, u32[]{:S(2)}) collective-permute-start(bf16[1,192,512]{2,1,0:T(8,128)(2,1)S(1)} %grad_outer_1.1.refs_2_), channel_id=1, source_target_pairs={{0,2},{1,3},{2,0},{3,1},{4,6},{5,7},{6,4},{7,5},{8,10},{9,11},{10,... | collective-permute-start | bytes 589832 | tf_op jit(solution)/shard_map/ppermute | solution.py:269
  53.2 2.2 %collective-permute-done.10.refs_1_ = bf16[2,192,512]{2,1,0:T(8,128)(2,1)S(1)} collective-permute-done((bf16[2,192,512]{2,1,0:T(8,128)(2,1)S(1)}, bf16[2,192,512]{2,1,0:T(8,128)(2,1)S(1)}, u32[]{:S(2)}, u32[]{:S(2)}) %collective-permute-start.10) | collective-permute-done | bytes 393248 | tf_op jit(solution)/shard_map/ppermute | solution.py:269
  56.2 3.4 %collective-permute-done.14.refs_1_.refs_3_ = bf16[1,192,512]{2,1,0:T(8,128)(2,1)S(1)} collective-permute-done((bf16[1,192,512]{2,1,0:T(8,128)(2,1)S(1)}, bf16[1,192,512]{2,1,0:T(8,128)(2,1)S(1)}, u32[]{:S(2)}, u32[]{:S(2)}) %collective-permute-start.14) | collective-permute-done | bytes 196640 | tf_op jit(solution)/shard_map/ppermute | solution.py:269
  60.7 2.6 %collective-permute-start.18 = (bf16[2,192,512]{2,1,0:T(8,128)(2,1)S(1)}, bf16[2,192,512]{2,1,0:T(8,128)(2,1)S(1)}, u32[]{:S(2)}, u32[]{:S(2)}) collective-permute-start(bf16[2,192,512]{2,1,0:T(8,128)(2,1)S(1)} %behind_outer_2.1.refs_2_), channel_id=1, source_target_pairs={{0,2},{1,3},{2,0},{3,1},{4,6},{5,7},{6,4},{7,5},{8,10},{9,11},{10,... | collective-permute-start | bytes 1179656 | tf_op jit(solution)/shard_map/ppermute | solution.py:269
  63.5 4.7 %collective-permute-start.17 = (bf16[2,192,512]{2,1,0:T(8,128)(2,1)S(1)}, bf16[2,192,512]{2,1,0:T(8,128)(2,1)S(1)}, u32[]{:S(2)}, u32[]{:S(2)}) collective-permute-start(bf16[2,192,512]{2,1,0:T(8,128)(2,1)S(1)} %ahead_outer_2.1.refs_2_), channel_id=1, source_target_pairs={{0,2},{1,3},{2,0},{3,1},{4,6},{5,7},{6,4},{7,5},{8,10},{9,11},{10,... | collective-permute-start | bytes 1179656 | tf_op jit(solution)/shard_map/ppermute | solution.py:269
  68.2 3.9 %collective-permute-start.21 = (bf16[1,192,512]{2,1,0:T(8,128)(2,1)S(1)}, bf16[1,192,512]{2,1,0:T(8,128)(2,1)S(1)}, u32[]{:S(2)}, u32[]{:S(2)}) collective-permute-start(bf16[1,192,512]{2,1,0:T(8,128)(2,1)S(1)} %grad_third_1.1.refs_1_), channel_id=1, source_target_pairs={{0,2},{1,3},{2,0},{3,1},{4,6},{5,7},{6,4},{7,5},{8,10},{9,11},{10,... | collective-permute-start | bytes 589832 | tf_op jit(solution)/shard_map/ppermute | solution.py:269
  72.9 2.9 %collective-permute-done.17.refs_0_.refs_1_ = bf16[2,192,512]{2,1,0:T(8,128)(2,1)S(1)} collective-permute-done((bf16[2,192,512]{2,1,0:T(8,128)(2,1)S(1)}, bf16[2,192,512]{2,1,0:T(8,128)(2,1)S(1)}, u32[]{:S(2)}, u32[]{:S(2)}) %collective-permute-start.17) | collective-permute-done | bytes 393248 | tf_op jit(solution)/shard_map/ppermute | solution.py:269
  76.6 3.4 %collective-permute-done.21.refs_3_ = bf16[1,192,512]{2,1,0:T(8,128)(2,1)S(1)} collective-permute-done((bf16[1,192,512]{2,1,0:T(8,128)(2,1)S(1)}, bf16[1,192,512]{2,1,0:T(8,128)(2,1)S(1)}, u32[]{:S(2)}, u32[]{:S(2)}) %collective-permute-start.21) | collective-permute-done | bytes 196640 | tf_op jit(solution)/shard_map/ppermute | solution.py:269
  81.6 2.8 %collective-permute-start.23 = (bf16[1,192,512]{2,1,0:T(8,128)(2,1)S(1)}, bf16[1,192,512]{2,1,0:T(8,128)(2,1)S(1)}, u32[]{:S(2)}, u32[]{:S(2)}) collective-permute-start(bf16[1,192,512]{2,1,0:T(8,128)(2,1)S(1)} %ahead_back_1.1.refs_1_), channel_id=1, source_target_pairs={{0,2},{1,3},{2,0},{3,1},{4,6},{5,7},{6,4},{7,5},{8,10},{9,11},{10,... | collective-permute-start | bytes 589832 | tf_op jit(solution)/shard_map/ppermute | solution.py:269
  84.4 5.8 %collective-permute-done.24.refs_0_.refs_3_ = bf16[2,192,512]{2,1,0:T(8,128)(2,1)S(1)} collective-permute-done((bf16[2,192,512]{2,1,0:T(8,128)(2,1)S(1)}, bf16[2,192,512]{2,1,0:T(8,128)(2,1)S(1)}, u32[]{:S(2)}, u32[]{:S(2)}) %collective-permute-start.24) | collective-permute-done | bytes 393248 | tf_op jit(solution)/shard_map/ppermute | solution.py:269
  93.0 2.1 %behind_out_0.1 = (bf16[192,896]{1,0:T(8,128)(2,1)S(1)}, bf16[192,896]{1,0:T(8,128)(2,1)S(1)}) custom-call(bf16[2,192,512]{2,1,0:T(8,128)(2,1)S(1)} %behind_act_0.1.refs_0_.refs_3_, bf16[2,192,512]{2,1,0:T(8,128)(2,1)S(1)} %behind_first_0.1.refs_1_, bf16[2,192,512]{2,1,0:T(8,128)(2,1)S(1)} %collective-permute-done.22.refs_1_.refs_2_, ...), custom_call_target="tpu_custom_call" | custom-call | flops 20000000000 | bytes 1024 | tf_op jit(solution)/shard_map/behind_out_0/pallas_call | solution.py:43
  98.2 4.2 %collective-permute-start.27 = (bf16[2,192,512]{2,1,0:T(8,128)(2,1)S(1)}, bf16[2,192,512]{2,1,0:T(8,128)(2,1)S(1)}, u32[]{:S(2)}, u32[]{:S(2)}) collective-permute-start(bf16[2,192,512]{2,1,0:T(8,128)(2,1)S(1)} %behind_back_2.1.refs_1_), channel_id=1, source_target_pairs={{0,2},{1,3},{2,0},{3,1},{4,6},{5,7},{6,4},{7,5},{8,10},{9,11},{10,... | collective-permute-start | bytes 1179656 | tf_op jit(solution)/shard_map/ppermute | solution.py:269
  102.6 11.3 %collective-permute-start.34 = (bf16[192,896]{1,0:T(8,128)(2,1)S(1)}, bf16[192,896]{1,0:T(8,128)(2,1)S(1)}, u32[]{:S(2)}, u32[]{:S(2)}) collective-permute-start(bf16[192,896]{1,0:T(8,128)(2,1)S(1)} %behind_shares.1.refs_5_), channel_id=1, source_target_pairs={{8,0},{9,1},{10,2},{11,3},{12,4},{13,5},{14,6},{15,7},{16,8},{17,9... | collective-permute-start | bytes 1032200 | tf_op jit(solution)/shard_map/ppermute | solution.py:293
  115.8 6.3 %collective-permute-start.35 = (bf16[192,896]{1,0:T(8,128)(2,1)S(1)}, bf16[192,896]{1,0:T(8,128)(2,1)S(1)}, u32[]{:S(2)}, u32[]{:S(2)}) collective-permute-start(bf16[192,896]{1,0:T(8,128)(2,1)S(1)} %get-tuple-element.14.refs_2_), channel_id=1, source_target_pairs={{8,1},{9,0},{10,3},{11,2},{12,5},{13,4},{14,7},{15,6},{16,9},{17,8... | collective-permute-start | bytes 1032200 | tf_op jit(solution)/shard_map/ppermute | solution.py:293
  124.1 3.6 %collective-permute-start.30 = (bf16[192,896]{1,0:T(8,128)(2,1)S(1)}, bf16[192,896]{1,0:T(8,128)(2,1)S(1)}, u32[]{:S(2)}, u32[]{:S(2)}) collective-permute-start(bf16[192,896]{1,0:T(8,128)(2,1)S(1)} %ahead_shares.1.refs_6_), channel_id=1, source_target_pairs={{0,8},{1,9},{2,10},{3,11},{4,12},{5,13},{6,14},{7,15},{8,16},{9,17... | collective-permute-start | bytes 1032200 | tf_op jit(solution)/shard_map/ppermute | solution.py:293
  129.4 2.2 %collective-permute-start.32 = (bf16[192,896]{1,0:T(8,128)(2,1)S(1)}, bf16[192,896]{1,0:T(8,128)(2,1)S(1)}, u32[]{:S(2)}, u32[]{:S(2)}) collective-permute-start(bf16[192,896]{1,0:T(8,128)(2,1)S(1)} %get-tuple-element.15.refs_3_), channel_id=1, source_target_pairs={{0,9},{1,8},{2,11},{3,10},{4,13},{5,12},{6,15},{7,14},{8,17},{9,16... | collective-permute-start | bytes 1032200 | tf_op jit(solution)/shard_map/ppermute | solution.py:293
  131.6 1.9 %collective-permute-start.33 = (bf16[192,896]{1,0:T(8,128)(2,1)S(1)}, bf16[192,896]{1,0:T(8,128)(2,1)S(1)}, u32[]{:S(2)}, u32[]{:S(2)}) collective-permute-start(bf16[192,896]{1,0:T(8,128)(2,1)S(1)} %get-tuple-element.16), channel_id=1, source_target_pairs={{0,8},{1,9},{2,10},{3,11},{4,12},{5,13},{6,14},{7,15},{8,16},{9,17... | collective-permute-start | bytes 1032200 | tf_op jit(solution)/shard_map/ppermute | solution.py:293
  134.5 3.5 %collective-permute-done.32.refs_1_ = bf16[192,896]{1,0:T(8,128)(2,1)S(1)} collective-permute-done((bf16[192,896]{1,0:T(8,128)(2,1)S(1)}, bf16[192,896]{1,0:T(8,128)(2,1)S(1)}, u32[]{:S(2)}, u32[]{:S(2)}) %collective-permute-start.32) | collective-permute-done | bytes 344096 | tf_op jit(solution)/shard_map/ppermute | solution.py:293
  (123 shorter events, 48.8 us)
Async XLA Ops:
  1.6 9.9 %collective-permute-start.2 = (bf16[192,896]{1,0:T(8,128)(2,1)S(1)}, bf16[192,896]{1,0:T(8,128)(2,1)S(1)}, u32[]{:S(2)}, u32[]{:S(2)}) collective-permute-start(bf16[192,896]{1,0:T(8,128)(2,1)S(1)} %slice_bitcast_fusion.refs_0_), channel_id=1, source_target_pairs={{0,1},{1,0},{2,3},{3,2},{4,5},{5,4},{6,7},{7,6},{8,9},{9,8},{10,11... | collective-permute-start | bytes 1032200 | tf_op jit(solution)/shard_map/ppermute | solution.py:284
  4.9 14.0 %collective-permute-start = (bf16[192,896]{1,0:T(8,128)(2,1)S(1)}, bf16[192,896]{1,0:T(8,128)(2,1)S(1)}, u32[]{:S(2)}, u32[]{:S(2)}) collective-permute-start(bf16[192,896]{1,0:T(8,128)(2,1)S(1)} %ahead_rows_0.1.refs_1_.refs_0_), channel_id=1, source_target_pairs={{0,1},{1,0},{2,3},{3,2},{4,5},{5,4},{6,7},{7,6},{8,9},{9,8},{10,11... | collective-permute-start | bytes 1032200 | tf_op jit(solution)/shard_map/ppermute | solution.py:284
  6.0 21.5 %collective-permute-start.1 = (bf16[192,896]{1,0:T(8,128)(2,1)S(1)}, bf16[192,896]{1,0:T(8,128)(2,1)S(1)}, u32[]{:S(2)}, u32[]{:S(2)}) collective-permute-start(bf16[192,896]{1,0:T(8,128)(2,1)S(1)} %grad_rows_0.1.refs_3_.refs_0_), channel_id=1, source_target_pairs={{0,1},{1,0},{2,3},{3,2},{4,5},{5,4},{6,7},{7,6},{8,9},{9,8},{10,11... | collective-permute-start | bytes 1032200 | tf_op jit(solution)/shard_map/ppermute | solution.py:284
  17.3 16.4 %collective-permute-start.6 = (bf16[192,896]{1,0:T(8,128)(2,1)S(1)}, bf16[192,896]{1,0:T(8,128)(2,1)S(1)}, u32[]{:S(2)}, u32[]{:S(2)}) collective-permute-start(bf16[192,896]{1,0:T(8,128)(2,1)S(1)} %behind_rows_1.1.refs_3_.refs_0_.refs_2_), channel_id=1, source_target_pairs={{0,1},{1,0},{2,3},{3,2},{4,5},{5,4},{6,7},{7,6},{8,9},{9,8},{10,11... | collective-permute-start | bytes 1032200 | tf_op jit(solution)/shard_map/ppermute | solution.py:284
  25.8 10.9 %collective-permute-start.8 = (bf16[2,192,512]{2,1,0:T(8,128)(2,1)S(1)}, bf16[2,192,512]{2,1,0:T(8,128)(2,1)S(1)}, u32[]{:S(2)}, u32[]{:S(2)}) collective-permute-start(bf16[2,192,512]{2,1,0:T(8,128)(2,1)S(1)} %ahead_far_0.1.refs_2_.refs_0_), channel_id=1, source_target_pairs={{0,2},{1,3},{2,0},{3,1},{4,6},{5,7},{6,4},{7,5},{8,10},{9,11},{10,... | collective-permute-start | bytes 1179656 | tf_op jit(solution)/shard_map/ppermute | solution.py:269
  26.7 10.8 %collective-permute-start.7 = (bf16[2,192,512]{2,1,0:T(8,128)(2,1)S(1)}, bf16[2,192,512]{2,1,0:T(8,128)(2,1)S(1)}, u32[]{:S(2)}, u32[]{:S(2)}) collective-permute-start(bf16[2,192,512]{2,1,0:T(8,128)(2,1)S(1)} %behind_middle_0.1.refs_3_), channel_id=1, source_target_pairs={{0,0},{1,1},{2,4},{3,5},{4,2},{5,3},{6,6},{7,7},{8,8},{9,9},{10,12... | collective-permute-start | bytes 1179656 | tf_op jit(solution)/shard_map/ppermute | solution.py:269
  28.6 14.1 %collective-permute-start.5 = (bf16[1,192,512]{2,1,0:T(8,128)(2,1)S(1)}, bf16[1,192,512]{2,1,0:T(8,128)(2,1)S(1)}, u32[]{:S(2)}, u32[]{:S(2)}) collective-permute-start(bf16[1,192,512]{2,1,0:T(8,128)(2,1)S(1)} %grad_far_0.1.refs_1_.refs_0_), channel_id=1, source_target_pairs={{0,2},{1,3},{2,0},{3,1},{4,6},{5,7},{6,4},{7,5},{8,10},{9,11},{10,... | collective-permute-start | bytes 589832 | tf_op jit(solution)/shard_map/ppermute | solution.py:269
  32.0 11.4 %collective-permute-start.4 = (bf16[192,896]{1,0:T(8,128)(2,1)S(1)}, bf16[192,896]{1,0:T(8,128)(2,1)S(1)}, u32[]{:S(2)}, u32[]{:S(2)}) collective-permute-start(bf16[192,896]{1,0:T(8,128)(2,1)S(1)} %ahead_rows_1.1.refs_3_.refs_0_.refs_2_), channel_id=1, source_target_pairs={{0,1},{1,0},{2,3},{3,2},{4,5},{5,4},{6,7},{7,6},{8,9},{9,8},{10,11... | collective-permute-start | bytes 1032200 | tf_op jit(solution)/shard_map/ppermute | solution.py:284
  36.8 9.6 %collective-permute-start.9 = (bf16[2,192,512]{2,1,0:T(8,128)(2,1)S(1)}, bf16[2,192,512]{2,1,0:T(8,128)(2,1)S(1)}, u32[]{:S(2)}, u32[]{:S(2)}) collective-permute-start(bf16[2,192,512]{2,1,0:T(8,128)(2,1)S(1)} %ahead_middle_0.1.refs_3_), channel_id=1, source_target_pairs={{0,0},{1,1},{2,4},{3,5},{4,2},{5,3},{6,6},{7,7},{8,8},{9,9},{10,12... | collective-permute-start | bytes 1179656 | tf_op jit(solution)/shard_map/ppermute | solution.py:269
  37.6 10.5 %collective-permute-start.11 = (bf16[2,192,512]{2,1,0:T(8,128)(2,1)S(1)}, bf16[2,192,512]{2,1,0:T(8,128)(2,1)S(1)}, u32[]{:S(2)}, u32[]{:S(2)}) collective-permute-start(bf16[2,192,512]{2,1,0:T(8,128)(2,1)S(1)} %behind_outer_1.1.refs_1_), channel_id=1, source_target_pairs={{0,2},{1,3},{2,0},{3,1},{4,6},{5,7},{6,4},{7,5},{8,10},{9,11},{10,... | collective-permute-start | bytes 1179656 | tf_op jit(solution)/shard_map/ppermute | solution.py:269
  48.1 12.5 %collective-permute-start.15 = (bf16[2,192,512]{2,1,0:T(8,128)(2,1)S(1)}, bf16[2,192,512]{2,1,0:T(8,128)(2,1)S(1)}, u32[]{:S(2)}, u32[]{:S(2)}) collective-permute-start(bf16[2,192,512]{2,1,0:T(8,128)(2,1)S(1)} %behind_middle_1.1.refs_3_), channel_id=1, source_target_pairs={{0,0},{1,1},{2,4},{3,5},{4,2},{5,3},{6,6},{7,7},{8,8},{9,9},{10,12... | collective-permute-start | bytes 1179656 | tf_op jit(solution)/shard_map/ppermute | solution.py:269
  60.7 11.4 %collective-permute-start.18 = (bf16[2,192,512]{2,1,0:T(8,128)(2,1)S(1)}, bf16[2,192,512]{2,1,0:T(8,128)(2,1)S(1)}, u32[]{:S(2)}, u32[]{:S(2)}) collective-permute-start(bf16[2,192,512]{2,1,0:T(8,128)(2,1)S(1)} %behind_outer_2.1.refs_2_), channel_id=1, source_target_pairs={{0,2},{1,3},{2,0},{3,1},{4,6},{5,7},{6,4},{7,5},{8,10},{9,11},{10,... | collective-permute-start | bytes 1179656 | tf_op jit(solution)/shard_map/ppermute | solution.py:269
  63.5 12.2 %collective-permute-start.17 = (bf16[2,192,512]{2,1,0:T(8,128)(2,1)S(1)}, bf16[2,192,512]{2,1,0:T(8,128)(2,1)S(1)}, u32[]{:S(2)}, u32[]{:S(2)}) collective-permute-start(bf16[2,192,512]{2,1,0:T(8,128)(2,1)S(1)} %ahead_outer_2.1.refs_2_), channel_id=1, source_target_pairs={{0,2},{1,3},{2,0},{3,1},{4,6},{5,7},{6,4},{7,5},{8,10},{9,11},{10,... | collective-permute-start | bytes 1179656 | tf_op jit(solution)/shard_map/ppermute | solution.py:269
  68.2 11.7 %collective-permute-start.21 = (bf16[1,192,512]{2,1,0:T(8,128)(2,1)S(1)}, bf16[1,192,512]{2,1,0:T(8,128)(2,1)S(1)}, u32[]{:S(2)}, u32[]{:S(2)}) collective-permute-start(bf16[1,192,512]{2,1,0:T(8,128)(2,1)S(1)} %grad_third_1.1.refs_1_), channel_id=1, source_target_pairs={{0,2},{1,3},{2,0},{3,1},{4,6},{5,7},{6,4},{7,5},{8,10},{9,11},{10,... | collective-permute-start | bytes 589832 | tf_op jit(solution)/shard_map/ppermute | solution.py:269
  80.3 9.9 %collective-permute-start.24 = (bf16[2,192,512]{2,1,0:T(8,128)(2,1)S(1)}, bf16[2,192,512]{2,1,0:T(8,128)(2,1)S(1)}, u32[]{:S(2)}, u32[]{:S(2)}) collective-permute-start(bf16[2,192,512]{2,1,0:T(8,128)(2,1)S(1)} %behind_back_1.1.refs_2_), channel_id=1, source_target_pairs={{0,2},{1,3},{2,0},{3,1},{4,6},{5,7},{6,4},{7,5},{8,10},{9,11},{10,... | collective-permute-start | bytes 1179656 | tf_op jit(solution)/shard_map/ppermute | solution.py:269
  81.6 10.7 %collective-permute-start.23 = (bf16[1,192,512]{2,1,0:T(8,128)(2,1)S(1)}, bf16[1,192,512]{2,1,0:T(8,128)(2,1)S(1)}, u32[]{:S(2)}, u32[]{:S(2)}) collective-permute-start(bf16[1,192,512]{2,1,0:T(8,128)(2,1)S(1)} %ahead_back_1.1.refs_1_), channel_id=1, source_target_pairs={{0,2},{1,3},{2,0},{3,1},{4,6},{5,7},{6,4},{7,5},{8,10},{9,11},{10,... | collective-permute-start | bytes 589832 | tf_op jit(solution)/shard_map/ppermute | solution.py:269
  92.3 10.1 %collective-permute-start.29 = (bf16[1,192,512]{2,1,0:T(8,128)(2,1)S(1)}, bf16[1,192,512]{2,1,0:T(8,128)(2,1)S(1)}, u32[]{:S(2)}, u32[]{:S(2)}) collective-permute-start(bf16[1,192,512]{2,1,0:T(8,128)(2,1)S(1)} %ahead_first_1.1.refs_5_.refs_1_), channel_id=1, source_target_pairs={{0,0},{1,1},{2,4},{3,5},{4,2},{5,3},{6,6},{7,7},{8,8},{9,9},{10,12... | collective-permute-start | bytes 589832 | tf_op jit(solution)/shard_map/ppermute | solution.py:269
  97.7 26.3 %collective-permute-start.25 = (bf16[192,896]{1,0:T(8,128)(2,1)S(1)}, bf16[192,896]{1,0:T(8,128)(2,1)S(1)}, u32[]{:S(2)}, u32[]{:S(2)}) collective-permute-start(bf16[192,896]{1,0:T(8,128)(2,1)S(1)} %get-tuple-element.12.refs_1_), channel_id=1, source_target_pairs={{0,1},{1,0},{2,3},{3,2},{4,5},{5,4},{6,7},{7,6},{8,9},{9,8},{10,11... | collective-permute-start | bytes 1032200 | tf_op jit(solution)/shard_map/ppermute | solution.py:284
  98.2 15.6 %collective-permute-start.27 = (bf16[2,192,512]{2,1,0:T(8,128)(2,1)S(1)}, bf16[2,192,512]{2,1,0:T(8,128)(2,1)S(1)}, u32[]{:S(2)}, u32[]{:S(2)}) collective-permute-start(bf16[2,192,512]{2,1,0:T(8,128)(2,1)S(1)} %behind_back_2.1.refs_1_), channel_id=1, source_target_pairs={{0,2},{1,3},{2,0},{3,1},{4,6},{5,7},{6,4},{7,5},{8,10},{9,11},{10,... | collective-permute-start | bytes 1179656 | tf_op jit(solution)/shard_map/ppermute | solution.py:269
  102.4 25.4 %collective-permute-start.31 = (bf16[1,192,512]{2,1,0:T(8,128)(2,1)S(1)}, bf16[1,192,512]{2,1,0:T(8,128)(2,1)S(1)}, u32[]{:S(2)}, u32[]{:S(2)}) collective-permute-start(bf16[1,192,512]{2,1,0:T(8,128)(2,1)S(1)} %ahead_back_2.1.refs_2_), channel_id=1, source_target_pairs={{0,2},{1,3},{2,0},{3,1},{4,6},{5,7},{6,4},{7,5},{8,10},{9,11},{10,... | collective-permute-start | bytes 589832 | tf_op jit(solution)/shard_map/ppermute | solution.py:269
  102.6 29.0 %collective-permute-start.34 = (bf16[192,896]{1,0:T(8,128)(2,1)S(1)}, bf16[192,896]{1,0:T(8,128)(2,1)S(1)}, u32[]{:S(2)}, u32[]{:S(2)}) collective-permute-start(bf16[192,896]{1,0:T(8,128)(2,1)S(1)} %behind_shares.1.refs_5_), channel_id=1, source_target_pairs={{8,0},{9,1},{10,2},{11,3},{12,4},{13,5},{14,6},{15,7},{16,8},{17,9... | collective-permute-start | bytes 1032200 | tf_op jit(solution)/shard_map/ppermute | solution.py:293
  115.8 17.7 %collective-permute-start.35 = (bf16[192,896]{1,0:T(8,128)(2,1)S(1)}, bf16[192,896]{1,0:T(8,128)(2,1)S(1)}, u32[]{:S(2)}, u32[]{:S(2)}) collective-permute-start(bf16[192,896]{1,0:T(8,128)(2,1)S(1)} %get-tuple-element.14.refs_2_), channel_id=1, source_target_pairs={{8,1},{9,0},{10,3},{11,2},{12,5},{13,4},{14,7},{15,6},{16,9},{17,8... | collective-permute-start | bytes 1032200 | tf_op jit(solution)/shard_map/ppermute | solution.py:293
  122.1 11.4 %collective-permute-start.36 = (bf16[192,896]{1,0:T(8,128)(2,1)S(1)}, bf16[192,896]{1,0:T(8,128)(2,1)S(1)}, u32[]{:S(2)}, u32[]{:S(2)}) collective-permute-start(bf16[192,896]{1,0:T(8,128)(2,1)S(1)} %get-tuple-element.17), channel_id=1, source_target_pairs={{8,0},{9,1},{10,2},{11,3},{12,4},{13,5},{14,6},{15,7},{16,8},{17,9... | collective-permute-start | bytes 1032200 | tf_op jit(solution)/shard_map/ppermute | solution.py:293
  124.1 15.3 %collective-permute-start.30 = (bf16[192,896]{1,0:T(8,128)(2,1)S(1)}, bf16[192,896]{1,0:T(8,128)(2,1)S(1)}, u32[]{:S(2)}, u32[]{:S(2)}) collective-permute-start(bf16[192,896]{1,0:T(8,128)(2,1)S(1)} %ahead_shares.1.refs_6_), channel_id=1, source_target_pairs={{0,8},{1,9},{2,10},{3,11},{4,12},{5,13},{6,14},{7,15},{8,16},{9,17... | collective-permute-start | bytes 1032200 | tf_op jit(solution)/shard_map/ppermute | solution.py:293
  (23 other events, 127.7 us)
